TPU v7x, 32 devices: a whole 2x2x4 slice. The times are simulated.
32 devices in a mesh: ka: 8 (over y, x, core), hist: 4 (over z).
Axes of the slice: x: 2, y: 2, z: 4, core: 2. Of those that a mesh axis runs over, the one named last changes fastest.
Arguments:
- green_row: float32 [256, 576, 128], P('hist', 'ka'), may hold values from -6 to 6
- screened: float32 [256, 576, 128], P('hist', 'ka'), may hold values from -0.2 to 0.2
- hamilton: float32 [576, 128], P('ka'), may hold values from -6 to 6
- equal_time: float32 [576, 128], P('ka'), may hold values from -0.5 to 2.5, as said below
- quad_class: int32 [256], P('hist'), may hold values from 0 to 3
- live_count: int32 [4], P('hist'), may hold values from 1 to 64
Outputs:
- green_next: float32 [256, 576, 128], P('hist', 'ka')
Inputs may be any that keep to these rules, and one draw needn't show every extreme that they name: `quad_class`: class c selects the weight q[c] of q = (0.375, 1.1666666, 0.9583333, 1.0). Stored times at positions live_count[j] or later inside block j carry no weight. `equal_time`: the imaginary diagonal entries are positive.
All inputs are finite; a program needn't handle non-finite values.
Results may differ from a plain program's by a relative error of at most 0.00005.
Values sent between devices are 32-bit elements; how exact they have to be, the bound alone decides.
No kernel may reach another device: no remote copies, remote signals or barrier semaphores. Data moves between devices by JAX's collectives and lax.ppermute only.
A program may use at most 64 MiB of HBM per device.

v0:
```python
import functools
import math

import jax
import jax.numpy as jnp
import ml_dtypes
import numpy as np
from jax import lax
from jax.experimental import pallas as pl
from jax.experimental.pallas import tpu as pltpu
from jax.sharding import PartitionSpec as P

SIDE = 24
BANDS = 8
ENTRIES = BANDS * BANDS
WIDTH = 2 * ENTRIES
TILE = 8
STEPS = 4

time_step = 0.1
hubbard = 1.0
quadrature = (0.375, 1.1666666, 0.9583333, 1.0)

IN_FLIGHT = 5

VMEM_LIMIT = 48 * 1024 * 1024


def lane_sign(shape):
    lane = lax.broadcasted_iota(jnp.int32, shape, len(shape) - 1)
    return lane < ENTRIES


def swap(x):
    return pltpu.roll(x, ENTRIES, 1)


def roll_blocks(x, blocks):
    return x if blocks == 0 else pltpu.roll(x, WIDTH - BANDS * blocks, x.ndim - 1)


def tree_sum(terms):
    while len(terms) > 1:
        terms = [sum(terms[i : i + 2][1:], terms[i]) for i in range(0, len(terms), 2)]
    return terms[0]


def dft24(x, sign, low):
    root3 = jnp.where(low, -1.0, 1.0) * (sign * math.sqrt(3.0) / 2)
    turn = jnp.where(low, -1.0, 1.0) * float(sign)
    half = math.sqrt(0.5)
    turn_half = turn * half
    columns = [[None] * 8 for _ in range(3)]
    for n2 in range(8):
        x0, x1, x2 = (x[(8 * n1 + 3 * n2) % 24] for n1 in range(3))
        total = x1 + x2
        base = x0 - 0.5 * total
        spin = swap(x1 - x2) * root3
        columns[0][n2] = x0 + total
        columns[1][n2] = base + spin
        columns[2][n2] = base - spin
    out = [None] * 24
    for k1 in range(3):
        c = columns[k1]
        a0, a1 = c[0] + c[4], c[0] - c[4]
        a2, a3 = c[2] + c[6], c[2] - c[6]
        a4, a5 = c[1] + c[5], c[1] - c[5]
        a6, a7 = c[3] + c[7], c[3] - c[7]
        b0, b1 = a0 + a2, a0 - a2
        b2, b3 = a4 + a6, a4 - a6
        i_a3 = swap(a3) * turn
        i_b3 = swap(b3) * turn
        c0, c1 = a1 + i_a3, a1 - i_a3
        p = (a5 - a7) * half
        m = swap(a5 + a7) * turn_half
        e, f = p + m, p - m
        values = [b0 + b2, c0 + e, b1 + i_b3, c1 - f, b0 - b2, c0 - e, b1 - i_b3, c1 + f]
        for k2 in range(8):
            out[(16 * k1 + 9 * k2) % 24] = values[k2]
    return out


def line_of(place, step, ref, count):
    lines = ref.shape[0] // (TILE * SIDE)
    return partner_of(place, step, count) * lines if count > 1 else 0


def load_line(ref, line):
    stride = ref.shape[0] // TILE
    return [ref[pl.ds(line * SIDE + k2, TILE, stride=stride), :] for k2 in range(SIDE)]


def fetch(place, order, block_refs, held_ref, sems):
    copies = [None] * len(block_refs)
    for step in order:
        source = block_refs[step]
        rows = held_ref.shape[1]
        if step == 0 and len(order) > 1:
            source = source.at[pl.ds(pl.multiple_of(place * rows, TILE), rows)]
        copies[step] = pltpu.make_async_copy(source, held_ref.at[step], sems.at[step])
        copies[step].start()
    return copies


def along_first(work_ref, sign, low, out_ref):
    def columns(pair, carry):
        for column in (2 * pair, 2 * pair + 1):
            rows = [work_ref[k1 * SIDE + column] for k1 in range(SIDE)]
            for r1, value in enumerate(dft24(rows, sign, low)):
                out_ref[r1 * SIDE + column] = value
        return carry

    lax.fori_loop(0, SIDE // 2, columns, 0)


def forward_kernel(order, place_ref, *refs):
    count = len(order)
    block_refs, (lattice_ref, work_ref, held_ref, sems) = refs[:count], refs[count:]
    low = lane_sign((TILE, WIDTH))
    place = place_ref[0]
    copies = fetch(place, order, block_refs, held_ref, sems)
    for step in order:
        copies[step].wait()
        green_ref = held_ref.at[step]
        first = line_of(place, step, green_ref, count)
        lines = green_ref.shape[0] // (TILE * SIDE)

        def along_second(i, carry):
            for r2, value in enumerate(dft24(load_line(green_ref, i), -1, low)):
                work_ref[(first + i) * SIDE + r2] = value
            return carry

        lax.fori_loop(0, lines, along_second, 0, unroll=lines <= 4)
    along_first(work_ref, -1, low, lattice_ref)


def backward_kernel(order, share, place_ref, lattice_ref, weight_ref, equal_ref, sign_ref, gather_ref, *refs):
    count = len(order)
    screen_refs, green_refs, partial_refs = refs[:count], refs[count : 2 * count], refs[2 * count : -7]
    work_ref, sigma_ref, sums_ref, screen_held, green_held, screen_sems, green_sems = refs[-7:]
    points = SIDE * SIDE
    low = lane_sign((TILE, WIDTH))
    turn = jnp.where(low, -1.0, 1.0)
    weights = weight_ref[...]
    place = place_ref[0]
    screen_copies = fetch(place, order, screen_refs, screen_held, screen_sems)
    green_copies = fetch(place, order, green_refs, green_held, green_sems)

    for step in order:
        screen_copies[step].wait()
        screen_ref = screen_held.at[step]
        first = line_of(place, step, screen_ref, count)
        lines = screen_ref.shape[0] // (TILE * SIDE)

        def along_second(i, carry):
            rows = []
            for r2, value in enumerate(load_line(screen_ref, i)):
                screen = value * weights
                other = swap(screen)
                lattice = lattice_ref[(first + i) * SIDE + r2]
                rows.append(
                    swap(lattice) * turn * jnp.where(low, screen, other)
                    - lattice * jnp.where(low, other, screen)
                )
            for k2, value in enumerate(dft24(rows, 1, low)):
                work_ref[(first + i) * SIDE + k2] = value
            return carry

        lax.fori_loop(0, lines, along_second, 0, unroll=lines <= 4)
    sigma_at = sigma_ref.reshape(points, TILE, WIDTH)
    along_first(work_ref, 1, low, sigma_at)

    for step in order:
        green_copies[step].wait()
        green_ref = green_held.at[step]
        first = line_of(place, step, green_ref, count) * SIDE
        block = green_ref.shape[0] // TILE
        tiles = block // TILE
        batch = max(n for n in (1, 2, 3) if tiles % n == 0)

        def contract(group, carry):
            values = []
            for tile in range(batch):
                tile = group * batch + tile
                start = (first + tile * TILE) * TILE
                sums = [None] * (STEPS * STEPS)
                for s in range(TILE):
                    sigma = sigma_ref[pl.ds(start + s, TILE, stride=TILE), :]
                    green = green_ref[pl.ds(pl.multiple_of(s * block + tile * TILE, TILE), TILE), :]
                    sigmas = [roll_blocks(sigma, STEPS * i) for i in range(STEPS)]
                    greens = [roll_blocks(green, j) for j in range(STEPS)]
                    for i in range(STEPS):
                        for j in range(STEPS):
                            term = sigmas[i] * greens[j]
                            spot = STEPS * i + j
                            sums[spot] = term if s == 0 else sums[spot] + term
                values.append((pl.ds(pl.multiple_of(step * block + tile * TILE, TILE), TILE), sums))
            for row, sums in values:
                for spot, value in enumerate(sums):
                    sums_ref[row, spot * WIDTH : (spot + 1) * WIDTH] = value
            return carry

        lax.fori_loop(0, tiles // batch, contract, 0)

    lane = lax.broadcasted_iota(jnp.int32, equal_ref.shape, 1)
    inner = lane - ENTRIES
    occupied = jnp.sum(jnp.where((inner >= 0) & (inner % (BANDS + 1) == 0), equal_ref[...], 0.0))
    spots = lax.broadcasted_iota(jnp.int32, (points, WIDTH), 1)
    on_diagonal = (spots < ENTRIES) & (spots % (BANDS + 1) == 0)
    total = jnp.where(on_diagonal, occupied * share, 0.0)
    lower = spots < ENTRIES
    for pair in range(STEPS * STEPS // 2):
        first_part = sums_ref[:, 2 * pair * WIDTH : (2 * pair + 1) * WIDTH]
        second_part = sums_ref[:, (2 * pair + 1) * WIDTH : (2 * pair + 2) * WIDTH]
        folded = jnp.where(lower, first_part, second_part) + sign_ref[pair : pair + 1, :] * swap(
            jnp.where(lower, second_part, first_part)
        )
        coarse = folded.astype(jnp.bfloat16)
        fine = (folded - coarse.astype(jnp.float32)).astype(jnp.bfloat16)
        gather = gather_ref[2 * pair * WIDTH : (2 * pair + 2) * WIDTH, :]
        both = jnp.concatenate([coarse, fine], axis=1)
        total = total + jnp.dot(both, gather, preferred_element_type=jnp.float32)
    parts = len(partial_refs)
    local = points // parts
    if count == parts:
        for step, partial_ref in enumerate(partial_refs):
            partial_ref[...] = total[step * local : (step + 1) * local]
    else:
        sigma_ref[:points, :] = total
        for step, partial_ref in enumerate(partial_refs):
            owner = partner_of(place, step, parts)
            partial_ref[...] = sigma_ref[pl.ds(owner * local, local), :]


def propagate_kernel(green_ref, effective_ref, spread_ref, out_ref, factor_ref):
    history, points, _ = green_ref.shape

    @pl.when(pl.program_id(0) == 0)
    def _():
        rest = effective_ref[...] * time_step
        pieces = []
        for _ in range(3):
            pieces.append(rest.astype(jnp.bfloat16).astype(jnp.float32))
            rest = rest - pieces[-1]
        stacked = jnp.concatenate(pieces, axis=0).astype(jnp.bfloat16)
        spread = jnp.dot(stacked, spread_ref[...], preferred_element_type=jnp.float32)
        factor_ref[...] = tree_sum([spread[n * points : (n + 1) * points] for n in range(3)])

    def advance(start, stop):
        green = green_ref[:, start:stop, :]
        greens = [roll_blocks(green, j) for j in range(STEPS)]
        terms = [green]
        for i in range(STEPS):
            total = None
            for j in range(STEPS):
                spot = STEPS * i + j
                factor = factor_ref[start:stop, spot * WIDTH : (spot + 1) * WIDTH]
                term = factor[None] * greens[j]
                total = term if total is None else total + term
            terms.append(roll_blocks(total, STEPS * i))
        out_ref[:, start:stop, :] = tree_sum(terms)

    for start in range(0, points, 2 * TILE):
        advance(start, min(start + 2 * TILE, points))


def gather_tables():
    blocks = 2 * BANDS
    pairs = STEPS * STEPS // 2
    table = np.zeros((pairs, 2, blocks, BANDS, 2, BANDS, BANDS), np.float32)
    signs = np.zeros((pairs, blocks, BANDS), np.float32)
    for pair in range(pairs):
        for p in range(blocks):
            i, j = divmod(2 * pair + p // BANDS, STEPS)
            h, a = divmod((p + STEPS * i) % blocks, BANDS)
            g, c = divmod((p + j) % blocks, BANDS)
            table[pair, :, p, :, h ^ g, a, c] = 1 if (h, g) == (0, 1) else -1
            signs[pair, p] = 1 if h == g else -1
    return signs.reshape(pairs, WIDTH), table.reshape(-1, WIDTH).astype(ml_dtypes.bfloat16)


def spread_table():
    blocks = 2 * BANDS
    table = np.zeros((2, BANDS, BANDS, STEPS, STEPS, blocks, BANDS), np.float32)
    for i in range(STEPS):
        for j in range(STEPS):
            for p in range(blocks):
                h, a = divmod((p - STEPS * i) % blocks, BANDS)
                g, b = divmod((p + j) % blocks, BANDS)
                table[1 if h == g else 0, a, b, i, j, p, :] = -1 if (h, g) == (1, 0) else 1
    return table.reshape(WIDTH, -1).astype(ml_dtypes.bfloat16)


def forward(place, greens, order):
    points = SIDE * SIDE
    count = len(greens)
    whole = pl.BlockSpec(memory_space=pltpu.VMEM)
    return pl.pallas_call(
        functools.partial(forward_kernel, order),
        out_shape=jax.ShapeDtypeStruct((points, TILE, WIDTH), jnp.float32),
        in_specs=[pl.BlockSpec(memory_space=pltpu.SMEM)] + [pl.BlockSpec(memory_space=pl.ANY)] * count,
        out_specs=whole,
        scratch_shapes=[
            pltpu.VMEM((points, TILE, WIDTH), jnp.float32),
            pltpu.VMEM((count, TILE * points // count, WIDTH), jnp.float32),
            pltpu.SemaphoreType.DMA((count,)),
        ],
        compiler_params=pltpu.CompilerParams(vmem_limit_bytes=VMEM_LIMIT),
        cost_estimate=pl.CostEstimate(
            flops=400 * points * TILE * WIDTH, bytes_accessed=8 * points * TILE * WIDTH, transcendentals=0
        ),
        name="forward",
    )(place, *greens)


def backward(place, lattice, screens, greens, weights, equal_time, order, share, parts):
    points = SIDE * SIDE
    count = len(greens)
    whole = pl.BlockSpec(memory_space=pltpu.VMEM)
    signs, gather = gather_tables()
    held = pltpu.VMEM((count, TILE * points // count, WIDTH), jnp.float32)
    return pl.pallas_call(
        functools.partial(backward_kernel, order, share),
        out_shape=[jax.ShapeDtypeStruct((points // parts, WIDTH), jnp.float32)] * parts,
        in_specs=[pl.BlockSpec(memory_space=pltpu.SMEM)]
        + [whole] * 5
        + [pl.BlockSpec(memory_space=pl.ANY)] * (2 * count),
        out_specs=[whole] * parts,
        scratch_shapes=[
            pltpu.VMEM((points, TILE, WIDTH), jnp.float32),
            pltpu.VMEM((TILE * points, WIDTH), jnp.float32),
            pltpu.VMEM((points, STEPS * STEPS * WIDTH), jnp.float32),
            held,
            held,
            pltpu.SemaphoreType.DMA((count,)),
            pltpu.SemaphoreType.DMA((count,)),
        ],
        compiler_params=pltpu.CompilerParams(vmem_limit_bytes=VMEM_LIMIT),
        cost_estimate=pl.CostEstimate(
            flops=800 * points * TILE * WIDTH, bytes_accessed=12 * points * TILE * WIDTH, transcendentals=0
        ),
        name="backward",
    )(place, lattice, weights, equal_time, jnp.asarray(signs), jnp.asarray(gather), *screens, *greens)


def propagate(greens, effective):
    history, points, width = greens.shape
    step = math.gcd(history, TILE)
    chunk = pl.BlockSpec((step, points, width), lambda i: (i, 0, 0))
    spread = spread_table()
    return pl.pallas_call(
        propagate_kernel,
        grid=(history // step,),
        out_shape=jax.ShapeDtypeStruct(greens.shape, jnp.float32),
        in_specs=[
            chunk,
            pl.BlockSpec((points, width), lambda i: (0, 0)),
            pl.BlockSpec(spread.shape, lambda i: (0, 0)),
        ],
        out_specs=chunk,
        scratch_shapes=[pltpu.VMEM((points, spread.shape[1]), jnp.float32)],
        compiler_params=pltpu.CompilerParams(vmem_limit_bytes=VMEM_LIMIT),
        cost_estimate=pl.CostEstimate(
            flops=32 * greens.size, bytes_accessed=8 * greens.size, transcendentals=0
        ),
        name="propagate",
    )(greens, effective, jnp.asarray(spread))


def partner_of(place, step, count):
    if count & (count - 1) == 0:
        return place ^ step
    return (place + step) % count


def exchange(value, axis, step, count):
    pairs = [(place, partner_of(place, step, count)) for place in range(count)]
    return lax.ppermute(value, axis, pairs)


def exchange_order(count):
    along = {}
    for step in range(1, count):
        along.setdefault(step // 2, []).append(step)
    single = [along[n] for n in along if n and n & (n - 1) == 0]
    mixed = [along[n] for n in along if n & (n - 1)]
    order = [step for steps in zip(*single) for step in steps]
    order += [step for steps in mixed for step in steps]
    return order + along[0]


def class_weights(quad_class):
    table = jnp.array(quadrature, jnp.float32)
    match = quad_class[:, None] == jnp.arange(4, dtype=jnp.int32)[None, :]
    return jnp.sum(jnp.where(match, table[None, :], jnp.float32(0.0)), axis=1)


def per_device(parts, blocks, green_row, screened, hamilton, equal_time, quad_class, live_count):
    history, local, width = green_row.shape
    points = local * parts
    times = history // parts
    place = lax.axis_index("ka")
    position = jnp.arange(history, dtype=jnp.int32)
    weights = jnp.where(
        position < live_count[0], time_step * class_weights(quad_class), jnp.float32(0.0)
    ) * jnp.float32(1.0 / points)
    weights = lax.dynamic_slice_in_dim(weights, place * times, times)

    if times == TILE and local % SIDE == 0:
        groups = 1
        order = exchange_order(parts)
        wholes = [x.reshape(parts * TILE * local, width) for x in (green_row, screened)]
        received = []
        for whole in wholes:
            for step in order:
                start = partner_of(place, step, parts) * (TILE * local)
                block = lax.dynamic_slice_in_dim(whole, start, TILE * local)
                if len(received) >= IN_FLIGHT:
                    block, _ = lax.optimization_barrier((block, received[-IN_FLIGHT]))
                received.append(exchange(block, "ka", step, parts))
        moved = []
        for n, whole in enumerate(wholes):
            found = dict(zip(order, received[n * (parts - 1) :]))
            moved.append([[whole] + [found[step] for step in range(1, parts)]])
        order = order + [0]
    else:
        groups = -(-times // TILE)
        order = [0]
        padding = groups * TILE - times
        moved = []
        for x in (green_row, screened):
            x = lax.all_to_all(x, "ka", split_axis=0, concat_axis=0, tiled=True)
            x = x.reshape(parts, times, local, width).transpose(1, 0, 2, 3).reshape(times, points, width)
            x = jnp.pad(x, ((0, padding), (0, 0), (0, 0))).reshape(groups, TILE * points, width)
            moved.append([[x[group]] for group in range(groups)])
        weights = jnp.pad(weights, (0, padding))
    weights = jnp.broadcast_to(weights.reshape(groups, TILE, 1), (groups, TILE, width))

    pieces = None
    for group in range(groups):
        green, screen = moved[0][group], moved[1][group]
        lattice = forward(place.reshape(1), green, order)
        share = hubbard / (points * blocks) if group == 0 else 0.0
        terms = backward(
            place.reshape(1), lattice, screen, green, weights[group], equal_time, order, share, parts
        )
        pieces = list(terms) if pieces is None else [a + b for a, b in zip(pieces, terms)]

    if parts % 2 == 0 and parts & (parts - 1) == 0:
        pairs = jnp.concatenate([pieces[step] for step in range(1, parts, 2)], axis=0)
        pairs = exchange(pairs, "ka", 1, parts)
        mine = jnp.concatenate([pieces[step] for step in range(0, parts, 2)], axis=0) + pairs
        pieces = [mine[n * local : (n + 1) * local] for n in range(parts // 2)]
        partial_value = tree_sum(
            pieces[:1] + [exchange(pieces[n], "ka", 2 * n, parts) for n in range(1, parts // 2)]
        )
    else:
        partial_value = tree_sum(
            pieces[:1] + [exchange(pieces[step], "ka", step, parts) for step in range(1, parts)]
        )
    collision = tree_sum(
        [partial_value] + [exchange(partial_value, "hist", step, blocks) for step in range(1, blocks)]
    )
    return propagate(green_row, hamilton + collision)


def solution(mesh):
    in_specs = (
        P("hist", "ka", None),
        P("hist", "ka", None),
        P("ka", None),
        P("ka", None),
        P("hist"),
        P("hist"),
    )
    out_specs = P("hist", "ka", None)
    return jax.shard_map(
        functools.partial(per_device, mesh.shape["ka"], mesh.shape["hist"]),
        mesh=mesh,
        in_specs=in_specs,
        out_specs=out_specs,
        check_vma=False,
    )
```

profile of v0, /device:TPU:0, one launch (start us, length us, event | category | flops | bytes accessed | tf_op | source)
XLA Modules:
  0.0 99.7 jit_solution(14582693732157736981)
XLA Ops:
  0.0 1.8 %constant_dynamic-slice_fusion.7 = (f32[576,128]{1,0:T(8,128)S(1)}, f32[576,128]{1,0:T(8,128)S(1)}, f32[576,128]{1,0:T(8,128)S(1)}, f32[576,128]{1,0:T(8,128)S(1...) fusion(f32[4608,128]{1,0:T(8,128)} %bitcast.5, s32[]{:T(128)S(6)} %select_n.45, ...), kind=kLoop, calls=%fused_computation.12 | loop fusion | bytes 4128796 | tf_op jit(solution)/shard_map/dynamic_slice | solution.py:417
  1.8 0.0 copy-start.8
  1.8 0.0 copy-start.9
  1.8 2.5 %collective-permute-start.4 = (f32[576,128]{1,0:T(8,128)S(1)}, f32[576,128]{1,0:T(8,128)S(1)}, u32[]{:S(2)}, u32[]{:S(2)}) collective-permute-start(f32[576,128]{1,0:T(8,128)S(1)} %get-tuple-element.48), channel_id=1, source_target_pairs={{0,20},{4,16},{8,28},{12,24},{16,4},{20,0},{24,12},{28,8},{1,21},{... | collective-permute-start | bytes 884744 | tf_op jit(solution)/shard_map/ppermute | solution.py:378
  4.3 1.8 %collective-permute-start.3 = (f32[576,128]{1,0:T(8,128)S(1)}, f32[576,128]{1,0:T(8,128)S(1)}, u32[]{:S(2)}, u32[]{:S(2)}) collective-permute-start(f32[576,128]{1,0:T(8,128)S(1)} %get-tuple-element.49), channel_id=1, source_target_pairs={{0,12},{4,8},{8,4},{12,0},{16,28},{20,24},{24,20},{28,16},{1,13},{... | collective-permute-start | bytes 884744 | tf_op jit(solution)/shard_map/ppermute | solution.py:378
  6.1 0.5 collective-permute-start.2
  6.6 0.0 collective-permute-start
  6.6 3.0 %collective-permute-start.5 = (f32[576,128]{1,0:T(8,128)S(1)}, f32[576,128]{1,0:T(8,128)S(1)}, u32[]{:S(2)}, u32[]{:S(2)}) collective-permute-start(f32[576,128]{1,0:T(8,128)S(1)} %get-tuple-element.47), channel_id=1, source_target_pairs={{0,24},{4,28},{8,16},{12,20},{16,8},{20,12},{24,0},{28,4},{1,25},{... | collective-permute-start | bytes 884744 | tf_op jit(solution)/shard_map/ppermute | solution.py:378
  9.6 1.2 %constant_dynamic-slice_fusion = (f32[576,128]{1,0:T(8,128)}, f32[576,128]{1,0:T(8,128)}, f32[576,128]{1,0:T(8,128)}, f32[576,128]{1,0:T(8,128)}, f32[576,128]{1...) fusion(f32[4608,128]{1,0:T(8,128)S(1)} %bitcast.9, s32[]{:T(128)S(6)} %select_n.45, s32[]{:T(128)S(6)} %select_n.44, ...), kind=kLoop, calls=%fused_computation.5 | loop fusion | bytes 4128796 | tf_op jit(solution)/shard_map/dynamic_slice | solution.py:417
  10.7 1.0 collective-permute-done.4.refs_5_.refs_13_
  11.7 2.5 %collective-permute-start.7 = (f32[576,128]{1,0:T(8,128)S(1)}, f32[576,128]{1,0:T(8,128)S(1)}, u32[]{:S(2)}, u32[]{:S(2)}) collective-permute-start(f32[576,128]{1,0:T(8,128)S(1)} %get-tuple-element.24), channel_id=1, source_target_pairs={{0,16},{4,20},{8,24},{12,28},{16,0},{20,4},{24,8},{28,12},{1,17},{... | collective-permute-start | bytes 884744 | tf_op jit(solution)/shard_map/ppermute | solution.py:378
  14.2 1.5 %collective-permute-start.9 = (f32[576,128]{1,0:T(8,128)S(1)}, f32[576,128]{1,0:T(8,128)S(1)}, u32[]{:S(2)}, u32[]{:S(2)}) collective-permute-start(f32[576,128]{1,0:T(8,128)S(1)} %get-tuple-element.26), channel_id=1, source_target_pairs={{0,8},{4,12},{8,0},{12,4},{16,24},{20,28},{24,16},{28,20},{1,9},{5... | collective-permute-start | bytes 884744 | tf_op jit(solution)/shard_map/ppermute | solution.py:378
  15.7 5.1 %collective-permute-done.2.refs_2_.refs_10_ = f32[576,128]{1,0:T(8,128)S(1)} collective-permute-done((f32[576,128]{1,0:T(8,128)S(1)}, f32[576,128]{1,0:T(8,128)S(1)}, u32[]{:S(2)}, u32[]{:S(2)}) %collective-permute-start.2) | collective-permute-done | bytes 294944 | tf_op jit(solution)/shard_map/ppermute | solution.py:378
  20.8 0.0 collective-permute-done.refs_4_.refs_12_
  20.8 1.5 %collective-permute-start.1 = (f32[576,128]{1,0:T(8,128)S(1)}, f32[576,128]{1,0:T(8,128)S(1)}, u32[]{:S(2)}, u32[]{:S(2)}) collective-permute-start(f32[576,128]{1,0:T(8,128)S(1)} %get-tuple-element.22), channel_id=1, source_target_pairs={{0,4},{4,0},{8,12},{12,8},{16,20},{20,16},{24,28},{28,24},{1,5},{5... | collective-permute-start | bytes 884744 | tf_op jit(solution)/shard_map/ppermute | solution.py:378
  22.3 4.1 %collective-permute-done.5.refs_6_.refs_14_ = f32[576,128]{1,0:T(8,128)S(1)} collective-permute-done((f32[576,128]{1,0:T(8,128)S(1)}, f32[576,128]{1,0:T(8,128)S(1)}, u32[]{:S(2)}, u32[]{:S(2)}) %collective-permute-start.5) | collective-permute-done | bytes 294944 | tf_op jit(solution)/shard_map/ppermute | solution.py:378
  26.4 0.5 collective-permute-start.10
  26.9 3.9 %collective-permute-done.7.refs_4_ = f32[576,128]{1,0:T(8,128)S(1)} collective-permute-done((f32[576,128]{1,0:T(8,128)S(1)}, f32[576,128]{1,0:T(8,128)S(1)}, u32[]{:S(2)}, u32[]{:S(2)}) %collective-permute-start.7) | collective-permute-done | bytes 294944 | tf_op jit(solution)/shard_map/ppermute | solution.py:378
  30.8 2.6 %collective-permute-done.9.refs_2_ = f32[576,128]{1,0:T(8,128)S(1)} collective-permute-done((f32[576,128]{1,0:T(8,128)S(1)}, f32[576,128]{1,0:T(8,128)S(1)}, u32[]{:S(2)}, u32[]{:S(2)}) %collective-permute-start.9) | collective-permute-done | bytes 294944 | tf_op jit(solution)/shard_map/ppermute | solution.py:378
  33.4 0.7 collective-permute-start.13
  34.2 4.8 %collective-permute-done.6.refs_7_.refs_15_ = f32[576,128]{1,0:T(8,128)S(1)} collective-permute-done((f32[576,128]{1,0:T(8,128)S(1)}, f32[576,128]{1,0:T(8,128)S(1)}, u32[]{:S(2)}, u32[]{:S(2)}) %collective-permute-start.6) | collective-permute-done | bytes 294944 | tf_op jit(solution)/shard_map/ppermute | solution.py:378
  39.0 1.7 %collective-permute-start.11 = (f32[576,128]{1,0:T(8,128)}, f32[576,128]{1,0:T(8,128)}, u32[]{:S(2)}, u32[]{:S(2)}) collective-permute-start(f32[576,128]{1,0:T(8,128)} %get-tuple-element.28), channel_id=1, source_target_pairs={{0,20},{4,16},{8,28},{12,24},{16,4},{20,0},{24,12},{28,8},{1,21},{... | collective-permute-start | bytes 884744 | tf_op jit(solution)/shard_map/ppermute | solution.py:378
  40.6 0.0 collective-permute-done.1.refs_1_.refs_9_
  40.7 1.4 %collective-permute-start.12 = (f32[576,128]{1,0:T(8,128)}, f32[576,128]{1,0:T(8,128)}, u32[]{:S(2)}, u32[]{:S(2)}) collective-permute-start(f32[576,128]{1,0:T(8,128)} %get-tuple-element.29), channel_id=1, source_target_pairs={{0,24},{4,28},{8,16},{12,20},{16,8},{20,12},{24,0},{28,4},{1,25},{... | collective-permute-start | bytes 884744 | tf_op jit(solution)/shard_map/ppermute | solution.py:378
  42.1 0.1 select_reduce_fusion
  42.8 0.1 dynamic_slice.52
  42.9 3.9 %forward.1.lattice_ref = f32[576,8,128]{2,1,0:T(8,128)S(1)} custom-call(s32[1]{0:T(128)} %bitcast.place_ref, f32[4608,128]{1,0:T(8,128)} %bitcast.6, f32[576,128]{1,0:T(8,128)S(1)} %collective-permute-done.1.refs_1_.refs_9_, f32[576,128]{1,0:T(8,128)S(1)} %collective-permute-done.2.refs_2_.refs_10_, f32[576,128]{1,0:T(8,128)S(1)} %collective-permute-done.3.refs_3_.refs_11_, ...), custom_call_target="tpu_custom_call" | custom-call | flops 235929600 | bytes 4718592 | tf_op jit(solution)/shard_map/forward/pallas_call | solution.py:298
  46.8 0.0 copy-start.1
  46.8 1.4 %copy-done.1 = f32[576,8,128]{2,1,0:T(8,128)} copy-done((f32[576,8,128]{2,1,0:T(8,128)}, f32[576,8,128]{2,1,0:T(8,128)S(1)}, u32[]{:S(2)}) %copy-start.1) | copy-done | bytes 2359320
  48.2 3.5 %collective-permute-done.13.refs_7_ = f32[576,128]{1,0:T(8,128)S(1)} collective-permute-done((f32[576,128]{1,0:T(8,128)}, f32[576,128]{1,0:T(8,128)S(1)}, u32[]{:S(2)}, u32[]{:S(2)}) %collective-permute-start.13) | collective-permute-done | bytes 294944 | tf_op jit(solution)/shard_map/ppermute | solution.py:378
  51.7 9.2 %collective-permute-done.11.refs_5_ = f32[576,128]{1,0:T(8,128)} collective-permute-done((f32[576,128]{1,0:T(8,128)}, f32[576,128]{1,0:T(8,128)}, u32[]{:S(2)}, u32[]{:S(2)}) %collective-permute-start.11) | collective-permute-done | bytes 294944 | tf_op jit(solution)/shard_map/ppermute | solution.py:378
  60.9 0.1 squeeze.7.weight_ref
  61.0 0.0 copy-start
  61.0 0.0 copy-start.2
  61.0 14.2 %backward.1 = (f32[72,128]{1,0:T(8,128)S(1)}, f32[72,128]{1,0:T(8,128)S(1)}, f32[72,128]{1,0:T(8,128)S(1)}, f32[72,128]{1,0:T(8,128)S(1)}, f32[72,128]{1,0:T(8,1...) custom-call(s32[1]{0:T(128)} %bitcast.place_ref, f32[576,8,128]{2,1,0:T(8,128)} %copy-done.1, ...), custom_call_target="tpu_custom_call" | custom-call | flops 471859200 | bytes 7077888 | tf_op jit(solution)/shard_map/backward/pallas_call | solution.py:322
  75.3 0.2 collective-permute-start.14
  75.5 1.3 %collective-permute-done.14 = f32[288,128]{1,0:T(8,128)S(1)} collective-permute-done((f32[288,128]{1,0:T(8,128)S(1)}, f32[288,128]{1,0:T(8,128)S(1)}, u32[]{:S(2)}, u32[]{:S(2)}) %collective-permute-start.14) | collective-permute-done | bytes 147488 | tf_op jit(solution)/shard_map/ppermute | solution.py:378
  76.7 1.4 %collective-permute-start.17 = (f32[72,128]{1,0:T(8,128)S(1)}, f32[72,128]{1,0:T(8,128)S(1)}, u32[]{:S(2)}, u32[]{:S(2)}) collective-permute-start(f32[72,128]{1,0:T(8,128)S(1)} %get-tuple-element.53), channel_id=1, source_target_pairs={{0,24},{4,28},{8,16},{12,20},{16,8},{20,12},{24,0},{28,4},{1,25},{... | collective-permute-start | bytes 110600 | tf_op jit(solution)/shard_map/ppermute | solution.py:378
  78.1 1.4 %collective-permute-start.16 = (f32[72,128]{1,0:T(8,128)S(1)}, f32[72,128]{1,0:T(8,128)S(1)}, u32[]{:S(2)}, u32[]{:S(2)}) collective-permute-start(f32[72,128]{1,0:T(8,128)S(1)} %get-tuple-element.54), channel_id=1, source_target_pairs={{0,16},{4,20},{8,24},{12,28},{16,0},{20,4},{24,8},{28,12},{1,17},{... | collective-permute-start | bytes 110600 | tf_op jit(solution)/shard_map/ppermute | solution.py:378
  79.5 0.8 collective-permute-start.15
  80.3 1.4 %collective-permute-done.17 = f32[72,128]{1,0:T(8,128)S(1)} collective-permute-done((f32[72,128]{1,0:T(8,128)S(1)}, f32[72,128]{1,0:T(8,128)S(1)}, u32[]{:S(2)}, u32[]{:S(2)}) %collective-permute-start.17) | collective-permute-done | bytes 36896 | tf_op jit(solution)/shard_map/ppermute | solution.py:378
  81.7 0.4 collective-permute-done.16
  82.1 1.4 %collective-permute-done.15 = f32[72,128]{1,0:T(8,128)S(1)} collective-permute-done((f32[72,128]{1,0:T(8,128)S(1)}, f32[72,128]{1,0:T(8,128)S(1)}, u32[]{:S(2)}, u32[]{:S(2)}) %collective-permute-start.15) | collective-permute-done | bytes 36896 | tf_op jit(solution)/shard_map/ppermute | solution.py:378
  83.5 3.7 %collective-permute-start.20 = (f32[72,128]{1,0:T(8,128)S(1)}, f32[72,128]{1,0:T(8,128)S(1)}, u32[]{:S(2)}, u32[]{:S(2)}) collective-permute-start(f32[72,128]{1,0:T(8,128)S(1)} %fusion), channel_id=1, source_target_pairs={{0,3},{1,2},{2,1},{3,0},{4,7},{5,6},{6,5},{7,4},{8,11},{9,10},{10,... | collective-permute-start | bytes 110600 | tf_op jit(solution)/shard_map/ppermute | solution.py:378
  87.1 0.8 collective-permute-start.18
  87.9 1.4 %collective-permute-done.20 = f32[72,128]{1,0:T(8,128)S(1)} collective-permute-done((f32[72,128]{1,0:T(8,128)S(1)}, f32[72,128]{1,0:T(8,128)S(1)}, u32[]{:S(2)}, u32[]{:S(2)}) %collective-permute-start.20) | collective-permute-done | bytes 36896 | tf_op jit(solution)/shard_map/ppermute | solution.py:378
  89.3 2.7 %collective-permute-done.19 = f32[72,128]{1,0:T(8,128)S(1)} collective-permute-done((f32[72,128]{1,0:T(8,128)S(1)}, f32[72,128]{1,0:T(8,128)S(1)}, u32[]{:S(2)}, u32[]{:S(2)}) %collective-permute-start.19) | collective-permute-done | bytes 36896 | tf_op jit(solution)/shard_map/ppermute | solution.py:378
  92.0 7.7 %propagate.1 = f32[64,72,128]{2,1,0:T(8,128)} custom-call(f32[64,72,128]{2,1,0:T(8,128)S(1)} %copy-done, f32[72,128]{1,0:T(8,128)S(1)} %add_add_fusion.effective_ref, bf16[128,2048]{1,0:T(8,128)(2,1)S(1)} %copy-done.2), custom_call_target="tpu_custom_call" | custom-call | flops 18874368 | bytes 4718592 | tf_op jit(solution)/shard_map/propagate/pallas_call | solution.py:351
  (28 shorter events, 0.1 us)
Async XLA Ops:
  0.0 9.6 %copy-start.6 = (f32[64,72,128]{2,1,0:T(8,128)S(1)}, f32[64,72,128]{2,1,0:T(8,128)}, u32[]{:S(2)}) copy-start(f32[64,72,128]{2,1,0:T(8,128)} %param.11) | copy-start | bytes 7077892
  1.8 40.3 %copy-start.8 = (s32[64]{0:T(128)S(1)}, s32[64]{0:T(128)}, u32[]{:S(2)}) copy-start(s32[64]{0:T(128)} %param.14) | copy-start | bytes 772
  1.8 40.3 %copy-start.9 = (f32[4]{0:T(128)S(1)}, f32[4]{0:T(128)}, u32[]{:S(2)}) copy-start(f32[4]{0:T(128)} %constant.44.clone) | copy-start | bytes 52
  1.8 9.9 %collective-permute-start.4 = (f32[576,128]{1,0:T(8,128)S(1)}, f32[576,128]{1,0:T(8,128)S(1)}, u32[]{:S(2)}, u32[]{:S(2)}) collective-permute-start(f32[576,128]{1,0:T(8,128)S(1)} %get-tuple-element.48), channel_id=1, source_target_pairs={{0,20},{4,16},{8,28},{12,24},{16,4},{20,0},{24,12},{28,8},{1,21},{... | collective-permute-start | bytes 884744 | tf_op jit(solution)/shard_map/ppermute | solution.py:378
  4.3 9.9 %collective-permute-start.3 = (f32[576,128]{1,0:T(8,128)S(1)}, f32[576,128]{1,0:T(8,128)S(1)}, u32[]{:S(2)}, u32[]{:S(2)}) collective-permute-start(f32[576,128]{1,0:T(8,128)S(1)} %get-tuple-element.49), channel_id=1, source_target_pairs={{0,12},{4,8},{8,4},{12,0},{16,28},{20,24},{24,20},{28,16},{1,13},{... | collective-permute-start | bytes 884744 | tf_op jit(solution)/shard_map/ppermute | solution.py:378
  6.1 14.7 %collective-permute-start.2 = (f32[576,128]{1,0:T(8,128)S(1)}, f32[576,128]{1,0:T(8,128)S(1)}, u32[]{:S(2)}, u32[]{:S(2)}) collective-permute-start(f32[576,128]{1,0:T(8,128)S(1)} %get-tuple-element.50), channel_id=1, source_target_pairs={{0,8},{4,12},{8,0},{12,4},{16,24},{20,28},{24,16},{28,20},{1,9},{5... | collective-permute-start | bytes 884744 | tf_op jit(solution)/shard_map/ppermute | solution.py:378
  6.6 14.2 %collective-permute-start = (f32[576,128]{1,0:T(8,128)S(1)}, f32[576,128]{1,0:T(8,128)S(1)}, u32[]{:S(2)}, u32[]{:S(2)}) collective-permute-start(f32[576,128]{1,0:T(8,128)S(1)} %get-tuple-element.51), channel_id=1, source_target_pairs={{0,16},{4,20},{8,24},{12,28},{16,0},{20,4},{24,8},{28,12},{1,17},{... | collective-permute-start | bytes 884744 | tf_op jit(solution)/shard_map/ppermute | solution.py:378
  6.6 19.8 %collective-permute-start.5 = (f32[576,128]{1,0:T(8,128)S(1)}, f32[576,128]{1,0:T(8,128)S(1)}, u32[]{:S(2)}, u32[]{:S(2)}) collective-permute-start(f32[576,128]{1,0:T(8,128)S(1)} %get-tuple-element.47), channel_id=1, source_target_pairs={{0,24},{4,28},{8,16},{12,20},{16,8},{20,12},{24,0},{28,4},{1,25},{... | collective-permute-start | bytes 884744 | tf_op jit(solution)/shard_map/ppermute | solution.py:378
  11.7 19.1 %collective-permute-start.7 = (f32[576,128]{1,0:T(8,128)S(1)}, f32[576,128]{1,0:T(8,128)S(1)}, u32[]{:S(2)}, u32[]{:S(2)}) collective-permute-start(f32[576,128]{1,0:T(8,128)S(1)} %get-tuple-element.24), channel_id=1, source_target_pairs={{0,16},{4,20},{8,24},{12,28},{16,0},{20,4},{24,8},{28,12},{1,17},{... | collective-permute-start | bytes 884744 | tf_op jit(solution)/shard_map/ppermute | solution.py:378
  14.2 19.3 %collective-permute-start.9 = (f32[576,128]{1,0:T(8,128)S(1)}, f32[576,128]{1,0:T(8,128)S(1)}, u32[]{:S(2)}, u32[]{:S(2)}) collective-permute-start(f32[576,128]{1,0:T(8,128)S(1)} %get-tuple-element.26), channel_id=1, source_target_pairs={{0,8},{4,12},{8,0},{12,4},{16,24},{20,28},{24,16},{28,20},{1,9},{5... | collective-permute-start | bytes 884744 | tf_op jit(solution)/shard_map/ppermute | solution.py:378
  20.8 18.2 %collective-permute-start.6 = (f32[576,128]{1,0:T(8,128)S(1)}, f32[576,128]{1,0:T(8,128)S(1)}, u32[]{:S(2)}, u32[]{:S(2)}) collective-permute-start(f32[576,128]{1,0:T(8,128)S(1)} %get-tuple-element.23), channel_id=1, source_target_pairs={{0,28},{4,24},{8,20},{12,16},{16,12},{20,8},{24,4},{28,0},{1,29},{... | collective-permute-start | bytes 884744 | tf_op jit(solution)/shard_map/ppermute | solution.py:378
  20.8 19.9 %collective-permute-start.1 = (f32[576,128]{1,0:T(8,128)S(1)}, f32[576,128]{1,0:T(8,128)S(1)}, u32[]{:S(2)}, u32[]{:S(2)}) collective-permute-start(f32[576,128]{1,0:T(8,128)S(1)} %get-tuple-element.22), channel_id=1, source_target_pairs={{0,4},{4,0},{8,12},{12,8},{16,20},{20,16},{24,28},{28,24},{1,5},{5... | collective-permute-start | bytes 884744 | tf_op jit(solution)/shard_map/ppermute | solution.py:378
  26.4 21.8 %collective-permute-start.10 = (f32[576,128]{1,0:T(8,128)}, f32[576,128]{1,0:T(8,128)S(1)}, u32[]{:S(2)}, u32[]{:S(2)}) collective-permute-start(f32[576,128]{1,0:T(8,128)} %get-tuple-element.27), channel_id=1, source_target_pairs={{0,12},{4,8},{8,4},{12,0},{16,28},{20,24},{24,20},{28,16},{1,13},{... | collective-permute-start | bytes 884744 | tf_op jit(solution)/shard_map/ppermute | solution.py:378
  30.8 17.4 %collective-permute-start.8 = (f32[576,128]{1,0:T(8,128)}, f32[576,128]{1,0:T(8,128)S(1)}, u32[]{:S(2)}, u32[]{:S(2)}) collective-permute-start(f32[576,128]{1,0:T(8,128)} %get-tuple-element.25), channel_id=1, source_target_pairs={{0,4},{4,0},{8,12},{12,8},{16,20},{20,16},{24,28},{28,24},{1,5},{5... | collective-permute-start | bytes 884744 | tf_op jit(solution)/shard_map/ppermute | solution.py:378
  33.4 18.3 %collective-permute-start.13 = (f32[576,128]{1,0:T(8,128)}, f32[576,128]{1,0:T(8,128)S(1)}, u32[]{:S(2)}, u32[]{:S(2)}) collective-permute-start(f32[576,128]{1,0:T(8,128)} %get-tuple-element.30), channel_id=1, source_target_pairs={{0,28},{4,24},{8,20},{12,16},{16,12},{20,8},{24,4},{28,0},{1,29},{... | collective-permute-start | bytes 884744 | tf_op jit(solution)/shard_map/ppermute | solution.py:378
  39.0 22.0 %collective-permute-start.11 = (f32[576,128]{1,0:T(8,128)}, f32[576,128]{1,0:T(8,128)}, u32[]{:S(2)}, u32[]{:S(2)}) collective-permute-start(f32[576,128]{1,0:T(8,128)} %get-tuple-element.28), channel_id=1, source_target_pairs={{0,20},{4,16},{8,28},{12,24},{16,4},{20,0},{24,12},{28,8},{1,21},{... | collective-permute-start | bytes 884744 | tf_op jit(solution)/shard_map/ppermute | solution.py:378
  40.7 20.3 %collective-permute-start.12 = (f32[576,128]{1,0:T(8,128)}, f32[576,128]{1,0:T(8,128)}, u32[]{:S(2)}, u32[]{:S(2)}) collective-permute-start(f32[576,128]{1,0:T(8,128)} %get-tuple-element.29), channel_id=1, source_target_pairs={{0,24},{4,28},{8,16},{12,20},{16,8},{20,12},{24,0},{28,4},{1,25},{... | collective-permute-start | bytes 884744 | tf_op jit(solution)/shard_map/ppermute | solution.py:378
  42.9 18.1 %copy-start.3 = (bf16[2048,128]{1,0:T(8,128)(2,1)S(1)}, bf16[2048,128]{1,0:T(8,128)(2,1)}, u32[]{:S(2)}) copy-start(bf16[2048,128]{1,0:T(8,128)(2,1)} %constant.46.clone.gather_ref) | copy-start | bytes 1572868
  42.9 18.1 %copy-start.4 = (f32[72,128]{1,0:T(8,128)S(1)}, f32[72,128]{1,0:T(8,128)}, u32[]{:S(2)}) copy-start(f32[72,128]{1,0:T(8,128)} %equal_ref.1) | copy-start | bytes 110596
  42.9 18.1 %copy-start.5 = (f32[8,128]{1,0:T(8,128)S(1)}, f32[8,128]{1,0:T(8,128)}, u32[]{:S(2)}) copy-start(f32[8,128]{1,0:T(8,128)} %constant.45.clone.sign_ref) | copy-start | bytes 12292
  46.8 1.4 %copy-start.1 = (f32[576,8,128]{2,1,0:T(8,128)}, f32[576,8,128]{2,1,0:T(8,128)S(1)}, u32[]{:S(2)}) copy-start(f32[576,8,128]{2,1,0:T(8,128)S(1)} %forward.1.lattice_ref) | copy-start | bytes 7077892
  61.0 31.0 %copy-start.7 = (f32[72,128]{1,0:T(8,128)S(1)}, f32[72,128]{1,0:T(8,128)}, u32[]{:S(2)}) copy-start(f32[72,128]{1,0:T(8,128)} %param.12) | copy-start | bytes 110596
  61.0 31.0 %copy-start = (f32[64,72,128]{2,1,0:T(8,128)S(1)}, f32[64,72,128]{2,1,0:T(8,128)}, u32[]{:S(2)}) copy-start(f32[64,72,128]{2,1,0:T(8,128)} %green_ref.1) | copy-start | bytes 7077892
  61.0 31.0 %copy-start.2 = (bf16[128,2048]{1,0:T(8,128)(2,1)S(1)}, bf16[128,2048]{1,0:T(8,128)(2,1)}, u32[]{:S(2)}) copy-start(bf16[128,2048]{1,0:T(8,128)(2,1)} %constant.47.clone.spread_ref) | copy-start | bytes 1572868
  75.3 1.4 %collective-permute-start.14 = (f32[288,128]{1,0:T(8,128)S(1)}, f32[288,128]{1,0:T(8,128)S(1)}, u32[]{:S(2)}, u32[]{:S(2)}) collective-permute-start(f32[288,128]{1,0:T(8,128)S(1)} %pad_maximum_fusion), channel_id=1, source_target_pairs={{0,4},{4,0},{8,12},{12,8},{16,20},{20,16},{24,28},{28,24},{1,5},{5... | collective-permute-start | bytes 442376 | tf_op jit(solution)/shard_map/ppermute | solution.py:378
  76.7 4.9 %collective-permute-start.17 = (f32[72,128]{1,0:T(8,128)S(1)}, f32[72,128]{1,0:T(8,128)S(1)}, u32[]{:S(2)}, u32[]{:S(2)}) collective-permute-start(f32[72,128]{1,0:T(8,128)S(1)} %get-tuple-element.53), channel_id=1, source_target_pairs={{0,24},{4,28},{8,16},{12,20},{16,8},{20,12},{24,0},{28,4},{1,25},{... | collective-permute-start | bytes 110600 | tf_op jit(solution)/shard_map/ppermute | solution.py:378
  78.1 4.0 %collective-permute-start.16 = (f32[72,128]{1,0:T(8,128)S(1)}, f32[72,128]{1,0:T(8,128)S(1)}, u32[]{:S(2)}, u32[]{:S(2)}) collective-permute-start(f32[72,128]{1,0:T(8,128)S(1)} %get-tuple-element.54), channel_id=1, source_target_pairs={{0,16},{4,20},{8,24},{12,28},{16,0},{20,4},{24,8},{28,12},{1,17},{... | collective-permute-start | bytes 110600 | tf_op jit(solution)/shard_map/ppermute | solution.py:378
  79.5 4.0 %collective-permute-start.15 = (f32[72,128]{1,0:T(8,128)S(1)}, f32[72,128]{1,0:T(8,128)S(1)}, u32[]{:S(2)}, u32[]{:S(2)}) collective-permute-start(f32[72,128]{1,0:T(8,128)S(1)} %get-tuple-element.55), channel_id=1, source_target_pairs={{0,8},{4,12},{8,0},{12,4},{16,24},{20,28},{24,16},{28,20},{1,9},{5... | collective-permute-start | bytes 110600 | tf_op jit(solution)/shard_map/ppermute | solution.py:378
  83.5 5.8 %collective-permute-start.20 = (f32[72,128]{1,0:T(8,128)S(1)}, f32[72,128]{1,0:T(8,128)S(1)}, u32[]{:S(2)}, u32[]{:S(2)}) collective-permute-start(f32[72,128]{1,0:T(8,128)S(1)} %fusion), channel_id=1, source_target_pairs={{0,3},{1,2},{2,1},{3,0},{4,7},{5,6},{6,5},{7,4},{8,11},{9,10},{10,... | collective-permute-start | bytes 110600 | tf_op jit(solution)/shard_map/ppermute | solution.py:378
  87.1 4.9 %collective-permute-start.19 = (f32[72,128]{1,0:T(8,128)S(1)}, f32[72,128]{1,0:T(8,128)S(1)}, u32[]{:S(2)}, u32[]{:S(2)}) collective-permute-start(f32[72,128]{1,0:T(8,128)S(1)} %fusion), channel_id=1, source_target_pairs={{0,2},{1,3},{2,0},{3,1},{4,6},{5,7},{6,4},{7,5},{8,10},{9,11},{10,... | collective-permute-start | bytes 110600 | tf_op jit(solution)/shard_map/ppermute | solution.py:378
  87.1 4.9 %collective-permute-start.18 = (f32[72,128]{1,0:T(8,128)S(1)}, f32[72,128]{1,0:T(8,128)S(1)}, u32[]{:S(2)}, u32[]{:S(2)}) collective-permute-start(f32[72,128]{1,0:T(8,128)S(1)} %fusion), channel_id=1, source_target_pairs={{0,1},{1,0},{2,3},{3,2},{4,5},{5,4},{6,7},{7,6},{8,9},{9,8},{10,11... | collective-permute-start | bytes 110600 | tf_op jit(solution)/shard_map/ppermute | solution.py:378
where the time goes:
time: 99.9 us; the launch traced here: 99.7 us
  waiting for transfers between devices  42.7 us (43%)
  Pallas kernels  25.8 us (26%)
  starting transfers between devices  25.7 us (26%)
  local copies, waits for them, and re-layouts  4.57 us (5%)
    ppermute x21, waiting for transfers between devices, exchange(): return lax.ppermute(value, axis, pairs)  42.7 us
    ppermute x21, starting transfers between devices, exchange(): return lax.ppermute(value, axis, pairs)  25.7 us
    pallas_call x1, Pallas kernels, backward(): pl.pallas_call(functools.partial(backward_kernel, order, share), out_shap...  14.2 us
    pallas_call x1, Pallas kernels, propagate(): pl.pallas_call(propagate_kernel, grid=(history // step,), out_shape=jax.S...  7.68 us
    pallas_call x1, Pallas kernels, forward(): pl.pallas_call(functools.partial(forward_kernel, order), out_shape=jax.Sh...  3.91 us
    dynamic_slice x2, local copies, waits for them, and re-layouts, per_device(): block = lax.dynamic_slice_in_dim(whole, start, TILE * local)  2.96 us
  transfers between devices with their start and end apart: 21, of which 14 were waited for; matrix products, arithmetic and copies ran while one was open for 1% of the time, Pallas kernels for 4%

commit v1 on v0

--- a/solution.py
+++ b/solution.py
@@ -22,6 +22,8 @@
 quadrature = (0.375, 1.1666666, 0.9583333, 1.0)
 
 IN_FLIGHT = 5
+
+AHEAD = 3
 
 VMEM_LIMIT = 48 * 1024 * 1024
 
@@ -80,11 +82,6 @@
     return out
 
 
-def line_of(place, step, ref, count):
-    lines = ref.shape[0] // (TILE * SIDE)
-    return partner_of(place, step, count) * lines if count > 1 else 0
-
-
 def load_line(ref, line):
     stride = ref.shape[0] // TILE
     return [ref[pl.ds(line * SIDE + k2, TILE, stride=stride), :] for k2 in range(SIDE)]
@@ -97,17 +94,20 @@
         rows = held_ref.shape[1]
         if step == 0 and len(order) > 1:
             source = source.at[pl.ds(pl.multiple_of(place * rows, TILE), rows)]
-        copies[step] = pltpu.make_async_copy(source, held_ref.at[step], sems.at[step])
+        slot = partner_of(place, step, len(order))
+        copies[step] = pltpu.make_async_copy(source, held_ref.at[slot], sems.at[step])
         copies[step].start()
     return copies
 
 
 def along_first(work_ref, sign, low, out_ref):
     def columns(pair, carry):
-        for column in (2 * pair, 2 * pair + 1):
-            rows = [work_ref[k1 * SIDE + column] for k1 in range(SIDE)]
-            for r1, value in enumerate(dft24(rows, sign, low)):
-                out_ref[r1 * SIDE + column] = value
+        both = (2 * pair, 2 * pair + 1)
+        rows = [[work_ref[k1 * SIDE + column] for k1 in range(SIDE)] for column in both]
+        values = [dft24(row, sign, low) for row in rows]
+        for column, value in zip(both, values):
+            for r1 in range(SIDE):
+                out_ref[r1 * SIDE + column] = value[r1]
         return carry
 
     lax.fori_loop(0, SIDE // 2, columns, 0)
@@ -121,9 +121,10 @@
     copies = fetch(place, order, block_refs, held_ref, sems)
     for step in order:
         copies[step].wait()
-        green_ref = held_ref.at[step]
-        first = line_of(place, step, green_ref, count)
+        slot = partner_of(place, step, count)
+        green_ref = held_ref.at[slot]
         lines = green_ref.shape[0] // (TILE * SIDE)
+        first = slot * lines
 
         def along_second(i, carry):
             for r2, value in enumerate(dft24(load_line(green_ref, i), -1, low)):
@@ -136,8 +137,8 @@
 
 def backward_kernel(order, share, place_ref, lattice_ref, weight_ref, equal_ref, sign_ref, gather_ref, *refs):
     count = len(order)
-    screen_refs, green_refs, partial_refs = refs[:count], refs[count : 2 * count], refs[2 * count : -7]
-    work_ref, sigma_ref, sums_ref, screen_held, green_held, screen_sems, green_sems = refs[-7:]
+    screen_refs, green_refs, partial_ref = refs[:count], refs[count : 2 * count], refs[2 * count]
+    work_ref, sigma_ref, sums_ref, pieces_ref, screen_held, green_held, screen_sems, green_sems = refs[2 * count + 1 :]
     points = SIDE * SIDE
     low = lane_sign((TILE, WIDTH))
     turn = jnp.where(low, -1.0, 1.0)
@@ -148,9 +149,10 @@
 
     for step in order:
         screen_copies[step].wait()
-        screen_ref = screen_held.at[step]
-        first = line_of(place, step, screen_ref, count)
+        slot = partner_of(place, step, count)
+        screen_ref = screen_held.at[slot]
         lines = screen_ref.shape[0] // (TILE * SIDE)
+        first = slot * lines
 
         def along_second(i, carry):
             rows = []
@@ -172,42 +174,45 @@
 
     for step in order:
         green_copies[step].wait()
-        green_ref = green_held.at[step]
-        first = line_of(place, step, green_ref, count) * SIDE
-        block = green_ref.shape[0] // TILE
-        tiles = block // TILE
-        batch = max(n for n in (1, 2, 3) if tiles % n == 0)
-
-        def contract(group, carry):
-            values = []
-            for tile in range(batch):
-                tile = group * batch + tile
-                start = (first + tile * TILE) * TILE
-                sums = [None] * (STEPS * STEPS)
-                for s in range(TILE):
-                    sigma = sigma_ref[pl.ds(start + s, TILE, stride=TILE), :]
-                    green = green_ref[pl.ds(pl.multiple_of(s * block + tile * TILE, TILE), TILE), :]
-                    sigmas = [roll_blocks(sigma, STEPS * i) for i in range(STEPS)]
-                    greens = [roll_blocks(green, j) for j in range(STEPS)]
-                    for i in range(STEPS):
-                        for j in range(STEPS):
-                            term = sigmas[i] * greens[j]
-                            spot = STEPS * i + j
-                            sums[spot] = term if s == 0 else sums[spot] + term
-                values.append((pl.ds(pl.multiple_of(step * block + tile * TILE, TILE), TILE), sums))
-            for row, sums in values:
+    block = green_held.shape[1] // TILE
+    tiles = block // TILE
+    batch = max(n for n in range(1, 10) if tiles % n == 0)
+
+    def contract(group, carry):
+        first = group * batch
+        green_row = (first // tiles) * TILE * block + (first % tiles) * TILE
+        units = [(tile, s) for tile in range(batch) for s in range(TILE)]
+
+        def prepare(tile, s):
+            sigma = sigma_ref[pl.ds((first + tile) * TILE * TILE + s, TILE, stride=TILE), :]
+            row = pl.multiple_of(green_row + s * block + tile * TILE, TILE)
+            green = greens_ref[pl.ds(row, TILE), :]
+            return (
+                [roll_blocks(sigma, STEPS * i) for i in range(STEPS)],
+                [roll_blocks(green, j) for j in range(STEPS)],
+            )
+
+        ready = [prepare(*unit) for unit in units[:AHEAD]]
+        for n, (tile, s) in enumerate(units):
+            if n + AHEAD < len(units):
+                ready.append(prepare(*units[n + AHEAD]))
+            sigmas, greens = ready.pop(0)
+            terms = [sigma * green for sigma in sigmas for green in greens]
+            sums = terms if s == 0 else [a + b for a, b in zip(sums, terms)]
+            if s == TILE - 1:
+                row = pl.ds(pl.multiple_of((first + tile) * TILE, TILE), TILE)
                 for spot, value in enumerate(sums):
                     sums_ref[row, spot * WIDTH : (spot + 1) * WIDTH] = value
-            return carry
-
-        lax.fori_loop(0, tiles // batch, contract, 0)
+        return carry
+
+    greens_ref = green_held.reshape(TILE * points, WIDTH)
+    lax.fori_loop(0, points // (TILE * batch), contract, 0)
 
     lane = lax.broadcasted_iota(jnp.int32, equal_ref.shape, 1)
     inner = lane - ENTRIES
     occupied = jnp.sum(jnp.where((inner >= 0) & (inner % (BANDS + 1) == 0), equal_ref[...], 0.0))
     spots = lax.broadcasted_iota(jnp.int32, (points, WIDTH), 1)
     on_diagonal = (spots < ENTRIES) & (spots % (BANDS + 1) == 0)
-    total = jnp.where(on_diagonal, occupied * share, 0.0)
     lower = spots < ENTRIES
     for pair in range(STEPS * STEPS // 2):
         first_part = sums_ref[:, 2 * pair * WIDTH : (2 * pair + 1) * WIDTH]
@@ -217,19 +222,10 @@
         )
         coarse = folded.astype(jnp.bfloat16)
         fine = (folded - coarse.astype(jnp.float32)).astype(jnp.bfloat16)
-        gather = gather_ref[2 * pair * WIDTH : (2 * pair + 2) * WIDTH, :]
-        both = jnp.concatenate([coarse, fine], axis=1)
-        total = total + jnp.dot(both, gather, preferred_element_type=jnp.float32)
-    parts = len(partial_refs)
-    local = points // parts
-    if count == parts:
-        for step, partial_ref in enumerate(partial_refs):
-            partial_ref[...] = total[step * local : (step + 1) * local]
-    else:
-        sigma_ref[:points, :] = total
-        for step, partial_ref in enumerate(partial_refs):
-            owner = partner_of(place, step, parts)
-            partial_ref[...] = sigma_ref[pl.ds(owner * local, local), :]
+        pieces_ref[:, 2 * pair * WIDTH : (2 * pair + 1) * WIDTH] = coarse
+        pieces_ref[:, (2 * pair + 1) * WIDTH : (2 * pair + 2) * WIDTH] = fine
+    total = jnp.dot(pieces_ref[...], gather_ref[...], preferred_element_type=jnp.float32)
+    partial_ref[...] = total + jnp.where(on_diagonal, occupied * share, 0.0)
 
 
 def propagate_kernel(green_ref, effective_ref, spread_ref, out_ref, factor_ref):
@@ -246,10 +242,19 @@
         spread = jnp.dot(stacked, spread_ref[...], preferred_element_type=jnp.float32)
         factor_ref[...] = tree_sum([spread[n * points : (n + 1) * points] for n in range(3)])
 
-    def advance(start, stop):
-        green = green_ref[:, start:stop, :]
-        greens = [roll_blocks(green, j) for j in range(STEPS)]
-        terms = [green]
+    starts = list(range(0, points, TILE))
+
+    def prepare(start):
+        green = green_ref[:, start : min(start + TILE, points), :]
+        return [roll_blocks(green, j) for j in range(STEPS)]
+
+    ready = prepare(starts[0])
+    for n, start in enumerate(starts):
+        greens = ready
+        if n + 1 < len(starts):
+            ready = prepare(starts[n + 1])
+        stop = min(start + TILE, points)
+        terms = [greens[0]]
         for i in range(STEPS):
             total = None
             for j in range(STEPS):
@@ -259,9 +264,6 @@
                 total = term if total is None else total + term
             terms.append(roll_blocks(total, STEPS * i))
         out_ref[:, start:stop, :] = tree_sum(terms)
-
-    for start in range(0, points, 2 * TILE):
-        advance(start, min(start + 2 * TILE, points))
 
 
 def gather_tables():
@@ -313,7 +315,7 @@
     )(place, *greens)
 
 
-def backward(place, lattice, screens, greens, weights, equal_time, order, share, parts):
+def backward(place, lattice, screens, greens, weights, equal_time, order, share):
     points = SIDE * SIDE
     count = len(greens)
     whole = pl.BlockSpec(memory_space=pltpu.VMEM)
@@ -321,15 +323,16 @@
     held = pltpu.VMEM((count, TILE * points // count, WIDTH), jnp.float32)
     return pl.pallas_call(
         functools.partial(backward_kernel, order, share),
-        out_shape=[jax.ShapeDtypeStruct((points // parts, WIDTH), jnp.float32)] * parts,
+        out_shape=jax.ShapeDtypeStruct((points, WIDTH), jnp.float32),
         in_specs=[pl.BlockSpec(memory_space=pltpu.SMEM)]
         + [whole] * 5
         + [pl.BlockSpec(memory_space=pl.ANY)] * (2 * count),
-        out_specs=[whole] * parts,
+        out_specs=whole,
         scratch_shapes=[
             pltpu.VMEM((points, TILE, WIDTH), jnp.float32),
             pltpu.VMEM((TILE * points, WIDTH), jnp.float32),
             pltpu.VMEM((points, STEPS * STEPS * WIDTH), jnp.float32),
+            pltpu.VMEM((points, STEPS * STEPS * WIDTH), jnp.bfloat16),
             held,
             held,
             pltpu.SemaphoreType.DMA((count,)),
@@ -368,6 +371,8 @@
 
 
 def partner_of(place, step, count):
+    if count == 1:
+        return 0
     if count & (count - 1) == 0:
         return place ^ step
     return (place + step) % count
@@ -436,31 +441,27 @@
         weights = jnp.pad(weights, (0, padding))
     weights = jnp.broadcast_to(weights.reshape(groups, TILE, 1), (groups, TILE, width))
 
-    pieces = None
+    partial_value = None
     for group in range(groups):
         green, screen = moved[0][group], moved[1][group]
         lattice = forward(place.reshape(1), green, order)
         share = hubbard / (points * blocks) if group == 0 else 0.0
-        terms = backward(
-            place.reshape(1), lattice, screen, green, weights[group], equal_time, order, share, parts
+        term = backward(
+            place.reshape(1), lattice, screen, green, weights[group], equal_time, order, share
         )
-        pieces = list(terms) if pieces is None else [a + b for a, b in zip(pieces, terms)]
-
-    if parts % 2 == 0 and parts & (parts - 1) == 0:
-        pairs = jnp.concatenate([pieces[step] for step in range(1, parts, 2)], axis=0)
-        pairs = exchange(pairs, "ka", 1, parts)
-        mine = jnp.concatenate([pieces[step] for step in range(0, parts, 2)], axis=0) + pairs
-        pieces = [mine[n * local : (n + 1) * local] for n in range(parts // 2)]
-        partial_value = tree_sum(
-            pieces[:1] + [exchange(pieces[n], "ka", 2 * n, parts) for n in range(1, parts // 2)]
+        partial_value = term if partial_value is None else partial_value + term
+
+    shares = lax.all_to_all(
+        partial_value.reshape(parts, local, width), "ka", split_axis=0, concat_axis=0, tiled=True
+    )
+    collision = jnp.sum(shares, axis=0)
+    if blocks & (blocks - 1) == 0:
+        for bit in range(blocks.bit_length() - 1):
+            collision = collision + exchange(collision, "hist", 1 << bit, blocks)
+    else:
+        collision = tree_sum(
+            [collision] + [exchange(collision, "hist", step, blocks) for step in range(1, blocks)]
         )
-    else:
-        partial_value = tree_sum(
-            pieces[:1] + [exchange(pieces[step], "ka", step, parts) for step in range(1, parts)]
-        )
-    collision = tree_sum(
-        [partial_value] + [exchange(partial_value, "hist", step, blocks) for step in range(1, blocks)]
-    )
     return propagate(green_row, hamilton + collision)
 
 

time: 99.9 us -> 109 us (1.091)
  local copies, waits for them, and re-layouts: 4.57 us -> 15.4 us
  blocking collectives: 0 us -> 9.66 us
  waiting for transfers between devices: 42.7 us -> 36.7 us
  starting transfers between devices: 25.7 us -> 21.7 us
  Pallas kernels: 25.8 us -> 23.7 us
    unnamed x20 -> x50, local copies, waits for them, and re-layouts: 1.44 us -> 12.3 us
    all_to_all x0 -> x1, blocking collectives: none -> 9.66 us  [per_device(): lax.all_to_all(partial_value.reshape(parts, local, width), 'ka', split_ax...]
    ppermute x21 -> x16, waiting for transfers between devices: 42.7 us -> 36.7 us  [exchange(): return lax.ppermute(value, axis, pairs)]
    ppermute x21 -> x16, starting transfers between devices: 25.7 us -> 21.7 us  [exchange(): return lax.ppermute(value, axis, pairs)]
    pallas_call x1, Pallas kernels: 7.68 us -> 6.5 us  [propagate(): pl.pallas_call(propagate_kernel, grid=(history // step,), out_shape=jax.S...]
  transfers between devices with their start and end apart: 21 -> 16, of which waited for: 14 -> 10; matrix products, arithmetic and copies ran while one was open for 1% -> 1% of each run, Pallas kernels for 4% -> 4%
where the time goes in v1:
time: 109 us
  waiting for transfers between devices  36.7 us (34%)
  Pallas kernels  23.7 us (22%)
  starting transfers between devices  21.7 us (20%)
  local copies, waits for them, and re-layouts  15.4 us (14%)
  blocking collectives  9.66 us (9%)
    ppermute x16, waiting for transfers between devices, exchange(): return lax.ppermute(value, axis, pairs)  36.7 us
    ppermute x16, starting transfers between devices, exchange(): return lax.ppermute(value, axis, pairs)  21.7 us
    pallas_call x1, Pallas kernels, backward(): pl.pallas_call(functools.partial(backward_kernel, order, share), out_shap...  13.3 us
    unnamed x50, local copies, waits for them, and re-layouts  12.3 us
    all_to_all x1, blocking collectives, per_device(): lax.all_to_all(partial_value.reshape(parts, local, width), 'ka', split_ax...  9.66 us
    pallas_call x1, Pallas kernels, propagate(): pl.pallas_call(propagate_kernel, grid=(history // step,), out_shape=jax.S...  6.5 us
    pallas_call x1, Pallas kernels, forward(): pl.pallas_call(functools.partial(forward_kernel, order), out_shape=jax.Sh...  3.93 us
    dynamic_slice x2, local copies, waits for them, and re-layouts, per_device(): block = lax.dynamic_slice_in_dim(whole, start, TILE * local)  2.91 us
  transfers between devices with their start and end apart: 16, of which 10 were waited for; matrix products, arithmetic and copies ran while one was open for 1% of the time, Pallas kernels for 4%

profile of v1, /device:TPU:0, one launch (start us, length us, event | category | flops | bytes accessed | tf_op | source)
XLA Modules:
  0.0 108.9 jit_solution(1016928571208759907)
XLA Ops:
  0.0 1.8 %constant_dynamic-slice_fusion.7 = (f32[576,128]{1,0:T(8,128)S(1)}, f32[576,128]{1,0:T(8,128)S(1)}, f32[576,128]{1,0:T(8,128)S(1)}, f32[576,128]{1,0:T(8,128)S(1...) fusion(f32[4608,128]{1,0:T(8,128)} %bitcast.6, s32[]{:T(128)S(6)} %select_n.45, ...), kind=kLoop, calls=%fused_computation.8 | loop fusion | bytes 4128796 | tf_op jit(solution)/shard_map/dynamic_slice | solution.py:422
  1.8 0.0 copy-start.24
  1.8 2.5 %collective-permute-start.4 = (f32[576,128]{1,0:T(8,128)S(1)}, f32[576,128]{1,0:T(8,128)S(1)}, u32[]{:S(2)}, u32[]{:S(2)}) collective-permute-start(f32[576,128]{1,0:T(8,128)S(1)} %get-tuple-element.32), channel_id=1, source_target_pairs={{0,20},{4,16},{8,28},{12,24},{16,4},{20,0},{24,12},{28,8},{1,21},{... | collective-permute-start | bytes 884744 | tf_op jit(solution)/shard_map/ppermute | solution.py:383
  4.3 1.8 %collective-permute-start.3 = (f32[576,128]{1,0:T(8,128)S(1)}, f32[576,128]{1,0:T(8,128)S(1)}, u32[]{:S(2)}, u32[]{:S(2)}) collective-permute-start(f32[576,128]{1,0:T(8,128)S(1)} %get-tuple-element.33), channel_id=1, source_target_pairs={{0,12},{4,8},{8,4},{12,0},{16,28},{20,24},{24,20},{28,16},{1,13},{... | collective-permute-start | bytes 884744 | tf_op jit(solution)/shard_map/ppermute | solution.py:383
  6.1 0.5 collective-permute-start.2
  6.6 3.0 %collective-permute-start.5 = (f32[576,128]{1,0:T(8,128)S(1)}, f32[576,128]{1,0:T(8,128)S(1)}, u32[]{:S(2)}, u32[]{:S(2)}) collective-permute-start(f32[576,128]{1,0:T(8,128)S(1)} %get-tuple-element.31), channel_id=1, source_target_pairs={{0,24},{4,28},{8,16},{12,20},{16,8},{20,12},{24,0},{28,4},{1,25},{... | collective-permute-start | bytes 884744 | tf_op jit(solution)/shard_map/ppermute | solution.py:383
  9.6 1.1 %constant_dynamic-slice_fusion = (f32[576,128]{1,0:T(8,128)}, f32[576,128]{1,0:T(8,128)}, f32[576,128]{1,0:T(8,128)}, f32[576,128]{1,0:T(8,128)}, f32[576,128]{1...) fusion(f32[4608,128]{1,0:T(8,128)S(1)} %bitcast.11, s32[]{:T(128)S(6)} %select_n.45, s32[]{:T(128)S(6)} %select_n.44, ...), kind=kLoop, calls=%fused_computation.1 | loop fusion | bytes 4128796 | tf_op jit(solution)/shard_map/dynamic_slice | solution.py:422
  10.7 1.0 collective-permute-done.4.refs_5_.refs_13_
  11.7 2.5 %collective-permute-start.7 = (f32[576,128]{1,0:T(8,128)S(1)}, f32[576,128]{1,0:T(8,128)S(1)}, u32[]{:S(2)}, u32[]{:S(2)}) collective-permute-start(f32[576,128]{1,0:T(8,128)S(1)} %get-tuple-element.16), channel_id=1, source_target_pairs={{0,16},{4,20},{8,24},{12,28},{16,0},{20,4},{24,8},{28,12},{1,17},{... | collective-permute-start | bytes 884744 | tf_op jit(solution)/shard_map/ppermute | solution.py:383
  14.1 1.5 %collective-permute-start.9 = (f32[576,128]{1,0:T(8,128)S(1)}, f32[576,128]{1,0:T(8,128)S(1)}, u32[]{:S(2)}, u32[]{:S(2)}) collective-permute-start(f32[576,128]{1,0:T(8,128)S(1)} %get-tuple-element.18), channel_id=1, source_target_pairs={{0,8},{4,12},{8,0},{12,4},{16,24},{20,28},{24,16},{28,20},{1,9},{5... | collective-permute-start | bytes 884744 | tf_op jit(solution)/shard_map/ppermute | solution.py:383
  15.6 5.1 %collective-permute-done.2.refs_2_.refs_10_ = f32[576,128]{1,0:T(8,128)S(1)} collective-permute-done((f32[576,128]{1,0:T(8,128)S(1)}, f32[576,128]{1,0:T(8,128)S(1)}, u32[]{:S(2)}, u32[]{:S(2)}) %collective-permute-start.2) | collective-permute-done | bytes 294944 | tf_op jit(solution)/shard_map/ppermute | solution.py:383
  20.8 1.5 %collective-permute-start.1 = (f32[576,128]{1,0:T(8,128)S(1)}, f32[576,128]{1,0:T(8,128)S(1)}, u32[]{:S(2)}, u32[]{:S(2)}) collective-permute-start(f32[576,128]{1,0:T(8,128)S(1)} %get-tuple-element.14), channel_id=1, source_target_pairs={{0,4},{4,0},{8,12},{12,8},{16,20},{20,16},{24,28},{28,24},{1,5},{5... | collective-permute-start | bytes 884744 | tf_op jit(solution)/shard_map/ppermute | solution.py:383
  22.3 4.1 %collective-permute-done.5.refs_6_.refs_14_ = f32[576,128]{1,0:T(8,128)S(1)} collective-permute-done((f32[576,128]{1,0:T(8,128)S(1)}, f32[576,128]{1,0:T(8,128)S(1)}, u32[]{:S(2)}, u32[]{:S(2)}) %collective-permute-start.5) | collective-permute-done | bytes 294944 | tf_op jit(solution)/shard_map/ppermute | solution.py:383
  26.4 0.5 collective-permute-start.10
  26.9 3.9 %collective-permute-done.7.refs_4_ = f32[576,128]{1,0:T(8,128)S(1)} collective-permute-done((f32[576,128]{1,0:T(8,128)S(1)}, f32[576,128]{1,0:T(8,128)S(1)}, u32[]{:S(2)}, u32[]{:S(2)}) %collective-permute-start.7) | collective-permute-done | bytes 294944 | tf_op jit(solution)/shard_map/ppermute | solution.py:383
  30.8 2.6 %collective-permute-done.9.refs_2_ = f32[576,128]{1,0:T(8,128)S(1)} collective-permute-done((f32[576,128]{1,0:T(8,128)S(1)}, f32[576,128]{1,0:T(8,128)S(1)}, u32[]{:S(2)}, u32[]{:S(2)}) %collective-permute-start.9) | collective-permute-done | bytes 294944 | tf_op jit(solution)/shard_map/ppermute | solution.py:383
  33.4 0.7 collective-permute-start.13
  34.2 4.8 %collective-permute-done.6.refs_7_.refs_15_ = f32[576,128]{1,0:T(8,128)S(1)} collective-permute-done((f32[576,128]{1,0:T(8,128)S(1)}, f32[576,128]{1,0:T(8,128)S(1)}, u32[]{:S(2)}, u32[]{:S(2)}) %collective-permute-start.6) | collective-permute-done | bytes 294944 | tf_op jit(solution)/shard_map/ppermute | solution.py:383
  39.0 1.7 %collective-permute-start.11 = (f32[576,128]{1,0:T(8,128)}, f32[576,128]{1,0:T(8,128)}, u32[]{:S(2)}, u32[]{:S(2)}) collective-permute-start(f32[576,128]{1,0:T(8,128)} %get-tuple-element.20), channel_id=1, source_target_pairs={{0,20},{4,16},{8,28},{12,24},{16,4},{20,0},{24,12},{28,8},{1,21},{... | collective-permute-start | bytes 884744 | tf_op jit(solution)/shard_map/ppermute | solution.py:383
  40.6 1.4 %collective-permute-start.12 = (f32[576,128]{1,0:T(8,128)}, f32[576,128]{1,0:T(8,128)}, u32[]{:S(2)}, u32[]{:S(2)}) collective-permute-start(f32[576,128]{1,0:T(8,128)} %get-tuple-element.21), channel_id=1, source_target_pairs={{0,24},{4,28},{8,16},{12,20},{16,8},{20,12},{24,0},{28,4},{1,25},{... | collective-permute-start | bytes 884744 | tf_op jit(solution)/shard_map/ppermute | solution.py:383
  42.1 0.1 select_reduce_fusion
  42.8 0.1 dynamic_slice.52
  42.9 3.9 %forward.1.lattice_ref = f32[576,8,128]{2,1,0:T(8,128)S(1)} custom-call(s32[1]{0:T(128)} %bitcast.place_ref, f32[4608,128]{1,0:T(8,128)} %bitcast.7, f32[576,128]{1,0:T(8,128)S(1)} %collective-permute-done.1.refs_1_.refs_9_, f32[576,128]{1,0:T(8,128)S(1)} %collective-permute-done.2.refs_2_.refs_10_, f32[576,128]{1,0:T(8,128)S(1)} %collective-permute-done.3.refs_3_.refs_11_, ...), custom_call_target="tpu_custom_call" | custom-call | flops 235929600 | bytes 4718592 | tf_op jit(solution)/shard_map/forward/pallas_call | solution.py:300
  46.9 1.4 %copy-done.1 = f32[576,8,128]{2,1,0:T(8,128)} copy-done((f32[576,8,128]{2,1,0:T(8,128)}, f32[576,8,128]{2,1,0:T(8,128)S(1)}, u32[]{:S(2)}) %copy-start.1) | copy-done | bytes 2359320
  48.3 0.7 copy-done.14
  49.0 0.7 copy-done.16
  49.8 1.9 %collective-permute-done.13.refs_7_ = f32[576,128]{1,0:T(8,128)S(1)} collective-permute-done((f32[576,128]{1,0:T(8,128)}, f32[576,128]{1,0:T(8,128)S(1)}, u32[]{:S(2)}, u32[]{:S(2)}) %collective-permute-start.13) | collective-permute-done | bytes 294944 | tf_op jit(solution)/shard_map/ppermute | solution.py:383
  51.7 0.7 copy-done.18
  52.4 8.5 %collective-permute-done.11.refs_5_ = f32[576,128]{1,0:T(8,128)} collective-permute-done((f32[576,128]{1,0:T(8,128)}, f32[576,128]{1,0:T(8,128)}, u32[]{:S(2)}, u32[]{:S(2)}) %collective-permute-start.11) | collective-permute-done | bytes 294944 | tf_op jit(solution)/shard_map/ppermute | solution.py:383
  60.9 0.1 squeeze.7.weight_ref
  61.0 1.0 copy-done.3
  62.0 1.0 copy-done.5
  62.9 1.0 copy-done.7
  63.9 1.0 copy-done.11
  64.9 1.0 copy-done.13
  65.8 1.0 copy-done.15
  66.8 1.0 copy-done.17
  67.7 1.0 copy-done.19
  68.7 13.3 %backward.1 = f32[576,128]{1,0:T(8,128)S(1)} custom-call(s32[1]{0:T(128)} %bitcast.place_ref, f32[576,8,128]{2,1,0:T(8,128)} %copy-done.1, f32[8,128]{1,0:T(8,128)S(1)} %squeeze.7.weight_ref, f32[72,128]{1,0:T(8,128)S(1)} %copy-done.20, f32[8,128]{1,0:T(8,128)S(1)} %copy-done.21, bf16[2048,128]{1,0:T(8,128)(2,1)S(1)} %copy-done.9, f32[4608,128]{1,0:T(8,128)} %bitcast.10, ...), custom_call_target="tpu_custom_call" | custom-call | flops 471859200 | bytes 7077888 | tf_op jit(solution)/shard_map/backward/pallas_call | solution.py:324
  82.0 9.7 %all_to_all.5 = f32[8,72,128]{2,1,0:T(8,128)S(1)} all-to-all(f32[8,72,128]{2,1,0:T(8,128)S(1)} %bitcast.9), channel_id=1, replica_groups=mesh['ka'=8,'hist'=4] {'ka'}, dimensions={0} | all-to-all | bytes 589824 | tf_op jit(solution)/shard_map/all_to_all | solution.py:454
  91.7 1.6 %collective-permute-start.14 = (f32[72,128]{1,0:T(8,128)S(1)}, f32[72,128]{1,0:T(8,128)S(1)}, u32[]{:S(2)}, u32[]{:S(2)}) collective-permute-start(f32[72,128]{1,0:T(8,128)S(1)} %reduce_sum.19), channel_id=1, source_target_pairs={{0,1},{1,0},{2,3},{3,2},{4,5},{5,4},{6,7},{7,6},{8,9},{9,8},{10,11... | collective-permute-start | bytes 110600 | tf_op jit(solution)/shard_map/ppermute | solution.py:383
  93.3 2.4 %collective-permute-done.14 = f32[72,128]{1,0:T(8,128)S(1)} collective-permute-done((f32[72,128]{1,0:T(8,128)S(1)}, f32[72,128]{1,0:T(8,128)S(1)}, u32[]{:S(2)}, u32[]{:S(2)}) %collective-permute-start.14) | collective-permute-done | bytes 36896 | tf_op jit(solution)/shard_map/ppermute | solution.py:383
  95.7 2.5 %collective-permute-start.15 = (f32[72,128]{1,0:T(8,128)S(1)}, f32[72,128]{1,0:T(8,128)S(1)}, u32[]{:S(2)}, u32[]{:S(2)}) collective-permute-start(f32[72,128]{1,0:T(8,128)S(1)} %add.48), channel_id=1, source_target_pairs={{0,2},{1,3},{2,0},{3,1},{4,6},{5,7},{6,4},{7,5},{8,10},{9,11},{10,... | collective-permute-start | bytes 110600 | tf_op jit(solution)/shard_map/ppermute | solution.py:383
  98.3 2.3 %collective-permute-done.15 = f32[72,128]{1,0:T(8,128)S(1)} collective-permute-done((f32[72,128]{1,0:T(8,128)S(1)}, f32[72,128]{1,0:T(8,128)S(1)}, u32[]{:S(2)}, u32[]{:S(2)}) %collective-permute-start.15) | collective-permute-done | bytes 36896 | tf_op jit(solution)/shard_map/ppermute | solution.py:383
  100.6 0.8 add_add_fusion.effective_ref
  101.4 0.0 copy-start.8
  101.4 1.0 copy-done.8
  102.4 6.5 %propagate.1 = f32[64,72,128]{2,1,0:T(8,128)} custom-call(f32[64,72,128]{2,1,0:T(8,128)S(1)} %copy-done, f32[72,128]{1,0:T(8,128)S(1)} %add_add_fusion.effective_ref, bf16[128,2048]{1,0:T(8,128)(2,1)S(1)} %copy-done.8), custom_call_target="tpu_custom_call" | custom-call | flops 18874368 | bytes 4718592 | tf_op jit(solution)/shard_map/propagate/pallas_call | solution.py:354
  (47 shorter events, 0.1 us)
Async XLA Ops:
  0.0 9.6 %copy-start.22 = (f32[64,72,128]{2,1,0:T(8,128)S(1)}, f32[64,72,128]{2,1,0:T(8,128)}, u32[]{:S(2)}) copy-start(f32[64,72,128]{2,1,0:T(8,128)} %param.11) | copy-start | bytes 7077892
  1.8 40.3 %copy-start.23 = (s32[64]{0:T(128)S(1)}, s32[64]{0:T(128)}, u32[]{:S(2)}) copy-start(s32[64]{0:T(128)} %param.14) | copy-start | bytes 772
  1.8 40.3 %copy-start.24 = (f32[4]{0:T(128)S(1)}, f32[4]{0:T(128)}, u32[]{:S(2)}) copy-start(f32[4]{0:T(128)} %constant.44.clone) | copy-start | bytes 52
  1.8 9.9 %collective-permute-start.4 = (f32[576,128]{1,0:T(8,128)S(1)}, f32[576,128]{1,0:T(8,128)S(1)}, u32[]{:S(2)}, u32[]{:S(2)}) collective-permute-start(f32[576,128]{1,0:T(8,128)S(1)} %get-tuple-element.32), channel_id=1, source_target_pairs={{0,20},{4,16},{8,28},{12,24},{16,4},{20,0},{24,12},{28,8},{1,21},{... | collective-permute-start | bytes 884744 | tf_op jit(solution)/shard_map/ppermute | solution.py:383
  4.3 9.9 %collective-permute-start.3 = (f32[576,128]{1,0:T(8,128)S(1)}, f32[576,128]{1,0:T(8,128)S(1)}, u32[]{:S(2)}, u32[]{:S(2)}) collective-permute-start(f32[576,128]{1,0:T(8,128)S(1)} %get-tuple-element.33), channel_id=1, source_target_pairs={{0,12},{4,8},{8,4},{12,0},{16,28},{20,24},{24,20},{28,16},{1,13},{... | collective-permute-start | bytes 884744 | tf_op jit(solution)/shard_map/ppermute | solution.py:383
  6.1 14.7 %collective-permute-start.2 = (f32[576,128]{1,0:T(8,128)S(1)}, f32[576,128]{1,0:T(8,128)S(1)}, u32[]{:S(2)}, u32[]{:S(2)}) collective-permute-start(f32[576,128]{1,0:T(8,128)S(1)} %get-tuple-element.34), channel_id=1, source_target_pairs={{0,8},{4,12},{8,0},{12,4},{16,24},{20,28},{24,16},{28,20},{1,9},{5... | collective-permute-start | bytes 884744 | tf_op jit(solution)/shard_map/ppermute | solution.py:383
  6.6 14.2 %collective-permute-start = (f32[576,128]{1,0:T(8,128)S(1)}, f32[576,128]{1,0:T(8,128)S(1)}, u32[]{:S(2)}, u32[]{:S(2)}) collective-permute-start(f32[576,128]{1,0:T(8,128)S(1)} %get-tuple-element.35), channel_id=1, source_target_pairs={{0,16},{4,20},{8,24},{12,28},{16,0},{20,4},{24,8},{28,12},{1,17},{... | collective-permute-start | bytes 884744 | tf_op jit(solution)/shard_map/ppermute | solution.py:383
  6.6 19.8 %collective-permute-start.5 = (f32[576,128]{1,0:T(8,128)S(1)}, f32[576,128]{1,0:T(8,128)S(1)}, u32[]{:S(2)}, u32[]{:S(2)}) collective-permute-start(f32[576,128]{1,0:T(8,128)S(1)} %get-tuple-element.31), channel_id=1, source_target_pairs={{0,24},{4,28},{8,16},{12,20},{16,8},{20,12},{24,0},{28,4},{1,25},{... | collective-permute-start | bytes 884744 | tf_op jit(solution)/shard_map/ppermute | solution.py:383
  11.7 19.1 %collective-permute-start.7 = (f32[576,128]{1,0:T(8,128)S(1)}, f32[576,128]{1,0:T(8,128)S(1)}, u32[]{:S(2)}, u32[]{:S(2)}) collective-permute-start(f32[576,128]{1,0:T(8,128)S(1)} %get-tuple-element.16), channel_id=1, source_target_pairs={{0,16},{4,20},{8,24},{12,28},{16,0},{20,4},{24,8},{28,12},{1,17},{... | collective-permute-start | bytes 884744 | tf_op jit(solution)/shard_map/ppermute | solution.py:383
  14.1 19.3 %collective-permute-start.9 = (f32[576,128]{1,0:T(8,128)S(1)}, f32[576,128]{1,0:T(8,128)S(1)}, u32[]{:S(2)}, u32[]{:S(2)}) collective-permute-start(f32[576,128]{1,0:T(8,128)S(1)} %get-tuple-element.18), channel_id=1, source_target_pairs={{0,8},{4,12},{8,0},{12,4},{16,24},{20,28},{24,16},{28,20},{1,9},{5... | collective-permute-start | bytes 884744 | tf_op jit(solution)/shard_map/ppermute | solution.py:383
  20.7 18.2 %collective-permute-start.6 = (f32[576,128]{1,0:T(8,128)S(1)}, f32[576,128]{1,0:T(8,128)S(1)}, u32[]{:S(2)}, u32[]{:S(2)}) collective-permute-start(f32[576,128]{1,0:T(8,128)S(1)} %get-tuple-element.15), channel_id=1, source_target_pairs={{0,28},{4,24},{8,20},{12,16},{16,12},{20,8},{24,4},{28,0},{1,29},{... | collective-permute-start | bytes 884744 | tf_op jit(solution)/shard_map/ppermute | solution.py:383
  20.8 19.9 %collective-permute-start.1 = (f32[576,128]{1,0:T(8,128)S(1)}, f32[576,128]{1,0:T(8,128)S(1)}, u32[]{:S(2)}, u32[]{:S(2)}) collective-permute-start(f32[576,128]{1,0:T(8,128)S(1)} %get-tuple-element.14), channel_id=1, source_target_pairs={{0,4},{4,0},{8,12},{12,8},{16,20},{20,16},{24,28},{28,24},{1,5},{5... | collective-permute-start | bytes 884744 | tf_op jit(solution)/shard_map/ppermute | solution.py:383
  26.4 20.4 %copy-start.2 = (f32[576,128]{1,0:T(8,128)}, f32[576,128]{1,0:T(8,128)S(1)}, u32[]{:S(2)}) copy-start(f32[576,128]{1,0:T(8,128)S(1)} %collective-permute-done.5.refs_6_.refs_14_) | copy-start | bytes 884740
  26.4 21.9 %collective-permute-start.10 = (f32[576,128]{1,0:T(8,128)}, f32[576,128]{1,0:T(8,128)S(1)}, u32[]{:S(2)}, u32[]{:S(2)}) collective-permute-start(f32[576,128]{1,0:T(8,128)} %get-tuple-element.19), channel_id=1, source_target_pairs={{0,12},{4,8},{8,4},{12,0},{16,28},{20,24},{24,20},{28,16},{1,13},{... | collective-permute-start | bytes 884744 | tf_op jit(solution)/shard_map/ppermute | solution.py:383
  30.8 16.0 %copy-start.10 = (f32[576,128]{1,0:T(8,128)}, f32[576,128]{1,0:T(8,128)S(1)}, u32[]{:S(2)}) copy-start(f32[576,128]{1,0:T(8,128)S(1)} %collective-permute-done.7.refs_4_) | copy-start | bytes 884740
  30.8 18.2 %collective-permute-start.8 = (f32[576,128]{1,0:T(8,128)}, f32[576,128]{1,0:T(8,128)S(1)}, u32[]{:S(2)}, u32[]{:S(2)}) collective-permute-start(f32[576,128]{1,0:T(8,128)} %get-tuple-element.17), channel_id=1, source_target_pairs={{0,4},{4,0},{8,12},{12,8},{16,20},{20,16},{24,28},{28,24},{1,5},{5... | collective-permute-start | bytes 884744 | tf_op jit(solution)/shard_map/ppermute | solution.py:383
  33.4 13.4 %copy-start.12 = (f32[576,128]{1,0:T(8,128)}, f32[576,128]{1,0:T(8,128)S(1)}, u32[]{:S(2)}) copy-start(f32[576,128]{1,0:T(8,128)S(1)} %collective-permute-done.9.refs_2_) | copy-start | bytes 884740
  33.4 18.3 %collective-permute-start.13 = (f32[576,128]{1,0:T(8,128)}, f32[576,128]{1,0:T(8,128)S(1)}, u32[]{:S(2)}, u32[]{:S(2)}) collective-permute-start(f32[576,128]{1,0:T(8,128)} %get-tuple-element.22), channel_id=1, source_target_pairs={{0,28},{4,24},{8,20},{12,16},{16,12},{20,8},{24,4},{28,0},{1,29},{... | collective-permute-start | bytes 884744 | tf_op jit(solution)/shard_map/ppermute | solution.py:383
  39.0 7.9 %copy-start.4 = (f32[576,128]{1,0:T(8,128)}, f32[576,128]{1,0:T(8,128)S(1)}, u32[]{:S(2)}) copy-start(f32[576,128]{1,0:T(8,128)S(1)} %collective-permute-done.6.refs_7_.refs_15_) | copy-start | bytes 884740
  39.0 22.0 %collective-permute-start.11 = (f32[576,128]{1,0:T(8,128)}, f32[576,128]{1,0:T(8,128)}, u32[]{:S(2)}, u32[]{:S(2)}) collective-permute-start(f32[576,128]{1,0:T(8,128)} %get-tuple-element.20), channel_id=1, source_target_pairs={{0,20},{4,16},{8,28},{12,24},{16,4},{20,0},{24,12},{28,8},{1,21},{... | collective-permute-start | bytes 884744 | tf_op jit(solution)/shard_map/ppermute | solution.py:383
  40.6 6.2 %copy-start.6 = (f32[576,128]{1,0:T(8,128)}, f32[576,128]{1,0:T(8,128)S(1)}, u32[]{:S(2)}) copy-start(f32[576,128]{1,0:T(8,128)S(1)} %collective-permute-done.1.refs_1_.refs_9_) | copy-start | bytes 884740
  40.6 20.3 %collective-permute-start.12 = (f32[576,128]{1,0:T(8,128)}, f32[576,128]{1,0:T(8,128)}, u32[]{:S(2)}, u32[]{:S(2)}) collective-permute-start(f32[576,128]{1,0:T(8,128)} %get-tuple-element.21), channel_id=1, source_target_pairs={{0,24},{4,28},{8,16},{12,20},{16,8},{20,12},{24,0},{28,4},{1,25},{... | collective-permute-start | bytes 884744 | tf_op jit(solution)/shard_map/ppermute | solution.py:383
  42.9 18.1 %copy-start.9 = (bf16[2048,128]{1,0:T(8,128)(2,1)S(1)}, bf16[2048,128]{1,0:T(8,128)(2,1)}, u32[]{:S(2)}) copy-start(bf16[2048,128]{1,0:T(8,128)(2,1)} %constant.46.clone.gather_ref) | copy-start | bytes 1572868
  42.9 18.1 %copy-start.20 = (f32[72,128]{1,0:T(8,128)S(1)}, f32[72,128]{1,0:T(8,128)}, u32[]{:S(2)}) copy-start(f32[72,128]{1,0:T(8,128)} %equal_ref.1) | copy-start | bytes 110596
  42.9 18.1 %copy-start.21 = (f32[8,128]{1,0:T(8,128)S(1)}, f32[8,128]{1,0:T(8,128)}, u32[]{:S(2)}) copy-start(f32[8,128]{1,0:T(8,128)} %constant.45.clone.sign_ref) | copy-start | bytes 12292
  46.9 1.4 %copy-start.1 = (f32[576,8,128]{2,1,0:T(8,128)}, f32[576,8,128]{2,1,0:T(8,128)S(1)}, u32[]{:S(2)}) copy-start(f32[576,8,128]{2,1,0:T(8,128)S(1)} %forward.1.lattice_ref) | copy-start | bytes 7077892
  48.3 0.7 copy-start.14
  49.0 0.7 copy-start.16
  51.7 0.7 copy-start.18
  61.0 1.0 copy-start.3
  62.0 1.0 copy-start.5
  62.9 1.0 copy-start.7
  63.9 1.0 copy-start.11
  64.9 1.0 copy-start.13
  65.8 1.0 copy-start.15
  66.8 1.0 copy-start.17
  67.7 1.0 copy-start.19
  68.7 32.7 %copy-start = (f32[64,72,128]{2,1,0:T(8,128)S(1)}, f32[64,72,128]{2,1,0:T(8,128)}, u32[]{:S(2)}) copy-start(f32[64,72,128]{2,1,0:T(8,128)} %green_ref.1) | copy-start | bytes 7077892
  91.7 4.0 %collective-permute-start.14 = (f32[72,128]{1,0:T(8,128)S(1)}, f32[72,128]{1,0:T(8,128)S(1)}, u32[]{:S(2)}, u32[]{:S(2)}) collective-permute-start(f32[72,128]{1,0:T(8,128)S(1)} %reduce_sum.19), channel_id=1, source_target_pairs={{0,1},{1,0},{2,3},{3,2},{4,5},{5,4},{6,7},{7,6},{8,9},{9,8},{10,11... | collective-permute-start | bytes 110600 | tf_op jit(solution)/shard_map/ppermute | solution.py:383
  95.7 4.9 %collective-permute-start.15 = (f32[72,128]{1,0:T(8,128)S(1)}, f32[72,128]{1,0:T(8,128)S(1)}, u32[]{:S(2)}, u32[]{:S(2)}) collective-permute-start(f32[72,128]{1,0:T(8,128)S(1)} %add.48), channel_id=1, source_target_pairs={{0,2},{1,3},{2,0},{3,1},{4,6},{5,7},{6,4},{7,5},{8,10},{9,11},{10,... | collective-permute-start | bytes 110600 | tf_op jit(solution)/shard_map/ppermute | solution.py:383
  101.4 1.0 copy-start.8

commit v2 on v1

v2 whole, which is shorter than its diff:
```python
import functools
import math

import jax
import jax.numpy as jnp
import ml_dtypes
import numpy as np
from jax import lax
from jax.experimental import pallas as pl
from jax.experimental.pallas import tpu as pltpu
from jax.sharding import PartitionSpec as P

SIDE = 24
BANDS = 8
ENTRIES = BANDS * BANDS
WIDTH = 2 * ENTRIES
TILE = 8
STEPS = 4

time_step = 0.1
hubbard = 1.0
quadrature = (0.375, 1.1666666, 0.9583333, 1.0)

LATE = 3
AHEAD = 3


def lane_sign(shape):
    lane = lax.broadcasted_iota(jnp.int32, shape, len(shape) - 1)
    return lane < ENTRIES


def swap(x):
    return pltpu.roll(x, ENTRIES, 1)


def roll_blocks(x, blocks):
    return x if blocks == 0 else pltpu.roll(x, WIDTH - BANDS * blocks, x.ndim - 1)


def tree_sum(terms):
    while len(terms) > 1:
        terms = [sum(terms[i : i + 2][1:], terms[i]) for i in range(0, len(terms), 2)]
    return terms[0]


def dft24(x, sign, low):
    root3 = jnp.where(low, -1.0, 1.0) * (sign * math.sqrt(3.0) / 2)
    turn = jnp.where(low, -1.0, 1.0) * float(sign)
    half = math.sqrt(0.5)
    turn_half = turn * half
    columns = [[None] * 8 for _ in range(3)]
    for n2 in range(8):
        x0, x1, x2 = (x[(8 * n1 + 3 * n2) % 24] for n1 in range(3))
        total = x1 + x2
        base = x0 - 0.5 * total
        spin = swap(x1 - x2) * root3
        columns[0][n2] = x0 + total
        columns[1][n2] = base + spin
        columns[2][n2] = base - spin
    out = [None] * 24
    for k1 in range(3):
        c = columns[k1]
        a0, a1 = c[0] + c[4], c[0] - c[4]
        a2, a3 = c[2] + c[6], c[2] - c[6]
        a4, a5 = c[1] + c[5], c[1] - c[5]
        a6, a7 = c[3] + c[7], c[3] - c[7]
        b0, b1 = a0 + a2, a0 - a2
        b2, b3 = a4 + a6, a4 - a6
        i_a3 = swap(a3) * turn
        i_b3 = swap(b3) * turn
        c0, c1 = a1 + i_a3, a1 - i_a3
        p = (a5 - a7) * half
        m = swap(a5 + a7) * turn_half
        e, f = p + m, p - m
        values = [b0 + b2, c0 + e, b1 + i_b3, c1 - f, b0 - b2, c0 - e, b1 - i_b3, c1 + f]
        for k2 in range(8):
            out[(16 * k1 + 9 * k2) % 24] = values[k2]
    return out


def load_line(ref, line):
    stride = ref.shape[0] // TILE
    return [ref[pl.ds(line * SIDE + k2, TILE, stride=stride), :] for k2 in range(SIDE)]


def fetch(place, steps, block_refs, held_ref, sems):
    copies = []
    for slot, (step, source) in enumerate(zip(steps, block_refs)):
        rows = held_ref.shape[1]
        if step == 0 and source.shape[0] != rows:
            source = source.at[pl.ds(pl.multiple_of(place * rows, TILE), rows)]
        copies.append(pltpu.make_async_copy(source, held_ref.at[slot], sems.at[slot]))
        copies[-1].start()
    return copies


def along_first(work_ref, sign, low, out_ref):
    def columns(pair, carry):
        both = (2 * pair, 2 * pair + 1)
        rows = [[work_ref[k1 * SIDE + column] for k1 in range(SIDE)] for column in both]
        values = [dft24(row, sign, low) for row in rows]
        for column, value in zip(both, values):
            for r1 in range(SIDE):
                out_ref[r1 * SIDE + column] = value[r1]
        return carry

    lax.fori_loop(0, SIDE // 2, columns, 0)


def roll_kernel(green_ref, greens_ref):
    def rolls(s, carry):
        green = green_ref[s]
        for j in range(STEPS):
            greens_ref[j, s] = roll_blocks(green, j)
        return carry

    lax.fori_loop(0, green_ref.shape[0], rolls, 0)


def forward_kernel(steps, parts, place_ref, *refs):
    block_refs, (lattice_ref, greens_ref, work_ref, held_ref, sems) = refs[: len(steps)], refs[len(steps) :]
    low = lane_sign((TILE, WIDTH))
    place = place_ref[0]
    copies = fetch(place, steps, block_refs, held_ref, sems)
    rows = held_ref.shape[1]
    lines = rows // (TILE * SIDE)
    for slot, step in enumerate(steps):
        copies[slot].wait()
        green_ref = held_ref.at[slot]
        owner = partner_of(place, step, parts)

        def along_second(i, carry):
            for r2, value in enumerate(dft24(load_line(green_ref, i), -1, low)):
                work_ref[(owner * lines + i) * SIDE + r2] = value
            return carry

        lax.fori_loop(0, lines, along_second, 0, unroll=lines <= 4)
        green = green_ref[...]
        spot = pl.ds(pl.multiple_of(owner * rows, TILE), rows)
        for j in range(STEPS):
            greens_ref[j, spot, :] = roll_blocks(green, j)
    along_first(work_ref, -1, low, lattice_ref)


def product_lines(steps, parts, place, lattice_ref, weights, screen_refs, held_ref, sems, work_ref):
    low = lane_sign((TILE, WIDTH))
    turn = jnp.where(low, -1.0, 1.0)
    copies = fetch(place, steps, screen_refs, held_ref, sems)
    lines = held_ref.shape[1] // (TILE * SIDE)
    for slot, step in enumerate(steps):
        copies[slot].wait()
        screen_ref = held_ref.at[slot]
        first = partner_of(place, step, parts) * lines

        def along_second(i, carry):
            rows = []
            for r2, value in enumerate(load_line(screen_ref, i)):
                screen = value * weights
                other = swap(screen)
                lattice = lattice_ref[(first + i) * SIDE + r2]
                rows.append(
                    swap(lattice) * turn * jnp.where(low, screen, other)
                    - lattice * jnp.where(low, other, screen)
                )
            for k2, value in enumerate(dft24(rows, 1, low)):
                work_ref[(first + i) * SIDE + k2] = value
            return carry

        lax.fori_loop(0, lines, along_second, 0, unroll=lines <= 4)


def early_kernel(steps, parts, place_ref, lattice_ref, weight_ref, *refs):
    screen_refs, (work_ref, held_ref, sems) = refs[: len(steps)], refs[len(steps) :]
    product_lines(
        steps, parts, place_ref[0], lattice_ref, weight_ref[...], screen_refs, held_ref, sems, work_ref
    )


def backward_kernel(
    steps, parts, share, place_ref, lattice_ref, weight_ref, equal_ref, sign_ref, gather_ref, greens_ref, *refs
):
    screen_refs, refs = refs[: len(steps)], refs[len(steps) :]
    _, partial_ref, work_ref, sigma_ref, sums_ref, pieces_ref, *late = refs
    points = SIDE * SIDE
    low = lane_sign((TILE, WIDTH))
    if steps:
        held_ref, sems = late
        product_lines(
            steps, parts, place_ref[0], lattice_ref, weight_ref[...], screen_refs, held_ref, sems, work_ref
        )
    sigma_at = sigma_ref.reshape(points, TILE, WIDTH)
    along_first(work_ref, 1, low, sigma_at)

    block = points // parts
    tiles = block // TILE
    batch = max(n for n in range(1, 10) if tiles % n == 0)

    def contract(group, carry):
        first = group * batch
        green_row = (first // tiles) * TILE * block + (first % tiles) * TILE
        units = [(tile, s) for tile in range(batch) for s in range(TILE)]

        def prepare(tile, s):
            sigma = sigma_ref[pl.ds((first + tile) * TILE * TILE + s, TILE, stride=TILE), :]
            row = pl.multiple_of(green_row + s * block + tile * TILE, TILE)
            return (
                [roll_blocks(sigma, STEPS * i) for i in range(STEPS)],
                [greens_ref[j, pl.ds(row, TILE), :] for j in range(STEPS)],
            )

        ready = [prepare(*unit) for unit in units[:AHEAD]]
        for n, (tile, s) in enumerate(units):
            if n + AHEAD < len(units):
                ready.append(prepare(*units[n + AHEAD]))
            sigmas, greens = ready.pop(0)
            terms = [sigma * green for sigma in sigmas for green in greens]
            sums = terms if s == 0 else [a + b for a, b in zip(sums, terms)]
            if s == TILE - 1:
                row = pl.ds(pl.multiple_of((first + tile) * TILE, TILE), TILE)
                for spot, value in enumerate(sums):
                    sums_ref[row, spot * WIDTH : (spot + 1) * WIDTH] = value
        return carry

    lax.fori_loop(0, points // (TILE * batch), contract, 0)

    lane = lax.broadcasted_iota(jnp.int32, equal_ref.shape, 1)
    inner = lane - ENTRIES
    occupied = jnp.sum(jnp.where((inner >= 0) & (inner % (BANDS + 1) == 0), equal_ref[...], 0.0))
    spots = lax.broadcasted_iota(jnp.int32, (points, WIDTH), 1)
    on_diagonal = (spots < ENTRIES) & (spots % (BANDS + 1) == 0)
    lower = spots < ENTRIES
    for pair in range(STEPS * STEPS // 2):
        first_part = sums_ref[:, 2 * pair * WIDTH : (2 * pair + 1) * WIDTH]
        second_part = sums_ref[:, (2 * pair + 1) * WIDTH : (2 * pair + 2) * WIDTH]
        folded = jnp.where(lower, first_part, second_part) + sign_ref[pair : pair + 1, :] * swap(
            jnp.where(lower, second_part, first_part)
        )
        coarse = folded.astype(jnp.bfloat16)
        fine = (folded - coarse.astype(jnp.float32)).astype(jnp.bfloat16)
        pieces_ref[:, 2 * pair * WIDTH : (2 * pair + 1) * WIDTH] = coarse
        pieces_ref[:, (2 * pair + 1) * WIDTH : (2 * pair + 2) * WIDTH] = fine
    total = jnp.dot(pieces_ref[...], gather_ref[...], preferred_element_type=jnp.float32)
    partial_ref[...] = total + jnp.where(on_diagonal, occupied * share, 0.0)


def propagate_kernel(greens_ref, effective_ref, spread_ref, out_ref, factor_ref, held_ref, sems):
    _, history, points, _ = greens_ref.shape
    rest = effective_ref[...] * time_step
    pieces = []
    for _ in range(3):
        pieces.append(rest.astype(jnp.bfloat16).astype(jnp.float32))
        rest = rest - pieces[-1]
    stacked = jnp.concatenate(pieces, axis=0).astype(jnp.bfloat16)
    spread = jnp.dot(stacked, spread_ref[...], preferred_element_type=jnp.float32)
    factor_ref[...] = tree_sum([spread[n * points : (n + 1) * points] for n in range(3)])

    slots, chunk = held_ref.shape[:2]

    def copy(number, slot):
        return pltpu.make_async_copy(
            held_ref.at[slot], out_ref.at[pl.ds(number * chunk, chunk)], sems.at[slot]
        )

    def advance(group, carry):
        for slot in range(slots):
            number = group * slots + slot

            @pl.when(group > 0)
            def _():
                copy(number - slots, slot).wait()

            times = pl.ds(number * chunk, chunk)
            for start in range(0, points, TILE):
                stop = min(start + TILE, points)
                greens = [greens_ref[j, times, start:stop, :] for j in range(STEPS)]
                terms = [greens[0]]
                for i in range(STEPS):
                    total = None
                    for j in range(STEPS):
                        spot = STEPS * i + j
                        factor = factor_ref[start:stop, spot * WIDTH : (spot + 1) * WIDTH]
                        term = factor[None] * greens[j]
                        total = term if total is None else total + term
                    terms.append(roll_blocks(total, STEPS * i))
                held_ref[slot, :, start:stop, :] = tree_sum(terms)
            copy(number, slot).start()
        return carry

    groups = history // (chunk * slots)
    lax.fori_loop(0, groups, advance, 0)
    for slot in range(slots):
        copy((groups - 1) * slots + slot, slot).wait()


def gather_tables():
    blocks = 2 * BANDS
    pairs = STEPS * STEPS // 2
    table = np.zeros((pairs, 2, blocks, BANDS, 2, BANDS, BANDS), np.float32)
    signs = np.zeros((pairs, blocks, BANDS), np.float32)
    for pair in range(pairs):
        for p in range(blocks):
            i, j = divmod(2 * pair + p // BANDS, STEPS)
            h, a = divmod((p + STEPS * i) % blocks, BANDS)
            g, c = divmod((p + j) % blocks, BANDS)
            table[pair, :, p, :, h ^ g, a, c] = 1 if (h, g) == (0, 1) else -1
            signs[pair, p] = 1 if h == g else -1
    return signs.reshape(pairs, WIDTH), table.reshape(-1, WIDTH).astype(ml_dtypes.bfloat16)


def spread_table():
    blocks = 2 * BANDS
    table = np.zeros((2, BANDS, BANDS, STEPS, STEPS, blocks, BANDS), np.float32)
    for i in range(STEPS):
        for j in range(STEPS):
            for p in range(blocks):
                h, a = divmod((p - STEPS * i) % blocks, BANDS)
                g, b = divmod((p + j) % blocks, BANDS)
                table[1 if h == g else 0, a, b, i, j, p, :] = -1 if (h, g) == (1, 0) else 1
    return table.reshape(WIDTH, -1).astype(ml_dtypes.bfloat16)


def in_vmem():
    return pl.BlockSpec(memory_space=pltpu.VMEM)


def in_smem():
    return pl.BlockSpec(memory_space=pltpu.SMEM)


def anywhere():
    return pl.BlockSpec(memory_space=pl.ANY)


def params(megabytes):
    return pltpu.CompilerParams(vmem_limit_bytes=megabytes * 1024 * 1024)


def cost(per_element, arrays):
    size = SIDE * SIDE * TILE * WIDTH
    return pl.CostEstimate(flops=per_element * size, bytes_accessed=4 * arrays * size, transcendentals=0)


def held_blocks(count, parts):
    return [
        pltpu.VMEM((count, TILE * SIDE * SIDE // parts, WIDTH), jnp.float32),
        pltpu.SemaphoreType.DMA((count,)),
    ]


def forward(place, greens, steps, parts):
    points = SIDE * SIDE
    return pl.pallas_call(
        functools.partial(forward_kernel, steps, parts),
        out_shape=[
            jax.ShapeDtypeStruct((points, TILE, WIDTH), jnp.float32),
            jax.ShapeDtypeStruct((STEPS, TILE * points, WIDTH), jnp.float32),
        ],
        in_specs=[in_smem()] + [anywhere()] * len(steps),
        out_specs=[in_vmem()] * 2,
        scratch_shapes=[pltpu.VMEM((points, TILE, WIDTH), jnp.float32)] + held_blocks(len(steps), parts),
        compiler_params=params(24),
        cost_estimate=cost(400, 6),
        name="forward",
    )(place, *greens)


def early_lines(place, lattice, weights, screens, steps, parts):
    points = SIDE * SIDE
    return pl.pallas_call(
        functools.partial(early_kernel, steps, parts),
        out_shape=jax.ShapeDtypeStruct((points, TILE, WIDTH), jnp.float32),
        in_specs=[in_smem(), in_vmem(), in_vmem()] + [anywhere()] * len(steps),
        out_specs=in_vmem(),
        scratch_shapes=held_blocks(len(steps), parts),
        compiler_params=params(16),
        cost_estimate=cost(150, 3),
        name="early",
    )(place, lattice, weights, *screens)


def backward(place, lattice, weights, equal_time, greens, screens, work, steps, parts, share):
    points = SIDE * SIDE
    signs, gather = gather_tables()
    inputs = (place, lattice, weights, equal_time, jnp.asarray(signs), jnp.asarray(gather), greens, *screens, work)
    partial_value, _ = pl.pallas_call(
        functools.partial(backward_kernel, steps, parts, share),
        out_shape=[
            jax.ShapeDtypeStruct((points, WIDTH), jnp.float32),
            jax.ShapeDtypeStruct((points, TILE, WIDTH), jnp.float32),
        ],
        in_specs=[in_smem()] + [in_vmem()] * 6 + [anywhere()] * len(steps) + [in_vmem()],
        out_specs=[in_vmem()] * 2,
        input_output_aliases={len(inputs) - 1: 1},
        scratch_shapes=[
            pltpu.VMEM((TILE * points, WIDTH), jnp.float32),
            pltpu.VMEM((points, STEPS * STEPS * WIDTH), jnp.float32),
            pltpu.VMEM((points, STEPS * STEPS * WIDTH), jnp.bfloat16),
        ]
        + (held_blocks(len(steps), parts) if steps else []),
        compiler_params=params(36),
        cost_estimate=cost(800, 6),
        name="backward",
    )(*inputs)
    return partial_value


def roll_own(greens):
    return pl.pallas_call(
        roll_kernel,
        out_shape=jax.ShapeDtypeStruct((STEPS, *greens.shape), jnp.float32),
        in_specs=[in_vmem()],
        out_specs=in_vmem(),
        compiler_params=params(24),
        cost_estimate=cost(3, 5),
        name="roll_own",
    )(greens)


def propagate(greens, effective):
    _, history, points, width = greens.shape
    chunk = math.gcd(history // 2, TILE)
    spread = spread_table()
    return pl.pallas_call(
        propagate_kernel,
        out_shape=jax.ShapeDtypeStruct(greens.shape[1:], jnp.float32),
        in_specs=[in_vmem()] * 3,
        out_specs=anywhere(),
        scratch_shapes=[
            pltpu.VMEM((points, spread.shape[1]), jnp.float32),
            pltpu.VMEM((2, chunk, points, width), jnp.float32),
            pltpu.SemaphoreType.DMA((2,)),
        ],
        compiler_params=params(24),
        cost_estimate=cost(32, 5),
        name="propagate",
    )(greens, effective, jnp.asarray(spread))


def partner_of(place, step, count):
    if count == 1:
        return 0
    if count & (count - 1) == 0:
        return place ^ step
    return (place + step) % count


def exchange(value, axis, step, count):
    pairs = [(place, partner_of(place, step, count)) for place in range(count)]
    return lax.ppermute(value, axis, pairs)


def exchange_order(count):
    along = {}
    for step in range(1, count):
        along.setdefault(step // 2, []).append(step)
    single = [along[n] for n in along if n and n & (n - 1) == 0]
    mixed = [along[n] for n in along if n & (n - 1)]
    order = along[0] + [step for steps in zip(*single) for step in steps]
    return order + [step for steps in mixed for step in steps]


def class_weights(quad_class):
    table = jnp.array(quadrature, jnp.float32)
    match = quad_class[:, None] == jnp.arange(4, dtype=jnp.int32)[None, :]
    return jnp.sum(jnp.where(match, table[None, :], jnp.float32(0.0)), axis=1)


def per_device(parts, blocks, green_row, screened, hamilton, equal_time, quad_class, live_count):
    history, local, width = green_row.shape
    points = local * parts
    times = history // parts
    place = lax.axis_index("ka")
    position = jnp.arange(history, dtype=jnp.int32)
    weights = jnp.where(
        position < live_count[0], time_step * class_weights(quad_class), jnp.float32(0.0)
    ) * jnp.float32(1.0 / points)
    weights = lax.dynamic_slice_in_dim(weights, place * times, times)

    if times == TILE and local % SIDE == 0:
        groups, sources = 1, parts
        order = exchange_order(parts)
        moved = []
        for x in (green_row, screened):
            whole = x.reshape(parts * TILE * local, width)
            found = {0: whole}
            for step in order:
                start = partner_of(place, step, parts) * (TILE * local)
                block = lax.dynamic_slice_in_dim(whole, start, TILE * local)
                found[step] = exchange(block, "ka", step, parts)
            moved.append([found])
        order = [0] + order
    else:
        groups, sources = -(-times // TILE), 1
        order = [0]
        padding = groups * TILE - times
        moved = []
        for x in (green_row, screened):
            x = lax.all_to_all(x, "ka", split_axis=0, concat_axis=0, tiled=True)
            x = x.reshape(parts, times, local, width).transpose(1, 0, 2, 3).reshape(times, points, width)
            x = jnp.pad(x, ((0, padding), (0, 0), (0, 0))).reshape(groups, TILE * points, width)
            moved.append([{0: x[group]} for group in range(groups)])
        weights = jnp.pad(weights, (0, padding))
    weights = jnp.broadcast_to(weights.reshape(groups, TILE, 1), (groups, TILE, width))

    early = order[: max(1, len(order) - LATE)]
    late = order[len(early) :]
    seat = place.reshape(1)
    partial_value = None
    for group in range(groups):
        green, screen = moved[0][group], moved[1][group]
        lattice, greens = forward(seat, [green[step] for step in order], order, sources)
        work = early_lines(seat, lattice, weights[group], [screen[step] for step in early], early, sources)
        share = hubbard / (points * blocks) if group == 0 else 0.0
        term = backward(
            seat, lattice, weights[group], equal_time, greens, [screen[step] for step in late], work,
            late, sources, share,
        )
        partial_value = term if partial_value is None else partial_value + term
    own_greens = roll_own(green_row)

    owners = [partner_of(place, step, parts) for step in range(parts)]
    pieces = [lax.dynamic_slice_in_dim(partial_value, owner * local, local) for owner in owners]
    if parts % 2 == 0 and parts & (parts - 1) == 0:
        pairs = jnp.concatenate([pieces[step] for step in range(1, parts, 2)], axis=0)
        pairs = exchange(pairs, "ka", 1, parts)
        mine = jnp.concatenate([pieces[step] for step in range(0, parts, 2)], axis=0) + pairs
        pieces = [mine[n * local : (n + 1) * local] for n in range(parts // 2)]
        collision = tree_sum(
            pieces[:1] + [exchange(pieces[n], "ka", 2 * n, parts) for n in range(1, parts // 2)]
        )
    else:
        collision = tree_sum(
            pieces[:1] + [exchange(pieces[step], "ka", step, parts) for step in range(1, parts)]
        )
    collision = tree_sum(
        [collision] + [exchange(collision, "hist", step, blocks) for step in range(1, blocks)]
    )
    return propagate(own_greens, hamilton + collision)


def solution(mesh):
    in_specs = (
        P("hist", "ka", None),
        P("hist", "ka", None),
        P("ka", None),
        P("ka", None),
        P("hist"),
        P("hist"),
    )
    out_specs = P("hist", "ka", None)
    return jax.shard_map(
        functools.partial(per_device, mesh.shape["ka"], mesh.shape["hist"]),
        mesh=mesh,
        in_specs=in_specs,
        out_specs=out_specs,
        check_vma=False,
    )
```

time: 109 us -> 94.5 us (0.87)
  blocking collectives: 9.66 us -> 0 us
  waiting for transfers between devices: 36.7 us -> 30.2 us
  local copies, waits for them, and re-layouts: 15.4 us -> 9.82 us
  Pallas kernels: 23.7 us -> 27.7 us
  starting transfers between devices: 21.7 us -> 25.4 us
    all_to_all x1 -> x0, blocking collectives: 9.66 us -> none  [per_device(): lax.all_to_all(partial_value.reshape(parts, local, width), 'ka', split_ax...]
    ppermute x16 -> x21, waiting for transfers between devices: 36.7 us -> 30.2 us  [exchange(): return lax.ppermute(value, axis, pairs)]
    unnamed x50 -> x40, local copies, waits for them, and re-layouts: 12.3 us -> 6.67 us
    pallas_call x3 -> x5, Pallas kernels: 23.7 us -> 27.7 us  [the longest x1 8.18 us: backward(): pl.pallas_call(functools.partial(backward_kernel, steps, parts, share), o...]
    ppermute x16 -> x21, starting transfers between devices: 21.7 us -> 25.4 us  [exchange(): return lax.ppermute(value, axis, pairs)]
  transfers between devices with their start and end apart: 16 -> 21, of which waited for: 10 -> 9; matrix products, arithmetic and copies ran while one was open for 1% -> 1% of each run, Pallas kernels for 4% -> 15%
where the time goes in v2:
time: 94.5 us; the launch traced here: 94.3 us
  waiting for transfers between devices  30.2 us (32%)
  Pallas kernels  27.7 us (29%)
  starting transfers between devices  25.4 us (27%)
  local copies, waits for them, and re-layouts  9.82 us (10%)
    ppermute x21, waiting for transfers between devices, exchange(): return lax.ppermute(value, axis, pairs)  30.2 us
    ppermute x21, starting transfers between devices, exchange(): return lax.ppermute(value, axis, pairs)  25.4 us
    pallas_call x1, Pallas kernels, backward(): pl.pallas_call(functools.partial(backward_kernel, steps, parts, share), o...  8.18 us
    unnamed x40, local copies, waits for them, and re-layouts  6.67 us
    pallas_call x1, Pallas kernels, roll_own(): pl.pallas_call(roll_kernel, out_shape=jax.ShapeDtypeStruct((STEPS, *green...  6.12 us
    pallas_call x1, Pallas kernels, forward(): pl.pallas_call(functools.partial(forward_kernel, steps, parts), out_shape...  5.79 us
    pallas_call x1, Pallas kernels, propagate(): pl.pallas_call(propagate_kernel, out_shape=jax.ShapeDtypeStruct(greens.sh...  5.4 us
    dynamic_slice x2, local copies, waits for them, and re-layouts, per_device(): block = lax.dynamic_slice_in_dim(whole, start, TILE * local)  2.94 us
  transfers between devices with their start and end apart: 21, of which 9 were waited for; matrix products, arithmetic and copies ran while one was open for 1% of the time, Pallas kernels for 15%

profile of v2, /device:TPU:0, one launch (start us, length us, event | category | flops | bytes accessed | tf_op | source)
XLA Modules:
  0.0 94.3 jit_solution(1103179594971544542)
XLA Ops:
  0.0 1.8 %constant_dynamic-slice_fusion.15 = (f32[576,128]{1,0:T(8,128)S(1)}, f32[576,128]{1,0:T(8,128)S(1)}, f32[576,128]{1,0:T(8,128)S(1)}, f32[576,128]{1,0:T(8,128)S(...) fusion(f32[4608,128]{1,0:T(8,128)} %bitcast.5, s32[]{:T(128)S(6)} %select_n.69, ...), kind=kLoop, calls=%fused_computation.20 | loop fusion | bytes 4128796 | tf_op jit(solution)/shard_map/dynamic_slice | solution.py:489
  1.8 0.5 collective-permute-start
  2.4 2.6 %collective-permute-start.1 = (f32[576,128]{1,0:T(8,128)S(1)}, f32[576,128]{1,0:T(8,128)S(1)}, u32[]{:S(2)}, u32[]{:S(2)}) collective-permute-start(f32[576,128]{1,0:T(8,128)S(1)} %get-tuple-element.23), channel_id=1, source_target_pairs={{0,8},{4,12},{8,0},{12,4},{16,24},{20,28},{24,16},{28,20},{1,9},{5... | collective-permute-start | bytes 884744 | tf_op jit(solution)/shard_map/ppermute | solution.py:450
  4.9 1.5 %collective-permute-start.2 = (f32[576,128]{1,0:T(8,128)S(1)}, f32[576,128]{1,0:T(8,128)S(1)}, u32[]{:S(2)}, u32[]{:S(2)}) collective-permute-start(f32[576,128]{1,0:T(8,128)S(1)} %get-tuple-element.22), channel_id=1, source_target_pairs={{0,16},{4,20},{8,24},{12,28},{16,0},{20,4},{24,8},{28,12},{1,17},{... | collective-permute-start | bytes 884744 | tf_op jit(solution)/shard_map/ppermute | solution.py:450
  6.4 0.0 collective-permute-start.3
  6.5 0.3 collective-permute-start.4
  6.7 1.2 %constant_dynamic-slice_fusion.8 = (f32[576,128]{1,0:T(8,128)}, f32[576,128]{1,0:T(8,128)}, f32[576,128]{1,0:T(8,128)S(1)}, f32[576,128]{1,0:T(8,128)S(1)}, f32[...) fusion(f32[4608,128]{1,0:T(8,128)S(1)} %bitcast.7, s32[]{:T(128)S(6)} %select_n.66, s32[]{:T(128)S(6)} %select_n.65, ...), kind=kLoop, calls=%fused_computation.13 | loop fusion | bytes 4128796 | tf_op jit(solution)/shard_map/dynamic_slice | solution.py:489
  7.9 2.9 %collective-permute-start.5 = (f32[576,128]{1,0:T(8,128)S(1)}, f32[576,128]{1,0:T(8,128)S(1)}, u32[]{:S(2)}, u32[]{:S(2)}) collective-permute-start(f32[576,128]{1,0:T(8,128)S(1)} %get-tuple-element.19), channel_id=1, source_target_pairs={{0,24},{4,28},{8,16},{12,20},{16,8},{20,12},{24,0},{28,4},{1,25},{... | collective-permute-start | bytes 884744 | tf_op jit(solution)/shard_map/ppermute | solution.py:450
  10.8 2.0 %collective-permute-done.1.refs_2_ = f32[576,128]{1,0:T(8,128)S(1)} collective-permute-done((f32[576,128]{1,0:T(8,128)S(1)}, f32[576,128]{1,0:T(8,128)S(1)}, u32[]{:S(2)}, u32[]{:S(2)}) %collective-permute-start.1) | collective-permute-done | bytes 294944 | tf_op jit(solution)/shard_map/ppermute | solution.py:450
  12.8 1.7 %collective-permute-start.6 = (f32[576,128]{1,0:T(8,128)S(1)}, f32[576,128]{1,0:T(8,128)S(1)}, u32[]{:S(2)}, u32[]{:S(2)}) collective-permute-start(f32[576,128]{1,0:T(8,128)S(1)} %get-tuple-element.18), channel_id=1, source_target_pairs={{0,28},{4,24},{8,20},{12,16},{16,12},{20,8},{24,4},{28,0},{1,29},{... | collective-permute-start | bytes 884744 | tf_op jit(solution)/shard_map/ppermute | solution.py:450
  14.5 0.3 collective-permute-done.2.refs_3_
  14.8 1.0 %collective-permute-start.10 = (f32[576,128]{1,0:T(8,128)S(1)}, f32[576,128]{1,0:T(8,128)S(1)}, u32[]{:S(2)}, u32[]{:S(2)}) collective-permute-start(f32[576,128]{1,0:T(8,128)S(1)} %get-tuple-element.14), channel_id=1, source_target_pairs={{0,4},{4,0},{8,12},{12,8},{16,20},{20,16},{24,28},{28,24},{1,5},{5... | collective-permute-start | bytes 884744 | tf_op jit(solution)/shard_map/ppermute | solution.py:450
  15.8 2.8 %collective-permute-done.3.refs_4_ = f32[576,128]{1,0:T(8,128)S(1)} collective-permute-done((f32[576,128]{1,0:T(8,128)S(1)}, f32[576,128]{1,0:T(8,128)S(1)}, u32[]{:S(2)}, u32[]{:S(2)}) %collective-permute-start.3) | collective-permute-done | bytes 294944 | tf_op jit(solution)/shard_map/ppermute | solution.py:450
  18.6 1.6 %collective-permute-start.11 = (f32[576,128]{1,0:T(8,128)S(1)}, f32[576,128]{1,0:T(8,128)S(1)}, u32[]{:S(2)}, u32[]{:S(2)}) collective-permute-start(f32[576,128]{1,0:T(8,128)S(1)} %get-tuple-element.13), channel_id=1, source_target_pairs={{0,8},{4,12},{8,0},{12,4},{16,24},{20,28},{24,16},{28,20},{1,9},{5... | collective-permute-start | bytes 884744 | tf_op jit(solution)/shard_map/ppermute | solution.py:450
  20.1 11.9 %collective-permute-done.4.refs_5_ = f32[576,128]{1,0:T(8,128)S(1)} collective-permute-done((f32[576,128]{1,0:T(8,128)S(1)}, f32[576,128]{1,0:T(8,128)S(1)}, u32[]{:S(2)}, u32[]{:S(2)}) %collective-permute-start.4) | collective-permute-done | bytes 294944 | tf_op jit(solution)/shard_map/ppermute | solution.py:450
  32.0 0.7 copy-done.5
  32.7 1.7 %collective-permute-start.12 = (f32[576,128]{1,0:T(8,128)}, f32[576,128]{1,0:T(8,128)}, u32[]{:S(2)}, u32[]{:S(2)}) collective-permute-start(f32[576,128]{1,0:T(8,128)} %get-tuple-element.12), channel_id=1, source_target_pairs={{0,16},{4,20},{8,24},{12,28},{16,0},{20,4},{24,8},{28,12},{1,17},{... | collective-permute-start | bytes 884744 | tf_op jit(solution)/shard_map/ppermute | solution.py:450
  34.4 0.7 copy-done.7
  35.1 0.3 collective-permute-start.13
  35.4 0.7 copy-done.9
  36.1 0.2 collective-permute-start.7
  36.4 0.7 copy-done.11
  37.1 2.7 %collective-permute-start.8 = (f32[576,128]{1,0:T(8,128)}, f32[576,128]{1,0:T(8,128)}, u32[]{:S(2)}, u32[]{:S(2)}) collective-permute-start(f32[576,128]{1,0:T(8,128)} %get-tuple-element.16), channel_id=1, source_target_pairs={{0,24},{4,28},{8,16},{12,20},{16,8},{20,12},{24,0},{28,4},{1,25},{... | collective-permute-start | bytes 884744 | tf_op jit(solution)/shard_map/ppermute | solution.py:450
  39.8 0.7 copy-done.13
  40.5 0.2 collective-permute-start.9
  40.7 0.1 select_reduce_fusion
  41.5 0.1 dynamic_slice.76
  41.6 1.1 %copy-done.6 = f32[576,128]{1,0:T(8,128)S(1)} copy-done((f32[576,128]{1,0:T(8,128)S(1)}, f32[576,128]{1,0:T(8,128)}, u32[]{:S(2)}) %copy-start.6) | copy-done | bytes 294936
  42.7 1.0 %copy-done.8 = f32[576,128]{1,0:T(8,128)S(1)} copy-done((f32[576,128]{1,0:T(8,128)S(1)}, f32[576,128]{1,0:T(8,128)}, u32[]{:S(2)}) %copy-start.8) | copy-done | bytes 294936
  43.6 1.0 %copy-done.10 = f32[576,128]{1,0:T(8,128)S(1)} copy-done((f32[576,128]{1,0:T(8,128)S(1)}, f32[576,128]{1,0:T(8,128)}, u32[]{:S(2)}) %copy-start.10) | copy-done | bytes 294936
  44.6 5.8 %forward.1 = (f32[576,8,128]{2,1,0:T(8,128)S(1)}, f32[4,4608,128]{2,1,0:T(8,128)S(1)}) custom-call(s32[1]{0:T(128)} %bitcast.place_ref, f32[4608,128]{1,0:T(8,128)S(1)} %bitcast.6, f32[576,128]{1,0:T(8,128)S(1)} %collective-permute-done.refs_1_, f32[576,128]{1,0:T(8,128)S(1)} %collective-permute-done.1.refs_2_, ...), custom_call_target="tpu_custom_call" | custom-call | flops 235929600 | bytes 14155776 | tf_op jit(solution)/shard_map/forward/pallas_call | solution.py:353
  50.4 0.1 squeeze.8.weight_ref
  50.5 2.2 %early.1.refs_3_ = f32[576,8,128]{2,1,0:T(8,128)S(1)} custom-call(s32[1]{0:T(128)} %bitcast.place_ref, f32[576,8,128]{2,1,0:T(8,128)S(1)} %get-tuple-element.8.lattice_ref, f32[8,128]{1,0:T(8,128)S(1)} %squeeze.8.weight_ref, f32[4608,128]{1,0:T(8,128)S(1)} %bitcast.8, f32[576,128]{1,0:T(8,128)S(1)} %copy-done.12, f32[576,128]{1,0:T(8,128)S(1)} %copy-done.14, ...), custom_call_target="tpu_custom_call" | custom-call | flops 88473600 | bytes 7077888 | tf_op jit(solution)/shard_map/early/pallas_call | solution.py:370
  52.8 8.9 %collective-permute-done.7.refs_0_ = f32[576,128]{1,0:T(8,128)} collective-permute-done((f32[576,128]{1,0:T(8,128)}, f32[576,128]{1,0:T(8,128)}, u32[]{:S(2)}, u32[]{:S(2)}) %collective-permute-start.7) | collective-permute-done | bytes 294944 | tf_op jit(solution)/shard_map/ppermute | solution.py:450
  61.7 8.2 %backward.1 = (f32[576,128]{1,0:T(8,128)S(1)}, f32[576,8,128]{2,1,0:T(8,128)S(1)}) custom-call(s32[1]{0:T(128)} %bitcast.place_ref, f32[576,8,128]{2,1,0:T(8,128)S(1)} %get-tuple-element.8.lattice_ref, f32[8,128]{1,0:T(8,128)S(1)} %squeeze.8.weight_ref, f32[72,128]{1,0:T(8,128)S(1)} %copy-done.15, ...), custom_call_target="tpu_custom_call", output_to_operand_aliasing={{1}: (10, {})} | custom-call | flops 471859200 | bytes 14155776 | tf_op jit(solution)/shard_map/backward/pallas_call | solution.py:386
  69.9 0.2 collective-permute-start.14
  70.1 1.3 %collective-permute-done.14 = f32[288,128]{1,0:T(8,128)S(1)} collective-permute-done((f32[288,128]{1,0:T(8,128)S(1)}, f32[288,128]{1,0:T(8,128)S(1)}, u32[]{:S(2)}, u32[]{:S(2)}) %collective-permute-start.14) | collective-permute-done | bytes 147488 | tf_op jit(solution)/shard_map/ppermute | solution.py:450
  71.4 0.1 collective-permute-start.15
  71.5 1.9 %collective-permute-start.16 = (f32[72,128]{1,0:T(8,128)S(1)}, f32[72,128]{1,0:T(8,128)S(1)}, u32[]{:S(2)}, u32[]{:S(2)}) collective-permute-start(f32[72,128]{1,0:T(8,128)S(1)} %get-tuple-element.34), channel_id=1, source_target_pairs={{0,16},{4,20},{8,24},{12,28},{16,0},{20,4},{24,8},{28,12},{1,17},{... | collective-permute-start | bytes 110600 | tf_op jit(solution)/shard_map/ppermute | solution.py:450
  73.3 1.6 %collective-permute-start.17 = (f32[72,128]{1,0:T(8,128)S(1)}, f32[72,128]{1,0:T(8,128)S(1)}, u32[]{:S(2)}, u32[]{:S(2)}) collective-permute-start(f32[72,128]{1,0:T(8,128)S(1)} %get-tuple-element.33), channel_id=1, source_target_pairs={{0,24},{4,28},{8,16},{12,20},{16,8},{20,12},{24,0},{28,4},{1,25},{... | collective-permute-start | bytes 110600 | tf_op jit(solution)/shard_map/ppermute | solution.py:450
  75.0 0.5 collective-permute-done.15
  75.4 0.1 collective-permute-done.16
  75.5 2.7 %collective-permute-done.17 = f32[72,128]{1,0:T(8,128)S(1)} collective-permute-done((f32[72,128]{1,0:T(8,128)S(1)}, f32[72,128]{1,0:T(8,128)S(1)}, u32[]{:S(2)}, u32[]{:S(2)}) %collective-permute-start.17) | collective-permute-done | bytes 36896 | tf_op jit(solution)/shard_map/ppermute | solution.py:450
  78.2 1.7 %collective-permute-start.18 = (f32[72,128]{1,0:T(8,128)S(1)}, f32[72,128]{1,0:T(8,128)S(1)}, u32[]{:S(2)}, u32[]{:S(2)}) collective-permute-start(f32[72,128]{1,0:T(8,128)S(1)} %fusion), channel_id=1, source_target_pairs={{0,1},{1,0},{2,3},{3,2},{4,5},{5,4},{6,7},{7,6},{8,9},{9,8},{10,11... | collective-permute-start | bytes 110600 | tf_op jit(solution)/shard_map/ppermute | solution.py:450
  79.9 2.6 %collective-permute-start.19 = (f32[72,128]{1,0:T(8,128)S(1)}, f32[72,128]{1,0:T(8,128)S(1)}, u32[]{:S(2)}, u32[]{:S(2)}) collective-permute-start(f32[72,128]{1,0:T(8,128)S(1)} %fusion), channel_id=1, source_target_pairs={{0,2},{1,3},{2,0},{3,1},{4,6},{5,7},{6,4},{7,5},{8,10},{9,11},{10,... | collective-permute-start | bytes 110600 | tf_op jit(solution)/shard_map/ppermute | solution.py:450
  82.5 0.2 collective-permute-start.20
  82.7 6.1 %roll_own.1.greens_ref = f32[4,64,72,128]{3,2,1,0:T(8,128)S(1)} custom-call(f32[64,72,128]{2,1,0:T(8,128)S(1)} %copy-done), custom_call_target="tpu_custom_call" | custom-call | flops 1769472 | bytes 11796480 | tf_op jit(solution)/shard_map/roll_own/pallas_call | solution.py:409
  88.9 5.4 %propagate.1 = f32[64,72,128]{2,1,0:T(8,128)} custom-call(f32[4,64,72,128]{3,2,1,0:T(8,128)S(1)} %roll_own.1.greens_ref, f32[72,128]{1,0:T(8,128)S(1)} %add_add_fusion.effective_ref, bf16[128,2048]{1,0:T(8,128)(2,1)S(1)} %copy-done.3), custom_call_target="tpu_custom_call" | custom-call | flops 18874368 | bytes 11796480 | tf_op jit(solution)/shard_map/propagate/pallas_call | solution.py:424
  (51 shorter events, 0.2 us)
Async XLA Ops:
  0.0 6.7 %copy-start.1 = (f32[64,72,128]{2,1,0:T(8,128)S(1)}, f32[64,72,128]{2,1,0:T(8,128)}, u32[]{:S(2)}) copy-start(f32[64,72,128]{2,1,0:T(8,128)} %param.11) | copy-start | bytes 7077892
  1.8 38.9 %copy-start.18 = (s32[64]{0:T(128)S(1)}, s32[64]{0:T(128)}, u32[]{:S(2)}) copy-start(s32[64]{0:T(128)} %param.14) | copy-start | bytes 772
  1.8 38.9 %copy-start.19 = (f32[4]{0:T(128)S(1)}, f32[4]{0:T(128)}, u32[]{:S(2)}) copy-start(f32[4]{0:T(128)} %constant.46.clone) | copy-start | bytes 52
  1.8 39.7 %copy-start = (f32[64,72,128]{2,1,0:T(8,128)S(1)}, f32[64,72,128]{2,1,0:T(8,128)}, u32[]{:S(2)}) copy-start(f32[64,72,128]{2,1,0:T(8,128)} %green_ref.1) | copy-start | bytes 7077892
  1.8 6.1 %collective-permute-start = (f32[576,128]{1,0:T(8,128)S(1)}, f32[576,128]{1,0:T(8,128)S(1)}, u32[]{:S(2)}, u32[]{:S(2)}) collective-permute-start(f32[576,128]{1,0:T(8,128)S(1)} %get-tuple-element.24), channel_id=1, source_target_pairs={{0,4},{4,0},{8,12},{12,8},{16,20},{20,16},{24,28},{28,24},{1,5},{5... | collective-permute-start | bytes 884744 | tf_op jit(solution)/shard_map/ppermute | solution.py:450
  2.4 10.4 %collective-permute-start.1 = (f32[576,128]{1,0:T(8,128)S(1)}, f32[576,128]{1,0:T(8,128)S(1)}, u32[]{:S(2)}, u32[]{:S(2)}) collective-permute-start(f32[576,128]{1,0:T(8,128)S(1)} %get-tuple-element.23), channel_id=1, source_target_pairs={{0,8},{4,12},{8,0},{12,4},{16,24},{20,28},{24,16},{28,20},{1,9},{5... | collective-permute-start | bytes 884744 | tf_op jit(solution)/shard_map/ppermute | solution.py:450
  4.9 9.9 %collective-permute-start.2 = (f32[576,128]{1,0:T(8,128)S(1)}, f32[576,128]{1,0:T(8,128)S(1)}, u32[]{:S(2)}, u32[]{:S(2)}) collective-permute-start(f32[576,128]{1,0:T(8,128)S(1)} %get-tuple-element.22), channel_id=1, source_target_pairs={{0,16},{4,20},{8,24},{12,28},{16,0},{20,4},{24,8},{28,12},{1,17},{... | collective-permute-start | bytes 884744 | tf_op jit(solution)/shard_map/ppermute | solution.py:450
  6.4 12.1 %collective-permute-start.3 = (f32[576,128]{1,0:T(8,128)S(1)}, f32[576,128]{1,0:T(8,128)S(1)}, u32[]{:S(2)}, u32[]{:S(2)}) collective-permute-start(f32[576,128]{1,0:T(8,128)S(1)} %get-tuple-element.21), channel_id=1, source_target_pairs={{0,12},{4,8},{8,4},{12,0},{16,28},{20,24},{24,20},{28,16},{1,13},{... | collective-permute-start | bytes 884744 | tf_op jit(solution)/shard_map/ppermute | solution.py:450
  6.5 25.5 %collective-permute-start.4 = (f32[576,128]{1,0:T(8,128)S(1)}, f32[576,128]{1,0:T(8,128)S(1)}, u32[]{:S(2)}, u32[]{:S(2)}) collective-permute-start(f32[576,128]{1,0:T(8,128)S(1)} %get-tuple-element.20), channel_id=1, source_target_pairs={{0,20},{4,16},{8,28},{12,24},{16,4},{20,0},{24,12},{28,8},{1,21},{... | collective-permute-start | bytes 884744 | tf_op jit(solution)/shard_map/ppermute | solution.py:450
  7.9 26.5 %collective-permute-start.5 = (f32[576,128]{1,0:T(8,128)S(1)}, f32[576,128]{1,0:T(8,128)S(1)}, u32[]{:S(2)}, u32[]{:S(2)}) collective-permute-start(f32[576,128]{1,0:T(8,128)S(1)} %get-tuple-element.19), channel_id=1, source_target_pairs={{0,24},{4,28},{8,16},{12,20},{16,8},{20,12},{24,0},{28,4},{1,25},{... | collective-permute-start | bytes 884744 | tf_op jit(solution)/shard_map/ppermute | solution.py:450
  12.8 22.6 %collective-permute-start.6 = (f32[576,128]{1,0:T(8,128)S(1)}, f32[576,128]{1,0:T(8,128)S(1)}, u32[]{:S(2)}, u32[]{:S(2)}) collective-permute-start(f32[576,128]{1,0:T(8,128)S(1)} %get-tuple-element.18), channel_id=1, source_target_pairs={{0,28},{4,24},{8,20},{12,16},{16,12},{20,8},{24,4},{28,0},{1,29},{... | collective-permute-start | bytes 884744 | tf_op jit(solution)/shard_map/ppermute | solution.py:450
  14.8 21.6 %collective-permute-start.10 = (f32[576,128]{1,0:T(8,128)S(1)}, f32[576,128]{1,0:T(8,128)S(1)}, u32[]{:S(2)}, u32[]{:S(2)}) collective-permute-start(f32[576,128]{1,0:T(8,128)S(1)} %get-tuple-element.14), channel_id=1, source_target_pairs={{0,4},{4,0},{8,12},{12,8},{16,20},{20,16},{24,28},{28,24},{1,5},{5... | collective-permute-start | bytes 884744 | tf_op jit(solution)/shard_map/ppermute | solution.py:450
  18.6 21.2 %collective-permute-start.11 = (f32[576,128]{1,0:T(8,128)S(1)}, f32[576,128]{1,0:T(8,128)S(1)}, u32[]{:S(2)}, u32[]{:S(2)}) collective-permute-start(f32[576,128]{1,0:T(8,128)S(1)} %get-tuple-element.13), channel_id=1, source_target_pairs={{0,8},{4,12},{8,0},{12,4},{16,24},{20,28},{24,16},{28,20},{1,9},{5... | collective-permute-start | bytes 884744 | tf_op jit(solution)/shard_map/ppermute | solution.py:450
  32.0 0.7 copy-start.5
  32.7 17.7 %collective-permute-start.12 = (f32[576,128]{1,0:T(8,128)}, f32[576,128]{1,0:T(8,128)}, u32[]{:S(2)}, u32[]{:S(2)}) collective-permute-start(f32[576,128]{1,0:T(8,128)} %get-tuple-element.12), channel_id=1, source_target_pairs={{0,16},{4,20},{8,24},{12,28},{16,0},{20,4},{24,8},{28,12},{1,17},{... | collective-permute-start | bytes 884744 | tf_op jit(solution)/shard_map/ppermute | solution.py:450
  34.4 0.7 copy-start.7
  35.1 15.3 %collective-permute-start.13 = (f32[576,128]{1,0:T(8,128)}, f32[576,128]{1,0:T(8,128)}, u32[]{:S(2)}, u32[]{:S(2)}) collective-permute-start(f32[576,128]{1,0:T(8,128)} %get-tuple-element.11), channel_id=1, source_target_pairs={{0,12},{4,8},{8,4},{12,0},{16,28},{20,24},{24,20},{28,16},{1,13},{... | collective-permute-start | bytes 884744 | tf_op jit(solution)/shard_map/ppermute | solution.py:450
  35.4 0.7 copy-start.9
  36.1 25.5 %collective-permute-start.7 = (f32[576,128]{1,0:T(8,128)}, f32[576,128]{1,0:T(8,128)}, u32[]{:S(2)}, u32[]{:S(2)}) collective-permute-start(f32[576,128]{1,0:T(8,128)} %get-tuple-element.17), channel_id=1, source_target_pairs={{0,20},{4,16},{8,28},{12,24},{16,4},{20,0},{24,12},{28,8},{1,21},{... | collective-permute-start | bytes 884744 | tf_op jit(solution)/shard_map/ppermute | solution.py:450
  36.4 0.7 copy-start.11
  37.1 24.6 %collective-permute-start.8 = (f32[576,128]{1,0:T(8,128)}, f32[576,128]{1,0:T(8,128)}, u32[]{:S(2)}, u32[]{:S(2)}) collective-permute-start(f32[576,128]{1,0:T(8,128)} %get-tuple-element.16), channel_id=1, source_target_pairs={{0,24},{4,28},{8,16},{12,20},{16,8},{20,12},{24,0},{28,4},{1,25},{... | collective-permute-start | bytes 884744 | tf_op jit(solution)/shard_map/ppermute | solution.py:450
  39.8 0.7 copy-start.13
  40.5 21.1 %collective-permute-start.9 = (f32[576,128]{1,0:T(8,128)}, f32[576,128]{1,0:T(8,128)}, u32[]{:S(2)}, u32[]{:S(2)}) collective-permute-start(f32[576,128]{1,0:T(8,128)} %get-tuple-element.15), channel_id=1, source_target_pairs={{0,28},{4,24},{8,20},{12,16},{16,12},{20,8},{24,4},{28,0},{1,29},{... | collective-permute-start | bytes 884744 | tf_op jit(solution)/shard_map/ppermute | solution.py:450
  41.6 8.9 %copy-start.2 = (f32[64,72,128]{2,1,0:T(8,128)S(1)}, f32[64,72,128]{2,1,0:T(8,128)}, u32[]{:S(2)}) copy-start(f32[64,72,128]{2,1,0:T(8,128)} %param.11) | copy-start | bytes 7077892
  41.6 1.1 %copy-start.6 = (f32[576,128]{1,0:T(8,128)S(1)}, f32[576,128]{1,0:T(8,128)}, u32[]{:S(2)}) copy-start(f32[576,128]{1,0:T(8,128)} %copy-done.5) | copy-start | bytes 884740
  42.7 1.0 %copy-start.8 = (f32[576,128]{1,0:T(8,128)S(1)}, f32[576,128]{1,0:T(8,128)}, u32[]{:S(2)}) copy-start(f32[576,128]{1,0:T(8,128)} %copy-done.7) | copy-start | bytes 884740
  43.6 1.0 %copy-start.10 = (f32[576,128]{1,0:T(8,128)S(1)}, f32[576,128]{1,0:T(8,128)}, u32[]{:S(2)}) copy-start(f32[576,128]{1,0:T(8,128)} %copy-done.9) | copy-start | bytes 884740
  44.6 5.9 %copy-start.12 = (f32[576,128]{1,0:T(8,128)S(1)}, f32[576,128]{1,0:T(8,128)}, u32[]{:S(2)}) copy-start(f32[576,128]{1,0:T(8,128)} %copy-done.11) | copy-start | bytes 884740
  44.6 5.9 %copy-start.14 = (f32[576,128]{1,0:T(8,128)S(1)}, f32[576,128]{1,0:T(8,128)}, u32[]{:S(2)}) copy-start(f32[576,128]{1,0:T(8,128)} %copy-done.13) | copy-start | bytes 884740
  50.5 11.1 %copy-start.4 = (bf16[2048,128]{1,0:T(8,128)(2,1)S(1)}, bf16[2048,128]{1,0:T(8,128)(2,1)}, u32[]{:S(2)}) copy-start(bf16[2048,128]{1,0:T(8,128)(2,1)} %constant.48.clone.gather_ref) | copy-start | bytes 1572868
  50.5 11.1 %copy-start.15 = (f32[72,128]{1,0:T(8,128)S(1)}, f32[72,128]{1,0:T(8,128)}, u32[]{:S(2)}) copy-start(f32[72,128]{1,0:T(8,128)} %equal_ref.1) | copy-start | bytes 110596
  50.5 11.1 %copy-start.16 = (f32[8,128]{1,0:T(8,128)S(1)}, f32[8,128]{1,0:T(8,128)}, u32[]{:S(2)}) copy-start(f32[8,128]{1,0:T(8,128)} %constant.47.clone.sign_ref) | copy-start | bytes 12292
  69.9 1.4 %collective-permute-start.14 = (f32[288,128]{1,0:T(8,128)S(1)}, f32[288,128]{1,0:T(8,128)S(1)}, u32[]{:S(2)}, u32[]{:S(2)}) collective-permute-start(f32[288,128]{1,0:T(8,128)S(1)} %pad_maximum_fusion), channel_id=1, source_target_pairs={{0,4},{4,0},{8,12},{12,8},{16,20},{20,16},{24,28},{28,24},{1,5},{5... | collective-permute-start | bytes 442376 | tf_op jit(solution)/shard_map/ppermute | solution.py:450
  71.4 4.0 %collective-permute-start.15 = (f32[72,128]{1,0:T(8,128)S(1)}, f32[72,128]{1,0:T(8,128)S(1)}, u32[]{:S(2)}, u32[]{:S(2)}) collective-permute-start(f32[72,128]{1,0:T(8,128)S(1)} %get-tuple-element.35), channel_id=1, source_target_pairs={{0,8},{4,12},{8,0},{12,4},{16,24},{20,28},{24,16},{28,20},{1,9},{5... | collective-permute-start | bytes 110600 | tf_op jit(solution)/shard_map/ppermute | solution.py:450
  71.5 4.0 %collective-permute-start.16 = (f32[72,128]{1,0:T(8,128)S(1)}, f32[72,128]{1,0:T(8,128)S(1)}, u32[]{:S(2)}, u32[]{:S(2)}) collective-permute-start(f32[72,128]{1,0:T(8,128)S(1)} %get-tuple-element.34), channel_id=1, source_target_pairs={{0,16},{4,20},{8,24},{12,28},{16,0},{20,4},{24,8},{28,12},{1,17},{... | collective-permute-start | bytes 110600 | tf_op jit(solution)/shard_map/ppermute | solution.py:450
  73.3 4.9 %collective-permute-start.17 = (f32[72,128]{1,0:T(8,128)S(1)}, f32[72,128]{1,0:T(8,128)S(1)}, u32[]{:S(2)}, u32[]{:S(2)}) collective-permute-start(f32[72,128]{1,0:T(8,128)S(1)} %get-tuple-element.33), channel_id=1, source_target_pairs={{0,24},{4,28},{8,16},{12,20},{16,8},{20,12},{24,0},{28,4},{1,25},{... | collective-permute-start | bytes 110600 | tf_op jit(solution)/shard_map/ppermute | solution.py:450
  78.2 10.6 %copy-start.17 = (f32[72,128]{1,0:T(8,128)S(1)}, f32[72,128]{1,0:T(8,128)}, u32[]{:S(2)}) copy-start(f32[72,128]{1,0:T(8,128)} %param.12) | copy-start | bytes 110596
  78.2 10.7 %copy-start.3 = (bf16[128,2048]{1,0:T(8,128)(2,1)S(1)}, bf16[128,2048]{1,0:T(8,128)(2,1)}, u32[]{:S(2)}) copy-start(bf16[128,2048]{1,0:T(8,128)(2,1)} %constant.49.clone.spread_ref) | copy-start | bytes 1572868
  78.2 10.6 %collective-permute-start.18 = (f32[72,128]{1,0:T(8,128)S(1)}, f32[72,128]{1,0:T(8,128)S(1)}, u32[]{:S(2)}, u32[]{:S(2)}) collective-permute-start(f32[72,128]{1,0:T(8,128)S(1)} %fusion), channel_id=1, source_target_pairs={{0,1},{1,0},{2,3},{3,2},{4,5},{5,4},{6,7},{7,6},{8,9},{9,8},{10,11... | collective-permute-start | bytes 110600 | tf_op jit(solution)/shard_map/ppermute | solution.py:450
  79.9 8.9 %collective-permute-start.19 = (f32[72,128]{1,0:T(8,128)S(1)}, f32[72,128]{1,0:T(8,128)S(1)}, u32[]{:S(2)}, u32[]{:S(2)}) collective-permute-start(f32[72,128]{1,0:T(8,128)S(1)} %fusion), channel_id=1, source_target_pairs={{0,2},{1,3},{2,0},{3,1},{4,6},{5,7},{6,4},{7,5},{8,10},{9,11},{10,... | collective-permute-start | bytes 110600 | tf_op jit(solution)/shard_map/ppermute | solution.py:450
  82.5 6.4 %collective-permute-start.20 = (f32[72,128]{1,0:T(8,128)S(1)}, f32[72,128]{1,0:T(8,128)S(1)}, u32[]{:S(2)}, u32[]{:S(2)}) collective-permute-start(f32[72,128]{1,0:T(8,128)S(1)} %fusion), channel_id=1, source_target_pairs={{0,3},{1,2},{2,1},{3,0},{4,7},{5,6},{6,5},{7,4},{8,11},{9,10},{10,... | collective-permute-start | bytes 110600 | tf_op jit(solution)/shard_map/ppermute | solution.py:450

commit v3 on v2

--- a/solution.py
+++ b/solution.py
@@ -21,6 +21,7 @@
 hubbard = 1.0
 quadrature = (0.375, 1.1666666, 0.9583333, 1.0)
 
+PITCH = 9
 LATE = 3
 AHEAD = 3
 
@@ -95,27 +96,43 @@
     return copies
 
 
-def along_first(work_ref, sign, low, out_ref):
+def along_first(work_ref, sign, low, store):
     def columns(pair, carry):
         both = (2 * pair, 2 * pair + 1)
         rows = [[work_ref[k1 * SIDE + column] for k1 in range(SIDE)] for column in both]
         values = [dft24(row, sign, low) for row in rows]
         for column, value in zip(both, values):
             for r1 in range(SIDE):
-                out_ref[r1 * SIDE + column] = value[r1]
+                store(r1 * SIDE + column, value[r1])
         return carry
 
     lax.fori_loop(0, SIDE // 2, columns, 0)
 
 
+def pick_kernel(steps, parts, place_ref, whole_ref, *refs):
+    block_refs, sems = refs[:-1], refs[-1]
+    copies = []
+    for n, (step, block_ref) in enumerate(zip(steps, block_refs)):
+        rows = block_ref.shape[0]
+        start = pl.multiple_of(partner_of(place_ref[0], step, parts) * rows, TILE)
+        copies.append(pltpu.make_async_copy(whole_ref.at[pl.ds(start, rows)], block_ref, sems.at[n]))
+        copies[-1].start()
+    for copy in copies:
+        copy.wait()
+
+
 def roll_kernel(green_ref, greens_ref):
-    def rolls(s, carry):
-        green = green_ref[s]
+    batch = math.gcd(green_ref.shape[0], STEPS)
+
+    def rolls(n, carry):
+        times = pl.ds(n * batch, batch)
+        green = green_ref[times]
+        rolled = [roll_blocks(green, j) for j in range(STEPS)]
         for j in range(STEPS):
-            greens_ref[j, s] = roll_blocks(green, j)
+            greens_ref[j, times] = rolled[j]
         return carry
 
-    lax.fori_loop(0, green_ref.shape[0], rolls, 0)
+    lax.fori_loop(0, green_ref.shape[0] // batch, rolls, 0)
 
 
 def forward_kernel(steps, parts, place_ref, *refs):
@@ -140,7 +157,11 @@
         spot = pl.ds(pl.multiple_of(owner * rows, TILE), rows)
         for j in range(STEPS):
             greens_ref[j, spot, :] = roll_blocks(green, j)
-    along_first(work_ref, -1, low, lattice_ref)
+
+    def store(point, value):
+        lattice_ref[point] = value
+
+    along_first(work_ref, -1, low, store)
 
 
 def product_lines(steps, parts, place, lattice_ref, weights, screen_refs, held_ref, sems, work_ref):
@@ -170,7 +191,7 @@
         lax.fori_loop(0, lines, along_second, 0, unroll=lines <= 4)
 
 
-def early_kernel(steps, parts, place_ref, lattice_ref, weight_ref, *refs):
+def early_kernel(steps, parts, place_ref, lattice_ref, weight_ref, _, *refs):
     screen_refs, (work_ref, held_ref, sems) = refs[: len(steps)], refs[len(steps) :]
     product_lines(
         steps, parts, place_ref[0], lattice_ref, weight_ref[...], screen_refs, held_ref, sems, work_ref
@@ -189,8 +210,11 @@
         product_lines(
             steps, parts, place_ref[0], lattice_ref, weight_ref[...], screen_refs, held_ref, sems, work_ref
         )
-    sigma_at = sigma_ref.reshape(points, TILE, WIDTH)
-    along_first(work_ref, 1, low, sigma_at)
+
+    def store(point, value):
+        sigma_ref[pl.ds(point * PITCH, TILE), :] = value
+
+    along_first(work_ref, 1, low, store)
 
     block = points // parts
     tiles = block // TILE
@@ -202,7 +226,7 @@
         units = [(tile, s) for tile in range(batch) for s in range(TILE)]
 
         def prepare(tile, s):
-            sigma = sigma_ref[pl.ds((first + tile) * TILE * TILE + s, TILE, stride=TILE), :]
+            sigma = sigma_ref[pl.ds((first + tile) * TILE * PITCH + s, TILE, stride=PITCH), :]
             row = pl.multiple_of(green_row + s * block + tile * TILE, TILE)
             return (
                 [roll_blocks(sigma, STEPS * i) for i in range(STEPS)],
@@ -365,18 +389,18 @@
     )(place, *greens)
 
 
-def early_lines(place, lattice, weights, screens, steps, parts):
+def early_lines(place, lattice, weights, before, screens, steps, parts):
     points = SIDE * SIDE
     return pl.pallas_call(
         functools.partial(early_kernel, steps, parts),
         out_shape=jax.ShapeDtypeStruct((points, TILE, WIDTH), jnp.float32),
-        in_specs=[in_smem(), in_vmem(), in_vmem()] + [anywhere()] * len(steps),
+        in_specs=[in_smem(), in_vmem(), in_vmem(), anywhere()] + [anywhere()] * len(steps),
         out_specs=in_vmem(),
         scratch_shapes=held_blocks(len(steps), parts),
         compiler_params=params(16),
         cost_estimate=cost(150, 3),
         name="early",
-    )(place, lattice, weights, *screens)
+    )(place, lattice, weights, before, *screens)
 
 
 def backward(place, lattice, weights, equal_time, greens, screens, work, steps, parts, share):
@@ -393,7 +417,7 @@
         out_specs=[in_vmem()] * 2,
         input_output_aliases={len(inputs) - 1: 1},
         scratch_shapes=[
-            pltpu.VMEM((TILE * points, WIDTH), jnp.float32),
+            pltpu.VMEM((PITCH * points, WIDTH), jnp.float32),
             pltpu.VMEM((points, STEPS * STEPS * WIDTH), jnp.float32),
             pltpu.VMEM((points, STEPS * STEPS * WIDTH), jnp.bfloat16),
         ]
@@ -403,6 +427,21 @@
         name="backward",
     )(*inputs)
     return partial_value
+
+
+def pick(place, whole, steps, parts):
+    rows = whole.shape[0] // parts
+    return pl.pallas_call(
+        functools.partial(pick_kernel, steps, parts),
+        out_shape=[jax.ShapeDtypeStruct((rows, whole.shape[1]), whole.dtype)] * len(steps),
+        in_specs=[in_smem(), anywhere()],
+        out_specs=[anywhere()] * len(steps),
+        scratch_shapes=[pltpu.SemaphoreType.DMA((len(steps),))],
+        cost_estimate=pl.CostEstimate(
+            flops=0, bytes_accessed=8 * len(steps) * rows * whole.shape[1], transcendentals=0
+        ),
+        name="pick",
+    )(place, whole)
 
 
 def roll_own(greens):
@@ -456,8 +495,8 @@
         along.setdefault(step // 2, []).append(step)
     single = [along[n] for n in along if n and n & (n - 1) == 0]
     mixed = [along[n] for n in along if n & (n - 1)]
-    order = along[0] + [step for steps in zip(*single) for step in steps]
-    return order + [step for steps in mixed for step in steps]
+    order = [step for steps in zip(*single[::-1]) for step in steps]
+    return order + [step for steps in mixed for step in steps] + along[0]
 
 
 def class_weights(quad_class):
@@ -471,6 +510,7 @@
     points = local * parts
     times = history // parts
     place = lax.axis_index("ka")
+    seat = place.reshape(1)
     position = jnp.arange(history, dtype=jnp.int32)
     weights = jnp.where(
         position < live_count[0], time_step * class_weights(quad_class), jnp.float32(0.0)
@@ -483,10 +523,11 @@
         moved = []
         for x in (green_row, screened):
             whole = x.reshape(parts * TILE * local, width)
+            picked = pick(seat, whole, order[:2], parts) if x is green_row else []
             found = {0: whole}
-            for step in order:
+            for n, step in enumerate(order):
                 start = partner_of(place, step, parts) * (TILE * local)
-                block = lax.dynamic_slice_in_dim(whole, start, TILE * local)
+                block = picked[n] if n < len(picked) else lax.dynamic_slice_in_dim(whole, start, TILE * local)
                 found[step] = exchange(block, "ka", step, parts)
             moved.append([found])
         order = [0] + order
@@ -505,19 +546,20 @@
 
     early = order[: max(1, len(order) - LATE)]
     late = order[len(early) :]
-    seat = place.reshape(1)
+    own_greens = roll_own(green_row)
     partial_value = None
     for group in range(groups):
         green, screen = moved[0][group], moved[1][group]
         lattice, greens = forward(seat, [green[step] for step in order], order, sources)
-        work = early_lines(seat, lattice, weights[group], [screen[step] for step in early], early, sources)
+        work = early_lines(
+            seat, lattice, weights[group], own_greens, [screen[step] for step in early], early, sources
+        )
         share = hubbard / (points * blocks) if group == 0 else 0.0
         term = backward(
             seat, lattice, weights[group], equal_time, greens, [screen[step] for step in late], work,
             late, sources, share,
         )
         partial_value = term if partial_value is None else partial_value + term
-    own_greens = roll_own(green_row)
 
     owners = [partner_of(place, step, parts) for step in range(parts)]
     pieces = [lax.dynamic_slice_in_dim(partial_value, owner * local, local) for owner in owners]

time: 94.5 us -> 99.7 us (1.055)
  Pallas kernels: 27.7 us -> 43.6 us
  waiting for transfers between devices: 30.2 us -> 22.6 us
  starting transfers between devices: 25.4 us -> 21.9 us
    pallas_call x0 -> x1, Pallas kernels: none -> 19 us  [pick(): pl.pallas_call(functools.partial(pick_kernel, steps, parts), out_shape=[j...]
    ppermute x21, waiting for transfers between devices: 30.2 us -> 22.6 us  [exchange(): return lax.ppermute(value, axis, pairs)]
    ppermute x21, starting transfers between devices: 25.4 us -> 21.9 us  [exchange(): return lax.ppermute(value, axis, pairs)]
    pallas_call x1, Pallas kernels: 6.12 us -> 2.92 us  [roll_own(): pl.pallas_call(roll_kernel, out_shape=jax.ShapeDtypeStruct((STEPS, *green...]
    dynamic_slice x2, local copies, waits for them, and re-layouts: 2.94 us -> 5.45 us  [per_device(): lax.dynamic_slice_in_dim(whole, start, TILE * local)]
    unnamed x40 -> x38, local copies, waits for them, and re-layouts: 6.67 us -> 4.59 us
  transfers between devices with their start and end apart: 21 -> 21, of which waited for: 9 -> 10; matrix products, arithmetic and copies ran while one was open for 1% -> 3% of each run, Pallas kernels for 15% -> 30%
where the time goes in v3:
time: 99.7 us; the launch traced here: 99.5 us
  Pallas kernels  43.6 us (44%)
  waiting for transfers between devices  22.6 us (23%)
  starting transfers between devices  21.9 us (22%)
  local copies, waits for them, and re-layouts  10.2 us (10%)
    ppermute x21, waiting for transfers between devices, exchange(): return lax.ppermute(value, axis, pairs)  22.6 us
    ppermute x21, starting transfers between devices, exchange(): return lax.ppermute(value, axis, pairs)  21.9 us
    pallas_call x1, Pallas kernels, pick(): pl.pallas_call(functools.partial(pick_kernel, steps, parts), out_shape=[j...  19 us
    pallas_call x1, Pallas kernels, backward(): pl.pallas_call(functools.partial(backward_kernel, steps, parts, share), o...  8.12 us
    pallas_call x1, Pallas kernels, forward(): pl.pallas_call(functools.partial(forward_kernel, steps, parts), out_shape...  5.74 us
    dynamic_slice x2, local copies, waits for them, and re-layouts, per_device(): lax.dynamic_slice_in_dim(whole, start, TILE * local)  5.45 us
    pallas_call x1, Pallas kernels, propagate(): pl.pallas_call(propagate_kernel, out_shape=jax.ShapeDtypeStruct(greens.sh...  5.17 us
    unnamed x38, local copies, waits for them, and re-layouts  4.59 us
  transfers between devices with their start and end apart: 21, of which 10 were waited for; matrix products, arithmetic and copies ran while one was open for 3% of the time, Pallas kernels for 30%

profile of v3, /device:TPU:0, one launch (start us, length us, event | category | flops | bytes accessed | tf_op | source)
XLA Modules:
  0.0 99.5 jit_solution(2877849697070504143)
XLA Ops:
  0.0 2.5 %constant_dynamic-slice_fusion.15 = (f32[576,128]{1,0:T(8,128)}, f32[576,128]{1,0:T(8,128)}, f32[576,128]{1,0:T(8,128)}, f32[576,128]{1,0:T(8,128)}, f32[576,128]{1,0:T(8,128)}) fusion(f32[4608,128]{1,0:T(8,128)} %bitcast.5, s32[]{:T(128)S(6)} %select_n.65, s32[]{:T(128)S(6)} %select_n.64, s32[]{:T(128)S(6)} %select_n.63, s32[]{:T(128)S(6)} %select_n.62, ...), kind=kLoop, calls=%fused_computation.20 | loop fusion | bytes 2949140 | tf_op jit(solution)/shard_map/dynamic_slice | solution.py:530
  2.5 2.4 %collective-permute-start.2 = (f32[576,128]{1,0:T(8,128)}, f32[576,128]{1,0:T(8,128)S(1)}, u32[]{:S(2)}, u32[]{:S(2)}) collective-permute-start(f32[576,128]{1,0:T(8,128)} %get-tuple-element.26), channel_id=1, source_target_pairs={{0,20},{4,16},{8,28},{12,24},{16,4},{20,0},{24,12},{28,8},{1,21},{... | collective-permute-start | bytes 884744 | tf_op jit(solution)/shard_map/ppermute | solution.py:489
  4.9 1.8 %collective-permute-start.3 = (f32[576,128]{1,0:T(8,128)}, f32[576,128]{1,0:T(8,128)S(1)}, u32[]{:S(2)}, u32[]{:S(2)}) collective-permute-start(f32[576,128]{1,0:T(8,128)} %get-tuple-element.25), channel_id=1, source_target_pairs={{0,12},{4,8},{8,4},{12,0},{16,28},{20,24},{24,20},{28,16},{1,13},{... | collective-permute-start | bytes 884744 | tf_op jit(solution)/shard_map/ppermute | solution.py:489
  6.6 2.1 %collective-permute-start.5 = (f32[576,128]{1,0:T(8,128)}, f32[576,128]{1,0:T(8,128)S(1)}, u32[]{:S(2)}, u32[]{:S(2)}) collective-permute-start(f32[576,128]{1,0:T(8,128)} %get-tuple-element.23), channel_id=1, source_target_pairs={{0,28},{4,24},{8,20},{12,16},{16,12},{20,8},{24,4},{28,0},{1,29},{... | collective-permute-start | bytes 884744 | tf_op jit(solution)/shard_map/ppermute | solution.py:489
  8.7 1.0 collective-permute-start.6
  9.7 3.0 %constant_dynamic-slice_fusion.8 = (f32[576,128]{1,0:T(8,128)}, f32[576,128]{1,0:T(8,128)}, f32[576,128]{1,0:T(8,128)}, f32[576,128]{1,0:T(8,128)}, f32[576,128]...) fusion(f32[4608,128]{1,0:T(8,128)} %bitcast.8, s32[]{:T(128)S(6)} %select_n.62, s32[]{:T(128)S(6)} %select_n.61, ...), kind=kLoop, calls=%fused_computation.13 | loop fusion | bytes 4128796 | tf_op jit(solution)/shard_map/dynamic_slice | solution.py:530
  12.7 19.0 %pick.1 = (f32[576,128]{1,0:T(8,128)}, f32[576,128]{1,0:T(8,128)}) custom-call(s32[1]{0:T(128)} %bitcast.place_ref, f32[4608,128]{1,0:T(8,128)} %bitcast.6), custom_call_target="tpu_custom_call" | custom-call | bytes 1179648 | tf_op jit(solution)/shard_map/pick/pallas_call | solution.py:434
  31.7 0.6 collective-permute-start
  32.3 0.1 collective-permute-start.1
  32.4 1.9 %collective-permute-start.10 = (f32[576,128]{1,0:T(8,128)}, f32[576,128]{1,0:T(8,128)S(1)}, u32[]{:S(2)}, u32[]{:S(2)}) collective-permute-start(f32[576,128]{1,0:T(8,128)} %get-tuple-element.18), channel_id=1, source_target_pairs={{0,16},{4,20},{8,24},{12,28},{16,0},{20,4},{24,8},{28,12},{1,17},{... | collective-permute-start | bytes 884744 | tf_op jit(solution)/shard_map/ppermute | solution.py:489
  34.3 1.5 %collective-permute-start.11 = (f32[576,128]{1,0:T(8,128)}, f32[576,128]{1,0:T(8,128)S(1)}, u32[]{:S(2)}, u32[]{:S(2)}) collective-permute-start(f32[576,128]{1,0:T(8,128)} %get-tuple-element.17), channel_id=1, source_target_pairs={{0,8},{4,12},{8,0},{12,4},{16,24},{20,28},{24,16},{28,20},{1,9},{5... | collective-permute-start | bytes 884744 | tf_op jit(solution)/shard_map/ppermute | solution.py:489
  35.8 6.0 %collective-permute-done.refs_1_ = f32[576,128]{1,0:T(8,128)S(1)} collective-permute-done((f32[576,128]{1,0:T(8,128)}, f32[576,128]{1,0:T(8,128)S(1)}, u32[]{:S(2)}, u32[]{:S(2)}) %collective-permute-start) | collective-permute-done | bytes 294944 | tf_op jit(solution)/shard_map/ppermute | solution.py:489
  41.8 0.7 copy-done.6
  42.5 0.7 copy-done.8
  43.3 1.3 %collective-permute-start.7 = (f32[576,128]{1,0:T(8,128)}, f32[576,128]{1,0:T(8,128)}, u32[]{:S(2)}, u32[]{:S(2)}) collective-permute-start(f32[576,128]{1,0:T(8,128)} %get-tuple-element.21), channel_id=1, source_target_pairs={{0,24},{4,28},{8,16},{12,20},{16,8},{20,12},{24,0},{28,4},{1,25},{... | collective-permute-start | bytes 884744 | tf_op jit(solution)/shard_map/ppermute | solution.py:489
  44.6 3.6 %collective-permute-done.10.refs_1_ = f32[576,128]{1,0:T(8,128)S(1)} collective-permute-done((f32[576,128]{1,0:T(8,128)}, f32[576,128]{1,0:T(8,128)S(1)}, u32[]{:S(2)}, u32[]{:S(2)}) %collective-permute-start.10) | collective-permute-done | bytes 294944 | tf_op jit(solution)/shard_map/ppermute | solution.py:489
  48.1 0.7 copy-done.10
  48.9 0.7 copy-done.12
  49.6 0.1 collective-permute-start.9
  49.7 0.1 select_reduce_fusion
  50.5 0.1 dynamic_slice.68
  50.6 2.9 %roll_own.1._.greens_ref = f32[4,64,72,128]{3,2,1,0:T(8,128)S(1)} custom-call(f32[64,72,128]{2,1,0:T(8,128)S(1)} %copy-done), custom_call_target="tpu_custom_call" | custom-call | flops 1769472 | bytes 11796480 | tf_op jit(solution)/shard_map/roll_own/pallas_call | solution.py:448
  53.5 0.0 copy-start.3
  53.5 5.7 %forward.1 = (f32[576,8,128]{2,1,0:T(8,128)S(1)}, f32[4,4608,128]{2,1,0:T(8,128)S(1)}) custom-call(s32[1]{0:T(128)} %bitcast.place_ref, f32[4608,128]{1,0:T(8,128)S(1)} %bitcast.7, f32[576,128]{1,0:T(8,128)S(1)} %copy-done.7, f32[576,128]{1,0:T(8,128)S(1)} %copy-done.9, f32[576,128]{1,0:T(8,128)S(1)} %collective-permute-done.2.refs_3_, ...), custom_call_target="tpu_custom_call" | custom-call | flops 235929600 | bytes 14155776 | tf_op jit(solution)/shard_map/forward/pallas_call | solution.py:377
  59.3 0.0 copy-start.1
  59.3 0.1 squeeze.8.weight_ref
  59.4 0.0 copy-start.14
  59.4 0.0 copy-start.15
  59.4 2.7 %early.1.refs_3_ = f32[576,8,128]{2,1,0:T(8,128)S(1)} custom-call(s32[1]{0:T(128)} %bitcast.place_ref, f32[576,8,128]{2,1,0:T(8,128)S(1)} %get-tuple-element.12.lattice_ref, f32[8,128]{1,0:T(8,128)S(1)} %squeeze.8.weight_ref, f32[4,64,72,128]{3,2,1,0:T(8,128)S(1)} %roll_own.1._.greens_ref, f32[4608,128]{1,0:T(8,128)S(1)} %bitcast.9, ...), custom_call_target="tpu_custom_call" | custom-call | flops 88473600 | bytes 7077888 | tf_op jit(solution)/shard_map/early/pallas_call | solution.py:394
  62.1 0.3 collective-permute-done.7.refs_0_
  62.4 3.8 %collective-permute-done.8.refs_1_ = f32[576,128]{1,0:T(8,128)} collective-permute-done((f32[576,128]{1,0:T(8,128)}, f32[576,128]{1,0:T(8,128)}, u32[]{:S(2)}, u32[]{:S(2)}) %collective-permute-start.8) | collective-permute-done | bytes 294944 | tf_op jit(solution)/shard_map/ppermute | solution.py:489
  66.2 0.0 copy-start.2
  66.3 1.7 %copy-done.2 = f32[576,8,128]{2,1,0:T(8,128)S(1)} copy-done((f32[576,8,128]{2,1,0:T(8,128)S(1)}, f32[576,8,128]{2,1,0:T(8,128)}, u32[]{:S(2)}) %copy-start.2) | copy-done | bytes 2359320
  67.9 8.1 %backward.1 = (f32[576,128]{1,0:T(8,128)S(1)}, f32[576,8,128]{2,1,0:T(8,128)S(1)}) custom-call(s32[1]{0:T(128)} %bitcast.place_ref, f32[576,8,128]{2,1,0:T(8,128)S(1)} %copy-done.2, f32[8,128]{1,0:T(8,128)S(1)} %squeeze.8.weight_ref, f32[72,128]{1,0:T(8,128)S(1)} %copy-done.14, f32[8,128]{1,0:T(8,128)S(1)} %copy-done.15, ...), custom_call_target="tpu_custom_call", output_to_operand_aliasing={{1}: (10, {})} | custom-call | flops 471859200 | bytes 14155776 | tf_op jit(solution)/shard_map/backward/pallas_call | solution.py:410
  76.1 1.1 %collective-permute-start.14 = (f32[288,128]{1,0:T(8,128)S(1)}, f32[288,128]{1,0:T(8,128)S(1)}, u32[]{:S(2)}, u32[]{:S(2)}) collective-permute-start(f32[288,128]{1,0:T(8,128)S(1)} %pad_maximum_fusion), channel_id=1, source_target_pairs={{0,4},{4,0},{8,12},{12,8},{16,20},{20,16},{24,28},{28,24},{1,5},{5... | collective-permute-start | bytes 442376 | tf_op jit(solution)/shard_map/ppermute | solution.py:489
  77.2 1.0 %collective-permute-done.14 = f32[288,128]{1,0:T(8,128)S(1)} collective-permute-done((f32[288,128]{1,0:T(8,128)S(1)}, f32[288,128]{1,0:T(8,128)S(1)}, u32[]{:S(2)}, u32[]{:S(2)}) %collective-permute-start.14) | collective-permute-done | bytes 147488 | tf_op jit(solution)/shard_map/ppermute | solution.py:489
  78.3 0.6 collective-permute-start.15
  78.9 0.4 collective-permute-start.16
  79.3 2.6 %collective-permute-start.17 = (f32[72,128]{1,0:T(8,128)S(1)}, f32[72,128]{1,0:T(8,128)S(1)}, u32[]{:S(2)}, u32[]{:S(2)}) collective-permute-start(f32[72,128]{1,0:T(8,128)S(1)} %get-tuple-element.35), channel_id=1, source_target_pairs={{0,24},{4,28},{8,16},{12,20},{16,8},{20,12},{24,0},{28,4},{1,25},{... | collective-permute-start | bytes 110600 | tf_op jit(solution)/shard_map/ppermute | solution.py:489
  81.9 0.5 collective-permute-done.15
  82.3 0.9 collective-permute-done.16
  83.3 0.9 collective-permute-done.17
  84.2 1.8 %collective-permute-start.18 = (f32[72,128]{1,0:T(8,128)S(1)}, f32[72,128]{1,0:T(8,128)S(1)}, u32[]{:S(2)}, u32[]{:S(2)}) collective-permute-start(f32[72,128]{1,0:T(8,128)S(1)} %fusion), channel_id=1, source_target_pairs={{0,1},{1,0},{2,3},{3,2},{4,5},{5,4},{6,7},{7,6},{8,9},{9,8},{10,11... | collective-permute-start | bytes 110600 | tf_op jit(solution)/shard_map/ppermute | solution.py:489
  85.9 2.6 %collective-permute-start.19 = (f32[72,128]{1,0:T(8,128)S(1)}, f32[72,128]{1,0:T(8,128)S(1)}, u32[]{:S(2)}, u32[]{:S(2)}) collective-permute-start(f32[72,128]{1,0:T(8,128)S(1)} %fusion), channel_id=1, source_target_pairs={{0,2},{1,3},{2,0},{3,1},{4,6},{5,7},{6,4},{7,5},{8,10},{9,11},{10,... | collective-permute-start | bytes 110600 | tf_op jit(solution)/shard_map/ppermute | solution.py:489
  88.5 0.1 collective-permute-start.20
  88.6 2.9 %collective-permute-done.19 = f32[72,128]{1,0:T(8,128)S(1)} collective-permute-done((f32[72,128]{1,0:T(8,128)S(1)}, f32[72,128]{1,0:T(8,128)S(1)}, u32[]{:S(2)}, u32[]{:S(2)}) %collective-permute-start.19) | collective-permute-done | bytes 36896 | tf_op jit(solution)/shard_map/ppermute | solution.py:489
  91.5 2.8 %collective-permute-done.20 = f32[72,128]{1,0:T(8,128)S(1)} collective-permute-done((f32[72,128]{1,0:T(8,128)S(1)}, f32[72,128]{1,0:T(8,128)S(1)}, u32[]{:S(2)}, u32[]{:S(2)}) %collective-permute-start.20) | collective-permute-done | bytes 36896 | tf_op jit(solution)/shard_map/ppermute | solution.py:489
  94.3 5.2 %propagate.1 = f32[64,72,128]{2,1,0:T(8,128)} custom-call(f32[4,64,72,128]{3,2,1,0:T(8,128)S(1)} %roll_own.1._.greens_ref, f32[72,128]{1,0:T(8,128)S(1)} %add_add_fusion.effective_ref, bf16[128,2048]{1,0:T(8,128)(2,1)S(1)} %copy-done.4), custom_call_target="tpu_custom_call" | custom-call | flops 18874368 | bytes 11796480 | tf_op jit(solution)/shard_map/propagate/pallas_call | solution.py:463
  (50 shorter events, 0.2 us)
Async XLA Ops:
  2.5 29.2 %collective-permute-start.2 = (f32[576,128]{1,0:T(8,128)}, f32[576,128]{1,0:T(8,128)S(1)}, u32[]{:S(2)}, u32[]{:S(2)}) collective-permute-start(f32[576,128]{1,0:T(8,128)} %get-tuple-element.26), channel_id=1, source_target_pairs={{0,20},{4,16},{8,28},{12,24},{16,4},{20,0},{24,12},{28,8},{1,21},{... | collective-permute-start | bytes 884744 | tf_op jit(solution)/shard_map/ppermute | solution.py:489
  4.9 27.4 %collective-permute-start.3 = (f32[576,128]{1,0:T(8,128)}, f32[576,128]{1,0:T(8,128)S(1)}, u32[]{:S(2)}, u32[]{:S(2)}) collective-permute-start(f32[576,128]{1,0:T(8,128)} %get-tuple-element.25), channel_id=1, source_target_pairs={{0,12},{4,8},{8,4},{12,0},{16,28},{20,24},{24,20},{28,16},{1,13},{... | collective-permute-start | bytes 884744 | tf_op jit(solution)/shard_map/ppermute | solution.py:489
  6.6 25.7 %collective-permute-start.4 = (f32[576,128]{1,0:T(8,128)}, f32[576,128]{1,0:T(8,128)S(1)}, u32[]{:S(2)}, u32[]{:S(2)}) collective-permute-start(f32[576,128]{1,0:T(8,128)} %get-tuple-element.24), channel_id=1, source_target_pairs={{0,24},{4,28},{8,16},{12,20},{16,8},{20,12},{24,0},{28,4},{1,25},{... | collective-permute-start | bytes 884744 | tf_op jit(solution)/shard_map/ppermute | solution.py:489
  6.6 27.7 %collective-permute-start.5 = (f32[576,128]{1,0:T(8,128)}, f32[576,128]{1,0:T(8,128)S(1)}, u32[]{:S(2)}, u32[]{:S(2)}) collective-permute-start(f32[576,128]{1,0:T(8,128)} %get-tuple-element.23), channel_id=1, source_target_pairs={{0,28},{4,24},{8,20},{12,16},{16,12},{20,8},{24,4},{28,0},{1,29},{... | collective-permute-start | bytes 884744 | tf_op jit(solution)/shard_map/ppermute | solution.py:489
  8.7 27.1 %collective-permute-start.6 = (f32[576,128]{1,0:T(8,128)}, f32[576,128]{1,0:T(8,128)}, u32[]{:S(2)}, u32[]{:S(2)}) collective-permute-start(f32[576,128]{1,0:T(8,128)} %get-tuple-element.22), channel_id=1, source_target_pairs={{0,4},{4,0},{8,12},{12,8},{16,20},{20,16},{24,28},{28,24},{1,5},{5... | collective-permute-start | bytes 884744 | tf_op jit(solution)/shard_map/ppermute | solution.py:489
  9.7 40.0 %copy-start.17 = (s32[64]{0:T(128)S(1)}, s32[64]{0:T(128)}, u32[]{:S(2)}) copy-start(s32[64]{0:T(128)} %param.14) | copy-start | bytes 772
  9.7 40.0 %copy-start.18 = (f32[4]{0:T(128)S(1)}, f32[4]{0:T(128)}, u32[]{:S(2)}) copy-start(f32[4]{0:T(128)} %constant.46.clone) | copy-start | bytes 52
  9.7 40.9 %copy-start = (f32[64,72,128]{2,1,0:T(8,128)S(1)}, f32[64,72,128]{2,1,0:T(8,128)}, u32[]{:S(2)}) copy-start(f32[64,72,128]{2,1,0:T(8,128)} %green_ref.1) | copy-start | bytes 7077892
  31.7 10.1 %collective-permute-start = (f32[576,128]{1,0:T(8,128)}, f32[576,128]{1,0:T(8,128)S(1)}, u32[]{:S(2)}, u32[]{:S(2)}) collective-permute-start(f32[576,128]{1,0:T(8,128)} %get-tuple-element.10), channel_id=1, source_target_pairs={{0,16},{4,20},{8,24},{12,28},{16,0},{20,4},{24,8},{28,12},{1,17},{... | collective-permute-start | bytes 884744 | tf_op jit(solution)/shard_map/ppermute | solution.py:489
  32.3 10.3 %collective-permute-start.1 = (f32[576,128]{1,0:T(8,128)}, f32[576,128]{1,0:T(8,128)S(1)}, u32[]{:S(2)}, u32[]{:S(2)}) collective-permute-start(f32[576,128]{1,0:T(8,128)} %get-tuple-element.11), channel_id=1, source_target_pairs={{0,8},{4,12},{8,0},{12,4},{16,24},{20,28},{24,16},{28,20},{1,9},{5... | collective-permute-start | bytes 884744 | tf_op jit(solution)/shard_map/ppermute | solution.py:489
  32.4 15.8 %collective-permute-start.10 = (f32[576,128]{1,0:T(8,128)}, f32[576,128]{1,0:T(8,128)S(1)}, u32[]{:S(2)}, u32[]{:S(2)}) collective-permute-start(f32[576,128]{1,0:T(8,128)} %get-tuple-element.18), channel_id=1, source_target_pairs={{0,16},{4,20},{8,24},{12,28},{16,0},{20,4},{24,8},{28,12},{1,17},{... | collective-permute-start | bytes 884744 | tf_op jit(solution)/shard_map/ppermute | solution.py:489
  34.3 14.5 %collective-permute-start.11 = (f32[576,128]{1,0:T(8,128)}, f32[576,128]{1,0:T(8,128)S(1)}, u32[]{:S(2)}, u32[]{:S(2)}) collective-permute-start(f32[576,128]{1,0:T(8,128)} %get-tuple-element.17), channel_id=1, source_target_pairs={{0,8},{4,12},{8,0},{12,4},{16,24},{20,28},{24,16},{28,20},{1,9},{5... | collective-permute-start | bytes 884744 | tf_op jit(solution)/shard_map/ppermute | solution.py:489
  35.8 23.5 %collective-permute-start.12 = (f32[576,128]{1,0:T(8,128)}, f32[576,128]{1,0:T(8,128)}, u32[]{:S(2)}, u32[]{:S(2)}) collective-permute-start(f32[576,128]{1,0:T(8,128)} %get-tuple-element.16), channel_id=1, source_target_pairs={{0,20},{4,16},{8,28},{12,24},{16,4},{20,0},{24,12},{28,8},{1,21},{... | collective-permute-start | bytes 884744 | tf_op jit(solution)/shard_map/ppermute | solution.py:489
  41.8 0.7 copy-start.6
  42.5 16.8 %collective-permute-start.13 = (f32[576,128]{1,0:T(8,128)}, f32[576,128]{1,0:T(8,128)}, u32[]{:S(2)}, u32[]{:S(2)}) collective-permute-start(f32[576,128]{1,0:T(8,128)} %get-tuple-element.15), channel_id=1, source_target_pairs={{0,12},{4,8},{8,4},{12,0},{16,28},{20,24},{24,20},{28,16},{1,13},{... | collective-permute-start | bytes 884744 | tf_op jit(solution)/shard_map/ppermute | solution.py:489
  42.5 0.7 copy-start.8
  43.3 19.1 %collective-permute-start.7 = (f32[576,128]{1,0:T(8,128)}, f32[576,128]{1,0:T(8,128)}, u32[]{:S(2)}, u32[]{:S(2)}) collective-permute-start(f32[576,128]{1,0:T(8,128)} %get-tuple-element.21), channel_id=1, source_target_pairs={{0,24},{4,28},{8,16},{12,20},{16,8},{20,12},{24,0},{28,4},{1,25},{... | collective-permute-start | bytes 884744 | tf_op jit(solution)/shard_map/ppermute | solution.py:489
  48.1 0.7 copy-start.10
  48.9 17.4 %collective-permute-start.8 = (f32[576,128]{1,0:T(8,128)}, f32[576,128]{1,0:T(8,128)}, u32[]{:S(2)}, u32[]{:S(2)}) collective-permute-start(f32[576,128]{1,0:T(8,128)} %get-tuple-element.20), channel_id=1, source_target_pairs={{0,28},{4,24},{8,20},{12,16},{16,12},{20,8},{24,4},{28,0},{1,29},{... | collective-permute-start | bytes 884744 | tf_op jit(solution)/shard_map/ppermute | solution.py:489
  48.9 0.7 copy-start.12
  49.6 16.6 %collective-permute-start.9 = (f32[576,128]{1,0:T(8,128)}, f32[576,128]{1,0:T(8,128)}, u32[]{:S(2)}, u32[]{:S(2)}) collective-permute-start(f32[576,128]{1,0:T(8,128)} %get-tuple-element.19), channel_id=1, source_target_pairs={{0,4},{4,0},{8,12},{12,8},{16,20},{20,16},{24,28},{28,24},{1,5},{5... | collective-permute-start | bytes 884744 | tf_op jit(solution)/shard_map/ppermute | solution.py:489
  50.6 2.9 %copy-start.7 = (f32[576,128]{1,0:T(8,128)S(1)}, f32[576,128]{1,0:T(8,128)}, u32[]{:S(2)}) copy-start(f32[576,128]{1,0:T(8,128)} %copy-done.6) | copy-start | bytes 884740
  50.6 3.0 %copy-start.9 = (f32[576,128]{1,0:T(8,128)S(1)}, f32[576,128]{1,0:T(8,128)}, u32[]{:S(2)}) copy-start(f32[576,128]{1,0:T(8,128)} %copy-done.8) | copy-start | bytes 884740
  53.5 5.9 %copy-start.3 = (f32[64,72,128]{2,1,0:T(8,128)S(1)}, f32[64,72,128]{2,1,0:T(8,128)}, u32[]{:S(2)}) copy-start(f32[64,72,128]{2,1,0:T(8,128)} %param.11) | copy-start | bytes 7077892
  53.5 5.9 %copy-start.11 = (f32[576,128]{1,0:T(8,128)S(1)}, f32[576,128]{1,0:T(8,128)}, u32[]{:S(2)}) copy-start(f32[576,128]{1,0:T(8,128)} %copy-done.10) | copy-start | bytes 884740
  53.5 5.9 %copy-start.13 = (f32[576,128]{1,0:T(8,128)S(1)}, f32[576,128]{1,0:T(8,128)}, u32[]{:S(2)}) copy-start(f32[576,128]{1,0:T(8,128)} %copy-done.12) | copy-start | bytes 884740
  59.3 2.8 %copy-start.1 = (f32[576,8,128]{2,1,0:T(8,128)}, f32[576,8,128]{2,1,0:T(8,128)S(1)}, u32[]{:S(2)}) copy-start(f32[576,8,128]{2,1,0:T(8,128)S(1)} %get-tuple-element.12.lattice_ref) | copy-start | bytes 7077892
  59.4 6.8 %copy-start.5 = (bf16[2048,128]{1,0:T(8,128)(2,1)S(1)}, bf16[2048,128]{1,0:T(8,128)(2,1)}, u32[]{:S(2)}) copy-start(bf16[2048,128]{1,0:T(8,128)(2,1)} %constant.48.clone.gather_ref) | copy-start | bytes 1572868
  59.4 6.8 %copy-start.14 = (f32[72,128]{1,0:T(8,128)S(1)}, f32[72,128]{1,0:T(8,128)}, u32[]{:S(2)}) copy-start(f32[72,128]{1,0:T(8,128)} %equal_ref.1) | copy-start | bytes 110596
  59.4 6.8 %copy-start.15 = (f32[8,128]{1,0:T(8,128)S(1)}, f32[8,128]{1,0:T(8,128)}, u32[]{:S(2)}) copy-start(f32[8,128]{1,0:T(8,128)} %constant.47.clone.sign_ref) | copy-start | bytes 12292
  66.2 1.7 %copy-start.2 = (f32[576,8,128]{2,1,0:T(8,128)S(1)}, f32[576,8,128]{2,1,0:T(8,128)}, u32[]{:S(2)}) copy-start(f32[576,8,128]{2,1,0:T(8,128)} %copy-done.1) | copy-start | bytes 7077892
  67.9 26.4 %copy-start.16 = (f32[72,128]{1,0:T(8,128)S(1)}, f32[72,128]{1,0:T(8,128)}, u32[]{:S(2)}) copy-start(f32[72,128]{1,0:T(8,128)} %param.12) | copy-start | bytes 110596
  67.9 26.4 %copy-start.4 = (bf16[128,2048]{1,0:T(8,128)(2,1)S(1)}, bf16[128,2048]{1,0:T(8,128)(2,1)}, u32[]{:S(2)}) copy-start(bf16[128,2048]{1,0:T(8,128)(2,1)} %constant.49.clone.spread_ref) | copy-start | bytes 1572868
  76.1 2.1 %collective-permute-start.14 = (f32[288,128]{1,0:T(8,128)S(1)}, f32[288,128]{1,0:T(8,128)S(1)}, u32[]{:S(2)}, u32[]{:S(2)}) collective-permute-start(f32[288,128]{1,0:T(8,128)S(1)} %pad_maximum_fusion), channel_id=1, source_target_pairs={{0,4},{4,0},{8,12},{12,8},{16,20},{20,16},{24,28},{28,24},{1,5},{5... | collective-permute-start | bytes 442376 | tf_op jit(solution)/shard_map/ppermute | solution.py:489
  78.3 4.0 %collective-permute-start.15 = (f32[72,128]{1,0:T(8,128)S(1)}, f32[72,128]{1,0:T(8,128)S(1)}, u32[]{:S(2)}, u32[]{:S(2)}) collective-permute-start(f32[72,128]{1,0:T(8,128)S(1)} %get-tuple-element.37), channel_id=1, source_target_pairs={{0,8},{4,12},{8,0},{12,4},{16,24},{20,28},{24,16},{28,20},{1,9},{5... | collective-permute-start | bytes 110600 | tf_op jit(solution)/shard_map/ppermute | solution.py:489
  78.9 4.4 %collective-permute-start.16 = (f32[72,128]{1,0:T(8,128)S(1)}, f32[72,128]{1,0:T(8,128)S(1)}, u32[]{:S(2)}, u32[]{:S(2)}) collective-permute-start(f32[72,128]{1,0:T(8,128)S(1)} %get-tuple-element.36), channel_id=1, source_target_pairs={{0,16},{4,20},{8,24},{12,28},{16,0},{20,4},{24,8},{28,12},{1,17},{... | collective-permute-start | bytes 110600 | tf_op jit(solution)/shard_map/ppermute | solution.py:489
  79.3 4.9 %collective-permute-start.17 = (f32[72,128]{1,0:T(8,128)S(1)}, f32[72,128]{1,0:T(8,128)S(1)}, u32[]{:S(2)}, u32[]{:S(2)}) collective-permute-start(f32[72,128]{1,0:T(8,128)S(1)} %get-tuple-element.35), channel_id=1, source_target_pairs={{0,24},{4,28},{8,16},{12,20},{16,8},{20,12},{24,0},{28,4},{1,25},{... | collective-permute-start | bytes 110600 | tf_op jit(solution)/shard_map/ppermute | solution.py:489
  84.2 4.5 %collective-permute-start.18 = (f32[72,128]{1,0:T(8,128)S(1)}, f32[72,128]{1,0:T(8,128)S(1)}, u32[]{:S(2)}, u32[]{:S(2)}) collective-permute-start(f32[72,128]{1,0:T(8,128)S(1)} %fusion), channel_id=1, source_target_pairs={{0,1},{1,0},{2,3},{3,2},{4,5},{5,4},{6,7},{7,6},{8,9},{9,8},{10,11... | collective-permute-start | bytes 110600 | tf_op jit(solution)/shard_map/ppermute | solution.py:489
  85.9 5.6 %collective-permute-start.19 = (f32[72,128]{1,0:T(8,128)S(1)}, f32[72,128]{1,0:T(8,128)S(1)}, u32[]{:S(2)}, u32[]{:S(2)}) collective-permute-start(f32[72,128]{1,0:T(8,128)S(1)} %fusion), channel_id=1, source_target_pairs={{0,2},{1,3},{2,0},{3,1},{4,6},{5,7},{6,4},{7,5},{8,10},{9,11},{10,... | collective-permute-start | bytes 110600 | tf_op jit(solution)/shard_map/ppermute | solution.py:489
  88.5 5.8 %collective-permute-start.20 = (f32[72,128]{1,0:T(8,128)S(1)}, f32[72,128]{1,0:T(8,128)S(1)}, u32[]{:S(2)}, u32[]{:S(2)}) collective-permute-start(f32[72,128]{1,0:T(8,128)S(1)} %fusion), channel_id=1, source_target_pairs={{0,3},{1,2},{2,1},{3,0},{4,7},{5,6},{6,5},{7,4},{8,11},{9,10},{10,... | collective-permute-start | bytes 110600 | tf_op jit(solution)/shard_map/ppermute | solution.py:489

commit v4 on v3

--- a/solution.py
+++ b/solution.py
@@ -21,7 +21,6 @@
 hubbard = 1.0
 quadrature = (0.375, 1.1666666, 0.9583333, 1.0)
 
-PITCH = 9
 LATE = 3
 AHEAD = 3
 
@@ -97,28 +96,15 @@
 
 
 def along_first(work_ref, sign, low, store):
-    def columns(pair, carry):
-        both = (2 * pair, 2 * pair + 1)
-        rows = [[work_ref[k1 * SIDE + column] for k1 in range(SIDE)] for column in both]
-        values = [dft24(row, sign, low) for row in rows]
-        for column, value in zip(both, values):
-            for r1 in range(SIDE):
-                store(r1 * SIDE + column, value[r1])
-        return carry
-
-    lax.fori_loop(0, SIDE // 2, columns, 0)
-
-
-def pick_kernel(steps, parts, place_ref, whole_ref, *refs):
-    block_refs, sems = refs[:-1], refs[-1]
-    copies = []
-    for n, (step, block_ref) in enumerate(zip(steps, block_refs)):
-        rows = block_ref.shape[0]
-        start = pl.multiple_of(partner_of(place_ref[0], step, parts) * rows, TILE)
-        copies.append(pltpu.make_async_copy(whole_ref.at[pl.ds(start, rows)], block_ref, sems.at[n]))
-        copies[-1].start()
-    for copy in copies:
-        copy.wait()
+    def load(column):
+        return [work_ref[k1 * SIDE + column] for k1 in range(SIDE)]
+
+    rows = load(0)
+    for column in range(SIDE):
+        following = load(column + 1) if column + 1 < SIDE else None
+        for r1, value in enumerate(dft24(rows, sign, low)):
+            store(r1 * SIDE + column, value)
+        rows = following
 
 
 def roll_kernel(green_ref, greens_ref):
@@ -169,26 +155,36 @@
     turn = jnp.where(low, -1.0, 1.0)
     copies = fetch(place, steps, screen_refs, held_ref, sems)
     lines = held_ref.shape[1] // (TILE * SIDE)
-    for slot, step in enumerate(steps):
-        copies[slot].wait()
-        screen_ref = held_ref.at[slot]
-        first = partner_of(place, step, parts) * lines
-
-        def along_second(i, carry):
-            rows = []
-            for r2, value in enumerate(load_line(screen_ref, i)):
-                screen = value * weights
-                other = swap(screen)
-                lattice = lattice_ref[(first + i) * SIDE + r2]
-                rows.append(
-                    swap(lattice) * turn * jnp.where(low, screen, other)
-                    - lattice * jnp.where(low, other, screen)
-                )
-            for k2, value in enumerate(dft24(rows, 1, low)):
-                work_ref[(first + i) * SIDE + k2] = value
-            return carry
-
-        lax.fori_loop(0, lines, along_second, 0, unroll=lines <= 4)
+    for copy in copies:
+        copy.wait()
+
+    def load(slot, step, i):
+        line = partner_of(place, step, parts) * lines + i
+        rows = []
+        for r2, value in enumerate(load_line(held_ref.at[slot], i)):
+            screen = value * weights
+            other = swap(screen)
+            lattice = lattice_ref[line * SIDE + r2]
+            rows.append(
+                swap(lattice) * turn * jnp.where(low, screen, other)
+                - lattice * jnp.where(low, other, screen)
+            )
+        return line, rows
+
+    def store(line, rows):
+        for k2, value in enumerate(dft24(rows, 1, low)):
+            work_ref[line * SIDE + k2] = value
+
+    if lines > 4:
+        for slot, step in enumerate(steps):
+            lax.fori_loop(0, lines, lambda i, carry: store(*load(slot, step, i)), None)
+        return
+    each = [(slot, step, i) for slot, step in enumerate(steps) for i in range(lines)]
+    ready = load(*each[0])
+    for n in range(len(each)):
+        present = ready
+        ready = load(*each[n + 1]) if n + 1 < len(each) else None
+        store(*present)
 
 
 def early_kernel(steps, parts, place_ref, lattice_ref, weight_ref, _, *refs):
@@ -212,7 +208,7 @@
         )
 
     def store(point, value):
-        sigma_ref[pl.ds(point * PITCH, TILE), :] = value
+        sigma_ref[pl.ds(point * TILE, TILE), :] = value
 
     along_first(work_ref, 1, low, store)
 
@@ -226,7 +222,7 @@
         units = [(tile, s) for tile in range(batch) for s in range(TILE)]
 
         def prepare(tile, s):
-            sigma = sigma_ref[pl.ds((first + tile) * TILE * PITCH + s, TILE, stride=PITCH), :]
+            sigma = sigma_ref[pl.ds((first + tile) * TILE * TILE + s, TILE, stride=TILE), :]
             row = pl.multiple_of(green_row + s * block + tile * TILE, TILE)
             return (
                 [roll_blocks(sigma, STEPS * i) for i in range(STEPS)],
@@ -294,20 +290,26 @@
             def _():
                 copy(number - slots, slot).wait()
 
-            times = pl.ds(number * chunk, chunk)
+            batch = math.gcd(chunk, 4)
+            pending = None
             for start in range(0, points, TILE):
                 stop = min(start + TILE, points)
-                greens = [greens_ref[j, times, start:stop, :] for j in range(STEPS)]
-                terms = [greens[0]]
-                for i in range(STEPS):
-                    total = None
-                    for j in range(STEPS):
-                        spot = STEPS * i + j
-                        factor = factor_ref[start:stop, spot * WIDTH : (spot + 1) * WIDTH]
-                        term = factor[None] * greens[j]
-                        total = term if total is None else total + term
-                    terms.append(roll_blocks(total, STEPS * i))
-                held_ref[slot, :, start:stop, :] = tree_sum(terms)
+                for first in range(0, chunk, batch):
+                    times = pl.ds(number * chunk + first, batch)
+                    greens = [greens_ref[j, times, start:stop, :] for j in range(STEPS)]
+                    terms = [greens[0]]
+                    for i in range(STEPS):
+                        total = None
+                        for j in range(STEPS):
+                            spot = STEPS * i + j
+                            factor = factor_ref[start:stop, spot * WIDTH : (spot + 1) * WIDTH]
+                            term = factor[None] * greens[j]
+                            total = term if total is None else total + term
+                        terms.append(roll_blocks(total, STEPS * i))
+                    if pending is not None:
+                        held_ref[pending[0]] = tree_sum(pending[1])
+                    pending = ((slot, slice(first, first + batch), slice(start, stop)), terms)
+            held_ref[pending[0]] = tree_sum(pending[1])
             copy(number, slot).start()
         return carry
 
@@ -383,7 +385,7 @@
         in_specs=[in_smem()] + [anywhere()] * len(steps),
         out_specs=[in_vmem()] * 2,
         scratch_shapes=[pltpu.VMEM((points, TILE, WIDTH), jnp.float32)] + held_blocks(len(steps), parts),
-        compiler_params=params(24),
+        compiler_params=params(8),
         cost_estimate=cost(400, 6),
         name="forward",
     )(place, *greens)
@@ -397,7 +399,7 @@
         in_specs=[in_smem(), in_vmem(), in_vmem(), anywhere()] + [anywhere()] * len(steps),
         out_specs=in_vmem(),
         scratch_shapes=held_blocks(len(steps), parts),
-        compiler_params=params(16),
+        compiler_params=params(4),
         cost_estimate=cost(150, 3),
         name="early",
     )(place, lattice, weights, before, *screens)
@@ -417,31 +419,16 @@
         out_specs=[in_vmem()] * 2,
         input_output_aliases={len(inputs) - 1: 1},
         scratch_shapes=[
-            pltpu.VMEM((PITCH * points, WIDTH), jnp.float32),
+            pltpu.VMEM((TILE * points, WIDTH), jnp.float32),
             pltpu.VMEM((points, STEPS * STEPS * WIDTH), jnp.float32),
             pltpu.VMEM((points, STEPS * STEPS * WIDTH), jnp.bfloat16),
         ]
         + (held_blocks(len(steps), parts) if steps else []),
-        compiler_params=params(36),
+        compiler_params=params(16),
         cost_estimate=cost(800, 6),
         name="backward",
     )(*inputs)
     return partial_value
-
-
-def pick(place, whole, steps, parts):
-    rows = whole.shape[0] // parts
-    return pl.pallas_call(
-        functools.partial(pick_kernel, steps, parts),
-        out_shape=[jax.ShapeDtypeStruct((rows, whole.shape[1]), whole.dtype)] * len(steps),
-        in_specs=[in_smem(), anywhere()],
-        out_specs=[anywhere()] * len(steps),
-        scratch_shapes=[pltpu.SemaphoreType.DMA((len(steps),))],
-        cost_estimate=pl.CostEstimate(
-            flops=0, bytes_accessed=8 * len(steps) * rows * whole.shape[1], transcendentals=0
-        ),
-        name="pick",
-    )(place, whole)
 
 
 def roll_own(greens):
@@ -450,7 +437,7 @@
         out_shape=jax.ShapeDtypeStruct((STEPS, *greens.shape), jnp.float32),
         in_specs=[in_vmem()],
         out_specs=in_vmem(),
-        compiler_params=params(24),
+        compiler_params=params(4),
         cost_estimate=cost(3, 5),
         name="roll_own",
     )(greens)
@@ -470,7 +457,7 @@
             pltpu.VMEM((2, chunk, points, width), jnp.float32),
             pltpu.SemaphoreType.DMA((2,)),
         ],
-        compiler_params=params(24),
+        compiler_params=params(6),
         cost_estimate=cost(32, 5),
         name="propagate",
     )(greens, effective, jnp.asarray(spread))
@@ -523,11 +510,10 @@
         moved = []
         for x in (green_row, screened):
             whole = x.reshape(parts * TILE * local, width)
-            picked = pick(seat, whole, order[:2], parts) if x is green_row else []
             found = {0: whole}
-            for n, step in enumerate(order):
+            for step in order:
                 start = partner_of(place, step, parts) * (TILE * local)
-                block = picked[n] if n < len(picked) else lax.dynamic_slice_in_dim(whole, start, TILE * local)
+                block = lax.dynamic_slice_in_dim(whole, start, TILE * local)
                 found[step] = exchange(block, "ka", step, parts)
             moved.append([found])
         order = [0] + order
@@ -569,14 +555,14 @@
         mine = jnp.concatenate([pieces[step] for step in range(0, parts, 2)], axis=0) + pairs
         pieces = [mine[n * local : (n + 1) * local] for n in range(parts // 2)]
         collision = tree_sum(
-            pieces[:1] + [exchange(pieces[n], "ka", 2 * n, parts) for n in range(1, parts // 2)]
+            pieces[:1] + [exchange(pieces[n], "ka", 2 * n, parts) for n in range(parts // 2 - 1, 0, -1)]
         )
     else:
         collision = tree_sum(
             pieces[:1] + [exchange(pieces[step], "ka", step, parts) for step in range(1, parts)]
         )
     collision = tree_sum(
-        [collision] + [exchange(collision, "hist", step, blocks) for step in range(1, blocks)]
+        [collision] + [exchange(collision, "hist", step, blocks) for step in range(blocks - 1, 0, -1)]
     )
     return propagate(own_greens, hamilton + collision)
 

time: 99.7 us -> 87.9 us (0.88)
  Pallas kernels: 43.6 us -> 25.5 us
  waiting for transfers between devices: 22.6 us -> 29.3 us
  local copies, waits for them, and re-layouts: 10.2 us -> 6.81 us
  starting transfers between devices: 21.9 us -> 25.2 us
    pallas_call x1 -> x0, Pallas kernels: 19 us -> none  [pick(): pl.pallas_call(functools.partial(pick_kernel, steps, parts), out_shape=[j...]
    ppermute x21, waiting for transfers between devices: 22.6 us -> 29.3 us  [exchange(): return lax.ppermute(value, axis, pairs)]
    ppermute x21, starting transfers between devices: 21.9 us -> 25.2 us  [exchange(): return lax.ppermute(value, axis, pairs)]
    dynamic_slice x2, local copies, waits for them, and re-layouts: 5.45 us -> 2.94 us  [per_device(): block = lax.dynamic_slice_in_dim(whole, start, TILE * local)]
    unnamed x38 -> x40, local copies, waits for them, and re-layouts: 4.59 us -> 3.66 us
  transfers between devices with their start and end apart: 21 -> 21, of which waited for: 10 -> 14; matrix products, arithmetic and copies ran while one was open for 3% -> 2% of each run, Pallas kernels for 30% -> 14%
where the time goes in v4:
time: 87.9 us; the launch traced here: 87.8 us
  waiting for transfers between devices  29.3 us (33%)
  Pallas kernels  25.5 us (29%)
  starting transfers between devices  25.2 us (29%)
  local copies, waits for them, and re-layouts  6.81 us (8%)
  between operations  0.92 us (1%)
    ppermute x21, waiting for transfers between devices, exchange(): return lax.ppermute(value, axis, pairs)  29.3 us
    ppermute x21, starting transfers between devices, exchange(): return lax.ppermute(value, axis, pairs)  25.2 us
    pallas_call x1, Pallas kernels, backward(): pl.pallas_call(functools.partial(backward_kernel, steps, parts, share), o...  8.46 us
    pallas_call x1, Pallas kernels, forward(): pl.pallas_call(functools.partial(forward_kernel, steps, parts), out_shape...  5.78 us
    pallas_call x1, Pallas kernels, propagate(): pl.pallas_call(propagate_kernel, out_shape=jax.ShapeDtypeStruct(greens.sh...  5.03 us
    unnamed x40, local copies, waits for them, and re-layouts  3.66 us
    pallas_call x1, Pallas kernels, early_lines(): pl.pallas_call(functools.partial(early_kernel, steps, parts), out_shape=j...  3.26 us
    dynamic_slice x2, local copies, waits for them, and re-layouts, per_device(): block = lax.dynamic_slice_in_dim(whole, start, TILE * local)  2.94 us
  transfers between devices with their start and end apart: 21, of which 14 were waited for; matrix products, arithmetic and copies ran while one was open for 2% of the time, Pallas kernels for 14%

profile of v4, /device:TPU:0, one launch (start us, length us, event | category | flops | bytes accessed | tf_op | source)
XLA Modules:
  0.0 87.8 jit_solution(15863335679312729364)
XLA Ops:
  0.0 1.8 %constant_dynamic-slice_fusion.15 = (f32[576,128]{1,0:T(8,128)S(1)}, f32[576,128]{1,0:T(8,128)S(1)}, f32[576,128]{1,0:T(8,128)S(1)}, f32[576,128]{1,0:T(8,128)S(...) fusion(f32[4608,128]{1,0:T(8,128)} %bitcast.5, s32[]{:T(128)S(6)} %select_n.69, ...), kind=kLoop, calls=%fused_computation.20 | loop fusion | bytes 4128796 | tf_op jit(solution)/shard_map/dynamic_slice | solution.py:516
  1.8 3.0 %collective-permute-start = (f32[576,128]{1,0:T(8,128)S(1)}, f32[576,128]{1,0:T(8,128)S(1)}, u32[]{:S(2)}, u32[]{:S(2)}) collective-permute-start(f32[576,128]{1,0:T(8,128)S(1)} %get-tuple-element.24), channel_id=1, source_target_pairs={{0,16},{4,20},{8,24},{12,28},{16,0},{20,4},{24,8},{28,12},{1,17},{... | collective-permute-start | bytes 884744 | tf_op jit(solution)/shard_map/ppermute | solution.py:476
  4.9 1.5 %collective-permute-start.1 = (f32[576,128]{1,0:T(8,128)S(1)}, f32[576,128]{1,0:T(8,128)S(1)}, u32[]{:S(2)}, u32[]{:S(2)}) collective-permute-start(f32[576,128]{1,0:T(8,128)S(1)} %get-tuple-element.23), channel_id=1, source_target_pairs={{0,8},{4,12},{8,0},{12,4},{16,24},{20,28},{24,16},{28,20},{1,9},{5... | collective-permute-start | bytes 884744 | tf_op jit(solution)/shard_map/ppermute | solution.py:476
  6.4 0.3 collective-permute-start.3
  6.7 2.9 %collective-permute-start.4 = (f32[576,128]{1,0:T(8,128)S(1)}, f32[576,128]{1,0:T(8,128)S(1)}, u32[]{:S(2)}, u32[]{:S(2)}) collective-permute-start(f32[576,128]{1,0:T(8,128)S(1)} %get-tuple-element.20), channel_id=1, source_target_pairs={{0,24},{4,28},{8,16},{12,20},{16,8},{20,12},{24,0},{28,4},{1,25},{... | collective-permute-start | bytes 884744 | tf_op jit(solution)/shard_map/ppermute | solution.py:476
  9.6 1.2 %constant_dynamic-slice_fusion.8 = (f32[576,128]{1,0:T(8,128)}, f32[576,128]{1,0:T(8,128)}, f32[576,128]{1,0:T(8,128)S(1)}, f32[576,128]{1,0:T(8,128)S(1)}, f32[...) fusion(f32[4608,128]{1,0:T(8,128)S(1)} %bitcast.7, s32[]{:T(128)S(6)} %select_n.66, s32[]{:T(128)S(6)} %select_n.65, ...), kind=kLoop, calls=%fused_computation.13 | loop fusion | bytes 4128796 | tf_op jit(solution)/shard_map/dynamic_slice | solution.py:516
  10.7 2.0 %collective-permute-done.refs_1_ = f32[576,128]{1,0:T(8,128)S(1)} collective-permute-done((f32[576,128]{1,0:T(8,128)S(1)}, f32[576,128]{1,0:T(8,128)S(1)}, u32[]{:S(2)}, u32[]{:S(2)}) %collective-permute-start) | collective-permute-done | bytes 294944 | tf_op jit(solution)/shard_map/ppermute | solution.py:476
  12.7 0.4 collective-permute-start.5
  13.1 1.7 %collective-permute-done.1.refs_2_ = f32[576,128]{1,0:T(8,128)S(1)} collective-permute-done((f32[576,128]{1,0:T(8,128)S(1)}, f32[576,128]{1,0:T(8,128)S(1)}, u32[]{:S(2)}, u32[]{:S(2)}) %collective-permute-start.1) | collective-permute-done | bytes 294944 | tf_op jit(solution)/shard_map/ppermute | solution.py:476
  14.8 1.0 %collective-permute-start.6 = (f32[576,128]{1,0:T(8,128)S(1)}, f32[576,128]{1,0:T(8,128)S(1)}, u32[]{:S(2)}, u32[]{:S(2)}) collective-permute-start(f32[576,128]{1,0:T(8,128)S(1)} %get-tuple-element.18), channel_id=1, source_target_pairs={{0,4},{4,0},{8,12},{12,8},{16,20},{20,16},{24,28},{28,24},{1,5},{5... | collective-permute-start | bytes 884744 | tf_op jit(solution)/shard_map/ppermute | solution.py:476
  15.8 1.8 %collective-permute-done.2.refs_3_ = f32[576,128]{1,0:T(8,128)S(1)} collective-permute-done((f32[576,128]{1,0:T(8,128)S(1)}, f32[576,128]{1,0:T(8,128)S(1)}, u32[]{:S(2)}, u32[]{:S(2)}) %collective-permute-start.2) | collective-permute-done | bytes 294944 | tf_op jit(solution)/shard_map/ppermute | solution.py:476
  17.6 1.2 %collective-permute-start.10 = (f32[576,128]{1,0:T(8,128)S(1)}, f32[576,128]{1,0:T(8,128)S(1)}, u32[]{:S(2)}, u32[]{:S(2)}) collective-permute-start(f32[576,128]{1,0:T(8,128)S(1)} %get-tuple-element.14), channel_id=1, source_target_pairs={{0,16},{4,20},{8,24},{12,28},{16,0},{20,4},{24,8},{28,12},{1,17},{... | collective-permute-start | bytes 884744 | tf_op jit(solution)/shard_map/ppermute | solution.py:476
  18.8 1.3 %collective-permute-done.3.refs_4_ = f32[576,128]{1,0:T(8,128)S(1)} collective-permute-done((f32[576,128]{1,0:T(8,128)S(1)}, f32[576,128]{1,0:T(8,128)S(1)}, u32[]{:S(2)}, u32[]{:S(2)}) %collective-permute-start.3) | collective-permute-done | bytes 294944 | tf_op jit(solution)/shard_map/ppermute | solution.py:476
  20.1 0.5 collective-permute-start.11
  20.7 6.3 %collective-permute-done.4.refs_5_ = f32[576,128]{1,0:T(8,128)S(1)} collective-permute-done((f32[576,128]{1,0:T(8,128)S(1)}, f32[576,128]{1,0:T(8,128)S(1)}, u32[]{:S(2)}, u32[]{:S(2)}) %collective-permute-start.4) | collective-permute-done | bytes 294944 | tf_op jit(solution)/shard_map/ppermute | solution.py:476
  27.0 0.7 copy-done.5
  27.7 5.1 %collective-permute-done.5.refs_6_ = f32[576,128]{1,0:T(8,128)S(1)} collective-permute-done((f32[576,128]{1,0:T(8,128)S(1)}, f32[576,128]{1,0:T(8,128)S(1)}, u32[]{:S(2)}, u32[]{:S(2)}) %collective-permute-start.5) | collective-permute-done | bytes 294944 | tf_op jit(solution)/shard_map/ppermute | solution.py:476
  32.8 0.7 copy-done.7
  33.5 1.9 %collective-permute-start.13 = (f32[576,128]{1,0:T(8,128)}, f32[576,128]{1,0:T(8,128)}, u32[]{:S(2)}, u32[]{:S(2)}) collective-permute-start(f32[576,128]{1,0:T(8,128)} %get-tuple-element.11), channel_id=1, source_target_pairs={{0,12},{4,8},{8,4},{12,0},{16,28},{20,24},{24,20},{28,16},{1,13},{... | collective-permute-start | bytes 884744 | tf_op jit(solution)/shard_map/ppermute | solution.py:476
  35.4 0.7 copy-done.9
  36.1 1.5 %collective-permute-start.7 = (f32[576,128]{1,0:T(8,128)}, f32[576,128]{1,0:T(8,128)}, u32[]{:S(2)}, u32[]{:S(2)}) collective-permute-start(f32[576,128]{1,0:T(8,128)} %get-tuple-element.17), channel_id=1, source_target_pairs={{0,24},{4,28},{8,16},{12,20},{16,8},{20,12},{24,0},{28,4},{1,25},{... | collective-permute-start | bytes 884744 | tf_op jit(solution)/shard_map/ppermute | solution.py:476
  37.6 0.8 collective-permute-done.10.refs_1_
  38.4 0.7 copy-done.11
  39.1 2.4 %collective-permute-start.8 = (f32[576,128]{1,0:T(8,128)}, f32[576,128]{1,0:T(8,128)}, u32[]{:S(2)}, u32[]{:S(2)}) collective-permute-start(f32[576,128]{1,0:T(8,128)} %get-tuple-element.16), channel_id=1, source_target_pairs={{0,28},{4,24},{8,20},{12,16},{16,12},{20,8},{24,4},{28,0},{1,29},{... | collective-permute-start | bytes 884744 | tf_op jit(solution)/shard_map/ppermute | solution.py:476
  41.6 0.7 copy-done.13
  42.3 0.1 select_reduce_fusion
  43.1 0.1 dynamic_slice.76
  43.2 2.9 %roll_own.1._.greens_ref = f32[4,64,72,128]{3,2,1,0:T(8,128)S(1)} custom-call(f32[64,72,128]{2,1,0:T(8,128)S(1)} %copy-done), custom_call_target="tpu_custom_call" | custom-call | flops 1769472 | bytes 11796480 | tf_op jit(solution)/shard_map/roll_own/pallas_call | solution.py:435
  46.2 5.8 %forward.1 = (f32[576,8,128]{2,1,0:T(8,128)S(1)}, f32[4,4608,128]{2,1,0:T(8,128)S(1)}) custom-call(s32[1]{0:T(128)} %bitcast.place_ref, f32[4608,128]{1,0:T(8,128)S(1)} %bitcast.6, f32[576,128]{1,0:T(8,128)S(1)} %collective-permute-done.refs_1_, f32[576,128]{1,0:T(8,128)S(1)} %collective-permute-done.1.refs_2_, ...), custom_call_target="tpu_custom_call" | custom-call | flops 235929600 | bytes 14155776 | tf_op jit(solution)/shard_map/forward/pallas_call | solution.py:379
  52.0 0.1 squeeze.8.weight_ref
  52.1 0.0 copy-start.16
  52.1 3.3 %early.1.refs_3_ = f32[576,8,128]{2,1,0:T(8,128)S(1)} custom-call(s32[1]{0:T(128)} %bitcast.place_ref, f32[576,8,128]{2,1,0:T(8,128)S(1)} %get-tuple-element.8.lattice_ref, f32[8,128]{1,0:T(8,128)S(1)} %squeeze.8.weight_ref, f32[4,64,72,128]{3,2,1,0:T(8,128)S(1)} %roll_own.1._.greens_ref, f32[4608,128]{1,0:T(8,128)S(1)} %bitcast.8, ...), custom_call_target="tpu_custom_call" | custom-call | flops 88473600 | bytes 7077888 | tf_op jit(solution)/shard_map/early/pallas_call | solution.py:396
  55.4 1.6 %collective-permute-done.8.refs_1_ = f32[576,128]{1,0:T(8,128)} collective-permute-done((f32[576,128]{1,0:T(8,128)}, f32[576,128]{1,0:T(8,128)}, u32[]{:S(2)}, u32[]{:S(2)}) %collective-permute-start.8) | collective-permute-done | bytes 294944 | tf_op jit(solution)/shard_map/ppermute | solution.py:476
  56.9 0.0 copy-start.3
  57.0 8.5 %backward.1 = (f32[576,128]{1,0:T(8,128)S(1)}, f32[576,8,128]{2,1,0:T(8,128)S(1)}) custom-call(s32[1]{0:T(128)} %bitcast.place_ref, f32[576,8,128]{2,1,0:T(8,128)S(1)} %get-tuple-element.8.lattice_ref, f32[8,128]{1,0:T(8,128)S(1)} %squeeze.8.weight_ref, f32[72,128]{1,0:T(8,128)S(1)} %copy-done.15, ...), custom_call_target="tpu_custom_call", output_to_operand_aliasing={{1}: (10, {})} | custom-call | flops 471859200 | bytes 14155776 | tf_op jit(solution)/shard_map/backward/pallas_call | solution.py:412
  65.5 0.5 collective-permute-start.14
  66.0 1.0 %collective-permute-done.14 = f32[288,128]{1,0:T(8,128)S(1)} collective-permute-done((f32[288,128]{1,0:T(8,128)S(1)}, f32[288,128]{1,0:T(8,128)S(1)}, u32[]{:S(2)}, u32[]{:S(2)}) %collective-permute-start.14) | collective-permute-done | bytes 147488 | tf_op jit(solution)/shard_map/ppermute | solution.py:476
  67.0 2.7 %collective-permute-start.15 = (f32[72,128]{1,0:T(8,128)S(1)}, f32[72,128]{1,0:T(8,128)S(1)}, u32[]{:S(2)}, u32[]{:S(2)}) collective-permute-start(f32[72,128]{1,0:T(8,128)S(1)} %get-tuple-element.35), channel_id=1, source_target_pairs={{0,24},{4,28},{8,16},{12,20},{16,8},{20,12},{24,0},{28,4},{1,25},{... | collective-permute-start | bytes 110600 | tf_op jit(solution)/shard_map/ppermute | solution.py:476
  69.7 0.5 collective-permute-start.16
  70.2 0.4 collective-permute-start.17
  70.6 1.4 %collective-permute-done.15 = f32[72,128]{1,0:T(8,128)S(1)} collective-permute-done((f32[72,128]{1,0:T(8,128)S(1)}, f32[72,128]{1,0:T(8,128)S(1)}, u32[]{:S(2)}, u32[]{:S(2)}) %collective-permute-start.15) | collective-permute-done | bytes 36896 | tf_op jit(solution)/shard_map/ppermute | solution.py:476
  72.0 1.7 %collective-permute-done.16 = f32[72,128]{1,0:T(8,128)S(1)} collective-permute-done((f32[72,128]{1,0:T(8,128)S(1)}, f32[72,128]{1,0:T(8,128)S(1)}, u32[]{:S(2)}, u32[]{:S(2)}) %collective-permute-start.16) | collective-permute-done | bytes 36896 | tf_op jit(solution)/shard_map/ppermute | solution.py:476
  73.7 0.5 collective-permute-done.17
  74.2 3.7 %collective-permute-start.18 = (f32[72,128]{1,0:T(8,128)S(1)}, f32[72,128]{1,0:T(8,128)S(1)}, u32[]{:S(2)}, u32[]{:S(2)}) collective-permute-start(f32[72,128]{1,0:T(8,128)S(1)} %fusion), channel_id=1, source_target_pairs={{0,3},{1,2},{2,1},{3,0},{4,7},{5,6},{6,5},{7,4},{8,11},{9,10},{10,... | collective-permute-start | bytes 110600 | tf_op jit(solution)/shard_map/ppermute | solution.py:476
  77.9 0.8 collective-permute-start.20
  78.6 1.4 %collective-permute-done.18 = f32[72,128]{1,0:T(8,128)S(1)} collective-permute-done((f32[72,128]{1,0:T(8,128)S(1)}, f32[72,128]{1,0:T(8,128)S(1)}, u32[]{:S(2)}, u32[]{:S(2)}) %collective-permute-start.18) | collective-permute-done | bytes 36896 | tf_op jit(solution)/shard_map/ppermute | solution.py:476
  80.0 2.7 %collective-permute-done.19 = f32[72,128]{1,0:T(8,128)S(1)} collective-permute-done((f32[72,128]{1,0:T(8,128)S(1)}, f32[72,128]{1,0:T(8,128)S(1)}, u32[]{:S(2)}, u32[]{:S(2)}) %collective-permute-start.19) | collective-permute-done | bytes 36896 | tf_op jit(solution)/shard_map/ppermute | solution.py:476
  82.7 5.0 %propagate.1 = f32[64,72,128]{2,1,0:T(8,128)} custom-call(f32[4,64,72,128]{3,2,1,0:T(8,128)S(1)} %roll_own.1._.greens_ref, f32[72,128]{1,0:T(8,128)S(1)} %add_add_fusion.effective_ref, bf16[128,2048]{1,0:T(8,128)(2,1)S(1)} %copy-done.3), custom_call_target="tpu_custom_call" | custom-call | flops 18874368 | bytes 11796480 | tf_op jit(solution)/shard_map/propagate/pallas_call | solution.py:450
  (51 shorter events, 0.2 us)
Async XLA Ops:
  0.0 9.6 %copy-start.1 = (f32[64,72,128]{2,1,0:T(8,128)S(1)}, f32[64,72,128]{2,1,0:T(8,128)}, u32[]{:S(2)}) copy-start(f32[64,72,128]{2,1,0:T(8,128)} %param.11) | copy-start | bytes 7077892
  1.8 40.5 %copy-start.18 = (s32[64]{0:T(128)S(1)}, s32[64]{0:T(128)}, u32[]{:S(2)}) copy-start(s32[64]{0:T(128)} %param.14) | copy-start | bytes 772
  1.8 40.5 %copy-start.19 = (f32[4]{0:T(128)S(1)}, f32[4]{0:T(128)}, u32[]{:S(2)}) copy-start(f32[4]{0:T(128)} %constant.46.clone) | copy-start | bytes 52
  1.8 41.3 %copy-start = (f32[64,72,128]{2,1,0:T(8,128)S(1)}, f32[64,72,128]{2,1,0:T(8,128)}, u32[]{:S(2)}) copy-start(f32[64,72,128]{2,1,0:T(8,128)} %green_ref.1) | copy-start | bytes 7077892
  1.8 10.9 %collective-permute-start = (f32[576,128]{1,0:T(8,128)S(1)}, f32[576,128]{1,0:T(8,128)S(1)}, u32[]{:S(2)}, u32[]{:S(2)}) collective-permute-start(f32[576,128]{1,0:T(8,128)S(1)} %get-tuple-element.24), channel_id=1, source_target_pairs={{0,16},{4,20},{8,24},{12,28},{16,0},{20,4},{24,8},{28,12},{1,17},{... | collective-permute-start | bytes 884744 | tf_op jit(solution)/shard_map/ppermute | solution.py:476
  4.9 9.9 %collective-permute-start.1 = (f32[576,128]{1,0:T(8,128)S(1)}, f32[576,128]{1,0:T(8,128)S(1)}, u32[]{:S(2)}, u32[]{:S(2)}) collective-permute-start(f32[576,128]{1,0:T(8,128)S(1)} %get-tuple-element.23), channel_id=1, source_target_pairs={{0,8},{4,12},{8,0},{12,4},{16,24},{20,28},{24,16},{28,20},{1,9},{5... | collective-permute-start | bytes 884744 | tf_op jit(solution)/shard_map/ppermute | solution.py:476
  6.4 11.2 %collective-permute-start.2 = (f32[576,128]{1,0:T(8,128)S(1)}, f32[576,128]{1,0:T(8,128)S(1)}, u32[]{:S(2)}, u32[]{:S(2)}) collective-permute-start(f32[576,128]{1,0:T(8,128)S(1)} %get-tuple-element.22), channel_id=1, source_target_pairs={{0,20},{4,16},{8,28},{12,24},{16,4},{20,0},{24,12},{28,8},{1,21},{... | collective-permute-start | bytes 884744 | tf_op jit(solution)/shard_map/ppermute | solution.py:476
  6.4 13.8 %collective-permute-start.3 = (f32[576,128]{1,0:T(8,128)S(1)}, f32[576,128]{1,0:T(8,128)S(1)}, u32[]{:S(2)}, u32[]{:S(2)}) collective-permute-start(f32[576,128]{1,0:T(8,128)S(1)} %get-tuple-element.21), channel_id=1, source_target_pairs={{0,12},{4,8},{8,4},{12,0},{16,28},{20,24},{24,20},{28,16},{1,13},{... | collective-permute-start | bytes 884744 | tf_op jit(solution)/shard_map/ppermute | solution.py:476
  6.7 20.3 %collective-permute-start.4 = (f32[576,128]{1,0:T(8,128)S(1)}, f32[576,128]{1,0:T(8,128)S(1)}, u32[]{:S(2)}, u32[]{:S(2)}) collective-permute-start(f32[576,128]{1,0:T(8,128)S(1)} %get-tuple-element.20), channel_id=1, source_target_pairs={{0,24},{4,28},{8,16},{12,20},{16,8},{20,12},{24,0},{28,4},{1,25},{... | collective-permute-start | bytes 884744 | tf_op jit(solution)/shard_map/ppermute | solution.py:476
  12.7 20.1 %collective-permute-start.5 = (f32[576,128]{1,0:T(8,128)S(1)}, f32[576,128]{1,0:T(8,128)S(1)}, u32[]{:S(2)}, u32[]{:S(2)}) collective-permute-start(f32[576,128]{1,0:T(8,128)S(1)} %get-tuple-element.19), channel_id=1, source_target_pairs={{0,28},{4,24},{8,20},{12,16},{16,12},{20,8},{24,4},{28,0},{1,29},{... | collective-permute-start | bytes 884744 | tf_op jit(solution)/shard_map/ppermute | solution.py:476
  14.8 20.6 %collective-permute-start.6 = (f32[576,128]{1,0:T(8,128)S(1)}, f32[576,128]{1,0:T(8,128)S(1)}, u32[]{:S(2)}, u32[]{:S(2)}) collective-permute-start(f32[576,128]{1,0:T(8,128)S(1)} %get-tuple-element.18), channel_id=1, source_target_pairs={{0,4},{4,0},{8,12},{12,8},{16,20},{20,16},{24,28},{28,24},{1,5},{5... | collective-permute-start | bytes 884744 | tf_op jit(solution)/shard_map/ppermute | solution.py:476
  17.6 20.8 %collective-permute-start.10 = (f32[576,128]{1,0:T(8,128)S(1)}, f32[576,128]{1,0:T(8,128)S(1)}, u32[]{:S(2)}, u32[]{:S(2)}) collective-permute-start(f32[576,128]{1,0:T(8,128)S(1)} %get-tuple-element.14), channel_id=1, source_target_pairs={{0,16},{4,20},{8,24},{12,28},{16,0},{20,4},{24,8},{28,12},{1,17},{... | collective-permute-start | bytes 884744 | tf_op jit(solution)/shard_map/ppermute | solution.py:476
  20.1 21.4 %collective-permute-start.11 = (f32[576,128]{1,0:T(8,128)S(1)}, f32[576,128]{1,0:T(8,128)S(1)}, u32[]{:S(2)}, u32[]{:S(2)}) collective-permute-start(f32[576,128]{1,0:T(8,128)S(1)} %get-tuple-element.13), channel_id=1, source_target_pairs={{0,8},{4,12},{8,0},{12,4},{16,24},{20,28},{24,16},{28,20},{1,9},{5... | collective-permute-start | bytes 884744 | tf_op jit(solution)/shard_map/ppermute | solution.py:476
  27.0 0.7 copy-start.5
  27.7 24.2 %collective-permute-start.12 = (f32[576,128]{1,0:T(8,128)}, f32[576,128]{1,0:T(8,128)}, u32[]{:S(2)}, u32[]{:S(2)}) collective-permute-start(f32[576,128]{1,0:T(8,128)} %get-tuple-element.12), channel_id=1, source_target_pairs={{0,20},{4,16},{8,28},{12,24},{16,4},{20,0},{24,12},{28,8},{1,21},{... | collective-permute-start | bytes 884744 | tf_op jit(solution)/shard_map/ppermute | solution.py:476
  32.8 0.7 copy-start.7
  33.5 18.4 %collective-permute-start.13 = (f32[576,128]{1,0:T(8,128)}, f32[576,128]{1,0:T(8,128)}, u32[]{:S(2)}, u32[]{:S(2)}) collective-permute-start(f32[576,128]{1,0:T(8,128)} %get-tuple-element.11), channel_id=1, source_target_pairs={{0,12},{4,8},{8,4},{12,0},{16,28},{20,24},{24,20},{28,16},{1,13},{... | collective-permute-start | bytes 884744 | tf_op jit(solution)/shard_map/ppermute | solution.py:476
  35.4 0.7 copy-start.9
  36.1 19.3 %collective-permute-start.7 = (f32[576,128]{1,0:T(8,128)}, f32[576,128]{1,0:T(8,128)}, u32[]{:S(2)}, u32[]{:S(2)}) collective-permute-start(f32[576,128]{1,0:T(8,128)} %get-tuple-element.17), channel_id=1, source_target_pairs={{0,24},{4,28},{8,16},{12,20},{16,8},{20,12},{24,0},{28,4},{1,25},{... | collective-permute-start | bytes 884744 | tf_op jit(solution)/shard_map/ppermute | solution.py:476
  38.4 0.7 copy-start.11
  39.1 17.8 %collective-permute-start.8 = (f32[576,128]{1,0:T(8,128)}, f32[576,128]{1,0:T(8,128)}, u32[]{:S(2)}, u32[]{:S(2)}) collective-permute-start(f32[576,128]{1,0:T(8,128)} %get-tuple-element.16), channel_id=1, source_target_pairs={{0,28},{4,24},{8,20},{12,16},{16,12},{20,8},{24,4},{28,0},{1,29},{... | collective-permute-start | bytes 884744 | tf_op jit(solution)/shard_map/ppermute | solution.py:476
  41.6 0.7 copy-start.13
  42.3 14.6 %collective-permute-start.9 = (f32[576,128]{1,0:T(8,128)}, f32[576,128]{1,0:T(8,128)}, u32[]{:S(2)}, u32[]{:S(2)}) collective-permute-start(f32[576,128]{1,0:T(8,128)} %get-tuple-element.15), channel_id=1, source_target_pairs={{0,4},{4,0},{8,12},{12,8},{16,20},{20,16},{24,28},{28,24},{1,5},{5... | collective-permute-start | bytes 884744 | tf_op jit(solution)/shard_map/ppermute | solution.py:476
  43.2 3.0 %copy-start.6 = (f32[576,128]{1,0:T(8,128)S(1)}, f32[576,128]{1,0:T(8,128)}, u32[]{:S(2)}) copy-start(f32[576,128]{1,0:T(8,128)} %copy-done.5) | copy-start | bytes 884740
  43.2 3.0 %copy-start.8 = (f32[576,128]{1,0:T(8,128)S(1)}, f32[576,128]{1,0:T(8,128)}, u32[]{:S(2)}) copy-start(f32[576,128]{1,0:T(8,128)} %copy-done.7) | copy-start | bytes 884740
  43.2 3.0 %copy-start.10 = (f32[576,128]{1,0:T(8,128)S(1)}, f32[576,128]{1,0:T(8,128)}, u32[]{:S(2)}) copy-start(f32[576,128]{1,0:T(8,128)} %copy-done.9) | copy-start | bytes 884740
  46.1 5.9 %copy-start.2 = (f32[64,72,128]{2,1,0:T(8,128)S(1)}, f32[64,72,128]{2,1,0:T(8,128)}, u32[]{:S(2)}) copy-start(f32[64,72,128]{2,1,0:T(8,128)} %param.11) | copy-start | bytes 7077892
  46.1 5.9 %copy-start.12 = (f32[576,128]{1,0:T(8,128)S(1)}, f32[576,128]{1,0:T(8,128)}, u32[]{:S(2)}) copy-start(f32[576,128]{1,0:T(8,128)} %copy-done.11) | copy-start | bytes 884740
  46.1 5.9 %copy-start.14 = (f32[576,128]{1,0:T(8,128)S(1)}, f32[576,128]{1,0:T(8,128)}, u32[]{:S(2)}) copy-start(f32[576,128]{1,0:T(8,128)} %copy-done.13) | copy-start | bytes 884740
  52.1 4.9 %copy-start.4 = (bf16[2048,128]{1,0:T(8,128)(2,1)S(1)}, bf16[2048,128]{1,0:T(8,128)(2,1)}, u32[]{:S(2)}) copy-start(bf16[2048,128]{1,0:T(8,128)(2,1)} %constant.48.clone.gather_ref) | copy-start | bytes 1572868
  52.1 4.9 %copy-start.15 = (f32[72,128]{1,0:T(8,128)S(1)}, f32[72,128]{1,0:T(8,128)}, u32[]{:S(2)}) copy-start(f32[72,128]{1,0:T(8,128)} %equal_ref.1) | copy-start | bytes 110596
  52.1 4.9 %copy-start.16 = (f32[8,128]{1,0:T(8,128)S(1)}, f32[8,128]{1,0:T(8,128)}, u32[]{:S(2)}) copy-start(f32[8,128]{1,0:T(8,128)} %constant.47.clone.sign_ref) | copy-start | bytes 12292
  56.9 25.8 %copy-start.17 = (f32[72,128]{1,0:T(8,128)S(1)}, f32[72,128]{1,0:T(8,128)}, u32[]{:S(2)}) copy-start(f32[72,128]{1,0:T(8,128)} %param.12) | copy-start | bytes 110596
  56.9 25.8 %copy-start.3 = (bf16[128,2048]{1,0:T(8,128)(2,1)S(1)}, bf16[128,2048]{1,0:T(8,128)(2,1)}, u32[]{:S(2)}) copy-start(bf16[128,2048]{1,0:T(8,128)(2,1)} %constant.49.clone.spread_ref) | copy-start | bytes 1572868
  65.5 1.5 %collective-permute-start.14 = (f32[288,128]{1,0:T(8,128)S(1)}, f32[288,128]{1,0:T(8,128)S(1)}, u32[]{:S(2)}, u32[]{:S(2)}) collective-permute-start(f32[288,128]{1,0:T(8,128)S(1)} %pad_maximum_fusion), channel_id=1, source_target_pairs={{0,4},{4,0},{8,12},{12,8},{16,20},{20,16},{24,28},{28,24},{1,5},{5... | collective-permute-start | bytes 442376 | tf_op jit(solution)/shard_map/ppermute | solution.py:476
  67.0 4.9 %collective-permute-start.15 = (f32[72,128]{1,0:T(8,128)S(1)}, f32[72,128]{1,0:T(8,128)S(1)}, u32[]{:S(2)}, u32[]{:S(2)}) collective-permute-start(f32[72,128]{1,0:T(8,128)S(1)} %get-tuple-element.35), channel_id=1, source_target_pairs={{0,24},{4,28},{8,16},{12,20},{16,8},{20,12},{24,0},{28,4},{1,25},{... | collective-permute-start | bytes 110600 | tf_op jit(solution)/shard_map/ppermute | solution.py:476
  69.7 4.0 %collective-permute-start.16 = (f32[72,128]{1,0:T(8,128)S(1)}, f32[72,128]{1,0:T(8,128)S(1)}, u32[]{:S(2)}, u32[]{:S(2)}) collective-permute-start(f32[72,128]{1,0:T(8,128)S(1)} %get-tuple-element.34), channel_id=1, source_target_pairs={{0,16},{4,20},{8,24},{12,28},{16,0},{20,4},{24,8},{28,12},{1,17},{... | collective-permute-start | bytes 110600 | tf_op jit(solution)/shard_map/ppermute | solution.py:476
  70.2 4.0 %collective-permute-start.17 = (f32[72,128]{1,0:T(8,128)S(1)}, f32[72,128]{1,0:T(8,128)S(1)}, u32[]{:S(2)}, u32[]{:S(2)}) collective-permute-start(f32[72,128]{1,0:T(8,128)S(1)} %get-tuple-element.33), channel_id=1, source_target_pairs={{0,8},{4,12},{8,0},{12,4},{16,24},{20,28},{24,16},{28,20},{1,9},{5... | collective-permute-start | bytes 110600 | tf_op jit(solution)/shard_map/ppermute | solution.py:476
  74.2 5.8 %collective-permute-start.18 = (f32[72,128]{1,0:T(8,128)S(1)}, f32[72,128]{1,0:T(8,128)S(1)}, u32[]{:S(2)}, u32[]{:S(2)}) collective-permute-start(f32[72,128]{1,0:T(8,128)S(1)} %fusion), channel_id=1, source_target_pairs={{0,3},{1,2},{2,1},{3,0},{4,7},{5,6},{6,5},{7,4},{8,11},{9,10},{10,... | collective-permute-start | bytes 110600 | tf_op jit(solution)/shard_map/ppermute | solution.py:476
  77.9 4.9 %collective-permute-start.19 = (f32[72,128]{1,0:T(8,128)S(1)}, f32[72,128]{1,0:T(8,128)S(1)}, u32[]{:S(2)}, u32[]{:S(2)}) collective-permute-start(f32[72,128]{1,0:T(8,128)S(1)} %fusion), channel_id=1, source_target_pairs={{0,2},{1,3},{2,0},{3,1},{4,6},{5,7},{6,4},{7,5},{8,10},{9,11},{10,... | collective-permute-start | bytes 110600 | tf_op jit(solution)/shard_map/ppermute | solution.py:476
  77.9 4.9 %collective-permute-start.20 = (f32[72,128]{1,0:T(8,128)S(1)}, f32[72,128]{1,0:T(8,128)S(1)}, u32[]{:S(2)}, u32[]{:S(2)}) collective-permute-start(f32[72,128]{1,0:T(8,128)S(1)} %fusion), channel_id=1, source_target_pairs={{0,1},{1,0},{2,3},{3,2},{4,5},{5,4},{6,7},{7,6},{8,9},{9,8},{10,11... | collective-permute-start | bytes 110600 | tf_op jit(solution)/shard_map/ppermute | solution.py:476

commit v5 on v4

--- a/solution.py
+++ b/solution.py
@@ -42,6 +42,25 @@
     while len(terms) > 1:
         terms = [sum(terms[i : i + 2][1:], terms[i]) for i in range(0, len(terms), 2)]
     return terms[0]
+
+
+def merge_lanes(values):
+    lane = lax.broadcasted_iota(jnp.int32, values[0].shape, 1)
+    while len(values) > 1:
+        half = len(values) // 2
+        lower = lane & half == 0
+        merged = []
+        for x, y in zip(values[:half], values[half:]):
+            rest = jnp.where(lower, y, x)
+            other = jnp.where(lower, pltpu.roll(rest, WIDTH - half, 1), pltpu.roll(rest, half, 1))
+            merged.append(jnp.where(lower, x, y) + other)
+        values = merged
+    return values[0]
+
+
+def split(x):
+    high = x.astype(jnp.bfloat16)
+    return jnp.concatenate([high, (x - high.astype(jnp.float32)).astype(jnp.bfloat16)], axis=1)
 
 
 def dft24(x, sign, low):
@@ -84,17 +103,6 @@
     return [ref[pl.ds(line * SIDE + k2, TILE, stride=stride), :] for k2 in range(SIDE)]
 
 
-def fetch(place, steps, block_refs, held_ref, sems):
-    copies = []
-    for slot, (step, source) in enumerate(zip(steps, block_refs)):
-        rows = held_ref.shape[1]
-        if step == 0 and source.shape[0] != rows:
-            source = source.at[pl.ds(pl.multiple_of(place * rows, TILE), rows)]
-        copies.append(pltpu.make_async_copy(source, held_ref.at[slot], sems.at[slot]))
-        copies[-1].start()
-    return copies
-
-
 def along_first(work_ref, sign, low, store):
     def load(column):
         return [work_ref[k1 * SIDE + column] for k1 in range(SIDE)]
@@ -122,15 +130,12 @@
 
 
 def forward_kernel(steps, parts, place_ref, *refs):
-    block_refs, (lattice_ref, greens_ref, work_ref, held_ref, sems) = refs[: len(steps)], refs[len(steps) :]
+    block_refs, (lattice_ref, greens_ref, work_ref) = refs[: len(steps)], refs[len(steps) :]
     low = lane_sign((TILE, WIDTH))
     place = place_ref[0]
-    copies = fetch(place, steps, block_refs, held_ref, sems)
-    rows = held_ref.shape[1]
+    rows = block_refs[0].shape[0]
     lines = rows // (TILE * SIDE)
-    for slot, step in enumerate(steps):
-        copies[slot].wait()
-        green_ref = held_ref.at[slot]
+    for step, green_ref in zip(steps, block_refs):
         owner = partner_of(place, step, parts)
 
         def along_second(i, carry):
@@ -150,18 +155,15 @@
     along_first(work_ref, -1, low, store)
 
 
-def product_lines(steps, parts, place, lattice_ref, weights, screen_refs, held_ref, sems, work_ref):
+def product_lines(steps, parts, place, lattice_ref, weights, screen_refs, work_ref):
     low = lane_sign((TILE, WIDTH))
     turn = jnp.where(low, -1.0, 1.0)
-    copies = fetch(place, steps, screen_refs, held_ref, sems)
-    lines = held_ref.shape[1] // (TILE * SIDE)
-    for copy in copies:
-        copy.wait()
-
-    def load(slot, step, i):
+    lines = screen_refs[0].shape[0] // (TILE * SIDE)
+
+    def load(screen_ref, step, i):
         line = partner_of(place, step, parts) * lines + i
         rows = []
-        for r2, value in enumerate(load_line(held_ref.at[slot], i)):
+        for r2, value in enumerate(load_line(screen_ref, i)):
             screen = value * weights
             other = swap(screen)
             lattice = lattice_ref[line * SIDE + r2]
@@ -176,36 +178,28 @@
             work_ref[line * SIDE + k2] = value
 
     if lines > 4:
-        for slot, step in enumerate(steps):
-            lax.fori_loop(0, lines, lambda i, carry: store(*load(slot, step, i)), None)
+        for screen_ref, step in zip(screen_refs, steps):
+            lax.fori_loop(0, lines, lambda i, carry: store(*load(screen_ref, step, i)), None)
         return
-    each = [(slot, step, i) for slot, step in enumerate(steps) for i in range(lines)]
-    ready = load(*each[0])
-    for n in range(len(each)):
-        present = ready
-        ready = load(*each[n + 1]) if n + 1 < len(each) else None
-        store(*present)
+    for screen_ref, step in zip(screen_refs, steps):
+        for i in range(lines):
+            store(*load(screen_ref, step, i))
 
 
 def early_kernel(steps, parts, place_ref, lattice_ref, weight_ref, _, *refs):
-    screen_refs, (work_ref, held_ref, sems) = refs[: len(steps)], refs[len(steps) :]
-    product_lines(
-        steps, parts, place_ref[0], lattice_ref, weight_ref[...], screen_refs, held_ref, sems, work_ref
-    )
+    *screen_refs, work_ref = refs
+    product_lines(steps, parts, place_ref[0], lattice_ref, weight_ref[...], screen_refs, work_ref)
 
 
 def backward_kernel(
     steps, parts, share, place_ref, lattice_ref, weight_ref, equal_ref, sign_ref, gather_ref, greens_ref, *refs
 ):
     screen_refs, refs = refs[: len(steps)], refs[len(steps) :]
-    _, partial_ref, work_ref, sigma_ref, sums_ref, pieces_ref, *late = refs
+    _, partial_ref, work_ref, sigma_ref, sums_ref = refs
     points = SIDE * SIDE
     low = lane_sign((TILE, WIDTH))
     if steps:
-        held_ref, sems = late
-        product_lines(
-            steps, parts, place_ref[0], lattice_ref, weight_ref[...], screen_refs, held_ref, sems, work_ref
-        )
+        product_lines(steps, parts, place_ref[0], lattice_ref, weight_ref[...], screen_refs, work_ref)
 
     def store(point, value):
         sigma_ref[pl.ds(point * TILE, TILE), :] = value
@@ -237,9 +231,13 @@
             terms = [sigma * green for sigma in sigmas for green in greens]
             sums = terms if s == 0 else [a + b for a, b in zip(sums, terms)]
             if s == TILE - 1:
+                folded = [
+                    jnp.where(low, sums[2 * q], sums[2 * q + 1])
+                    + sign_ref[q] * swap(jnp.where(low, sums[2 * q + 1], sums[2 * q]))
+                    for q in range(BANDS)
+                ]
                 row = pl.ds(pl.multiple_of((first + tile) * TILE, TILE), TILE)
-                for spot, value in enumerate(sums):
-                    sums_ref[row, spot * WIDTH : (spot + 1) * WIDTH] = value
+                sums_ref[row, :] = merge_lanes(folded)
         return carry
 
     lax.fori_loop(0, points // (TILE * batch), contract, 0)
@@ -249,31 +247,15 @@
     occupied = jnp.sum(jnp.where((inner >= 0) & (inner % (BANDS + 1) == 0), equal_ref[...], 0.0))
     spots = lax.broadcasted_iota(jnp.int32, (points, WIDTH), 1)
     on_diagonal = (spots < ENTRIES) & (spots % (BANDS + 1) == 0)
-    lower = spots < ENTRIES
-    for pair in range(STEPS * STEPS // 2):
-        first_part = sums_ref[:, 2 * pair * WIDTH : (2 * pair + 1) * WIDTH]
-        second_part = sums_ref[:, (2 * pair + 1) * WIDTH : (2 * pair + 2) * WIDTH]
-        folded = jnp.where(lower, first_part, second_part) + sign_ref[pair : pair + 1, :] * swap(
-            jnp.where(lower, second_part, first_part)
-        )
-        coarse = folded.astype(jnp.bfloat16)
-        fine = (folded - coarse.astype(jnp.float32)).astype(jnp.bfloat16)
-        pieces_ref[:, 2 * pair * WIDTH : (2 * pair + 1) * WIDTH] = coarse
-        pieces_ref[:, (2 * pair + 1) * WIDTH : (2 * pair + 2) * WIDTH] = fine
-    total = jnp.dot(pieces_ref[...], gather_ref[...], preferred_element_type=jnp.float32)
+    total = jnp.dot(split(sums_ref[...]), gather_ref[...], preferred_element_type=jnp.float32)
     partial_ref[...] = total + jnp.where(on_diagonal, occupied * share, 0.0)
 
 
 def propagate_kernel(greens_ref, effective_ref, spread_ref, out_ref, factor_ref, held_ref, sems):
     _, history, points, _ = greens_ref.shape
-    rest = effective_ref[...] * time_step
-    pieces = []
-    for _ in range(3):
-        pieces.append(rest.astype(jnp.bfloat16).astype(jnp.float32))
-        rest = rest - pieces[-1]
-    stacked = jnp.concatenate(pieces, axis=0).astype(jnp.bfloat16)
-    spread = jnp.dot(stacked, spread_ref[...], preferred_element_type=jnp.float32)
-    factor_ref[...] = tree_sum([spread[n * points : (n + 1) * points] for n in range(3)])
+    factor_ref[...] = jnp.dot(
+        split(effective_ref[...] * time_step), spread_ref[...], preferred_element_type=jnp.float32
+    )
 
     slots, chunk = held_ref.shape[:2]
 
@@ -321,17 +303,16 @@
 
 def gather_tables():
     blocks = 2 * BANDS
-    pairs = STEPS * STEPS // 2
-    table = np.zeros((pairs, 2, blocks, BANDS, 2, BANDS, BANDS), np.float32)
-    signs = np.zeros((pairs, blocks, BANDS), np.float32)
-    for pair in range(pairs):
+    table = np.zeros((2, blocks, BANDS, 2, BANDS, BANDS), np.float32)
+    signs = np.zeros((BANDS, TILE, blocks, BANDS), np.float32)
+    for pair in range(BANDS):
         for p in range(blocks):
             i, j = divmod(2 * pair + p // BANDS, STEPS)
             h, a = divmod((p + STEPS * i) % blocks, BANDS)
             g, c = divmod((p + j) % blocks, BANDS)
-            table[pair, :, p, :, h ^ g, a, c] = 1 if (h, g) == (0, 1) else -1
-            signs[pair, p] = 1 if h == g else -1
-    return signs.reshape(pairs, WIDTH), table.reshape(-1, WIDTH).astype(ml_dtypes.bfloat16)
+            table[:, p, pair, h ^ g, a, c] = 1 if (h, g) == (0, 1) else -1
+            signs[pair, :, p] = 1 if h == g else -1
+    return signs.reshape(BANDS, TILE, WIDTH), table.reshape(2 * WIDTH, WIDTH).astype(ml_dtypes.bfloat16)
 
 
 def spread_table():
@@ -343,7 +324,7 @@
                 h, a = divmod((p - STEPS * i) % blocks, BANDS)
                 g, b = divmod((p + j) % blocks, BANDS)
                 table[1 if h == g else 0, a, b, i, j, p, :] = -1 if (h, g) == (1, 0) else 1
-    return table.reshape(WIDTH, -1).astype(ml_dtypes.bfloat16)
+    return np.tile(table.reshape(WIDTH, -1), (2, 1)).astype(ml_dtypes.bfloat16)
 
 
 def in_vmem():
@@ -365,13 +346,6 @@
 def cost(per_element, arrays):
     size = SIDE * SIDE * TILE * WIDTH
     return pl.CostEstimate(flops=per_element * size, bytes_accessed=4 * arrays * size, transcendentals=0)
-
-
-def held_blocks(count, parts):
-    return [
-        pltpu.VMEM((count, TILE * SIDE * SIDE // parts, WIDTH), jnp.float32),
-        pltpu.SemaphoreType.DMA((count,)),
-    ]
 
 
 def forward(place, greens, steps, parts):
@@ -382,10 +356,10 @@
             jax.ShapeDtypeStruct((points, TILE, WIDTH), jnp.float32),
             jax.ShapeDtypeStruct((STEPS, TILE * points, WIDTH), jnp.float32),
         ],
-        in_specs=[in_smem()] + [anywhere()] * len(steps),
+        in_specs=[in_smem()] + [in_vmem()] * len(steps),
         out_specs=[in_vmem()] * 2,
-        scratch_shapes=[pltpu.VMEM((points, TILE, WIDTH), jnp.float32)] + held_blocks(len(steps), parts),
-        compiler_params=params(8),
+        scratch_shapes=[pltpu.VMEM((points, TILE, WIDTH), jnp.float32)],
+        compiler_params=params(6),
         cost_estimate=cost(400, 6),
         name="forward",
     )(place, *greens)
@@ -396,9 +370,8 @@
     return pl.pallas_call(
         functools.partial(early_kernel, steps, parts),
         out_shape=jax.ShapeDtypeStruct((points, TILE, WIDTH), jnp.float32),
-        in_specs=[in_smem(), in_vmem(), in_vmem(), anywhere()] + [anywhere()] * len(steps),
+        in_specs=[in_smem(), in_vmem(), in_vmem(), anywhere()] + [in_vmem()] * len(steps),
         out_specs=in_vmem(),
-        scratch_shapes=held_blocks(len(steps), parts),
         compiler_params=params(4),
         cost_estimate=cost(150, 3),
         name="early",
@@ -415,16 +388,14 @@
             jax.ShapeDtypeStruct((points, WIDTH), jnp.float32),
             jax.ShapeDtypeStruct((points, TILE, WIDTH), jnp.float32),
         ],
-        in_specs=[in_smem()] + [in_vmem()] * 6 + [anywhere()] * len(steps) + [in_vmem()],
+        in_specs=[in_smem()] + [in_vmem()] * (7 + len(steps)),
         out_specs=[in_vmem()] * 2,
         input_output_aliases={len(inputs) - 1: 1},
         scratch_shapes=[
             pltpu.VMEM((TILE * points, WIDTH), jnp.float32),
-            pltpu.VMEM((points, STEPS * STEPS * WIDTH), jnp.float32),
-            pltpu.VMEM((points, STEPS * STEPS * WIDTH), jnp.bfloat16),
-        ]
-        + (held_blocks(len(steps), parts) if steps else []),
-        compiler_params=params(16),
+            pltpu.VMEM((points, WIDTH), jnp.float32),
+        ],
+        compiler_params=params(8),
         cost_estimate=cost(800, 6),
         name="backward",
     )(*inputs)
@@ -510,11 +481,11 @@
         moved = []
         for x in (green_row, screened):
             whole = x.reshape(parts * TILE * local, width)
-            found = {0: whole}
-            for step in order:
+            found = {}
+            for step in [0] + order:
                 start = partner_of(place, step, parts) * (TILE * local)
                 block = lax.dynamic_slice_in_dim(whole, start, TILE * local)
-                found[step] = exchange(block, "ka", step, parts)
+                found[step] = exchange(block, "ka", step, parts) if step else block
             moved.append([found])
         order = [0] + order
     else:

time: 87.9 us -> 93.6 us (1.065)
  Pallas kernels: 25.5 us -> 31.7 us
  waiting for transfers between devices: 29.3 us -> 26.7 us
  local copies, waits for them, and re-layouts: 6.81 us -> 8.32 us
    pallas_call x1, Pallas kernels: 8.46 us -> 14 us  [backward(): pl.pallas_call(functools.partial(backward_kernel, steps, parts, share), o...]
    ppermute x21, waiting for transfers between devices: 29.3 us -> 26.7 us  [exchange(): return lax.ppermute(value, axis, pairs)]
    unnamed x40 -> x46, local copies, waits for them, and re-layouts: 3.66 us -> 5.05 us
  transfers between devices with their start and end apart: 21 -> 21, of which waited for: 14 -> 14; matrix products, arithmetic and copies ran while one was open for 2% -> 1% of each run, Pallas kernels for 14% -> 13%
where the time goes in v5:
time: 93.6 us; the launch traced here: 93.5 us
  Pallas kernels  31.7 us (34%)
  waiting for transfers between devices  26.7 us (29%)
  starting transfers between devices  25.7 us (27%)
  local copies, waits for them, and re-layouts  8.32 us (9%)
    ppermute x21, waiting for transfers between devices, exchange(): return lax.ppermute(value, axis, pairs)  26.7 us
    ppermute x21, starting transfers between devices, exchange(): return lax.ppermute(value, axis, pairs)  25.7 us
    pallas_call x1, Pallas kernels, backward(): pl.pallas_call(functools.partial(backward_kernel, steps, parts, share), o...  14 us
    pallas_call x1, Pallas kernels, forward(): pl.pallas_call(functools.partial(forward_kernel, steps, parts), out_shape...  5.78 us
    pallas_call x1, Pallas kernels, propagate(): pl.pallas_call(propagate_kernel, out_shape=jax.ShapeDtypeStruct(greens.sh...  5.08 us
    unnamed x46, local copies, waits for them, and re-layouts  5.05 us
    pallas_call x1, Pallas kernels, early_lines(): pl.pallas_call(functools.partial(early_kernel, steps, parts), out_shape=j...  3.89 us
    dynamic_slice x2, local copies, waits for them, and re-layouts, per_device(): block = lax.dynamic_slice_in_dim(whole, start, TILE * local)  3.06 us
  transfers between devices with their start and end apart: 21, of which 14 were waited for; matrix products, arithmetic and copies ran while one was open for 1% of the time, Pallas kernels for 13%

profile of v5, /device:TPU:0, one launch (start us, length us, event | category | flops | bytes accessed | tf_op | source)
XLA Modules:
  0.0 93.5 jit_solution(1344175063287689646)
XLA Ops:
  0.0 1.9 %constant_dynamic-slice_fusion.16 = (f32[576,128]{1,0:T(8,128)S(1)}, f32[576,128]{1,0:T(8,128)S(1)}, f32[576,128]{1,0:T(8,128)S(1)}, f32[576,128]{1,0:T(8,128)S(...) fusion(f32[4608,128]{1,0:T(8,128)} %bitcast.5, ...), kind=kLoop, calls=%fused_computation.21 | loop fusion | bytes 4718624 | tf_op jit(solution)/shard_map/dynamic_slice | solution.py:487
  1.9 3.0 %collective-permute-start = (f32[576,128]{1,0:T(8,128)S(1)}, f32[576,128]{1,0:T(8,128)S(1)}, u32[]{:S(2)}, u32[]{:S(2)}) collective-permute-start(f32[576,128]{1,0:T(8,128)S(1)} %get-tuple-element.25), channel_id=1, source_target_pairs={{0,16},{4,20},{8,24},{12,28},{16,0},{20,4},{24,8},{28,12},{1,17},{... | collective-permute-start | bytes 884744 | tf_op jit(solution)/shard_map/ppermute | solution.py:447
  4.9 1.5 %collective-permute-start.1 = (f32[576,128]{1,0:T(8,128)S(1)}, f32[576,128]{1,0:T(8,128)S(1)}, u32[]{:S(2)}, u32[]{:S(2)}) collective-permute-start(f32[576,128]{1,0:T(8,128)S(1)} %get-tuple-element.24), channel_id=1, source_target_pairs={{0,8},{4,12},{8,0},{12,4},{16,24},{20,28},{24,16},{28,20},{1,9},{5... | collective-permute-start | bytes 884744 | tf_op jit(solution)/shard_map/ppermute | solution.py:447
  6.4 0.3 collective-permute-start.3
  6.8 2.9 %collective-permute-start.4 = (f32[576,128]{1,0:T(8,128)S(1)}, f32[576,128]{1,0:T(8,128)S(1)}, u32[]{:S(2)}, u32[]{:S(2)}) collective-permute-start(f32[576,128]{1,0:T(8,128)S(1)} %get-tuple-element.21), channel_id=1, source_target_pairs={{0,24},{4,28},{8,16},{12,20},{16,8},{20,12},{24,0},{28,4},{1,25},{... | collective-permute-start | bytes 884744 | tf_op jit(solution)/shard_map/ppermute | solution.py:447
  9.7 1.2 %constant_dynamic-slice_fusion.8 = (f32[576,128]{1,0:T(8,128)}, f32[576,128]{1,0:T(8,128)}, f32[576,128]{1,0:T(8,128)S(1)}, f32[576,128]{1,0:T(8,128)S(1)}, f32[...) fusion(f32[4608,128]{1,0:T(8,128)S(1)} %bitcast.6, s32[]{:T(128)S(6)} %select_n.71, ...), kind=kLoop, calls=%fused_computation.13 | loop fusion | bytes 4718624 | tf_op jit(solution)/shard_map/dynamic_slice | solution.py:487
  10.8 2.0 %collective-permute-done.refs_1_ = f32[576,128]{1,0:T(8,128)S(1)} collective-permute-done((f32[576,128]{1,0:T(8,128)S(1)}, f32[576,128]{1,0:T(8,128)S(1)}, u32[]{:S(2)}, u32[]{:S(2)}) %collective-permute-start) | collective-permute-done | bytes 294944 | tf_op jit(solution)/shard_map/ppermute | solution.py:447
  12.8 0.4 collective-permute-start.5
  13.2 1.7 %collective-permute-done.1.refs_2_ = f32[576,128]{1,0:T(8,128)S(1)} collective-permute-done((f32[576,128]{1,0:T(8,128)S(1)}, f32[576,128]{1,0:T(8,128)S(1)}, u32[]{:S(2)}, u32[]{:S(2)}) %collective-permute-start.1) | collective-permute-done | bytes 294944 | tf_op jit(solution)/shard_map/ppermute | solution.py:447
  14.9 1.0 %collective-permute-start.6 = (f32[576,128]{1,0:T(8,128)S(1)}, f32[576,128]{1,0:T(8,128)S(1)}, u32[]{:S(2)}, u32[]{:S(2)}) collective-permute-start(f32[576,128]{1,0:T(8,128)S(1)} %get-tuple-element.19), channel_id=1, source_target_pairs={{0,4},{4,0},{8,12},{12,8},{16,20},{20,16},{24,28},{28,24},{1,5},{5... | collective-permute-start | bytes 884744 | tf_op jit(solution)/shard_map/ppermute | solution.py:447
  15.9 1.8 %collective-permute-done.2.refs_3_ = f32[576,128]{1,0:T(8,128)S(1)} collective-permute-done((f32[576,128]{1,0:T(8,128)S(1)}, f32[576,128]{1,0:T(8,128)S(1)}, u32[]{:S(2)}, u32[]{:S(2)}) %collective-permute-start.2) | collective-permute-done | bytes 294944 | tf_op jit(solution)/shard_map/ppermute | solution.py:447
  17.7 0.7 copy-done.2
  18.4 1.2 %collective-permute-start.10 = (f32[576,128]{1,0:T(8,128)S(1)}, f32[576,128]{1,0:T(8,128)S(1)}, u32[]{:S(2)}, u32[]{:S(2)}) collective-permute-start(f32[576,128]{1,0:T(8,128)S(1)} %get-tuple-element.14), channel_id=1, source_target_pairs={{0,16},{4,20},{8,24},{12,28},{16,0},{20,4},{24,8},{28,12},{1,17},{... | collective-permute-start | bytes 884744 | tf_op jit(solution)/shard_map/ppermute | solution.py:447
  19.6 0.6 collective-permute-done.3.refs_4_
  20.2 0.7 copy-done.4
  20.9 0.9 collective-permute-start.11
  21.8 5.3 %collective-permute-done.4.refs_5_ = f32[576,128]{1,0:T(8,128)S(1)} collective-permute-done((f32[576,128]{1,0:T(8,128)S(1)}, f32[576,128]{1,0:T(8,128)S(1)}, u32[]{:S(2)}, u32[]{:S(2)}) %collective-permute-start.4) | collective-permute-done | bytes 294944 | tf_op jit(solution)/shard_map/ppermute | solution.py:447
  27.1 0.7 copy-done.6
  27.8 5.1 %collective-permute-done.5.refs_6_ = f32[576,128]{1,0:T(8,128)S(1)} collective-permute-done((f32[576,128]{1,0:T(8,128)S(1)}, f32[576,128]{1,0:T(8,128)S(1)}, u32[]{:S(2)}, u32[]{:S(2)}) %collective-permute-start.5) | collective-permute-done | bytes 294944 | tf_op jit(solution)/shard_map/ppermute | solution.py:447
  32.9 0.7 copy-done.8
  33.6 1.9 %collective-permute-start.13 = (f32[576,128]{1,0:T(8,128)}, f32[576,128]{1,0:T(8,128)}, u32[]{:S(2)}, u32[]{:S(2)}) collective-permute-start(f32[576,128]{1,0:T(8,128)} %get-tuple-element.11), channel_id=1, source_target_pairs={{0,12},{4,8},{8,4},{12,0},{16,28},{20,24},{24,20},{28,16},{1,13},{... | collective-permute-start | bytes 884744 | tf_op jit(solution)/shard_map/ppermute | solution.py:447
  35.5 0.7 copy-done.10
  36.2 1.5 %collective-permute-start.7 = (f32[576,128]{1,0:T(8,128)}, f32[576,128]{1,0:T(8,128)}, u32[]{:S(2)}, u32[]{:S(2)}) collective-permute-start(f32[576,128]{1,0:T(8,128)} %get-tuple-element.18), channel_id=1, source_target_pairs={{0,24},{4,28},{8,16},{12,20},{16,8},{20,12},{24,0},{28,4},{1,25},{... | collective-permute-start | bytes 884744 | tf_op jit(solution)/shard_map/ppermute | solution.py:447
  37.7 0.8 collective-permute-done.10.refs_1_
  38.5 0.7 copy-done.12
  39.2 2.4 %collective-permute-start.8 = (f32[576,128]{1,0:T(8,128)}, f32[576,128]{1,0:T(8,128)}, u32[]{:S(2)}, u32[]{:S(2)}) collective-permute-start(f32[576,128]{1,0:T(8,128)} %get-tuple-element.17), channel_id=1, source_target_pairs={{0,28},{4,24},{8,20},{12,16},{16,12},{20,8},{24,4},{28,0},{1,29},{... | collective-permute-start | bytes 884744 | tf_op jit(solution)/shard_map/ppermute | solution.py:447
  41.7 0.7 copy-done.14
  42.4 0.2 collective-permute-start.9
  42.6 0.1 select_reduce_fusion
  43.4 0.1 dynamic_slice.83
  43.5 2.9 %roll_own.1._.greens_ref = f32[4,64,72,128]{3,2,1,0:T(8,128)S(1)} custom-call(f32[64,72,128]{2,1,0:T(8,128)S(1)} %copy-done), custom_call_target="tpu_custom_call" | custom-call | flops 1769472 | bytes 11796480 | tf_op jit(solution)/shard_map/roll_own/pallas_call | solution.py:406
  46.5 5.8 %forward.1 = (f32[576,8,128]{2,1,0:T(8,128)S(1)}, f32[4,4608,128]{2,1,0:T(8,128)S(1)}) custom-call(s32[1]{0:T(128)} %bitcast.place_ref, f32[576,128]{1,0:T(8,128)S(1)} %get-tuple-element.26.refs_0_, f32[576,128]{1,0:T(8,128)S(1)} %collective-permute-done.refs_1_, f32[576,128]{1,0:T(8,128)S(1)} %collective-permute-done.1.refs_2_, f32[576,128]{1,0:T(8,128)S(1)} %copy-done.3, ...), custom_call_target="tpu_custom_call" | custom-call | flops 235929600 | bytes 14155776 | tf_op jit(solution)/shard_map/forward/pallas_call | solution.py:353
  52.4 3.9 %early.1.refs_3_ = f32[576,8,128]{2,1,0:T(8,128)S(1)} custom-call(s32[1]{0:T(128)} %bitcast.place_ref, f32[576,8,128]{2,1,0:T(8,128)S(1)} %get-tuple-element.8.lattice_ref, f32[8,128]{1,0:T(8,128)S(1)} %squeeze.8.weight_ref, f32[4,64,72,128]{3,2,1,0:T(8,128)S(1)} %roll_own.1._.greens_ref, f32[576,128]{1,0:T(8,128)S(1)} %get-tuple-element.15.refs_0_, ...), custom_call_target="tpu_custom_call" | custom-call | flops 88473600 | bytes 7077888 | tf_op jit(solution)/shard_map/early/pallas_call | solution.py:370
  56.3 0.7 collective-permute-done.8.refs_1_
  57.0 14.0 %backward.1 = (f32[576,128]{1,0:T(8,128)S(1)}, f32[576,8,128]{2,1,0:T(8,128)S(1)}) custom-call(s32[1]{0:T(128)} %bitcast.place_ref, f32[576,8,128]{2,1,0:T(8,128)S(1)} %get-tuple-element.8.lattice_ref, f32[8,128]{1,0:T(8,128)S(1)} %squeeze.8.weight_ref, f32[72,128]{1,0:T(8,128)S(1)} %copy-done.17, ...), custom_call_target="tpu_custom_call", output_to_operand_aliasing={{1}: (10, {})} | custom-call | flops 471859200 | bytes 14155776 | tf_op jit(solution)/shard_map/backward/pallas_call | solution.py:385
  71.1 0.5 collective-permute-start.14
  71.6 1.0 %collective-permute-done.14 = f32[288,128]{1,0:T(8,128)S(1)} collective-permute-done((f32[288,128]{1,0:T(8,128)S(1)}, f32[288,128]{1,0:T(8,128)S(1)}, u32[]{:S(2)}, u32[]{:S(2)}) %collective-permute-start.14) | collective-permute-done | bytes 147488 | tf_op jit(solution)/shard_map/ppermute | solution.py:447
  72.7 2.7 %collective-permute-start.15 = (f32[72,128]{1,0:T(8,128)S(1)}, f32[72,128]{1,0:T(8,128)S(1)}, u32[]{:S(2)}, u32[]{:S(2)}) collective-permute-start(f32[72,128]{1,0:T(8,128)S(1)} %get-tuple-element.37), channel_id=1, source_target_pairs={{0,24},{4,28},{8,16},{12,20},{16,8},{20,12},{24,0},{28,4},{1,25},{... | collective-permute-start | bytes 110600 | tf_op jit(solution)/shard_map/ppermute | solution.py:447
  75.4 0.5 collective-permute-start.16
  75.9 0.4 collective-permute-start.17
  76.2 1.4 %collective-permute-done.15 = f32[72,128]{1,0:T(8,128)S(1)} collective-permute-done((f32[72,128]{1,0:T(8,128)S(1)}, f32[72,128]{1,0:T(8,128)S(1)}, u32[]{:S(2)}, u32[]{:S(2)}) %collective-permute-start.15) | collective-permute-done | bytes 36896 | tf_op jit(solution)/shard_map/ppermute | solution.py:447
  77.6 1.7 %collective-permute-done.16 = f32[72,128]{1,0:T(8,128)S(1)} collective-permute-done((f32[72,128]{1,0:T(8,128)S(1)}, f32[72,128]{1,0:T(8,128)S(1)}, u32[]{:S(2)}, u32[]{:S(2)}) %collective-permute-start.16) | collective-permute-done | bytes 36896 | tf_op jit(solution)/shard_map/ppermute | solution.py:447
  79.3 0.5 collective-permute-done.17
  79.8 3.7 %collective-permute-start.18 = (f32[72,128]{1,0:T(8,128)S(1)}, f32[72,128]{1,0:T(8,128)S(1)}, u32[]{:S(2)}, u32[]{:S(2)}) collective-permute-start(f32[72,128]{1,0:T(8,128)S(1)} %fusion), channel_id=1, source_target_pairs={{0,3},{1,2},{2,1},{3,0},{4,7},{5,6},{6,5},{7,4},{8,11},{9,10},{10,... | collective-permute-start | bytes 110600 | tf_op jit(solution)/shard_map/ppermute | solution.py:447
  83.5 0.8 collective-permute-start.20
  84.3 1.4 %collective-permute-done.18 = f32[72,128]{1,0:T(8,128)S(1)} collective-permute-done((f32[72,128]{1,0:T(8,128)S(1)}, f32[72,128]{1,0:T(8,128)S(1)}, u32[]{:S(2)}, u32[]{:S(2)}) %collective-permute-start.18) | collective-permute-done | bytes 36896 | tf_op jit(solution)/shard_map/ppermute | solution.py:447
  85.7 2.7 %collective-permute-done.19 = f32[72,128]{1,0:T(8,128)S(1)} collective-permute-done((f32[72,128]{1,0:T(8,128)S(1)}, f32[72,128]{1,0:T(8,128)S(1)}, u32[]{:S(2)}, u32[]{:S(2)}) %collective-permute-start.19) | collective-permute-done | bytes 36896 | tf_op jit(solution)/shard_map/ppermute | solution.py:447
  88.4 5.1 %propagate.1 = f32[64,72,128]{2,1,0:T(8,128)} custom-call(f32[4,64,72,128]{3,2,1,0:T(8,128)S(1)} %roll_own.1._.greens_ref, f32[72,128]{1,0:T(8,128)S(1)} %add_add_fusion.effective_ref, bf16[256,2048]{1,0:T(8,128)(2,1)S(1)} %copy-done.1), custom_call_target="tpu_custom_call" | custom-call | flops 18874368 | bytes 11796480 | tf_op jit(solution)/shard_map/propagate/pallas_call | solution.py:421
  (57 shorter events, 0.3 us)
Async XLA Ops:
  0.0 9.6 %copy-start.19 = (f32[64,72,128]{2,1,0:T(8,128)S(1)}, f32[64,72,128]{2,1,0:T(8,128)}, u32[]{:S(2)}) copy-start(f32[64,72,128]{2,1,0:T(8,128)} %param.11) | copy-start | bytes 7077892
  1.9 10.9 %collective-permute-start = (f32[576,128]{1,0:T(8,128)S(1)}, f32[576,128]{1,0:T(8,128)S(1)}, u32[]{:S(2)}, u32[]{:S(2)}) collective-permute-start(f32[576,128]{1,0:T(8,128)S(1)} %get-tuple-element.25), channel_id=1, source_target_pairs={{0,16},{4,20},{8,24},{12,28},{16,0},{20,4},{24,8},{28,12},{1,17},{... | collective-permute-start | bytes 884744 | tf_op jit(solution)/shard_map/ppermute | solution.py:447
  4.9 9.9 %collective-permute-start.1 = (f32[576,128]{1,0:T(8,128)S(1)}, f32[576,128]{1,0:T(8,128)S(1)}, u32[]{:S(2)}, u32[]{:S(2)}) collective-permute-start(f32[576,128]{1,0:T(8,128)S(1)} %get-tuple-element.24), channel_id=1, source_target_pairs={{0,8},{4,12},{8,0},{12,4},{16,24},{20,28},{24,16},{28,20},{1,9},{5... | collective-permute-start | bytes 884744 | tf_op jit(solution)/shard_map/ppermute | solution.py:447
  6.4 11.2 %collective-permute-start.2 = (f32[576,128]{1,0:T(8,128)S(1)}, f32[576,128]{1,0:T(8,128)S(1)}, u32[]{:S(2)}, u32[]{:S(2)}) collective-permute-start(f32[576,128]{1,0:T(8,128)S(1)} %get-tuple-element.23), channel_id=1, source_target_pairs={{0,20},{4,16},{8,28},{12,24},{16,4},{20,0},{24,12},{28,8},{1,21},{... | collective-permute-start | bytes 884744 | tf_op jit(solution)/shard_map/ppermute | solution.py:447
  6.4 13.8 %collective-permute-start.3 = (f32[576,128]{1,0:T(8,128)S(1)}, f32[576,128]{1,0:T(8,128)S(1)}, u32[]{:S(2)}, u32[]{:S(2)}) collective-permute-start(f32[576,128]{1,0:T(8,128)S(1)} %get-tuple-element.22), channel_id=1, source_target_pairs={{0,12},{4,8},{8,4},{12,0},{16,28},{20,24},{24,20},{28,16},{1,13},{... | collective-permute-start | bytes 884744 | tf_op jit(solution)/shard_map/ppermute | solution.py:447
  6.8 20.3 %collective-permute-start.4 = (f32[576,128]{1,0:T(8,128)S(1)}, f32[576,128]{1,0:T(8,128)S(1)}, u32[]{:S(2)}, u32[]{:S(2)}) collective-permute-start(f32[576,128]{1,0:T(8,128)S(1)} %get-tuple-element.21), channel_id=1, source_target_pairs={{0,24},{4,28},{8,16},{12,20},{16,8},{20,12},{24,0},{28,4},{1,25},{... | collective-permute-start | bytes 884744 | tf_op jit(solution)/shard_map/ppermute | solution.py:447
  9.6 33.0 %copy-start.21 = (s32[64]{0:T(128)S(1)}, s32[64]{0:T(128)}, u32[]{:S(2)}) copy-start(s32[64]{0:T(128)} %param.14) | copy-start | bytes 772
  9.6 33.0 %copy-start.22 = (f32[4]{0:T(128)S(1)}, f32[4]{0:T(128)}, u32[]{:S(2)}) copy-start(f32[4]{0:T(128)} %constant.46.clone) | copy-start | bytes 52
  9.7 33.8 %copy-start = (f32[64,72,128]{2,1,0:T(8,128)S(1)}, f32[64,72,128]{2,1,0:T(8,128)}, u32[]{:S(2)}) copy-start(f32[64,72,128]{2,1,0:T(8,128)} %green_ref.1) | copy-start | bytes 7077892
  12.8 20.1 %collective-permute-start.5 = (f32[576,128]{1,0:T(8,128)S(1)}, f32[576,128]{1,0:T(8,128)S(1)}, u32[]{:S(2)}, u32[]{:S(2)}) collective-permute-start(f32[576,128]{1,0:T(8,128)S(1)} %get-tuple-element.20), channel_id=1, source_target_pairs={{0,28},{4,24},{8,20},{12,16},{16,12},{20,8},{24,4},{28,0},{1,29},{... | collective-permute-start | bytes 884744 | tf_op jit(solution)/shard_map/ppermute | solution.py:447
  14.9 20.6 %collective-permute-start.6 = (f32[576,128]{1,0:T(8,128)S(1)}, f32[576,128]{1,0:T(8,128)S(1)}, u32[]{:S(2)}, u32[]{:S(2)}) collective-permute-start(f32[576,128]{1,0:T(8,128)S(1)} %get-tuple-element.19), channel_id=1, source_target_pairs={{0,4},{4,0},{8,12},{12,8},{16,20},{20,16},{24,28},{28,24},{1,5},{5... | collective-permute-start | bytes 884744 | tf_op jit(solution)/shard_map/ppermute | solution.py:447
  17.7 0.7 copy-start.2
  18.4 20.1 %collective-permute-start.10 = (f32[576,128]{1,0:T(8,128)S(1)}, f32[576,128]{1,0:T(8,128)S(1)}, u32[]{:S(2)}, u32[]{:S(2)}) collective-permute-start(f32[576,128]{1,0:T(8,128)S(1)} %get-tuple-element.14), channel_id=1, source_target_pairs={{0,16},{4,20},{8,24},{12,28},{16,0},{20,4},{24,8},{28,12},{1,17},{... | collective-permute-start | bytes 884744 | tf_op jit(solution)/shard_map/ppermute | solution.py:447
  20.2 0.7 copy-start.4
  20.9 20.7 %collective-permute-start.11 = (f32[576,128]{1,0:T(8,128)S(1)}, f32[576,128]{1,0:T(8,128)S(1)}, u32[]{:S(2)}, u32[]{:S(2)}) collective-permute-start(f32[576,128]{1,0:T(8,128)S(1)} %get-tuple-element.13), channel_id=1, source_target_pairs={{0,8},{4,12},{8,0},{12,4},{16,24},{20,28},{24,16},{28,20},{1,9},{5... | collective-permute-start | bytes 884744 | tf_op jit(solution)/shard_map/ppermute | solution.py:447
  27.1 0.7 copy-start.6
  27.8 24.5 %collective-permute-start.12 = (f32[576,128]{1,0:T(8,128)}, f32[576,128]{1,0:T(8,128)}, u32[]{:S(2)}, u32[]{:S(2)}) collective-permute-start(f32[576,128]{1,0:T(8,128)} %get-tuple-element.12), channel_id=1, source_target_pairs={{0,20},{4,16},{8,28},{12,24},{16,4},{20,0},{24,12},{28,8},{1,21},{... | collective-permute-start | bytes 884744 | tf_op jit(solution)/shard_map/ppermute | solution.py:447
  32.9 0.7 copy-start.8
  33.6 18.7 %collective-permute-start.13 = (f32[576,128]{1,0:T(8,128)}, f32[576,128]{1,0:T(8,128)}, u32[]{:S(2)}, u32[]{:S(2)}) collective-permute-start(f32[576,128]{1,0:T(8,128)} %get-tuple-element.11), channel_id=1, source_target_pairs={{0,12},{4,8},{8,4},{12,0},{16,28},{20,24},{24,20},{28,16},{1,13},{... | collective-permute-start | bytes 884744 | tf_op jit(solution)/shard_map/ppermute | solution.py:447
  35.4 0.7 copy-start.10
  36.2 20.1 %collective-permute-start.7 = (f32[576,128]{1,0:T(8,128)}, f32[576,128]{1,0:T(8,128)}, u32[]{:S(2)}, u32[]{:S(2)}) collective-permute-start(f32[576,128]{1,0:T(8,128)} %get-tuple-element.18), channel_id=1, source_target_pairs={{0,24},{4,28},{8,16},{12,20},{16,8},{20,12},{24,0},{28,4},{1,25},{... | collective-permute-start | bytes 884744 | tf_op jit(solution)/shard_map/ppermute | solution.py:447
  38.5 0.7 copy-start.12
  39.2 17.8 %collective-permute-start.8 = (f32[576,128]{1,0:T(8,128)}, f32[576,128]{1,0:T(8,128)}, u32[]{:S(2)}, u32[]{:S(2)}) collective-permute-start(f32[576,128]{1,0:T(8,128)} %get-tuple-element.17), channel_id=1, source_target_pairs={{0,28},{4,24},{8,20},{12,16},{16,12},{20,8},{24,4},{28,0},{1,29},{... | collective-permute-start | bytes 884744 | tf_op jit(solution)/shard_map/ppermute | solution.py:447
  41.7 0.7 copy-start.14
  42.4 14.6 %collective-permute-start.9 = (f32[576,128]{1,0:T(8,128)}, f32[576,128]{1,0:T(8,128)}, u32[]{:S(2)}, u32[]{:S(2)}) collective-permute-start(f32[576,128]{1,0:T(8,128)} %get-tuple-element.16), channel_id=1, source_target_pairs={{0,4},{4,0},{8,12},{12,8},{16,20},{20,16},{24,28},{28,24},{1,5},{5... | collective-permute-start | bytes 884744 | tf_op jit(solution)/shard_map/ppermute | solution.py:447
  43.5 3.0 %copy-start.3 = (f32[576,128]{1,0:T(8,128)S(1)}, f32[576,128]{1,0:T(8,128)}, u32[]{:S(2)}) copy-start(f32[576,128]{1,0:T(8,128)} %copy-done.2) | copy-start | bytes 884740
  43.5 3.0 %copy-start.5 = (f32[576,128]{1,0:T(8,128)S(1)}, f32[576,128]{1,0:T(8,128)}, u32[]{:S(2)}) copy-start(f32[576,128]{1,0:T(8,128)} %copy-done.4) | copy-start | bytes 884740
  43.5 3.0 %copy-start.7 = (f32[576,128]{1,0:T(8,128)S(1)}, f32[576,128]{1,0:T(8,128)}, u32[]{:S(2)}) copy-start(f32[576,128]{1,0:T(8,128)} %copy-done.6) | copy-start | bytes 884740
  43.5 3.0 %copy-start.9 = (f32[576,128]{1,0:T(8,128)S(1)}, f32[576,128]{1,0:T(8,128)}, u32[]{:S(2)}) copy-start(f32[576,128]{1,0:T(8,128)} %copy-done.8) | copy-start | bytes 884740
  43.5 3.0 %copy-start.11 = (f32[576,128]{1,0:T(8,128)S(1)}, f32[576,128]{1,0:T(8,128)}, u32[]{:S(2)}) copy-start(f32[576,128]{1,0:T(8,128)} %copy-done.10) | copy-start | bytes 884740
  46.4 6.0 %copy-start.13 = (f32[576,128]{1,0:T(8,128)S(1)}, f32[576,128]{1,0:T(8,128)}, u32[]{:S(2)}) copy-start(f32[576,128]{1,0:T(8,128)} %copy-done.12) | copy-start | bytes 884740
  46.4 5.9 %copy-start.15 = (f32[576,128]{1,0:T(8,128)S(1)}, f32[576,128]{1,0:T(8,128)}, u32[]{:S(2)}) copy-start(f32[576,128]{1,0:T(8,128)} %copy-done.14) | copy-start | bytes 884740
  52.4 4.6 %copy-start.16 = (bf16[256,128]{1,0:T(8,128)(2,1)S(1)}, bf16[256,128]{1,0:T(8,128)(2,1)}, u32[]{:S(2)}) copy-start(bf16[256,128]{1,0:T(8,128)(2,1)} %constant.48.clone.gather_ref) | copy-start | bytes 196612
  52.4 4.6 %copy-start.17 = (f32[72,128]{1,0:T(8,128)S(1)}, f32[72,128]{1,0:T(8,128)}, u32[]{:S(2)}) copy-start(f32[72,128]{1,0:T(8,128)} %equal_ref.1) | copy-start | bytes 110596
  52.4 4.6 %copy-start.18 = (f32[8,8,128]{2,1,0:T(8,128)S(1)}, f32[8,8,128]{2,1,0:T(8,128)}, u32[]{:S(2)}) copy-start(f32[8,8,128]{2,1,0:T(8,128)} %constant.47.clone.sign_ref) | copy-start | bytes 98308
  57.0 31.4 %copy-start.20 = (f32[72,128]{1,0:T(8,128)S(1)}, f32[72,128]{1,0:T(8,128)}, u32[]{:S(2)}) copy-start(f32[72,128]{1,0:T(8,128)} %param.12) | copy-start | bytes 110596
  71.1 17.3 %copy-start.1 = (bf16[256,2048]{1,0:T(8,128)(2,1)S(1)}, bf16[256,2048]{1,0:T(8,128)(2,1)}, u32[]{:S(2)}) copy-start(bf16[256,2048]{1,0:T(8,128)(2,1)} %constant.49.clone.spread_ref) | copy-start | bytes 3145732
  71.1 1.5 %collective-permute-start.14 = (f32[288,128]{1,0:T(8,128)S(1)}, f32[288,128]{1,0:T(8,128)S(1)}, u32[]{:S(2)}, u32[]{:S(2)}) collective-permute-start(f32[288,128]{1,0:T(8,128)S(1)} %pad_maximum_fusion), channel_id=1, source_target_pairs={{0,4},{4,0},{8,12},{12,8},{16,20},{20,16},{24,28},{28,24},{1,5},{5... | collective-permute-start | bytes 442376 | tf_op jit(solution)/shard_map/ppermute | solution.py:447
  72.7 4.9 %collective-permute-start.15 = (f32[72,128]{1,0:T(8,128)S(1)}, f32[72,128]{1,0:T(8,128)S(1)}, u32[]{:S(2)}, u32[]{:S(2)}) collective-permute-start(f32[72,128]{1,0:T(8,128)S(1)} %get-tuple-element.37), channel_id=1, source_target_pairs={{0,24},{4,28},{8,16},{12,20},{16,8},{20,12},{24,0},{28,4},{1,25},{... | collective-permute-start | bytes 110600 | tf_op jit(solution)/shard_map/ppermute | solution.py:447
  75.4 4.0 %collective-permute-start.16 = (f32[72,128]{1,0:T(8,128)S(1)}, f32[72,128]{1,0:T(8,128)S(1)}, u32[]{:S(2)}, u32[]{:S(2)}) collective-permute-start(f32[72,128]{1,0:T(8,128)S(1)} %get-tuple-element.36), channel_id=1, source_target_pairs={{0,16},{4,20},{8,24},{12,28},{16,0},{20,4},{24,8},{28,12},{1,17},{... | collective-permute-start | bytes 110600 | tf_op jit(solution)/shard_map/ppermute | solution.py:447
  75.9 4.0 %collective-permute-start.17 = (f32[72,128]{1,0:T(8,128)S(1)}, f32[72,128]{1,0:T(8,128)S(1)}, u32[]{:S(2)}, u32[]{:S(2)}) collective-permute-start(f32[72,128]{1,0:T(8,128)S(1)} %get-tuple-element.35), channel_id=1, source_target_pairs={{0,8},{4,12},{8,0},{12,4},{16,24},{20,28},{24,16},{28,20},{1,9},{5... | collective-permute-start | bytes 110600 | tf_op jit(solution)/shard_map/ppermute | solution.py:447
  79.8 5.8 %collective-permute-start.18 = (f32[72,128]{1,0:T(8,128)S(1)}, f32[72,128]{1,0:T(8,128)S(1)}, u32[]{:S(2)}, u32[]{:S(2)}) collective-permute-start(f32[72,128]{1,0:T(8,128)S(1)} %fusion), channel_id=1, source_target_pairs={{0,3},{1,2},{2,1},{3,0},{4,7},{5,6},{6,5},{7,4},{8,11},{9,10},{10,... | collective-permute-start | bytes 110600 | tf_op jit(solution)/shard_map/ppermute | solution.py:447
  83.5 4.9 %collective-permute-start.19 = (f32[72,128]{1,0:T(8,128)S(1)}, f32[72,128]{1,0:T(8,128)S(1)}, u32[]{:S(2)}, u32[]{:S(2)}) collective-permute-start(f32[72,128]{1,0:T(8,128)S(1)} %fusion), channel_id=1, source_target_pairs={{0,2},{1,3},{2,0},{3,1},{4,6},{5,7},{6,4},{7,5},{8,10},{9,11},{10,... | collective-permute-start | bytes 110600 | tf_op jit(solution)/shard_map/ppermute | solution.py:447
  83.5 4.9 %collective-permute-start.20 = (f32[72,128]{1,0:T(8,128)S(1)}, f32[72,128]{1,0:T(8,128)S(1)}, u32[]{:S(2)}, u32[]{:S(2)}) collective-permute-start(f32[72,128]{1,0:T(8,128)S(1)} %fusion), channel_id=1, source_target_pairs={{0,1},{1,0},{2,3},{3,2},{4,5},{5,4},{6,7},{7,6},{8,9},{9,8},{10,11... | collective-permute-start | bytes 110600 | tf_op jit(solution)/shard_map/ppermute | solution.py:447

commit v6 on v5

--- a/solution.py
+++ b/solution.py
@@ -15,14 +15,15 @@
 ENTRIES = BANDS * BANDS
 WIDTH = 2 * ENTRIES
 TILE = 8
-STEPS = 4
+BABY, GIANT = 8, 2
 
 time_step = 0.1
 hubbard = 1.0
 quadrature = (0.375, 1.1666666, 0.9583333, 1.0)
 
-LATE = 3
-AHEAD = 3
+ROLLED = 192
+HANDED = 2
+LATE = 2
 
 
 def lane_sign(shape):
@@ -42,20 +43,6 @@
     while len(terms) > 1:
         terms = [sum(terms[i : i + 2][1:], terms[i]) for i in range(0, len(terms), 2)]
     return terms[0]
-
-
-def merge_lanes(values):
-    lane = lax.broadcasted_iota(jnp.int32, values[0].shape, 1)
-    while len(values) > 1:
-        half = len(values) // 2
-        lower = lane & half == 0
-        merged = []
-        for x, y in zip(values[:half], values[half:]):
-            rest = jnp.where(lower, y, x)
-            other = jnp.where(lower, pltpu.roll(rest, WIDTH - half, 1), pltpu.roll(rest, half, 1))
-            merged.append(jnp.where(lower, x, y) + other)
-        values = merged
-    return values[0]
 
 
 def split(x):
@@ -98,31 +85,38 @@
     return out
 
 
+def fenced(place):
+    return pl.when(place >= 0)
+
+
 def load_line(ref, line):
     stride = ref.shape[0] // TILE
     return [ref[pl.ds(line * SIDE + k2, TILE, stride=stride), :] for k2 in range(SIDE)]
 
 
 def along_first(work_ref, sign, low, store):
-    def load(column):
-        return [work_ref[k1 * SIDE + column] for k1 in range(SIDE)]
-
-    rows = load(0)
-    for column in range(SIDE):
-        following = load(column + 1) if column + 1 < SIDE else None
-        for r1, value in enumerate(dft24(rows, sign, low)):
-            store(r1 * SIDE + column, value)
-        rows = following
-
-
-def roll_kernel(green_ref, greens_ref):
-    batch = math.gcd(green_ref.shape[0], STEPS)
+    def columns(pair, carry):
+        both = (2 * pair, 2 * pair + 1)
+        rows = [[work_ref[k1 * SIDE + column] for k1 in range(SIDE)] for column in both]
+        values = [dft24(row, sign, low) for row in rows]
+        for column, value in zip(both, values):
+            for r1 in range(SIDE):
+                store(r1 * SIDE + column, value[r1])
+        return carry
+
+    lax.fori_loop(0, SIDE // 2, columns, 0)
+
+
+def roll_kernel(place_ref, green_ref, whole_ref, greens_ref, block_ref, *, step, parts):
+    rows = block_ref.shape[0]
+    block_ref[...] = whole_ref[pl.ds(pl.multiple_of(partner_of(place_ref[0], step, parts) * rows, TILE), rows), :]
+    batch = math.gcd(green_ref.shape[0], 4)
 
     def rolls(n, carry):
         times = pl.ds(n * batch, batch)
         green = green_ref[times]
-        rolled = [roll_blocks(green, j) for j in range(STEPS)]
-        for j in range(STEPS):
+        rolled = [roll_blocks(green, j) for j in range(BABY)]
+        for j in range(BABY):
             greens_ref[j, times] = rolled[j]
         return carry
 
@@ -143,16 +137,26 @@
                 work_ref[(owner * lines + i) * SIDE + r2] = value
             return carry
 
-        lax.fori_loop(0, lines, along_second, 0, unroll=lines <= 4)
-        green = green_ref[...]
-        spot = pl.ds(pl.multiple_of(owner * rows, TILE), rows)
-        for j in range(STEPS):
-            greens_ref[j, spot, :] = roll_blocks(green, j)
+        @fenced(place)
+        def _():
+            lax.fori_loop(0, lines, along_second, 0, unroll=lines <= 4)
 
     def store(point, value):
         lattice_ref[point] = value
 
     along_first(work_ref, -1, low, store)
+
+    for step, green_ref in zip(steps, block_refs):
+
+        def rolls(n, carry):
+            green = green_ref[pl.ds(n * ROLLED, ROLLED), :]
+            start = partner_of(place, step, parts) * rows + n * ROLLED
+            spot = pl.ds(pl.multiple_of(start, TILE), ROLLED)
+            for j in range(BABY):
+                greens_ref[j, spot, :] = roll_blocks(green, j)
+            return carry
+
+        lax.fori_loop(0, rows // ROLLED, rolls, 0)
 
 
 def product_lines(steps, parts, place, lattice_ref, weights, screen_refs, work_ref):
@@ -177,16 +181,16 @@
         for k2, value in enumerate(dft24(rows, 1, low)):
             work_ref[line * SIDE + k2] = value
 
-    if lines > 4:
-        for screen_ref, step in zip(screen_refs, steps):
-            lax.fori_loop(0, lines, lambda i, carry: store(*load(screen_ref, step, i)), None)
-        return
     for screen_ref, step in zip(screen_refs, steps):
-        for i in range(lines):
-            store(*load(screen_ref, step, i))
-
-
-def early_kernel(steps, parts, place_ref, lattice_ref, weight_ref, _, *refs):
+
+        @fenced(place)
+        def _():
+            lax.fori_loop(
+                0, lines, lambda i, carry: store(*load(screen_ref, step, i)), None, unroll=lines <= 4
+            )
+
+
+def early_kernel(steps, parts, place_ref, lattice_ref, weight_ref, *refs):
     *screen_refs, work_ref = refs
     product_lines(steps, parts, place_ref[0], lattice_ref, weight_ref[...], screen_refs, work_ref)
 
@@ -195,7 +199,7 @@
     steps, parts, share, place_ref, lattice_ref, weight_ref, equal_ref, sign_ref, gather_ref, greens_ref, *refs
 ):
     screen_refs, refs = refs[: len(steps)], refs[len(steps) :]
-    _, partial_ref, work_ref, sigma_ref, sums_ref = refs
+    _, partial_ref, work_ref, sigma_ref, sums_ref, pieces_ref = refs
     points = SIDE * SIDE
     low = lane_sign((TILE, WIDTH))
     if steps:
@@ -208,36 +212,23 @@
 
     block = points // parts
     tiles = block // TILE
-    batch = max(n for n in range(1, 10) if tiles % n == 0)
+    batch = max(n for n in (1, 2, 3) if tiles % n == 0)
 
     def contract(group, carry):
         first = group * batch
         green_row = (first // tiles) * TILE * block + (first % tiles) * TILE
-        units = [(tile, s) for tile in range(batch) for s in range(TILE)]
-
-        def prepare(tile, s):
-            sigma = sigma_ref[pl.ds((first + tile) * TILE * TILE + s, TILE, stride=TILE), :]
-            row = pl.multiple_of(green_row + s * block + tile * TILE, TILE)
-            return (
-                [roll_blocks(sigma, STEPS * i) for i in range(STEPS)],
-                [greens_ref[j, pl.ds(row, TILE), :] for j in range(STEPS)],
-            )
-
-        ready = [prepare(*unit) for unit in units[:AHEAD]]
-        for n, (tile, s) in enumerate(units):
-            if n + AHEAD < len(units):
-                ready.append(prepare(*units[n + AHEAD]))
-            sigmas, greens = ready.pop(0)
-            terms = [sigma * green for sigma in sigmas for green in greens]
-            sums = terms if s == 0 else [a + b for a, b in zip(sums, terms)]
-            if s == TILE - 1:
-                folded = [
-                    jnp.where(low, sums[2 * q], sums[2 * q + 1])
-                    + sign_ref[q] * swap(jnp.where(low, sums[2 * q + 1], sums[2 * q]))
-                    for q in range(BANDS)
-                ]
-                row = pl.ds(pl.multiple_of((first + tile) * TILE, TILE), TILE)
-                sums_ref[row, :] = merge_lanes(folded)
+        values = []
+        for tile in range(batch):
+            sums = None
+            for s in range(TILE):
+                sigma = sigma_ref[pl.ds((first + tile) * TILE * TILE + s, TILE, stride=TILE), :]
+                row = pl.ds(pl.multiple_of(green_row + s * block + tile * TILE, TILE), TILE)
+                greens = [greens_ref[j, row, :] for j in range(BABY)]
+                terms = [part * green for part in (sigma, swap(sigma)) for green in greens]
+                sums = terms if s == 0 else [a + b for a, b in zip(sums, terms)]
+            row = pl.ds(pl.multiple_of((first + tile) * TILE, TILE), TILE)
+            for spot, value in enumerate(sums):
+                sums_ref[row, spot * WIDTH : (spot + 1) * WIDTH] = value
         return carry
 
     lax.fori_loop(0, points // (TILE * batch), contract, 0)
@@ -247,7 +238,18 @@
     occupied = jnp.sum(jnp.where((inner >= 0) & (inner % (BANDS + 1) == 0), equal_ref[...], 0.0))
     spots = lax.broadcasted_iota(jnp.int32, (points, WIDTH), 1)
     on_diagonal = (spots < ENTRIES) & (spots % (BANDS + 1) == 0)
-    total = jnp.dot(split(sums_ref[...]), gather_ref[...], preferred_element_type=jnp.float32)
+    lower = spots < ENTRIES
+    for pair in range(BABY * GIANT // 2):
+        first_part = sums_ref[:, 2 * pair * WIDTH : (2 * pair + 1) * WIDTH]
+        second_part = sums_ref[:, (2 * pair + 1) * WIDTH : (2 * pair + 2) * WIDTH]
+        folded = jnp.where(lower, first_part, second_part) + sign_ref[pair : pair + 1, :] * swap(
+            jnp.where(lower, second_part, first_part)
+        )
+        coarse = folded.astype(jnp.bfloat16)
+        fine = (folded - coarse.astype(jnp.float32)).astype(jnp.bfloat16)
+        pieces_ref[:, 2 * pair * WIDTH : (2 * pair + 1) * WIDTH] = coarse
+        pieces_ref[:, (2 * pair + 1) * WIDTH : (2 * pair + 2) * WIDTH] = fine
+    total = jnp.dot(pieces_ref[...], gather_ref[...], preferred_element_type=jnp.float32)
     partial_ref[...] = total + jnp.where(on_diagonal, occupied * share, 0.0)
 
 
@@ -272,26 +274,19 @@
             def _():
                 copy(number - slots, slot).wait()
 
-            batch = math.gcd(chunk, 4)
-            pending = None
             for start in range(0, points, TILE):
                 stop = min(start + TILE, points)
-                for first in range(0, chunk, batch):
-                    times = pl.ds(number * chunk + first, batch)
-                    greens = [greens_ref[j, times, start:stop, :] for j in range(STEPS)]
-                    terms = [greens[0]]
-                    for i in range(STEPS):
-                        total = None
-                        for j in range(STEPS):
-                            spot = STEPS * i + j
-                            factor = factor_ref[start:stop, spot * WIDTH : (spot + 1) * WIDTH]
-                            term = factor[None] * greens[j]
-                            total = term if total is None else total + term
-                        terms.append(roll_blocks(total, STEPS * i))
-                    if pending is not None:
-                        held_ref[pending[0]] = tree_sum(pending[1])
-                    pending = ((slot, slice(first, first + batch), slice(start, stop)), terms)
-            held_ref[pending[0]] = tree_sum(pending[1])
+                greens = [greens_ref[j, pl.ds(number * chunk, chunk), start:stop, :] for j in range(BABY)]
+                terms = [greens[0]]
+                for i in range(GIANT):
+                    total = None
+                    for j in range(BABY):
+                        spot = BABY * i + j
+                        factor = factor_ref[start:stop, spot * WIDTH : (spot + 1) * WIDTH]
+                        term = factor[None] * greens[j]
+                        total = term if total is None else total + term
+                    terms.append(roll_blocks(total, BABY * i))
+                held_ref[slot, :, start:stop, :] = tree_sum(terms)
             copy(number, slot).start()
         return carry
 
@@ -303,25 +298,26 @@
 
 def gather_tables():
     blocks = 2 * BANDS
-    table = np.zeros((2, blocks, BANDS, 2, BANDS, BANDS), np.float32)
-    signs = np.zeros((BANDS, TILE, blocks, BANDS), np.float32)
-    for pair in range(BANDS):
+    pairs = BABY * GIANT // 2
+    table = np.zeros((pairs, 2, blocks, BANDS, 2, BANDS, BANDS), np.float32)
+    signs = np.zeros((pairs, blocks, BANDS), np.float32)
+    for pair in range(pairs):
         for p in range(blocks):
-            i, j = divmod(2 * pair + p // BANDS, STEPS)
-            h, a = divmod((p + STEPS * i) % blocks, BANDS)
+            i, j = divmod(2 * pair + p // BANDS, BABY)
+            h, a = divmod((p + BABY * i) % blocks, BANDS)
             g, c = divmod((p + j) % blocks, BANDS)
-            table[:, p, pair, h ^ g, a, c] = 1 if (h, g) == (0, 1) else -1
-            signs[pair, :, p] = 1 if h == g else -1
-    return signs.reshape(BANDS, TILE, WIDTH), table.reshape(2 * WIDTH, WIDTH).astype(ml_dtypes.bfloat16)
+            table[pair, :, p, :, h ^ g, a, c] = 1 if (h, g) == (0, 1) else -1
+            signs[pair, p] = 1 if h == g else -1
+    return signs.reshape(pairs, WIDTH), table.reshape(-1, WIDTH).astype(ml_dtypes.bfloat16)
 
 
 def spread_table():
     blocks = 2 * BANDS
-    table = np.zeros((2, BANDS, BANDS, STEPS, STEPS, blocks, BANDS), np.float32)
-    for i in range(STEPS):
-        for j in range(STEPS):
+    table = np.zeros((2, BANDS, BANDS, GIANT, BABY, blocks, BANDS), np.float32)
+    for i in range(GIANT):
+        for j in range(BABY):
             for p in range(blocks):
-                h, a = divmod((p - STEPS * i) % blocks, BANDS)
+                h, a = divmod((p - BABY * i) % blocks, BANDS)
                 g, b = divmod((p + j) % blocks, BANDS)
                 table[1 if h == g else 0, a, b, i, j, p, :] = -1 if (h, g) == (1, 0) else 1
     return np.tile(table.reshape(WIDTH, -1), (2, 1)).astype(ml_dtypes.bfloat16)
@@ -354,7 +350,7 @@
         functools.partial(forward_kernel, steps, parts),
         out_shape=[
             jax.ShapeDtypeStruct((points, TILE, WIDTH), jnp.float32),
-            jax.ShapeDtypeStruct((STEPS, TILE * points, WIDTH), jnp.float32),
+            jax.ShapeDtypeStruct((BABY, TILE * points, WIDTH), jnp.float32),
         ],
         in_specs=[in_smem()] + [in_vmem()] * len(steps),
         out_specs=[in_vmem()] * 2,
@@ -365,17 +361,17 @@
     )(place, *greens)
 
 
-def early_lines(place, lattice, weights, before, screens, steps, parts):
+def early_lines(place, lattice, weights, screens, steps, parts):
     points = SIDE * SIDE
     return pl.pallas_call(
         functools.partial(early_kernel, steps, parts),
         out_shape=jax.ShapeDtypeStruct((points, TILE, WIDTH), jnp.float32),
-        in_specs=[in_smem(), in_vmem(), in_vmem(), anywhere()] + [in_vmem()] * len(steps),
+        in_specs=[in_smem(), in_vmem(), in_vmem()] + [in_vmem()] * len(steps),
         out_specs=in_vmem(),
         compiler_params=params(4),
         cost_estimate=cost(150, 3),
         name="early",
-    )(place, lattice, weights, before, *screens)
+    )(place, lattice, weights, *screens)
 
 
 def backward(place, lattice, weights, equal_time, greens, screens, work, steps, parts, share):
@@ -393,25 +389,30 @@
         input_output_aliases={len(inputs) - 1: 1},
         scratch_shapes=[
             pltpu.VMEM((TILE * points, WIDTH), jnp.float32),
-            pltpu.VMEM((points, WIDTH), jnp.float32),
+            pltpu.VMEM((points, BABY * GIANT * WIDTH), jnp.float32),
+            pltpu.VMEM((points, BABY * GIANT * WIDTH), jnp.bfloat16),
         ],
-        compiler_params=params(8),
+        compiler_params=params(16),
         cost_estimate=cost(800, 6),
         name="backward",
     )(*inputs)
     return partial_value
 
 
-def roll_own(greens):
+def roll_own(place, greens, whole, step, parts):
+    rows = whole.shape[0] // parts
     return pl.pallas_call(
-        roll_kernel,
-        out_shape=jax.ShapeDtypeStruct((STEPS, *greens.shape), jnp.float32),
-        in_specs=[in_vmem()],
-        out_specs=in_vmem(),
+        functools.partial(roll_kernel, step=step, parts=parts),
+        out_shape=[
+            jax.ShapeDtypeStruct((BABY, *greens.shape), jnp.float32),
+            jax.ShapeDtypeStruct((rows, whole.shape[1]), whole.dtype),
+        ],
+        in_specs=[in_smem(), in_vmem(), in_vmem()],
+        out_specs=[in_vmem()] * 2,
         compiler_params=params(4),
-        cost_estimate=cost(3, 5),
+        cost_estimate=cost(8, 9),
         name="roll_own",
-    )(greens)
+    )(place, greens, whole)
 
 
 def propagate(greens, effective):
@@ -454,7 +455,7 @@
     single = [along[n] for n in along if n and n & (n - 1) == 0]
     mixed = [along[n] for n in along if n & (n - 1)]
     order = [step for steps in zip(*single[::-1]) for step in steps]
-    return order + [step for steps in mixed for step in steps] + along[0]
+    return order + along[0] + [step for steps in mixed for step in steps]
 
 
 def class_weights(quad_class):
@@ -478,13 +479,17 @@
     if times == TILE and local % SIDE == 0:
         groups, sources = 1, parts
         order = exchange_order(parts)
+        wholes = [x.reshape(parts * TILE * local, width) for x in (green_row, screened)]
+        waiting = order[HANDED]
+        own_greens, handed = roll_own(seat, green_row, wholes[1], waiting, parts)
         moved = []
-        for x in (green_row, screened):
-            whole = x.reshape(parts * TILE * local, width)
+        for whole in wholes:
             found = {}
             for step in [0] + order:
                 start = partner_of(place, step, parts) * (TILE * local)
                 block = lax.dynamic_slice_in_dim(whole, start, TILE * local)
+                if whole is wholes[1] and step == waiting:
+                    block = handed
                 found[step] = exchange(block, "ka", step, parts) if step else block
             moved.append([found])
         order = [0] + order
@@ -499,18 +504,16 @@
             x = jnp.pad(x, ((0, padding), (0, 0), (0, 0))).reshape(groups, TILE * points, width)
             moved.append([{0: x[group]} for group in range(groups)])
         weights = jnp.pad(weights, (0, padding))
+        own_greens, _ = roll_own(seat, green_row, screened.reshape(-1, width), 0, 1)
     weights = jnp.broadcast_to(weights.reshape(groups, TILE, 1), (groups, TILE, width))
 
     early = order[: max(1, len(order) - LATE)]
     late = order[len(early) :]
-    own_greens = roll_own(green_row)
     partial_value = None
     for group in range(groups):
         green, screen = moved[0][group], moved[1][group]
         lattice, greens = forward(seat, [green[step] for step in order], order, sources)
-        work = early_lines(
-            seat, lattice, weights[group], own_greens, [screen[step] for step in early], early, sources
-        )
+        work = early_lines(seat, lattice, weights[group], [screen[step] for step in early], early, sources)
         share = hubbard / (points * blocks) if group == 0 else 0.0
         term = backward(
             seat, lattice, weights[group], equal_time, greens, [screen[step] for step in late], work,

time: 93.6 us -> 95.2 us (1.017)
  Pallas kernels: 31.7 us -> 33.8 us
  local copies, waits for them, and re-layouts: 8.32 us -> 9.67 us
  waiting for transfers between devices: 26.7 us -> 25.7 us
    pallas_call x1, Pallas kernels: 14 us -> 8.86 us  [backward(): pl.pallas_call(functools.partial(backward_kernel, steps, parts, share), o...]
    pallas_call x1, Pallas kernels: 5.78 us -> 9.3 us  [forward(): pl.pallas_call(functools.partial(forward_kernel, steps, parts), out_shape...]
    pallas_call x1, Pallas kernels: 2.92 us -> 5.77 us  [roll_own(): pl.pallas_call(functools.partial(roll_kernel, step=step, parts=parts), ou...]
    unnamed x46 -> x30, local copies, waits for them, and re-layouts: 5.05 us -> 6.53 us
    ppermute x21, waiting for transfers between devices: 26.7 us -> 25.7 us  [exchange(): return lax.ppermute(value, axis, pairs)]
  transfers between devices with their start and end apart: 21 -> 21, of which waited for: 14 -> 12; matrix products, arithmetic and copies ran while one was open for 1% -> 1% of each run, Pallas kernels for 13% -> 21%
where the time goes in v6:
time: 95.2 us; the launch traced here: 95.1 us
  Pallas kernels  33.8 us (36%)
  waiting for transfers between devices  25.7 us (27%)
  starting transfers between devices  24.9 us (26%)
  local copies, waits for them, and re-layouts  9.67 us (10%)
    ppermute x21, waiting for transfers between devices, exchange(): return lax.ppermute(value, axis, pairs)  25.7 us
    ppermute x21, starting transfers between devices, exchange(): return lax.ppermute(value, axis, pairs)  24.9 us
    pallas_call x1, Pallas kernels, forward(): pl.pallas_call(functools.partial(forward_kernel, steps, parts), out_shape...  9.3 us
    pallas_call x1, Pallas kernels, backward(): pl.pallas_call(functools.partial(backward_kernel, steps, parts, share), o...  8.86 us
    unnamed x30, local copies, waits for them, and re-layouts  6.53 us
    pallas_call x1, Pallas kernels, roll_own(): pl.pallas_call(functools.partial(roll_kernel, step=step, parts=parts), ou...  5.77 us
    pallas_call x1, Pallas kernels, propagate(): pl.pallas_call(propagate_kernel, out_shape=jax.ShapeDtypeStruct(greens.sh...  5.21 us
    pallas_call x1, Pallas kernels, early_lines(): pl.pallas_call(functools.partial(early_kernel, steps, parts), out_shape=j...  4.63 us
  transfers between devices with their start and end apart: 21, of which 12 were waited for; matrix products, arithmetic and copies ran while one was open for 1% of the time, Pallas kernels for 21%

profile of v6, /device:TPU:0, one launch (start us, length us, event | category | flops | bytes accessed | tf_op | source)
XLA Modules:
  0.0 95.1 jit_solution(15012194579643763565)
XLA Ops:
  0.0 1.9 %constant_dynamic-slice_fusion.15 = (f32[576,128]{1,0:T(8,128)S(1)}, f32[576,128]{1,0:T(8,128)S(1)}, f32[576,128]{1,0:T(8,128)S(1)}, f32[576,128]{1,0:T(8,128)S(...) fusion(f32[4608,128]{1,0:T(8,128)} %bitcast.7, ...), kind=kLoop, calls=%fused_computation.20 | loop fusion | bytes 4718624 | tf_op jit(solution)/shard_map/dynamic_slice | solution.py:490
  1.9 0.0 copy-start.1
  1.9 3.0 %collective-permute-start = (f32[576,128]{1,0:T(8,128)S(1)}, f32[576,128]{1,0:T(8,128)S(1)}, u32[]{:S(2)}, u32[]{:S(2)}) collective-permute-start(f32[576,128]{1,0:T(8,128)S(1)} %get-tuple-element.28), channel_id=1, source_target_pairs={{0,16},{4,20},{8,24},{12,28},{16,0},{20,4},{24,8},{28,12},{1,17},{... | collective-permute-start | bytes 884744 | tf_op jit(solution)/shard_map/ppermute | solution.py:448
  4.9 1.5 %collective-permute-start.1 = (f32[576,128]{1,0:T(8,128)S(1)}, f32[576,128]{1,0:T(8,128)S(1)}, u32[]{:S(2)}, u32[]{:S(2)}) collective-permute-start(f32[576,128]{1,0:T(8,128)S(1)} %get-tuple-element.27), channel_id=1, source_target_pairs={{0,8},{4,12},{8,0},{12,4},{16,24},{20,28},{24,16},{28,20},{1,9},{5... | collective-permute-start | bytes 884744 | tf_op jit(solution)/shard_map/ppermute | solution.py:448
  6.4 0.3 collective-permute-start.3
  6.8 0.3 collective-permute-start.4
  7.1 1.0 %constant_dynamic-slice_fusion.8 = (f32[576,128]{1,0:T(8,128)}, f32[576,128]{1,0:T(8,128)}, f32[576,128]{1,0:T(8,128)S(1)}, f32[576,128]{1,0:T(8,128)S(1)}, f32[...) fusion(f32[4608,128]{1,0:T(8,128)S(1)} %bitcast.8, s32[]{:T(128)S(6)} %select_n.71, s32[]{:T(128)S(6)} %select_n.70, ...), kind=kLoop, calls=%fused_computation.13 | loop fusion | bytes 4128796 | tf_op jit(solution)/shard_map/dynamic_slice | solution.py:490
  8.1 4.6 %collective-permute-done.refs_1_ = f32[576,128]{1,0:T(8,128)S(1)} collective-permute-done((f32[576,128]{1,0:T(8,128)S(1)}, f32[576,128]{1,0:T(8,128)S(1)}, u32[]{:S(2)}, u32[]{:S(2)}) %collective-permute-start) | collective-permute-done | bytes 294944 | tf_op jit(solution)/shard_map/ppermute | solution.py:448
  12.8 3.0 %collective-permute-start.5 = (f32[576,128]{1,0:T(8,128)S(1)}, f32[576,128]{1,0:T(8,128)S(1)}, u32[]{:S(2)}, u32[]{:S(2)}) collective-permute-start(f32[576,128]{1,0:T(8,128)S(1)} %get-tuple-element.23), channel_id=1, source_target_pairs={{0,24},{4,28},{8,16},{12,20},{16,8},{20,12},{24,0},{28,4},{1,25},{... | collective-permute-start | bytes 884744 | tf_op jit(solution)/shard_map/ppermute | solution.py:448
  15.8 0.0 collective-permute-done.1.refs_2_
  15.8 0.0 collective-permute-start.6
  15.8 1.9 %collective-permute-done.2.refs_3_ = f32[576,128]{1,0:T(8,128)S(1)} collective-permute-done((f32[576,128]{1,0:T(8,128)S(1)}, f32[576,128]{1,0:T(8,128)S(1)}, u32[]{:S(2)}, u32[]{:S(2)}) %collective-permute-start.2) | collective-permute-done | bytes 294944 | tf_op jit(solution)/shard_map/ppermute | solution.py:448
  17.7 1.2 %collective-permute-start.9 = (f32[576,128]{1,0:T(8,128)S(1)}, f32[576,128]{1,0:T(8,128)S(1)}, u32[]{:S(2)}, u32[]{:S(2)}) collective-permute-start(f32[576,128]{1,0:T(8,128)S(1)} %get-tuple-element.18), channel_id=1, source_target_pairs={{0,16},{4,20},{8,24},{12,28},{16,0},{20,4},{24,8},{28,12},{1,17},{... | collective-permute-start | bytes 884744 | tf_op jit(solution)/shard_map/ppermute | solution.py:448
  18.9 1.3 %collective-permute-done.3.refs_4_ = f32[576,128]{1,0:T(8,128)S(1)} collective-permute-done((f32[576,128]{1,0:T(8,128)S(1)}, f32[576,128]{1,0:T(8,128)S(1)}, u32[]{:S(2)}, u32[]{:S(2)}) %collective-permute-start.3) | collective-permute-done | bytes 294944 | tf_op jit(solution)/shard_map/ppermute | solution.py:448
  20.2 0.5 collective-permute-start.10
  20.7 5.8 %roll_own.1 = (f32[8,64,72,128]{3,2,1,0:T(8,128)S(1)}, f32[576,128]{1,0:T(8,128)}) custom-call(s32[1]{0:T(128)} %bitcast.place_ref, f32[64,72,128]{2,1,0:T(8,128)S(1)} %copy-done.1, f32[4608,128]{1,0:T(8,128)S(1)} %bitcast.9), custom_call_target="tpu_custom_call" | custom-call | flops 4718592 | bytes 21233664 | tf_op jit(solution)/shard_map/roll_own/pallas_call | solution.py:404
  26.5 6.5 %copy-done = f32[8,64,72,128]{3,2,1,0:T(8,128)} copy-done((f32[8,64,72,128]{3,2,1,0:T(8,128)}, f32[8,64,72,128]{3,2,1,0:T(8,128)S(1)}, u32[]{:S(2)}) %copy-start) | copy-done | bytes 18874392
  33.0 1.4 %collective-permute-start.7 = (f32[576,128]{1,0:T(8,128)}, f32[576,128]{1,0:T(8,128)}, u32[]{:S(2)}, u32[]{:S(2)}) collective-permute-start(f32[576,128]{1,0:T(8,128)} %get-tuple-element.21), channel_id=1, source_target_pairs={{0,24},{4,28},{8,16},{12,20},{16,8},{20,12},{24,0},{28,4},{1,25},{... | collective-permute-start | bytes 884744 | tf_op jit(solution)/shard_map/ppermute | solution.py:448
  34.4 0.0 collective-permute-done.5.refs_6_
  34.4 2.6 %collective-permute-start.8 = (f32[576,128]{1,0:T(8,128)}, f32[576,128]{1,0:T(8,128)}, u32[]{:S(2)}, u32[]{:S(2)}) collective-permute-start(f32[576,128]{1,0:T(8,128)} %get-tuple-element.20), channel_id=1, source_target_pairs={{0,28},{4,24},{8,20},{12,16},{16,12},{20,8},{24,4},{28,0},{1,29},{... | collective-permute-start | bytes 884744 | tf_op jit(solution)/shard_map/ppermute | solution.py:448
  37.0 1.5 %collective-permute-done.9.refs_1_ = f32[576,128]{1,0:T(8,128)S(1)} collective-permute-done((f32[576,128]{1,0:T(8,128)S(1)}, f32[576,128]{1,0:T(8,128)S(1)}, u32[]{:S(2)}, u32[]{:S(2)}) %collective-permute-start.9) | collective-permute-done | bytes 294944 | tf_op jit(solution)/shard_map/ppermute | solution.py:448
  38.5 2.4 %collective-permute-start.12 = (f32[576,128]{1,0:T(8,128)}, f32[576,128]{1,0:T(8,128)}, u32[]{:S(2)}, u32[]{:S(2)}) collective-permute-start(f32[576,128]{1,0:T(8,128)} %get-tuple-element.16), channel_id=1, source_target_pairs={{0,12},{4,8},{8,4},{12,0},{16,28},{20,24},{24,20},{28,16},{1,13},{... | collective-permute-start | bytes 884744 | tf_op jit(solution)/shard_map/ppermute | solution.py:448
  40.9 0.4 collective-permute-start.13
  41.3 0.1 select_reduce_fusion
  42.0 0.1 dynamic_slice.80
  42.1 0.0 copy-start.6
  42.1 9.3 %forward.1 = (f32[576,8,128]{2,1,0:T(8,128)S(1)}, f32[8,4608,128]{2,1,0:T(8,128)S(1)}) custom-call(s32[1]{0:T(128)} %bitcast.place_ref, f32[576,128]{1,0:T(8,128)S(1)} %get-tuple-element.29.refs_0_, f32[576,128]{1,0:T(8,128)S(1)} %collective-permute-done.refs_1_, f32[576,128]{1,0:T(8,128)S(1)} %collective-permute-done.1.refs_2_, ...), custom_call_target="tpu_custom_call" | custom-call | flops 235929600 | bytes 14155776 | tf_op jit(solution)/shard_map/forward/pallas_call | solution.py:349
  51.4 6.1 %collective-permute-done.11.refs_3_ = f32[576,128]{1,0:T(8,128)S(1)} collective-permute-done((f32[576,128]{1,0:T(8,128)}, f32[576,128]{1,0:T(8,128)S(1)}, u32[]{:S(2)}, u32[]{:S(2)}) %collective-permute-start.11) | collective-permute-done | bytes 294944 | tf_op jit(solution)/shard_map/ppermute | solution.py:448
  57.5 0.1 squeeze.8.weight_ref
  57.6 4.6 %early.1.refs_2_ = f32[576,8,128]{2,1,0:T(8,128)S(1)} custom-call(s32[1]{0:T(128)} %bitcast.place_ref, f32[576,8,128]{2,1,0:T(8,128)S(1)} %get-tuple-element.11.lattice_ref, f32[8,128]{1,0:T(8,128)S(1)} %squeeze.8.weight_ref, f32[576,128]{1,0:T(8,128)S(1)} %get-tuple-element.19.refs_0_, f32[576,128]{1,0:T(8,128)S(1)} %collective-permute-done.9.refs_1_, ...), custom_call_target="tpu_custom_call" | custom-call | flops 88473600 | bytes 7077888 | tf_op jit(solution)/shard_map/early/pallas_call | solution.py:366
  62.2 0.0 copy-start.7
  62.3 8.9 %backward.1 = (f32[576,128]{1,0:T(8,128)S(1)}, f32[576,8,128]{2,1,0:T(8,128)S(1)}) custom-call(s32[1]{0:T(128)} %bitcast.place_ref, f32[576,8,128]{2,1,0:T(8,128)S(1)} %get-tuple-element.11.lattice_ref, f32[8,128]{1,0:T(8,128)S(1)} %squeeze.8.weight_ref, f32[72,128]{1,0:T(8,128)S(1)} %copy-done.5, ...), custom_call_target="tpu_custom_call", output_to_operand_aliasing={{1}: (9, {})} | custom-call | flops 471859200 | bytes 14155776 | tf_op jit(solution)/shard_map/backward/pallas_call | solution.py:381
  71.1 0.0 copy-start.3
  71.2 0.2 collective-permute-start.14
  71.5 1.2 %collective-permute-done.14 = f32[288,128]{1,0:T(8,128)S(1)} collective-permute-done((f32[288,128]{1,0:T(8,128)S(1)}, f32[288,128]{1,0:T(8,128)S(1)}, u32[]{:S(2)}, u32[]{:S(2)}) %collective-permute-start.14) | collective-permute-done | bytes 147488 | tf_op jit(solution)/shard_map/ppermute | solution.py:448
  72.7 2.5 %collective-permute-start.15 = (f32[72,128]{1,0:T(8,128)S(1)}, f32[72,128]{1,0:T(8,128)S(1)}, u32[]{:S(2)}, u32[]{:S(2)}) collective-permute-start(f32[72,128]{1,0:T(8,128)S(1)} %get-tuple-element.40), channel_id=1, source_target_pairs={{0,24},{4,28},{8,16},{12,20},{16,8},{20,12},{24,0},{28,4},{1,25},{... | collective-permute-start | bytes 110600 | tf_op jit(solution)/shard_map/ppermute | solution.py:448
  75.2 0.6 collective-permute-start.16
  75.8 0.4 collective-permute-start.17
  76.3 1.4 %collective-permute-done.15 = f32[72,128]{1,0:T(8,128)S(1)} collective-permute-done((f32[72,128]{1,0:T(8,128)S(1)}, f32[72,128]{1,0:T(8,128)S(1)}, u32[]{:S(2)}, u32[]{:S(2)}) %collective-permute-start.15) | collective-permute-done | bytes 36896 | tf_op jit(solution)/shard_map/ppermute | solution.py:448
  77.6 1.5 %collective-permute-done.16 = f32[72,128]{1,0:T(8,128)S(1)} collective-permute-done((f32[72,128]{1,0:T(8,128)S(1)}, f32[72,128]{1,0:T(8,128)S(1)}, u32[]{:S(2)}, u32[]{:S(2)}) %collective-permute-start.16) | collective-permute-done | bytes 36896 | tf_op jit(solution)/shard_map/ppermute | solution.py:448
  79.2 0.6 collective-permute-done.17
  79.8 2.7 %collective-permute-start.19 = (f32[72,128]{1,0:T(8,128)S(1)}, f32[72,128]{1,0:T(8,128)S(1)}, u32[]{:S(2)}, u32[]{:S(2)}) collective-permute-start(f32[72,128]{1,0:T(8,128)S(1)} %fusion), channel_id=1, source_target_pairs={{0,2},{1,3},{2,0},{3,1},{4,6},{5,7},{6,4},{7,5},{8,10},{9,11},{10,... | collective-permute-start | bytes 110600 | tf_op jit(solution)/shard_map/ppermute | solution.py:448
  82.5 1.6 %collective-permute-start.20 = (f32[72,128]{1,0:T(8,128)S(1)}, f32[72,128]{1,0:T(8,128)S(1)}, u32[]{:S(2)}, u32[]{:S(2)}) collective-permute-start(f32[72,128]{1,0:T(8,128)S(1)} %fusion), channel_id=1, source_target_pairs={{0,1},{1,0},{2,3},{3,2},{4,5},{5,4},{6,7},{7,6},{8,9},{9,8},{10,11... | collective-permute-start | bytes 110600 | tf_op jit(solution)/shard_map/ppermute | solution.py:448
  84.0 0.2 collective-permute-start.18
  84.3 0.8 collective-permute-done.19
  85.1 1.8 %collective-permute-done.20 = f32[72,128]{1,0:T(8,128)S(1)} collective-permute-done((f32[72,128]{1,0:T(8,128)S(1)}, f32[72,128]{1,0:T(8,128)S(1)}, u32[]{:S(2)}, u32[]{:S(2)}) %collective-permute-start.20) | collective-permute-done | bytes 36896 | tf_op jit(solution)/shard_map/ppermute | solution.py:448
  86.8 3.0 %collective-permute-done.18 = f32[72,128]{1,0:T(8,128)S(1)} collective-permute-done((f32[72,128]{1,0:T(8,128)S(1)}, f32[72,128]{1,0:T(8,128)S(1)}, u32[]{:S(2)}, u32[]{:S(2)}) %collective-permute-start.18) | collective-permute-done | bytes 36896 | tf_op jit(solution)/shard_map/ppermute | solution.py:448
  89.9 5.2 %propagate.1 = f32[64,72,128]{2,1,0:T(8,128)} custom-call(f32[8,64,72,128]{3,2,1,0:T(8,128)S(1)} %bitcast.6, f32[72,128]{1,0:T(8,128)S(1)} %add_add_fusion.effective_ref, bf16[256,2048]{1,0:T(8,128)(2,1)S(1)} %copy-done.3), custom_call_target="tpu_custom_call" | custom-call | flops 18874368 | bytes 11796480 | tf_op jit(solution)/shard_map/propagate/pallas_call | solution.py:422
  (42 shorter events, 0.2 us)
Async XLA Ops:
  0.0 7.1 %copy-start.2 = (f32[64,72,128]{2,1,0:T(8,128)S(1)}, f32[64,72,128]{2,1,0:T(8,128)}, u32[]{:S(2)}) copy-start(f32[64,72,128]{2,1,0:T(8,128)} %param.11) | copy-start | bytes 7077892
  1.9 18.8 %copy-start.1 = (f32[64,72,128]{2,1,0:T(8,128)S(1)}, f32[64,72,128]{2,1,0:T(8,128)}, u32[]{:S(2)}) copy-start(f32[64,72,128]{2,1,0:T(8,128)} %green_ref.1) | copy-start | bytes 7077892
  1.9 10.9 %collective-permute-start = (f32[576,128]{1,0:T(8,128)S(1)}, f32[576,128]{1,0:T(8,128)S(1)}, u32[]{:S(2)}, u32[]{:S(2)}) collective-permute-start(f32[576,128]{1,0:T(8,128)S(1)} %get-tuple-element.28), channel_id=1, source_target_pairs={{0,16},{4,20},{8,24},{12,28},{16,0},{20,4},{24,8},{28,12},{1,17},{... | collective-permute-start | bytes 884744 | tf_op jit(solution)/shard_map/ppermute | solution.py:448
  4.9 10.8 %collective-permute-start.1 = (f32[576,128]{1,0:T(8,128)S(1)}, f32[576,128]{1,0:T(8,128)S(1)}, u32[]{:S(2)}, u32[]{:S(2)}) collective-permute-start(f32[576,128]{1,0:T(8,128)S(1)} %get-tuple-element.27), channel_id=1, source_target_pairs={{0,8},{4,12},{8,0},{12,4},{16,24},{20,28},{24,16},{28,20},{1,9},{5... | collective-permute-start | bytes 884744 | tf_op jit(solution)/shard_map/ppermute | solution.py:448
  6.4 11.2 %collective-permute-start.2 = (f32[576,128]{1,0:T(8,128)S(1)}, f32[576,128]{1,0:T(8,128)S(1)}, u32[]{:S(2)}, u32[]{:S(2)}) collective-permute-start(f32[576,128]{1,0:T(8,128)S(1)} %get-tuple-element.26), channel_id=1, source_target_pairs={{0,20},{4,16},{8,28},{12,24},{16,4},{20,0},{24,12},{28,8},{1,21},{... | collective-permute-start | bytes 884744 | tf_op jit(solution)/shard_map/ppermute | solution.py:448
  6.4 13.8 %collective-permute-start.3 = (f32[576,128]{1,0:T(8,128)S(1)}, f32[576,128]{1,0:T(8,128)S(1)}, u32[]{:S(2)}, u32[]{:S(2)}) collective-permute-start(f32[576,128]{1,0:T(8,128)S(1)} %get-tuple-element.25), channel_id=1, source_target_pairs={{0,12},{4,8},{8,4},{12,0},{16,28},{20,24},{24,20},{28,16},{1,13},{... | collective-permute-start | bytes 884744 | tf_op jit(solution)/shard_map/ppermute | solution.py:448
  6.8 26.2 %collective-permute-start.4 = (f32[576,128]{1,0:T(8,128)S(1)}, f32[576,128]{1,0:T(8,128)S(1)}, u32[]{:S(2)}, u32[]{:S(2)}) collective-permute-start(f32[576,128]{1,0:T(8,128)S(1)} %get-tuple-element.24), channel_id=1, source_target_pairs={{0,4},{4,0},{8,12},{12,8},{16,20},{20,16},{24,28},{28,24},{1,5},{5... | collective-permute-start | bytes 884744 | tf_op jit(solution)/shard_map/ppermute | solution.py:448
  12.8 21.6 %collective-permute-start.5 = (f32[576,128]{1,0:T(8,128)S(1)}, f32[576,128]{1,0:T(8,128)S(1)}, u32[]{:S(2)}, u32[]{:S(2)}) collective-permute-start(f32[576,128]{1,0:T(8,128)S(1)} %get-tuple-element.23), channel_id=1, source_target_pairs={{0,24},{4,28},{8,16},{12,20},{16,8},{20,12},{24,0},{28,4},{1,25},{... | collective-permute-start | bytes 884744 | tf_op jit(solution)/shard_map/ppermute | solution.py:448
  15.8 21.3 %collective-permute-start.6 = (f32[576,128]{1,0:T(8,128)S(1)}, f32[576,128]{1,0:T(8,128)S(1)}, u32[]{:S(2)}, u32[]{:S(2)}) collective-permute-start(f32[576,128]{1,0:T(8,128)S(1)} %get-tuple-element.22), channel_id=1, source_target_pairs={{0,28},{4,24},{8,20},{12,16},{16,12},{20,8},{24,4},{28,0},{1,29},{... | collective-permute-start | bytes 884744 | tf_op jit(solution)/shard_map/ppermute | solution.py:448
  17.7 20.8 %collective-permute-start.9 = (f32[576,128]{1,0:T(8,128)S(1)}, f32[576,128]{1,0:T(8,128)S(1)}, u32[]{:S(2)}, u32[]{:S(2)}) collective-permute-start(f32[576,128]{1,0:T(8,128)S(1)} %get-tuple-element.18), channel_id=1, source_target_pairs={{0,16},{4,20},{8,24},{12,28},{16,0},{20,4},{24,8},{28,12},{1,17},{... | collective-permute-start | bytes 884744 | tf_op jit(solution)/shard_map/ppermute | solution.py:448
  20.2 20.7 %collective-permute-start.10 = (f32[576,128]{1,0:T(8,128)S(1)}, f32[576,128]{1,0:T(8,128)S(1)}, u32[]{:S(2)}, u32[]{:S(2)}) collective-permute-start(f32[576,128]{1,0:T(8,128)S(1)} %get-tuple-element.17), channel_id=1, source_target_pairs={{0,8},{4,12},{8,0},{12,4},{16,24},{20,28},{24,16},{28,20},{1,9},{5... | collective-permute-start | bytes 884744 | tf_op jit(solution)/shard_map/ppermute | solution.py:448
  20.7 20.5 %copy-start.8 = (s32[64]{0:T(128)S(1)}, s32[64]{0:T(128)}, u32[]{:S(2)}) copy-start(s32[64]{0:T(128)} %param.14) | copy-start | bytes 772
  20.7 20.5 %copy-start.9 = (f32[4]{0:T(128)S(1)}, f32[4]{0:T(128)}, u32[]{:S(2)}) copy-start(f32[4]{0:T(128)} %constant.46.clone) | copy-start | bytes 52
  26.5 6.5 %copy-start = (f32[8,64,72,128]{3,2,1,0:T(8,128)}, f32[8,64,72,128]{3,2,1,0:T(8,128)S(1)}, u32[]{:S(2)}) copy-start(f32[8,64,72,128]{3,2,1,0:T(8,128)S(1)} %get-tuple-element.10.greens_ref) | copy-start | bytes 56623108
  33.0 29.2 %collective-permute-start.7 = (f32[576,128]{1,0:T(8,128)}, f32[576,128]{1,0:T(8,128)}, u32[]{:S(2)}, u32[]{:S(2)}) collective-permute-start(f32[576,128]{1,0:T(8,128)} %get-tuple-element.21), channel_id=1, source_target_pairs={{0,24},{4,28},{8,16},{12,20},{16,8},{20,12},{24,0},{28,4},{1,25},{... | collective-permute-start | bytes 884744 | tf_op jit(solution)/shard_map/ppermute | solution.py:448
  34.4 27.8 %collective-permute-start.8 = (f32[576,128]{1,0:T(8,128)}, f32[576,128]{1,0:T(8,128)}, u32[]{:S(2)}, u32[]{:S(2)}) collective-permute-start(f32[576,128]{1,0:T(8,128)} %get-tuple-element.20), channel_id=1, source_target_pairs={{0,28},{4,24},{8,20},{12,16},{16,12},{20,8},{24,4},{28,0},{1,29},{... | collective-permute-start | bytes 884744 | tf_op jit(solution)/shard_map/ppermute | solution.py:448
  37.0 20.5 %collective-permute-start.11 = (f32[576,128]{1,0:T(8,128)}, f32[576,128]{1,0:T(8,128)S(1)}, u32[]{:S(2)}, u32[]{:S(2)}) collective-permute-start(f32[576,128]{1,0:T(8,128)} %get-tuple-element.13), channel_id=1, source_target_pairs={{0,20},{4,16},{8,28},{12,24},{16,4},{20,0},{24,12},{28,8},{1,21},{... | collective-permute-start | bytes 884744 | tf_op jit(solution)/shard_map/ppermute | solution.py:448
  38.5 19.0 %collective-permute-start.12 = (f32[576,128]{1,0:T(8,128)}, f32[576,128]{1,0:T(8,128)}, u32[]{:S(2)}, u32[]{:S(2)}) collective-permute-start(f32[576,128]{1,0:T(8,128)} %get-tuple-element.16), channel_id=1, source_target_pairs={{0,12},{4,8},{8,4},{12,0},{16,28},{20,24},{24,20},{28,16},{1,13},{... | collective-permute-start | bytes 884744 | tf_op jit(solution)/shard_map/ppermute | solution.py:448
  40.9 16.6 %collective-permute-start.13 = (f32[576,128]{1,0:T(8,128)}, f32[576,128]{1,0:T(8,128)}, u32[]{:S(2)}, u32[]{:S(2)}) collective-permute-start(f32[576,128]{1,0:T(8,128)} %get-tuple-element.15), channel_id=1, source_target_pairs={{0,4},{4,0},{8,12},{12,8},{16,20},{20,16},{24,28},{28,24},{1,5},{5... | collective-permute-start | bytes 884744 | tf_op jit(solution)/shard_map/ppermute | solution.py:448
  42.1 20.1 %copy-start.4 = (bf16[2048,128]{1,0:T(8,128)(2,1)S(1)}, bf16[2048,128]{1,0:T(8,128)(2,1)}, u32[]{:S(2)}) copy-start(bf16[2048,128]{1,0:T(8,128)(2,1)} %constant.48.clone.gather_ref) | copy-start | bytes 1572868
  42.1 20.1 %copy-start.5 = (f32[72,128]{1,0:T(8,128)S(1)}, f32[72,128]{1,0:T(8,128)}, u32[]{:S(2)}) copy-start(f32[72,128]{1,0:T(8,128)} %equal_ref.1) | copy-start | bytes 110596
  42.1 20.1 %copy-start.6 = (f32[8,128]{1,0:T(8,128)S(1)}, f32[8,128]{1,0:T(8,128)}, u32[]{:S(2)}) copy-start(f32[8,128]{1,0:T(8,128)} %constant.47.clone.sign_ref) | copy-start | bytes 12292
  42.1 47.7 %slice-start = ((s8[18874368]{0:T(1024)(128)(4,1)}), s8[4194304]{0:T(1024)(128)(4,1)S(1)}, s32[]{:S(2)}) async-start(s8[18874368]{0:T(1024)(128)(4,1)} %bitcast.5), calls=%async_computation | async-start | bytes 8388608
  57.6 32.3 %slice-start.1 = ((s8[18874368]{0:T(1024)(128)(4,1)}), s8[4194304]{0:T(1024)(128)(4,1)S(1)}, s32[]{:S(2)}) async-start(s8[18874368]{0:T(1024)(128)(4,1)} %bitcast.5), calls=%async_computation.1 | async-start | bytes 8388608
  62.2 27.5 %copy-start.7 = (f32[72,128]{1,0:T(8,128)S(1)}, f32[72,128]{1,0:T(8,128)}, u32[]{:S(2)}) copy-start(f32[72,128]{1,0:T(8,128)} %param.12) | copy-start | bytes 110596
  62.3 27.6 %slice-start.2 = ((s8[18874368]{0:T(1024)(128)(4,1)}), s8[4194304]{0:T(1024)(128)(4,1)S(1)}, s32[]{:S(2)}) async-start(s8[18874368]{0:T(1024)(128)(4,1)} %bitcast.5), calls=%async_computation.2 | async-start | bytes 8388608
  62.3 27.6 %slice-start.3 = ((s8[18874368]{0:T(1024)(128)(4,1)}), s8[4194304]{0:T(1024)(128)(4,1)S(1)}, s32[]{:S(2)}) async-start(s8[18874368]{0:T(1024)(128)(4,1)} %bitcast.5), calls=%async_computation.3 | async-start | bytes 8388608
  62.3 27.6 %slice-start.4 = ((s8[18874368]{0:T(1024)(128)(4,1)}), s8[2097152]{0:T(1024)(128)(4,1)S(1)}, s32[]{:S(2)}) async-start(s8[18874368]{0:T(1024)(128)(4,1)} %bitcast.5), calls=%async_computation.4 | async-start | bytes 4194304
  71.1 18.7 %copy-start.3 = (bf16[256,2048]{1,0:T(8,128)(2,1)S(1)}, bf16[256,2048]{1,0:T(8,128)(2,1)}, u32[]{:S(2)}) copy-start(bf16[256,2048]{1,0:T(8,128)(2,1)} %constant.49.clone.spread_ref) | copy-start | bytes 3145732
  71.2 1.4 %collective-permute-start.14 = (f32[288,128]{1,0:T(8,128)S(1)}, f32[288,128]{1,0:T(8,128)S(1)}, u32[]{:S(2)}, u32[]{:S(2)}) collective-permute-start(f32[288,128]{1,0:T(8,128)S(1)} %pad_maximum_fusion), channel_id=1, source_target_pairs={{0,4},{4,0},{8,12},{12,8},{16,20},{20,16},{24,28},{28,24},{1,5},{5... | collective-permute-start | bytes 442376 | tf_op jit(solution)/shard_map/ppermute | solution.py:448
  72.7 4.9 %collective-permute-start.15 = (f32[72,128]{1,0:T(8,128)S(1)}, f32[72,128]{1,0:T(8,128)S(1)}, u32[]{:S(2)}, u32[]{:S(2)}) collective-permute-start(f32[72,128]{1,0:T(8,128)S(1)} %get-tuple-element.40), channel_id=1, source_target_pairs={{0,24},{4,28},{8,16},{12,20},{16,8},{20,12},{24,0},{28,4},{1,25},{... | collective-permute-start | bytes 110600 | tf_op jit(solution)/shard_map/ppermute | solution.py:448
  75.2 4.0 %collective-permute-start.16 = (f32[72,128]{1,0:T(8,128)S(1)}, f32[72,128]{1,0:T(8,128)S(1)}, u32[]{:S(2)}, u32[]{:S(2)}) collective-permute-start(f32[72,128]{1,0:T(8,128)S(1)} %get-tuple-element.39), channel_id=1, source_target_pairs={{0,16},{4,20},{8,24},{12,28},{16,0},{20,4},{24,8},{28,12},{1,17},{... | collective-permute-start | bytes 110600 | tf_op jit(solution)/shard_map/ppermute | solution.py:448
  75.8 4.0 %collective-permute-start.17 = (f32[72,128]{1,0:T(8,128)S(1)}, f32[72,128]{1,0:T(8,128)S(1)}, u32[]{:S(2)}, u32[]{:S(2)}) collective-permute-start(f32[72,128]{1,0:T(8,128)S(1)} %get-tuple-element.38), channel_id=1, source_target_pairs={{0,8},{4,12},{8,0},{12,4},{16,24},{20,28},{24,16},{28,20},{1,9},{5... | collective-permute-start | bytes 110600 | tf_op jit(solution)/shard_map/ppermute | solution.py:448
  79.8 5.3 %collective-permute-start.19 = (f32[72,128]{1,0:T(8,128)S(1)}, f32[72,128]{1,0:T(8,128)S(1)}, u32[]{:S(2)}, u32[]{:S(2)}) collective-permute-start(f32[72,128]{1,0:T(8,128)S(1)} %fusion), channel_id=1, source_target_pairs={{0,2},{1,3},{2,0},{3,1},{4,6},{5,7},{6,4},{7,5},{8,10},{9,11},{10,... | collective-permute-start | bytes 110600 | tf_op jit(solution)/shard_map/ppermute | solution.py:448
  82.5 4.4 %collective-permute-start.20 = (f32[72,128]{1,0:T(8,128)S(1)}, f32[72,128]{1,0:T(8,128)S(1)}, u32[]{:S(2)}, u32[]{:S(2)}) collective-permute-start(f32[72,128]{1,0:T(8,128)S(1)} %fusion), channel_id=1, source_target_pairs={{0,1},{1,0},{2,3},{3,2},{4,5},{5,4},{6,7},{7,6},{8,9},{9,8},{10,11... | collective-permute-start | bytes 110600 | tf_op jit(solution)/shard_map/ppermute | solution.py:448
  84.0 5.8 %collective-permute-start.18 = (f32[72,128]{1,0:T(8,128)S(1)}, f32[72,128]{1,0:T(8,128)S(1)}, u32[]{:S(2)}, u32[]{:S(2)}) collective-permute-start(f32[72,128]{1,0:T(8,128)S(1)} %fusion), channel_id=1, source_target_pairs={{0,3},{1,2},{2,1},{3,0},{4,7},{5,6},{6,5},{7,4},{8,11},{9,10},{10,... | collective-permute-start | bytes 110600 | tf_op jit(solution)/shard_map/ppermute | solution.py:448

commit v7 on v3

--- a/solution.py
+++ b/solution.py
@@ -21,8 +21,7 @@
 hubbard = 1.0
 quadrature = (0.375, 1.1666666, 0.9583333, 1.0)
 
-PITCH = 9
-LATE = 3
+LATE = 2
 AHEAD = 3
 
 
@@ -43,6 +42,11 @@
     while len(terms) > 1:
         terms = [sum(terms[i : i + 2][1:], terms[i]) for i in range(0, len(terms), 2)]
     return terms[0]
+
+
+def split(x):
+    high = x.astype(jnp.bfloat16)
+    return jnp.concatenate([high, (x - high.astype(jnp.float32)).astype(jnp.bfloat16)], axis=1)
 
 
 def dft24(x, sign, low):
@@ -109,18 +113,6 @@
     lax.fori_loop(0, SIDE // 2, columns, 0)
 
 
-def pick_kernel(steps, parts, place_ref, whole_ref, *refs):
-    block_refs, sems = refs[:-1], refs[-1]
-    copies = []
-    for n, (step, block_ref) in enumerate(zip(steps, block_refs)):
-        rows = block_ref.shape[0]
-        start = pl.multiple_of(partner_of(place_ref[0], step, parts) * rows, TILE)
-        copies.append(pltpu.make_async_copy(whole_ref.at[pl.ds(start, rows)], block_ref, sems.at[n]))
-        copies[-1].start()
-    for copy in copies:
-        copy.wait()
-
-
 def roll_kernel(green_ref, greens_ref):
     batch = math.gcd(green_ref.shape[0], STEPS)
 
@@ -212,7 +204,7 @@
         )
 
     def store(point, value):
-        sigma_ref[pl.ds(point * PITCH, TILE), :] = value
+        sigma_ref[pl.ds(point * TILE, TILE), :] = value
 
     along_first(work_ref, 1, low, store)
 
@@ -226,7 +218,7 @@
         units = [(tile, s) for tile in range(batch) for s in range(TILE)]
 
         def prepare(tile, s):
-            sigma = sigma_ref[pl.ds((first + tile) * TILE * PITCH + s, TILE, stride=PITCH), :]
+            sigma = sigma_ref[pl.ds((first + tile) * TILE * TILE + s, TILE, stride=TILE), :]
             row = pl.multiple_of(green_row + s * block + tile * TILE, TILE)
             return (
                 [roll_blocks(sigma, STEPS * i) for i in range(STEPS)],
@@ -270,14 +262,9 @@
 
 def propagate_kernel(greens_ref, effective_ref, spread_ref, out_ref, factor_ref, held_ref, sems):
     _, history, points, _ = greens_ref.shape
-    rest = effective_ref[...] * time_step
-    pieces = []
-    for _ in range(3):
-        pieces.append(rest.astype(jnp.bfloat16).astype(jnp.float32))
-        rest = rest - pieces[-1]
-    stacked = jnp.concatenate(pieces, axis=0).astype(jnp.bfloat16)
-    spread = jnp.dot(stacked, spread_ref[...], preferred_element_type=jnp.float32)
-    factor_ref[...] = tree_sum([spread[n * points : (n + 1) * points] for n in range(3)])
+    factor_ref[...] = jnp.dot(
+        split(effective_ref[...] * time_step), spread_ref[...], preferred_element_type=jnp.float32
+    )
 
     slots, chunk = held_ref.shape[:2]
 
@@ -341,7 +328,7 @@
                 h, a = divmod((p - STEPS * i) % blocks, BANDS)
                 g, b = divmod((p + j) % blocks, BANDS)
                 table[1 if h == g else 0, a, b, i, j, p, :] = -1 if (h, g) == (1, 0) else 1
-    return table.reshape(WIDTH, -1).astype(ml_dtypes.bfloat16)
+    return np.tile(table.reshape(WIDTH, -1), (2, 1)).astype(ml_dtypes.bfloat16)
 
 
 def in_vmem():
@@ -383,7 +370,7 @@
         in_specs=[in_smem()] + [anywhere()] * len(steps),
         out_specs=[in_vmem()] * 2,
         scratch_shapes=[pltpu.VMEM((points, TILE, WIDTH), jnp.float32)] + held_blocks(len(steps), parts),
-        compiler_params=params(24),
+        compiler_params=params(8),
         cost_estimate=cost(400, 6),
         name="forward",
     )(place, *greens)
@@ -397,7 +384,7 @@
         in_specs=[in_smem(), in_vmem(), in_vmem(), anywhere()] + [anywhere()] * len(steps),
         out_specs=in_vmem(),
         scratch_shapes=held_blocks(len(steps), parts),
-        compiler_params=params(16),
+        compiler_params=params(4),
         cost_estimate=cost(150, 3),
         name="early",
     )(place, lattice, weights, before, *screens)
@@ -417,31 +404,16 @@
         out_specs=[in_vmem()] * 2,
         input_output_aliases={len(inputs) - 1: 1},
         scratch_shapes=[
-            pltpu.VMEM((PITCH * points, WIDTH), jnp.float32),
+            pltpu.VMEM((TILE * points, WIDTH), jnp.float32),
             pltpu.VMEM((points, STEPS * STEPS * WIDTH), jnp.float32),
             pltpu.VMEM((points, STEPS * STEPS * WIDTH), jnp.bfloat16),
         ]
         + (held_blocks(len(steps), parts) if steps else []),
-        compiler_params=params(36),
+        compiler_params=params(16),
         cost_estimate=cost(800, 6),
         name="backward",
     )(*inputs)
     return partial_value
-
-
-def pick(place, whole, steps, parts):
-    rows = whole.shape[0] // parts
-    return pl.pallas_call(
-        functools.partial(pick_kernel, steps, parts),
-        out_shape=[jax.ShapeDtypeStruct((rows, whole.shape[1]), whole.dtype)] * len(steps),
-        in_specs=[in_smem(), anywhere()],
-        out_specs=[anywhere()] * len(steps),
-        scratch_shapes=[pltpu.SemaphoreType.DMA((len(steps),))],
-        cost_estimate=pl.CostEstimate(
-            flops=0, bytes_accessed=8 * len(steps) * rows * whole.shape[1], transcendentals=0
-        ),
-        name="pick",
-    )(place, whole)
 
 
 def roll_own(greens):
@@ -450,7 +422,7 @@
         out_shape=jax.ShapeDtypeStruct((STEPS, *greens.shape), jnp.float32),
         in_specs=[in_vmem()],
         out_specs=in_vmem(),
-        compiler_params=params(24),
+        compiler_params=params(4),
         cost_estimate=cost(3, 5),
         name="roll_own",
     )(greens)
@@ -470,7 +442,7 @@
             pltpu.VMEM((2, chunk, points, width), jnp.float32),
             pltpu.SemaphoreType.DMA((2,)),
         ],
-        compiler_params=params(24),
+        compiler_params=params(6),
         cost_estimate=cost(32, 5),
         name="propagate",
     )(greens, effective, jnp.asarray(spread))
@@ -496,7 +468,7 @@
     single = [along[n] for n in along if n and n & (n - 1) == 0]
     mixed = [along[n] for n in along if n & (n - 1)]
     order = [step for steps in zip(*single[::-1]) for step in steps]
-    return order + [step for steps in mixed for step in steps] + along[0]
+    return order + along[0] + [step for steps in mixed for step in steps]
 
 
 def class_weights(quad_class):
@@ -521,13 +493,12 @@
         groups, sources = 1, parts
         order = exchange_order(parts)
         moved = []
-        for x in (green_row, screened):
-            whole = x.reshape(parts * TILE * local, width)
-            picked = pick(seat, whole, order[:2], parts) if x is green_row else []
+        wholes = [x.reshape(parts * TILE * local, width) for x in (green_row, screened)]
+        for whole in wholes:
             found = {0: whole}
-            for n, step in enumerate(order):
+            for step in order:
                 start = partner_of(place, step, parts) * (TILE * local)
-                block = picked[n] if n < len(picked) else lax.dynamic_slice_in_dim(whole, start, TILE * local)
+                block = lax.dynamic_slice_in_dim(whole, start, TILE * local)
                 found[step] = exchange(block, "ka", step, parts)
             moved.append([found])
         order = [0] + order
@@ -569,14 +540,14 @@
         mine = jnp.concatenate([pieces[step] for step in range(0, parts, 2)], axis=0) + pairs
         pieces = [mine[n * local : (n + 1) * local] for n in range(parts // 2)]
         collision = tree_sum(
-            pieces[:1] + [exchange(pieces[n], "ka", 2 * n, parts) for n in range(1, parts // 2)]
+            pieces[:1] + [exchange(pieces[n], "ka", 2 * n, parts) for n in range(parts // 2 - 1, 0, -1)]
         )
     else:
         collision = tree_sum(
             pieces[:1] + [exchange(pieces[step], "ka", step, parts) for step in range(1, parts)]
         )
     collision = tree_sum(
-        [collision] + [exchange(collision, "hist", step, blocks) for step in range(1, blocks)]
+        [collision] + [exchange(collision, "hist", step, blocks) for step in range(blocks - 1, 0, -1)]
     )
     return propagate(own_greens, hamilton + collision)
 

time: 99.7 us -> 87.3 us (0.88)
  Pallas kernels: 43.6 us -> 24.7 us
  waiting for transfers between devices: 22.6 us -> 31.9 us
  local copies, waits for them, and re-layouts: 10.2 us -> 6.8 us
    pallas_call x1 -> x0, Pallas kernels: 19 us -> none  [pick(): pl.pallas_call(functools.partial(pick_kernel, steps, parts), out_shape=[j...]
    ppermute x21, waiting for transfers between devices: 22.6 us -> 31.9 us  [exchange(): return lax.ppermute(value, axis, pairs)]
    dynamic_slice x2, local copies, waits for them, and re-layouts: 5.45 us -> 2.94 us  [per_device(): block = lax.dynamic_slice_in_dim(whole, start, TILE * local)]
    unnamed x38 -> x40, local copies, waits for them, and re-layouts: 4.59 us -> 3.66 us
  transfers between devices with their start and end apart: 21 -> 21, of which waited for: 10 -> 13; matrix products, arithmetic and copies ran while one was open for 3% -> 2% of each run, Pallas kernels for 30% -> 14%
where the time goes in v7:
time: 87.3 us; the launch traced here: 87.2 us
  waiting for transfers between devices  31.9 us (37%)
  Pallas kernels  24.7 us (28%)
  starting transfers between devices  22.7 us (26%)
  local copies, waits for them, and re-layouts  6.8 us (8%)
  between operations  0.92 us (1%)
    ppermute x21, waiting for transfers between devices, exchange(): return lax.ppermute(value, axis, pairs)  31.9 us
    ppermute x21, starting transfers between devices, exchange(): return lax.ppermute(value, axis, pairs)  22.7 us
    pallas_call x1, Pallas kernels, backward(): pl.pallas_call(functools.partial(backward_kernel, steps, parts, share), o...  7.74 us
    pallas_call x1, Pallas kernels, forward(): pl.pallas_call(functools.partial(forward_kernel, steps, parts), out_shape...  5.8 us
    pallas_call x1, Pallas kernels, propagate(): pl.pallas_call(propagate_kernel, out_shape=jax.ShapeDtypeStruct(greens.sh...  5.09 us
    unnamed x40, local copies, waits for them, and re-layouts  3.66 us
    pallas_call x1, Pallas kernels, early_lines(): pl.pallas_call(functools.partial(early_kernel, steps, parts), out_shape=j...  3.11 us
    dynamic_slice x2, local copies, waits for them, and re-layouts, per_device(): block = lax.dynamic_slice_in_dim(whole, start, TILE * local)  2.94 us
  transfers between devices with their start and end apart: 21, of which 13 were waited for; matrix products, arithmetic and copies ran while one was open for 2% of the time, Pallas kernels for 14%

profile of v7, /device:TPU:0, one launch (start us, length us, event | category | flops | bytes accessed | tf_op | source)
XLA Modules:
  0.0 87.2 jit_solution(11053555646544143768)
XLA Ops:
  0.0 1.8 %constant_dynamic-slice_fusion.15 = (f32[576,128]{1,0:T(8,128)S(1)}, f32[576,128]{1,0:T(8,128)S(1)}, f32[576,128]{1,0:T(8,128)S(1)}, f32[576,128]{1,0:T(8,128)S(...) fusion(f32[4608,128]{1,0:T(8,128)} %bitcast.5, s32[]{:T(128)S(6)} %select_n.69, ...), kind=kLoop, calls=%fused_computation.20 | loop fusion | bytes 4128796 | tf_op jit(solution)/shard_map/dynamic_slice | solution.py:501
  1.8 0.0 copy-start.19
  1.8 3.0 %collective-permute-start = (f32[576,128]{1,0:T(8,128)S(1)}, f32[576,128]{1,0:T(8,128)S(1)}, u32[]{:S(2)}, u32[]{:S(2)}) collective-permute-start(f32[576,128]{1,0:T(8,128)S(1)} %get-tuple-element.24), channel_id=1, source_target_pairs={{0,16},{4,20},{8,24},{12,28},{16,0},{20,4},{24,8},{28,12},{1,17},{... | collective-permute-start | bytes 884744 | tf_op jit(solution)/shard_map/ppermute | solution.py:461
  4.9 1.5 %collective-permute-start.1 = (f32[576,128]{1,0:T(8,128)S(1)}, f32[576,128]{1,0:T(8,128)S(1)}, u32[]{:S(2)}, u32[]{:S(2)}) collective-permute-start(f32[576,128]{1,0:T(8,128)S(1)} %get-tuple-element.23), channel_id=1, source_target_pairs={{0,8},{4,12},{8,0},{12,4},{16,24},{20,28},{24,16},{28,20},{1,9},{5... | collective-permute-start | bytes 884744 | tf_op jit(solution)/shard_map/ppermute | solution.py:461
  6.4 0.3 collective-permute-start.3
  6.7 0.3 collective-permute-start.4
  7.0 1.2 %constant_dynamic-slice_fusion.8 = (f32[576,128]{1,0:T(8,128)}, f32[576,128]{1,0:T(8,128)}, f32[576,128]{1,0:T(8,128)S(1)}, f32[576,128]{1,0:T(8,128)S(1)}, f32[...) fusion(f32[4608,128]{1,0:T(8,128)S(1)} %bitcast.7, s32[]{:T(128)S(6)} %select_n.67, s32[]{:T(128)S(6)} %select_n.66, ...), kind=kLoop, calls=%fused_computation.13 | loop fusion | bytes 4128796 | tf_op jit(solution)/shard_map/dynamic_slice | solution.py:501
  8.2 4.5 %collective-permute-done.refs_1_ = f32[576,128]{1,0:T(8,128)S(1)} collective-permute-done((f32[576,128]{1,0:T(8,128)S(1)}, f32[576,128]{1,0:T(8,128)S(1)}, u32[]{:S(2)}, u32[]{:S(2)}) %collective-permute-start) | collective-permute-done | bytes 294944 | tf_op jit(solution)/shard_map/ppermute | solution.py:461
  12.7 3.0 %collective-permute-start.5 = (f32[576,128]{1,0:T(8,128)S(1)}, f32[576,128]{1,0:T(8,128)S(1)}, u32[]{:S(2)}, u32[]{:S(2)}) collective-permute-start(f32[576,128]{1,0:T(8,128)S(1)} %get-tuple-element.19), channel_id=1, source_target_pairs={{0,24},{4,28},{8,16},{12,20},{16,8},{20,12},{24,0},{28,4},{1,25},{... | collective-permute-start | bytes 884744 | tf_op jit(solution)/shard_map/ppermute | solution.py:461
  15.7 1.9 %collective-permute-done.2.refs_3_ = f32[576,128]{1,0:T(8,128)S(1)} collective-permute-done((f32[576,128]{1,0:T(8,128)S(1)}, f32[576,128]{1,0:T(8,128)S(1)}, u32[]{:S(2)}, u32[]{:S(2)}) %collective-permute-start.2) | collective-permute-done | bytes 294944 | tf_op jit(solution)/shard_map/ppermute | solution.py:461
  17.6 1.5 %collective-permute-start.10 = (f32[576,128]{1,0:T(8,128)S(1)}, f32[576,128]{1,0:T(8,128)S(1)}, u32[]{:S(2)}, u32[]{:S(2)}) collective-permute-start(f32[576,128]{1,0:T(8,128)S(1)} %get-tuple-element.14), channel_id=1, source_target_pairs={{0,8},{4,12},{8,0},{12,4},{16,24},{20,28},{24,16},{28,20},{1,9},{5... | collective-permute-start | bytes 884744 | tf_op jit(solution)/shard_map/ppermute | solution.py:461
  19.1 1.0 %collective-permute-done.3.refs_4_ = f32[576,128]{1,0:T(8,128)S(1)} collective-permute-done((f32[576,128]{1,0:T(8,128)S(1)}, f32[576,128]{1,0:T(8,128)S(1)}, u32[]{:S(2)}, u32[]{:S(2)}) %collective-permute-start.3) | collective-permute-done | bytes 294944 | tf_op jit(solution)/shard_map/ppermute | solution.py:461
  20.1 0.7 collective-permute-start.11
  20.9 0.7 copy-done.5
  21.6 1.5 %collective-permute-start.12 = (f32[576,128]{1,0:T(8,128)}, f32[576,128]{1,0:T(8,128)}, u32[]{:S(2)}, u32[]{:S(2)}) collective-permute-start(f32[576,128]{1,0:T(8,128)} %get-tuple-element.12), channel_id=1, source_target_pairs={{0,12},{4,8},{8,4},{12,0},{16,28},{20,24},{24,20},{28,16},{1,13},{... | collective-permute-start | bytes 884744 | tf_op jit(solution)/shard_map/ppermute | solution.py:461
  23.1 4.0 %collective-permute-done.5.refs_6_ = f32[576,128]{1,0:T(8,128)S(1)} collective-permute-done((f32[576,128]{1,0:T(8,128)S(1)}, f32[576,128]{1,0:T(8,128)S(1)}, u32[]{:S(2)}, u32[]{:S(2)}) %collective-permute-start.5) | collective-permute-done | bytes 294944 | tf_op jit(solution)/shard_map/ppermute | solution.py:461
  27.0 0.7 copy-done.7
  27.7 5.1 %collective-permute-done.6.refs_7_ = f32[576,128]{1,0:T(8,128)S(1)} collective-permute-done((f32[576,128]{1,0:T(8,128)S(1)}, f32[576,128]{1,0:T(8,128)S(1)}, u32[]{:S(2)}, u32[]{:S(2)}) %collective-permute-start.6) | collective-permute-done | bytes 294944 | tf_op jit(solution)/shard_map/ppermute | solution.py:461
  32.8 0.7 copy-done.9
  33.5 0.5 collective-permute-start.9
  34.1 6.1 %collective-permute-done.10.refs_2_ = f32[576,128]{1,0:T(8,128)S(1)} collective-permute-done((f32[576,128]{1,0:T(8,128)S(1)}, f32[576,128]{1,0:T(8,128)S(1)}, u32[]{:S(2)}, u32[]{:S(2)}) %collective-permute-start.10) | collective-permute-done | bytes 294944 | tf_op jit(solution)/shard_map/ppermute | solution.py:461
  40.1 0.7 copy-done.11
  40.8 1.4 %collective-permute-start.7 = (f32[576,128]{1,0:T(8,128)}, f32[576,128]{1,0:T(8,128)}, u32[]{:S(2)}, u32[]{:S(2)}) collective-permute-start(f32[576,128]{1,0:T(8,128)} %get-tuple-element.17), channel_id=1, source_target_pairs={{0,24},{4,28},{8,16},{12,20},{16,8},{20,12},{24,0},{28,4},{1,25},{... | collective-permute-start | bytes 884744 | tf_op jit(solution)/shard_map/ppermute | solution.py:461
  42.3 0.7 copy-done.13
  43.0 0.1 select_reduce_fusion
  43.7 0.1 dynamic_slice.76
  43.9 2.9 %roll_own.1._.greens_ref = f32[4,64,72,128]{3,2,1,0:T(8,128)S(1)} custom-call(f32[64,72,128]{2,1,0:T(8,128)S(1)} %copy-done), custom_call_target="tpu_custom_call" | custom-call | flops 1769472 | bytes 11796480 | tf_op jit(solution)/shard_map/roll_own/pallas_call | solution.py:420
  46.8 0.0 copy-start.2
  46.8 5.8 %forward.1 = (f32[576,8,128]{2,1,0:T(8,128)S(1)}, f32[4,4608,128]{2,1,0:T(8,128)S(1)}) custom-call(s32[1]{0:T(128)} %bitcast.place_ref, f32[4608,128]{1,0:T(8,128)S(1)} %bitcast.6, f32[576,128]{1,0:T(8,128)S(1)} %collective-permute-done.refs_1_, f32[576,128]{1,0:T(8,128)S(1)} %collective-permute-done.1.refs_2_, ...), custom_call_target="tpu_custom_call" | custom-call | flops 235929600 | bytes 14155776 | tf_op jit(solution)/shard_map/forward/pallas_call | solution.py:364
  52.7 0.1 squeeze.8.weight_ref
  52.8 0.0 copy-start.16
  52.8 3.1 %early.1.refs_2_ = f32[576,8,128]{2,1,0:T(8,128)S(1)} custom-call(s32[1]{0:T(128)} %bitcast.place_ref, f32[576,8,128]{2,1,0:T(8,128)S(1)} %get-tuple-element.8.lattice_ref, f32[8,128]{1,0:T(8,128)S(1)} %squeeze.8.weight_ref, f32[4,64,72,128]{3,2,1,0:T(8,128)S(1)} %roll_own.1._.greens_ref, f32[4608,128]{1,0:T(8,128)S(1)} %bitcast.8, ...), custom_call_target="tpu_custom_call" | custom-call | flops 88473600 | bytes 7077888 | tf_op jit(solution)/shard_map/early/pallas_call | solution.py:381
  55.9 0.8 collective-permute-done.8.refs_1_
  56.7 7.7 %backward.1 = (f32[576,128]{1,0:T(8,128)S(1)}, f32[576,8,128]{2,1,0:T(8,128)S(1)}) custom-call(s32[1]{0:T(128)} %bitcast.place_ref, f32[576,8,128]{2,1,0:T(8,128)S(1)} %get-tuple-element.8.lattice_ref, f32[8,128]{1,0:T(8,128)S(1)} %squeeze.8.weight_ref, f32[72,128]{1,0:T(8,128)S(1)} %copy-done.15, ...), custom_call_target="tpu_custom_call", output_to_operand_aliasing={{1}: (9, {})} | custom-call | flops 471859200 | bytes 14155776 | tf_op jit(solution)/shard_map/backward/pallas_call | solution.py:397
  64.5 0.0 copy-start.3
  64.6 0.9 %collective-permute-start.14 = (f32[288,128]{1,0:T(8,128)S(1)}, f32[288,128]{1,0:T(8,128)S(1)}, u32[]{:S(2)}, u32[]{:S(2)}) collective-permute-start(f32[288,128]{1,0:T(8,128)S(1)} %pad_maximum_fusion), channel_id=1, source_target_pairs={{0,4},{4,0},{8,12},{12,8},{16,20},{20,16},{24,28},{28,24},{1,5},{5... | collective-permute-start | bytes 442376 | tf_op jit(solution)/shard_map/ppermute | solution.py:461
  65.5 1.0 %collective-permute-done.14 = f32[288,128]{1,0:T(8,128)S(1)} collective-permute-done((f32[288,128]{1,0:T(8,128)S(1)}, f32[288,128]{1,0:T(8,128)S(1)}, u32[]{:S(2)}, u32[]{:S(2)}) %collective-permute-start.14) | collective-permute-done | bytes 147488 | tf_op jit(solution)/shard_map/ppermute | solution.py:461
  66.5 2.5 %collective-permute-start.15 = (f32[72,128]{1,0:T(8,128)S(1)}, f32[72,128]{1,0:T(8,128)S(1)}, u32[]{:S(2)}, u32[]{:S(2)}) collective-permute-start(f32[72,128]{1,0:T(8,128)S(1)} %get-tuple-element.35), channel_id=1, source_target_pairs={{0,24},{4,28},{8,16},{12,20},{16,8},{20,12},{24,0},{28,4},{1,25},{... | collective-permute-start | bytes 110600 | tf_op jit(solution)/shard_map/ppermute | solution.py:461
  69.0 0.6 collective-permute-start.16
  69.5 0.5 collective-permute-start.17
  70.1 1.4 %collective-permute-done.15 = f32[72,128]{1,0:T(8,128)S(1)} collective-permute-done((f32[72,128]{1,0:T(8,128)S(1)}, f32[72,128]{1,0:T(8,128)S(1)}, u32[]{:S(2)}, u32[]{:S(2)}) %collective-permute-start.15) | collective-permute-done | bytes 36896 | tf_op jit(solution)/shard_map/ppermute | solution.py:461
  71.5 1.5 %collective-permute-done.16 = f32[72,128]{1,0:T(8,128)S(1)} collective-permute-done((f32[72,128]{1,0:T(8,128)S(1)}, f32[72,128]{1,0:T(8,128)S(1)}, u32[]{:S(2)}, u32[]{:S(2)}) %collective-permute-start.16) | collective-permute-done | bytes 36896 | tf_op jit(solution)/shard_map/ppermute | solution.py:461
  72.9 0.6 collective-permute-done.17
  73.5 3.7 %collective-permute-start.18 = (f32[72,128]{1,0:T(8,128)S(1)}, f32[72,128]{1,0:T(8,128)S(1)}, u32[]{:S(2)}, u32[]{:S(2)}) collective-permute-start(f32[72,128]{1,0:T(8,128)S(1)} %fusion), channel_id=1, source_target_pairs={{0,3},{1,2},{2,1},{3,0},{4,7},{5,6},{6,5},{7,4},{8,11},{9,10},{10,... | collective-permute-start | bytes 110600 | tf_op jit(solution)/shard_map/ppermute | solution.py:461
  77.2 0.8 collective-permute-start.20
  78.0 1.4 %collective-permute-done.18 = f32[72,128]{1,0:T(8,128)S(1)} collective-permute-done((f32[72,128]{1,0:T(8,128)S(1)}, f32[72,128]{1,0:T(8,128)S(1)}, u32[]{:S(2)}, u32[]{:S(2)}) %collective-permute-start.18) | collective-permute-done | bytes 36896 | tf_op jit(solution)/shard_map/ppermute | solution.py:461
  79.4 2.7 %collective-permute-done.19 = f32[72,128]{1,0:T(8,128)S(1)} collective-permute-done((f32[72,128]{1,0:T(8,128)S(1)}, f32[72,128]{1,0:T(8,128)S(1)}, u32[]{:S(2)}, u32[]{:S(2)}) %collective-permute-start.19) | collective-permute-done | bytes 36896 | tf_op jit(solution)/shard_map/ppermute | solution.py:461
  82.1 5.1 %propagate.1 = f32[64,72,128]{2,1,0:T(8,128)} custom-call(f32[4,64,72,128]{3,2,1,0:T(8,128)S(1)} %roll_own.1._.greens_ref, f32[72,128]{1,0:T(8,128)S(1)} %add_add_fusion.effective_ref, bf16[256,2048]{1,0:T(8,128)(2,1)S(1)} %copy-done.3), custom_call_target="tpu_custom_call" | custom-call | flops 18874368 | bytes 11796480 | tf_op jit(solution)/shard_map/propagate/pallas_call | solution.py:435
  (51 shorter events, 0.2 us)
Async XLA Ops:
  0.0 7.0 %copy-start.1 = (f32[64,72,128]{2,1,0:T(8,128)S(1)}, f32[64,72,128]{2,1,0:T(8,128)}, u32[]{:S(2)}) copy-start(f32[64,72,128]{2,1,0:T(8,128)} %param.11) | copy-start | bytes 7077892
  1.8 41.2 %copy-start.18 = (s32[64]{0:T(128)S(1)}, s32[64]{0:T(128)}, u32[]{:S(2)}) copy-start(s32[64]{0:T(128)} %param.14) | copy-start | bytes 772
  1.8 41.2 %copy-start.19 = (f32[4]{0:T(128)S(1)}, f32[4]{0:T(128)}, u32[]{:S(2)}) copy-start(f32[4]{0:T(128)} %constant.46.clone) | copy-start | bytes 52
  1.8 42.0 %copy-start = (f32[64,72,128]{2,1,0:T(8,128)S(1)}, f32[64,72,128]{2,1,0:T(8,128)}, u32[]{:S(2)}) copy-start(f32[64,72,128]{2,1,0:T(8,128)} %green_ref.1) | copy-start | bytes 7077892
  1.8 10.9 %collective-permute-start = (f32[576,128]{1,0:T(8,128)S(1)}, f32[576,128]{1,0:T(8,128)S(1)}, u32[]{:S(2)}, u32[]{:S(2)}) collective-permute-start(f32[576,128]{1,0:T(8,128)S(1)} %get-tuple-element.24), channel_id=1, source_target_pairs={{0,16},{4,20},{8,24},{12,28},{16,0},{20,4},{24,8},{28,12},{1,17},{... | collective-permute-start | bytes 884744 | tf_op jit(solution)/shard_map/ppermute | solution.py:461
  4.9 10.8 %collective-permute-start.1 = (f32[576,128]{1,0:T(8,128)S(1)}, f32[576,128]{1,0:T(8,128)S(1)}, u32[]{:S(2)}, u32[]{:S(2)}) collective-permute-start(f32[576,128]{1,0:T(8,128)S(1)} %get-tuple-element.23), channel_id=1, source_target_pairs={{0,8},{4,12},{8,0},{12,4},{16,24},{20,28},{24,16},{28,20},{1,9},{5... | collective-permute-start | bytes 884744 | tf_op jit(solution)/shard_map/ppermute | solution.py:461
  6.4 11.2 %collective-permute-start.2 = (f32[576,128]{1,0:T(8,128)S(1)}, f32[576,128]{1,0:T(8,128)S(1)}, u32[]{:S(2)}, u32[]{:S(2)}) collective-permute-start(f32[576,128]{1,0:T(8,128)S(1)} %get-tuple-element.22), channel_id=1, source_target_pairs={{0,20},{4,16},{8,28},{12,24},{16,4},{20,0},{24,12},{28,8},{1,21},{... | collective-permute-start | bytes 884744 | tf_op jit(solution)/shard_map/ppermute | solution.py:461
  6.4 13.8 %collective-permute-start.3 = (f32[576,128]{1,0:T(8,128)S(1)}, f32[576,128]{1,0:T(8,128)S(1)}, u32[]{:S(2)}, u32[]{:S(2)}) collective-permute-start(f32[576,128]{1,0:T(8,128)S(1)} %get-tuple-element.21), channel_id=1, source_target_pairs={{0,12},{4,8},{8,4},{12,0},{16,28},{20,24},{24,20},{28,16},{1,13},{... | collective-permute-start | bytes 884744 | tf_op jit(solution)/shard_map/ppermute | solution.py:461
  6.7 14.2 %collective-permute-start.4 = (f32[576,128]{1,0:T(8,128)S(1)}, f32[576,128]{1,0:T(8,128)S(1)}, u32[]{:S(2)}, u32[]{:S(2)}) collective-permute-start(f32[576,128]{1,0:T(8,128)S(1)} %get-tuple-element.20), channel_id=1, source_target_pairs={{0,4},{4,0},{8,12},{12,8},{16,20},{20,16},{24,28},{28,24},{1,5},{5... | collective-permute-start | bytes 884744 | tf_op jit(solution)/shard_map/ppermute | solution.py:461
  12.7 14.3 %collective-permute-start.5 = (f32[576,128]{1,0:T(8,128)S(1)}, f32[576,128]{1,0:T(8,128)S(1)}, u32[]{:S(2)}, u32[]{:S(2)}) collective-permute-start(f32[576,128]{1,0:T(8,128)S(1)} %get-tuple-element.19), channel_id=1, source_target_pairs={{0,24},{4,28},{8,16},{12,20},{16,8},{20,12},{24,0},{28,4},{1,25},{... | collective-permute-start | bytes 884744 | tf_op jit(solution)/shard_map/ppermute | solution.py:461
  15.7 17.1 %collective-permute-start.6 = (f32[576,128]{1,0:T(8,128)S(1)}, f32[576,128]{1,0:T(8,128)S(1)}, u32[]{:S(2)}, u32[]{:S(2)}) collective-permute-start(f32[576,128]{1,0:T(8,128)S(1)} %get-tuple-element.18), channel_id=1, source_target_pairs={{0,28},{4,24},{8,20},{12,16},{16,12},{20,8},{24,4},{28,0},{1,29},{... | collective-permute-start | bytes 884744 | tf_op jit(solution)/shard_map/ppermute | solution.py:461
  17.6 22.5 %collective-permute-start.10 = (f32[576,128]{1,0:T(8,128)S(1)}, f32[576,128]{1,0:T(8,128)S(1)}, u32[]{:S(2)}, u32[]{:S(2)}) collective-permute-start(f32[576,128]{1,0:T(8,128)S(1)} %get-tuple-element.14), channel_id=1, source_target_pairs={{0,8},{4,12},{8,0},{12,4},{16,24},{20,28},{24,16},{28,20},{1,9},{5... | collective-permute-start | bytes 884744 | tf_op jit(solution)/shard_map/ppermute | solution.py:461
  20.1 22.1 %collective-permute-start.11 = (f32[576,128]{1,0:T(8,128)S(1)}, f32[576,128]{1,0:T(8,128)S(1)}, u32[]{:S(2)}, u32[]{:S(2)}) collective-permute-start(f32[576,128]{1,0:T(8,128)S(1)} %get-tuple-element.13), channel_id=1, source_target_pairs={{0,20},{4,16},{8,28},{12,24},{16,4},{20,0},{24,12},{28,8},{1,21},{... | collective-permute-start | bytes 884744 | tf_op jit(solution)/shard_map/ppermute | solution.py:461
  20.9 0.7 copy-start.5
  21.6 31.1 %collective-permute-start.12 = (f32[576,128]{1,0:T(8,128)}, f32[576,128]{1,0:T(8,128)}, u32[]{:S(2)}, u32[]{:S(2)}) collective-permute-start(f32[576,128]{1,0:T(8,128)} %get-tuple-element.12), channel_id=1, source_target_pairs={{0,12},{4,8},{8,4},{12,0},{16,28},{20,24},{24,20},{28,16},{1,13},{... | collective-permute-start | bytes 884744 | tf_op jit(solution)/shard_map/ppermute | solution.py:461
  27.0 0.7 copy-start.7
  27.7 24.9 %collective-permute-start.13 = (f32[576,128]{1,0:T(8,128)}, f32[576,128]{1,0:T(8,128)}, u32[]{:S(2)}, u32[]{:S(2)}) collective-permute-start(f32[576,128]{1,0:T(8,128)} %get-tuple-element.11), channel_id=1, source_target_pairs={{0,4},{4,0},{8,12},{12,8},{16,20},{20,16},{24,28},{28,24},{1,5},{5... | collective-permute-start | bytes 884744 | tf_op jit(solution)/shard_map/ppermute | solution.py:461
  32.8 0.7 copy-start.9
  33.5 19.1 %collective-permute-start.9 = (f32[576,128]{1,0:T(8,128)}, f32[576,128]{1,0:T(8,128)}, u32[]{:S(2)}, u32[]{:S(2)}) collective-permute-start(f32[576,128]{1,0:T(8,128)} %get-tuple-element.15), channel_id=1, source_target_pairs={{0,16},{4,20},{8,24},{12,28},{16,0},{20,4},{24,8},{28,12},{1,17},{... | collective-permute-start | bytes 884744 | tf_op jit(solution)/shard_map/ppermute | solution.py:461
  40.1 0.7 copy-start.11
  40.8 15.1 %collective-permute-start.7 = (f32[576,128]{1,0:T(8,128)}, f32[576,128]{1,0:T(8,128)}, u32[]{:S(2)}, u32[]{:S(2)}) collective-permute-start(f32[576,128]{1,0:T(8,128)} %get-tuple-element.17), channel_id=1, source_target_pairs={{0,24},{4,28},{8,16},{12,20},{16,8},{20,12},{24,0},{28,4},{1,25},{... | collective-permute-start | bytes 884744 | tf_op jit(solution)/shard_map/ppermute | solution.py:461
  42.3 0.7 copy-start.13
  43.0 13.7 %collective-permute-start.8 = (f32[576,128]{1,0:T(8,128)}, f32[576,128]{1,0:T(8,128)}, u32[]{:S(2)}, u32[]{:S(2)}) collective-permute-start(f32[576,128]{1,0:T(8,128)} %get-tuple-element.16), channel_id=1, source_target_pairs={{0,28},{4,24},{8,20},{12,16},{16,12},{20,8},{24,4},{28,0},{1,29},{... | collective-permute-start | bytes 884744 | tf_op jit(solution)/shard_map/ppermute | solution.py:461
  43.8 3.0 %copy-start.6 = (f32[576,128]{1,0:T(8,128)S(1)}, f32[576,128]{1,0:T(8,128)}, u32[]{:S(2)}) copy-start(f32[576,128]{1,0:T(8,128)} %copy-done.5) | copy-start | bytes 884740
  43.8 3.0 %copy-start.8 = (f32[576,128]{1,0:T(8,128)S(1)}, f32[576,128]{1,0:T(8,128)}, u32[]{:S(2)}) copy-start(f32[576,128]{1,0:T(8,128)} %copy-done.7) | copy-start | bytes 884740
  43.8 3.0 %copy-start.10 = (f32[576,128]{1,0:T(8,128)S(1)}, f32[576,128]{1,0:T(8,128)}, u32[]{:S(2)}) copy-start(f32[576,128]{1,0:T(8,128)} %copy-done.9) | copy-start | bytes 884740
  46.8 6.0 %copy-start.2 = (f32[64,72,128]{2,1,0:T(8,128)S(1)}, f32[64,72,128]{2,1,0:T(8,128)}, u32[]{:S(2)}) copy-start(f32[64,72,128]{2,1,0:T(8,128)} %param.11) | copy-start | bytes 7077892
  46.8 6.0 %copy-start.12 = (f32[576,128]{1,0:T(8,128)S(1)}, f32[576,128]{1,0:T(8,128)}, u32[]{:S(2)}) copy-start(f32[576,128]{1,0:T(8,128)} %copy-done.11) | copy-start | bytes 884740
  46.8 6.0 %copy-start.14 = (f32[576,128]{1,0:T(8,128)S(1)}, f32[576,128]{1,0:T(8,128)}, u32[]{:S(2)}) copy-start(f32[576,128]{1,0:T(8,128)} %copy-done.13) | copy-start | bytes 884740
  52.8 4.0 %copy-start.4 = (bf16[2048,128]{1,0:T(8,128)(2,1)S(1)}, bf16[2048,128]{1,0:T(8,128)(2,1)}, u32[]{:S(2)}) copy-start(bf16[2048,128]{1,0:T(8,128)(2,1)} %constant.48.clone.gather_ref) | copy-start | bytes 1572868
  52.8 4.0 %copy-start.15 = (f32[72,128]{1,0:T(8,128)S(1)}, f32[72,128]{1,0:T(8,128)}, u32[]{:S(2)}) copy-start(f32[72,128]{1,0:T(8,128)} %equal_ref.1) | copy-start | bytes 110596
  52.8 4.0 %copy-start.16 = (f32[8,128]{1,0:T(8,128)S(1)}, f32[8,128]{1,0:T(8,128)}, u32[]{:S(2)}) copy-start(f32[8,128]{1,0:T(8,128)} %constant.47.clone.sign_ref) | copy-start | bytes 12292
  56.7 25.3 %copy-start.17 = (f32[72,128]{1,0:T(8,128)S(1)}, f32[72,128]{1,0:T(8,128)}, u32[]{:S(2)}) copy-start(f32[72,128]{1,0:T(8,128)} %param.12) | copy-start | bytes 110596
  64.5 17.6 %copy-start.3 = (bf16[256,2048]{1,0:T(8,128)(2,1)S(1)}, bf16[256,2048]{1,0:T(8,128)(2,1)}, u32[]{:S(2)}) copy-start(bf16[256,2048]{1,0:T(8,128)(2,1)} %constant.49.clone.spread_ref) | copy-start | bytes 3145732
  64.6 1.9 %collective-permute-start.14 = (f32[288,128]{1,0:T(8,128)S(1)}, f32[288,128]{1,0:T(8,128)S(1)}, u32[]{:S(2)}, u32[]{:S(2)}) collective-permute-start(f32[288,128]{1,0:T(8,128)S(1)} %pad_maximum_fusion), channel_id=1, source_target_pairs={{0,4},{4,0},{8,12},{12,8},{16,20},{20,16},{24,28},{28,24},{1,5},{5... | collective-permute-start | bytes 442376 | tf_op jit(solution)/shard_map/ppermute | solution.py:461
  66.5 4.9 %collective-permute-start.15 = (f32[72,128]{1,0:T(8,128)S(1)}, f32[72,128]{1,0:T(8,128)S(1)}, u32[]{:S(2)}, u32[]{:S(2)}) collective-permute-start(f32[72,128]{1,0:T(8,128)S(1)} %get-tuple-element.35), channel_id=1, source_target_pairs={{0,24},{4,28},{8,16},{12,20},{16,8},{20,12},{24,0},{28,4},{1,25},{... | collective-permute-start | bytes 110600 | tf_op jit(solution)/shard_map/ppermute | solution.py:461
  69.0 4.0 %collective-permute-start.16 = (f32[72,128]{1,0:T(8,128)S(1)}, f32[72,128]{1,0:T(8,128)S(1)}, u32[]{:S(2)}, u32[]{:S(2)}) collective-permute-start(f32[72,128]{1,0:T(8,128)S(1)} %get-tuple-element.34), channel_id=1, source_target_pairs={{0,16},{4,20},{8,24},{12,28},{16,0},{20,4},{24,8},{28,12},{1,17},{... | collective-permute-start | bytes 110600 | tf_op jit(solution)/shard_map/ppermute | solution.py:461
  69.5 4.0 %collective-permute-start.17 = (f32[72,128]{1,0:T(8,128)S(1)}, f32[72,128]{1,0:T(8,128)S(1)}, u32[]{:S(2)}, u32[]{:S(2)}) collective-permute-start(f32[72,128]{1,0:T(8,128)S(1)} %get-tuple-element.33), channel_id=1, source_target_pairs={{0,8},{4,12},{8,0},{12,4},{16,24},{20,28},{24,16},{28,20},{1,9},{5... | collective-permute-start | bytes 110600 | tf_op jit(solution)/shard_map/ppermute | solution.py:461
  73.5 5.8 %collective-permute-start.18 = (f32[72,128]{1,0:T(8,128)S(1)}, f32[72,128]{1,0:T(8,128)S(1)}, u32[]{:S(2)}, u32[]{:S(2)}) collective-permute-start(f32[72,128]{1,0:T(8,128)S(1)} %fusion), channel_id=1, source_target_pairs={{0,3},{1,2},{2,1},{3,0},{4,7},{5,6},{6,5},{7,4},{8,11},{9,10},{10,... | collective-permute-start | bytes 110600 | tf_op jit(solution)/shard_map/ppermute | solution.py:461
  77.2 4.9 %collective-permute-start.19 = (f32[72,128]{1,0:T(8,128)S(1)}, f32[72,128]{1,0:T(8,128)S(1)}, u32[]{:S(2)}, u32[]{:S(2)}) collective-permute-start(f32[72,128]{1,0:T(8,128)S(1)} %fusion), channel_id=1, source_target_pairs={{0,2},{1,3},{2,0},{3,1},{4,6},{5,7},{6,4},{7,5},{8,10},{9,11},{10,... | collective-permute-start | bytes 110600 | tf_op jit(solution)/shard_map/ppermute | solution.py:461
  77.2 4.9 %collective-permute-start.20 = (f32[72,128]{1,0:T(8,128)S(1)}, f32[72,128]{1,0:T(8,128)S(1)}, u32[]{:S(2)}, u32[]{:S(2)}) collective-permute-start(f32[72,128]{1,0:T(8,128)S(1)} %fusion), channel_id=1, source_target_pairs={{0,1},{1,0},{2,3},{3,2},{4,5},{5,4},{6,7},{7,6},{8,9},{9,8},{10,11... | collective-permute-start | bytes 110600 | tf_op jit(solution)/shard_map/ppermute | solution.py:461

commit v8 on v7

--- a/solution.py
+++ b/solution.py
@@ -190,12 +190,9 @@
     )
 
 
-def backward_kernel(
-    steps, parts, share, place_ref, lattice_ref, weight_ref, equal_ref, sign_ref, gather_ref, greens_ref, *refs
-):
+def sigma_kernel(steps, parts, place_ref, lattice_ref, weight_ref, *refs):
     screen_refs, refs = refs[: len(steps)], refs[len(steps) :]
-    _, partial_ref, work_ref, sigma_ref, sums_ref, pieces_ref, *late = refs
-    points = SIDE * SIDE
+    _, work_ref, sigma_ref, *late = refs
     low = lane_sign((TILE, WIDTH))
     if steps:
         held_ref, sems = late
@@ -208,18 +205,24 @@
 
     along_first(work_ref, 1, low, store)
 
-    block = points // parts
+
+def contract_kernel(share, owner_ref, sigma_ref, equal_ref, sign_ref, gather_ref, greens_ref, *refs):
+    partial_ref, sums_ref, pieces_ref = refs[-3:]
+    low = lane_sign((TILE, WIDTH))
+    points = partial_ref.shape[0]
+    block = points // owner_ref.shape[0]
     tiles = block // TILE
     batch = max(n for n in range(1, 10) if tiles % n == 0)
 
     def contract(group, carry):
-        first = group * batch
-        green_row = (first // tiles) * TILE * block + (first % tiles) * TILE
+        slot, first = group // (tiles // batch), group % (tiles // batch) * batch
+        owner = owner_ref[slot]
         units = [(tile, s) for tile in range(batch) for s in range(TILE)]
 
         def prepare(tile, s):
-            sigma = sigma_ref[pl.ds((first + tile) * TILE * TILE + s, TILE, stride=TILE), :]
-            row = pl.multiple_of(green_row + s * block + tile * TILE, TILE)
+            point = owner * block + (first + tile) * TILE
+            sigma = sigma_ref[pl.ds(point * TILE + s, TILE, stride=TILE), :]
+            row = pl.multiple_of((owner * TILE + s) * block + (first + tile) * TILE, TILE)
             return (
                 [roll_blocks(sigma, STEPS * i) for i in range(STEPS)],
                 [greens_ref[j, pl.ds(row, TILE), :] for j in range(STEPS)],
@@ -233,7 +236,7 @@
             terms = [sigma * green for sigma in sigmas for green in greens]
             sums = terms if s == 0 else [a + b for a, b in zip(sums, terms)]
             if s == TILE - 1:
-                row = pl.ds(pl.multiple_of((first + tile) * TILE, TILE), TILE)
+                row = pl.ds(pl.multiple_of(slot * block + (first + tile) * TILE, TILE), TILE)
                 for spot, value in enumerate(sums):
                     sums_ref[row, spot * WIDTH : (spot + 1) * WIDTH] = value
         return carry
@@ -245,19 +248,16 @@
     occupied = jnp.sum(jnp.where((inner >= 0) & (inner % (BANDS + 1) == 0), equal_ref[...], 0.0))
     spots = lax.broadcasted_iota(jnp.int32, (points, WIDTH), 1)
     on_diagonal = (spots < ENTRIES) & (spots % (BANDS + 1) == 0)
-    lower = spots < ENTRIES
+    lower = lax.broadcasted_iota(jnp.int32, (sums_ref.shape[0], WIDTH), 1) < ENTRIES
     for pair in range(STEPS * STEPS // 2):
         first_part = sums_ref[:, 2 * pair * WIDTH : (2 * pair + 1) * WIDTH]
         second_part = sums_ref[:, (2 * pair + 1) * WIDTH : (2 * pair + 2) * WIDTH]
         folded = jnp.where(lower, first_part, second_part) + sign_ref[pair : pair + 1, :] * swap(
             jnp.where(lower, second_part, first_part)
         )
-        coarse = folded.astype(jnp.bfloat16)
-        fine = (folded - coarse.astype(jnp.float32)).astype(jnp.bfloat16)
-        pieces_ref[:, 2 * pair * WIDTH : (2 * pair + 1) * WIDTH] = coarse
-        pieces_ref[:, (2 * pair + 1) * WIDTH : (2 * pair + 2) * WIDTH] = fine
+        pieces_ref[:, 2 * pair * WIDTH : (2 * pair + 2) * WIDTH] = split(folded)
     total = jnp.dot(pieces_ref[...], gather_ref[...], preferred_element_type=jnp.float32)
-    partial_ref[...] = total + jnp.where(on_diagonal, occupied * share, 0.0)
+    partial_ref[...] = total[:points] + jnp.where(on_diagonal, occupied * share, 0.0)
 
 
 def propagate_kernel(greens_ref, effective_ref, spread_ref, out_ref, factor_ref, held_ref, sems):
@@ -390,30 +390,43 @@
     )(place, lattice, weights, before, *screens)
 
 
-def backward(place, lattice, weights, equal_time, greens, screens, work, steps, parts, share):
+def sigma_of(place, lattice, weights, screens, work, steps, parts):
     points = SIDE * SIDE
+    inputs = (place, lattice, weights, *screens, work)
+    work, sigma = pl.pallas_call(
+        functools.partial(sigma_kernel, steps, parts),
+        out_shape=[
+            jax.ShapeDtypeStruct((points, TILE, WIDTH), jnp.float32),
+            jax.ShapeDtypeStruct((TILE * points, WIDTH), jnp.float32),
+        ],
+        in_specs=[in_smem()] + [in_vmem()] * 2 + [anywhere()] * len(steps) + [in_vmem()],
+        out_specs=[in_vmem()] * 2,
+        input_output_aliases={len(inputs) - 1: 0},
+        scratch_shapes=held_blocks(len(steps), parts) if steps else [],
+        compiler_params=params(4),
+        cost_estimate=cost(200, 6),
+        name="sigma",
+    )(*inputs)
+    return sigma
+
+
+def contract(owners, sigma, equal_time, greens, block, share, before=()):
+    points = owners.shape[0] * block
+    rows = -(-points // 16) * 16
     signs, gather = gather_tables()
-    inputs = (place, lattice, weights, equal_time, jnp.asarray(signs), jnp.asarray(gather), greens, *screens, work)
-    partial_value, _ = pl.pallas_call(
-        functools.partial(backward_kernel, steps, parts, share),
-        out_shape=[
-            jax.ShapeDtypeStruct((points, WIDTH), jnp.float32),
-            jax.ShapeDtypeStruct((points, TILE, WIDTH), jnp.float32),
+    return pl.pallas_call(
+        functools.partial(contract_kernel, share),
+        out_shape=jax.ShapeDtypeStruct((points, WIDTH), jnp.float32),
+        in_specs=[in_smem()] + [in_vmem()] * 5 + [anywhere()] * len(before),
+        out_specs=in_vmem(),
+        scratch_shapes=[
+            pltpu.VMEM((rows, STEPS * STEPS * WIDTH), jnp.float32),
+            pltpu.VMEM((rows, STEPS * STEPS * WIDTH), jnp.bfloat16),
         ],
-        in_specs=[in_smem()] + [in_vmem()] * 6 + [anywhere()] * len(steps) + [in_vmem()],
-        out_specs=[in_vmem()] * 2,
-        input_output_aliases={len(inputs) - 1: 1},
-        scratch_shapes=[
-            pltpu.VMEM((TILE * points, WIDTH), jnp.float32),
-            pltpu.VMEM((points, STEPS * STEPS * WIDTH), jnp.float32),
-            pltpu.VMEM((points, STEPS * STEPS * WIDTH), jnp.bfloat16),
-        ]
-        + (held_blocks(len(steps), parts) if steps else []),
-        compiler_params=params(16),
-        cost_estimate=cost(800, 6),
-        name="backward",
-    )(*inputs)
-    return partial_value
+        compiler_params=params(10),
+        cost_estimate=cost(70 * owners.shape[0], 6),
+        name="contract",
+    )(owners, sigma, equal_time, jnp.asarray(signs), jnp.asarray(gather), greens, *before)
 
 
 def roll_own(greens):
@@ -518,31 +531,45 @@
     early = order[: max(1, len(order) - LATE)]
     late = order[len(early) :]
     own_greens = roll_own(green_row)
-    partial_value = None
+    share = hubbard / (points * blocks)
+    sigmas = []
     for group in range(groups):
         green, screen = moved[0][group], moved[1][group]
         lattice, greens = forward(seat, [green[step] for step in order], order, sources)
         work = early_lines(
             seat, lattice, weights[group], own_greens, [screen[step] for step in early], early, sources
         )
-        share = hubbard / (points * blocks) if group == 0 else 0.0
-        term = backward(
-            seat, lattice, weights[group], equal_time, greens, [screen[step] for step in late], work,
-            late, sources, share,
-        )
-        partial_value = term if partial_value is None else partial_value + term
-
-    owners = [partner_of(place, step, parts) for step in range(parts)]
-    pieces = [lax.dynamic_slice_in_dim(partial_value, owner * local, local) for owner in owners]
-    if parts % 2 == 0 and parts & (parts - 1) == 0:
-        pairs = jnp.concatenate([pieces[step] for step in range(1, parts, 2)], axis=0)
-        pairs = exchange(pairs, "ka", 1, parts)
-        mine = jnp.concatenate([pieces[step] for step in range(0, parts, 2)], axis=0) + pairs
-        pieces = [mine[n * local : (n + 1) * local] for n in range(parts // 2)]
-        collision = tree_sum(
-            pieces[:1] + [exchange(pieces[n], "ka", 2 * n, parts) for n in range(parts // 2 - 1, 0, -1)]
-        )
+        sigma = sigma_of(
+            seat, lattice, weights[group], [screen[step] for step in late], work, late, sources
+        )
+        sigmas.append((sigma, greens))
+
+    if sources == parts and parts % 2 == 0 and parts & (parts - 1) == 0:
+        (sigma, greens), = sigmas
+
+        def blocks_of(steps, before=()):
+            owners = jnp.stack([partner_of(place, step, parts) for step in steps])
+            return contract(owners, sigma, equal_time, greens, local, share, before)
+
+        others = exchange(blocks_of(list(range(3, parts, 2))), "ka", 1, parts)
+        others = blocks_of(list(range(2, parts, 2))) + others
+        pieces = [
+            exchange(others[(n - 1) * local : n * local], "ka", 2 * n, parts)
+            for n in range(parts // 2 - 1, 0, -1)
+        ]
+        chip = blocks_of([1, 0], (others,))
+        pieces += [exchange(chip[:local], "ka", 1, parts), chip[local:]]
+        collision = tree_sum(pieces)
     else:
+        whole = jnp.zeros((1,), jnp.int32)
+        partial_value = tree_sum(
+            [
+                contract(whole, sigma, equal_time, greens, points, share if group == 0 else 0.0)
+                for group, (sigma, greens) in enumerate(sigmas)
+            ]
+        )
+        owners = [partner_of(place, step, parts) for step in range(parts)]
+        pieces = [lax.dynamic_slice_in_dim(partial_value, owner * local, local) for owner in owners]
         collision = tree_sum(
             pieces[:1] + [exchange(pieces[step], "ka", step, parts) for step in range(1, parts)]
         )

time: 87.3 us -> 101 us (1.16)
  waiting for transfers between devices: 31.9 us -> 41.5 us
  starting transfers between devices: 22.7 us -> 24.9 us
  Pallas kernels: 24.7 us -> 26.8 us
    ppermute x21 -> x22, waiting for transfers between devices: 31.9 us -> 41.5 us  [exchange(): return lax.ppermute(value, axis, pairs)]
    ppermute x21 -> x22, starting transfers between devices: 22.7 us -> 24.9 us  [exchange(): return lax.ppermute(value, axis, pairs)]
    pallas_call x1 -> x4, Pallas kernels: 7.74 us -> 9.68 us  [the longest x3 5.85 us: contract(): pl.pallas_call(functools.partial(contract_kernel, share), out_shape=jax.S...]
    unnamed x40 -> x38, local copies, waits for them, and re-layouts: 3.66 us -> 3.67 us
  transfers between devices with their start and end apart: 21 -> 22, of which waited for: 13 -> 11; matrix products, arithmetic and copies ran while one was open for 2% -> 1% of each run, Pallas kernels for 14% -> 14%
where the time goes in v8:
time: 101 us
  waiting for transfers between devices  41.5 us (41%)
  Pallas kernels  26.8 us (27%)
  starting transfers between devices  24.9 us (25%)
  local copies, waits for them, and re-layouts  6.78 us (7%)
    ppermute x22, waiting for transfers between devices, exchange(): return lax.ppermute(value, axis, pairs)  41.5 us
    ppermute x22, starting transfers between devices, exchange(): return lax.ppermute(value, axis, pairs)  24.9 us
    pallas_call x3, Pallas kernels, contract(): pl.pallas_call(functools.partial(contract_kernel, share), out_shape=jax.S...  5.85 us
    pallas_call x1, Pallas kernels, forward(): pl.pallas_call(functools.partial(forward_kernel, steps, parts), out_shape...  5.8 us
    pallas_call x1, Pallas kernels, propagate(): pl.pallas_call(propagate_kernel, out_shape=jax.ShapeDtypeStruct(greens.sh...  5.33 us
    pallas_call x1, Pallas kernels, sigma_of(): pl.pallas_call(functools.partial(sigma_kernel, steps, parts), out_shape=[...  3.83 us
    unnamed x38, local copies, waits for them, and re-layouts  3.67 us
    pallas_call x1, Pallas kernels, early_lines(): pl.pallas_call(functools.partial(early_kernel, steps, parts), out_shape=j...  3.07 us
  transfers between devices with their start and end apart: 22, of which 11 were waited for; matrix products, arithmetic and copies ran while one was open for 1% of the time, Pallas kernels for 14%

profile of v8, /device:TPU:0, one launch (start us, length us, event | category | flops | bytes accessed | tf_op | source)
XLA Modules:
  0.0 101.2 jit_solution(1810359580352165636)
XLA Ops:
  0.0 2.8 %constant_dynamic-slice_fusion = (f32[576,128]{1,0:T(8,128)S(1)}, f32[576,128]{1,0:T(8,128)S(1)}, f32[576,128]{1,0:T(8,128)}, f32[576,128]{1,0:T(8,128)}, f32[57...) fusion(f32[4608,128]{1,0:T(8,128)} %bitcast.14, s32[]{:T(128)S(6)} %select_n.43, s32[]{:T(128)S(6)} %select_n.42, ...), kind=kLoop, calls=%fused_computation.2 | loop fusion | bytes 4128796 | tf_op jit(solution)/shard_map/dynamic_slice | solution.py:514
  2.8 0.5 collective-permute-start.13
  3.3 2.6 %collective-permute-start.12 = (f32[576,128]{1,0:T(8,128)S(1)}, f32[576,128]{1,0:T(8,128)S(1)}, u32[]{:S(2)}, u32[]{:S(2)}) collective-permute-start(f32[576,128]{1,0:T(8,128)S(1)} %get-tuple-element.12), channel_id=1, source_target_pairs={{0,12},{4,8},{8,4},{12,0},{16,28},{20,24},{24,20},{28,16},{1,13},{... | collective-permute-start | bytes 884744 | tf_op jit(solution)/shard_map/ppermute | solution.py:474
  5.9 0.2 constant_dynamic-slice_fusion.7
  6.1 1.2 %collective-permute-start.6 = (f32[576,128]{1,0:T(8,128)S(1)}, f32[576,128]{1,0:T(8,128)S(1)}, u32[]{:S(2)}, u32[]{:S(2)}) collective-permute-start(f32[576,128]{1,0:T(8,128)S(1)} %get-tuple-element.18), channel_id=1, source_target_pairs={{0,28},{4,24},{8,20},{12,16},{16,12},{20,8},{24,4},{28,0},{1,29},{... | collective-permute-start | bytes 884744 | tf_op jit(solution)/shard_map/ppermute | solution.py:474
  7.3 1.4 %collective-permute-start.5 = (f32[576,128]{1,0:T(8,128)S(1)}, f32[576,128]{1,0:T(8,128)S(1)}, u32[]{:S(2)}, u32[]{:S(2)}) collective-permute-start(f32[576,128]{1,0:T(8,128)S(1)} %get-tuple-element.19), channel_id=1, source_target_pairs={{0,24},{4,28},{8,16},{12,20},{16,8},{20,12},{24,0},{28,4},{1,25},{... | collective-permute-start | bytes 884744 | tf_op jit(solution)/shard_map/ppermute | solution.py:474
  8.7 0.2 collective-permute-start.4
  8.9 0.7 copy-done.11
  9.6 0.4 collective-permute-start.3
  10.1 3.2 %collective-permute-done.12.refs_4_ = f32[576,128]{1,0:T(8,128)S(1)} collective-permute-done((f32[576,128]{1,0:T(8,128)S(1)}, f32[576,128]{1,0:T(8,128)S(1)}, u32[]{:S(2)}, u32[]{:S(2)}) %collective-permute-start.12) | collective-permute-done | bytes 294944 | tf_op jit(solution)/shard_map/ppermute | solution.py:474
  13.3 0.7 copy-done.13
  14.0 2.2 %collective-permute-start.2 = (f32[576,128]{1,0:T(8,128)S(1)}, f32[576,128]{1,0:T(8,128)S(1)}, u32[]{:S(2)}, u32[]{:S(2)}) collective-permute-start(f32[576,128]{1,0:T(8,128)S(1)} %get-tuple-element.22), channel_id=1, source_target_pairs={{0,20},{4,16},{8,28},{12,24},{16,4},{20,0},{24,12},{28,8},{1,21},{... | collective-permute-start | bytes 884744 | tf_op jit(solution)/shard_map/ppermute | solution.py:474
  16.2 4.3 %collective-permute-done.6.refs_7_ = f32[576,128]{1,0:T(8,128)S(1)} collective-permute-done((f32[576,128]{1,0:T(8,128)S(1)}, f32[576,128]{1,0:T(8,128)S(1)}, u32[]{:S(2)}, u32[]{:S(2)}) %collective-permute-start.6) | collective-permute-done | bytes 294944 | tf_op jit(solution)/shard_map/ppermute | solution.py:474
  20.5 1.5 %collective-permute-start.1 = (f32[576,128]{1,0:T(8,128)S(1)}, f32[576,128]{1,0:T(8,128)S(1)}, u32[]{:S(2)}, u32[]{:S(2)}) collective-permute-start(f32[576,128]{1,0:T(8,128)S(1)} %get-tuple-element.23), channel_id=1, source_target_pairs={{0,8},{4,12},{8,0},{12,4},{16,24},{20,28},{24,16},{28,20},{1,9},{5... | collective-permute-start | bytes 884744 | tf_op jit(solution)/shard_map/ppermute | solution.py:474
  22.0 5.9 %collective-permute-done.5.refs_6_ = f32[576,128]{1,0:T(8,128)S(1)} collective-permute-done((f32[576,128]{1,0:T(8,128)S(1)}, f32[576,128]{1,0:T(8,128)S(1)}, u32[]{:S(2)}, u32[]{:S(2)}) %collective-permute-start.5) | collective-permute-done | bytes 294944 | tf_op jit(solution)/shard_map/ppermute | solution.py:474
  28.6 0.1 select_reduce_fusion
  28.6 0.4 collective-permute-start.11
  29.0 3.2 %collective-permute-done.3.refs_4_ = f32[576,128]{1,0:T(8,128)S(1)} collective-permute-done((f32[576,128]{1,0:T(8,128)S(1)}, f32[576,128]{1,0:T(8,128)S(1)}, u32[]{:S(2)}, u32[]{:S(2)}) %collective-permute-start.3) | collective-permute-done | bytes 294944 | tf_op jit(solution)/shard_map/ppermute | solution.py:474
  32.3 1.3 %collective-permute-start.10 = (f32[576,128]{1,0:T(8,128)}, f32[576,128]{1,0:T(8,128)}, u32[]{:S(2)}, u32[]{:S(2)}) collective-permute-start(f32[576,128]{1,0:T(8,128)} %get-tuple-element.14), channel_id=1, source_target_pairs={{0,8},{4,12},{8,0},{12,4},{16,24},{20,28},{24,16},{28,20},{1,9},{5... | collective-permute-start | bytes 884744 | tf_op jit(solution)/shard_map/ppermute | solution.py:474
  33.6 0.7 copy-done.5
  34.3 1.5 %collective-permute-start.9 = (f32[576,128]{1,0:T(8,128)}, f32[576,128]{1,0:T(8,128)}, u32[]{:S(2)}, u32[]{:S(2)}) collective-permute-start(f32[576,128]{1,0:T(8,128)} %get-tuple-element.15), channel_id=1, source_target_pairs={{0,16},{4,20},{8,24},{12,28},{16,0},{20,4},{24,8},{28,12},{1,17},{... | collective-permute-start | bytes 884744 | tf_op jit(solution)/shard_map/ppermute | solution.py:474
  35.8 3.2 %collective-permute-done.1.refs_2_ = f32[576,128]{1,0:T(8,128)S(1)} collective-permute-done((f32[576,128]{1,0:T(8,128)S(1)}, f32[576,128]{1,0:T(8,128)S(1)}, u32[]{:S(2)}, u32[]{:S(2)}) %collective-permute-start.1) | collective-permute-done | bytes 294944 | tf_op jit(solution)/shard_map/ppermute | solution.py:474
  39.0 0.7 copy-done.7
  39.8 1.6 %collective-permute-start.8 = (f32[576,128]{1,0:T(8,128)}, f32[576,128]{1,0:T(8,128)}, u32[]{:S(2)}, u32[]{:S(2)}) collective-permute-start(f32[576,128]{1,0:T(8,128)} %get-tuple-element.16), channel_id=1, source_target_pairs={{0,28},{4,24},{8,20},{12,16},{16,12},{20,8},{24,4},{28,0},{1,29},{... | collective-permute-start | bytes 884744 | tf_op jit(solution)/shard_map/ppermute | solution.py:474
  41.3 0.7 copy-done.9
  42.0 1.4 %collective-permute-start.7 = (f32[576,128]{1,0:T(8,128)}, f32[576,128]{1,0:T(8,128)}, u32[]{:S(2)}, u32[]{:S(2)}) collective-permute-start(f32[576,128]{1,0:T(8,128)} %get-tuple-element.17), channel_id=1, source_target_pairs={{0,24},{4,28},{8,16},{12,20},{16,8},{20,12},{24,0},{28,4},{1,25},{... | collective-permute-start | bytes 884744 | tf_op jit(solution)/shard_map/ppermute | solution.py:474
  43.5 2.9 %roll_own.1._.greens_ref = f32[4,64,72,128]{3,2,1,0:T(8,128)S(1)} custom-call(f32[64,72,128]{2,1,0:T(8,128)S(1)} %copy-done), custom_call_target="tpu_custom_call" | custom-call | flops 1769472 | bytes 11796480 | tf_op jit(solution)/shard_map/roll_own/pallas_call | solution.py:433
  46.7 5.8 %forward.1 = (f32[576,8,128]{2,1,0:T(8,128)S(1)}, f32[4,4608,128]{2,1,0:T(8,128)S(1)}) custom-call(s32[1]{0:T(128)} %bitcast.3.place_ref, f32[4608,128]{1,0:T(8,128)S(1)} %bitcast.13, f32[576,128]{1,0:T(8,128)S(1)} %copy-done.10, f32[576,128]{1,0:T(8,128)S(1)} %copy-done.8, f32[576,128]{1,0:T(8,128)S(1)} %copy-done.6, ...), custom_call_target="tpu_custom_call" | custom-call | flops 235929600 | bytes 14155776 | tf_op jit(solution)/shard_map/forward/pallas_call | solution.py:364
  52.5 12.8 %collective-permute-done.9.refs_1_ = f32[576,128]{1,0:T(8,128)} collective-permute-done((f32[576,128]{1,0:T(8,128)}, f32[576,128]{1,0:T(8,128)}, u32[]{:S(2)}, u32[]{:S(2)}) %collective-permute-start.9) | collective-permute-done | bytes 294944 | tf_op jit(solution)/shard_map/ppermute | solution.py:474
  65.4 3.1 %early.1.refs_2_ = f32[576,8,128]{2,1,0:T(8,128)S(1)} custom-call(s32[1]{0:T(128)} %bitcast.3.place_ref, f32[576,8,128]{2,1,0:T(8,128)S(1)} %get-tuple-element.8.lattice_ref, f32[8,128]{1,0:T(8,128)S(1)} %squeeze.8.weight_ref, f32[4,64,72,128]{3,2,1,0:T(8,128)S(1)} %roll_own.1._.greens_ref, f32[4608,128]{1,0:T(8,128)S(1)} %bitcast.15, ...), custom_call_target="tpu_custom_call" | custom-call | flops 88473600 | bytes 7077888 | tf_op jit(solution)/shard_map/early/pallas_call | solution.py:381
  68.5 3.8 %sigma.1 = (f32[576,8,128]{2,1,0:T(8,128)S(1)}, f32[4608,128]{1,0:T(8,128)S(1)}) custom-call(s32[1]{0:T(128)} %bitcast.3.place_ref, f32[576,8,128]{2,1,0:T(8,128)S(1)} %get-tuple-element.8.lattice_ref, f32[8,128]{1,0:T(8,128)S(1)} %squeeze.8.weight_ref, f32[576,128]{1,0:T(8,128)} %collective-permute-done.7.refs_0_, ...), custom_call_target="tpu_custom_call", output_to_operand_aliasing={{0}: (5, {})} | custom-call | flops 117964800 | bytes 14155776 | tf_op jit(solution)/shard_map/sigma/pallas_call | solution.py:396
  72.4 2.1 %contract.4 = f32[216,128]{1,0:T(8,128)S(1)} custom-call(s32[3]{0:T(128)S(1)} %pad_add_fusion.1.owner_ref, f32[4608,128]{1,0:T(8,128)S(1)} %get-tuple-element.9.sigma_ref, f32[72,128]{1,0:T(8,128)S(1)} %copy-done.4, f32[8,128]{1,0:T(8,128)S(1)} %copy-done.15, bf16[2048,128]{1,0:T(8,128)(2,1)S(1)} %copy-done.2, f32[4,4608,128]{2,1,0:T(8,128)S(1)} %get-tuple-element.10.greens_ref), custom_call_target="tpu_custom_call" | custom-call | flops 123863040 | bytes 14155776 | tf_op jit(solution)/shard_map/contract/pallas_call | solution.py:417
  74.5 0.2 collective-permute-start.14
  74.7 2.1 %contract.3 = f32[216,128]{1,0:T(8,128)S(1)} custom-call(s32[3]{0:T(128)S(1)} %pad_add_fusion.owner_ref, f32[4608,128]{1,0:T(8,128)S(1)} %get-tuple-element.9.sigma_ref, f32[72,128]{1,0:T(8,128)S(1)} %copy-done.4, f32[8,128]{1,0:T(8,128)S(1)} %copy-done.15, bf16[2048,128]{1,0:T(8,128)(2,1)S(1)} %copy-done.2, f32[4,4608,128]{2,1,0:T(8,128)S(1)} %get-tuple-element.10.greens_ref), custom_call_target="tpu_custom_call" | custom-call | flops 123863040 | bytes 14155776 | tf_op jit(solution)/shard_map/contract/pallas_call | solution.py:417
  76.9 1.6 %contract.5 = f32[144,128]{1,0:T(8,128)S(1)} custom-call(s32[2]{0:T(128)S(1)} %pad_add_fusion.2.owner_ref, f32[4608,128]{1,0:T(8,128)S(1)} %get-tuple-element.9.sigma_ref, f32[72,128]{1,0:T(8,128)S(1)} %copy-done.4, f32[8,128]{1,0:T(8,128)S(1)} %copy-done.15, bf16[2048,128]{1,0:T(8,128)(2,1)S(1)} %copy-done.2, ...), custom_call_target="tpu_custom_call" | custom-call | flops 82575360 | bytes 14155776 | tf_op jit(solution)/shard_map/contract/pallas_call | solution.py:417
  78.6 0.5 collective-permute-start.18
  79.0 0.3 collective-permute-start.16
  79.3 1.7 %collective-permute-start.17 = (f32[72,128]{1,0:T(8,128)S(1)}, f32[72,128]{1,0:T(8,128)S(1)}, u32[]{:S(2)}, u32[]{:S(2)}) collective-permute-start(f32[72,128]{1,0:T(8,128)S(1)} %get-tuple-element.26), channel_id=1, source_target_pairs={{0,8},{4,12},{8,0},{12,4},{16,24},{20,28},{24,16},{28,20},{1,9},{5... | collective-permute-start | bytes 110600 | tf_op jit(solution)/shard_map/ppermute | solution.py:474
  81.0 1.5 %collective-permute-start.15 = (f32[72,128]{1,0:T(8,128)S(1)}, f32[72,128]{1,0:T(8,128)S(1)}, u32[]{:S(2)}, u32[]{:S(2)}) collective-permute-start(f32[72,128]{1,0:T(8,128)S(1)} %get-tuple-element.27), channel_id=1, source_target_pairs={{0,24},{4,28},{8,16},{12,20},{16,8},{20,12},{24,0},{28,4},{1,25},{... | collective-permute-start | bytes 110600 | tf_op jit(solution)/shard_map/ppermute | solution.py:474
  82.5 0.5 collective-permute-done.16
  83.0 0.3 collective-permute-done.17
  83.3 2.6 %collective-permute-done.15 = f32[72,128]{1,0:T(8,128)S(1)} collective-permute-done((f32[72,128]{1,0:T(8,128)S(1)}, f32[72,128]{1,0:T(8,128)S(1)}, u32[]{:S(2)}, u32[]{:S(2)}) %collective-permute-start.15) | collective-permute-done | bytes 36896 | tf_op jit(solution)/shard_map/ppermute | solution.py:474
  85.9 1.6 %collective-permute-start.21 = (f32[72,128]{1,0:T(8,128)S(1)}, f32[72,128]{1,0:T(8,128)S(1)}, u32[]{:S(2)}, u32[]{:S(2)}) collective-permute-start(f32[72,128]{1,0:T(8,128)S(1)} %slice_add_fusion), channel_id=1, source_target_pairs={{0,1},{1,0},{2,3},{3,2},{4,5},{5,4},{6,7},{7,6},{8,9},{9,8},{10,11... | collective-permute-start | bytes 110600 | tf_op jit(solution)/shard_map/ppermute | solution.py:474
  87.5 2.6 %collective-permute-start.20 = (f32[72,128]{1,0:T(8,128)S(1)}, f32[72,128]{1,0:T(8,128)S(1)}, u32[]{:S(2)}, u32[]{:S(2)}) collective-permute-start(f32[72,128]{1,0:T(8,128)S(1)} %slice_add_fusion), channel_id=1, source_target_pairs={{0,2},{1,3},{2,0},{3,1},{4,6},{5,7},{6,4},{7,5},{8,10},{9,11},{10,... | collective-permute-start | bytes 110600 | tf_op jit(solution)/shard_map/ppermute | solution.py:474
  90.1 0.2 collective-permute-start.19
  90.3 2.8 %collective-permute-done.20 = f32[72,128]{1,0:T(8,128)S(1)} collective-permute-done((f32[72,128]{1,0:T(8,128)S(1)}, f32[72,128]{1,0:T(8,128)S(1)}, u32[]{:S(2)}, u32[]{:S(2)}) %collective-permute-start.20) | collective-permute-done | bytes 36896 | tf_op jit(solution)/shard_map/ppermute | solution.py:474
  93.1 2.7 %collective-permute-done.19 = f32[72,128]{1,0:T(8,128)S(1)} collective-permute-done((f32[72,128]{1,0:T(8,128)S(1)}, f32[72,128]{1,0:T(8,128)S(1)}, u32[]{:S(2)}, u32[]{:S(2)}) %collective-permute-start.19) | collective-permute-done | bytes 36896 | tf_op jit(solution)/shard_map/ppermute | solution.py:474
  95.9 5.3 %propagate.1 = f32[64,72,128]{2,1,0:T(8,128)} custom-call(f32[4,64,72,128]{3,2,1,0:T(8,128)S(1)} %roll_own.1._.greens_ref, f32[72,128]{1,0:T(8,128)S(1)} %add_add_fusion.effective_ref, bf16[256,2048]{1,0:T(8,128)(2,1)S(1)} %copy-done.3), custom_call_target="tpu_custom_call" | custom-call | flops 18874368 | bytes 11796480 | tf_op jit(solution)/shard_map/propagate/pallas_call | solution.py:448
  (56 shorter events, 0.6 us)
Async XLA Ops:
  0.0 5.9 %copy-start = (f32[64,72,128]{2,1,0:T(8,128)S(1)}, f32[64,72,128]{2,1,0:T(8,128)}, u32[]{:S(2)}) copy-start(f32[64,72,128]{2,1,0:T(8,128)} %green_ref.1) | copy-start | bytes 7077892
  2.8 25.7 %copy-start.17 = (s32[64]{0:T(128)S(1)}, s32[64]{0:T(128)}, u32[]{:S(2)}) copy-start(s32[64]{0:T(128)} %param.18) | copy-start | bytes 772
  2.8 25.7 %copy-start.18 = (f32[4]{0:T(128)S(1)}, f32[4]{0:T(128)}, u32[]{:S(2)}) copy-start(f32[4]{0:T(128)} %constant.44.clone) | copy-start | bytes 52
  2.8 6.1 %collective-permute-start.13 = (f32[576,128]{1,0:T(8,128)S(1)}, f32[576,128]{1,0:T(8,128)S(1)}, u32[]{:S(2)}, u32[]{:S(2)}) collective-permute-start(f32[576,128]{1,0:T(8,128)S(1)} %get-tuple-element.11), channel_id=1, source_target_pairs={{0,4},{4,0},{8,12},{12,8},{16,20},{20,16},{24,28},{28,24},{1,5},{5... | collective-permute-start | bytes 884744 | tf_op jit(solution)/shard_map/ppermute | solution.py:474
  3.3 10.0 %collective-permute-start.12 = (f32[576,128]{1,0:T(8,128)S(1)}, f32[576,128]{1,0:T(8,128)S(1)}, u32[]{:S(2)}, u32[]{:S(2)}) collective-permute-start(f32[576,128]{1,0:T(8,128)S(1)} %get-tuple-element.12), channel_id=1, source_target_pairs={{0,12},{4,8},{8,4},{12,0},{16,28},{20,24},{24,20},{28,16},{1,13},{... | collective-permute-start | bytes 884744 | tf_op jit(solution)/shard_map/ppermute | solution.py:474
  6.1 14.4 %collective-permute-start.6 = (f32[576,128]{1,0:T(8,128)S(1)}, f32[576,128]{1,0:T(8,128)S(1)}, u32[]{:S(2)}, u32[]{:S(2)}) collective-permute-start(f32[576,128]{1,0:T(8,128)S(1)} %get-tuple-element.18), channel_id=1, source_target_pairs={{0,28},{4,24},{8,20},{12,16},{16,12},{20,8},{24,4},{28,0},{1,29},{... | collective-permute-start | bytes 884744 | tf_op jit(solution)/shard_map/ppermute | solution.py:474
  7.3 20.6 %collective-permute-start.5 = (f32[576,128]{1,0:T(8,128)S(1)}, f32[576,128]{1,0:T(8,128)S(1)}, u32[]{:S(2)}, u32[]{:S(2)}) collective-permute-start(f32[576,128]{1,0:T(8,128)S(1)} %get-tuple-element.19), channel_id=1, source_target_pairs={{0,24},{4,28},{8,16},{12,20},{16,8},{20,12},{24,0},{28,4},{1,25},{... | collective-permute-start | bytes 884744 | tf_op jit(solution)/shard_map/ppermute | solution.py:474
  8.7 19.9 %collective-permute-start.4 = (f32[576,128]{1,0:T(8,128)S(1)}, f32[576,128]{1,0:T(8,128)S(1)}, u32[]{:S(2)}, u32[]{:S(2)}) collective-permute-start(f32[576,128]{1,0:T(8,128)S(1)} %get-tuple-element.20), channel_id=1, source_target_pairs={{0,4},{4,0},{8,12},{12,8},{16,20},{20,16},{24,28},{28,24},{1,5},{5... | collective-permute-start | bytes 884744 | tf_op jit(solution)/shard_map/ppermute | solution.py:474
  8.9 0.7 copy-start.11
  9.6 22.6 %collective-permute-start.3 = (f32[576,128]{1,0:T(8,128)S(1)}, f32[576,128]{1,0:T(8,128)S(1)}, u32[]{:S(2)}, u32[]{:S(2)}) collective-permute-start(f32[576,128]{1,0:T(8,128)S(1)} %get-tuple-element.21), channel_id=1, source_target_pairs={{0,12},{4,8},{8,4},{12,0},{16,28},{20,24},{24,20},{28,16},{1,13},{... | collective-permute-start | bytes 884744 | tf_op jit(solution)/shard_map/ppermute | solution.py:474
  13.2 0.7 copy-start.13
  14.0 19.6 %collective-permute-start.2 = (f32[576,128]{1,0:T(8,128)S(1)}, f32[576,128]{1,0:T(8,128)S(1)}, u32[]{:S(2)}, u32[]{:S(2)}) collective-permute-start(f32[576,128]{1,0:T(8,128)S(1)} %get-tuple-element.22), channel_id=1, source_target_pairs={{0,20},{4,16},{8,28},{12,24},{16,4},{20,0},{24,12},{28,8},{1,21},{... | collective-permute-start | bytes 884744 | tf_op jit(solution)/shard_map/ppermute | solution.py:474
  20.5 18.6 %collective-permute-start.1 = (f32[576,128]{1,0:T(8,128)S(1)}, f32[576,128]{1,0:T(8,128)S(1)}, u32[]{:S(2)}, u32[]{:S(2)}) collective-permute-start(f32[576,128]{1,0:T(8,128)S(1)} %get-tuple-element.23), channel_id=1, source_target_pairs={{0,8},{4,12},{8,0},{12,4},{16,24},{20,28},{24,16},{28,20},{1,9},{5... | collective-permute-start | bytes 884744 | tf_op jit(solution)/shard_map/ppermute | solution.py:474
  27.9 13.4 %collective-permute-start = (f32[576,128]{1,0:T(8,128)S(1)}, f32[576,128]{1,0:T(8,128)S(1)}, u32[]{:S(2)}, u32[]{:S(2)}) collective-permute-start(f32[576,128]{1,0:T(8,128)S(1)} %get-tuple-element.24), channel_id=1, source_target_pairs={{0,16},{4,20},{8,24},{12,28},{16,0},{20,4},{24,8},{28,12},{1,17},{... | collective-permute-start | bytes 884744 | tf_op jit(solution)/shard_map/ppermute | solution.py:474
  28.6 23.8 %collective-permute-start.11 = (f32[576,128]{1,0:T(8,128)}, f32[576,128]{1,0:T(8,128)}, u32[]{:S(2)}, u32[]{:S(2)}) collective-permute-start(f32[576,128]{1,0:T(8,128)} %get-tuple-element.13), channel_id=1, source_target_pairs={{0,20},{4,16},{8,28},{12,24},{16,4},{20,0},{24,12},{28,8},{1,21},{... | collective-permute-start | bytes 884744 | tf_op jit(solution)/shard_map/ppermute | solution.py:474
  32.3 20.2 %collective-permute-start.10 = (f32[576,128]{1,0:T(8,128)}, f32[576,128]{1,0:T(8,128)}, u32[]{:S(2)}, u32[]{:S(2)}) collective-permute-start(f32[576,128]{1,0:T(8,128)} %get-tuple-element.14), channel_id=1, source_target_pairs={{0,8},{4,12},{8,0},{12,4},{16,24},{20,28},{24,16},{28,20},{1,9},{5... | collective-permute-start | bytes 884744 | tf_op jit(solution)/shard_map/ppermute | solution.py:474
  33.6 0.7 copy-start.5
  34.3 31.0 %collective-permute-start.9 = (f32[576,128]{1,0:T(8,128)}, f32[576,128]{1,0:T(8,128)}, u32[]{:S(2)}, u32[]{:S(2)}) collective-permute-start(f32[576,128]{1,0:T(8,128)} %get-tuple-element.15), channel_id=1, source_target_pairs={{0,16},{4,20},{8,24},{12,28},{16,0},{20,4},{24,8},{28,12},{1,17},{... | collective-permute-start | bytes 884744 | tf_op jit(solution)/shard_map/ppermute | solution.py:474
  39.0 0.7 copy-start.7
  39.8 28.7 %collective-permute-start.8 = (f32[576,128]{1,0:T(8,128)}, f32[576,128]{1,0:T(8,128)}, u32[]{:S(2)}, u32[]{:S(2)}) collective-permute-start(f32[576,128]{1,0:T(8,128)} %get-tuple-element.16), channel_id=1, source_target_pairs={{0,28},{4,24},{8,20},{12,16},{16,12},{20,8},{24,4},{28,0},{1,29},{... | collective-permute-start | bytes 884744 | tf_op jit(solution)/shard_map/ppermute | solution.py:474
  41.3 0.7 copy-start.9
  42.0 26.5 %collective-permute-start.7 = (f32[576,128]{1,0:T(8,128)}, f32[576,128]{1,0:T(8,128)}, u32[]{:S(2)}, u32[]{:S(2)}) collective-permute-start(f32[576,128]{1,0:T(8,128)} %get-tuple-element.17), channel_id=1, source_target_pairs={{0,24},{4,28},{8,16},{12,20},{16,8},{20,12},{24,0},{28,4},{1,25},{... | collective-permute-start | bytes 884744 | tf_op jit(solution)/shard_map/ppermute | solution.py:474
  43.5 3.1 %copy-start.6 = (f32[576,128]{1,0:T(8,128)S(1)}, f32[576,128]{1,0:T(8,128)}, u32[]{:S(2)}) copy-start(f32[576,128]{1,0:T(8,128)} %copy-done.5) | copy-start | bytes 884740
  43.5 3.1 %copy-start.8 = (f32[576,128]{1,0:T(8,128)S(1)}, f32[576,128]{1,0:T(8,128)}, u32[]{:S(2)}) copy-start(f32[576,128]{1,0:T(8,128)} %copy-done.7) | copy-start | bytes 884740
  43.5 3.1 %copy-start.10 = (f32[576,128]{1,0:T(8,128)S(1)}, f32[576,128]{1,0:T(8,128)}, u32[]{:S(2)}) copy-start(f32[576,128]{1,0:T(8,128)} %copy-done.9) | copy-start | bytes 884740
  46.5 18.9 %copy-start.1 = (f32[64,72,128]{2,1,0:T(8,128)S(1)}, f32[64,72,128]{2,1,0:T(8,128)}, u32[]{:S(2)}) copy-start(f32[64,72,128]{2,1,0:T(8,128)} %param.15) | copy-start | bytes 7077892
  46.5 18.9 %copy-start.12 = (f32[576,128]{1,0:T(8,128)S(1)}, f32[576,128]{1,0:T(8,128)}, u32[]{:S(2)}) copy-start(f32[576,128]{1,0:T(8,128)} %copy-done.11) | copy-start | bytes 884740
  46.5 18.9 %copy-start.14 = (f32[576,128]{1,0:T(8,128)S(1)}, f32[576,128]{1,0:T(8,128)}, u32[]{:S(2)}) copy-start(f32[576,128]{1,0:T(8,128)} %copy-done.13) | copy-start | bytes 884740
  68.4 3.9 %copy-start.2 = (bf16[2048,128]{1,0:T(8,128)(2,1)S(1)}, bf16[2048,128]{1,0:T(8,128)(2,1)}, u32[]{:S(2)}) copy-start(bf16[2048,128]{1,0:T(8,128)(2,1)} %constant.46.clone.gather_ref) | copy-start | bytes 1572868
  68.5 3.9 %copy-start.4 = (f32[72,128]{1,0:T(8,128)S(1)}, f32[72,128]{1,0:T(8,128)}, u32[]{:S(2)}) copy-start(f32[72,128]{1,0:T(8,128)} %equal_ref.5) | copy-start | bytes 110596
  68.5 3.9 %copy-start.15 = (f32[8,128]{1,0:T(8,128)S(1)}, f32[8,128]{1,0:T(8,128)}, u32[]{:S(2)}) copy-start(f32[8,128]{1,0:T(8,128)} %constant.45.clone.sign_ref) | copy-start | bytes 12292
  74.5 2.4 %collective-permute-start.14 = (f32[216,128]{1,0:T(8,128)S(1)}, f32[216,128]{1,0:T(8,128)S(1)}, u32[]{:S(2)}, u32[]{:S(2)}) collective-permute-start(f32[216,128]{1,0:T(8,128)S(1)} %contract.4), channel_id=1, source_target_pairs={{0,4},{4,0},{8,12},{12,8},{16,20},{20,16},{24,28},{28,24},{1,5},{5... | collective-permute-start | bytes 331784 | tf_op jit(solution)/shard_map/ppermute | solution.py:474
  76.9 19.0 %copy-start.16 = (f32[72,128]{1,0:T(8,128)S(1)}, f32[72,128]{1,0:T(8,128)}, u32[]{:S(2)}) copy-start(f32[72,128]{1,0:T(8,128)} %param.16) | copy-start | bytes 110596
  76.9 19.0 %copy-start.3 = (bf16[256,2048]{1,0:T(8,128)(2,1)S(1)}, bf16[256,2048]{1,0:T(8,128)(2,1)}, u32[]{:S(2)}) copy-start(bf16[256,2048]{1,0:T(8,128)(2,1)} %constant.47.clone.spread_ref) | copy-start | bytes 3145732
  78.6 4.0 %collective-permute-start.18 = (f32[72,128]{1,0:T(8,128)S(1)}, f32[72,128]{1,0:T(8,128)S(1)}, u32[]{:S(2)}, u32[]{:S(2)}) collective-permute-start(f32[72,128]{1,0:T(8,128)S(1)} %slice.23), channel_id=1, source_target_pairs={{0,4},{4,0},{8,12},{12,8},{16,20},{20,16},{24,28},{28,24},{1,5},{5... | collective-permute-start | bytes 110600 | tf_op jit(solution)/shard_map/ppermute | solution.py:474
  79.0 4.0 %collective-permute-start.16 = (f32[72,128]{1,0:T(8,128)S(1)}, f32[72,128]{1,0:T(8,128)S(1)}, u32[]{:S(2)}, u32[]{:S(2)}) collective-permute-start(f32[72,128]{1,0:T(8,128)S(1)} %get-tuple-element.25), channel_id=1, source_target_pairs={{0,16},{4,20},{8,24},{12,28},{16,0},{20,4},{24,8},{28,12},{1,17},{... | collective-permute-start | bytes 110600 | tf_op jit(solution)/shard_map/ppermute | solution.py:474
  79.3 4.0 %collective-permute-start.17 = (f32[72,128]{1,0:T(8,128)S(1)}, f32[72,128]{1,0:T(8,128)S(1)}, u32[]{:S(2)}, u32[]{:S(2)}) collective-permute-start(f32[72,128]{1,0:T(8,128)S(1)} %get-tuple-element.26), channel_id=1, source_target_pairs={{0,8},{4,12},{8,0},{12,4},{16,24},{20,28},{24,16},{28,20},{1,9},{5... | collective-permute-start | bytes 110600 | tf_op jit(solution)/shard_map/ppermute | solution.py:474
  81.0 4.9 %collective-permute-start.15 = (f32[72,128]{1,0:T(8,128)S(1)}, f32[72,128]{1,0:T(8,128)S(1)}, u32[]{:S(2)}, u32[]{:S(2)}) collective-permute-start(f32[72,128]{1,0:T(8,128)S(1)} %get-tuple-element.27), channel_id=1, source_target_pairs={{0,24},{4,28},{8,16},{12,20},{16,8},{20,12},{24,0},{28,4},{1,25},{... | collective-permute-start | bytes 110600 | tf_op jit(solution)/shard_map/ppermute | solution.py:474
  85.9 4.5 %collective-permute-start.21 = (f32[72,128]{1,0:T(8,128)S(1)}, f32[72,128]{1,0:T(8,128)S(1)}, u32[]{:S(2)}, u32[]{:S(2)}) collective-permute-start(f32[72,128]{1,0:T(8,128)S(1)} %slice_add_fusion), channel_id=1, source_target_pairs={{0,1},{1,0},{2,3},{3,2},{4,5},{5,4},{6,7},{7,6},{8,9},{9,8},{10,11... | collective-permute-start | bytes 110600 | tf_op jit(solution)/shard_map/ppermute | solution.py:474
  87.5 5.6 %collective-permute-start.20 = (f32[72,128]{1,0:T(8,128)S(1)}, f32[72,128]{1,0:T(8,128)S(1)}, u32[]{:S(2)}, u32[]{:S(2)}) collective-permute-start(f32[72,128]{1,0:T(8,128)S(1)} %slice_add_fusion), channel_id=1, source_target_pairs={{0,2},{1,3},{2,0},{3,1},{4,6},{5,7},{6,4},{7,5},{8,10},{9,11},{10,... | collective-permute-start | bytes 110600 | tf_op jit(solution)/shard_map/ppermute | solution.py:474
  90.1 5.8 %collective-permute-start.19 = (f32[72,128]{1,0:T(8,128)S(1)}, f32[72,128]{1,0:T(8,128)S(1)}, u32[]{:S(2)}, u32[]{:S(2)}) collective-permute-start(f32[72,128]{1,0:T(8,128)S(1)} %slice_add_fusion), channel_id=1, source_target_pairs={{0,3},{1,2},{2,1},{3,0},{4,7},{5,6},{6,5},{7,4},{8,11},{9,10},{10,... | collective-permute-start | bytes 110600 | tf_op jit(solution)/shard_map/ppermute | solution.py:474

commit v9 on v8

--- a/solution.py
+++ b/solution.py
@@ -21,6 +21,8 @@
 hubbard = 1.0
 quadrature = (0.375, 1.1666666, 0.9583333, 1.0)
 
+HANDED = 2
+LARGE = 1e30
 LATE = 2
 AHEAD = 3
 
@@ -113,8 +115,10 @@
     lax.fori_loop(0, SIDE // 2, columns, 0)
 
 
-def roll_kernel(green_ref, greens_ref):
-    batch = math.gcd(green_ref.shape[0], STEPS)
+def roll_kernel(place_ref, green_ref, whole_ref, greens_ref, block_ref, *, step, parts):
+    rows = block_ref.shape[0]
+    block_ref[...] = whole_ref[pl.ds(pl.multiple_of(partner_of(place_ref[0], step, parts) * rows, TILE), rows), :]
+    batch = math.gcd(green_ref.shape[0], 4)
 
     def rolls(n, carry):
         times = pl.ds(n * batch, batch)
@@ -183,8 +187,8 @@
         lax.fori_loop(0, lines, along_second, 0, unroll=lines <= 4)
 
 
-def early_kernel(steps, parts, place_ref, lattice_ref, weight_ref, _, *refs):
-    screen_refs, (work_ref, held_ref, sems) = refs[: len(steps)], refs[len(steps) :]
+def early_kernel(steps, parts, place_ref, lattice_ref, weight_ref, *refs):
+    screen_refs, (*_, work_ref, held_ref, sems) = refs[: len(steps)], refs[len(steps) :]
     product_lines(
         steps, parts, place_ref[0], lattice_ref, weight_ref[...], screen_refs, held_ref, sems, work_ref
     )
@@ -376,18 +380,22 @@
     )(place, *greens)
 
 
-def early_lines(place, lattice, weights, before, screens, steps, parts):
+def early_lines(place, lattice, weights, screens, steps, parts, work=None):
     points = SIDE * SIDE
+    inputs = (place, lattice, weights, *screens) + (() if work is None else (work,))
     return pl.pallas_call(
         functools.partial(early_kernel, steps, parts),
         out_shape=jax.ShapeDtypeStruct((points, TILE, WIDTH), jnp.float32),
-        in_specs=[in_smem(), in_vmem(), in_vmem(), anywhere()] + [anywhere()] * len(steps),
+        in_specs=[in_smem(), in_vmem(), in_vmem()]
+        + [anywhere()] * len(steps)
+        + [in_vmem()] * (work is not None),
         out_specs=in_vmem(),
+        input_output_aliases={} if work is None else {len(inputs) - 1: 0},
         scratch_shapes=held_blocks(len(steps), parts),
         compiler_params=params(4),
-        cost_estimate=cost(150, 3),
+        cost_estimate=cost(25 * len(steps), 3),
         name="early",
-    )(place, lattice, weights, before, *screens)
+    )(*inputs)
 
 
 def sigma_of(place, lattice, weights, screens, work, steps, parts):
@@ -429,16 +437,20 @@
     )(owners, sigma, equal_time, jnp.asarray(signs), jnp.asarray(gather), greens, *before)
 
 
-def roll_own(greens):
+def roll_own(place, greens, whole, step, parts):
+    rows = whole.shape[0] // parts
     return pl.pallas_call(
-        roll_kernel,
-        out_shape=jax.ShapeDtypeStruct((STEPS, *greens.shape), jnp.float32),
-        in_specs=[in_vmem()],
-        out_specs=in_vmem(),
+        functools.partial(roll_kernel, step=step, parts=parts),
+        out_shape=[
+            jax.ShapeDtypeStruct((STEPS, *greens.shape), jnp.float32),
+            jax.ShapeDtypeStruct((rows, whole.shape[1]), whole.dtype),
+        ],
+        in_specs=[in_smem(), in_vmem(), in_vmem()],
+        out_specs=[in_vmem()] * 2,
         compiler_params=params(4),
-        cost_estimate=cost(3, 5),
+        cost_estimate=cost(8, 9),
         name="roll_own",
-    )(greens)
+    )(place, greens, whole)
 
 
 def propagate(greens, effective):
@@ -484,6 +496,10 @@
     return order + along[0] + [step for steps in mixed for step in steps]
 
 
+def after(index, received):
+    return index + (received[0, 0] > LARGE).astype(jnp.int32)
+
+
 def class_weights(quad_class):
     table = jnp.array(quadrature, jnp.float32)
     match = quad_class[:, None] == jnp.arange(4, dtype=jnp.int32)[None, :]
@@ -507,13 +523,25 @@
         order = exchange_order(parts)
         moved = []
         wholes = [x.reshape(parts * TILE * local, width) for x in (green_row, screened)]
-        for whole in wholes:
-            found = {0: whole}
-            for step in order:
+        first, diagonal = order[: parts - 1 - LATE], order[parts - 1 - LATE :]
+
+        def send(whole, steps, found, received=None):
+            for step in steps:
                 start = partner_of(place, step, parts) * (TILE * local)
+                if received is not None:
+                    start = after(start, received)
                 block = lax.dynamic_slice_in_dim(whole, start, TILE * local)
+                if whole is wholes[1] and step == order[HANDED]:
+                    block = handed
                 found[step] = exchange(block, "ka", step, parts)
-            moved.append([found])
+
+        own_greens, handed = roll_own(seat, green_row, wholes[1], order[HANDED], parts)
+        found_green, found_screen = {0: wholes[0]}, {0: wholes[1]}
+        send(wholes[0], first, found_green)
+        send(wholes[0], diagonal, found_green)
+        send(wholes[1], first, found_screen, found_green[first[0]])
+        send(wholes[1], diagonal, found_screen, found_green[diagonal[-1]])
+        moved = [[found_green], [found_screen]]
         order = [0] + order
     else:
         groups, sources = -(-times // TILE), 1
@@ -526,21 +554,22 @@
             x = jnp.pad(x, ((0, padding), (0, 0), (0, 0))).reshape(groups, TILE * points, width)
             moved.append([{0: x[group]} for group in range(groups)])
         weights = jnp.pad(weights, (0, padding))
+        own_greens, _ = roll_own(seat, green_row, screened.reshape(-1, width), 0, 1)
     weights = jnp.broadcast_to(weights.reshape(groups, TILE, 1), (groups, TILE, width))
 
     early = order[: max(1, len(order) - LATE)]
     late = order[len(early) :]
-    own_greens = roll_own(green_row)
     share = hubbard / (points * blocks)
     sigmas = []
     for group in range(groups):
         green, screen = moved[0][group], moved[1][group]
         lattice, greens = forward(seat, [green[step] for step in order], order, sources)
-        work = early_lines(
-            seat, lattice, weights[group], own_greens, [screen[step] for step in early], early, sources
-        )
+        work = early_lines(seat, lattice, weights[group], [screen[step] for step in early], early, sources)
+        for step in late[:-1]:
+            work = early_lines(seat, lattice, weights[group], [screen[step]], [step], sources, work)
+        last = late[-1:]
         sigma = sigma_of(
-            seat, lattice, weights[group], [screen[step] for step in late], work, late, sources
+            seat, lattice, weights[group], [screen[step] for step in last], work, last, sources
         )
         sigmas.append((sigma, greens))
 
@@ -551,14 +580,13 @@
             owners = jnp.stack([partner_of(place, step, parts) for step in steps])
             return contract(owners, sigma, equal_time, greens, local, share, before)
 
-        others = exchange(blocks_of(list(range(3, parts, 2))), "ka", 1, parts)
-        others = blocks_of(list(range(2, parts, 2))) + others
+        others = exchange(blocks_of([*range(3, parts, 2), 1]), "ka", 1, parts)
+        far = blocks_of(list(range(2, parts, 2))) + others[:-local]
         pieces = [
-            exchange(others[(n - 1) * local : n * local], "ka", 2 * n, parts)
+            exchange(far[(n - 1) * local : n * local], "ka", 2 * n, parts)
             for n in range(parts // 2 - 1, 0, -1)
         ]
-        chip = blocks_of([1, 0], (others,))
-        pieces += [exchange(chip[:local], "ka", 1, parts), chip[local:]]
+        pieces += [blocks_of([0], pieces[:1]), others[-local:]]
         collision = tree_sum(pieces)
     else:
         whole = jnp.zeros((1,), jnp.int32)

time: 101 us -> 92.5 us (0.916)
  waiting for transfers between devices: 41.5 us -> 27.4 us
  local copies, waits for them, and re-layouts: 6.78 us -> 12.2 us
  Pallas kernels: 26.8 us -> 25.3 us
  between operations: 0.91 us -> 2.21 us
    ppermute x22 -> x21, waiting for transfers between devices: 41.5 us -> 27.4 us  [exchange(): return lax.ppermute(value, axis, pairs)]
    dynamic_slice x2, local copies, waits for them, and re-layouts: 2.95 us -> 5.62 us  [send(): block = lax.dynamic_slice_in_dim(whole, start, TILE * local)]
    unnamed x38 -> x28, local copies, waits for them, and re-layouts: 3.67 us -> 5.36 us
    pallas_call x1, Pallas kernels: 3.83 us -> 2.46 us  [sigma_of(): pl.pallas_call(functools.partial(sigma_kernel, steps, parts), out_shape=[...]
    slice x2 -> x3, local copies, waits for them, and re-layouts: 0.01 us -> 1.05 us  [the longest x2 1.04 us: after(): return index + (received[0, 0] > LARGE).astype(jnp.int32)]
    pallas_call x1 -> x2, Pallas kernels: 3.07 us -> 3.15 us  [early_lines(): pl.pallas_call(functools.partial(early_kernel, steps, parts), out_shape=j...]
    ppermute x22 -> x21, starting transfers between devices: 24.9 us -> 24.8 us  [exchange(): return lax.ppermute(value, axis, pairs)]
  transfers between devices with their start and end apart: 22 -> 21, of which waited for: 11 -> 8; matrix products, arithmetic and copies ran while one was open for 1% -> 5% of each run, Pallas kernels for 14% -> 16%
where the time goes in v9:
time: 92.5 us; the launch traced here: 92.3 us
  waiting for transfers between devices  27.4 us (30%)
  Pallas kernels  25.3 us (27%)
  starting transfers between devices  24.8 us (27%)
  local copies, waits for them, and re-layouts  12.2 us (13%)
  between operations  2.21 us (2%)
    ppermute x21, waiting for transfers between devices, exchange(): return lax.ppermute(value, axis, pairs)  27.4 us
    ppermute x21, starting transfers between devices, exchange(): return lax.ppermute(value, axis, pairs)  24.8 us
    pallas_call x1, Pallas kernels, forward(): pl.pallas_call(functools.partial(forward_kernel, steps, parts), out_shape...  5.62 us
    dynamic_slice x2, local copies, waits for them, and re-layouts, send(): block = lax.dynamic_slice_in_dim(whole, start, TILE * local)  5.62 us
    unnamed x28, local copies, waits for them, and re-layouts  5.36 us
    pallas_call x1, Pallas kernels, propagate(): pl.pallas_call(propagate_kernel, out_shape=jax.ShapeDtypeStruct(greens.sh...  5.33 us
    pallas_call x3, Pallas kernels, contract(): pl.pallas_call(functools.partial(contract_kernel, share), out_shape=jax.S...  5.28 us
    pallas_call x1, Pallas kernels, roll_own(): pl.pallas_call(functools.partial(roll_kernel, step=step, parts=parts), ou...  3.49 us
  transfers between devices with their start and end apart: 21, of which 8 were waited for; matrix products, arithmetic and copies ran while one was open for 5% of the time, Pallas kernels for 16%

profile of v9, /device:TPU:0, one launch (start us, length us, event | category | flops | bytes accessed | tf_op | source)
XLA Modules:
  0.0 92.3 jit_solution(105032659281378121)
XLA Ops:
  0.0 2.9 %constant_dynamic-slice_fusion.6 = (f32[576,128]{1,0:T(8,128)S(1)}, f32[576,128]{1,0:T(8,128)}, f32[576,128]{1,0:T(8,128)}, f32[576,128]{1,0:T(8,128)}, f32[576,...) fusion(f32[4608,128]{1,0:T(8,128)} %bitcast.14, s32[]{:T(128)S(6)} %select_n.56, s32[]{:T(128)S(6)} %select_n.55, ...), kind=kLoop, calls=%fused_computation.9 | loop fusion | bytes 4128796 | tf_op jit(solution)/shard_map/dynamic_slice | solution.py:533
  2.9 3.3 %collective-permute-start.6 = (f32[576,128]{1,0:T(8,128)S(1)}, f32[576,128]{1,0:T(8,128)S(1)}, u32[]{:S(2)}, u32[]{:S(2)}) collective-permute-start(f32[576,128]{1,0:T(8,128)S(1)} %get-tuple-element.21), channel_id=1, source_target_pairs={{0,28},{4,24},{8,20},{12,16},{16,12},{20,8},{24,4},{28,0},{1,29},{... | collective-permute-start | bytes 884744 | tf_op jit(solution)/shard_map/ppermute | solution.py:486
  6.2 0.5 collective-permute-start
  6.7 1.5 %collective-permute-start.5 = (f32[576,128]{1,0:T(8,128)}, f32[576,128]{1,0:T(8,128)S(1)}, u32[]{:S(2)}, u32[]{:S(2)}) collective-permute-start(f32[576,128]{1,0:T(8,128)} %get-tuple-element.22), channel_id=1, source_target_pairs={{0,24},{4,28},{8,16},{12,20},{16,8},{20,12},{24,0},{28,4},{1,25},{... | collective-permute-start | bytes 884744 | tf_op jit(solution)/shard_map/ppermute | solution.py:486
  8.2 0.1 collective-permute-start.4
  8.4 1.5 %collective-permute-start.3 = (f32[576,128]{1,0:T(8,128)}, f32[576,128]{1,0:T(8,128)}, u32[]{:S(2)}, u32[]{:S(2)}) collective-permute-start(f32[576,128]{1,0:T(8,128)} %get-tuple-element.24), channel_id=1, source_target_pairs={{0,12},{4,8},{8,4},{12,0},{16,28},{20,24},{24,20},{28,16},{1,13},{... | collective-permute-start | bytes 884744 | tf_op jit(solution)/shard_map/ppermute | solution.py:486
  9.8 1.7 %copy-done.1 = f32[64,72,128]{2,1,0:T(8,128)S(1)} copy-done((f32[64,72,128]{2,1,0:T(8,128)S(1)}, f32[64,72,128]{2,1,0:T(8,128)}, u32[]{:S(2)}) %copy-start.1) | copy-done | bytes 2359320
  11.5 3.5 %roll_own.1 = (f32[4,64,72,128]{3,2,1,0:T(8,128)S(1)}, f32[576,128]{1,0:T(8,128)}) custom-call(s32[1]{0:T(128)} %bitcast.place_ref.owner_ref, f32[64,72,128]{2,1,0:T(8,128)S(1)} %copy-done, f32[4608,128]{1,0:T(8,128)S(1)} %bitcast.17), custom_call_target="tpu_custom_call" | custom-call | flops 4718592 | bytes 21233664 | tf_op jit(solution)/shard_map/roll_own/pallas_call | solution.py:442
  15.0 3.6 %copy-done.3 = f32[4,64,72,128]{3,2,1,0:T(8,128)} copy-done((f32[4,64,72,128]{3,2,1,0:T(8,128)}, f32[4,64,72,128]{3,2,1,0:T(8,128)S(1)}, u32[]{:S(2)}) %copy-start.3) | copy-done | bytes 9437208
  18.6 0.3 collective-permute-start.2
  18.9 0.5 slice.32
  20.1 6.4 %collective-permute-done.refs_1_ = f32[576,128]{1,0:T(8,128)S(1)} collective-permute-done((f32[576,128]{1,0:T(8,128)}, f32[576,128]{1,0:T(8,128)S(1)}, u32[]{:S(2)}, u32[]{:S(2)}) %collective-permute-start) | collective-permute-done | bytes 294944 | tf_op jit(solution)/shard_map/ppermute | solution.py:486
  26.5 2.2 %collective-permute-start.1 = (f32[576,128]{1,0:T(8,128)}, f32[576,128]{1,0:T(8,128)}, u32[]{:S(2)}, u32[]{:S(2)}) collective-permute-start(f32[576,128]{1,0:T(8,128)} %get-tuple-element.26), channel_id=1, source_target_pairs={{0,8},{4,12},{8,0},{12,4},{16,24},{20,28},{24,16},{28,20},{1,9},{5... | collective-permute-start | bytes 884744 | tf_op jit(solution)/shard_map/ppermute | solution.py:486
  28.7 0.5 slice.33
  29.9 2.7 %constant_dynamic-slice_fusion = (f32[576,128]{1,0:T(8,128)}, f32[576,128]{1,0:T(8,128)}, f32[576,128]{1,0:T(8,128)}, f32[576,128]{1,0:T(8,128)}, f32[576,128]{1,0:T(8,128)}, /*index=5*/f32[576,128]{1,0:T(8,128)}) fusion(f32[4608,128]{1,0:T(8,128)} %bitcast.16, s32[]{:T(128)S(6)} %select_n.65, s32[]{:T(128)S(6)} %select_n.64, s32[]{:T(128)S(6)} %select_n.63, ...), kind=kLoop, calls=%fused_computation.3 | loop fusion | bytes 3538968 | tf_op jit(solution)/shard_map/dynamic_slice | solution.py:533
  32.6 0.0 collective-permute-start.11
  32.7 1.4 %collective-permute-start.13 = (f32[576,128]{1,0:T(8,128)}, f32[576,128]{1,0:T(8,128)}, u32[]{:S(2)}, u32[]{:S(2)}) collective-permute-start(f32[576,128]{1,0:T(8,128)} %get-tuple-element.15), channel_id=1, source_target_pairs={{0,4},{4,0},{8,12},{12,8},{16,20},{20,16},{24,28},{28,24},{1,5},{5... | collective-permute-start | bytes 884744 | tf_op jit(solution)/shard_map/ppermute | solution.py:486
  34.8 0.1 select_reduce_fusion
  34.9 0.4 collective-permute-start.12
  35.3 1.3 %collective-permute-start.10 = (f32[576,128]{1,0:T(8,128)}, f32[576,128]{1,0:T(8,128)S(1)}, u32[]{:S(2)}, u32[]{:S(2)}) collective-permute-start(f32[576,128]{1,0:T(8,128)} %get-tuple-element.17), channel_id=1, source_target_pairs={{0,8},{4,12},{8,0},{12,4},{16,24},{20,28},{24,16},{28,20},{1,9},{5... | collective-permute-start | bytes 884744 | tf_op jit(solution)/shard_map/ppermute | solution.py:486
  36.6 1.5 %collective-permute-start.9 = (f32[576,128]{1,0:T(8,128)}, f32[576,128]{1,0:T(8,128)S(1)}, u32[]{:S(2)}, u32[]{:S(2)}) collective-permute-start(f32[576,128]{1,0:T(8,128)} %get-tuple-element.18), channel_id=1, source_target_pairs={{0,16},{4,20},{8,24},{12,28},{16,0},{20,4},{24,8},{28,12},{1,17},{... | collective-permute-start | bytes 884744 | tf_op jit(solution)/shard_map/ppermute | solution.py:486
  38.0 4.2 %collective-permute-done.11.refs_3_ = f32[576,128]{1,0:T(8,128)} collective-permute-done((f32[576,128]{1,0:T(8,128)}, f32[576,128]{1,0:T(8,128)}, u32[]{:S(2)}, u32[]{:S(2)}) %collective-permute-start.11) | collective-permute-done | bytes 294944 | tf_op jit(solution)/shard_map/ppermute | solution.py:486
  42.2 1.6 %collective-permute-start.8 = (f32[576,128]{1,0:T(8,128)}, f32[576,128]{1,0:T(8,128)S(1)}, u32[]{:S(2)}, u32[]{:S(2)}) collective-permute-start(f32[576,128]{1,0:T(8,128)} %get-tuple-element.19), channel_id=1, source_target_pairs={{0,24},{4,28},{8,16},{12,20},{16,8},{20,12},{24,0},{28,4},{1,25},{... | collective-permute-start | bytes 884744 | tf_op jit(solution)/shard_map/ppermute | solution.py:486
  43.8 0.8 collective-permute-start.7
  44.6 0.1 dynamic_slice.49
  44.7 0.1 pad_add_fusion.1.owner_ref
  44.8 5.6 %forward.1 = (f32[576,8,128]{2,1,0:T(8,128)S(1)}, f32[4,4608,128]{2,1,0:T(8,128)S(1)}) custom-call(s32[1]{0:T(128)} %bitcast.place_ref.owner_ref, f32[4608,128]{1,0:T(8,128)S(1)} %bitcast.15, f32[576,128]{1,0:T(8,128)S(1)} %collective-permute-done.refs_1_, f32[576,128]{1,0:T(8,128)} %collective-permute-done.1.refs_2_, ...), custom_call_target="tpu_custom_call" | custom-call | flops 235929600 | bytes 14155776 | tf_op jit(solution)/shard_map/forward/pallas_call | solution.py:368
  50.4 0.6 collective-permute-done.10.refs_2_
  51.0 0.1 squeeze.5.weight_ref
  51.0 2.7 %early.2.refs_1_ = f32[576,8,128]{2,1,0:T(8,128)S(1)} custom-call(s32[1]{0:T(128)} %bitcast.place_ref.owner_ref, f32[576,8,128]{2,1,0:T(8,128)S(1)} %get-tuple-element.11.lattice_ref, f32[8,128]{1,0:T(8,128)S(1)} %squeeze.5.weight_ref, f32[4608,128]{1,0:T(8,128)S(1)} %bitcast.18, f32[576,128]{1,0:T(8,128)S(1)} %collective-permute-done.9.refs_1_, ...), custom_call_target="tpu_custom_call" | custom-call | flops 88473600 | bytes 7077888 | tf_op jit(solution)/shard_map/early/pallas_call | solution.py:386
  53.7 3.7 %collective-permute-done.8.refs_0_ = f32[576,128]{1,0:T(8,128)S(1)} collective-permute-done((f32[576,128]{1,0:T(8,128)}, f32[576,128]{1,0:T(8,128)S(1)}, u32[]{:S(2)}, u32[]{:S(2)}) %collective-permute-start.8) | collective-permute-done | bytes 294944 | tf_op jit(solution)/shard_map/ppermute | solution.py:486
  57.4 0.5 early.3.refs_1_
  57.9 0.0 copy-start.4
  57.9 5.4 %collective-permute-done.7.refs_0_ = f32[576,128]{1,0:T(8,128)S(1)} collective-permute-done((f32[576,128]{1,0:T(8,128)}, f32[576,128]{1,0:T(8,128)S(1)}, u32[]{:S(2)}, u32[]{:S(2)}) %collective-permute-start.7) | collective-permute-done | bytes 294944 | tf_op jit(solution)/shard_map/ppermute | solution.py:486
  63.3 2.5 %sigma.1 = (f32[576,8,128]{2,1,0:T(8,128)S(1)}, f32[4608,128]{1,0:T(8,128)S(1)}) custom-call(s32[1]{0:T(128)} %bitcast.place_ref.owner_ref, f32[576,8,128]{2,1,0:T(8,128)S(1)} %get-tuple-element.11.lattice_ref, f32[8,128]{1,0:T(8,128)S(1)} %squeeze.5.weight_ref, f32[576,128]{1,0:T(8,128)S(1)} %collective-permute-done.7.refs_0_, ...), custom_call_target="tpu_custom_call", output_to_operand_aliasing={{0}: (4, {})} | custom-call | flops 117964800 | bytes 14155776 | tf_op jit(solution)/shard_map/sigma/pallas_call | solution.py:404
  65.8 2.5 %contract.4 = f32[288,128]{1,0:T(8,128)S(1)} custom-call(s32[4]{0:T(128)S(1)} %pad_add_fusion.1.owner_ref, f32[4608,128]{1,0:T(8,128)S(1)} %get-tuple-element.13.sigma_ref, f32[72,128]{1,0:T(8,128)S(1)} %copy-done.6, f32[8,128]{1,0:T(8,128)S(1)} %copy-done.7, bf16[2048,128]{1,0:T(8,128)(2,1)S(1)} %copy-done.4, f32[4,4608,128]{2,1,0:T(8,128)S(1)} %get-tuple-element.14.greens_ref), custom_call_target="tpu_custom_call" | custom-call | flops 165150720 | bytes 14155776 | tf_op jit(solution)/shard_map/contract/pallas_call | solution.py:425
  68.4 0.2 collective-permute-start.14
  68.6 0.1 pad_add_fusion.owner_ref
  68.6 2.1 %contract.3 = f32[216,128]{1,0:T(8,128)S(1)} custom-call(s32[3]{0:T(128)S(1)} %pad_add_fusion.owner_ref, f32[4608,128]{1,0:T(8,128)S(1)} %get-tuple-element.13.sigma_ref, f32[72,128]{1,0:T(8,128)S(1)} %copy-done.6, f32[8,128]{1,0:T(8,128)S(1)} %copy-done.7, bf16[2048,128]{1,0:T(8,128)(2,1)S(1)} %copy-done.4, f32[4,4608,128]{2,1,0:T(8,128)S(1)} %get-tuple-element.14.greens_ref), custom_call_target="tpu_custom_call" | custom-call | flops 123863040 | bytes 14155776 | tf_op jit(solution)/shard_map/contract/pallas_call | solution.py:425
  70.8 1.6 %collective-permute-start.15 = (f32[72,128]{1,0:T(8,128)S(1)}, f32[72,128]{1,0:T(8,128)S(1)}, u32[]{:S(2)}, u32[]{:S(2)}) collective-permute-start(f32[72,128]{1,0:T(8,128)S(1)} %get-tuple-element.30), channel_id=1, source_target_pairs={{0,24},{4,28},{8,16},{12,20},{16,8},{20,12},{24,0},{28,4},{1,25},{... | collective-permute-start | bytes 110600 | tf_op jit(solution)/shard_map/ppermute | solution.py:486
  72.4 2.0 %collective-permute-start.17 = (f32[72,128]{1,0:T(8,128)S(1)}, f32[72,128]{1,0:T(8,128)S(1)}, u32[]{:S(2)}, u32[]{:S(2)}) collective-permute-start(f32[72,128]{1,0:T(8,128)S(1)} %get-tuple-element.29), channel_id=1, source_target_pairs={{0,8},{4,12},{8,0},{12,4},{16,24},{20,28},{24,16},{28,20},{1,9},{5... | collective-permute-start | bytes 110600 | tf_op jit(solution)/shard_map/ppermute | solution.py:486
  74.4 1.4 %collective-permute-done.15.refs_0_ = f32[72,128]{1,0:T(8,128)S(1)} collective-permute-done((f32[72,128]{1,0:T(8,128)S(1)}, f32[72,128]{1,0:T(8,128)S(1)}, u32[]{:S(2)}, u32[]{:S(2)}) %collective-permute-start.15) | collective-permute-done | bytes 36896 | tf_op jit(solution)/shard_map/ppermute | solution.py:486
  75.8 0.6 contract.5
  76.4 2.1 %collective-permute-start.20 = (f32[72,128]{1,0:T(8,128)S(1)}, f32[72,128]{1,0:T(8,128)S(1)}, u32[]{:S(2)}, u32[]{:S(2)}) collective-permute-start(f32[72,128]{1,0:T(8,128)S(1)} %slice_add_fusion.1), channel_id=1, source_target_pairs={{0,1},{1,0},{2,3},{3,2},{4,5},{5,4},{6,7},{7,6},{8,9},{9,8},{10,11... | collective-permute-start | bytes 110600 | tf_op jit(solution)/shard_map/ppermute | solution.py:486
  78.5 2.6 %collective-permute-start.19 = (f32[72,128]{1,0:T(8,128)S(1)}, f32[72,128]{1,0:T(8,128)S(1)}, u32[]{:S(2)}, u32[]{:S(2)}) collective-permute-start(f32[72,128]{1,0:T(8,128)S(1)} %slice_add_fusion.1), channel_id=1, source_target_pairs={{0,2},{1,3},{2,0},{3,1},{4,6},{5,7},{6,4},{7,5},{8,10},{9,11},{10,... | collective-permute-start | bytes 110600 | tf_op jit(solution)/shard_map/ppermute | solution.py:486
  81.1 2.6 %collective-permute-done.19 = f32[72,128]{1,0:T(8,128)S(1)} collective-permute-done((f32[72,128]{1,0:T(8,128)S(1)}, f32[72,128]{1,0:T(8,128)S(1)}, u32[]{:S(2)}, u32[]{:S(2)}) %collective-permute-start.19) | collective-permute-done | bytes 36896 | tf_op jit(solution)/shard_map/ppermute | solution.py:486
  83.7 3.1 %collective-permute-done.18 = f32[72,128]{1,0:T(8,128)S(1)} collective-permute-done((f32[72,128]{1,0:T(8,128)S(1)}, f32[72,128]{1,0:T(8,128)S(1)}, u32[]{:S(2)}, u32[]{:S(2)}) %collective-permute-start.18) | collective-permute-done | bytes 36896 | tf_op jit(solution)/shard_map/ppermute | solution.py:486
  86.9 5.3 %propagate.1 = f32[64,72,128]{2,1,0:T(8,128)} custom-call(f32[4,64,72,128]{3,2,1,0:T(8,128)S(1)} %bitcast.20, f32[72,128]{1,0:T(8,128)S(1)} %add_add_fusion.effective_ref, bf16[256,2048]{1,0:T(8,128)(2,1)S(1)} %copy-done.5), custom_call_target="tpu_custom_call" | custom-call | flops 18874368 | bytes 11796480 | tf_op jit(solution)/shard_map/propagate/pallas_call | solution.py:460
  (46 shorter events, 0.2 us)
Async XLA Ops:
  0.0 9.8 %copy-start = (f32[64,72,128]{2,1,0:T(8,128)S(1)}, f32[64,72,128]{2,1,0:T(8,128)}, u32[]{:S(2)}) copy-start(f32[64,72,128]{2,1,0:T(8,128)} %green_ref.1) | copy-start | bytes 7077892
  2.9 15.7 %collective-permute-start.6 = (f32[576,128]{1,0:T(8,128)S(1)}, f32[576,128]{1,0:T(8,128)S(1)}, u32[]{:S(2)}, u32[]{:S(2)}) collective-permute-start(f32[576,128]{1,0:T(8,128)S(1)} %get-tuple-element.21), channel_id=1, source_target_pairs={{0,28},{4,24},{8,20},{12,16},{16,12},{20,8},{24,4},{28,0},{1,29},{... | collective-permute-start | bytes 884744 | tf_op jit(solution)/shard_map/ppermute | solution.py:486
  6.2 20.2 %collective-permute-start = (f32[576,128]{1,0:T(8,128)}, f32[576,128]{1,0:T(8,128)S(1)}, u32[]{:S(2)}, u32[]{:S(2)}) collective-permute-start(f32[576,128]{1,0:T(8,128)} %get-tuple-element.27), channel_id=1, source_target_pairs={{0,16},{4,20},{8,24},{12,28},{16,0},{20,4},{24,8},{28,12},{1,17},{... | collective-permute-start | bytes 884744 | tf_op jit(solution)/shard_map/ppermute | solution.py:486
  6.7 25.9 %collective-permute-start.5 = (f32[576,128]{1,0:T(8,128)}, f32[576,128]{1,0:T(8,128)S(1)}, u32[]{:S(2)}, u32[]{:S(2)}) collective-permute-start(f32[576,128]{1,0:T(8,128)} %get-tuple-element.22), channel_id=1, source_target_pairs={{0,24},{4,28},{8,16},{12,20},{16,8},{20,12},{24,0},{28,4},{1,25},{... | collective-permute-start | bytes 884744 | tf_op jit(solution)/shard_map/ppermute | solution.py:486
  8.2 24.4 %collective-permute-start.4 = (f32[576,128]{1,0:T(8,128)}, f32[576,128]{1,0:T(8,128)S(1)}, u32[]{:S(2)}, u32[]{:S(2)}) collective-permute-start(f32[576,128]{1,0:T(8,128)} %get-tuple-element.23), channel_id=1, source_target_pairs={{0,4},{4,0},{8,12},{12,8},{16,20},{20,16},{24,28},{28,24},{1,5},{5... | collective-permute-start | bytes 884744 | tf_op jit(solution)/shard_map/ppermute | solution.py:486
  8.4 26.5 %collective-permute-start.3 = (f32[576,128]{1,0:T(8,128)}, f32[576,128]{1,0:T(8,128)}, u32[]{:S(2)}, u32[]{:S(2)}) collective-permute-start(f32[576,128]{1,0:T(8,128)} %get-tuple-element.24), channel_id=1, source_target_pairs={{0,12},{4,8},{8,4},{12,0},{16,28},{20,24},{24,20},{28,16},{1,13},{... | collective-permute-start | bytes 884744 | tf_op jit(solution)/shard_map/ppermute | solution.py:486
  9.8 1.7 %copy-start.1 = (f32[64,72,128]{2,1,0:T(8,128)S(1)}, f32[64,72,128]{2,1,0:T(8,128)}, u32[]{:S(2)}) copy-start(f32[64,72,128]{2,1,0:T(8,128)} %param.15) | copy-start | bytes 7077892
  15.0 3.6 %copy-start.3 = (f32[4,64,72,128]{3,2,1,0:T(8,128)}, f32[4,64,72,128]{3,2,1,0:T(8,128)S(1)}, u32[]{:S(2)}) copy-start(f32[4,64,72,128]{3,2,1,0:T(8,128)S(1)} %get-tuple-element.10.greens_ref) | copy-start | bytes 28311556
  18.6 16.1 %copy-start.9 = (s32[64]{0:T(128)S(1)}, s32[64]{0:T(128)}, u32[]{:S(2)}) copy-start(s32[64]{0:T(128)} %param.18) | copy-start | bytes 772
  18.6 16.1 %copy-start.10 = (f32[4]{0:T(128)S(1)}, f32[4]{0:T(128)}, u32[]{:S(2)}) copy-start(f32[4]{0:T(128)} %constant.48.clone) | copy-start | bytes 52
  18.6 16.6 %collective-permute-start.2 = (f32[576,128]{1,0:T(8,128)}, f32[576,128]{1,0:T(8,128)}, u32[]{:S(2)}, u32[]{:S(2)}) collective-permute-start(f32[576,128]{1,0:T(8,128)} %get-tuple-element.25), channel_id=1, source_target_pairs={{0,20},{4,16},{8,28},{12,24},{16,4},{20,0},{24,12},{28,8},{1,21},{... | collective-permute-start | bytes 884744 | tf_op jit(solution)/shard_map/ppermute | solution.py:486
  26.5 10.1 %collective-permute-start.1 = (f32[576,128]{1,0:T(8,128)}, f32[576,128]{1,0:T(8,128)}, u32[]{:S(2)}, u32[]{:S(2)}) collective-permute-start(f32[576,128]{1,0:T(8,128)} %get-tuple-element.26), channel_id=1, source_target_pairs={{0,8},{4,12},{8,0},{12,4},{16,24},{20,28},{24,16},{28,20},{1,9},{5... | collective-permute-start | bytes 884744 | tf_op jit(solution)/shard_map/ppermute | solution.py:486
  32.6 9.6 %collective-permute-start.11 = (f32[576,128]{1,0:T(8,128)}, f32[576,128]{1,0:T(8,128)}, u32[]{:S(2)}, u32[]{:S(2)}) collective-permute-start(f32[576,128]{1,0:T(8,128)} %get-tuple-element.12), channel_id=1, source_target_pairs={{0,20},{4,16},{8,28},{12,24},{16,4},{20,0},{24,12},{28,8},{1,21},{... | collective-permute-start | bytes 884744 | tf_op jit(solution)/shard_map/ppermute | solution.py:486
  32.7 11.1 %collective-permute-start.13 = (f32[576,128]{1,0:T(8,128)}, f32[576,128]{1,0:T(8,128)}, u32[]{:S(2)}, u32[]{:S(2)}) collective-permute-start(f32[576,128]{1,0:T(8,128)} %get-tuple-element.15), channel_id=1, source_target_pairs={{0,4},{4,0},{8,12},{12,8},{16,20},{20,16},{24,28},{28,24},{1,5},{5... | collective-permute-start | bytes 884744 | tf_op jit(solution)/shard_map/ppermute | solution.py:486
  34.8 16.3 %copy-start.2 = (f32[64,72,128]{2,1,0:T(8,128)S(1)}, f32[64,72,128]{2,1,0:T(8,128)}, u32[]{:S(2)}) copy-start(f32[64,72,128]{2,1,0:T(8,128)} %param.15) | copy-start | bytes 7077892
  34.9 15.5 %collective-permute-start.12 = (f32[576,128]{1,0:T(8,128)}, f32[576,128]{1,0:T(8,128)S(1)}, u32[]{:S(2)}, u32[]{:S(2)}) collective-permute-start(f32[576,128]{1,0:T(8,128)} %get-tuple-element.16), channel_id=1, source_target_pairs={{0,12},{4,8},{8,4},{12,0},{16,28},{20,24},{24,20},{28,16},{1,13},{... | collective-permute-start | bytes 884744 | tf_op jit(solution)/shard_map/ppermute | solution.py:486
  35.3 15.7 %collective-permute-start.10 = (f32[576,128]{1,0:T(8,128)}, f32[576,128]{1,0:T(8,128)S(1)}, u32[]{:S(2)}, u32[]{:S(2)}) collective-permute-start(f32[576,128]{1,0:T(8,128)} %get-tuple-element.17), channel_id=1, source_target_pairs={{0,8},{4,12},{8,0},{12,4},{16,24},{20,28},{24,16},{28,20},{1,9},{5... | collective-permute-start | bytes 884744 | tf_op jit(solution)/shard_map/ppermute | solution.py:486
  36.6 14.4 %collective-permute-start.9 = (f32[576,128]{1,0:T(8,128)}, f32[576,128]{1,0:T(8,128)S(1)}, u32[]{:S(2)}, u32[]{:S(2)}) collective-permute-start(f32[576,128]{1,0:T(8,128)} %get-tuple-element.18), channel_id=1, source_target_pairs={{0,16},{4,20},{8,24},{12,28},{16,0},{20,4},{24,8},{28,12},{1,17},{... | collective-permute-start | bytes 884744 | tf_op jit(solution)/shard_map/ppermute | solution.py:486
  42.2 15.2 %collective-permute-start.8 = (f32[576,128]{1,0:T(8,128)}, f32[576,128]{1,0:T(8,128)S(1)}, u32[]{:S(2)}, u32[]{:S(2)}) collective-permute-start(f32[576,128]{1,0:T(8,128)} %get-tuple-element.19), channel_id=1, source_target_pairs={{0,24},{4,28},{8,16},{12,20},{16,8},{20,12},{24,0},{28,4},{1,25},{... | collective-permute-start | bytes 884744 | tf_op jit(solution)/shard_map/ppermute | solution.py:486
  43.8 19.6 %collective-permute-start.7 = (f32[576,128]{1,0:T(8,128)}, f32[576,128]{1,0:T(8,128)S(1)}, u32[]{:S(2)}, u32[]{:S(2)}) collective-permute-start(f32[576,128]{1,0:T(8,128)} %get-tuple-element.20), channel_id=1, source_target_pairs={{0,28},{4,24},{8,20},{12,16},{16,12},{20,8},{24,4},{28,0},{1,29},{... | collective-permute-start | bytes 884744 | tf_op jit(solution)/shard_map/ppermute | solution.py:486
  57.9 8.0 %copy-start.4 = (bf16[2048,128]{1,0:T(8,128)(2,1)S(1)}, bf16[2048,128]{1,0:T(8,128)(2,1)}, u32[]{:S(2)}) copy-start(bf16[2048,128]{1,0:T(8,128)(2,1)} %constant.50.clone.gather_ref) | copy-start | bytes 1572868
  57.9 7.9 %copy-start.6 = (f32[72,128]{1,0:T(8,128)S(1)}, f32[72,128]{1,0:T(8,128)}, u32[]{:S(2)}) copy-start(f32[72,128]{1,0:T(8,128)} %equal_ref.5) | copy-start | bytes 110596
  57.9 7.9 %copy-start.7 = (f32[8,128]{1,0:T(8,128)S(1)}, f32[8,128]{1,0:T(8,128)}, u32[]{:S(2)}) copy-start(f32[8,128]{1,0:T(8,128)} %constant.49.clone.sign_ref) | copy-start | bytes 12292
  68.4 2.4 %collective-permute-start.14 = (f32[288,128]{1,0:T(8,128)S(1)}, f32[288,128]{1,0:T(8,128)S(1)}, u32[]{:S(2)}, u32[]{:S(2)}) collective-permute-start(f32[288,128]{1,0:T(8,128)S(1)} %contract.4), channel_id=1, source_target_pairs={{0,4},{4,0},{8,12},{12,8},{16,20},{20,16},{24,28},{28,24},{1,5},{5... | collective-permute-start | bytes 442376 | tf_op jit(solution)/shard_map/ppermute | solution.py:486
  68.6 18.2 %slice-start = ((s8[9437184]{0:T(1024)(128)(4,1)}), s8[4194304]{0:T(1024)(128)(4,1)S(1)}, s32[]{:S(2)}) async-start(s8[9437184]{0:T(1024)(128)(4,1)} %bitcast.19), calls=%async_computation | async-start | bytes 8388608
  68.6 18.2 %slice-start.1 = ((s8[9437184]{0:T(1024)(128)(4,1)}), s8[1048576]{0:T(1024)(128)(4,1)S(1)}, s32[]{:S(2)}) async-start(s8[9437184]{0:T(1024)(128)(4,1)} %bitcast.19), calls=%async_computation.1 | async-start | bytes 2097152
  70.8 5.0 %collective-permute-start.15 = (f32[72,128]{1,0:T(8,128)S(1)}, f32[72,128]{1,0:T(8,128)S(1)}, u32[]{:S(2)}, u32[]{:S(2)}) collective-permute-start(f32[72,128]{1,0:T(8,128)S(1)} %get-tuple-element.30), channel_id=1, source_target_pairs={{0,24},{4,28},{8,16},{12,20},{16,8},{20,12},{24,0},{28,4},{1,25},{... | collective-permute-start | bytes 110600 | tf_op jit(solution)/shard_map/ppermute | solution.py:486
  72.4 4.0 %collective-permute-start.16 = (f32[72,128]{1,0:T(8,128)S(1)}, f32[72,128]{1,0:T(8,128)S(1)}, u32[]{:S(2)}, u32[]{:S(2)}) collective-permute-start(f32[72,128]{1,0:T(8,128)S(1)} %get-tuple-element.28), channel_id=1, source_target_pairs={{0,16},{4,20},{8,24},{12,28},{16,0},{20,4},{24,8},{28,12},{1,17},{... | collective-permute-start | bytes 110600 | tf_op jit(solution)/shard_map/ppermute | solution.py:486
  72.4 14.5 %copy-start.8 = (f32[72,128]{1,0:T(8,128)S(1)}, f32[72,128]{1,0:T(8,128)}, u32[]{:S(2)}) copy-start(f32[72,128]{1,0:T(8,128)} %param.16) | copy-start | bytes 110596
  72.4 14.5 %slice-start.2 = ((s8[9437184]{0:T(1024)(128)(4,1)}), s8[4194304]{0:T(1024)(128)(4,1)S(1)}, s32[]{:S(2)}) async-start(s8[9437184]{0:T(1024)(128)(4,1)} %bitcast.19), calls=%async_computation.2 | async-start | bytes 8388608
  72.4 14.5 %copy-start.5 = (bf16[256,2048]{1,0:T(8,128)(2,1)S(1)}, bf16[256,2048]{1,0:T(8,128)(2,1)}, u32[]{:S(2)}) copy-start(bf16[256,2048]{1,0:T(8,128)(2,1)} %constant.51.clone.spread_ref) | copy-start | bytes 3145732
  72.4 4.0 %collective-permute-start.17 = (f32[72,128]{1,0:T(8,128)S(1)}, f32[72,128]{1,0:T(8,128)S(1)}, u32[]{:S(2)}, u32[]{:S(2)}) collective-permute-start(f32[72,128]{1,0:T(8,128)S(1)} %get-tuple-element.29), channel_id=1, source_target_pairs={{0,8},{4,12},{8,0},{12,4},{16,24},{20,28},{24,16},{28,20},{1,9},{5... | collective-permute-start | bytes 110600 | tf_op jit(solution)/shard_map/ppermute | solution.py:486
  76.4 4.7 %collective-permute-start.20 = (f32[72,128]{1,0:T(8,128)S(1)}, f32[72,128]{1,0:T(8,128)S(1)}, u32[]{:S(2)}, u32[]{:S(2)}) collective-permute-start(f32[72,128]{1,0:T(8,128)S(1)} %slice_add_fusion.1), channel_id=1, source_target_pairs={{0,1},{1,0},{2,3},{3,2},{4,5},{5,4},{6,7},{7,6},{8,9},{9,8},{10,11... | collective-permute-start | bytes 110600 | tf_op jit(solution)/shard_map/ppermute | solution.py:486
  78.5 5.2 %collective-permute-start.19 = (f32[72,128]{1,0:T(8,128)S(1)}, f32[72,128]{1,0:T(8,128)S(1)}, u32[]{:S(2)}, u32[]{:S(2)}) collective-permute-start(f32[72,128]{1,0:T(8,128)S(1)} %slice_add_fusion.1), channel_id=1, source_target_pairs={{0,2},{1,3},{2,0},{3,1},{4,6},{5,7},{6,4},{7,5},{8,10},{9,11},{10,... | collective-permute-start | bytes 110600 | tf_op jit(solution)/shard_map/ppermute | solution.py:486
  81.1 5.8 %collective-permute-start.18 = (f32[72,128]{1,0:T(8,128)S(1)}, f32[72,128]{1,0:T(8,128)S(1)}, u32[]{:S(2)}, u32[]{:S(2)}) collective-permute-start(f32[72,128]{1,0:T(8,128)S(1)} %slice_add_fusion.1), channel_id=1, source_target_pairs={{0,3},{1,2},{2,1},{3,0},{4,7},{5,6},{6,5},{7,4},{8,11},{9,10},{10,... | collective-permute-start | bytes 110600 | tf_op jit(solution)/shard_map/ppermute | solution.py:486

commit v10 on v8

--- a/solution.py
+++ b/solution.py
@@ -183,8 +183,8 @@
         lax.fori_loop(0, lines, along_second, 0, unroll=lines <= 4)
 
 
-def early_kernel(steps, parts, place_ref, lattice_ref, weight_ref, _, *refs):
-    screen_refs, (work_ref, held_ref, sems) = refs[: len(steps)], refs[len(steps) :]
+def early_kernel(steps, parts, place_ref, lattice_ref, weight_ref, *refs):
+    screen_refs, (*_, work_ref, held_ref, sems) = refs[: len(steps)], refs[len(steps) :]
     product_lines(
         steps, parts, place_ref[0], lattice_ref, weight_ref[...], screen_refs, held_ref, sems, work_ref
     )
@@ -376,18 +376,22 @@
     )(place, *greens)
 
 
-def early_lines(place, lattice, weights, before, screens, steps, parts):
+def early_lines(place, lattice, weights, screens, steps, parts, work=None):
     points = SIDE * SIDE
+    inputs = (place, lattice, weights, *screens) + (() if work is None else (work,))
     return pl.pallas_call(
         functools.partial(early_kernel, steps, parts),
         out_shape=jax.ShapeDtypeStruct((points, TILE, WIDTH), jnp.float32),
-        in_specs=[in_smem(), in_vmem(), in_vmem(), anywhere()] + [anywhere()] * len(steps),
+        in_specs=[in_smem(), in_vmem(), in_vmem()]
+        + [anywhere()] * len(steps)
+        + [in_vmem()] * (work is not None),
         out_specs=in_vmem(),
+        input_output_aliases={} if work is None else {len(inputs) - 1: 0},
         scratch_shapes=held_blocks(len(steps), parts),
         compiler_params=params(4),
-        cost_estimate=cost(150, 3),
+        cost_estimate=cost(25 * len(steps), 3),
         name="early",
-    )(place, lattice, weights, before, *screens)
+    )(*inputs)
 
 
 def sigma_of(place, lattice, weights, screens, work, steps, parts):
@@ -507,6 +511,7 @@
         order = exchange_order(parts)
         moved = []
         wholes = [x.reshape(parts * TILE * local, width) for x in (green_row, screened)]
+        moved = []
         for whole in wholes:
             found = {0: whole}
             for step in order:
@@ -535,12 +540,15 @@
     sigmas = []
     for group in range(groups):
         green, screen = moved[0][group], moved[1][group]
-        lattice, greens = forward(seat, [green[step] for step in order], order, sources)
-        work = early_lines(
-            seat, lattice, weights[group], own_greens, [screen[step] for step in early], early, sources
-        )
+        listed = order[::-1]
+        lattice, greens = forward(seat, [green[step] for step in listed], listed, sources)
+        listed = early[-2::-1] + early[-1:]
+        work = early_lines(seat, lattice, weights[group], [screen[step] for step in listed], listed, sources)
+        for step in late[:-1]:
+            work = early_lines(seat, lattice, weights[group], [screen[step]], [step], sources, work)
+        last = late[-1:]
         sigma = sigma_of(
-            seat, lattice, weights[group], [screen[step] for step in late], work, late, sources
+            seat, lattice, weights[group], [screen[step] for step in last], work, last, sources
         )
         sigmas.append((sigma, greens))
 
@@ -551,14 +559,13 @@
             owners = jnp.stack([partner_of(place, step, parts) for step in steps])
             return contract(owners, sigma, equal_time, greens, local, share, before)
 
-        others = exchange(blocks_of(list(range(3, parts, 2))), "ka", 1, parts)
-        others = blocks_of(list(range(2, parts, 2))) + others
+        others = exchange(blocks_of([*range(3, parts, 2), 1]), "ka", 1, parts)
+        far = blocks_of(list(range(2, parts, 2))) + others[:-local]
         pieces = [
-            exchange(others[(n - 1) * local : n * local], "ka", 2 * n, parts)
+            exchange(far[(n - 1) * local : n * local], "ka", 2 * n, parts)
             for n in range(parts // 2 - 1, 0, -1)
         ]
-        chip = blocks_of([1, 0], (others,))
-        pieces += [exchange(chip[:local], "ka", 1, parts), chip[local:]]
+        pieces += [blocks_of([0], pieces[:1]), others[-local:]]
         collision = tree_sum(pieces)
     else:
         whole = jnp.zeros((1,), jnp.int32)

time: 101 us -> 87.1 us (0.86)
  waiting for transfers between devices: 41.5 us -> 30.1 us
  local copies, waits for them, and re-layouts: 6.78 us -> 4.09 us
  Pallas kernels: 26.8 us -> 25.1 us
  starting transfers between devices: 24.9 us -> 26.5 us
    ppermute x22 -> x21, waiting for transfers between devices: 41.5 us -> 30.1 us  [exchange(): return lax.ppermute(value, axis, pairs)]
    unnamed x38 -> x20, local copies, waits for them, and re-layouts: 3.67 us -> 0.05 us
    ppermute x22 -> x21, starting transfers between devices: 24.9 us -> 26.5 us  [exchange(): return lax.ppermute(value, axis, pairs)]
    pallas_call x1, Pallas kernels: 3.83 us -> 2.46 us  [sigma_of(): pl.pallas_call(functools.partial(sigma_kernel, steps, parts), out_shape=[...]
    pallas_call x1 -> x2, Pallas kernels: 3.07 us -> 3.52 us  [early_lines(): pl.pallas_call(functools.partial(early_kernel, steps, parts), out_shape=j...]
  transfers between devices with their start and end apart: 22 -> 21, of which waited for: 11 -> 11; matrix products, arithmetic and copies ran while one was open for 1% -> 2% of each run, Pallas kernels for 14% -> 17%
where the time goes in v10:
time: 87.1 us; the launch traced here: 87 us
  waiting for transfers between devices  30.1 us (35%)
  starting transfers between devices  26.5 us (30%)
  Pallas kernels  25.1 us (29%)
  local copies, waits for them, and re-layouts  4.09 us (5%)
    ppermute x21, waiting for transfers between devices, exchange(): return lax.ppermute(value, axis, pairs)  30.1 us
    ppermute x21, starting transfers between devices, exchange(): return lax.ppermute(value, axis, pairs)  26.5 us
    pallas_call x1, Pallas kernels, forward(): pl.pallas_call(functools.partial(forward_kernel, steps, parts), out_shape...  5.62 us
    pallas_call x1, Pallas kernels, propagate(): pl.pallas_call(propagate_kernel, out_shape=jax.ShapeDtypeStruct(greens.sh...  5.33 us
    pallas_call x3, Pallas kernels, contract(): pl.pallas_call(functools.partial(contract_kernel, share), out_shape=jax.S...  5.27 us
    dynamic_slice x2, local copies, waits for them, and re-layouts, per_device(): block = lax.dynamic_slice_in_dim(whole, start, TILE * local)  3.88 us
    pallas_call x2, Pallas kernels, early_lines(): pl.pallas_call(functools.partial(early_kernel, steps, parts), out_shape=j...  3.52 us
    pallas_call x1, Pallas kernels, roll_own(): pl.pallas_call(roll_kernel, out_shape=jax.ShapeDtypeStruct((STEPS, *green...  2.92 us
  transfers between devices with their start and end apart: 21, of which 11 were waited for; matrix products, arithmetic and copies ran while one was open for 2% of the time, Pallas kernels for 17%

profile of v10, /device:TPU:0, one launch (start us, length us, event | category | flops | bytes accessed | tf_op | source)
XLA Modules:
  0.0 87.0 jit_solution(5653908441459687663)
XLA Ops:
  0.0 2.6 %constant_dynamic-slice_fusion.7 = (f32[576,128]{1,0:T(8,128)}, f32[576,128]{1,0:T(8,128)}, f32[576,128]{1,0:T(8,128)}, f32[576,128]{1,0:T(8,128)S(1)}, f32[576,...) fusion(f32[4608,128]{1,0:T(8,128)} %bitcast.12, s32[]{:T(128)S(6)} %select_n.45, s32[]{:T(128)S(6)} %select_n.44, ...), kind=kLoop, calls=%fused_computation.10 | loop fusion | bytes 4128796 | tf_op jit(solution)/shard_map/dynamic_slice | solution.py:519
  2.6 3.4 %collective-permute-start = (f32[576,128]{1,0:T(8,128)S(1)}, f32[576,128]{1,0:T(8,128)S(1)}, u32[]{:S(2)}, u32[]{:S(2)}) collective-permute-start(f32[576,128]{1,0:T(8,128)S(1)} %get-tuple-element.24), channel_id=1, source_target_pairs={{0,28},{4,24},{8,20},{12,16},{16,12},{20,8},{24,4},{28,0},{1,29},{... | collective-permute-start | bytes 884744 | tf_op jit(solution)/shard_map/ppermute | solution.py:478
  6.0 0.6 collective-permute-start.1
  6.6 0.0 collective-permute-start.2
  6.7 1.4 %collective-permute-start.3 = (f32[576,128]{1,0:T(8,128)S(1)}, f32[576,128]{1,0:T(8,128)S(1)}, u32[]{:S(2)}, u32[]{:S(2)}) collective-permute-start(f32[576,128]{1,0:T(8,128)S(1)} %get-tuple-element.21), channel_id=1, source_target_pairs={{0,12},{4,8},{8,4},{12,0},{16,28},{20,24},{24,20},{28,16},{1,13},{... | collective-permute-start | bytes 884744 | tf_op jit(solution)/shard_map/ppermute | solution.py:478
  8.1 1.6 %collective-permute-start.4 = (f32[576,128]{1,0:T(8,128)}, f32[576,128]{1,0:T(8,128)}, u32[]{:S(2)}, u32[]{:S(2)}) collective-permute-start(f32[576,128]{1,0:T(8,128)} %get-tuple-element.20), channel_id=1, source_target_pairs={{0,20},{4,16},{8,28},{12,24},{16,4},{20,0},{24,12},{28,8},{1,21},{... | collective-permute-start | bytes 884744 | tf_op jit(solution)/shard_map/ppermute | solution.py:478
  9.6 1.3 %constant_dynamic-slice_fusion = (f32[576,128]{1,0:T(8,128)}, f32[576,128]{1,0:T(8,128)}, f32[576,128]{1,0:T(8,128)}, f32[576,128]{1,0:T(8,128)}, f32[576,128]{1...) fusion(f32[4608,128]{1,0:T(8,128)S(1)} %bitcast.14, s32[]{:T(128)S(6)} %select_n.41, s32[]{:T(128)S(6)} %select_n.45, ...), kind=kLoop, calls=%fused_computation.3 | loop fusion | bytes 4128796 | tf_op jit(solution)/shard_map/dynamic_slice | solution.py:519
  10.9 2.5 %collective-permute-done.refs_0_ = f32[576,128]{1,0:T(8,128)S(1)} collective-permute-done((f32[576,128]{1,0:T(8,128)S(1)}, f32[576,128]{1,0:T(8,128)S(1)}, u32[]{:S(2)}, u32[]{:S(2)}) %collective-permute-start) | collective-permute-done | bytes 294944 | tf_op jit(solution)/shard_map/ppermute | solution.py:478
  13.4 2.5 %collective-permute-start.5 = (f32[576,128]{1,0:T(8,128)}, f32[576,128]{1,0:T(8,128)}, u32[]{:S(2)}, u32[]{:S(2)}) collective-permute-start(f32[576,128]{1,0:T(8,128)} %get-tuple-element.19), channel_id=1, source_target_pairs={{0,8},{4,12},{8,0},{12,4},{16,24},{20,28},{24,16},{28,20},{1,9},{5... | collective-permute-start | bytes 884744 | tf_op jit(solution)/shard_map/ppermute | solution.py:478
  15.9 4.9 %collective-permute-done.1.refs_1_ = f32[576,128]{1,0:T(8,128)S(1)} collective-permute-done((f32[576,128]{1,0:T(8,128)S(1)}, f32[576,128]{1,0:T(8,128)S(1)}, u32[]{:S(2)}, u32[]{:S(2)}) %collective-permute-start.1) | collective-permute-done | bytes 294944 | tf_op jit(solution)/shard_map/ppermute | solution.py:478
  20.8 1.5 %collective-permute-start.6 = (f32[576,128]{1,0:T(8,128)}, f32[576,128]{1,0:T(8,128)}, u32[]{:S(2)}, u32[]{:S(2)}) collective-permute-start(f32[576,128]{1,0:T(8,128)} %get-tuple-element.18), channel_id=1, source_target_pairs={{0,16},{4,20},{8,24},{12,28},{16,0},{20,4},{24,8},{28,12},{1,17},{... | collective-permute-start | bytes 884744 | tf_op jit(solution)/shard_map/ppermute | solution.py:478
  22.3 4.8 %collective-permute-done.3.refs_3_ = f32[576,128]{1,0:T(8,128)S(1)} collective-permute-done((f32[576,128]{1,0:T(8,128)S(1)}, f32[576,128]{1,0:T(8,128)S(1)}, u32[]{:S(2)}, u32[]{:S(2)}) %collective-permute-start.3) | collective-permute-done | bytes 294944 | tf_op jit(solution)/shard_map/ppermute | solution.py:478
  27.0 1.5 %collective-permute-start.11 = (f32[576,128]{1,0:T(8,128)}, f32[576,128]{1,0:T(8,128)}, u32[]{:S(2)}, u32[]{:S(2)}) collective-permute-start(f32[576,128]{1,0:T(8,128)} %get-tuple-element.13), channel_id=1, source_target_pairs={{0,8},{4,12},{8,0},{12,4},{16,24},{20,28},{24,16},{28,20},{1,9},{5... | collective-permute-start | bytes 884744 | tf_op jit(solution)/shard_map/ppermute | solution.py:478
  29.2 0.1 select_reduce_fusion
  29.3 0.6 collective-permute-start.12
  29.9 3.6 %collective-permute-done.5.refs_5_ = f32[576,128]{1,0:T(8,128)} collective-permute-done((f32[576,128]{1,0:T(8,128)}, f32[576,128]{1,0:T(8,128)}, u32[]{:S(2)}, u32[]{:S(2)}) %collective-permute-start.5) | collective-permute-done | bytes 294944 | tf_op jit(solution)/shard_map/ppermute | solution.py:478
  33.5 0.1 collective-permute-start.13
  33.6 1.5 %collective-permute-start.9 = (f32[576,128]{1,0:T(8,128)}, f32[576,128]{1,0:T(8,128)S(1)}, u32[]{:S(2)}, u32[]{:S(2)}) collective-permute-start(f32[576,128]{1,0:T(8,128)} %get-tuple-element.15), channel_id=1, source_target_pairs={{0,12},{4,8},{8,4},{12,0},{16,28},{20,24},{24,20},{28,16},{1,13},{... | collective-permute-start | bytes 884744 | tf_op jit(solution)/shard_map/ppermute | solution.py:478
  35.1 3.8 %collective-permute-done.10.refs_1_ = f32[576,128]{1,0:T(8,128)} collective-permute-done((f32[576,128]{1,0:T(8,128)}, f32[576,128]{1,0:T(8,128)}, u32[]{:S(2)}, u32[]{:S(2)}) %collective-permute-start.10) | collective-permute-done | bytes 294944 | tf_op jit(solution)/shard_map/ppermute | solution.py:478
  38.9 3.2 %collective-permute-start.8 = (f32[576,128]{1,0:T(8,128)}, f32[576,128]{1,0:T(8,128)S(1)}, u32[]{:S(2)}, u32[]{:S(2)}) collective-permute-start(f32[576,128]{1,0:T(8,128)} %get-tuple-element.16), channel_id=1, source_target_pairs={{0,24},{4,28},{8,16},{12,20},{16,8},{20,12},{24,0},{28,4},{1,25},{... | collective-permute-start | bytes 884744 | tf_op jit(solution)/shard_map/ppermute | solution.py:478
  42.1 0.1 dynamic_slice.52
  42.2 0.1 pad_add_fusion.1.owner_ref
  42.3 5.6 %forward.1 = (f32[576,8,128]{2,1,0:T(8,128)S(1)}, f32[4,4608,128]{2,1,0:T(8,128)S(1)}) custom-call(s32[1]{0:T(128)} %bitcast.3.place_ref.owner_ref, f32[576,128]{1,0:T(8,128)S(1)} %collective-permute-done.refs_0_, f32[576,128]{1,0:T(8,128)S(1)} %collective-permute-done.1.refs_1_, f32[576,128]{1,0:T(8,128)S(1)} %collective-permute-done.2.refs_2_, ...), custom_call_target="tpu_custom_call" | custom-call | flops 235929600 | bytes 14155776 | tf_op jit(solution)/shard_map/forward/pallas_call | solution.py:364
  47.9 0.1 squeeze.9.weight_ref
  48.0 3.1 %early.2.refs_1_ = f32[576,8,128]{2,1,0:T(8,128)S(1)} custom-call(s32[1]{0:T(128)} %bitcast.3.place_ref.owner_ref, f32[576,8,128]{2,1,0:T(8,128)S(1)} %get-tuple-element.8.lattice_ref, f32[8,128]{1,0:T(8,128)S(1)} %squeeze.9.weight_ref, f32[576,128]{1,0:T(8,128)S(1)} %collective-permute-done.9.refs_0_, f32[576,128]{1,0:T(8,128)} %collective-permute-done.10.refs_1_, ...), custom_call_target="tpu_custom_call" | custom-call | flops 88473600 | bytes 7077888 | tf_op jit(solution)/shard_map/early/pallas_call | solution.py:382
  51.1 1.3 %collective-permute-done.8.refs_0_ = f32[576,128]{1,0:T(8,128)S(1)} collective-permute-done((f32[576,128]{1,0:T(8,128)}, f32[576,128]{1,0:T(8,128)S(1)}, u32[]{:S(2)}, u32[]{:S(2)}) %collective-permute-start.8) | collective-permute-done | bytes 294944 | tf_op jit(solution)/shard_map/ppermute | solution.py:478
  52.4 0.5 early.3.refs_1_
  52.8 0.0 copy-start.3
  52.8 0.0 copy-start.6
  52.9 4.9 %collective-permute-done.7.refs_0_ = f32[576,128]{1,0:T(8,128)S(1)} collective-permute-done((f32[576,128]{1,0:T(8,128)}, f32[576,128]{1,0:T(8,128)S(1)}, u32[]{:S(2)}, u32[]{:S(2)}) %collective-permute-start.7) | collective-permute-done | bytes 294944 | tf_op jit(solution)/shard_map/ppermute | solution.py:478
  57.8 2.5 %sigma.1 = (f32[576,8,128]{2,1,0:T(8,128)S(1)}, f32[4608,128]{1,0:T(8,128)S(1)}) custom-call(s32[1]{0:T(128)} %bitcast.3.place_ref.owner_ref, f32[576,8,128]{2,1,0:T(8,128)S(1)} %get-tuple-element.8.lattice_ref, f32[8,128]{1,0:T(8,128)S(1)} %squeeze.9.weight_ref, f32[576,128]{1,0:T(8,128)S(1)} %collective-permute-done.7.refs_0_, ...), custom_call_target="tpu_custom_call", output_to_operand_aliasing={{0}: (4, {})} | custom-call | flops 117964800 | bytes 14155776 | tf_op jit(solution)/shard_map/sigma/pallas_call | solution.py:400
  60.3 2.5 %contract.4 = f32[288,128]{1,0:T(8,128)S(1)} custom-call(s32[4]{0:T(128)S(1)} %pad_add_fusion.1.owner_ref, f32[4608,128]{1,0:T(8,128)S(1)} %get-tuple-element.9.sigma_ref, f32[72,128]{1,0:T(8,128)S(1)} %copy-done.5, f32[8,128]{1,0:T(8,128)S(1)} %copy-done.6, bf16[2048,128]{1,0:T(8,128)(2,1)S(1)} %copy-done.3, f32[4,4608,128]{2,1,0:T(8,128)S(1)} %get-tuple-element.10.greens_ref), custom_call_target="tpu_custom_call" | custom-call | flops 165150720 | bytes 14155776 | tf_op jit(solution)/shard_map/contract/pallas_call | solution.py:421
  62.8 0.2 collective-permute-start.14
  63.0 0.1 pad_add_fusion.owner_ref
  63.0 2.1 %contract.3 = f32[216,128]{1,0:T(8,128)S(1)} custom-call(s32[3]{0:T(128)S(1)} %pad_add_fusion.owner_ref, f32[4608,128]{1,0:T(8,128)S(1)} %get-tuple-element.9.sigma_ref, f32[72,128]{1,0:T(8,128)S(1)} %copy-done.5, f32[8,128]{1,0:T(8,128)S(1)} %copy-done.6, bf16[2048,128]{1,0:T(8,128)(2,1)S(1)} %copy-done.3, f32[4,4608,128]{2,1,0:T(8,128)S(1)} %get-tuple-element.10.greens_ref), custom_call_target="tpu_custom_call" | custom-call | flops 123863040 | bytes 14155776 | tf_op jit(solution)/shard_map/contract/pallas_call | solution.py:421
  65.2 3.4 %collective-permute-start.15 = (f32[72,128]{1,0:T(8,128)S(1)}, f32[72,128]{1,0:T(8,128)S(1)}, u32[]{:S(2)}, u32[]{:S(2)}) collective-permute-start(f32[72,128]{1,0:T(8,128)S(1)} %get-tuple-element.27), channel_id=1, source_target_pairs={{0,24},{4,28},{8,16},{12,20},{16,8},{20,12},{24,0},{28,4},{1,25},{... | collective-permute-start | bytes 110600 | tf_op jit(solution)/shard_map/ppermute | solution.py:478
  68.5 0.5 collective-permute-start.16
  69.0 0.1 collective-permute-start.17
  69.2 1.4 %collective-permute-done.15.refs_0_ = f32[72,128]{1,0:T(8,128)S(1)} collective-permute-done((f32[72,128]{1,0:T(8,128)S(1)}, f32[72,128]{1,0:T(8,128)S(1)}, u32[]{:S(2)}, u32[]{:S(2)}) %collective-permute-start.15) | collective-permute-done | bytes 36896 | tf_op jit(solution)/shard_map/ppermute | solution.py:478
  70.6 0.6 contract.5
  71.2 1.3 %collective-permute-done.16 = f32[72,128]{1,0:T(8,128)S(1)} collective-permute-done((f32[72,128]{1,0:T(8,128)S(1)}, f32[72,128]{1,0:T(8,128)S(1)}, u32[]{:S(2)}, u32[]{:S(2)}) %collective-permute-start.16) | collective-permute-done | bytes 36896 | tf_op jit(solution)/shard_map/ppermute | solution.py:478
  72.5 0.5 collective-permute-done.17
  73.0 0.0 copy-start.4
  73.0 3.7 %collective-permute-start.18 = (f32[72,128]{1,0:T(8,128)S(1)}, f32[72,128]{1,0:T(8,128)S(1)}, u32[]{:S(2)}, u32[]{:S(2)}) collective-permute-start(f32[72,128]{1,0:T(8,128)S(1)} %slice_add_fusion.1), channel_id=1, source_target_pairs={{0,3},{1,2},{2,1},{3,0},{4,7},{5,6},{6,5},{7,4},{8,11},{9,10},{10,... | collective-permute-start | bytes 110600 | tf_op jit(solution)/shard_map/ppermute | solution.py:478
  76.7 0.8 collective-permute-start.20
  77.5 2.9 %roll_own.1.greens_ref = f32[4,64,72,128]{3,2,1,0:T(8,128)S(1)} custom-call(f32[64,72,128]{2,1,0:T(8,128)S(1)} %copy-done), custom_call_target="tpu_custom_call" | custom-call | flops 1769472 | bytes 11796480 | tf_op jit(solution)/shard_map/roll_own/pallas_call | solution.py:437
  80.4 1.2 %collective-permute-done.19 = f32[72,128]{1,0:T(8,128)S(1)} collective-permute-done((f32[72,128]{1,0:T(8,128)S(1)}, f32[72,128]{1,0:T(8,128)S(1)}, u32[]{:S(2)}, u32[]{:S(2)}) %collective-permute-start.19) | collective-permute-done | bytes 36896 | tf_op jit(solution)/shard_map/ppermute | solution.py:478
  81.6 5.3 %propagate.1 = f32[64,72,128]{2,1,0:T(8,128)} custom-call(f32[4,64,72,128]{3,2,1,0:T(8,128)S(1)} %roll_own.1.greens_ref, f32[72,128]{1,0:T(8,128)S(1)} %add_add_fusion.effective_ref, bf16[256,2048]{1,0:T(8,128)(2,1)S(1)} %copy-done.4), custom_call_target="tpu_custom_call" | custom-call | flops 18874368 | bytes 11796480 | tf_op jit(solution)/shard_map/propagate/pallas_call | solution.py:452
  (35 shorter events, 0.1 us)
Async XLA Ops:
  0.0 9.6 %copy-start.1 = (f32[64,72,128]{2,1,0:T(8,128)S(1)}, f32[64,72,128]{2,1,0:T(8,128)}, u32[]{:S(2)}) copy-start(f32[64,72,128]{2,1,0:T(8,128)} %param.15) | copy-start | bytes 7077892
  2.6 26.6 %copy-start.8 = (s32[64]{0:T(128)S(1)}, s32[64]{0:T(128)}, u32[]{:S(2)}) copy-start(s32[64]{0:T(128)} %param.18) | copy-start | bytes 772
  2.6 26.6 %copy-start.9 = (f32[4]{0:T(128)S(1)}, f32[4]{0:T(128)}, u32[]{:S(2)}) copy-start(f32[4]{0:T(128)} %constant.44.clone) | copy-start | bytes 52
  2.6 39.7 %copy-start = (f32[64,72,128]{2,1,0:T(8,128)S(1)}, f32[64,72,128]{2,1,0:T(8,128)}, u32[]{:S(2)}) copy-start(f32[64,72,128]{2,1,0:T(8,128)} %green_ref.1) | copy-start | bytes 7077892
  2.6 10.8 %collective-permute-start = (f32[576,128]{1,0:T(8,128)S(1)}, f32[576,128]{1,0:T(8,128)S(1)}, u32[]{:S(2)}, u32[]{:S(2)}) collective-permute-start(f32[576,128]{1,0:T(8,128)S(1)} %get-tuple-element.24), channel_id=1, source_target_pairs={{0,28},{4,24},{8,20},{12,16},{16,12},{20,8},{24,4},{28,0},{1,29},{... | collective-permute-start | bytes 884744 | tf_op jit(solution)/shard_map/ppermute | solution.py:478
  6.0 14.8 %collective-permute-start.1 = (f32[576,128]{1,0:T(8,128)S(1)}, f32[576,128]{1,0:T(8,128)S(1)}, u32[]{:S(2)}, u32[]{:S(2)}) collective-permute-start(f32[576,128]{1,0:T(8,128)S(1)} %get-tuple-element.23), channel_id=1, source_target_pairs={{0,24},{4,28},{8,16},{12,20},{16,8},{20,12},{24,0},{28,4},{1,25},{... | collective-permute-start | bytes 884744 | tf_op jit(solution)/shard_map/ppermute | solution.py:478
  6.6 15.6 %collective-permute-start.2 = (f32[576,128]{1,0:T(8,128)S(1)}, f32[576,128]{1,0:T(8,128)S(1)}, u32[]{:S(2)}, u32[]{:S(2)}) collective-permute-start(f32[576,128]{1,0:T(8,128)S(1)} %get-tuple-element.22), channel_id=1, source_target_pairs={{0,4},{4,0},{8,12},{12,8},{16,20},{20,16},{24,28},{28,24},{1,5},{5... | collective-permute-start | bytes 884744 | tf_op jit(solution)/shard_map/ppermute | solution.py:478
  6.7 20.4 %collective-permute-start.3 = (f32[576,128]{1,0:T(8,128)S(1)}, f32[576,128]{1,0:T(8,128)S(1)}, u32[]{:S(2)}, u32[]{:S(2)}) collective-permute-start(f32[576,128]{1,0:T(8,128)S(1)} %get-tuple-element.21), channel_id=1, source_target_pairs={{0,12},{4,8},{8,4},{12,0},{16,28},{20,24},{24,20},{28,16},{1,13},{... | collective-permute-start | bytes 884744 | tf_op jit(solution)/shard_map/ppermute | solution.py:478
  8.1 21.2 %collective-permute-start.4 = (f32[576,128]{1,0:T(8,128)}, f32[576,128]{1,0:T(8,128)}, u32[]{:S(2)}, u32[]{:S(2)}) collective-permute-start(f32[576,128]{1,0:T(8,128)} %get-tuple-element.20), channel_id=1, source_target_pairs={{0,20},{4,16},{8,28},{12,24},{16,4},{20,0},{24,12},{28,8},{1,21},{... | collective-permute-start | bytes 884744 | tf_op jit(solution)/shard_map/ppermute | solution.py:478
  13.4 20.1 %collective-permute-start.5 = (f32[576,128]{1,0:T(8,128)}, f32[576,128]{1,0:T(8,128)}, u32[]{:S(2)}, u32[]{:S(2)}) collective-permute-start(f32[576,128]{1,0:T(8,128)} %get-tuple-element.19), channel_id=1, source_target_pairs={{0,8},{4,12},{8,0},{12,4},{16,24},{20,28},{24,16},{28,20},{1,9},{5... | collective-permute-start | bytes 884744 | tf_op jit(solution)/shard_map/ppermute | solution.py:478
  20.8 12.8 %collective-permute-start.6 = (f32[576,128]{1,0:T(8,128)}, f32[576,128]{1,0:T(8,128)}, u32[]{:S(2)}, u32[]{:S(2)}) collective-permute-start(f32[576,128]{1,0:T(8,128)} %get-tuple-element.18), channel_id=1, source_target_pairs={{0,16},{4,20},{8,24},{12,28},{16,0},{20,4},{24,8},{28,12},{1,17},{... | collective-permute-start | bytes 884744 | tf_op jit(solution)/shard_map/ppermute | solution.py:478
  22.3 16.6 %collective-permute-start.10 = (f32[576,128]{1,0:T(8,128)}, f32[576,128]{1,0:T(8,128)}, u32[]{:S(2)}, u32[]{:S(2)}) collective-permute-start(f32[576,128]{1,0:T(8,128)} %get-tuple-element.14), channel_id=1, source_target_pairs={{0,20},{4,16},{8,28},{12,24},{16,4},{20,0},{24,12},{28,8},{1,21},{... | collective-permute-start | bytes 884744 | tf_op jit(solution)/shard_map/ppermute | solution.py:478
  27.0 15.1 %collective-permute-start.11 = (f32[576,128]{1,0:T(8,128)}, f32[576,128]{1,0:T(8,128)}, u32[]{:S(2)}, u32[]{:S(2)}) collective-permute-start(f32[576,128]{1,0:T(8,128)} %get-tuple-element.13), channel_id=1, source_target_pairs={{0,8},{4,12},{8,0},{12,4},{16,24},{20,28},{24,16},{28,20},{1,9},{5... | collective-permute-start | bytes 884744 | tf_op jit(solution)/shard_map/ppermute | solution.py:478
  29.2 18.8 %copy-start.2 = (f32[64,72,128]{2,1,0:T(8,128)S(1)}, f32[64,72,128]{2,1,0:T(8,128)}, u32[]{:S(2)}) copy-start(f32[64,72,128]{2,1,0:T(8,128)} %param.15) | copy-start | bytes 7077892
  29.3 18.6 %collective-permute-start.12 = (f32[576,128]{1,0:T(8,128)}, f32[576,128]{1,0:T(8,128)S(1)}, u32[]{:S(2)}, u32[]{:S(2)}) collective-permute-start(f32[576,128]{1,0:T(8,128)} %get-tuple-element.12), channel_id=1, source_target_pairs={{0,16},{4,20},{8,24},{12,28},{16,0},{20,4},{24,8},{28,12},{1,17},{... | collective-permute-start | bytes 884744 | tf_op jit(solution)/shard_map/ppermute | solution.py:478
  33.5 14.4 %collective-permute-start.13 = (f32[576,128]{1,0:T(8,128)}, f32[576,128]{1,0:T(8,128)S(1)}, u32[]{:S(2)}, u32[]{:S(2)}) collective-permute-start(f32[576,128]{1,0:T(8,128)} %get-tuple-element.11), channel_id=1, source_target_pairs={{0,4},{4,0},{8,12},{12,8},{16,20},{20,16},{24,28},{28,24},{1,5},{5... | collective-permute-start | bytes 884744 | tf_op jit(solution)/shard_map/ppermute | solution.py:478
  33.6 14.3 %collective-permute-start.9 = (f32[576,128]{1,0:T(8,128)}, f32[576,128]{1,0:T(8,128)S(1)}, u32[]{:S(2)}, u32[]{:S(2)}) collective-permute-start(f32[576,128]{1,0:T(8,128)} %get-tuple-element.15), channel_id=1, source_target_pairs={{0,12},{4,8},{8,4},{12,0},{16,28},{20,24},{24,20},{28,16},{1,13},{... | collective-permute-start | bytes 884744 | tf_op jit(solution)/shard_map/ppermute | solution.py:478
  38.9 13.5 %collective-permute-start.8 = (f32[576,128]{1,0:T(8,128)}, f32[576,128]{1,0:T(8,128)S(1)}, u32[]{:S(2)}, u32[]{:S(2)}) collective-permute-start(f32[576,128]{1,0:T(8,128)} %get-tuple-element.16), channel_id=1, source_target_pairs={{0,24},{4,28},{8,16},{12,20},{16,8},{20,12},{24,0},{28,4},{1,25},{... | collective-permute-start | bytes 884744 | tf_op jit(solution)/shard_map/ppermute | solution.py:478
  42.1 15.7 %collective-permute-start.7 = (f32[576,128]{1,0:T(8,128)}, f32[576,128]{1,0:T(8,128)S(1)}, u32[]{:S(2)}, u32[]{:S(2)}) collective-permute-start(f32[576,128]{1,0:T(8,128)} %get-tuple-element.17), channel_id=1, source_target_pairs={{0,28},{4,24},{8,20},{12,16},{16,12},{20,8},{24,4},{28,0},{1,29},{... | collective-permute-start | bytes 884744 | tf_op jit(solution)/shard_map/ppermute | solution.py:478
  52.8 7.4 %copy-start.3 = (bf16[2048,128]{1,0:T(8,128)(2,1)S(1)}, bf16[2048,128]{1,0:T(8,128)(2,1)}, u32[]{:S(2)}) copy-start(bf16[2048,128]{1,0:T(8,128)(2,1)} %constant.46.clone.gather_ref) | copy-start | bytes 1572868
  52.8 7.4 %copy-start.5 = (f32[72,128]{1,0:T(8,128)S(1)}, f32[72,128]{1,0:T(8,128)}, u32[]{:S(2)}) copy-start(f32[72,128]{1,0:T(8,128)} %equal_ref.5) | copy-start | bytes 110596
  52.8 7.4 %copy-start.6 = (f32[8,128]{1,0:T(8,128)S(1)}, f32[8,128]{1,0:T(8,128)}, u32[]{:S(2)}) copy-start(f32[8,128]{1,0:T(8,128)} %constant.45.clone.sign_ref) | copy-start | bytes 12292
  62.8 2.3 %collective-permute-start.14 = (f32[288,128]{1,0:T(8,128)S(1)}, f32[288,128]{1,0:T(8,128)S(1)}, u32[]{:S(2)}, u32[]{:S(2)}) collective-permute-start(f32[288,128]{1,0:T(8,128)S(1)} %contract.4), channel_id=1, source_target_pairs={{0,4},{4,0},{8,12},{12,8},{16,20},{20,16},{24,28},{28,24},{1,5},{5... | collective-permute-start | bytes 442376 | tf_op jit(solution)/shard_map/ppermute | solution.py:478
  65.2 5.4 %collective-permute-start.15 = (f32[72,128]{1,0:T(8,128)S(1)}, f32[72,128]{1,0:T(8,128)S(1)}, u32[]{:S(2)}, u32[]{:S(2)}) collective-permute-start(f32[72,128]{1,0:T(8,128)S(1)} %get-tuple-element.27), channel_id=1, source_target_pairs={{0,24},{4,28},{8,16},{12,20},{16,8},{20,12},{24,0},{28,4},{1,25},{... | collective-permute-start | bytes 110600 | tf_op jit(solution)/shard_map/ppermute | solution.py:478
  68.5 4.0 %collective-permute-start.16 = (f32[72,128]{1,0:T(8,128)S(1)}, f32[72,128]{1,0:T(8,128)S(1)}, u32[]{:S(2)}, u32[]{:S(2)}) collective-permute-start(f32[72,128]{1,0:T(8,128)S(1)} %get-tuple-element.25), channel_id=1, source_target_pairs={{0,16},{4,20},{8,24},{12,28},{16,0},{20,4},{24,8},{28,12},{1,17},{... | collective-permute-start | bytes 110600 | tf_op jit(solution)/shard_map/ppermute | solution.py:478
  69.0 4.0 %collective-permute-start.17 = (f32[72,128]{1,0:T(8,128)S(1)}, f32[72,128]{1,0:T(8,128)S(1)}, u32[]{:S(2)}, u32[]{:S(2)}) collective-permute-start(f32[72,128]{1,0:T(8,128)S(1)} %get-tuple-element.26), channel_id=1, source_target_pairs={{0,8},{4,12},{8,0},{12,4},{16,24},{20,28},{24,16},{28,20},{1,9},{5... | collective-permute-start | bytes 110600 | tf_op jit(solution)/shard_map/ppermute | solution.py:478
  73.0 8.6 %copy-start.7 = (f32[72,128]{1,0:T(8,128)S(1)}, f32[72,128]{1,0:T(8,128)}, u32[]{:S(2)}) copy-start(f32[72,128]{1,0:T(8,128)} %param.16) | copy-start | bytes 110596
  73.0 8.6 %copy-start.4 = (bf16[256,2048]{1,0:T(8,128)(2,1)S(1)}, bf16[256,2048]{1,0:T(8,128)(2,1)}, u32[]{:S(2)}) copy-start(bf16[256,2048]{1,0:T(8,128)(2,1)} %constant.47.clone.spread_ref) | copy-start | bytes 3145732
  73.0 7.4 %collective-permute-start.18 = (f32[72,128]{1,0:T(8,128)S(1)}, f32[72,128]{1,0:T(8,128)S(1)}, u32[]{:S(2)}, u32[]{:S(2)}) collective-permute-start(f32[72,128]{1,0:T(8,128)S(1)} %slice_add_fusion.1), channel_id=1, source_target_pairs={{0,3},{1,2},{2,1},{3,0},{4,7},{5,6},{6,5},{7,4},{8,11},{9,10},{10,... | collective-permute-start | bytes 110600 | tf_op jit(solution)/shard_map/ppermute | solution.py:478
  76.7 4.9 %collective-permute-start.19 = (f32[72,128]{1,0:T(8,128)S(1)}, f32[72,128]{1,0:T(8,128)S(1)}, u32[]{:S(2)}, u32[]{:S(2)}) collective-permute-start(f32[72,128]{1,0:T(8,128)S(1)} %slice_add_fusion.1), channel_id=1, source_target_pairs={{0,2},{1,3},{2,0},{3,1},{4,6},{5,7},{6,4},{7,5},{8,10},{9,11},{10,... | collective-permute-start | bytes 110600 | tf_op jit(solution)/shard_map/ppermute | solution.py:478
  76.7 4.9 %collective-permute-start.20 = (f32[72,128]{1,0:T(8,128)S(1)}, f32[72,128]{1,0:T(8,128)S(1)}, u32[]{:S(2)}, u32[]{:S(2)}) collective-permute-start(f32[72,128]{1,0:T(8,128)S(1)} %slice_add_fusion.1), channel_id=1, source_target_pairs={{0,1},{1,0},{2,3},{3,2},{4,5},{5,4},{6,7},{7,6},{8,9},{9,8},{10,11... | collective-permute-start | bytes 110600 | tf_op jit(solution)/shard_map/ppermute | solution.py:478

commit v11 on v10

--- a/solution.py
+++ b/solution.py
@@ -540,9 +540,9 @@
     sigmas = []
     for group in range(groups):
         green, screen = moved[0][group], moved[1][group]
-        listed = order[::-1]
+        listed = order
         lattice, greens = forward(seat, [green[step] for step in listed], listed, sources)
-        listed = early[-2::-1] + early[-1:]
+        listed = early[-1:] + early[:-1]
         work = early_lines(seat, lattice, weights[group], [screen[step] for step in listed], listed, sources)
         for step in late[:-1]:
             work = early_lines(seat, lattice, weights[group], [screen[step]], [step], sources, work)

time: 87.1 us -> 86.5 us (level)
  starting transfers between devices: 26.5 us -> 22.9 us
  waiting for transfers between devices: 30.1 us -> 33.4 us
    ppermute x21, starting transfers between devices: 26.5 us -> 22.9 us  [exchange(): return lax.ppermute(value, axis, pairs)]
    ppermute x21, waiting for transfers between devices: 30.1 us -> 33.4 us  [exchange(): return lax.ppermute(value, axis, pairs)]
  transfers between devices with their start and end apart: 21 -> 21, of which waited for: 11 -> 12; matrix products, arithmetic and copies ran while one was open for 2% -> 2% of each run, Pallas kernels for 17% -> 17%
where the time goes in v11:
time: 86.5 us; the launch traced here: 86.4 us
  waiting for transfers between devices  33.4 us (39%)
  Pallas kernels  24.8 us (29%)
  starting transfers between devices  22.9 us (26%)
  local copies, waits for them, and re-layouts  4.09 us (5%)
  between operations  0.87 us (1%)
    ppermute x21, waiting for transfers between devices, exchange(): return lax.ppermute(value, axis, pairs)  33.4 us
    ppermute x21, starting transfers between devices, exchange(): return lax.ppermute(value, axis, pairs)  22.9 us
    pallas_call x1, Pallas kernels, forward(): pl.pallas_call(functools.partial(forward_kernel, steps, parts), out_shape...  5.62 us
    pallas_call x1, Pallas kernels, propagate(): pl.pallas_call(propagate_kernel, out_shape=jax.ShapeDtypeStruct(greens.sh...  5.33 us
    pallas_call x3, Pallas kernels, contract(): pl.pallas_call(functools.partial(contract_kernel, share), out_shape=jax.S...  5.27 us
    dynamic_slice x2, local copies, waits for them, and re-layouts, per_device(): block = lax.dynamic_slice_in_dim(whole, start, TILE * local)  3.88 us
    pallas_call x2, Pallas kernels, early_lines(): pl.pallas_call(functools.partial(early_kernel, steps, parts), out_shape=j...  3.19 us
    pallas_call x1, Pallas kernels, roll_own(): pl.pallas_call(roll_kernel, out_shape=jax.ShapeDtypeStruct((STEPS, *green...  2.92 us
  transfers between devices with their start and end apart: 21, of which 12 were waited for; matrix products, arithmetic and copies ran while one was open for 2% of the time, Pallas kernels for 17%

profile of v11, /device:TPU:0, one launch (start us, length us, event | category | flops | bytes accessed | tf_op | source)
XLA Modules:
  0.0 86.4 jit_solution(16611677427172204132)
XLA Ops:
  0.0 2.6 %constant_dynamic-slice_fusion.7 = (f32[576,128]{1,0:T(8,128)}, f32[576,128]{1,0:T(8,128)}, f32[576,128]{1,0:T(8,128)}, f32[576,128]{1,0:T(8,128)S(1)}, f32[576,...) fusion(f32[4608,128]{1,0:T(8,128)} %bitcast.12, s32[]{:T(128)S(6)} %select_n.45, s32[]{:T(128)S(6)} %select_n.44, ...), kind=kLoop, calls=%fused_computation.10 | loop fusion | bytes 4128796 | tf_op jit(solution)/shard_map/dynamic_slice | solution.py:519
  2.6 3.0 %collective-permute-start = (f32[576,128]{1,0:T(8,128)S(1)}, f32[576,128]{1,0:T(8,128)S(1)}, u32[]{:S(2)}, u32[]{:S(2)}) collective-permute-start(f32[576,128]{1,0:T(8,128)S(1)} %get-tuple-element.24), channel_id=1, source_target_pairs={{0,16},{4,20},{8,24},{12,28},{16,0},{20,4},{24,8},{28,12},{1,17},{... | collective-permute-start | bytes 884744 | tf_op jit(solution)/shard_map/ppermute | solution.py:478
  5.6 1.5 %collective-permute-start.1 = (f32[576,128]{1,0:T(8,128)S(1)}, f32[576,128]{1,0:T(8,128)S(1)}, u32[]{:S(2)}, u32[]{:S(2)}) collective-permute-start(f32[576,128]{1,0:T(8,128)S(1)} %get-tuple-element.23), channel_id=1, source_target_pairs={{0,8},{4,12},{8,0},{12,4},{16,24},{20,28},{24,16},{28,20},{1,9},{5... | collective-permute-start | bytes 884744 | tf_op jit(solution)/shard_map/ppermute | solution.py:478
  7.1 0.3 collective-permute-start.3
  7.5 0.3 collective-permute-start.4
  7.8 1.3 %constant_dynamic-slice_fusion = (f32[576,128]{1,0:T(8,128)}, f32[576,128]{1,0:T(8,128)}, f32[576,128]{1,0:T(8,128)}, f32[576,128]{1,0:T(8,128)}, f32[576,128]{1...) fusion(f32[4608,128]{1,0:T(8,128)S(1)} %bitcast.14, s32[]{:T(128)S(6)} %select_n.42, s32[]{:T(128)S(6)} %select_n.41, ...), kind=kLoop, calls=%fused_computation.3 | loop fusion | bytes 4128796 | tf_op jit(solution)/shard_map/dynamic_slice | solution.py:519
  9.1 4.4 %collective-permute-done.refs_1_ = f32[576,128]{1,0:T(8,128)S(1)} collective-permute-done((f32[576,128]{1,0:T(8,128)S(1)}, f32[576,128]{1,0:T(8,128)S(1)}, u32[]{:S(2)}, u32[]{:S(2)}) %collective-permute-start) | collective-permute-done | bytes 294944 | tf_op jit(solution)/shard_map/ppermute | solution.py:478
  13.5 3.0 %collective-permute-start.5 = (f32[576,128]{1,0:T(8,128)}, f32[576,128]{1,0:T(8,128)}, u32[]{:S(2)}, u32[]{:S(2)}) collective-permute-start(f32[576,128]{1,0:T(8,128)} %get-tuple-element.19), channel_id=1, source_target_pairs={{0,24},{4,28},{8,16},{12,20},{16,8},{20,12},{24,0},{28,4},{1,25},{... | collective-permute-start | bytes 884744 | tf_op jit(solution)/shard_map/ppermute | solution.py:478
  16.5 1.9 %collective-permute-done.2.refs_3_ = f32[576,128]{1,0:T(8,128)S(1)} collective-permute-done((f32[576,128]{1,0:T(8,128)S(1)}, f32[576,128]{1,0:T(8,128)S(1)}, u32[]{:S(2)}, u32[]{:S(2)}) %collective-permute-start.2) | collective-permute-done | bytes 294944 | tf_op jit(solution)/shard_map/ppermute | solution.py:478
  18.3 1.2 %collective-permute-start.10 = (f32[576,128]{1,0:T(8,128)}, f32[576,128]{1,0:T(8,128)}, u32[]{:S(2)}, u32[]{:S(2)}) collective-permute-start(f32[576,128]{1,0:T(8,128)} %get-tuple-element.14), channel_id=1, source_target_pairs={{0,16},{4,20},{8,24},{12,28},{16,0},{20,4},{24,8},{28,12},{1,17},{... | collective-permute-start | bytes 884744 | tf_op jit(solution)/shard_map/ppermute | solution.py:478
  19.5 1.3 %collective-permute-done.3.refs_4_ = f32[576,128]{1,0:T(8,128)S(1)} collective-permute-done((f32[576,128]{1,0:T(8,128)S(1)}, f32[576,128]{1,0:T(8,128)S(1)}, u32[]{:S(2)}, u32[]{:S(2)}) %collective-permute-start.3) | collective-permute-done | bytes 294944 | tf_op jit(solution)/shard_map/ppermute | solution.py:478
  20.9 0.5 collective-permute-start.11
  22.1 0.0 copy-start.2
  22.1 0.1 select_reduce_fusion
  22.2 1.7 %collective-permute-start.12 = (f32[576,128]{1,0:T(8,128)}, f32[576,128]{1,0:T(8,128)S(1)}, u32[]{:S(2)}, u32[]{:S(2)}) collective-permute-start(f32[576,128]{1,0:T(8,128)} %get-tuple-element.12), channel_id=1, source_target_pairs={{0,20},{4,16},{8,28},{12,24},{16,4},{20,0},{24,12},{28,8},{1,21},{... | collective-permute-start | bytes 884744 | tf_op jit(solution)/shard_map/ppermute | solution.py:478
  23.9 4.0 %collective-permute-done.5.refs_6_ = f32[576,128]{1,0:T(8,128)} collective-permute-done((f32[576,128]{1,0:T(8,128)}, f32[576,128]{1,0:T(8,128)}, u32[]{:S(2)}, u32[]{:S(2)}) %collective-permute-start.5) | collective-permute-done | bytes 294944 | tf_op jit(solution)/shard_map/ppermute | solution.py:478
  27.9 5.8 %collective-permute-done.6.refs_7_ = f32[576,128]{1,0:T(8,128)} collective-permute-done((f32[576,128]{1,0:T(8,128)}, f32[576,128]{1,0:T(8,128)}, u32[]{:S(2)}, u32[]{:S(2)}) %collective-permute-start.6) | collective-permute-done | bytes 294944 | tf_op jit(solution)/shard_map/ppermute | solution.py:478
  33.7 0.3 collective-permute-start.9
  34.0 5.3 %collective-permute-done.10.refs_2_ = f32[576,128]{1,0:T(8,128)} collective-permute-done((f32[576,128]{1,0:T(8,128)}, f32[576,128]{1,0:T(8,128)}, u32[]{:S(2)}, u32[]{:S(2)}) %collective-permute-start.10) | collective-permute-done | bytes 294944 | tf_op jit(solution)/shard_map/ppermute | solution.py:478
  39.3 2.5 %collective-permute-start.8 = (f32[576,128]{1,0:T(8,128)}, f32[576,128]{1,0:T(8,128)S(1)}, u32[]{:S(2)}, u32[]{:S(2)}) collective-permute-start(f32[576,128]{1,0:T(8,128)} %get-tuple-element.16), channel_id=1, source_target_pairs={{0,24},{4,28},{8,16},{12,20},{16,8},{20,12},{24,0},{28,4},{1,25},{... | collective-permute-start | bytes 884744 | tf_op jit(solution)/shard_map/ppermute | solution.py:478
  41.8 0.1 dynamic_slice.52
  41.8 0.1 pad_add_fusion.1.owner_ref
  41.9 5.6 %forward.1 = (f32[576,8,128]{2,1,0:T(8,128)S(1)}, f32[4,4608,128]{2,1,0:T(8,128)S(1)}) custom-call(s32[1]{0:T(128)} %bitcast.3.place_ref.owner_ref, f32[4608,128]{1,0:T(8,128)S(1)} %bitcast.13, f32[576,128]{1,0:T(8,128)S(1)} %collective-permute-done.refs_1_, f32[576,128]{1,0:T(8,128)S(1)} %collective-permute-done.1.refs_2_, ...), custom_call_target="tpu_custom_call" | custom-call | flops 235929600 | bytes 14155776 | tf_op jit(solution)/shard_map/forward/pallas_call | solution.py:364
  47.6 0.1 squeeze.9.weight_ref
  47.7 2.7 %early.2.refs_1_ = f32[576,8,128]{2,1,0:T(8,128)S(1)} custom-call(s32[1]{0:T(128)} %bitcast.3.place_ref.owner_ref, f32[576,8,128]{2,1,0:T(8,128)S(1)} %get-tuple-element.8.lattice_ref, f32[8,128]{1,0:T(8,128)S(1)} %squeeze.9.weight_ref, f32[576,128]{1,0:T(8,128)S(1)} %collective-permute-done.9.refs_0_, f32[4608,128]{1,0:T(8,128)S(1)} %bitcast.15, ...), custom_call_target="tpu_custom_call" | custom-call | flops 88473600 | bytes 7077888 | tf_op jit(solution)/shard_map/early/pallas_call | solution.py:382
  50.4 2.6 %collective-permute-done.8.refs_0_ = f32[576,128]{1,0:T(8,128)S(1)} collective-permute-done((f32[576,128]{1,0:T(8,128)}, f32[576,128]{1,0:T(8,128)S(1)}, u32[]{:S(2)}, u32[]{:S(2)}) %collective-permute-start.8) | collective-permute-done | bytes 294944 | tf_op jit(solution)/shard_map/ppermute | solution.py:478
  53.0 0.5 early.3.refs_1_
  53.5 0.0 copy-start.3
  53.5 0.0 copy-start.6
  53.5 4.0 %collective-permute-done.7.refs_0_ = f32[576,128]{1,0:T(8,128)S(1)} collective-permute-done((f32[576,128]{1,0:T(8,128)}, f32[576,128]{1,0:T(8,128)S(1)}, u32[]{:S(2)}, u32[]{:S(2)}) %collective-permute-start.7) | collective-permute-done | bytes 294944 | tf_op jit(solution)/shard_map/ppermute | solution.py:478
  57.5 2.5 %sigma.1 = (f32[576,8,128]{2,1,0:T(8,128)S(1)}, f32[4608,128]{1,0:T(8,128)S(1)}) custom-call(s32[1]{0:T(128)} %bitcast.3.place_ref.owner_ref, f32[576,8,128]{2,1,0:T(8,128)S(1)} %get-tuple-element.8.lattice_ref, f32[8,128]{1,0:T(8,128)S(1)} %squeeze.9.weight_ref, f32[576,128]{1,0:T(8,128)S(1)} %collective-permute-done.7.refs_0_, ...), custom_call_target="tpu_custom_call", output_to_operand_aliasing={{0}: (4, {})} | custom-call | flops 117964800 | bytes 14155776 | tf_op jit(solution)/shard_map/sigma/pallas_call | solution.py:400
  60.0 2.5 %contract.4 = f32[288,128]{1,0:T(8,128)S(1)} custom-call(s32[4]{0:T(128)S(1)} %pad_add_fusion.1.owner_ref, f32[4608,128]{1,0:T(8,128)S(1)} %get-tuple-element.9.sigma_ref, f32[72,128]{1,0:T(8,128)S(1)} %copy-done.5, f32[8,128]{1,0:T(8,128)S(1)} %copy-done.6, bf16[2048,128]{1,0:T(8,128)(2,1)S(1)} %copy-done.3, f32[4,4608,128]{2,1,0:T(8,128)S(1)} %get-tuple-element.10.greens_ref), custom_call_target="tpu_custom_call" | custom-call | flops 165150720 | bytes 14155776 | tf_op jit(solution)/shard_map/contract/pallas_call | solution.py:421
  62.5 0.6 collective-permute-start.14
  63.1 0.1 pad_add_fusion.owner_ref
  63.2 2.1 %contract.3 = f32[216,128]{1,0:T(8,128)S(1)} custom-call(s32[3]{0:T(128)S(1)} %pad_add_fusion.owner_ref, f32[4608,128]{1,0:T(8,128)S(1)} %get-tuple-element.9.sigma_ref, f32[72,128]{1,0:T(8,128)S(1)} %copy-done.5, f32[8,128]{1,0:T(8,128)S(1)} %copy-done.6, bf16[2048,128]{1,0:T(8,128)(2,1)S(1)} %copy-done.3, f32[4,4608,128]{2,1,0:T(8,128)S(1)} %get-tuple-element.10.greens_ref), custom_call_target="tpu_custom_call" | custom-call | flops 123863040 | bytes 14155776 | tf_op jit(solution)/shard_map/contract/pallas_call | solution.py:421
  65.3 2.6 %collective-permute-start.15 = (f32[72,128]{1,0:T(8,128)S(1)}, f32[72,128]{1,0:T(8,128)S(1)}, u32[]{:S(2)}, u32[]{:S(2)}) collective-permute-start(f32[72,128]{1,0:T(8,128)S(1)} %get-tuple-element.27), channel_id=1, source_target_pairs={{0,24},{4,28},{8,16},{12,20},{16,8},{20,12},{24,0},{28,4},{1,25},{... | collective-permute-start | bytes 110600 | tf_op jit(solution)/shard_map/ppermute | solution.py:478
  68.0 0.5 collective-permute-start.16
  68.5 0.4 collective-permute-start.17
  68.9 1.4 %collective-permute-done.15.refs_0_ = f32[72,128]{1,0:T(8,128)S(1)} collective-permute-done((f32[72,128]{1,0:T(8,128)S(1)}, f32[72,128]{1,0:T(8,128)S(1)}, u32[]{:S(2)}, u32[]{:S(2)}) %collective-permute-start.15) | collective-permute-done | bytes 36896 | tf_op jit(solution)/shard_map/ppermute | solution.py:478
  70.2 0.6 contract.5
  70.9 1.0 %collective-permute-done.16 = f32[72,128]{1,0:T(8,128)S(1)} collective-permute-done((f32[72,128]{1,0:T(8,128)S(1)}, f32[72,128]{1,0:T(8,128)S(1)}, u32[]{:S(2)}, u32[]{:S(2)}) %collective-permute-start.16) | collective-permute-done | bytes 36896 | tf_op jit(solution)/shard_map/ppermute | solution.py:478
  71.9 0.5 collective-permute-done.17
  72.5 0.0 copy-start.4
  72.5 3.7 %collective-permute-start.18 = (f32[72,128]{1,0:T(8,128)S(1)}, f32[72,128]{1,0:T(8,128)S(1)}, u32[]{:S(2)}, u32[]{:S(2)}) collective-permute-start(f32[72,128]{1,0:T(8,128)S(1)} %slice_add_fusion.1), channel_id=1, source_target_pairs={{0,3},{1,2},{2,1},{3,0},{4,7},{5,6},{6,5},{7,4},{8,11},{9,10},{10,... | collective-permute-start | bytes 110600 | tf_op jit(solution)/shard_map/ppermute | solution.py:478
  76.2 0.8 collective-permute-start.20
  76.9 2.9 %roll_own.1.greens_ref = f32[4,64,72,128]{3,2,1,0:T(8,128)S(1)} custom-call(f32[64,72,128]{2,1,0:T(8,128)S(1)} %copy-done), custom_call_target="tpu_custom_call" | custom-call | flops 1769472 | bytes 11796480 | tf_op jit(solution)/shard_map/roll_own/pallas_call | solution.py:437
  79.9 1.1 %collective-permute-done.19 = f32[72,128]{1,0:T(8,128)S(1)} collective-permute-done((f32[72,128]{1,0:T(8,128)S(1)}, f32[72,128]{1,0:T(8,128)S(1)}, u32[]{:S(2)}, u32[]{:S(2)}) %collective-permute-start.19) | collective-permute-done | bytes 36896 | tf_op jit(solution)/shard_map/ppermute | solution.py:478
  81.0 5.3 %propagate.1 = f32[64,72,128]{2,1,0:T(8,128)} custom-call(f32[4,64,72,128]{3,2,1,0:T(8,128)S(1)} %roll_own.1.greens_ref, f32[72,128]{1,0:T(8,128)S(1)} %add_add_fusion.effective_ref, bf16[256,2048]{1,0:T(8,128)(2,1)S(1)} %copy-done.4), custom_call_target="tpu_custom_call" | custom-call | flops 18874368 | bytes 11796480 | tf_op jit(solution)/shard_map/propagate/pallas_call | solution.py:452
  (35 shorter events, 0.1 us)
Async XLA Ops:
  0.0 7.8 %copy-start.1 = (f32[64,72,128]{2,1,0:T(8,128)S(1)}, f32[64,72,128]{2,1,0:T(8,128)}, u32[]{:S(2)}) copy-start(f32[64,72,128]{2,1,0:T(8,128)} %param.15) | copy-start | bytes 7077892
  2.6 19.5 %copy-start.8 = (s32[64]{0:T(128)S(1)}, s32[64]{0:T(128)}, u32[]{:S(2)}) copy-start(s32[64]{0:T(128)} %param.18) | copy-start | bytes 772
  2.6 19.5 %copy-start.9 = (f32[4]{0:T(128)S(1)}, f32[4]{0:T(128)}, u32[]{:S(2)}) copy-start(f32[4]{0:T(128)} %constant.44.clone) | copy-start | bytes 52
  2.6 39.3 %copy-start = (f32[64,72,128]{2,1,0:T(8,128)S(1)}, f32[64,72,128]{2,1,0:T(8,128)}, u32[]{:S(2)}) copy-start(f32[64,72,128]{2,1,0:T(8,128)} %green_ref.1) | copy-start | bytes 7077892
  2.6 10.9 %collective-permute-start = (f32[576,128]{1,0:T(8,128)S(1)}, f32[576,128]{1,0:T(8,128)S(1)}, u32[]{:S(2)}, u32[]{:S(2)}) collective-permute-start(f32[576,128]{1,0:T(8,128)S(1)} %get-tuple-element.24), channel_id=1, source_target_pairs={{0,16},{4,20},{8,24},{12,28},{16,0},{20,4},{24,8},{28,12},{1,17},{... | collective-permute-start | bytes 884744 | tf_op jit(solution)/shard_map/ppermute | solution.py:478
  5.6 10.8 %collective-permute-start.1 = (f32[576,128]{1,0:T(8,128)S(1)}, f32[576,128]{1,0:T(8,128)S(1)}, u32[]{:S(2)}, u32[]{:S(2)}) collective-permute-start(f32[576,128]{1,0:T(8,128)S(1)} %get-tuple-element.23), channel_id=1, source_target_pairs={{0,8},{4,12},{8,0},{12,4},{16,24},{20,28},{24,16},{28,20},{1,9},{5... | collective-permute-start | bytes 884744 | tf_op jit(solution)/shard_map/ppermute | solution.py:478
  7.1 11.2 %collective-permute-start.2 = (f32[576,128]{1,0:T(8,128)S(1)}, f32[576,128]{1,0:T(8,128)S(1)}, u32[]{:S(2)}, u32[]{:S(2)}) collective-permute-start(f32[576,128]{1,0:T(8,128)S(1)} %get-tuple-element.22), channel_id=1, source_target_pairs={{0,20},{4,16},{8,28},{12,24},{16,4},{20,0},{24,12},{28,8},{1,21},{... | collective-permute-start | bytes 884744 | tf_op jit(solution)/shard_map/ppermute | solution.py:478
  7.1 13.8 %collective-permute-start.3 = (f32[576,128]{1,0:T(8,128)S(1)}, f32[576,128]{1,0:T(8,128)S(1)}, u32[]{:S(2)}, u32[]{:S(2)}) collective-permute-start(f32[576,128]{1,0:T(8,128)S(1)} %get-tuple-element.21), channel_id=1, source_target_pairs={{0,12},{4,8},{8,4},{12,0},{16,28},{20,24},{24,20},{28,16},{1,13},{... | collective-permute-start | bytes 884744 | tf_op jit(solution)/shard_map/ppermute | solution.py:478
  7.5 14.7 %collective-permute-start.4 = (f32[576,128]{1,0:T(8,128)}, f32[576,128]{1,0:T(8,128)}, u32[]{:S(2)}, u32[]{:S(2)}) collective-permute-start(f32[576,128]{1,0:T(8,128)} %get-tuple-element.20), channel_id=1, source_target_pairs={{0,4},{4,0},{8,12},{12,8},{16,20},{20,16},{24,28},{28,24},{1,5},{5... | collective-permute-start | bytes 884744 | tf_op jit(solution)/shard_map/ppermute | solution.py:478
  13.5 14.4 %collective-permute-start.5 = (f32[576,128]{1,0:T(8,128)}, f32[576,128]{1,0:T(8,128)}, u32[]{:S(2)}, u32[]{:S(2)}) collective-permute-start(f32[576,128]{1,0:T(8,128)} %get-tuple-element.19), channel_id=1, source_target_pairs={{0,24},{4,28},{8,16},{12,20},{16,8},{20,12},{24,0},{28,4},{1,25},{... | collective-permute-start | bytes 884744 | tf_op jit(solution)/shard_map/ppermute | solution.py:478
  16.5 17.2 %collective-permute-start.6 = (f32[576,128]{1,0:T(8,128)}, f32[576,128]{1,0:T(8,128)}, u32[]{:S(2)}, u32[]{:S(2)}) collective-permute-start(f32[576,128]{1,0:T(8,128)} %get-tuple-element.18), channel_id=1, source_target_pairs={{0,28},{4,24},{8,20},{12,16},{16,12},{20,8},{24,4},{28,0},{1,29},{... | collective-permute-start | bytes 884744 | tf_op jit(solution)/shard_map/ppermute | solution.py:478
  18.3 20.9 %collective-permute-start.10 = (f32[576,128]{1,0:T(8,128)}, f32[576,128]{1,0:T(8,128)}, u32[]{:S(2)}, u32[]{:S(2)}) collective-permute-start(f32[576,128]{1,0:T(8,128)} %get-tuple-element.14), channel_id=1, source_target_pairs={{0,16},{4,20},{8,24},{12,28},{16,0},{20,4},{24,8},{28,12},{1,17},{... | collective-permute-start | bytes 884744 | tf_op jit(solution)/shard_map/ppermute | solution.py:478
  20.9 20.9 %collective-permute-start.11 = (f32[576,128]{1,0:T(8,128)}, f32[576,128]{1,0:T(8,128)}, u32[]{:S(2)}, u32[]{:S(2)}) collective-permute-start(f32[576,128]{1,0:T(8,128)} %get-tuple-element.13), channel_id=1, source_target_pairs={{0,8},{4,12},{8,0},{12,4},{16,24},{20,28},{24,16},{28,20},{1,9},{5... | collective-permute-start | bytes 884744 | tf_op jit(solution)/shard_map/ppermute | solution.py:478
  22.1 25.6 %copy-start.2 = (f32[64,72,128]{2,1,0:T(8,128)S(1)}, f32[64,72,128]{2,1,0:T(8,128)}, u32[]{:S(2)}) copy-start(f32[64,72,128]{2,1,0:T(8,128)} %param.15) | copy-start | bytes 7077892
  22.2 25.4 %collective-permute-start.12 = (f32[576,128]{1,0:T(8,128)}, f32[576,128]{1,0:T(8,128)S(1)}, u32[]{:S(2)}, u32[]{:S(2)}) collective-permute-start(f32[576,128]{1,0:T(8,128)} %get-tuple-element.12), channel_id=1, source_target_pairs={{0,20},{4,16},{8,28},{12,24},{16,4},{20,0},{24,12},{28,8},{1,21},{... | collective-permute-start | bytes 884744 | tf_op jit(solution)/shard_map/ppermute | solution.py:478
  27.9 19.7 %collective-permute-start.13 = (f32[576,128]{1,0:T(8,128)}, f32[576,128]{1,0:T(8,128)S(1)}, u32[]{:S(2)}, u32[]{:S(2)}) collective-permute-start(f32[576,128]{1,0:T(8,128)} %get-tuple-element.11), channel_id=1, source_target_pairs={{0,12},{4,8},{8,4},{12,0},{16,28},{20,24},{24,20},{28,16},{1,13},{... | collective-permute-start | bytes 884744 | tf_op jit(solution)/shard_map/ppermute | solution.py:478
  33.7 13.9 %collective-permute-start.9 = (f32[576,128]{1,0:T(8,128)}, f32[576,128]{1,0:T(8,128)S(1)}, u32[]{:S(2)}, u32[]{:S(2)}) collective-permute-start(f32[576,128]{1,0:T(8,128)} %get-tuple-element.15), channel_id=1, source_target_pairs={{0,4},{4,0},{8,12},{12,8},{16,20},{20,16},{24,28},{28,24},{1,5},{5... | collective-permute-start | bytes 884744 | tf_op jit(solution)/shard_map/ppermute | solution.py:478
  39.3 13.7 %collective-permute-start.8 = (f32[576,128]{1,0:T(8,128)}, f32[576,128]{1,0:T(8,128)S(1)}, u32[]{:S(2)}, u32[]{:S(2)}) collective-permute-start(f32[576,128]{1,0:T(8,128)} %get-tuple-element.16), channel_id=1, source_target_pairs={{0,24},{4,28},{8,16},{12,20},{16,8},{20,12},{24,0},{28,4},{1,25},{... | collective-permute-start | bytes 884744 | tf_op jit(solution)/shard_map/ppermute | solution.py:478
  41.8 15.7 %collective-permute-start.7 = (f32[576,128]{1,0:T(8,128)}, f32[576,128]{1,0:T(8,128)S(1)}, u32[]{:S(2)}, u32[]{:S(2)}) collective-permute-start(f32[576,128]{1,0:T(8,128)} %get-tuple-element.17), channel_id=1, source_target_pairs={{0,28},{4,24},{8,20},{12,16},{16,12},{20,8},{24,4},{28,0},{1,29},{... | collective-permute-start | bytes 884744 | tf_op jit(solution)/shard_map/ppermute | solution.py:478
  53.5 6.5 %copy-start.3 = (bf16[2048,128]{1,0:T(8,128)(2,1)S(1)}, bf16[2048,128]{1,0:T(8,128)(2,1)}, u32[]{:S(2)}) copy-start(bf16[2048,128]{1,0:T(8,128)(2,1)} %constant.46.clone.gather_ref) | copy-start | bytes 1572868
  53.5 6.5 %copy-start.5 = (f32[72,128]{1,0:T(8,128)S(1)}, f32[72,128]{1,0:T(8,128)}, u32[]{:S(2)}) copy-start(f32[72,128]{1,0:T(8,128)} %equal_ref.5) | copy-start | bytes 110596
  53.5 6.5 %copy-start.6 = (f32[8,128]{1,0:T(8,128)S(1)}, f32[8,128]{1,0:T(8,128)}, u32[]{:S(2)}) copy-start(f32[8,128]{1,0:T(8,128)} %constant.45.clone.sign_ref) | copy-start | bytes 12292
  62.5 2.8 %collective-permute-start.14 = (f32[288,128]{1,0:T(8,128)S(1)}, f32[288,128]{1,0:T(8,128)S(1)}, u32[]{:S(2)}, u32[]{:S(2)}) collective-permute-start(f32[288,128]{1,0:T(8,128)S(1)} %contract.4), channel_id=1, source_target_pairs={{0,4},{4,0},{8,12},{12,8},{16,20},{20,16},{24,28},{28,24},{1,5},{5... | collective-permute-start | bytes 442376 | tf_op jit(solution)/shard_map/ppermute | solution.py:478
  65.3 4.9 %collective-permute-start.15 = (f32[72,128]{1,0:T(8,128)S(1)}, f32[72,128]{1,0:T(8,128)S(1)}, u32[]{:S(2)}, u32[]{:S(2)}) collective-permute-start(f32[72,128]{1,0:T(8,128)S(1)} %get-tuple-element.27), channel_id=1, source_target_pairs={{0,24},{4,28},{8,16},{12,20},{16,8},{20,12},{24,0},{28,4},{1,25},{... | collective-permute-start | bytes 110600 | tf_op jit(solution)/shard_map/ppermute | solution.py:478
  68.0 4.0 %collective-permute-start.16 = (f32[72,128]{1,0:T(8,128)S(1)}, f32[72,128]{1,0:T(8,128)S(1)}, u32[]{:S(2)}, u32[]{:S(2)}) collective-permute-start(f32[72,128]{1,0:T(8,128)S(1)} %get-tuple-element.25), channel_id=1, source_target_pairs={{0,16},{4,20},{8,24},{12,28},{16,0},{20,4},{24,8},{28,12},{1,17},{... | collective-permute-start | bytes 110600 | tf_op jit(solution)/shard_map/ppermute | solution.py:478
  68.5 4.0 %collective-permute-start.17 = (f32[72,128]{1,0:T(8,128)S(1)}, f32[72,128]{1,0:T(8,128)S(1)}, u32[]{:S(2)}, u32[]{:S(2)}) collective-permute-start(f32[72,128]{1,0:T(8,128)S(1)} %get-tuple-element.26), channel_id=1, source_target_pairs={{0,8},{4,12},{8,0},{12,4},{16,24},{20,28},{24,16},{28,20},{1,9},{5... | collective-permute-start | bytes 110600 | tf_op jit(solution)/shard_map/ppermute | solution.py:478
  72.5 8.6 %copy-start.7 = (f32[72,128]{1,0:T(8,128)S(1)}, f32[72,128]{1,0:T(8,128)}, u32[]{:S(2)}) copy-start(f32[72,128]{1,0:T(8,128)} %param.16) | copy-start | bytes 110596
  72.5 8.6 %copy-start.4 = (bf16[256,2048]{1,0:T(8,128)(2,1)S(1)}, bf16[256,2048]{1,0:T(8,128)(2,1)}, u32[]{:S(2)}) copy-start(bf16[256,2048]{1,0:T(8,128)(2,1)} %constant.47.clone.spread_ref) | copy-start | bytes 3145732
  72.5 7.4 %collective-permute-start.18 = (f32[72,128]{1,0:T(8,128)S(1)}, f32[72,128]{1,0:T(8,128)S(1)}, u32[]{:S(2)}, u32[]{:S(2)}) collective-permute-start(f32[72,128]{1,0:T(8,128)S(1)} %slice_add_fusion.1), channel_id=1, source_target_pairs={{0,3},{1,2},{2,1},{3,0},{4,7},{5,6},{6,5},{7,4},{8,11},{9,10},{10,... | collective-permute-start | bytes 110600 | tf_op jit(solution)/shard_map/ppermute | solution.py:478
  76.2 4.9 %collective-permute-start.19 = (f32[72,128]{1,0:T(8,128)S(1)}, f32[72,128]{1,0:T(8,128)S(1)}, u32[]{:S(2)}, u32[]{:S(2)}) collective-permute-start(f32[72,128]{1,0:T(8,128)S(1)} %slice_add_fusion.1), channel_id=1, source_target_pairs={{0,2},{1,3},{2,0},{3,1},{4,6},{5,7},{6,4},{7,5},{8,10},{9,11},{10,... | collective-permute-start | bytes 110600 | tf_op jit(solution)/shard_map/ppermute | solution.py:478
  76.2 4.9 %collective-permute-start.20 = (f32[72,128]{1,0:T(8,128)S(1)}, f32[72,128]{1,0:T(8,128)S(1)}, u32[]{:S(2)}, u32[]{:S(2)}) collective-permute-start(f32[72,128]{1,0:T(8,128)S(1)} %slice_add_fusion.1), channel_id=1, source_target_pairs={{0,1},{1,0},{2,3},{3,2},{4,5},{5,4},{6,7},{7,6},{8,9},{9,8},{10,11... | collective-permute-start | bytes 110600 | tf_op jit(solution)/shard_map/ppermute | solution.py:478

commit v12 on v11

--- a/solution.py
+++ b/solution.py
@@ -113,6 +113,18 @@
     lax.fori_loop(0, SIDE // 2, columns, 0)
 
 
+def pick_kernel(steps, parts, place_ref, whole_ref, *refs):
+    block_refs, sems = refs[-1 - len(steps) : -1], refs[-1]
+    copies = []
+    for n, (step, block_ref) in enumerate(zip(steps, block_refs)):
+        rows = block_ref.shape[0]
+        start = pl.multiple_of(partner_of(place_ref[0], step, parts) * rows, TILE)
+        copies.append(pltpu.make_async_copy(whole_ref.at[pl.ds(start, rows)], block_ref, sems.at[n]))
+        copies[-1].start()
+    for copy in copies:
+        copy.wait()
+
+
 def roll_kernel(green_ref, greens_ref):
     batch = math.gcd(green_ref.shape[0], STEPS)
 
@@ -433,6 +445,20 @@
     )(owners, sigma, equal_time, jnp.asarray(signs), jnp.asarray(gather), greens, *before)
 
 
+def pick(place, whole, steps, parts, before=()):
+    rows, width = whole.shape[0] // parts, whole.shape[1]
+    return pl.pallas_call(
+        functools.partial(pick_kernel, steps, parts),
+        out_shape=[jax.ShapeDtypeStruct((rows, width), whole.dtype)] * len(steps),
+        in_specs=[in_smem(), anywhere()] + [anywhere()] * len(before),
+        out_specs=[in_vmem()] * len(steps),
+        scratch_shapes=[pltpu.SemaphoreType.DMA((len(steps),))],
+        compiler_params=params(56),
+        cost_estimate=cost(0, 2),
+        name="pick",
+    )(place, whole, *before)
+
+
 def roll_own(greens):
     return pl.pallas_call(
         roll_kernel,
@@ -511,12 +537,11 @@
         order = exchange_order(parts)
         moved = []
         wholes = [x.reshape(parts * TILE * local, width) for x in (green_row, screened)]
-        moved = []
+        moved, picked = [], []
         for whole in wholes:
             found = {0: whole}
-            for step in order:
-                start = partner_of(place, step, parts) * (TILE * local)
-                block = lax.dynamic_slice_in_dim(whole, start, TILE * local)
+            picked = pick(seat, whole, order, parts, picked[:1])
+            for step, block in zip(order, picked):
                 found[step] = exchange(block, "ka", step, parts)
             moved.append([found])
         order = [0] + order

time: 86.5 us -> 92.6 us (1.071)
  Pallas kernels: 24.8 us -> 30.9 us
  local copies, waits for them, and re-layouts: 4.09 us -> 5.57 us
  waiting for transfers between devices: 33.4 us -> 32.1 us
    pallas_call x0 -> x2, Pallas kernels: none -> 5.86 us  [pick(): pl.pallas_call(functools.partial(pick_kernel, steps, parts), out_shape=[j...]
    unnamed x20 -> x28, local copies, waits for them, and re-layouts: 0.05 us -> 5.41 us
    dynamic_slice x2 -> x0, local copies, waits for them, and re-layouts: 3.88 us -> none  [per_device(): block = lax.dynamic_slice_in_dim(whole, start, TILE * local)]
    ppermute x21, waiting for transfers between devices: 33.4 us -> 32.1 us  [exchange(): return lax.ppermute(value, axis, pairs)]
  transfers between devices with their start and end apart: 21 -> 21, of which waited for: 12 -> 12; matrix products, arithmetic and copies ran while one was open for 2% -> 0% of each run, Pallas kernels for 17% -> 19%
where the time goes in v12:
time: 92.6 us; the launch traced here: 92.4 us
  waiting for transfers between devices  32.1 us (35%)
  Pallas kernels  30.9 us (33%)
  starting transfers between devices  22.7 us (25%)
  local copies, waits for them, and re-layouts  5.57 us (6%)
    ppermute x21, waiting for transfers between devices, exchange(): return lax.ppermute(value, axis, pairs)  32.1 us
    ppermute x21, starting transfers between devices, exchange(): return lax.ppermute(value, axis, pairs)  22.7 us
    pallas_call x2, Pallas kernels, pick(): pl.pallas_call(functools.partial(pick_kernel, steps, parts), out_shape=[j...  5.86 us
    pallas_call x1, Pallas kernels, forward(): pl.pallas_call(functools.partial(forward_kernel, steps, parts), out_shape...  5.62 us
    unnamed x28, local copies, waits for them, and re-layouts  5.41 us
    pallas_call x1, Pallas kernels, propagate(): pl.pallas_call(propagate_kernel, out_shape=jax.ShapeDtypeStruct(greens.sh...  5.33 us
    pallas_call x3, Pallas kernels, contract(): pl.pallas_call(functools.partial(contract_kernel, share), out_shape=jax.S...  5.28 us
    pallas_call x2, Pallas kernels, early_lines(): pl.pallas_call(functools.partial(early_kernel, steps, parts), out_shape=j...  3.41 us
  transfers between devices with their start and end apart: 21, of which 12 were waited for; matrix products, arithmetic and copies ran while one was open for 0% of the time, Pallas kernels for 19%

profile of v12, /device:TPU:0, one launch (start us, length us, event | category | flops | bytes accessed | tf_op | source)
XLA Modules:
  0.0 92.4 jit_solution(10252978703588574510)
XLA Ops:
  0.0 3.0 %pick.2 = (f32[576,128]{1,0:T(8,128)}, f32[576,128]{1,0:T(8,128)}, f32[576,128]{1,0:T(8,128)}, f32[576,128]{1,0:T(8,128)}, f32[576,128]{1,0:T(8,128)}, /*index=5*/f32[576,128]{1,0:T(8,128)}, f32[576,128]{1,0:T(8,128)}) custom-call(s32[1]{0:T(128)} %bitcast.3.place_ref.owner_ref, f32[4608,128]{1,0:T(8,128)} %bitcast.12), custom_call_target="tpu_custom_call" | custom-call | bytes 4718592 | tf_op jit(solution)/shard_map/pick/pallas_call | solution.py:450
  3.0 3.0 %collective-permute-start = (f32[576,128]{1,0:T(8,128)}, f32[576,128]{1,0:T(8,128)S(1)}, u32[]{:S(2)}, u32[]{:S(2)}) collective-permute-start(f32[576,128]{1,0:T(8,128)} %get-tuple-element.22.refs_0_), channel_id=1, source_target_pairs={{0,16},{4,20},{8,24},{12,28},{16,0},{20,4},{24,8},{28,12},{1,17},{... | collective-permute-start | bytes 884744 | tf_op jit(solution)/shard_map/ppermute | solution.py:504
  6.1 1.5 %collective-permute-start.1 = (f32[576,128]{1,0:T(8,128)}, f32[576,128]{1,0:T(8,128)S(1)}, u32[]{:S(2)}, u32[]{:S(2)}) collective-permute-start(f32[576,128]{1,0:T(8,128)} %get-tuple-element.23), channel_id=1, source_target_pairs={{0,8},{4,12},{8,0},{12,4},{16,24},{20,28},{24,16},{28,20},{1,9},{5... | collective-permute-start | bytes 884744 | tf_op jit(solution)/shard_map/ppermute | solution.py:504
  7.5 0.3 collective-permute-start.3
  7.9 0.3 collective-permute-start.4
  8.2 2.9 %pick.3 = (f32[576,128]{1,0:T(8,128)}, f32[576,128]{1,0:T(8,128)}, f32[576,128]{1,0:T(8,128)}, f32[576,128]{1,0:T(8,128)}, f32[576,128]{1,0:T(8,128)}, /*index=5*/f32[576,128]{1,0:T(8,128)}, f32[576,128]{1,0:T(8,128)}) custom-call(s32[1]{0:T(128)} %bitcast.3.place_ref.owner_ref, f32[4608,128]{1,0:T(8,128)} %bitcast.14, f32[576,128]{1,0:T(8,128)} %get-tuple-element.22.refs_0_), custom_call_target="tpu_custom_call" | custom-call | bytes 4718592 | tf_op jit(solution)/shard_map/pick/pallas_call | solution.py:450
  11.1 3.0 %collective-permute-done.refs_1_ = f32[576,128]{1,0:T(8,128)S(1)} collective-permute-done((f32[576,128]{1,0:T(8,128)}, f32[576,128]{1,0:T(8,128)S(1)}, u32[]{:S(2)}, u32[]{:S(2)}) %collective-permute-start) | collective-permute-done | bytes 294944 | tf_op jit(solution)/shard_map/ppermute | solution.py:504
  14.1 3.0 %collective-permute-start.5 = (f32[576,128]{1,0:T(8,128)}, f32[576,128]{1,0:T(8,128)}, u32[]{:S(2)}, u32[]{:S(2)}) collective-permute-start(f32[576,128]{1,0:T(8,128)} %get-tuple-element.27), channel_id=1, source_target_pairs={{0,24},{4,28},{8,16},{12,20},{16,8},{20,12},{24,0},{28,4},{1,25},{... | collective-permute-start | bytes 884744 | tf_op jit(solution)/shard_map/ppermute | solution.py:504
  17.1 2.0 %collective-permute-done.2.refs_3_ = f32[576,128]{1,0:T(8,128)S(1)} collective-permute-done((f32[576,128]{1,0:T(8,128)}, f32[576,128]{1,0:T(8,128)S(1)}, u32[]{:S(2)}, u32[]{:S(2)}) %collective-permute-start.2) | collective-permute-done | bytes 294944 | tf_op jit(solution)/shard_map/ppermute | solution.py:504
  19.1 1.1 %collective-permute-start.10 = (f32[576,128]{1,0:T(8,128)}, f32[576,128]{1,0:T(8,128)}, u32[]{:S(2)}, u32[]{:S(2)}) collective-permute-start(f32[576,128]{1,0:T(8,128)} %get-tuple-element.33), channel_id=1, source_target_pairs={{0,16},{4,20},{8,24},{12,28},{16,0},{20,4},{24,8},{28,12},{1,17},{... | collective-permute-start | bytes 884744 | tf_op jit(solution)/shard_map/ppermute | solution.py:504
  20.2 1.5 %collective-permute-done.3.refs_4_ = f32[576,128]{1,0:T(8,128)S(1)} collective-permute-done((f32[576,128]{1,0:T(8,128)}, f32[576,128]{1,0:T(8,128)S(1)}, u32[]{:S(2)}, u32[]{:S(2)}) %collective-permute-start.3) | collective-permute-done | bytes 294944 | tf_op jit(solution)/shard_map/ppermute | solution.py:504
  21.6 0.5 collective-permute-start.11
  22.9 0.1 select_reduce_fusion
  22.9 1.6 %collective-permute-start.12 = (f32[576,128]{1,0:T(8,128)}, f32[576,128]{1,0:T(8,128)S(1)}, u32[]{:S(2)}, u32[]{:S(2)}) collective-permute-start(f32[576,128]{1,0:T(8,128)} %get-tuple-element.35), channel_id=1, source_target_pairs={{0,20},{4,16},{8,28},{12,24},{16,4},{20,0},{24,12},{28,8},{1,21},{... | collective-permute-start | bytes 884744 | tf_op jit(solution)/shard_map/ppermute | solution.py:504
  24.5 4.0 %collective-permute-done.5.refs_6_ = f32[576,128]{1,0:T(8,128)} collective-permute-done((f32[576,128]{1,0:T(8,128)}, f32[576,128]{1,0:T(8,128)}, u32[]{:S(2)}, u32[]{:S(2)}) %collective-permute-start.5) | collective-permute-done | bytes 294944 | tf_op jit(solution)/shard_map/ppermute | solution.py:504
  28.5 5.8 %collective-permute-done.6.refs_7_ = f32[576,128]{1,0:T(8,128)} collective-permute-done((f32[576,128]{1,0:T(8,128)}, f32[576,128]{1,0:T(8,128)}, u32[]{:S(2)}, u32[]{:S(2)}) %collective-permute-start.6) | collective-permute-done | bytes 294944 | tf_op jit(solution)/shard_map/ppermute | solution.py:504
  34.3 0.3 collective-permute-start.9
  34.6 5.3 %collective-permute-done.10.refs_2_ = f32[576,128]{1,0:T(8,128)} collective-permute-done((f32[576,128]{1,0:T(8,128)}, f32[576,128]{1,0:T(8,128)}, u32[]{:S(2)}, u32[]{:S(2)}) %collective-permute-start.10) | collective-permute-done | bytes 294944 | tf_op jit(solution)/shard_map/ppermute | solution.py:504
  39.9 2.5 %collective-permute-start.8 = (f32[576,128]{1,0:T(8,128)}, f32[576,128]{1,0:T(8,128)S(1)}, u32[]{:S(2)}, u32[]{:S(2)}) collective-permute-start(f32[576,128]{1,0:T(8,128)} %get-tuple-element.31), channel_id=1, source_target_pairs={{0,24},{4,28},{8,16},{12,20},{16,8},{20,12},{24,0},{28,4},{1,25},{... | collective-permute-start | bytes 884744 | tf_op jit(solution)/shard_map/ppermute | solution.py:504
  42.4 0.1 dynamic_slice.3
  42.5 0.1 pad_add_fusion.1.owner_ref
  42.6 5.6 %forward.1 = (f32[576,8,128]{2,1,0:T(8,128)S(1)}, f32[4,4608,128]{2,1,0:T(8,128)S(1)}) custom-call(s32[1]{0:T(128)} %bitcast.3.place_ref.owner_ref, f32[4608,128]{1,0:T(8,128)S(1)} %bitcast.13, f32[576,128]{1,0:T(8,128)S(1)} %collective-permute-done.refs_1_, f32[576,128]{1,0:T(8,128)S(1)} %collective-permute-done.1.refs_2_, ...), custom_call_target="tpu_custom_call" | custom-call | flops 235929600 | bytes 14155776 | tf_op jit(solution)/shard_map/forward/pallas_call | solution.py:376
  48.2 0.1 squeeze.9.weight_ref
  48.3 2.9 %early.2.refs_1_ = f32[576,8,128]{2,1,0:T(8,128)S(1)} custom-call(s32[1]{0:T(128)} %bitcast.3.place_ref.owner_ref, f32[576,8,128]{2,1,0:T(8,128)S(1)} %get-tuple-element.29.lattice_ref, f32[8,128]{1,0:T(8,128)S(1)} %squeeze.9.weight_ref, f32[576,128]{1,0:T(8,128)S(1)} %collective-permute-done.9.refs_0_, f32[4608,128]{1,0:T(8,128)S(1)} %bitcast.15, ...), custom_call_target="tpu_custom_call" | custom-call | flops 88473600 | bytes 7077888 | tf_op jit(solution)/shard_map/early/pallas_call | solution.py:394
  51.3 2.4 %collective-permute-done.8.refs_0_ = f32[576,128]{1,0:T(8,128)S(1)} collective-permute-done((f32[576,128]{1,0:T(8,128)}, f32[576,128]{1,0:T(8,128)S(1)}, u32[]{:S(2)}, u32[]{:S(2)}) %collective-permute-start.8) | collective-permute-done | bytes 294944 | tf_op jit(solution)/shard_map/ppermute | solution.py:504
  53.6 0.5 early.3.refs_1_
  54.1 0.0 copy-start.10
  54.1 4.0 %collective-permute-done.7.refs_0_ = f32[576,128]{1,0:T(8,128)S(1)} collective-permute-done((f32[576,128]{1,0:T(8,128)}, f32[576,128]{1,0:T(8,128)S(1)}, u32[]{:S(2)}, u32[]{:S(2)}) %collective-permute-start.7) | collective-permute-done | bytes 294944 | tf_op jit(solution)/shard_map/ppermute | solution.py:504
  58.1 2.5 %sigma.1 = (f32[576,8,128]{2,1,0:T(8,128)S(1)}, f32[4608,128]{1,0:T(8,128)S(1)}) custom-call(s32[1]{0:T(128)} %bitcast.3.place_ref.owner_ref, f32[576,8,128]{2,1,0:T(8,128)S(1)} %get-tuple-element.29.lattice_ref, f32[8,128]{1,0:T(8,128)S(1)} %squeeze.9.weight_ref, f32[576,128]{1,0:T(8,128)S(1)} %collective-permute-done.7.refs_0_, ...), custom_call_target="tpu_custom_call", output_to_operand_aliasing={{0}: (4, {})} | custom-call | flops 117964800 | bytes 14155776 | tf_op jit(solution)/shard_map/sigma/pallas_call | solution.py:412
  60.7 2.5 %contract.4 = f32[288,128]{1,0:T(8,128)S(1)} custom-call(s32[4]{0:T(128)S(1)} %pad_add_fusion.1.owner_ref, f32[4608,128]{1,0:T(8,128)S(1)} %get-tuple-element.37.sigma_ref, f32[72,128]{1,0:T(8,128)S(1)} %copy-done.9, f32[8,128]{1,0:T(8,128)S(1)} %copy-done.10, bf16[2048,128]{1,0:T(8,128)(2,1)S(1)} %copy-done.7, f32[4,4608,128]{2,1,0:T(8,128)S(1)} %get-tuple-element.38.greens_ref), custom_call_target="tpu_custom_call" | custom-call | flops 165150720 | bytes 14155776 | tf_op jit(solution)/shard_map/contract/pallas_call | solution.py:433
  63.2 0.6 collective-permute-start.14
  63.8 0.1 pad_add_fusion.owner_ref
  63.8 3.7 %copy-done.1 = f32[4,4608,128]{2,1,0:T(8,128)S(1)} copy-done((f32[4,4608,128]{2,1,0:T(8,128)S(1)}, f32[4,4608,128]{2,1,0:T(8,128)}, u32[]{:S(2)}) %copy-start.1) | copy-done | bytes 9437208
  67.5 1.7 %copy-done.5 = f32[4608,128]{1,0:T(8,128)S(1)} copy-done((f32[4608,128]{1,0:T(8,128)S(1)}, f32[4608,128]{1,0:T(8,128)}, u32[]{:S(2)}) %copy-start.5) | copy-done | bytes 2359320
  69.2 2.1 %contract.3 = f32[216,128]{1,0:T(8,128)S(1)} custom-call(s32[3]{0:T(128)S(1)} %pad_add_fusion.owner_ref, f32[4608,128]{1,0:T(8,128)S(1)} %copy-done.5, f32[72,128]{1,0:T(8,128)S(1)} %copy-done.9, f32[8,128]{1,0:T(8,128)S(1)} %copy-done.10, bf16[2048,128]{1,0:T(8,128)(2,1)S(1)} %copy-done.7, f32[4,4608,128]{2,1,0:T(8,128)S(1)} %copy-done.1), custom_call_target="tpu_custom_call" | custom-call | flops 123863040 | bytes 14155776 | tf_op jit(solution)/shard_map/contract/pallas_call | solution.py:433
  71.3 2.6 %collective-permute-start.15 = (f32[72,128]{1,0:T(8,128)S(1)}, f32[72,128]{1,0:T(8,128)S(1)}, u32[]{:S(2)}, u32[]{:S(2)}) collective-permute-start(f32[72,128]{1,0:T(8,128)S(1)} %get-tuple-element.41), channel_id=1, source_target_pairs={{0,24},{4,28},{8,16},{12,20},{16,8},{20,12},{24,0},{28,4},{1,25},{... | collective-permute-start | bytes 110600 | tf_op jit(solution)/shard_map/ppermute | solution.py:504
  74.0 0.5 collective-permute-start.16
  74.5 0.4 collective-permute-start.17
  74.9 1.4 %collective-permute-done.15.refs_0_ = f32[72,128]{1,0:T(8,128)S(1)} collective-permute-done((f32[72,128]{1,0:T(8,128)S(1)}, f32[72,128]{1,0:T(8,128)S(1)}, u32[]{:S(2)}, u32[]{:S(2)}) %collective-permute-start.15) | collective-permute-done | bytes 36896 | tf_op jit(solution)/shard_map/ppermute | solution.py:504
  76.3 0.7 contract.5
  76.9 1.0 %collective-permute-done.16 = f32[72,128]{1,0:T(8,128)S(1)} collective-permute-done((f32[72,128]{1,0:T(8,128)S(1)}, f32[72,128]{1,0:T(8,128)S(1)}, u32[]{:S(2)}, u32[]{:S(2)}) %collective-permute-start.16) | collective-permute-done | bytes 36896 | tf_op jit(solution)/shard_map/ppermute | solution.py:504
  77.9 0.5 collective-permute-done.17
  78.5 0.0 copy-start.8
  78.5 3.7 %collective-permute-start.18 = (f32[72,128]{1,0:T(8,128)S(1)}, f32[72,128]{1,0:T(8,128)S(1)}, u32[]{:S(2)}, u32[]{:S(2)}) collective-permute-start(f32[72,128]{1,0:T(8,128)S(1)} %slice_add_fusion.1), channel_id=1, source_target_pairs={{0,3},{1,2},{2,1},{3,0},{4,7},{5,6},{6,5},{7,4},{8,11},{9,10},{10,... | collective-permute-start | bytes 110600 | tf_op jit(solution)/shard_map/ppermute | solution.py:504
  82.2 0.8 collective-permute-start.20
  83.0 2.9 %roll_own.1.greens_ref = f32[4,64,72,128]{3,2,1,0:T(8,128)S(1)} custom-call(f32[64,72,128]{2,1,0:T(8,128)S(1)} %copy-done.3), custom_call_target="tpu_custom_call" | custom-call | flops 1769472 | bytes 11796480 | tf_op jit(solution)/shard_map/roll_own/pallas_call | solution.py:463
  85.9 1.1 %collective-permute-done.19 = f32[72,128]{1,0:T(8,128)S(1)} collective-permute-done((f32[72,128]{1,0:T(8,128)S(1)}, f32[72,128]{1,0:T(8,128)S(1)}, u32[]{:S(2)}, u32[]{:S(2)}) %collective-permute-start.19) | collective-permute-done | bytes 36896 | tf_op jit(solution)/shard_map/ppermute | solution.py:504
  87.1 5.3 %propagate.1 = f32[64,72,128]{2,1,0:T(8,128)} custom-call(f32[4,64,72,128]{3,2,1,0:T(8,128)S(1)} %roll_own.1.greens_ref, f32[72,128]{1,0:T(8,128)S(1)} %add_add_fusion.effective_ref, bf16[256,2048]{1,0:T(8,128)(2,1)S(1)} %copy-done.8), custom_call_target="tpu_custom_call" | custom-call | flops 18874368 | bytes 11796480 | tf_op jit(solution)/shard_map/propagate/pallas_call | solution.py:478
  (43 shorter events, 0.2 us)
Async XLA Ops:
  0.0 22.8 %copy-start.12 = (s32[64]{0:T(128)S(1)}, s32[64]{0:T(128)}, u32[]{:S(2)}) copy-start(s32[64]{0:T(128)} %param.18) | copy-start | bytes 772
  0.0 22.8 %copy-start.13 = (f32[4]{0:T(128)S(1)}, f32[4]{0:T(128)}, u32[]{:S(2)}) copy-start(f32[4]{0:T(128)} %constant.40.clone) | copy-start | bytes 52
  0.0 42.6 %copy-start.3 = (f32[64,72,128]{2,1,0:T(8,128)S(1)}, f32[64,72,128]{2,1,0:T(8,128)}, u32[]{:S(2)}) copy-start(f32[64,72,128]{2,1,0:T(8,128)} %green_ref.1) | copy-start | bytes 7077892
  3.0 11.1 %collective-permute-start = (f32[576,128]{1,0:T(8,128)}, f32[576,128]{1,0:T(8,128)S(1)}, u32[]{:S(2)}, u32[]{:S(2)}) collective-permute-start(f32[576,128]{1,0:T(8,128)} %get-tuple-element.22.refs_0_), channel_id=1, source_target_pairs={{0,16},{4,20},{8,24},{12,28},{16,0},{20,4},{24,8},{28,12},{1,17},{... | collective-permute-start | bytes 884744 | tf_op jit(solution)/shard_map/ppermute | solution.py:504
  6.1 11.0 %collective-permute-start.1 = (f32[576,128]{1,0:T(8,128)}, f32[576,128]{1,0:T(8,128)S(1)}, u32[]{:S(2)}, u32[]{:S(2)}) collective-permute-start(f32[576,128]{1,0:T(8,128)} %get-tuple-element.23), channel_id=1, source_target_pairs={{0,8},{4,12},{8,0},{12,4},{16,24},{20,28},{24,16},{28,20},{1,9},{5... | collective-permute-start | bytes 884744 | tf_op jit(solution)/shard_map/ppermute | solution.py:504
  7.5 11.5 %collective-permute-start.2 = (f32[576,128]{1,0:T(8,128)}, f32[576,128]{1,0:T(8,128)S(1)}, u32[]{:S(2)}, u32[]{:S(2)}) collective-permute-start(f32[576,128]{1,0:T(8,128)} %get-tuple-element.24), channel_id=1, source_target_pairs={{0,20},{4,16},{8,28},{12,24},{16,4},{20,0},{24,12},{28,8},{1,21},{... | collective-permute-start | bytes 884744 | tf_op jit(solution)/shard_map/ppermute | solution.py:504
  7.5 14.1 %collective-permute-start.3 = (f32[576,128]{1,0:T(8,128)}, f32[576,128]{1,0:T(8,128)S(1)}, u32[]{:S(2)}, u32[]{:S(2)}) collective-permute-start(f32[576,128]{1,0:T(8,128)} %get-tuple-element.25), channel_id=1, source_target_pairs={{0,12},{4,8},{8,4},{12,0},{16,28},{20,24},{24,20},{28,16},{1,13},{... | collective-permute-start | bytes 884744 | tf_op jit(solution)/shard_map/ppermute | solution.py:504
  7.9 15.1 %collective-permute-start.4 = (f32[576,128]{1,0:T(8,128)}, f32[576,128]{1,0:T(8,128)}, u32[]{:S(2)}, u32[]{:S(2)}) collective-permute-start(f32[576,128]{1,0:T(8,128)} %get-tuple-element.26), channel_id=1, source_target_pairs={{0,4},{4,0},{8,12},{12,8},{16,20},{20,16},{24,28},{28,24},{1,5},{5... | collective-permute-start | bytes 884744 | tf_op jit(solution)/shard_map/ppermute | solution.py:504
  14.1 14.4 %collective-permute-start.5 = (f32[576,128]{1,0:T(8,128)}, f32[576,128]{1,0:T(8,128)}, u32[]{:S(2)}, u32[]{:S(2)}) collective-permute-start(f32[576,128]{1,0:T(8,128)} %get-tuple-element.27), channel_id=1, source_target_pairs={{0,24},{4,28},{8,16},{12,20},{16,8},{20,12},{24,0},{28,4},{1,25},{... | collective-permute-start | bytes 884744 | tf_op jit(solution)/shard_map/ppermute | solution.py:504
  17.1 17.2 %collective-permute-start.6 = (f32[576,128]{1,0:T(8,128)}, f32[576,128]{1,0:T(8,128)}, u32[]{:S(2)}, u32[]{:S(2)}) collective-permute-start(f32[576,128]{1,0:T(8,128)} %get-tuple-element.28), channel_id=1, source_target_pairs={{0,28},{4,24},{8,20},{12,16},{16,12},{20,8},{24,4},{28,0},{1,29},{... | collective-permute-start | bytes 884744 | tf_op jit(solution)/shard_map/ppermute | solution.py:504
  19.1 20.8 %collective-permute-start.10 = (f32[576,128]{1,0:T(8,128)}, f32[576,128]{1,0:T(8,128)}, u32[]{:S(2)}, u32[]{:S(2)}) collective-permute-start(f32[576,128]{1,0:T(8,128)} %get-tuple-element.33), channel_id=1, source_target_pairs={{0,16},{4,20},{8,24},{12,28},{16,0},{20,4},{24,8},{28,12},{1,17},{... | collective-permute-start | bytes 884744 | tf_op jit(solution)/shard_map/ppermute | solution.py:504
  21.6 20.8 %collective-permute-start.11 = (f32[576,128]{1,0:T(8,128)}, f32[576,128]{1,0:T(8,128)}, u32[]{:S(2)}, u32[]{:S(2)}) collective-permute-start(f32[576,128]{1,0:T(8,128)} %get-tuple-element.34), channel_id=1, source_target_pairs={{0,8},{4,12},{8,0},{12,4},{16,24},{20,28},{24,16},{28,20},{1,9},{5... | collective-permute-start | bytes 884744 | tf_op jit(solution)/shard_map/ppermute | solution.py:504
  22.8 25.5 %copy-start.6 = (f32[64,72,128]{2,1,0:T(8,128)S(1)}, f32[64,72,128]{2,1,0:T(8,128)}, u32[]{:S(2)}) copy-start(f32[64,72,128]{2,1,0:T(8,128)} %param.15) | copy-start | bytes 7077892
  22.9 25.3 %collective-permute-start.12 = (f32[576,128]{1,0:T(8,128)}, f32[576,128]{1,0:T(8,128)S(1)}, u32[]{:S(2)}, u32[]{:S(2)}) collective-permute-start(f32[576,128]{1,0:T(8,128)} %get-tuple-element.35), channel_id=1, source_target_pairs={{0,20},{4,16},{8,28},{12,24},{16,4},{20,0},{24,12},{28,8},{1,21},{... | collective-permute-start | bytes 884744 | tf_op jit(solution)/shard_map/ppermute | solution.py:504
  28.5 19.7 %collective-permute-start.13 = (f32[576,128]{1,0:T(8,128)}, f32[576,128]{1,0:T(8,128)S(1)}, u32[]{:S(2)}, u32[]{:S(2)}) collective-permute-start(f32[576,128]{1,0:T(8,128)} %get-tuple-element.36), channel_id=1, source_target_pairs={{0,12},{4,8},{8,4},{12,0},{16,28},{20,24},{24,20},{28,16},{1,13},{... | collective-permute-start | bytes 884744 | tf_op jit(solution)/shard_map/ppermute | solution.py:504
  34.3 13.9 %collective-permute-start.9 = (f32[576,128]{1,0:T(8,128)}, f32[576,128]{1,0:T(8,128)S(1)}, u32[]{:S(2)}, u32[]{:S(2)}) collective-permute-start(f32[576,128]{1,0:T(8,128)} %get-tuple-element.32), channel_id=1, source_target_pairs={{0,4},{4,0},{8,12},{12,8},{16,20},{20,16},{24,28},{28,24},{1,5},{5... | collective-permute-start | bytes 884744 | tf_op jit(solution)/shard_map/ppermute | solution.py:504
  39.9 13.7 %collective-permute-start.8 = (f32[576,128]{1,0:T(8,128)}, f32[576,128]{1,0:T(8,128)S(1)}, u32[]{:S(2)}, u32[]{:S(2)}) collective-permute-start(f32[576,128]{1,0:T(8,128)} %get-tuple-element.31), channel_id=1, source_target_pairs={{0,24},{4,28},{8,16},{12,20},{16,8},{20,12},{24,0},{28,4},{1,25},{... | collective-permute-start | bytes 884744 | tf_op jit(solution)/shard_map/ppermute | solution.py:504
  42.4 15.7 %collective-permute-start.7 = (f32[576,128]{1,0:T(8,128)}, f32[576,128]{1,0:T(8,128)S(1)}, u32[]{:S(2)}, u32[]{:S(2)}) collective-permute-start(f32[576,128]{1,0:T(8,128)} %get-tuple-element.30), channel_id=1, source_target_pairs={{0,28},{4,24},{8,20},{12,16},{16,12},{20,8},{24,4},{28,0},{1,29},{... | collective-permute-start | bytes 884744 | tf_op jit(solution)/shard_map/ppermute | solution.py:504
  48.2 12.4 %copy-start = (f32[4,4608,128]{2,1,0:T(8,128)}, f32[4,4608,128]{2,1,0:T(8,128)S(1)}, u32[]{:S(2)}) copy-start(f32[4,4608,128]{2,1,0:T(8,128)S(1)} %get-tuple-element.38.greens_ref) | copy-start | bytes 28311556
  54.1 6.5 %copy-start.7 = (bf16[2048,128]{1,0:T(8,128)(2,1)S(1)}, bf16[2048,128]{1,0:T(8,128)(2,1)}, u32[]{:S(2)}) copy-start(bf16[2048,128]{1,0:T(8,128)(2,1)} %constant.42.clone.gather_ref) | copy-start | bytes 1572868
  54.1 6.5 %copy-start.9 = (f32[72,128]{1,0:T(8,128)S(1)}, f32[72,128]{1,0:T(8,128)}, u32[]{:S(2)}) copy-start(f32[72,128]{1,0:T(8,128)} %equal_ref.5) | copy-start | bytes 110596
  54.1 6.5 %copy-start.10 = (f32[8,128]{1,0:T(8,128)S(1)}, f32[8,128]{1,0:T(8,128)}, u32[]{:S(2)}) copy-start(f32[8,128]{1,0:T(8,128)} %constant.41.clone.sign_ref) | copy-start | bytes 12292
  60.6 2.6 %copy-start.4 = (f32[4608,128]{1,0:T(8,128)}, f32[4608,128]{1,0:T(8,128)S(1)}, u32[]{:S(2)}) copy-start(f32[4608,128]{1,0:T(8,128)S(1)} %get-tuple-element.37.sigma_ref) | copy-start | bytes 7077892
  63.2 8.1 %collective-permute-start.14 = (f32[288,128]{1,0:T(8,128)S(1)}, f32[288,128]{1,0:T(8,128)S(1)}, u32[]{:S(2)}, u32[]{:S(2)}) collective-permute-start(f32[288,128]{1,0:T(8,128)S(1)} %contract.4), channel_id=1, source_target_pairs={{0,4},{4,0},{8,12},{12,8},{16,20},{20,16},{24,28},{28,24},{1,5},{5... | collective-permute-start | bytes 442376 | tf_op jit(solution)/shard_map/ppermute | solution.py:504
  63.8 3.7 %copy-start.1 = (f32[4,4608,128]{2,1,0:T(8,128)S(1)}, f32[4,4608,128]{2,1,0:T(8,128)}, u32[]{:S(2)}) copy-start(f32[4,4608,128]{2,1,0:T(8,128)} %copy-done) | copy-start | bytes 28311556
  67.5 1.7 %copy-start.5 = (f32[4608,128]{1,0:T(8,128)S(1)}, f32[4608,128]{1,0:T(8,128)}, u32[]{:S(2)}) copy-start(f32[4608,128]{1,0:T(8,128)} %copy-done.4) | copy-start | bytes 7077892
  69.2 7.1 %copy-start.2 = (f32[4,4608,128]{2,1,0:T(8,128)S(1)}, f32[4,4608,128]{2,1,0:T(8,128)}, u32[]{:S(2)}) copy-start(f32[4,4608,128]{2,1,0:T(8,128)} %copy-done) | copy-start | bytes 28311556
  71.3 4.9 %collective-permute-start.15 = (f32[72,128]{1,0:T(8,128)S(1)}, f32[72,128]{1,0:T(8,128)S(1)}, u32[]{:S(2)}, u32[]{:S(2)}) collective-permute-start(f32[72,128]{1,0:T(8,128)S(1)} %get-tuple-element.41), channel_id=1, source_target_pairs={{0,24},{4,28},{8,16},{12,20},{16,8},{20,12},{24,0},{28,4},{1,25},{... | collective-permute-start | bytes 110600 | tf_op jit(solution)/shard_map/ppermute | solution.py:504
  74.0 4.0 %collective-permute-start.16 = (f32[72,128]{1,0:T(8,128)S(1)}, f32[72,128]{1,0:T(8,128)S(1)}, u32[]{:S(2)}, u32[]{:S(2)}) collective-permute-start(f32[72,128]{1,0:T(8,128)S(1)} %get-tuple-element.39), channel_id=1, source_target_pairs={{0,16},{4,20},{8,24},{12,28},{16,0},{20,4},{24,8},{28,12},{1,17},{... | collective-permute-start | bytes 110600 | tf_op jit(solution)/shard_map/ppermute | solution.py:504
  74.5 4.0 %collective-permute-start.17 = (f32[72,128]{1,0:T(8,128)S(1)}, f32[72,128]{1,0:T(8,128)S(1)}, u32[]{:S(2)}, u32[]{:S(2)}) collective-permute-start(f32[72,128]{1,0:T(8,128)S(1)} %get-tuple-element.40), channel_id=1, source_target_pairs={{0,8},{4,12},{8,0},{12,4},{16,24},{20,28},{24,16},{28,20},{1,9},{5... | collective-permute-start | bytes 110600 | tf_op jit(solution)/shard_map/ppermute | solution.py:504
  78.5 8.6 %copy-start.11 = (f32[72,128]{1,0:T(8,128)S(1)}, f32[72,128]{1,0:T(8,128)}, u32[]{:S(2)}) copy-start(f32[72,128]{1,0:T(8,128)} %param.16) | copy-start | bytes 110596
  78.5 8.6 %copy-start.8 = (bf16[256,2048]{1,0:T(8,128)(2,1)S(1)}, bf16[256,2048]{1,0:T(8,128)(2,1)}, u32[]{:S(2)}) copy-start(bf16[256,2048]{1,0:T(8,128)(2,1)} %constant.43.clone.spread_ref) | copy-start | bytes 3145732
  78.5 7.4 %collective-permute-start.18 = (f32[72,128]{1,0:T(8,128)S(1)}, f32[72,128]{1,0:T(8,128)S(1)}, u32[]{:S(2)}, u32[]{:S(2)}) collective-permute-start(f32[72,128]{1,0:T(8,128)S(1)} %slice_add_fusion.1), channel_id=1, source_target_pairs={{0,3},{1,2},{2,1},{3,0},{4,7},{5,6},{6,5},{7,4},{8,11},{9,10},{10,... | collective-permute-start | bytes 110600 | tf_op jit(solution)/shard_map/ppermute | solution.py:504
  82.2 4.9 %collective-permute-start.19 = (f32[72,128]{1,0:T(8,128)S(1)}, f32[72,128]{1,0:T(8,128)S(1)}, u32[]{:S(2)}, u32[]{:S(2)}) collective-permute-start(f32[72,128]{1,0:T(8,128)S(1)} %slice_add_fusion.1), channel_id=1, source_target_pairs={{0,2},{1,3},{2,0},{3,1},{4,6},{5,7},{6,4},{7,5},{8,10},{9,11},{10,... | collective-permute-start | bytes 110600 | tf_op jit(solution)/shard_map/ppermute | solution.py:504
  82.2 4.9 %collective-permute-start.20 = (f32[72,128]{1,0:T(8,128)S(1)}, f32[72,128]{1,0:T(8,128)S(1)}, u32[]{:S(2)}, u32[]{:S(2)}) collective-permute-start(f32[72,128]{1,0:T(8,128)S(1)} %slice_add_fusion.1), channel_id=1, source_target_pairs={{0,1},{1,0},{2,3},{3,2},{4,5},{5,4},{6,7},{7,6},{8,9},{9,8},{10,11... | collective-permute-start | bytes 110600 | tf_op jit(solution)/shard_map/ppermute | solution.py:504

commit v13 on v11

--- a/solution.py
+++ b/solution.py
@@ -113,18 +113,33 @@
     lax.fori_loop(0, SIDE // 2, columns, 0)
 
 
-def roll_kernel(green_ref, greens_ref):
-    batch = math.gcd(green_ref.shape[0], STEPS)
-
-    def rolls(n, carry):
-        times = pl.ds(n * batch, batch)
-        green = green_ref[times]
-        rolled = [roll_blocks(green, j) for j in range(STEPS)]
-        for j in range(STEPS):
-            greens_ref[j, times] = rolled[j]
+def times_of(ref, k):
+    history, points, width = ref.shape
+    if points % TILE:
+        return ref[:, k, :]
+    return ref.reshape(history * points, width)[pl.ds(k, history, stride=points), :]
+
+
+def split_kernel(green_ref, split_ref):
+    history, points, _ = green_ref.shape
+
+    def write(k):
+        green = times_of(green_ref, k)
+        high = green.astype(jnp.bfloat16)
+        split_ref[k, :history, :] = high
+        split_ref[k, history:, :] = (green - high.astype(jnp.float32)).astype(jnp.bfloat16)
+
+    if points % TILE:
+        for k in range(points):
+            write(k)
+        return
+
+    def some(n, carry):
+        for k in range(4):
+            write(4 * n + k)
         return carry
 
-    lax.fori_loop(0, green_ref.shape[0] // batch, rolls, 0)
+    lax.fori_loop(0, points // 4, some, 0)
 
 
 def forward_kernel(steps, parts, place_ref, *refs):
@@ -260,48 +275,62 @@
     partial_ref[...] = total[:points] + jnp.where(on_diagonal, occupied * share, 0.0)
 
 
-def propagate_kernel(greens_ref, effective_ref, spread_ref, out_ref, factor_ref, held_ref, sems):
-    _, history, points, _ = greens_ref.shape
+def propagate_kernel(green_ref, split_ref, effective_ref, spread_ref, out_ref, factor_ref, held_ref, sems):
+    history, points, _ = green_ref.shape
     factor_ref[...] = jnp.dot(
         split(effective_ref[...] * time_step), spread_ref[...], preferred_element_type=jnp.float32
     )
-
-    slots, chunk = held_ref.shape[:2]
+    tile = held_ref.shape[2]
+    row = lax.broadcasted_iota(jnp.int32, (BANDS, WIDTH), 0)
+    same = lax.broadcasted_iota(jnp.int32, (BANDS, WIDTH), 1) % BANDS == row
 
     def copy(number, slot):
         return pltpu.make_async_copy(
-            held_ref.at[slot], out_ref.at[pl.ds(number * chunk, chunk)], sems.at[slot]
+            held_ref.at[slot], out_ref.at[:, pl.ds(number * tile, tile), :], sems.at[slot]
         )
 
-    def advance(group, carry):
-        for slot in range(slots):
-            number = group * slots + slot
-
-            @pl.when(group > 0)
-            def _():
-                copy(number - slots, slot).wait()
-
-            times = pl.ds(number * chunk, chunk)
-            for start in range(0, points, TILE):
-                stop = min(start + TILE, points)
-                greens = [greens_ref[j, times, start:stop, :] for j in range(STEPS)]
-                terms = [greens[0]]
-                for i in range(STEPS):
-                    total = None
-                    for j in range(STEPS):
-                        spot = STEPS * i + j
-                        factor = factor_ref[start:stop, spot * WIDTH : (spot + 1) * WIDTH]
-                        term = factor[None] * greens[j]
-                        total = term if total is None else total + term
-                    terms.append(roll_blocks(total, STEPS * i))
-                held_ref[slot, :, start:stop, :] = tree_sum(terms)
-            copy(number, slot).start()
+    def matrix(factors, n):
+        parts = [
+            jnp.where(same, jnp.broadcast_to(factor[n : n + 1], same.shape), 0.0) for factor in factors
+        ]
+        return split(jnp.concatenate(parts, axis=0))
+
+    def advance(number, slot):
+        start = number * tile if points == tile else pl.multiple_of(number * tile, TILE)
+        factors = [
+            factor_ref[pl.ds(start, tile), spot * WIDTH : (spot + 1) * WIDTH] for spot in range(2 * BANDS)
+        ]
+        for n in range(tile):
+            k = number * tile + n
+            both = jnp.dot(split_ref[k], matrix(factors, n), preferred_element_type=jnp.float32)
+            added = both[:history, :WIDTH] + (both[:history, WIDTH:] + both[history:, :WIDTH])
+            result = times_of(green_ref, k) + added
+            if points % TILE:
+                held_ref[slot, :, n, :] = result
+            else:
+                rows = held_ref.reshape(2 * history * tile, WIDTH)
+                rows[pl.ds(slot * history * tile + n, history, stride=tile), :] = result
+        copy(number, slot).start()
+
+    tiles = points // tile
+    if tiles == 1:
+        advance(0, 0)
+        copy(0, 0).wait()
+        return
+
+    def step(number, carry):
+        slot = number % 2
+
+        @pl.when(number > 1)
+        def _():
+            copy(number - 2, slot).wait()
+
+        advance(number, slot)
         return carry
 
-    groups = history // (chunk * slots)
-    lax.fori_loop(0, groups, advance, 0)
-    for slot in range(slots):
-        copy((groups - 1) * slots + slot, slot).wait()
+    lax.fori_loop(0, tiles, step, 0)
+    for number in (tiles - 2, tiles - 1):
+        copy(number, number % 2).wait()
 
 
 def gather_tables():
@@ -320,14 +349,9 @@
 
 
 def spread_table():
-    blocks = 2 * BANDS
-    table = np.zeros((2, BANDS, BANDS, STEPS, STEPS, blocks, BANDS), np.float32)
-    for i in range(STEPS):
-        for j in range(STEPS):
-            for p in range(blocks):
-                h, a = divmod((p - STEPS * i) % blocks, BANDS)
-                g, b = divmod((p + j) % blocks, BANDS)
-                table[1 if h == g else 0, a, b, i, j, p, :] = -1 if (h, g) == (1, 0) else 1
+    table = np.zeros((2, BANDS, BANDS, 2, BANDS, 2, BANDS, BANDS), np.float32)
+    for h, g, a, b in np.ndindex(2, 2, BANDS, BANDS):
+        table[1 if h == g else 0, a, b, g, b, h, a, :] = -1 if (h, g) == (1, 0) else 1
     return np.tile(table.reshape(WIDTH, -1), (2, 1)).astype(ml_dtypes.bfloat16)
 
 
@@ -433,36 +457,37 @@
     )(owners, sigma, equal_time, jnp.asarray(signs), jnp.asarray(gather), greens, *before)
 
 
-def roll_own(greens):
+def split_own(greens):
+    history, points, width = greens.shape
     return pl.pallas_call(
-        roll_kernel,
-        out_shape=jax.ShapeDtypeStruct((STEPS, *greens.shape), jnp.float32),
+        split_kernel,
+        out_shape=jax.ShapeDtypeStruct((points, 2 * history, width), jnp.bfloat16),
         in_specs=[in_vmem()],
         out_specs=in_vmem(),
         compiler_params=params(4),
-        cost_estimate=cost(3, 5),
-        name="roll_own",
+        cost_estimate=cost(3, 2),
+        name="split_own",
     )(greens)
 
 
-def propagate(greens, effective):
-    _, history, points, width = greens.shape
-    chunk = math.gcd(history // 2, TILE)
+def propagate(greens, pieces, effective):
+    history, points, width = greens.shape
+    tile = points if points % TILE else TILE
     spread = spread_table()
     return pl.pallas_call(
         propagate_kernel,
-        out_shape=jax.ShapeDtypeStruct(greens.shape[1:], jnp.float32),
-        in_specs=[in_vmem()] * 3,
+        out_shape=jax.ShapeDtypeStruct(greens.shape, jnp.float32),
+        in_specs=[in_vmem()] * 4,
         out_specs=anywhere(),
         scratch_shapes=[
             pltpu.VMEM((points, spread.shape[1]), jnp.float32),
-            pltpu.VMEM((2, chunk, points, width), jnp.float32),
+            pltpu.VMEM((2, history, tile, width), jnp.float32),
             pltpu.SemaphoreType.DMA((2,)),
         ],
         compiler_params=params(6),
         cost_estimate=cost(32, 5),
         name="propagate",
-    )(greens, effective, jnp.asarray(spread))
+    )(greens, pieces, effective, jnp.asarray(spread))
 
 
 def partner_of(place, step, count):
@@ -535,7 +560,7 @@
 
     early = order[: max(1, len(order) - LATE)]
     late = order[len(early) :]
-    own_greens = roll_own(green_row)
+    own_pieces = split_own(green_row)
     share = hubbard / (points * blocks)
     sigmas = []
     for group in range(groups):
@@ -583,7 +608,7 @@
     collision = tree_sum(
         [collision] + [exchange(collision, "hist", step, blocks) for step in range(blocks - 1, 0, -1)]
     )
-    return propagate(own_greens, hamilton + collision)
+    return propagate(green_row, own_pieces, hamilton + collision)
 
 
 def solution(mesh):

time: 86.5 us -> 86.5 us (level)
  Pallas kernels: 24.8 us -> 22.4 us
  waiting for transfers between devices: 33.4 us -> 35.8 us
    ppermute x21, waiting for transfers between devices: 33.4 us -> 35.8 us  [exchange(): return lax.ppermute(value, axis, pairs)]
    pallas_call x1, Pallas kernels: 2.92 us -> 0.53 us  [split_own(): pl.pallas_call(split_kernel, out_shape=jax.ShapeDtypeStruct((points, 2 *...]
  transfers between devices with their start and end apart: 21 -> 21, of which waited for: 12 -> 13; matrix products, arithmetic and copies ran while one was open for 2% -> 2% of each run, Pallas kernels for 17% -> 14%
where the time goes in v13:
time: 86.5 us; the launch traced here: 86.4 us
  waiting for transfers between devices  35.8 us (41%)
  starting transfers between devices  22.9 us (26%)
  Pallas kernels  22.4 us (26%)
  local copies, waits for them, and re-layouts  4.09 us (5%)
  between operations  0.87 us (1%)
    ppermute x21, waiting for transfers between devices, exchange(): return lax.ppermute(value, axis, pairs)  35.8 us
    ppermute x21, starting transfers between devices, exchange(): return lax.ppermute(value, axis, pairs)  22.9 us
    pallas_call x1, Pallas kernels, forward(): pl.pallas_call(functools.partial(forward_kernel, steps, parts), out_shape...  5.62 us
    pallas_call x1, Pallas kernels, propagate(): pl.pallas_call(propagate_kernel, out_shape=jax.ShapeDtypeStruct(greens.sh...  5.34 us
    pallas_call x3, Pallas kernels, contract(): pl.pallas_call(functools.partial(contract_kernel, share), out_shape=jax.S...  5.27 us
    dynamic_slice x2, local copies, waits for them, and re-layouts, per_device(): block = lax.dynamic_slice_in_dim(whole, start, TILE * local)  3.88 us
    pallas_call x2, Pallas kernels, early_lines(): pl.pallas_call(functools.partial(early_kernel, steps, parts), out_shape=j...  3.19 us
    pallas_call x1, Pallas kernels, sigma_of(): pl.pallas_call(functools.partial(sigma_kernel, steps, parts), out_shape=[...  2.46 us
  transfers between devices with their start and end apart: 21, of which 13 were waited for; matrix products, arithmetic and copies ran while one was open for 2% of the time, Pallas kernels for 14%

profile of v13, /device:TPU:0, one launch (start us, length us, event | category | flops | bytes accessed | tf_op | source)
XLA Modules:
  0.0 86.4 jit_solution(12425703915354736770)
XLA Ops:
  0.0 2.6 %constant_dynamic-slice_fusion.7 = (f32[576,128]{1,0:T(8,128)}, f32[576,128]{1,0:T(8,128)}, f32[576,128]{1,0:T(8,128)}, f32[576,128]{1,0:T(8,128)S(1)}, f32[576,...) fusion(f32[4608,128]{1,0:T(8,128)} %bitcast.12, s32[]{:T(128)S(6)} %select_n.45, s32[]{:T(128)S(6)} %select_n.44, ...), kind=kLoop, calls=%fused_computation.10 | loop fusion | bytes 4128796 | tf_op jit(solution)/shard_map/dynamic_slice | solution.py:544
  2.6 3.0 %collective-permute-start = (f32[576,128]{1,0:T(8,128)S(1)}, f32[576,128]{1,0:T(8,128)S(1)}, u32[]{:S(2)}, u32[]{:S(2)}) collective-permute-start(f32[576,128]{1,0:T(8,128)S(1)} %get-tuple-element.24), channel_id=1, source_target_pairs={{0,16},{4,20},{8,24},{12,28},{16,0},{20,4},{24,8},{28,12},{1,17},{... | collective-permute-start | bytes 884744 | tf_op jit(solution)/shard_map/ppermute | solution.py:503
  5.6 1.5 %collective-permute-start.1 = (f32[576,128]{1,0:T(8,128)S(1)}, f32[576,128]{1,0:T(8,128)S(1)}, u32[]{:S(2)}, u32[]{:S(2)}) collective-permute-start(f32[576,128]{1,0:T(8,128)S(1)} %get-tuple-element.23), channel_id=1, source_target_pairs={{0,8},{4,12},{8,0},{12,4},{16,24},{20,28},{24,16},{28,20},{1,9},{5... | collective-permute-start | bytes 884744 | tf_op jit(solution)/shard_map/ppermute | solution.py:503
  7.1 0.3 collective-permute-start.3
  7.5 0.3 collective-permute-start.4
  7.8 1.3 %constant_dynamic-slice_fusion = (f32[576,128]{1,0:T(8,128)}, f32[576,128]{1,0:T(8,128)}, f32[576,128]{1,0:T(8,128)}, f32[576,128]{1,0:T(8,128)}, f32[576,128]{1...) fusion(f32[4608,128]{1,0:T(8,128)S(1)} %bitcast.14, s32[]{:T(128)S(6)} %select_n.42, s32[]{:T(128)S(6)} %select_n.41, ...), kind=kLoop, calls=%fused_computation.3 | loop fusion | bytes 4128796 | tf_op jit(solution)/shard_map/dynamic_slice | solution.py:544
  9.1 4.4 %collective-permute-done.refs_1_ = f32[576,128]{1,0:T(8,128)S(1)} collective-permute-done((f32[576,128]{1,0:T(8,128)S(1)}, f32[576,128]{1,0:T(8,128)S(1)}, u32[]{:S(2)}, u32[]{:S(2)}) %collective-permute-start) | collective-permute-done | bytes 294944 | tf_op jit(solution)/shard_map/ppermute | solution.py:503
  13.5 3.0 %collective-permute-start.5 = (f32[576,128]{1,0:T(8,128)}, f32[576,128]{1,0:T(8,128)}, u32[]{:S(2)}, u32[]{:S(2)}) collective-permute-start(f32[576,128]{1,0:T(8,128)} %get-tuple-element.19), channel_id=1, source_target_pairs={{0,24},{4,28},{8,16},{12,20},{16,8},{20,12},{24,0},{28,4},{1,25},{... | collective-permute-start | bytes 884744 | tf_op jit(solution)/shard_map/ppermute | solution.py:503
  16.5 1.9 %collective-permute-done.2.refs_3_ = f32[576,128]{1,0:T(8,128)S(1)} collective-permute-done((f32[576,128]{1,0:T(8,128)S(1)}, f32[576,128]{1,0:T(8,128)S(1)}, u32[]{:S(2)}, u32[]{:S(2)}) %collective-permute-start.2) | collective-permute-done | bytes 294944 | tf_op jit(solution)/shard_map/ppermute | solution.py:503
  18.3 1.2 %collective-permute-start.10 = (f32[576,128]{1,0:T(8,128)}, f32[576,128]{1,0:T(8,128)}, u32[]{:S(2)}, u32[]{:S(2)}) collective-permute-start(f32[576,128]{1,0:T(8,128)} %get-tuple-element.14), channel_id=1, source_target_pairs={{0,16},{4,20},{8,24},{12,28},{16,0},{20,4},{24,8},{28,12},{1,17},{... | collective-permute-start | bytes 884744 | tf_op jit(solution)/shard_map/ppermute | solution.py:503
  19.5 1.3 %collective-permute-done.3.refs_4_ = f32[576,128]{1,0:T(8,128)S(1)} collective-permute-done((f32[576,128]{1,0:T(8,128)S(1)}, f32[576,128]{1,0:T(8,128)S(1)}, u32[]{:S(2)}, u32[]{:S(2)}) %collective-permute-start.3) | collective-permute-done | bytes 294944 | tf_op jit(solution)/shard_map/ppermute | solution.py:503
  20.9 0.5 collective-permute-start.11
  22.1 0.1 select_reduce_fusion
  22.2 1.7 %collective-permute-start.12 = (f32[576,128]{1,0:T(8,128)}, f32[576,128]{1,0:T(8,128)S(1)}, u32[]{:S(2)}, u32[]{:S(2)}) collective-permute-start(f32[576,128]{1,0:T(8,128)} %get-tuple-element.12), channel_id=1, source_target_pairs={{0,20},{4,16},{8,28},{12,24},{16,4},{20,0},{24,12},{28,8},{1,21},{... | collective-permute-start | bytes 884744 | tf_op jit(solution)/shard_map/ppermute | solution.py:503
  23.9 4.0 %collective-permute-done.5.refs_6_ = f32[576,128]{1,0:T(8,128)} collective-permute-done((f32[576,128]{1,0:T(8,128)}, f32[576,128]{1,0:T(8,128)}, u32[]{:S(2)}, u32[]{:S(2)}) %collective-permute-start.5) | collective-permute-done | bytes 294944 | tf_op jit(solution)/shard_map/ppermute | solution.py:503
  27.9 5.8 %collective-permute-done.6.refs_7_ = f32[576,128]{1,0:T(8,128)} collective-permute-done((f32[576,128]{1,0:T(8,128)}, f32[576,128]{1,0:T(8,128)}, u32[]{:S(2)}, u32[]{:S(2)}) %collective-permute-start.6) | collective-permute-done | bytes 294944 | tf_op jit(solution)/shard_map/ppermute | solution.py:503
  33.7 0.3 collective-permute-start.9
  34.0 5.3 %collective-permute-done.10.refs_2_ = f32[576,128]{1,0:T(8,128)} collective-permute-done((f32[576,128]{1,0:T(8,128)}, f32[576,128]{1,0:T(8,128)}, u32[]{:S(2)}, u32[]{:S(2)}) %collective-permute-start.10) | collective-permute-done | bytes 294944 | tf_op jit(solution)/shard_map/ppermute | solution.py:503
  39.3 2.5 %collective-permute-start.8 = (f32[576,128]{1,0:T(8,128)}, f32[576,128]{1,0:T(8,128)S(1)}, u32[]{:S(2)}, u32[]{:S(2)}) collective-permute-start(f32[576,128]{1,0:T(8,128)} %get-tuple-element.16), channel_id=1, source_target_pairs={{0,24},{4,28},{8,16},{12,20},{16,8},{20,12},{24,0},{28,4},{1,25},{... | collective-permute-start | bytes 884744 | tf_op jit(solution)/shard_map/ppermute | solution.py:503
  41.8 0.1 dynamic_slice.52
  41.8 0.1 pad_add_fusion.1.owner_ref
  41.9 5.6 %forward.1 = (f32[576,8,128]{2,1,0:T(8,128)S(1)}, f32[4,4608,128]{2,1,0:T(8,128)S(1)}) custom-call(s32[1]{0:T(128)} %bitcast.3.place_ref.owner_ref, f32[4608,128]{1,0:T(8,128)S(1)} %bitcast.13, f32[576,128]{1,0:T(8,128)S(1)} %collective-permute-done.refs_1_, f32[576,128]{1,0:T(8,128)S(1)} %collective-permute-done.1.refs_2_, ...), custom_call_target="tpu_custom_call" | custom-call | flops 235929600 | bytes 14155776 | tf_op jit(solution)/shard_map/forward/pallas_call | solution.py:388
  47.6 0.1 squeeze.9.weight_ref
  47.7 2.7 %early.2.refs_1_ = f32[576,8,128]{2,1,0:T(8,128)S(1)} custom-call(s32[1]{0:T(128)} %bitcast.3.place_ref.owner_ref, f32[576,8,128]{2,1,0:T(8,128)S(1)} %get-tuple-element.8.lattice_ref, f32[8,128]{1,0:T(8,128)S(1)} %squeeze.9.weight_ref, f32[576,128]{1,0:T(8,128)S(1)} %collective-permute-done.9.refs_0_, f32[4608,128]{1,0:T(8,128)S(1)} %bitcast.15, ...), custom_call_target="tpu_custom_call" | custom-call | flops 88473600 | bytes 7077888 | tf_op jit(solution)/shard_map/early/pallas_call | solution.py:406
  50.4 2.6 %collective-permute-done.8.refs_0_ = f32[576,128]{1,0:T(8,128)S(1)} collective-permute-done((f32[576,128]{1,0:T(8,128)}, f32[576,128]{1,0:T(8,128)S(1)}, u32[]{:S(2)}, u32[]{:S(2)}) %collective-permute-start.8) | collective-permute-done | bytes 294944 | tf_op jit(solution)/shard_map/ppermute | solution.py:503
  53.0 0.5 early.3.refs_1_
  53.5 0.0 copy-start.3
  53.5 0.0 copy-start.6
  53.5 4.0 %collective-permute-done.7.refs_0_ = f32[576,128]{1,0:T(8,128)S(1)} collective-permute-done((f32[576,128]{1,0:T(8,128)}, f32[576,128]{1,0:T(8,128)S(1)}, u32[]{:S(2)}, u32[]{:S(2)}) %collective-permute-start.7) | collective-permute-done | bytes 294944 | tf_op jit(solution)/shard_map/ppermute | solution.py:503
  57.5 2.5 %sigma.1 = (f32[576,8,128]{2,1,0:T(8,128)S(1)}, f32[4608,128]{1,0:T(8,128)S(1)}) custom-call(s32[1]{0:T(128)} %bitcast.3.place_ref.owner_ref, f32[576,8,128]{2,1,0:T(8,128)S(1)} %get-tuple-element.8.lattice_ref, f32[8,128]{1,0:T(8,128)S(1)} %squeeze.9.weight_ref, f32[576,128]{1,0:T(8,128)S(1)} %collective-permute-done.7.refs_0_, ...), custom_call_target="tpu_custom_call", output_to_operand_aliasing={{0}: (4, {})} | custom-call | flops 117964800 | bytes 14155776 | tf_op jit(solution)/shard_map/sigma/pallas_call | solution.py:424
  60.0 2.5 %contract.4 = f32[288,128]{1,0:T(8,128)S(1)} custom-call(s32[4]{0:T(128)S(1)} %pad_add_fusion.1.owner_ref, f32[4608,128]{1,0:T(8,128)S(1)} %get-tuple-element.9.sigma_ref, f32[72,128]{1,0:T(8,128)S(1)} %copy-done.5, f32[8,128]{1,0:T(8,128)S(1)} %copy-done.6, bf16[2048,128]{1,0:T(8,128)(2,1)S(1)} %copy-done.3, f32[4,4608,128]{2,1,0:T(8,128)S(1)} %get-tuple-element.10.greens_ref), custom_call_target="tpu_custom_call" | custom-call | flops 165150720 | bytes 14155776 | tf_op jit(solution)/shard_map/contract/pallas_call | solution.py:445
  62.5 0.6 collective-permute-start.14
  63.1 0.1 pad_add_fusion.owner_ref
  63.2 2.1 %contract.3 = f32[216,128]{1,0:T(8,128)S(1)} custom-call(s32[3]{0:T(128)S(1)} %pad_add_fusion.owner_ref, f32[4608,128]{1,0:T(8,128)S(1)} %get-tuple-element.9.sigma_ref, f32[72,128]{1,0:T(8,128)S(1)} %copy-done.5, f32[8,128]{1,0:T(8,128)S(1)} %copy-done.6, bf16[2048,128]{1,0:T(8,128)(2,1)S(1)} %copy-done.3, f32[4,4608,128]{2,1,0:T(8,128)S(1)} %get-tuple-element.10.greens_ref), custom_call_target="tpu_custom_call" | custom-call | flops 123863040 | bytes 14155776 | tf_op jit(solution)/shard_map/contract/pallas_call | solution.py:445
  65.3 2.6 %collective-permute-start.15 = (f32[72,128]{1,0:T(8,128)S(1)}, f32[72,128]{1,0:T(8,128)S(1)}, u32[]{:S(2)}, u32[]{:S(2)}) collective-permute-start(f32[72,128]{1,0:T(8,128)S(1)} %get-tuple-element.27), channel_id=1, source_target_pairs={{0,24},{4,28},{8,16},{12,20},{16,8},{20,12},{24,0},{28,4},{1,25},{... | collective-permute-start | bytes 110600 | tf_op jit(solution)/shard_map/ppermute | solution.py:503
  68.0 0.5 collective-permute-start.16
  68.5 0.4 collective-permute-start.17
  68.9 1.4 %collective-permute-done.15.refs_0_ = f32[72,128]{1,0:T(8,128)S(1)} collective-permute-done((f32[72,128]{1,0:T(8,128)S(1)}, f32[72,128]{1,0:T(8,128)S(1)}, u32[]{:S(2)}, u32[]{:S(2)}) %collective-permute-start.15) | collective-permute-done | bytes 36896 | tf_op jit(solution)/shard_map/ppermute | solution.py:503
  70.2 0.6 contract.5
  70.9 1.0 %collective-permute-done.16 = f32[72,128]{1,0:T(8,128)S(1)} collective-permute-done((f32[72,128]{1,0:T(8,128)S(1)}, f32[72,128]{1,0:T(8,128)S(1)}, u32[]{:S(2)}, u32[]{:S(2)}) %collective-permute-start.16) | collective-permute-done | bytes 36896 | tf_op jit(solution)/shard_map/ppermute | solution.py:503
  71.9 0.5 collective-permute-done.17
  72.5 0.0 copy-start.4
  72.5 3.7 %collective-permute-start.18 = (f32[72,128]{1,0:T(8,128)S(1)}, f32[72,128]{1,0:T(8,128)S(1)}, u32[]{:S(2)}, u32[]{:S(2)}) collective-permute-start(f32[72,128]{1,0:T(8,128)S(1)} %slice_add_fusion.1), channel_id=1, source_target_pairs={{0,3},{1,2},{2,1},{3,0},{4,7},{5,6},{6,5},{7,4},{8,11},{9,10},{10,... | collective-permute-start | bytes 110600 | tf_op jit(solution)/shard_map/ppermute | solution.py:503
  76.2 0.8 collective-permute-start.20
  76.9 0.5 split_own.1.split_ref
  77.5 0.9 %collective-permute-done.18 = f32[72,128]{1,0:T(8,128)S(1)} collective-permute-done((f32[72,128]{1,0:T(8,128)S(1)}, f32[72,128]{1,0:T(8,128)S(1)}, u32[]{:S(2)}, u32[]{:S(2)}) %collective-permute-start.18) | collective-permute-done | bytes 36896 | tf_op jit(solution)/shard_map/ppermute | solution.py:503
  78.4 2.6 %collective-permute-done.19 = f32[72,128]{1,0:T(8,128)S(1)} collective-permute-done((f32[72,128]{1,0:T(8,128)S(1)}, f32[72,128]{1,0:T(8,128)S(1)}, u32[]{:S(2)}, u32[]{:S(2)}) %collective-permute-start.19) | collective-permute-done | bytes 36896 | tf_op jit(solution)/shard_map/ppermute | solution.py:503
  81.0 5.3 %propagate.1 = f32[64,72,128]{2,1,0:T(8,128)} custom-call(f32[64,72,128]{2,1,0:T(8,128)S(1)} %copy-done, bf16[72,128,128]{2,1,0:T(8,128)(2,1)S(1)} %split_own.1.split_ref, f32[72,128]{1,0:T(8,128)S(1)} %add_add_fusion.effective_ref, bf16[256,2048]{1,0:T(8,128)(2,1)S(1)} %copy-done.4), custom_call_target="tpu_custom_call" | custom-call | flops 18874368 | bytes 11796480 | tf_op jit(solution)/shard_map/propagate/pallas_call | solution.py:477
  (35 shorter events, 0.1 us)
Async XLA Ops:
  0.0 7.8 %copy-start.1 = (f32[64,72,128]{2,1,0:T(8,128)S(1)}, f32[64,72,128]{2,1,0:T(8,128)}, u32[]{:S(2)}) copy-start(f32[64,72,128]{2,1,0:T(8,128)} %param.15) | copy-start | bytes 7077892
  2.6 19.5 %copy-start.8 = (s32[64]{0:T(128)S(1)}, s32[64]{0:T(128)}, u32[]{:S(2)}) copy-start(s32[64]{0:T(128)} %param.18) | copy-start | bytes 772
  2.6 19.5 %copy-start.9 = (f32[4]{0:T(128)S(1)}, f32[4]{0:T(128)}, u32[]{:S(2)}) copy-start(f32[4]{0:T(128)} %constant.44.clone) | copy-start | bytes 52
  2.6 39.3 %copy-start = (f32[64,72,128]{2,1,0:T(8,128)S(1)}, f32[64,72,128]{2,1,0:T(8,128)}, u32[]{:S(2)}) copy-start(f32[64,72,128]{2,1,0:T(8,128)} %green_ref.3) | copy-start | bytes 7077892
  2.6 10.9 %collective-permute-start = (f32[576,128]{1,0:T(8,128)S(1)}, f32[576,128]{1,0:T(8,128)S(1)}, u32[]{:S(2)}, u32[]{:S(2)}) collective-permute-start(f32[576,128]{1,0:T(8,128)S(1)} %get-tuple-element.24), channel_id=1, source_target_pairs={{0,16},{4,20},{8,24},{12,28},{16,0},{20,4},{24,8},{28,12},{1,17},{... | collective-permute-start | bytes 884744 | tf_op jit(solution)/shard_map/ppermute | solution.py:503
  5.6 10.8 %collective-permute-start.1 = (f32[576,128]{1,0:T(8,128)S(1)}, f32[576,128]{1,0:T(8,128)S(1)}, u32[]{:S(2)}, u32[]{:S(2)}) collective-permute-start(f32[576,128]{1,0:T(8,128)S(1)} %get-tuple-element.23), channel_id=1, source_target_pairs={{0,8},{4,12},{8,0},{12,4},{16,24},{20,28},{24,16},{28,20},{1,9},{5... | collective-permute-start | bytes 884744 | tf_op jit(solution)/shard_map/ppermute | solution.py:503
  7.1 11.2 %collective-permute-start.2 = (f32[576,128]{1,0:T(8,128)S(1)}, f32[576,128]{1,0:T(8,128)S(1)}, u32[]{:S(2)}, u32[]{:S(2)}) collective-permute-start(f32[576,128]{1,0:T(8,128)S(1)} %get-tuple-element.22), channel_id=1, source_target_pairs={{0,20},{4,16},{8,28},{12,24},{16,4},{20,0},{24,12},{28,8},{1,21},{... | collective-permute-start | bytes 884744 | tf_op jit(solution)/shard_map/ppermute | solution.py:503
  7.1 13.8 %collective-permute-start.3 = (f32[576,128]{1,0:T(8,128)S(1)}, f32[576,128]{1,0:T(8,128)S(1)}, u32[]{:S(2)}, u32[]{:S(2)}) collective-permute-start(f32[576,128]{1,0:T(8,128)S(1)} %get-tuple-element.21), channel_id=1, source_target_pairs={{0,12},{4,8},{8,4},{12,0},{16,28},{20,24},{24,20},{28,16},{1,13},{... | collective-permute-start | bytes 884744 | tf_op jit(solution)/shard_map/ppermute | solution.py:503
  7.5 14.7 %collective-permute-start.4 = (f32[576,128]{1,0:T(8,128)}, f32[576,128]{1,0:T(8,128)}, u32[]{:S(2)}, u32[]{:S(2)}) collective-permute-start(f32[576,128]{1,0:T(8,128)} %get-tuple-element.20), channel_id=1, source_target_pairs={{0,4},{4,0},{8,12},{12,8},{16,20},{20,16},{24,28},{28,24},{1,5},{5... | collective-permute-start | bytes 884744 | tf_op jit(solution)/shard_map/ppermute | solution.py:503
  13.5 14.4 %collective-permute-start.5 = (f32[576,128]{1,0:T(8,128)}, f32[576,128]{1,0:T(8,128)}, u32[]{:S(2)}, u32[]{:S(2)}) collective-permute-start(f32[576,128]{1,0:T(8,128)} %get-tuple-element.19), channel_id=1, source_target_pairs={{0,24},{4,28},{8,16},{12,20},{16,8},{20,12},{24,0},{28,4},{1,25},{... | collective-permute-start | bytes 884744 | tf_op jit(solution)/shard_map/ppermute | solution.py:503
  16.5 17.2 %collective-permute-start.6 = (f32[576,128]{1,0:T(8,128)}, f32[576,128]{1,0:T(8,128)}, u32[]{:S(2)}, u32[]{:S(2)}) collective-permute-start(f32[576,128]{1,0:T(8,128)} %get-tuple-element.18), channel_id=1, source_target_pairs={{0,28},{4,24},{8,20},{12,16},{16,12},{20,8},{24,4},{28,0},{1,29},{... | collective-permute-start | bytes 884744 | tf_op jit(solution)/shard_map/ppermute | solution.py:503
  18.3 20.9 %collective-permute-start.10 = (f32[576,128]{1,0:T(8,128)}, f32[576,128]{1,0:T(8,128)}, u32[]{:S(2)}, u32[]{:S(2)}) collective-permute-start(f32[576,128]{1,0:T(8,128)} %get-tuple-element.14), channel_id=1, source_target_pairs={{0,16},{4,20},{8,24},{12,28},{16,0},{20,4},{24,8},{28,12},{1,17},{... | collective-permute-start | bytes 884744 | tf_op jit(solution)/shard_map/ppermute | solution.py:503
  20.9 20.9 %collective-permute-start.11 = (f32[576,128]{1,0:T(8,128)}, f32[576,128]{1,0:T(8,128)}, u32[]{:S(2)}, u32[]{:S(2)}) collective-permute-start(f32[576,128]{1,0:T(8,128)} %get-tuple-element.13), channel_id=1, source_target_pairs={{0,8},{4,12},{8,0},{12,4},{16,24},{20,28},{24,16},{28,20},{1,9},{5... | collective-permute-start | bytes 884744 | tf_op jit(solution)/shard_map/ppermute | solution.py:503
  22.1 25.6 %copy-start.2 = (f32[64,72,128]{2,1,0:T(8,128)S(1)}, f32[64,72,128]{2,1,0:T(8,128)}, u32[]{:S(2)}) copy-start(f32[64,72,128]{2,1,0:T(8,128)} %param.15) | copy-start | bytes 7077892
  22.2 25.4 %collective-permute-start.12 = (f32[576,128]{1,0:T(8,128)}, f32[576,128]{1,0:T(8,128)S(1)}, u32[]{:S(2)}, u32[]{:S(2)}) collective-permute-start(f32[576,128]{1,0:T(8,128)} %get-tuple-element.12), channel_id=1, source_target_pairs={{0,20},{4,16},{8,28},{12,24},{16,4},{20,0},{24,12},{28,8},{1,21},{... | collective-permute-start | bytes 884744 | tf_op jit(solution)/shard_map/ppermute | solution.py:503
  27.9 19.7 %collective-permute-start.13 = (f32[576,128]{1,0:T(8,128)}, f32[576,128]{1,0:T(8,128)S(1)}, u32[]{:S(2)}, u32[]{:S(2)}) collective-permute-start(f32[576,128]{1,0:T(8,128)} %get-tuple-element.11), channel_id=1, source_target_pairs={{0,12},{4,8},{8,4},{12,0},{16,28},{20,24},{24,20},{28,16},{1,13},{... | collective-permute-start | bytes 884744 | tf_op jit(solution)/shard_map/ppermute | solution.py:503
  33.7 13.9 %collective-permute-start.9 = (f32[576,128]{1,0:T(8,128)}, f32[576,128]{1,0:T(8,128)S(1)}, u32[]{:S(2)}, u32[]{:S(2)}) collective-permute-start(f32[576,128]{1,0:T(8,128)} %get-tuple-element.15), channel_id=1, source_target_pairs={{0,4},{4,0},{8,12},{12,8},{16,20},{20,16},{24,28},{28,24},{1,5},{5... | collective-permute-start | bytes 884744 | tf_op jit(solution)/shard_map/ppermute | solution.py:503
  39.3 13.7 %collective-permute-start.8 = (f32[576,128]{1,0:T(8,128)}, f32[576,128]{1,0:T(8,128)S(1)}, u32[]{:S(2)}, u32[]{:S(2)}) collective-permute-start(f32[576,128]{1,0:T(8,128)} %get-tuple-element.16), channel_id=1, source_target_pairs={{0,24},{4,28},{8,16},{12,20},{16,8},{20,12},{24,0},{28,4},{1,25},{... | collective-permute-start | bytes 884744 | tf_op jit(solution)/shard_map/ppermute | solution.py:503
  41.8 15.7 %collective-permute-start.7 = (f32[576,128]{1,0:T(8,128)}, f32[576,128]{1,0:T(8,128)S(1)}, u32[]{:S(2)}, u32[]{:S(2)}) collective-permute-start(f32[576,128]{1,0:T(8,128)} %get-tuple-element.17), channel_id=1, source_target_pairs={{0,28},{4,24},{8,20},{12,16},{16,12},{20,8},{24,4},{28,0},{1,29},{... | collective-permute-start | bytes 884744 | tf_op jit(solution)/shard_map/ppermute | solution.py:503
  53.5 6.5 %copy-start.3 = (bf16[2048,128]{1,0:T(8,128)(2,1)S(1)}, bf16[2048,128]{1,0:T(8,128)(2,1)}, u32[]{:S(2)}) copy-start(bf16[2048,128]{1,0:T(8,128)(2,1)} %constant.46.clone.gather_ref) | copy-start | bytes 1572868
  53.5 6.5 %copy-start.5 = (f32[72,128]{1,0:T(8,128)S(1)}, f32[72,128]{1,0:T(8,128)}, u32[]{:S(2)}) copy-start(f32[72,128]{1,0:T(8,128)} %equal_ref.5) | copy-start | bytes 110596
  53.5 6.5 %copy-start.6 = (f32[8,128]{1,0:T(8,128)S(1)}, f32[8,128]{1,0:T(8,128)}, u32[]{:S(2)}) copy-start(f32[8,128]{1,0:T(8,128)} %constant.45.clone.sign_ref) | copy-start | bytes 12292
  62.5 2.8 %collective-permute-start.14 = (f32[288,128]{1,0:T(8,128)S(1)}, f32[288,128]{1,0:T(8,128)S(1)}, u32[]{:S(2)}, u32[]{:S(2)}) collective-permute-start(f32[288,128]{1,0:T(8,128)S(1)} %contract.4), channel_id=1, source_target_pairs={{0,4},{4,0},{8,12},{12,8},{16,20},{20,16},{24,28},{28,24},{1,5},{5... | collective-permute-start | bytes 442376 | tf_op jit(solution)/shard_map/ppermute | solution.py:503
  65.3 4.9 %collective-permute-start.15 = (f32[72,128]{1,0:T(8,128)S(1)}, f32[72,128]{1,0:T(8,128)S(1)}, u32[]{:S(2)}, u32[]{:S(2)}) collective-permute-start(f32[72,128]{1,0:T(8,128)S(1)} %get-tuple-element.27), channel_id=1, source_target_pairs={{0,24},{4,28},{8,16},{12,20},{16,8},{20,12},{24,0},{28,4},{1,25},{... | collective-permute-start | bytes 110600 | tf_op jit(solution)/shard_map/ppermute | solution.py:503
  68.0 4.0 %collective-permute-start.16 = (f32[72,128]{1,0:T(8,128)S(1)}, f32[72,128]{1,0:T(8,128)S(1)}, u32[]{:S(2)}, u32[]{:S(2)}) collective-permute-start(f32[72,128]{1,0:T(8,128)S(1)} %get-tuple-element.25), channel_id=1, source_target_pairs={{0,16},{4,20},{8,24},{12,28},{16,0},{20,4},{24,8},{28,12},{1,17},{... | collective-permute-start | bytes 110600 | tf_op jit(solution)/shard_map/ppermute | solution.py:503
  68.5 4.0 %collective-permute-start.17 = (f32[72,128]{1,0:T(8,128)S(1)}, f32[72,128]{1,0:T(8,128)S(1)}, u32[]{:S(2)}, u32[]{:S(2)}) collective-permute-start(f32[72,128]{1,0:T(8,128)S(1)} %get-tuple-element.26), channel_id=1, source_target_pairs={{0,8},{4,12},{8,0},{12,4},{16,24},{20,28},{24,16},{28,20},{1,9},{5... | collective-permute-start | bytes 110600 | tf_op jit(solution)/shard_map/ppermute | solution.py:503
  72.5 8.6 %copy-start.7 = (f32[72,128]{1,0:T(8,128)S(1)}, f32[72,128]{1,0:T(8,128)}, u32[]{:S(2)}) copy-start(f32[72,128]{1,0:T(8,128)} %param.16) | copy-start | bytes 110596
  72.5 8.6 %copy-start.4 = (bf16[256,2048]{1,0:T(8,128)(2,1)S(1)}, bf16[256,2048]{1,0:T(8,128)(2,1)}, u32[]{:S(2)}) copy-start(bf16[256,2048]{1,0:T(8,128)(2,1)} %constant.47.clone.spread_ref) | copy-start | bytes 3145732
  72.5 5.9 %collective-permute-start.18 = (f32[72,128]{1,0:T(8,128)S(1)}, f32[72,128]{1,0:T(8,128)S(1)}, u32[]{:S(2)}, u32[]{:S(2)}) collective-permute-start(f32[72,128]{1,0:T(8,128)S(1)} %slice_add_fusion.1), channel_id=1, source_target_pairs={{0,3},{1,2},{2,1},{3,0},{4,7},{5,6},{6,5},{7,4},{8,11},{9,10},{10,... | collective-permute-start | bytes 110600 | tf_op jit(solution)/shard_map/ppermute | solution.py:503
  76.2 4.9 %collective-permute-start.19 = (f32[72,128]{1,0:T(8,128)S(1)}, f32[72,128]{1,0:T(8,128)S(1)}, u32[]{:S(2)}, u32[]{:S(2)}) collective-permute-start(f32[72,128]{1,0:T(8,128)S(1)} %slice_add_fusion.1), channel_id=1, source_target_pairs={{0,2},{1,3},{2,0},{3,1},{4,6},{5,7},{6,4},{7,5},{8,10},{9,11},{10,... | collective-permute-start | bytes 110600 | tf_op jit(solution)/shard_map/ppermute | solution.py:503
  76.2 4.9 %collective-permute-start.20 = (f32[72,128]{1,0:T(8,128)S(1)}, f32[72,128]{1,0:T(8,128)S(1)}, u32[]{:S(2)}, u32[]{:S(2)}) collective-permute-start(f32[72,128]{1,0:T(8,128)S(1)} %slice_add_fusion.1), channel_id=1, source_target_pairs={{0,1},{1,0},{2,3},{3,2},{4,5},{5,4},{6,7},{7,6},{8,9},{9,8},{10,11... | collective-permute-start | bytes 110600 | tf_op jit(solution)/shard_map/ppermute | solution.py:503

commit v14 on v13

--- a/solution.py
+++ b/solution.py
@@ -126,8 +126,9 @@
     def write(k):
         green = times_of(green_ref, k)
         high = green.astype(jnp.bfloat16)
-        split_ref[k, :history, :] = high
-        split_ref[k, history:, :] = (green - high.astype(jnp.float32)).astype(jnp.bfloat16)
+        low = (green - high.astype(jnp.float32)).astype(jnp.bfloat16)
+        for n, part in enumerate((high, low, high)):
+            split_ref[k, :, n * WIDTH : (n + 1) * WIDTH] = part
 
     if points % TILE:
         for k in range(points):
@@ -293,7 +294,10 @@
         parts = [
             jnp.where(same, jnp.broadcast_to(factor[n : n + 1], same.shape), 0.0) for factor in factors
         ]
-        return split(jnp.concatenate(parts, axis=0))
+        whole = jnp.concatenate(parts, axis=0)
+        high = whole.astype(jnp.bfloat16)
+        low = (whole - high.astype(jnp.float32)).astype(jnp.bfloat16)
+        return jnp.concatenate([high, high, low], axis=0)
 
     def advance(number, slot):
         start = number * tile if points == tile else pl.multiple_of(number * tile, TILE)
@@ -302,8 +306,7 @@
         ]
         for n in range(tile):
             k = number * tile + n
-            both = jnp.dot(split_ref[k], matrix(factors, n), preferred_element_type=jnp.float32)
-            added = both[:history, :WIDTH] + (both[:history, WIDTH:] + both[history:, :WIDTH])
+            added = jnp.dot(split_ref[k], matrix(factors, n), preferred_element_type=jnp.float32)
             result = times_of(green_ref, k) + added
             if points % TILE:
                 held_ref[slot, :, n, :] = result
@@ -461,7 +464,7 @@
     history, points, width = greens.shape
     return pl.pallas_call(
         split_kernel,
-        out_shape=jax.ShapeDtypeStruct((points, 2 * history, width), jnp.bfloat16),
+        out_shape=jax.ShapeDtypeStruct((points, history, 3 * width), jnp.bfloat16),
         in_specs=[in_vmem()],
         out_specs=in_vmem(),
         compiler_params=params(4),

time: 86.5 us -> 86.5 us (level)
  no operation moved by 1% of the time
where the time goes in v14:
time: 86.5 us; the launch traced here: 86.3 us
  waiting for transfers between devices  35.6 us (41%)
  starting transfers between devices  22.9 us (26%)
  Pallas kernels  22.6 us (26%)
  local copies, waits for them, and re-layouts  4.09 us (5%)
  between operations  0.87 us (1%)
    ppermute x21, waiting for transfers between devices, exchange(): return lax.ppermute(value, axis, pairs)  35.6 us
    ppermute x21, starting transfers between devices, exchange(): return lax.ppermute(value, axis, pairs)  22.9 us
    pallas_call x1, Pallas kernels, forward(): pl.pallas_call(functools.partial(forward_kernel, steps, parts), out_shape...  5.62 us
    pallas_call x1, Pallas kernels, propagate(): pl.pallas_call(propagate_kernel, out_shape=jax.ShapeDtypeStruct(greens.sh...  5.3 us
    pallas_call x3, Pallas kernels, contract(): pl.pallas_call(functools.partial(contract_kernel, share), out_shape=jax.S...  5.27 us
    dynamic_slice x2, local copies, waits for them, and re-layouts, per_device(): block = lax.dynamic_slice_in_dim(whole, start, TILE * local)  3.88 us
    pallas_call x2, Pallas kernels, early_lines(): pl.pallas_call(functools.partial(early_kernel, steps, parts), out_shape=j...  3.19 us
    pallas_call x1, Pallas kernels, sigma_of(): pl.pallas_call(functools.partial(sigma_kernel, steps, parts), out_shape=[...  2.46 us
  transfers between devices with their start and end apart: 21, of which 13 were waited for; matrix products, arithmetic and copies ran while one was open for 2% of the time, Pallas kernels for 14%

profile of v14, /device:TPU:0, one launch (start us, length us, event | category | flops | bytes accessed | tf_op | source)
XLA Modules:
  0.0 86.3 jit_solution(8446025452505073124)
XLA Ops:
  0.0 2.6 %constant_dynamic-slice_fusion.7 = (f32[576,128]{1,0:T(8,128)}, f32[576,128]{1,0:T(8,128)}, f32[576,128]{1,0:T(8,128)}, f32[576,128]{1,0:T(8,128)S(1)}, f32[576,...) fusion(f32[4608,128]{1,0:T(8,128)} %bitcast.12, s32[]{:T(128)S(6)} %select_n.45, s32[]{:T(128)S(6)} %select_n.44, ...), kind=kLoop, calls=%fused_computation.10 | loop fusion | bytes 4128796 | tf_op jit(solution)/shard_map/dynamic_slice | solution.py:547
  2.6 3.0 %collective-permute-start = (f32[576,128]{1,0:T(8,128)S(1)}, f32[576,128]{1,0:T(8,128)S(1)}, u32[]{:S(2)}, u32[]{:S(2)}) collective-permute-start(f32[576,128]{1,0:T(8,128)S(1)} %get-tuple-element.24), channel_id=1, source_target_pairs={{0,16},{4,20},{8,24},{12,28},{16,0},{20,4},{24,8},{28,12},{1,17},{... | collective-permute-start | bytes 884744 | tf_op jit(solution)/shard_map/ppermute | solution.py:506
  5.6 1.5 %collective-permute-start.1 = (f32[576,128]{1,0:T(8,128)S(1)}, f32[576,128]{1,0:T(8,128)S(1)}, u32[]{:S(2)}, u32[]{:S(2)}) collective-permute-start(f32[576,128]{1,0:T(8,128)S(1)} %get-tuple-element.23), channel_id=1, source_target_pairs={{0,8},{4,12},{8,0},{12,4},{16,24},{20,28},{24,16},{28,20},{1,9},{5... | collective-permute-start | bytes 884744 | tf_op jit(solution)/shard_map/ppermute | solution.py:506
  7.1 0.3 collective-permute-start.3
  7.5 0.3 collective-permute-start.4
  7.8 1.3 %constant_dynamic-slice_fusion = (f32[576,128]{1,0:T(8,128)}, f32[576,128]{1,0:T(8,128)}, f32[576,128]{1,0:T(8,128)}, f32[576,128]{1,0:T(8,128)}, f32[576,128]{1...) fusion(f32[4608,128]{1,0:T(8,128)S(1)} %bitcast.14, s32[]{:T(128)S(6)} %select_n.42, s32[]{:T(128)S(6)} %select_n.41, ...), kind=kLoop, calls=%fused_computation.3 | loop fusion | bytes 4128796 | tf_op jit(solution)/shard_map/dynamic_slice | solution.py:547
  9.1 4.4 %collective-permute-done.refs_1_ = f32[576,128]{1,0:T(8,128)S(1)} collective-permute-done((f32[576,128]{1,0:T(8,128)S(1)}, f32[576,128]{1,0:T(8,128)S(1)}, u32[]{:S(2)}, u32[]{:S(2)}) %collective-permute-start) | collective-permute-done | bytes 294944 | tf_op jit(solution)/shard_map/ppermute | solution.py:506
  13.5 3.0 %collective-permute-start.5 = (f32[576,128]{1,0:T(8,128)}, f32[576,128]{1,0:T(8,128)}, u32[]{:S(2)}, u32[]{:S(2)}) collective-permute-start(f32[576,128]{1,0:T(8,128)} %get-tuple-element.19), channel_id=1, source_target_pairs={{0,24},{4,28},{8,16},{12,20},{16,8},{20,12},{24,0},{28,4},{1,25},{... | collective-permute-start | bytes 884744 | tf_op jit(solution)/shard_map/ppermute | solution.py:506
  16.5 1.9 %collective-permute-done.2.refs_3_ = f32[576,128]{1,0:T(8,128)S(1)} collective-permute-done((f32[576,128]{1,0:T(8,128)S(1)}, f32[576,128]{1,0:T(8,128)S(1)}, u32[]{:S(2)}, u32[]{:S(2)}) %collective-permute-start.2) | collective-permute-done | bytes 294944 | tf_op jit(solution)/shard_map/ppermute | solution.py:506
  18.3 1.2 %collective-permute-start.10 = (f32[576,128]{1,0:T(8,128)}, f32[576,128]{1,0:T(8,128)}, u32[]{:S(2)}, u32[]{:S(2)}) collective-permute-start(f32[576,128]{1,0:T(8,128)} %get-tuple-element.14), channel_id=1, source_target_pairs={{0,16},{4,20},{8,24},{12,28},{16,0},{20,4},{24,8},{28,12},{1,17},{... | collective-permute-start | bytes 884744 | tf_op jit(solution)/shard_map/ppermute | solution.py:506
  19.5 1.3 %collective-permute-done.3.refs_4_ = f32[576,128]{1,0:T(8,128)S(1)} collective-permute-done((f32[576,128]{1,0:T(8,128)S(1)}, f32[576,128]{1,0:T(8,128)S(1)}, u32[]{:S(2)}, u32[]{:S(2)}) %collective-permute-start.3) | collective-permute-done | bytes 294944 | tf_op jit(solution)/shard_map/ppermute | solution.py:506
  20.9 0.5 collective-permute-start.11
  22.1 0.1 select_reduce_fusion
  22.2 1.7 %collective-permute-start.12 = (f32[576,128]{1,0:T(8,128)}, f32[576,128]{1,0:T(8,128)S(1)}, u32[]{:S(2)}, u32[]{:S(2)}) collective-permute-start(f32[576,128]{1,0:T(8,128)} %get-tuple-element.12), channel_id=1, source_target_pairs={{0,20},{4,16},{8,28},{12,24},{16,4},{20,0},{24,12},{28,8},{1,21},{... | collective-permute-start | bytes 884744 | tf_op jit(solution)/shard_map/ppermute | solution.py:506
  23.9 4.0 %collective-permute-done.5.refs_6_ = f32[576,128]{1,0:T(8,128)} collective-permute-done((f32[576,128]{1,0:T(8,128)}, f32[576,128]{1,0:T(8,128)}, u32[]{:S(2)}, u32[]{:S(2)}) %collective-permute-start.5) | collective-permute-done | bytes 294944 | tf_op jit(solution)/shard_map/ppermute | solution.py:506
  27.9 5.8 %collective-permute-done.6.refs_7_ = f32[576,128]{1,0:T(8,128)} collective-permute-done((f32[576,128]{1,0:T(8,128)}, f32[576,128]{1,0:T(8,128)}, u32[]{:S(2)}, u32[]{:S(2)}) %collective-permute-start.6) | collective-permute-done | bytes 294944 | tf_op jit(solution)/shard_map/ppermute | solution.py:506
  33.7 0.3 collective-permute-start.9
  34.0 5.3 %collective-permute-done.10.refs_2_ = f32[576,128]{1,0:T(8,128)} collective-permute-done((f32[576,128]{1,0:T(8,128)}, f32[576,128]{1,0:T(8,128)}, u32[]{:S(2)}, u32[]{:S(2)}) %collective-permute-start.10) | collective-permute-done | bytes 294944 | tf_op jit(solution)/shard_map/ppermute | solution.py:506
  39.3 2.5 %collective-permute-start.8 = (f32[576,128]{1,0:T(8,128)}, f32[576,128]{1,0:T(8,128)S(1)}, u32[]{:S(2)}, u32[]{:S(2)}) collective-permute-start(f32[576,128]{1,0:T(8,128)} %get-tuple-element.16), channel_id=1, source_target_pairs={{0,24},{4,28},{8,16},{12,20},{16,8},{20,12},{24,0},{28,4},{1,25},{... | collective-permute-start | bytes 884744 | tf_op jit(solution)/shard_map/ppermute | solution.py:506
  41.8 0.1 dynamic_slice.52
  41.8 0.1 pad_add_fusion.1.owner_ref
  41.9 5.6 %forward.1 = (f32[576,8,128]{2,1,0:T(8,128)S(1)}, f32[4,4608,128]{2,1,0:T(8,128)S(1)}) custom-call(s32[1]{0:T(128)} %bitcast.3.place_ref.owner_ref, f32[4608,128]{1,0:T(8,128)S(1)} %bitcast.13, f32[576,128]{1,0:T(8,128)S(1)} %collective-permute-done.refs_1_, f32[576,128]{1,0:T(8,128)S(1)} %collective-permute-done.1.refs_2_, ...), custom_call_target="tpu_custom_call" | custom-call | flops 235929600 | bytes 14155776 | tf_op jit(solution)/shard_map/forward/pallas_call | solution.py:391
  47.6 0.1 squeeze.9.weight_ref
  47.7 2.7 %early.2.refs_1_ = f32[576,8,128]{2,1,0:T(8,128)S(1)} custom-call(s32[1]{0:T(128)} %bitcast.3.place_ref.owner_ref, f32[576,8,128]{2,1,0:T(8,128)S(1)} %get-tuple-element.8.lattice_ref, f32[8,128]{1,0:T(8,128)S(1)} %squeeze.9.weight_ref, f32[576,128]{1,0:T(8,128)S(1)} %collective-permute-done.9.refs_0_, f32[4608,128]{1,0:T(8,128)S(1)} %bitcast.15, ...), custom_call_target="tpu_custom_call" | custom-call | flops 88473600 | bytes 7077888 | tf_op jit(solution)/shard_map/early/pallas_call | solution.py:409
  50.4 2.6 %collective-permute-done.8.refs_0_ = f32[576,128]{1,0:T(8,128)S(1)} collective-permute-done((f32[576,128]{1,0:T(8,128)}, f32[576,128]{1,0:T(8,128)S(1)}, u32[]{:S(2)}, u32[]{:S(2)}) %collective-permute-start.8) | collective-permute-done | bytes 294944 | tf_op jit(solution)/shard_map/ppermute | solution.py:506
  53.0 0.5 early.3.refs_1_
  53.5 0.0 copy-start.3
  53.5 0.0 copy-start.6
  53.5 4.0 %collective-permute-done.7.refs_0_ = f32[576,128]{1,0:T(8,128)S(1)} collective-permute-done((f32[576,128]{1,0:T(8,128)}, f32[576,128]{1,0:T(8,128)S(1)}, u32[]{:S(2)}, u32[]{:S(2)}) %collective-permute-start.7) | collective-permute-done | bytes 294944 | tf_op jit(solution)/shard_map/ppermute | solution.py:506
  57.5 2.5 %sigma.1 = (f32[576,8,128]{2,1,0:T(8,128)S(1)}, f32[4608,128]{1,0:T(8,128)S(1)}) custom-call(s32[1]{0:T(128)} %bitcast.3.place_ref.owner_ref, f32[576,8,128]{2,1,0:T(8,128)S(1)} %get-tuple-element.8.lattice_ref, f32[8,128]{1,0:T(8,128)S(1)} %squeeze.9.weight_ref, f32[576,128]{1,0:T(8,128)S(1)} %collective-permute-done.7.refs_0_, ...), custom_call_target="tpu_custom_call", output_to_operand_aliasing={{0}: (4, {})} | custom-call | flops 117964800 | bytes 14155776 | tf_op jit(solution)/shard_map/sigma/pallas_call | solution.py:427
  60.0 2.5 %contract.4 = f32[288,128]{1,0:T(8,128)S(1)} custom-call(s32[4]{0:T(128)S(1)} %pad_add_fusion.1.owner_ref, f32[4608,128]{1,0:T(8,128)S(1)} %get-tuple-element.9.sigma_ref, f32[72,128]{1,0:T(8,128)S(1)} %copy-done.5, f32[8,128]{1,0:T(8,128)S(1)} %copy-done.6, bf16[2048,128]{1,0:T(8,128)(2,1)S(1)} %copy-done.3, f32[4,4608,128]{2,1,0:T(8,128)S(1)} %get-tuple-element.10.greens_ref), custom_call_target="tpu_custom_call" | custom-call | flops 165150720 | bytes 14155776 | tf_op jit(solution)/shard_map/contract/pallas_call | solution.py:448
  62.5 0.6 collective-permute-start.14
  63.1 0.1 pad_add_fusion.owner_ref
  63.2 2.1 %contract.3 = f32[216,128]{1,0:T(8,128)S(1)} custom-call(s32[3]{0:T(128)S(1)} %pad_add_fusion.owner_ref, f32[4608,128]{1,0:T(8,128)S(1)} %get-tuple-element.9.sigma_ref, f32[72,128]{1,0:T(8,128)S(1)} %copy-done.5, f32[8,128]{1,0:T(8,128)S(1)} %copy-done.6, bf16[2048,128]{1,0:T(8,128)(2,1)S(1)} %copy-done.3, f32[4,4608,128]{2,1,0:T(8,128)S(1)} %get-tuple-element.10.greens_ref), custom_call_target="tpu_custom_call" | custom-call | flops 123863040 | bytes 14155776 | tf_op jit(solution)/shard_map/contract/pallas_call | solution.py:448
  65.3 2.6 %collective-permute-start.15 = (f32[72,128]{1,0:T(8,128)S(1)}, f32[72,128]{1,0:T(8,128)S(1)}, u32[]{:S(2)}, u32[]{:S(2)}) collective-permute-start(f32[72,128]{1,0:T(8,128)S(1)} %get-tuple-element.27), channel_id=1, source_target_pairs={{0,24},{4,28},{8,16},{12,20},{16,8},{20,12},{24,0},{28,4},{1,25},{... | collective-permute-start | bytes 110600 | tf_op jit(solution)/shard_map/ppermute | solution.py:506
  68.0 0.5 collective-permute-start.16
  68.5 0.4 collective-permute-start.17
  68.9 1.4 %collective-permute-done.15.refs_0_ = f32[72,128]{1,0:T(8,128)S(1)} collective-permute-done((f32[72,128]{1,0:T(8,128)S(1)}, f32[72,128]{1,0:T(8,128)S(1)}, u32[]{:S(2)}, u32[]{:S(2)}) %collective-permute-start.15) | collective-permute-done | bytes 36896 | tf_op jit(solution)/shard_map/ppermute | solution.py:506
  70.2 0.6 contract.5
  70.9 1.0 %collective-permute-done.16 = f32[72,128]{1,0:T(8,128)S(1)} collective-permute-done((f32[72,128]{1,0:T(8,128)S(1)}, f32[72,128]{1,0:T(8,128)S(1)}, u32[]{:S(2)}, u32[]{:S(2)}) %collective-permute-start.16) | collective-permute-done | bytes 36896 | tf_op jit(solution)/shard_map/ppermute | solution.py:506
  71.9 0.5 collective-permute-done.17
  72.5 0.0 copy-start.4
  72.5 3.7 %collective-permute-start.18 = (f32[72,128]{1,0:T(8,128)S(1)}, f32[72,128]{1,0:T(8,128)S(1)}, u32[]{:S(2)}, u32[]{:S(2)}) collective-permute-start(f32[72,128]{1,0:T(8,128)S(1)} %slice_add_fusion.1), channel_id=1, source_target_pairs={{0,3},{1,2},{2,1},{3,0},{4,7},{5,6},{6,5},{7,4},{8,11},{9,10},{10,... | collective-permute-start | bytes 110600 | tf_op jit(solution)/shard_map/ppermute | solution.py:506
  76.2 0.8 collective-permute-start.20
  76.9 0.8 split_own.1.split_ref
  77.7 0.7 collective-permute-done.18
  78.4 2.6 %collective-permute-done.19 = f32[72,128]{1,0:T(8,128)S(1)} collective-permute-done((f32[72,128]{1,0:T(8,128)S(1)}, f32[72,128]{1,0:T(8,128)S(1)}, u32[]{:S(2)}, u32[]{:S(2)}) %collective-permute-start.19) | collective-permute-done | bytes 36896 | tf_op jit(solution)/shard_map/ppermute | solution.py:506
  81.0 5.3 %propagate.1 = f32[64,72,128]{2,1,0:T(8,128)} custom-call(f32[64,72,128]{2,1,0:T(8,128)S(1)} %copy-done, bf16[72,64,384]{2,1,0:T(8,128)(2,1)S(1)} %split_own.1.split_ref, f32[72,128]{1,0:T(8,128)S(1)} %add_add_fusion.effective_ref, bf16[256,2048]{1,0:T(8,128)(2,1)S(1)} %copy-done.4), custom_call_target="tpu_custom_call" | custom-call | flops 18874368 | bytes 11796480 | tf_op jit(solution)/shard_map/propagate/pallas_call | solution.py:480
  (35 shorter events, 0.1 us)
Async XLA Ops:
  0.0 7.8 %copy-start.1 = (f32[64,72,128]{2,1,0:T(8,128)S(1)}, f32[64,72,128]{2,1,0:T(8,128)}, u32[]{:S(2)}) copy-start(f32[64,72,128]{2,1,0:T(8,128)} %param.15) | copy-start | bytes 7077892
  2.6 19.5 %copy-start.8 = (s32[64]{0:T(128)S(1)}, s32[64]{0:T(128)}, u32[]{:S(2)}) copy-start(s32[64]{0:T(128)} %param.18) | copy-start | bytes 772
  2.6 19.5 %copy-start.9 = (f32[4]{0:T(128)S(1)}, f32[4]{0:T(128)}, u32[]{:S(2)}) copy-start(f32[4]{0:T(128)} %constant.44.clone) | copy-start | bytes 52
  2.6 39.3 %copy-start = (f32[64,72,128]{2,1,0:T(8,128)S(1)}, f32[64,72,128]{2,1,0:T(8,128)}, u32[]{:S(2)}) copy-start(f32[64,72,128]{2,1,0:T(8,128)} %green_ref.3) | copy-start | bytes 7077892
  2.6 10.9 %collective-permute-start = (f32[576,128]{1,0:T(8,128)S(1)}, f32[576,128]{1,0:T(8,128)S(1)}, u32[]{:S(2)}, u32[]{:S(2)}) collective-permute-start(f32[576,128]{1,0:T(8,128)S(1)} %get-tuple-element.24), channel_id=1, source_target_pairs={{0,16},{4,20},{8,24},{12,28},{16,0},{20,4},{24,8},{28,12},{1,17},{... | collective-permute-start | bytes 884744 | tf_op jit(solution)/shard_map/ppermute | solution.py:506
  5.6 10.8 %collective-permute-start.1 = (f32[576,128]{1,0:T(8,128)S(1)}, f32[576,128]{1,0:T(8,128)S(1)}, u32[]{:S(2)}, u32[]{:S(2)}) collective-permute-start(f32[576,128]{1,0:T(8,128)S(1)} %get-tuple-element.23), channel_id=1, source_target_pairs={{0,8},{4,12},{8,0},{12,4},{16,24},{20,28},{24,16},{28,20},{1,9},{5... | collective-permute-start | bytes 884744 | tf_op jit(solution)/shard_map/ppermute | solution.py:506
  7.1 11.2 %collective-permute-start.2 = (f32[576,128]{1,0:T(8,128)S(1)}, f32[576,128]{1,0:T(8,128)S(1)}, u32[]{:S(2)}, u32[]{:S(2)}) collective-permute-start(f32[576,128]{1,0:T(8,128)S(1)} %get-tuple-element.22), channel_id=1, source_target_pairs={{0,20},{4,16},{8,28},{12,24},{16,4},{20,0},{24,12},{28,8},{1,21},{... | collective-permute-start | bytes 884744 | tf_op jit(solution)/shard_map/ppermute | solution.py:506
  7.1 13.8 %collective-permute-start.3 = (f32[576,128]{1,0:T(8,128)S(1)}, f32[576,128]{1,0:T(8,128)S(1)}, u32[]{:S(2)}, u32[]{:S(2)}) collective-permute-start(f32[576,128]{1,0:T(8,128)S(1)} %get-tuple-element.21), channel_id=1, source_target_pairs={{0,12},{4,8},{8,4},{12,0},{16,28},{20,24},{24,20},{28,16},{1,13},{... | collective-permute-start | bytes 884744 | tf_op jit(solution)/shard_map/ppermute | solution.py:506
  7.5 14.7 %collective-permute-start.4 = (f32[576,128]{1,0:T(8,128)}, f32[576,128]{1,0:T(8,128)}, u32[]{:S(2)}, u32[]{:S(2)}) collective-permute-start(f32[576,128]{1,0:T(8,128)} %get-tuple-element.20), channel_id=1, source_target_pairs={{0,4},{4,0},{8,12},{12,8},{16,20},{20,16},{24,28},{28,24},{1,5},{5... | collective-permute-start | bytes 884744 | tf_op jit(solution)/shard_map/ppermute | solution.py:506
  13.5 14.4 %collective-permute-start.5 = (f32[576,128]{1,0:T(8,128)}, f32[576,128]{1,0:T(8,128)}, u32[]{:S(2)}, u32[]{:S(2)}) collective-permute-start(f32[576,128]{1,0:T(8,128)} %get-tuple-element.19), channel_id=1, source_target_pairs={{0,24},{4,28},{8,16},{12,20},{16,8},{20,12},{24,0},{28,4},{1,25},{... | collective-permute-start | bytes 884744 | tf_op jit(solution)/shard_map/ppermute | solution.py:506
  16.5 17.2 %collective-permute-start.6 = (f32[576,128]{1,0:T(8,128)}, f32[576,128]{1,0:T(8,128)}, u32[]{:S(2)}, u32[]{:S(2)}) collective-permute-start(f32[576,128]{1,0:T(8,128)} %get-tuple-element.18), channel_id=1, source_target_pairs={{0,28},{4,24},{8,20},{12,16},{16,12},{20,8},{24,4},{28,0},{1,29},{... | collective-permute-start | bytes 884744 | tf_op jit(solution)/shard_map/ppermute | solution.py:506
  18.3 20.9 %collective-permute-start.10 = (f32[576,128]{1,0:T(8,128)}, f32[576,128]{1,0:T(8,128)}, u32[]{:S(2)}, u32[]{:S(2)}) collective-permute-start(f32[576,128]{1,0:T(8,128)} %get-tuple-element.14), channel_id=1, source_target_pairs={{0,16},{4,20},{8,24},{12,28},{16,0},{20,4},{24,8},{28,12},{1,17},{... | collective-permute-start | bytes 884744 | tf_op jit(solution)/shard_map/ppermute | solution.py:506
  20.9 20.9 %collective-permute-start.11 = (f32[576,128]{1,0:T(8,128)}, f32[576,128]{1,0:T(8,128)}, u32[]{:S(2)}, u32[]{:S(2)}) collective-permute-start(f32[576,128]{1,0:T(8,128)} %get-tuple-element.13), channel_id=1, source_target_pairs={{0,8},{4,12},{8,0},{12,4},{16,24},{20,28},{24,16},{28,20},{1,9},{5... | collective-permute-start | bytes 884744 | tf_op jit(solution)/shard_map/ppermute | solution.py:506
  22.1 25.6 %copy-start.2 = (f32[64,72,128]{2,1,0:T(8,128)S(1)}, f32[64,72,128]{2,1,0:T(8,128)}, u32[]{:S(2)}) copy-start(f32[64,72,128]{2,1,0:T(8,128)} %param.15) | copy-start | bytes 7077892
  22.2 25.4 %collective-permute-start.12 = (f32[576,128]{1,0:T(8,128)}, f32[576,128]{1,0:T(8,128)S(1)}, u32[]{:S(2)}, u32[]{:S(2)}) collective-permute-start(f32[576,128]{1,0:T(8,128)} %get-tuple-element.12), channel_id=1, source_target_pairs={{0,20},{4,16},{8,28},{12,24},{16,4},{20,0},{24,12},{28,8},{1,21},{... | collective-permute-start | bytes 884744 | tf_op jit(solution)/shard_map/ppermute | solution.py:506
  27.9 19.7 %collective-permute-start.13 = (f32[576,128]{1,0:T(8,128)}, f32[576,128]{1,0:T(8,128)S(1)}, u32[]{:S(2)}, u32[]{:S(2)}) collective-permute-start(f32[576,128]{1,0:T(8,128)} %get-tuple-element.11), channel_id=1, source_target_pairs={{0,12},{4,8},{8,4},{12,0},{16,28},{20,24},{24,20},{28,16},{1,13},{... | collective-permute-start | bytes 884744 | tf_op jit(solution)/shard_map/ppermute | solution.py:506
  33.7 13.9 %collective-permute-start.9 = (f32[576,128]{1,0:T(8,128)}, f32[576,128]{1,0:T(8,128)S(1)}, u32[]{:S(2)}, u32[]{:S(2)}) collective-permute-start(f32[576,128]{1,0:T(8,128)} %get-tuple-element.15), channel_id=1, source_target_pairs={{0,4},{4,0},{8,12},{12,8},{16,20},{20,16},{24,28},{28,24},{1,5},{5... | collective-permute-start | bytes 884744 | tf_op jit(solution)/shard_map/ppermute | solution.py:506
  39.3 13.7 %collective-permute-start.8 = (f32[576,128]{1,0:T(8,128)}, f32[576,128]{1,0:T(8,128)S(1)}, u32[]{:S(2)}, u32[]{:S(2)}) collective-permute-start(f32[576,128]{1,0:T(8,128)} %get-tuple-element.16), channel_id=1, source_target_pairs={{0,24},{4,28},{8,16},{12,20},{16,8},{20,12},{24,0},{28,4},{1,25},{... | collective-permute-start | bytes 884744 | tf_op jit(solution)/shard_map/ppermute | solution.py:506
  41.8 15.7 %collective-permute-start.7 = (f32[576,128]{1,0:T(8,128)}, f32[576,128]{1,0:T(8,128)S(1)}, u32[]{:S(2)}, u32[]{:S(2)}) collective-permute-start(f32[576,128]{1,0:T(8,128)} %get-tuple-element.17), channel_id=1, source_target_pairs={{0,28},{4,24},{8,20},{12,16},{16,12},{20,8},{24,4},{28,0},{1,29},{... | collective-permute-start | bytes 884744 | tf_op jit(solution)/shard_map/ppermute | solution.py:506
  53.5 6.5 %copy-start.3 = (bf16[2048,128]{1,0:T(8,128)(2,1)S(1)}, bf16[2048,128]{1,0:T(8,128)(2,1)}, u32[]{:S(2)}) copy-start(bf16[2048,128]{1,0:T(8,128)(2,1)} %constant.46.clone.gather_ref) | copy-start | bytes 1572868
  53.5 6.5 %copy-start.5 = (f32[72,128]{1,0:T(8,128)S(1)}, f32[72,128]{1,0:T(8,128)}, u32[]{:S(2)}) copy-start(f32[72,128]{1,0:T(8,128)} %equal_ref.5) | copy-start | bytes 110596
  53.5 6.5 %copy-start.6 = (f32[8,128]{1,0:T(8,128)S(1)}, f32[8,128]{1,0:T(8,128)}, u32[]{:S(2)}) copy-start(f32[8,128]{1,0:T(8,128)} %constant.45.clone.sign_ref) | copy-start | bytes 12292
  62.5 2.8 %collective-permute-start.14 = (f32[288,128]{1,0:T(8,128)S(1)}, f32[288,128]{1,0:T(8,128)S(1)}, u32[]{:S(2)}, u32[]{:S(2)}) collective-permute-start(f32[288,128]{1,0:T(8,128)S(1)} %contract.4), channel_id=1, source_target_pairs={{0,4},{4,0},{8,12},{12,8},{16,20},{20,16},{24,28},{28,24},{1,5},{5... | collective-permute-start | bytes 442376 | tf_op jit(solution)/shard_map/ppermute | solution.py:506
  65.3 4.9 %collective-permute-start.15 = (f32[72,128]{1,0:T(8,128)S(1)}, f32[72,128]{1,0:T(8,128)S(1)}, u32[]{:S(2)}, u32[]{:S(2)}) collective-permute-start(f32[72,128]{1,0:T(8,128)S(1)} %get-tuple-element.27), channel_id=1, source_target_pairs={{0,24},{4,28},{8,16},{12,20},{16,8},{20,12},{24,0},{28,4},{1,25},{... | collective-permute-start | bytes 110600 | tf_op jit(solution)/shard_map/ppermute | solution.py:506
  68.0 4.0 %collective-permute-start.16 = (f32[72,128]{1,0:T(8,128)S(1)}, f32[72,128]{1,0:T(8,128)S(1)}, u32[]{:S(2)}, u32[]{:S(2)}) collective-permute-start(f32[72,128]{1,0:T(8,128)S(1)} %get-tuple-element.25), channel_id=1, source_target_pairs={{0,16},{4,20},{8,24},{12,28},{16,0},{20,4},{24,8},{28,12},{1,17},{... | collective-permute-start | bytes 110600 | tf_op jit(solution)/shard_map/ppermute | solution.py:506
  68.5 4.0 %collective-permute-start.17 = (f32[72,128]{1,0:T(8,128)S(1)}, f32[72,128]{1,0:T(8,128)S(1)}, u32[]{:S(2)}, u32[]{:S(2)}) collective-permute-start(f32[72,128]{1,0:T(8,128)S(1)} %get-tuple-element.26), channel_id=1, source_target_pairs={{0,8},{4,12},{8,0},{12,4},{16,24},{20,28},{24,16},{28,20},{1,9},{5... | collective-permute-start | bytes 110600 | tf_op jit(solution)/shard_map/ppermute | solution.py:506
  72.5 8.6 %copy-start.7 = (f32[72,128]{1,0:T(8,128)S(1)}, f32[72,128]{1,0:T(8,128)}, u32[]{:S(2)}) copy-start(f32[72,128]{1,0:T(8,128)} %param.16) | copy-start | bytes 110596
  72.5 8.6 %copy-start.4 = (bf16[256,2048]{1,0:T(8,128)(2,1)S(1)}, bf16[256,2048]{1,0:T(8,128)(2,1)}, u32[]{:S(2)}) copy-start(bf16[256,2048]{1,0:T(8,128)(2,1)} %constant.47.clone.spread_ref) | copy-start | bytes 3145732
  72.5 5.9 %collective-permute-start.18 = (f32[72,128]{1,0:T(8,128)S(1)}, f32[72,128]{1,0:T(8,128)S(1)}, u32[]{:S(2)}, u32[]{:S(2)}) collective-permute-start(f32[72,128]{1,0:T(8,128)S(1)} %slice_add_fusion.1), channel_id=1, source_target_pairs={{0,3},{1,2},{2,1},{3,0},{4,7},{5,6},{6,5},{7,4},{8,11},{9,10},{10,... | collective-permute-start | bytes 110600 | tf_op jit(solution)/shard_map/ppermute | solution.py:506
  76.2 4.9 %collective-permute-start.19 = (f32[72,128]{1,0:T(8,128)S(1)}, f32[72,128]{1,0:T(8,128)S(1)}, u32[]{:S(2)}, u32[]{:S(2)}) collective-permute-start(f32[72,128]{1,0:T(8,128)S(1)} %slice_add_fusion.1), channel_id=1, source_target_pairs={{0,2},{1,3},{2,0},{3,1},{4,6},{5,7},{6,4},{7,5},{8,10},{9,11},{10,... | collective-permute-start | bytes 110600 | tf_op jit(solution)/shard_map/ppermute | solution.py:506
  76.2 4.9 %collective-permute-start.20 = (f32[72,128]{1,0:T(8,128)S(1)}, f32[72,128]{1,0:T(8,128)S(1)}, u32[]{:S(2)}, u32[]{:S(2)}) collective-permute-start(f32[72,128]{1,0:T(8,128)S(1)} %slice_add_fusion.1), channel_id=1, source_target_pairs={{0,1},{1,0},{2,3},{3,2},{4,5},{5,4},{6,7},{7,6},{8,9},{9,8},{10,11... | collective-permute-start | bytes 110600 | tf_op jit(solution)/shard_map/ppermute | solution.py:506

commit v15 on v14

--- a/solution.py
+++ b/solution.py
@@ -113,6 +113,18 @@
     lax.fori_loop(0, SIDE // 2, columns, 0)
 
 
+def pick_kernel(steps, parts, place_ref, whole_ref, *refs):
+    block_refs, sems = refs[-1 - len(steps) : -1], refs[-1]
+    copies = []
+    for n, (step, block_ref) in enumerate(zip(steps, block_refs)):
+        rows = block_ref.shape[0]
+        start = pl.multiple_of(partner_of(place_ref[0], step, parts) * rows, TILE)
+        copies.append(pltpu.make_async_copy(whole_ref.at[pl.ds(start, rows)], block_ref, sems.at[n]))
+        copies[-1].start()
+    for copy in copies:
+        copy.wait()
+
+
 def times_of(ref, k):
     history, points, width = ref.shape
     if points % TILE:
@@ -460,6 +472,20 @@
     )(owners, sigma, equal_time, jnp.asarray(signs), jnp.asarray(gather), greens, *before)
 
 
+def pick(place, whole, steps, parts, before=()):
+    rows, width = whole.shape[0] // parts, whole.shape[1]
+    return pl.pallas_call(
+        functools.partial(pick_kernel, steps, parts),
+        out_shape=[jax.ShapeDtypeStruct((rows, width), whole.dtype)] * len(steps),
+        in_specs=[in_smem(), anywhere()] + [anywhere()] * len(before),
+        out_specs=[in_vmem()] * len(steps),
+        scratch_shapes=[pltpu.SemaphoreType.DMA((len(steps),))],
+        compiler_params=params(56),
+        cost_estimate=cost(0, 2),
+        name="pick",
+    )(place, whole, *before)
+
+
 def split_own(greens):
     history, points, width = greens.shape
     return pl.pallas_call(
@@ -539,14 +565,15 @@
         order = exchange_order(parts)
         moved = []
         wholes = [x.reshape(parts * TILE * local, width) for x in (green_row, screened)]
+        blocks_of_green = [
+            lax.dynamic_slice_in_dim(wholes[0], partner_of(place, step, parts) * (TILE * local), TILE * local)
+            for step in order
+        ]
+        blocks_of_screen = pick(seat, wholes[1], order, parts, blocks_of_green[:1])
         moved = []
-        for whole in wholes:
-            found = {0: whole}
-            for step in order:
-                start = partner_of(place, step, parts) * (TILE * local)
-                block = lax.dynamic_slice_in_dim(whole, start, TILE * local)
-                found[step] = exchange(block, "ka", step, parts)
-            moved.append([found])
+        for whole, sent in zip(wholes, (blocks_of_green, blocks_of_screen)):
+            found = {step: exchange(block, "ka", step, parts) for step, block in zip(order, sent)}
+            moved.append([{0: whole, **found}])
         order = [0] + order
     else:
         groups, sources = -(-times // TILE), 1

time: 86.5 us -> 86.4 us (level)
  Pallas kernels: 22.6 us -> 25.4 us
  waiting for transfers between devices: 35.6 us -> 34 us
  local copies, waits for them, and re-layouts: 4.09 us -> 2.65 us
    pallas_call x0 -> x1, Pallas kernels: none -> 2.83 us  [pick(): pl.pallas_call(functools.partial(pick_kernel, steps, parts), out_shape=[j...]
    ppermute x21, waiting for transfers between devices: 35.6 us -> 34 us  [exchange(): return lax.ppermute(value, axis, pairs)]
    dynamic_slice x2 -> x1, local copies, waits for them, and re-layouts: 3.88 us -> 2.43 us  [per_device(): lax.dynamic_slice_in_dim(wholes[0], partner_of(place, step, parts) * (TIL...]
  transfers between devices with their start and end apart: 21 -> 21, of which waited for: 13 -> 13; matrix products, arithmetic and copies ran while one was open for 2% -> 0% of each run, Pallas kernels for 14% -> 18%
where the time goes in v15:
time: 86.4 us; the launch traced here: 86.2 us
  waiting for transfers between devices  34 us (39%)
  Pallas kernels  25.4 us (29%)
  starting transfers between devices  22.9 us (27%)
  local copies, waits for them, and re-layouts  2.65 us (3%)
  between operations  0.89 us (1%)
    ppermute x21, waiting for transfers between devices, exchange(): return lax.ppermute(value, axis, pairs)  34 us
    ppermute x21, starting transfers between devices, exchange(): return lax.ppermute(value, axis, pairs)  22.9 us
    pallas_call x1, Pallas kernels, forward(): pl.pallas_call(functools.partial(forward_kernel, steps, parts), out_shape...  5.62 us
    pallas_call x1, Pallas kernels, propagate(): pl.pallas_call(propagate_kernel, out_shape=jax.ShapeDtypeStruct(greens.sh...  5.29 us
    pallas_call x3, Pallas kernels, contract(): pl.pallas_call(functools.partial(contract_kernel, share), out_shape=jax.S...  5.27 us
    pallas_call x2, Pallas kernels, early_lines(): pl.pallas_call(functools.partial(early_kernel, steps, parts), out_shape=j...  3.19 us
    pallas_call x1, Pallas kernels, pick(): pl.pallas_call(functools.partial(pick_kernel, steps, parts), out_shape=[j...  2.83 us
    pallas_call x1, Pallas kernels, sigma_of(): pl.pallas_call(functools.partial(sigma_kernel, steps, parts), out_shape=[...  2.46 us
  transfers between devices with their start and end apart: 21, of which 13 were waited for; matrix products, arithmetic and copies ran while one was open for 0% of the time, Pallas kernels for 18%

profile of v15, /device:TPU:0, one launch (start us, length us, event | category | flops | bytes accessed | tf_op | source)
XLA Modules:
  0.0 86.2 jit_solution(3551403639766979744)
XLA Ops:
  0.0 2.4 %constant_dynamic-slice_fusion = (f32[576,128]{1,0:T(8,128)}, f32[576,128]{1,0:T(8,128)}, f32[576,128]{1,0:T(8,128)}, f32[576,128]{1,0:T(8,128)S(1)}, f32[576,12...) fusion(f32[4608,128]{1,0:T(8,128)} %bitcast.12, s32[]{:T(128)S(6)} %select_n.38, s32[]{:T(128)S(6)} %select_n.37, ...), kind=kLoop, calls=%fused_computation.6 | loop fusion | bytes 4128796 | tf_op jit(solution)/shard_map/dynamic_slice | solution.py:569
  2.5 3.0 %collective-permute-start = (f32[576,128]{1,0:T(8,128)S(1)}, f32[576,128]{1,0:T(8,128)S(1)}, u32[]{:S(2)}, u32[]{:S(2)}) collective-permute-start(f32[576,128]{1,0:T(8,128)S(1)} %get-tuple-element.31.refs_0_), channel_id=1, source_target_pairs={{0,16},{4,20},{8,24},{12,28},{16,0},{20,4},{24,8},{28,12},{1,17},{... | collective-permute-start | bytes 884744 | tf_op jit(solution)/shard_map/ppermute | solution.py:532
  5.5 1.5 %collective-permute-start.1 = (f32[576,128]{1,0:T(8,128)S(1)}, f32[576,128]{1,0:T(8,128)S(1)}, u32[]{:S(2)}, u32[]{:S(2)}) collective-permute-start(f32[576,128]{1,0:T(8,128)S(1)} %get-tuple-element.30), channel_id=1, source_target_pairs={{0,8},{4,12},{8,0},{12,4},{16,24},{20,28},{24,16},{28,20},{1,9},{5... | collective-permute-start | bytes 884744 | tf_op jit(solution)/shard_map/ppermute | solution.py:532
  7.0 0.3 collective-permute-start.3
  7.3 0.3 collective-permute-start.4
  7.6 2.8 %pick.1 = (f32[576,128]{1,0:T(8,128)}, f32[576,128]{1,0:T(8,128)}, f32[576,128]{1,0:T(8,128)}, f32[576,128]{1,0:T(8,128)}, f32[576,128]{1,0:T(8,128)}, /*index=5*/f32[576,128]{1,0:T(8,128)}, f32[576,128]{1,0:T(8,128)}) custom-call(s32[1]{0:T(128)} %bitcast.3.place_ref.owner_ref, f32[4608,128]{1,0:T(8,128)} %bitcast.14, f32[576,128]{1,0:T(8,128)} %copy-done.6), custom_call_target="tpu_custom_call" | custom-call | bytes 4718592 | tf_op jit(solution)/shard_map/pick/pallas_call | solution.py:477
  10.5 2.9 %collective-permute-done.refs_1_ = f32[576,128]{1,0:T(8,128)S(1)} collective-permute-done((f32[576,128]{1,0:T(8,128)S(1)}, f32[576,128]{1,0:T(8,128)S(1)}, u32[]{:S(2)}, u32[]{:S(2)}) %collective-permute-start) | collective-permute-done | bytes 294944 | tf_op jit(solution)/shard_map/ppermute | solution.py:532
  13.3 3.0 %collective-permute-start.5 = (f32[576,128]{1,0:T(8,128)}, f32[576,128]{1,0:T(8,128)}, u32[]{:S(2)}, u32[]{:S(2)}) collective-permute-start(f32[576,128]{1,0:T(8,128)} %get-tuple-element.26), channel_id=1, source_target_pairs={{0,24},{4,28},{8,16},{12,20},{16,8},{20,12},{24,0},{28,4},{1,25},{... | collective-permute-start | bytes 884744 | tf_op jit(solution)/shard_map/ppermute | solution.py:532
  16.3 1.9 %collective-permute-done.2.refs_3_ = f32[576,128]{1,0:T(8,128)S(1)} collective-permute-done((f32[576,128]{1,0:T(8,128)S(1)}, f32[576,128]{1,0:T(8,128)S(1)}, u32[]{:S(2)}, u32[]{:S(2)}) %collective-permute-start.2) | collective-permute-done | bytes 294944 | tf_op jit(solution)/shard_map/ppermute | solution.py:532
  18.2 1.2 %collective-permute-start.10 = (f32[576,128]{1,0:T(8,128)}, f32[576,128]{1,0:T(8,128)}, u32[]{:S(2)}, u32[]{:S(2)}) collective-permute-start(f32[576,128]{1,0:T(8,128)} %get-tuple-element.19), channel_id=1, source_target_pairs={{0,16},{4,20},{8,24},{12,28},{16,0},{20,4},{24,8},{28,12},{1,17},{... | collective-permute-start | bytes 884744 | tf_op jit(solution)/shard_map/ppermute | solution.py:532
  19.4 1.3 %collective-permute-done.3.refs_4_ = f32[576,128]{1,0:T(8,128)S(1)} collective-permute-done((f32[576,128]{1,0:T(8,128)S(1)}, f32[576,128]{1,0:T(8,128)S(1)}, u32[]{:S(2)}, u32[]{:S(2)}) %collective-permute-start.3) | collective-permute-done | bytes 294944 | tf_op jit(solution)/shard_map/ppermute | solution.py:532
  20.7 0.5 collective-permute-start.11
  22.0 0.1 select_reduce_fusion
  22.1 1.7 %collective-permute-start.12 = (f32[576,128]{1,0:T(8,128)}, f32[576,128]{1,0:T(8,128)S(1)}, u32[]{:S(2)}, u32[]{:S(2)}) collective-permute-start(f32[576,128]{1,0:T(8,128)} %get-tuple-element.21), channel_id=1, source_target_pairs={{0,20},{4,16},{8,28},{12,24},{16,4},{20,0},{24,12},{28,8},{1,21},{... | collective-permute-start | bytes 884744 | tf_op jit(solution)/shard_map/ppermute | solution.py:532
  23.7 4.0 %collective-permute-done.5.refs_6_ = f32[576,128]{1,0:T(8,128)} collective-permute-done((f32[576,128]{1,0:T(8,128)}, f32[576,128]{1,0:T(8,128)}, u32[]{:S(2)}, u32[]{:S(2)}) %collective-permute-start.5) | collective-permute-done | bytes 294944 | tf_op jit(solution)/shard_map/ppermute | solution.py:532
  27.7 5.8 %collective-permute-done.6.refs_7_ = f32[576,128]{1,0:T(8,128)} collective-permute-done((f32[576,128]{1,0:T(8,128)}, f32[576,128]{1,0:T(8,128)}, u32[]{:S(2)}, u32[]{:S(2)}) %collective-permute-start.6) | collective-permute-done | bytes 294944 | tf_op jit(solution)/shard_map/ppermute | solution.py:532
  33.5 0.3 collective-permute-start.9
  33.8 5.3 %collective-permute-done.10.refs_2_ = f32[576,128]{1,0:T(8,128)} collective-permute-done((f32[576,128]{1,0:T(8,128)}, f32[576,128]{1,0:T(8,128)}, u32[]{:S(2)}, u32[]{:S(2)}) %collective-permute-start.10) | collective-permute-done | bytes 294944 | tf_op jit(solution)/shard_map/ppermute | solution.py:532
  39.2 2.5 %collective-permute-start.8 = (f32[576,128]{1,0:T(8,128)}, f32[576,128]{1,0:T(8,128)S(1)}, u32[]{:S(2)}, u32[]{:S(2)}) collective-permute-start(f32[576,128]{1,0:T(8,128)} %get-tuple-element.17), channel_id=1, source_target_pairs={{0,24},{4,28},{8,16},{12,20},{16,8},{20,12},{24,0},{28,4},{1,25},{... | collective-permute-start | bytes 884744 | tf_op jit(solution)/shard_map/ppermute | solution.py:532
  41.6 0.1 dynamic_slice.31
  41.7 0.1 pad_add_fusion.1.owner_ref
  41.8 5.6 %forward.1 = (f32[576,8,128]{2,1,0:T(8,128)S(1)}, f32[4,4608,128]{2,1,0:T(8,128)S(1)}) custom-call(s32[1]{0:T(128)} %bitcast.3.place_ref.owner_ref, f32[4608,128]{1,0:T(8,128)S(1)} %bitcast.13, f32[576,128]{1,0:T(8,128)S(1)} %collective-permute-done.refs_1_, f32[576,128]{1,0:T(8,128)S(1)} %collective-permute-done.1.refs_2_, ...), custom_call_target="tpu_custom_call" | custom-call | flops 235929600 | bytes 14155776 | tf_op jit(solution)/shard_map/forward/pallas_call | solution.py:403
  47.4 0.1 squeeze.9.weight_ref
  47.5 2.7 %early.2.refs_1_ = f32[576,8,128]{2,1,0:T(8,128)S(1)} custom-call(s32[1]{0:T(128)} %bitcast.3.place_ref.owner_ref, f32[576,8,128]{2,1,0:T(8,128)S(1)} %get-tuple-element.15.lattice_ref, f32[8,128]{1,0:T(8,128)S(1)} %squeeze.9.weight_ref, f32[576,128]{1,0:T(8,128)S(1)} %collective-permute-done.9.refs_0_, f32[4608,128]{1,0:T(8,128)S(1)} %bitcast.15, ...), custom_call_target="tpu_custom_call" | custom-call | flops 88473600 | bytes 7077888 | tf_op jit(solution)/shard_map/early/pallas_call | solution.py:421
  50.3 2.6 %collective-permute-done.8.refs_0_ = f32[576,128]{1,0:T(8,128)S(1)} collective-permute-done((f32[576,128]{1,0:T(8,128)}, f32[576,128]{1,0:T(8,128)S(1)}, u32[]{:S(2)}, u32[]{:S(2)}) %collective-permute-start.8) | collective-permute-done | bytes 294944 | tf_op jit(solution)/shard_map/ppermute | solution.py:532
  52.9 0.5 early.3.refs_1_
  53.3 0.0 copy-start.2
  53.4 0.0 copy-start.5
  53.4 4.0 %collective-permute-done.7.refs_0_ = f32[576,128]{1,0:T(8,128)S(1)} collective-permute-done((f32[576,128]{1,0:T(8,128)}, f32[576,128]{1,0:T(8,128)S(1)}, u32[]{:S(2)}, u32[]{:S(2)}) %collective-permute-start.7) | collective-permute-done | bytes 294944 | tf_op jit(solution)/shard_map/ppermute | solution.py:532
  57.4 2.5 %sigma.1 = (f32[576,8,128]{2,1,0:T(8,128)S(1)}, f32[4608,128]{1,0:T(8,128)S(1)}) custom-call(s32[1]{0:T(128)} %bitcast.3.place_ref.owner_ref, f32[576,8,128]{2,1,0:T(8,128)S(1)} %get-tuple-element.15.lattice_ref, f32[8,128]{1,0:T(8,128)S(1)} %squeeze.9.weight_ref, f32[576,128]{1,0:T(8,128)S(1)} %collective-permute-done.7.refs_0_, ...), custom_call_target="tpu_custom_call", output_to_operand_aliasing={{0}: (4, {})} | custom-call | flops 117964800 | bytes 14155776 | tf_op jit(solution)/shard_map/sigma/pallas_call | solution.py:439
  59.9 2.5 %contract.4 = f32[288,128]{1,0:T(8,128)S(1)} custom-call(s32[4]{0:T(128)S(1)} %pad_add_fusion.1.owner_ref, f32[4608,128]{1,0:T(8,128)S(1)} %get-tuple-element.23.sigma_ref, f32[72,128]{1,0:T(8,128)S(1)} %copy-done.4, f32[8,128]{1,0:T(8,128)S(1)} %copy-done.5, bf16[2048,128]{1,0:T(8,128)(2,1)S(1)} %copy-done.2, f32[4,4608,128]{2,1,0:T(8,128)S(1)} %get-tuple-element.24.greens_ref), custom_call_target="tpu_custom_call" | custom-call | flops 165150720 | bytes 14155776 | tf_op jit(solution)/shard_map/contract/pallas_call | solution.py:460
  62.4 0.6 collective-permute-start.14
  63.0 0.1 pad_add_fusion.owner_ref
  63.0 2.1 %contract.3 = f32[216,128]{1,0:T(8,128)S(1)} custom-call(s32[3]{0:T(128)S(1)} %pad_add_fusion.owner_ref, f32[4608,128]{1,0:T(8,128)S(1)} %get-tuple-element.23.sigma_ref, f32[72,128]{1,0:T(8,128)S(1)} %copy-done.4, f32[8,128]{1,0:T(8,128)S(1)} %copy-done.5, bf16[2048,128]{1,0:T(8,128)(2,1)S(1)} %copy-done.2, f32[4,4608,128]{2,1,0:T(8,128)S(1)} %get-tuple-element.24.greens_ref), custom_call_target="tpu_custom_call" | custom-call | flops 123863040 | bytes 14155776 | tf_op jit(solution)/shard_map/contract/pallas_call | solution.py:460
  65.2 2.7 %collective-permute-start.15 = (f32[72,128]{1,0:T(8,128)S(1)}, f32[72,128]{1,0:T(8,128)S(1)}, u32[]{:S(2)}, u32[]{:S(2)}) collective-permute-start(f32[72,128]{1,0:T(8,128)S(1)} %get-tuple-element.34), channel_id=1, source_target_pairs={{0,24},{4,28},{8,16},{12,20},{16,8},{20,12},{24,0},{28,4},{1,25},{... | collective-permute-start | bytes 110600 | tf_op jit(solution)/shard_map/ppermute | solution.py:532
  67.8 0.5 collective-permute-start.16
  68.3 0.4 collective-permute-start.17
  68.7 1.4 %collective-permute-done.15.refs_0_ = f32[72,128]{1,0:T(8,128)S(1)} collective-permute-done((f32[72,128]{1,0:T(8,128)S(1)}, f32[72,128]{1,0:T(8,128)S(1)}, u32[]{:S(2)}, u32[]{:S(2)}) %collective-permute-start.15) | collective-permute-done | bytes 36896 | tf_op jit(solution)/shard_map/ppermute | solution.py:532
  70.1 0.6 contract.5
  70.7 1.1 %collective-permute-done.16 = f32[72,128]{1,0:T(8,128)S(1)} collective-permute-done((f32[72,128]{1,0:T(8,128)S(1)}, f32[72,128]{1,0:T(8,128)S(1)}, u32[]{:S(2)}, u32[]{:S(2)}) %collective-permute-start.16) | collective-permute-done | bytes 36896 | tf_op jit(solution)/shard_map/ppermute | solution.py:532
  71.8 0.5 collective-permute-done.17
  72.3 0.0 copy-start.3
  72.4 3.6 %collective-permute-start.18 = (f32[72,128]{1,0:T(8,128)S(1)}, f32[72,128]{1,0:T(8,128)S(1)}, u32[]{:S(2)}, u32[]{:S(2)}) collective-permute-start(f32[72,128]{1,0:T(8,128)S(1)} %slice_add_fusion.1), channel_id=1, source_target_pairs={{0,3},{1,2},{2,1},{3,0},{4,7},{5,6},{6,5},{7,4},{8,11},{9,10},{10,... | collective-permute-start | bytes 110600 | tf_op jit(solution)/shard_map/ppermute | solution.py:532
  76.0 0.8 collective-permute-start.20
  76.8 0.8 split_own.1.split_ref
  77.6 0.7 collective-permute-done.18
  78.3 2.6 %collective-permute-done.19 = f32[72,128]{1,0:T(8,128)S(1)} collective-permute-done((f32[72,128]{1,0:T(8,128)S(1)}, f32[72,128]{1,0:T(8,128)S(1)}, u32[]{:S(2)}, u32[]{:S(2)}) %collective-permute-start.19) | collective-permute-done | bytes 36896 | tf_op jit(solution)/shard_map/ppermute | solution.py:532
  80.9 5.3 %propagate.1 = f32[64,72,128]{2,1,0:T(8,128)} custom-call(f32[64,72,128]{2,1,0:T(8,128)S(1)} %copy-done, bf16[72,64,384]{2,1,0:T(8,128)(2,1)S(1)} %split_own.1.split_ref, f32[72,128]{1,0:T(8,128)S(1)} %add_add_fusion.effective_ref, bf16[256,2048]{1,0:T(8,128)(2,1)S(1)} %copy-done.3), custom_call_target="tpu_custom_call" | custom-call | flops 18874368 | bytes 11796480 | tf_op jit(solution)/shard_map/propagate/pallas_call | solution.py:506
  (35 shorter events, 0.1 us)
Async XLA Ops:
  2.4 5.2 %copy-start.6 = (f32[576,128]{1,0:T(8,128)}, f32[576,128]{1,0:T(8,128)S(1)}, u32[]{:S(2)}) copy-start(f32[576,128]{1,0:T(8,128)S(1)} %get-tuple-element.31.refs_0_) | copy-start | bytes 884740
  2.4 19.5 %copy-start.8 = (s32[64]{0:T(128)S(1)}, s32[64]{0:T(128)}, u32[]{:S(2)}) copy-start(s32[64]{0:T(128)} %param.18) | copy-start | bytes 772
  2.4 19.5 %copy-start.9 = (f32[4]{0:T(128)S(1)}, f32[4]{0:T(128)}, u32[]{:S(2)}) copy-start(f32[4]{0:T(128)} %constant.44.clone) | copy-start | bytes 52
  2.4 39.3 %copy-start = (f32[64,72,128]{2,1,0:T(8,128)S(1)}, f32[64,72,128]{2,1,0:T(8,128)}, u32[]{:S(2)}) copy-start(f32[64,72,128]{2,1,0:T(8,128)} %green_ref.3) | copy-start | bytes 7077892
  2.5 10.9 %collective-permute-start = (f32[576,128]{1,0:T(8,128)S(1)}, f32[576,128]{1,0:T(8,128)S(1)}, u32[]{:S(2)}, u32[]{:S(2)}) collective-permute-start(f32[576,128]{1,0:T(8,128)S(1)} %get-tuple-element.31.refs_0_), channel_id=1, source_target_pairs={{0,16},{4,20},{8,24},{12,28},{16,0},{20,4},{24,8},{28,12},{1,17},{... | collective-permute-start | bytes 884744 | tf_op jit(solution)/shard_map/ppermute | solution.py:532
  5.5 10.8 %collective-permute-start.1 = (f32[576,128]{1,0:T(8,128)S(1)}, f32[576,128]{1,0:T(8,128)S(1)}, u32[]{:S(2)}, u32[]{:S(2)}) collective-permute-start(f32[576,128]{1,0:T(8,128)S(1)} %get-tuple-element.30), channel_id=1, source_target_pairs={{0,8},{4,12},{8,0},{12,4},{16,24},{20,28},{24,16},{28,20},{1,9},{5... | collective-permute-start | bytes 884744 | tf_op jit(solution)/shard_map/ppermute | solution.py:532
  7.0 11.2 %collective-permute-start.2 = (f32[576,128]{1,0:T(8,128)S(1)}, f32[576,128]{1,0:T(8,128)S(1)}, u32[]{:S(2)}, u32[]{:S(2)}) collective-permute-start(f32[576,128]{1,0:T(8,128)S(1)} %get-tuple-element.29), channel_id=1, source_target_pairs={{0,20},{4,16},{8,28},{12,24},{16,4},{20,0},{24,12},{28,8},{1,21},{... | collective-permute-start | bytes 884744 | tf_op jit(solution)/shard_map/ppermute | solution.py:532
  7.0 13.8 %collective-permute-start.3 = (f32[576,128]{1,0:T(8,128)S(1)}, f32[576,128]{1,0:T(8,128)S(1)}, u32[]{:S(2)}, u32[]{:S(2)}) collective-permute-start(f32[576,128]{1,0:T(8,128)S(1)} %get-tuple-element.28), channel_id=1, source_target_pairs={{0,12},{4,8},{8,4},{12,0},{16,28},{20,24},{24,20},{28,16},{1,13},{... | collective-permute-start | bytes 884744 | tf_op jit(solution)/shard_map/ppermute | solution.py:532
  7.3 14.7 %collective-permute-start.4 = (f32[576,128]{1,0:T(8,128)}, f32[576,128]{1,0:T(8,128)}, u32[]{:S(2)}, u32[]{:S(2)}) collective-permute-start(f32[576,128]{1,0:T(8,128)} %get-tuple-element.27), channel_id=1, source_target_pairs={{0,4},{4,0},{8,12},{12,8},{16,20},{20,16},{24,28},{28,24},{1,5},{5... | collective-permute-start | bytes 884744 | tf_op jit(solution)/shard_map/ppermute | solution.py:532
  13.3 14.4 %collective-permute-start.5 = (f32[576,128]{1,0:T(8,128)}, f32[576,128]{1,0:T(8,128)}, u32[]{:S(2)}, u32[]{:S(2)}) collective-permute-start(f32[576,128]{1,0:T(8,128)} %get-tuple-element.26), channel_id=1, source_target_pairs={{0,24},{4,28},{8,16},{12,20},{16,8},{20,12},{24,0},{28,4},{1,25},{... | collective-permute-start | bytes 884744 | tf_op jit(solution)/shard_map/ppermute | solution.py:532
  16.3 17.2 %collective-permute-start.6 = (f32[576,128]{1,0:T(8,128)}, f32[576,128]{1,0:T(8,128)}, u32[]{:S(2)}, u32[]{:S(2)}) collective-permute-start(f32[576,128]{1,0:T(8,128)} %get-tuple-element.25), channel_id=1, source_target_pairs={{0,28},{4,24},{8,20},{12,16},{16,12},{20,8},{24,4},{28,0},{1,29},{... | collective-permute-start | bytes 884744 | tf_op jit(solution)/shard_map/ppermute | solution.py:532
  18.2 20.9 %collective-permute-start.10 = (f32[576,128]{1,0:T(8,128)}, f32[576,128]{1,0:T(8,128)}, u32[]{:S(2)}, u32[]{:S(2)}) collective-permute-start(f32[576,128]{1,0:T(8,128)} %get-tuple-element.19), channel_id=1, source_target_pairs={{0,16},{4,20},{8,24},{12,28},{16,0},{20,4},{24,8},{28,12},{1,17},{... | collective-permute-start | bytes 884744 | tf_op jit(solution)/shard_map/ppermute | solution.py:532
  20.7 20.9 %collective-permute-start.11 = (f32[576,128]{1,0:T(8,128)}, f32[576,128]{1,0:T(8,128)}, u32[]{:S(2)}, u32[]{:S(2)}) collective-permute-start(f32[576,128]{1,0:T(8,128)} %get-tuple-element.20), channel_id=1, source_target_pairs={{0,8},{4,12},{8,0},{12,4},{16,24},{20,28},{24,16},{28,20},{1,9},{5... | collective-permute-start | bytes 884744 | tf_op jit(solution)/shard_map/ppermute | solution.py:532
  22.0 25.6 %copy-start.1 = (f32[64,72,128]{2,1,0:T(8,128)S(1)}, f32[64,72,128]{2,1,0:T(8,128)}, u32[]{:S(2)}) copy-start(f32[64,72,128]{2,1,0:T(8,128)} %param.15) | copy-start | bytes 7077892
  22.1 25.4 %collective-permute-start.12 = (f32[576,128]{1,0:T(8,128)}, f32[576,128]{1,0:T(8,128)S(1)}, u32[]{:S(2)}, u32[]{:S(2)}) collective-permute-start(f32[576,128]{1,0:T(8,128)} %get-tuple-element.21), channel_id=1, source_target_pairs={{0,20},{4,16},{8,28},{12,24},{16,4},{20,0},{24,12},{28,8},{1,21},{... | collective-permute-start | bytes 884744 | tf_op jit(solution)/shard_map/ppermute | solution.py:532
  27.7 19.7 %collective-permute-start.13 = (f32[576,128]{1,0:T(8,128)}, f32[576,128]{1,0:T(8,128)S(1)}, u32[]{:S(2)}, u32[]{:S(2)}) collective-permute-start(f32[576,128]{1,0:T(8,128)} %get-tuple-element.22), channel_id=1, source_target_pairs={{0,12},{4,8},{8,4},{12,0},{16,28},{20,24},{24,20},{28,16},{1,13},{... | collective-permute-start | bytes 884744 | tf_op jit(solution)/shard_map/ppermute | solution.py:532
  33.5 13.9 %collective-permute-start.9 = (f32[576,128]{1,0:T(8,128)}, f32[576,128]{1,0:T(8,128)S(1)}, u32[]{:S(2)}, u32[]{:S(2)}) collective-permute-start(f32[576,128]{1,0:T(8,128)} %get-tuple-element.18), channel_id=1, source_target_pairs={{0,4},{4,0},{8,12},{12,8},{16,20},{20,16},{24,28},{28,24},{1,5},{5... | collective-permute-start | bytes 884744 | tf_op jit(solution)/shard_map/ppermute | solution.py:532
  39.2 13.7 %collective-permute-start.8 = (f32[576,128]{1,0:T(8,128)}, f32[576,128]{1,0:T(8,128)S(1)}, u32[]{:S(2)}, u32[]{:S(2)}) collective-permute-start(f32[576,128]{1,0:T(8,128)} %get-tuple-element.17), channel_id=1, source_target_pairs={{0,24},{4,28},{8,16},{12,20},{16,8},{20,12},{24,0},{28,4},{1,25},{... | collective-permute-start | bytes 884744 | tf_op jit(solution)/shard_map/ppermute | solution.py:532
  41.6 15.7 %collective-permute-start.7 = (f32[576,128]{1,0:T(8,128)}, f32[576,128]{1,0:T(8,128)S(1)}, u32[]{:S(2)}, u32[]{:S(2)}) collective-permute-start(f32[576,128]{1,0:T(8,128)} %get-tuple-element.16), channel_id=1, source_target_pairs={{0,28},{4,24},{8,20},{12,16},{16,12},{20,8},{24,4},{28,0},{1,29},{... | collective-permute-start | bytes 884744 | tf_op jit(solution)/shard_map/ppermute | solution.py:532
  53.3 6.5 %copy-start.2 = (bf16[2048,128]{1,0:T(8,128)(2,1)S(1)}, bf16[2048,128]{1,0:T(8,128)(2,1)}, u32[]{:S(2)}) copy-start(bf16[2048,128]{1,0:T(8,128)(2,1)} %constant.46.clone.gather_ref) | copy-start | bytes 1572868
  53.3 6.5 %copy-start.4 = (f32[72,128]{1,0:T(8,128)S(1)}, f32[72,128]{1,0:T(8,128)}, u32[]{:S(2)}) copy-start(f32[72,128]{1,0:T(8,128)} %equal_ref.5) | copy-start | bytes 110596
  53.4 6.5 %copy-start.5 = (f32[8,128]{1,0:T(8,128)S(1)}, f32[8,128]{1,0:T(8,128)}, u32[]{:S(2)}) copy-start(f32[8,128]{1,0:T(8,128)} %constant.45.clone.sign_ref) | copy-start | bytes 12292
  62.4 2.7 %collective-permute-start.14 = (f32[288,128]{1,0:T(8,128)S(1)}, f32[288,128]{1,0:T(8,128)S(1)}, u32[]{:S(2)}, u32[]{:S(2)}) collective-permute-start(f32[288,128]{1,0:T(8,128)S(1)} %contract.4), channel_id=1, source_target_pairs={{0,4},{4,0},{8,12},{12,8},{16,20},{20,16},{24,28},{28,24},{1,5},{5... | collective-permute-start | bytes 442376 | tf_op jit(solution)/shard_map/ppermute | solution.py:532
  65.2 4.9 %collective-permute-start.15 = (f32[72,128]{1,0:T(8,128)S(1)}, f32[72,128]{1,0:T(8,128)S(1)}, u32[]{:S(2)}, u32[]{:S(2)}) collective-permute-start(f32[72,128]{1,0:T(8,128)S(1)} %get-tuple-element.34), channel_id=1, source_target_pairs={{0,24},{4,28},{8,16},{12,20},{16,8},{20,12},{24,0},{28,4},{1,25},{... | collective-permute-start | bytes 110600 | tf_op jit(solution)/shard_map/ppermute | solution.py:532
  67.8 4.0 %collective-permute-start.16 = (f32[72,128]{1,0:T(8,128)S(1)}, f32[72,128]{1,0:T(8,128)S(1)}, u32[]{:S(2)}, u32[]{:S(2)}) collective-permute-start(f32[72,128]{1,0:T(8,128)S(1)} %get-tuple-element.32), channel_id=1, source_target_pairs={{0,16},{4,20},{8,24},{12,28},{16,0},{20,4},{24,8},{28,12},{1,17},{... | collective-permute-start | bytes 110600 | tf_op jit(solution)/shard_map/ppermute | solution.py:532
  68.3 4.0 %collective-permute-start.17 = (f32[72,128]{1,0:T(8,128)S(1)}, f32[72,128]{1,0:T(8,128)S(1)}, u32[]{:S(2)}, u32[]{:S(2)}) collective-permute-start(f32[72,128]{1,0:T(8,128)S(1)} %get-tuple-element.33), channel_id=1, source_target_pairs={{0,8},{4,12},{8,0},{12,4},{16,24},{20,28},{24,16},{28,20},{1,9},{5... | collective-permute-start | bytes 110600 | tf_op jit(solution)/shard_map/ppermute | solution.py:532
  72.3 8.5 %copy-start.7 = (f32[72,128]{1,0:T(8,128)S(1)}, f32[72,128]{1,0:T(8,128)}, u32[]{:S(2)}) copy-start(f32[72,128]{1,0:T(8,128)} %param.16) | copy-start | bytes 110596
  72.3 8.5 %copy-start.3 = (bf16[256,2048]{1,0:T(8,128)(2,1)S(1)}, bf16[256,2048]{1,0:T(8,128)(2,1)}, u32[]{:S(2)}) copy-start(bf16[256,2048]{1,0:T(8,128)(2,1)} %constant.47.clone.spread_ref) | copy-start | bytes 3145732
  72.4 5.9 %collective-permute-start.18 = (f32[72,128]{1,0:T(8,128)S(1)}, f32[72,128]{1,0:T(8,128)S(1)}, u32[]{:S(2)}, u32[]{:S(2)}) collective-permute-start(f32[72,128]{1,0:T(8,128)S(1)} %slice_add_fusion.1), channel_id=1, source_target_pairs={{0,3},{1,2},{2,1},{3,0},{4,7},{5,6},{6,5},{7,4},{8,11},{9,10},{10,... | collective-permute-start | bytes 110600 | tf_op jit(solution)/shard_map/ppermute | solution.py:532
  76.0 4.9 %collective-permute-start.19 = (f32[72,128]{1,0:T(8,128)S(1)}, f32[72,128]{1,0:T(8,128)S(1)}, u32[]{:S(2)}, u32[]{:S(2)}) collective-permute-start(f32[72,128]{1,0:T(8,128)S(1)} %slice_add_fusion.1), channel_id=1, source_target_pairs={{0,2},{1,3},{2,0},{3,1},{4,6},{5,7},{6,4},{7,5},{8,10},{9,11},{10,... | collective-permute-start | bytes 110600 | tf_op jit(solution)/shard_map/ppermute | solution.py:532
  76.0 4.9 %collective-permute-start.20 = (f32[72,128]{1,0:T(8,128)S(1)}, f32[72,128]{1,0:T(8,128)S(1)}, u32[]{:S(2)}, u32[]{:S(2)}) collective-permute-start(f32[72,128]{1,0:T(8,128)S(1)} %slice_add_fusion.1), channel_id=1, source_target_pairs={{0,1},{1,0},{2,3},{3,2},{4,5},{5,4},{6,7},{7,6},{8,9},{9,8},{10,11... | collective-permute-start | bytes 110600 | tf_op jit(solution)/shard_map/ppermute | solution.py:532

commit v16 on v15

--- a/solution.py
+++ b/solution.py
@@ -21,6 +21,7 @@
 hubbard = 1.0
 quadrature = (0.375, 1.1666666, 0.9583333, 1.0)
 
+AT_ONCE = 4
 LATE = 2
 AHEAD = 3
 
@@ -316,15 +317,19 @@
         factors = [
             factor_ref[pl.ds(start, tile), spot * WIDTH : (spot + 1) * WIDTH] for spot in range(2 * BANDS)
         ]
-        for n in range(tile):
-            k = number * tile + n
-            added = jnp.dot(split_ref[k], matrix(factors, n), preferred_element_type=jnp.float32)
-            result = times_of(green_ref, k) + added
-            if points % TILE:
-                held_ref[slot, :, n, :] = result
-            else:
-                rows = held_ref.reshape(2 * history * tile, WIDTH)
-                rows[pl.ds(slot * history * tile + n, history, stride=tile), :] = result
+        for first in range(0, tile, AT_ONCE):
+            batch = range(first, min(first + AT_ONCE, tile))
+            results = []
+            for n in batch:
+                k = number * tile + n
+                added = jnp.dot(split_ref[k], matrix(factors, n), preferred_element_type=jnp.float32)
+                results.append(times_of(green_ref, k) + added)
+            for n, result in zip(batch, results):
+                if points % TILE:
+                    held_ref[slot, :, n, :] = result
+                else:
+                    rows = held_ref.reshape(2 * history * tile, WIDTH)
+                    rows[pl.ds(slot * history * tile + n, history, stride=tile), :] = result
         copy(number, slot).start()
 
     tiles = points // tile

time: 86.4 us -> 86.4 us (level)
  no operation moved by 1% of the time
where the time goes in v16:
time: 86.4 us; the launch traced here: 86.2 us
  waiting for transfers between devices  34 us (39%)
  Pallas kernels  25.4 us (29%)
  starting transfers between devices  22.9 us (27%)
  local copies, waits for them, and re-layouts  2.65 us (3%)
  between operations  0.89 us (1%)
    ppermute x21, waiting for transfers between devices, exchange(): return lax.ppermute(value, axis, pairs)  34 us
    ppermute x21, starting transfers between devices, exchange(): return lax.ppermute(value, axis, pairs)  22.9 us
    pallas_call x1, Pallas kernels, forward(): pl.pallas_call(functools.partial(forward_kernel, steps, parts), out_shape...  5.62 us
    pallas_call x1, Pallas kernels, propagate(): pl.pallas_call(propagate_kernel, out_shape=jax.ShapeDtypeStruct(greens.sh...  5.29 us
    pallas_call x3, Pallas kernels, contract(): pl.pallas_call(functools.partial(contract_kernel, share), out_shape=jax.S...  5.27 us
    pallas_call x2, Pallas kernels, early_lines(): pl.pallas_call(functools.partial(early_kernel, steps, parts), out_shape=j...  3.19 us
    pallas_call x1, Pallas kernels, pick(): pl.pallas_call(functools.partial(pick_kernel, steps, parts), out_shape=[j...  2.83 us
    pallas_call x1, Pallas kernels, sigma_of(): pl.pallas_call(functools.partial(sigma_kernel, steps, parts), out_shape=[...  2.46 us
  transfers between devices with their start and end apart: 21, of which 13 were waited for; matrix products, arithmetic and copies ran while one was open for 0% of the time, Pallas kernels for 18%

profile of v16, /device:TPU:0, one launch (start us, length us, event | category | flops | bytes accessed | tf_op | source)
XLA Modules:
  0.0 86.2 jit_solution(3551403639766979744)
XLA Ops:
  0.0 2.4 %constant_dynamic-slice_fusion = (f32[576,128]{1,0:T(8,128)}, f32[576,128]{1,0:T(8,128)}, f32[576,128]{1,0:T(8,128)}, f32[576,128]{1,0:T(8,128)S(1)}, f32[576,12...) fusion(f32[4608,128]{1,0:T(8,128)} %bitcast.12, s32[]{:T(128)S(6)} %select_n.38, s32[]{:T(128)S(6)} %select_n.37, ...), kind=kLoop, calls=%fused_computation.6 | loop fusion | bytes 4128796 | tf_op jit(solution)/shard_map/dynamic_slice | solution.py:574
  2.5 3.0 %collective-permute-start = (f32[576,128]{1,0:T(8,128)S(1)}, f32[576,128]{1,0:T(8,128)S(1)}, u32[]{:S(2)}, u32[]{:S(2)}) collective-permute-start(f32[576,128]{1,0:T(8,128)S(1)} %get-tuple-element.31.refs_0_), channel_id=1, source_target_pairs={{0,16},{4,20},{8,24},{12,28},{16,0},{20,4},{24,8},{28,12},{1,17},{... | collective-permute-start | bytes 884744 | tf_op jit(solution)/shard_map/ppermute | solution.py:537
  5.5 1.5 %collective-permute-start.1 = (f32[576,128]{1,0:T(8,128)S(1)}, f32[576,128]{1,0:T(8,128)S(1)}, u32[]{:S(2)}, u32[]{:S(2)}) collective-permute-start(f32[576,128]{1,0:T(8,128)S(1)} %get-tuple-element.30), channel_id=1, source_target_pairs={{0,8},{4,12},{8,0},{12,4},{16,24},{20,28},{24,16},{28,20},{1,9},{5... | collective-permute-start | bytes 884744 | tf_op jit(solution)/shard_map/ppermute | solution.py:537
  7.0 0.3 collective-permute-start.3
  7.3 0.3 collective-permute-start.4
  7.6 2.8 %pick.1 = (f32[576,128]{1,0:T(8,128)}, f32[576,128]{1,0:T(8,128)}, f32[576,128]{1,0:T(8,128)}, f32[576,128]{1,0:T(8,128)}, f32[576,128]{1,0:T(8,128)}, /*index=5*/f32[576,128]{1,0:T(8,128)}, f32[576,128]{1,0:T(8,128)}) custom-call(s32[1]{0:T(128)} %bitcast.3.place_ref.owner_ref, f32[4608,128]{1,0:T(8,128)} %bitcast.14, f32[576,128]{1,0:T(8,128)} %copy-done.6), custom_call_target="tpu_custom_call" | custom-call | bytes 4718592 | tf_op jit(solution)/shard_map/pick/pallas_call | solution.py:482
  10.5 2.9 %collective-permute-done.refs_1_ = f32[576,128]{1,0:T(8,128)S(1)} collective-permute-done((f32[576,128]{1,0:T(8,128)S(1)}, f32[576,128]{1,0:T(8,128)S(1)}, u32[]{:S(2)}, u32[]{:S(2)}) %collective-permute-start) | collective-permute-done | bytes 294944 | tf_op jit(solution)/shard_map/ppermute | solution.py:537
  13.3 3.0 %collective-permute-start.5 = (f32[576,128]{1,0:T(8,128)}, f32[576,128]{1,0:T(8,128)}, u32[]{:S(2)}, u32[]{:S(2)}) collective-permute-start(f32[576,128]{1,0:T(8,128)} %get-tuple-element.26), channel_id=1, source_target_pairs={{0,24},{4,28},{8,16},{12,20},{16,8},{20,12},{24,0},{28,4},{1,25},{... | collective-permute-start | bytes 884744 | tf_op jit(solution)/shard_map/ppermute | solution.py:537
  16.3 1.9 %collective-permute-done.2.refs_3_ = f32[576,128]{1,0:T(8,128)S(1)} collective-permute-done((f32[576,128]{1,0:T(8,128)S(1)}, f32[576,128]{1,0:T(8,128)S(1)}, u32[]{:S(2)}, u32[]{:S(2)}) %collective-permute-start.2) | collective-permute-done | bytes 294944 | tf_op jit(solution)/shard_map/ppermute | solution.py:537
  18.2 1.2 %collective-permute-start.10 = (f32[576,128]{1,0:T(8,128)}, f32[576,128]{1,0:T(8,128)}, u32[]{:S(2)}, u32[]{:S(2)}) collective-permute-start(f32[576,128]{1,0:T(8,128)} %get-tuple-element.19), channel_id=1, source_target_pairs={{0,16},{4,20},{8,24},{12,28},{16,0},{20,4},{24,8},{28,12},{1,17},{... | collective-permute-start | bytes 884744 | tf_op jit(solution)/shard_map/ppermute | solution.py:537
  19.4 1.3 %collective-permute-done.3.refs_4_ = f32[576,128]{1,0:T(8,128)S(1)} collective-permute-done((f32[576,128]{1,0:T(8,128)S(1)}, f32[576,128]{1,0:T(8,128)S(1)}, u32[]{:S(2)}, u32[]{:S(2)}) %collective-permute-start.3) | collective-permute-done | bytes 294944 | tf_op jit(solution)/shard_map/ppermute | solution.py:537
  20.7 0.5 collective-permute-start.11
  22.0 0.1 select_reduce_fusion
  22.1 1.7 %collective-permute-start.12 = (f32[576,128]{1,0:T(8,128)}, f32[576,128]{1,0:T(8,128)S(1)}, u32[]{:S(2)}, u32[]{:S(2)}) collective-permute-start(f32[576,128]{1,0:T(8,128)} %get-tuple-element.21), channel_id=1, source_target_pairs={{0,20},{4,16},{8,28},{12,24},{16,4},{20,0},{24,12},{28,8},{1,21},{... | collective-permute-start | bytes 884744 | tf_op jit(solution)/shard_map/ppermute | solution.py:537
  23.7 4.0 %collective-permute-done.5.refs_6_ = f32[576,128]{1,0:T(8,128)} collective-permute-done((f32[576,128]{1,0:T(8,128)}, f32[576,128]{1,0:T(8,128)}, u32[]{:S(2)}, u32[]{:S(2)}) %collective-permute-start.5) | collective-permute-done | bytes 294944 | tf_op jit(solution)/shard_map/ppermute | solution.py:537
  27.7 5.8 %collective-permute-done.6.refs_7_ = f32[576,128]{1,0:T(8,128)} collective-permute-done((f32[576,128]{1,0:T(8,128)}, f32[576,128]{1,0:T(8,128)}, u32[]{:S(2)}, u32[]{:S(2)}) %collective-permute-start.6) | collective-permute-done | bytes 294944 | tf_op jit(solution)/shard_map/ppermute | solution.py:537
  33.5 0.3 collective-permute-start.9
  33.8 5.3 %collective-permute-done.10.refs_2_ = f32[576,128]{1,0:T(8,128)} collective-permute-done((f32[576,128]{1,0:T(8,128)}, f32[576,128]{1,0:T(8,128)}, u32[]{:S(2)}, u32[]{:S(2)}) %collective-permute-start.10) | collective-permute-done | bytes 294944 | tf_op jit(solution)/shard_map/ppermute | solution.py:537
  39.2 2.5 %collective-permute-start.8 = (f32[576,128]{1,0:T(8,128)}, f32[576,128]{1,0:T(8,128)S(1)}, u32[]{:S(2)}, u32[]{:S(2)}) collective-permute-start(f32[576,128]{1,0:T(8,128)} %get-tuple-element.17), channel_id=1, source_target_pairs={{0,24},{4,28},{8,16},{12,20},{16,8},{20,12},{24,0},{28,4},{1,25},{... | collective-permute-start | bytes 884744 | tf_op jit(solution)/shard_map/ppermute | solution.py:537
  41.6 0.1 dynamic_slice.31
  41.7 0.1 pad_add_fusion.1.owner_ref
  41.8 5.6 %forward.1 = (f32[576,8,128]{2,1,0:T(8,128)S(1)}, f32[4,4608,128]{2,1,0:T(8,128)S(1)}) custom-call(s32[1]{0:T(128)} %bitcast.3.place_ref.owner_ref, f32[4608,128]{1,0:T(8,128)S(1)} %bitcast.13, f32[576,128]{1,0:T(8,128)S(1)} %collective-permute-done.refs_1_, f32[576,128]{1,0:T(8,128)S(1)} %collective-permute-done.1.refs_2_, ...), custom_call_target="tpu_custom_call" | custom-call | flops 235929600 | bytes 14155776 | tf_op jit(solution)/shard_map/forward/pallas_call | solution.py:408
  47.4 0.1 squeeze.9.weight_ref
  47.5 2.7 %early.2.refs_1_ = f32[576,8,128]{2,1,0:T(8,128)S(1)} custom-call(s32[1]{0:T(128)} %bitcast.3.place_ref.owner_ref, f32[576,8,128]{2,1,0:T(8,128)S(1)} %get-tuple-element.15.lattice_ref, f32[8,128]{1,0:T(8,128)S(1)} %squeeze.9.weight_ref, f32[576,128]{1,0:T(8,128)S(1)} %collective-permute-done.9.refs_0_, f32[4608,128]{1,0:T(8,128)S(1)} %bitcast.15, ...), custom_call_target="tpu_custom_call" | custom-call | flops 88473600 | bytes 7077888 | tf_op jit(solution)/shard_map/early/pallas_call | solution.py:426
  50.3 2.6 %collective-permute-done.8.refs_0_ = f32[576,128]{1,0:T(8,128)S(1)} collective-permute-done((f32[576,128]{1,0:T(8,128)}, f32[576,128]{1,0:T(8,128)S(1)}, u32[]{:S(2)}, u32[]{:S(2)}) %collective-permute-start.8) | collective-permute-done | bytes 294944 | tf_op jit(solution)/shard_map/ppermute | solution.py:537
  52.9 0.5 early.3.refs_1_
  53.3 0.0 copy-start.2
  53.4 0.0 copy-start.5
  53.4 4.0 %collective-permute-done.7.refs_0_ = f32[576,128]{1,0:T(8,128)S(1)} collective-permute-done((f32[576,128]{1,0:T(8,128)}, f32[576,128]{1,0:T(8,128)S(1)}, u32[]{:S(2)}, u32[]{:S(2)}) %collective-permute-start.7) | collective-permute-done | bytes 294944 | tf_op jit(solution)/shard_map/ppermute | solution.py:537
  57.4 2.5 %sigma.1 = (f32[576,8,128]{2,1,0:T(8,128)S(1)}, f32[4608,128]{1,0:T(8,128)S(1)}) custom-call(s32[1]{0:T(128)} %bitcast.3.place_ref.owner_ref, f32[576,8,128]{2,1,0:T(8,128)S(1)} %get-tuple-element.15.lattice_ref, f32[8,128]{1,0:T(8,128)S(1)} %squeeze.9.weight_ref, f32[576,128]{1,0:T(8,128)S(1)} %collective-permute-done.7.refs_0_, ...), custom_call_target="tpu_custom_call", output_to_operand_aliasing={{0}: (4, {})} | custom-call | flops 117964800 | bytes 14155776 | tf_op jit(solution)/shard_map/sigma/pallas_call | solution.py:444
  59.9 2.5 %contract.4 = f32[288,128]{1,0:T(8,128)S(1)} custom-call(s32[4]{0:T(128)S(1)} %pad_add_fusion.1.owner_ref, f32[4608,128]{1,0:T(8,128)S(1)} %get-tuple-element.23.sigma_ref, f32[72,128]{1,0:T(8,128)S(1)} %copy-done.4, f32[8,128]{1,0:T(8,128)S(1)} %copy-done.5, bf16[2048,128]{1,0:T(8,128)(2,1)S(1)} %copy-done.2, f32[4,4608,128]{2,1,0:T(8,128)S(1)} %get-tuple-element.24.greens_ref), custom_call_target="tpu_custom_call" | custom-call | flops 165150720 | bytes 14155776 | tf_op jit(solution)/shard_map/contract/pallas_call | solution.py:465
  62.4 0.6 collective-permute-start.14
  63.0 0.1 pad_add_fusion.owner_ref
  63.0 2.1 %contract.3 = f32[216,128]{1,0:T(8,128)S(1)} custom-call(s32[3]{0:T(128)S(1)} %pad_add_fusion.owner_ref, f32[4608,128]{1,0:T(8,128)S(1)} %get-tuple-element.23.sigma_ref, f32[72,128]{1,0:T(8,128)S(1)} %copy-done.4, f32[8,128]{1,0:T(8,128)S(1)} %copy-done.5, bf16[2048,128]{1,0:T(8,128)(2,1)S(1)} %copy-done.2, f32[4,4608,128]{2,1,0:T(8,128)S(1)} %get-tuple-element.24.greens_ref), custom_call_target="tpu_custom_call" | custom-call | flops 123863040 | bytes 14155776 | tf_op jit(solution)/shard_map/contract/pallas_call | solution.py:465
  65.2 2.7 %collective-permute-start.15 = (f32[72,128]{1,0:T(8,128)S(1)}, f32[72,128]{1,0:T(8,128)S(1)}, u32[]{:S(2)}, u32[]{:S(2)}) collective-permute-start(f32[72,128]{1,0:T(8,128)S(1)} %get-tuple-element.34), channel_id=1, source_target_pairs={{0,24},{4,28},{8,16},{12,20},{16,8},{20,12},{24,0},{28,4},{1,25},{... | collective-permute-start | bytes 110600 | tf_op jit(solution)/shard_map/ppermute | solution.py:537
  67.8 0.5 collective-permute-start.16
  68.3 0.4 collective-permute-start.17
  68.7 1.4 %collective-permute-done.15.refs_0_ = f32[72,128]{1,0:T(8,128)S(1)} collective-permute-done((f32[72,128]{1,0:T(8,128)S(1)}, f32[72,128]{1,0:T(8,128)S(1)}, u32[]{:S(2)}, u32[]{:S(2)}) %collective-permute-start.15) | collective-permute-done | bytes 36896 | tf_op jit(solution)/shard_map/ppermute | solution.py:537
  70.1 0.6 contract.5
  70.7 1.1 %collective-permute-done.16 = f32[72,128]{1,0:T(8,128)S(1)} collective-permute-done((f32[72,128]{1,0:T(8,128)S(1)}, f32[72,128]{1,0:T(8,128)S(1)}, u32[]{:S(2)}, u32[]{:S(2)}) %collective-permute-start.16) | collective-permute-done | bytes 36896 | tf_op jit(solution)/shard_map/ppermute | solution.py:537
  71.8 0.5 collective-permute-done.17
  72.3 0.0 copy-start.3
  72.4 3.6 %collective-permute-start.18 = (f32[72,128]{1,0:T(8,128)S(1)}, f32[72,128]{1,0:T(8,128)S(1)}, u32[]{:S(2)}, u32[]{:S(2)}) collective-permute-start(f32[72,128]{1,0:T(8,128)S(1)} %slice_add_fusion.1), channel_id=1, source_target_pairs={{0,3},{1,2},{2,1},{3,0},{4,7},{5,6},{6,5},{7,4},{8,11},{9,10},{10,... | collective-permute-start | bytes 110600 | tf_op jit(solution)/shard_map/ppermute | solution.py:537
  76.0 0.8 collective-permute-start.20
  76.8 0.8 split_own.1.split_ref
  77.6 0.7 collective-permute-done.18
  78.3 2.6 %collective-permute-done.19 = f32[72,128]{1,0:T(8,128)S(1)} collective-permute-done((f32[72,128]{1,0:T(8,128)S(1)}, f32[72,128]{1,0:T(8,128)S(1)}, u32[]{:S(2)}, u32[]{:S(2)}) %collective-permute-start.19) | collective-permute-done | bytes 36896 | tf_op jit(solution)/shard_map/ppermute | solution.py:537
  80.9 5.3 %propagate.1 = f32[64,72,128]{2,1,0:T(8,128)} custom-call(f32[64,72,128]{2,1,0:T(8,128)S(1)} %copy-done, bf16[72,64,384]{2,1,0:T(8,128)(2,1)S(1)} %split_own.1.split_ref, f32[72,128]{1,0:T(8,128)S(1)} %add_add_fusion.effective_ref, bf16[256,2048]{1,0:T(8,128)(2,1)S(1)} %copy-done.3), custom_call_target="tpu_custom_call" | custom-call | flops 18874368 | bytes 11796480 | tf_op jit(solution)/shard_map/propagate/pallas_call | solution.py:511
  (35 shorter events, 0.1 us)
Async XLA Ops:
  2.4 5.2 %copy-start.6 = (f32[576,128]{1,0:T(8,128)}, f32[576,128]{1,0:T(8,128)S(1)}, u32[]{:S(2)}) copy-start(f32[576,128]{1,0:T(8,128)S(1)} %get-tuple-element.31.refs_0_) | copy-start | bytes 884740
  2.4 19.5 %copy-start.8 = (s32[64]{0:T(128)S(1)}, s32[64]{0:T(128)}, u32[]{:S(2)}) copy-start(s32[64]{0:T(128)} %param.18) | copy-start | bytes 772
  2.4 19.5 %copy-start.9 = (f32[4]{0:T(128)S(1)}, f32[4]{0:T(128)}, u32[]{:S(2)}) copy-start(f32[4]{0:T(128)} %constant.44.clone) | copy-start | bytes 52
  2.4 39.3 %copy-start = (f32[64,72,128]{2,1,0:T(8,128)S(1)}, f32[64,72,128]{2,1,0:T(8,128)}, u32[]{:S(2)}) copy-start(f32[64,72,128]{2,1,0:T(8,128)} %green_ref.3) | copy-start | bytes 7077892
  2.5 10.9 %collective-permute-start = (f32[576,128]{1,0:T(8,128)S(1)}, f32[576,128]{1,0:T(8,128)S(1)}, u32[]{:S(2)}, u32[]{:S(2)}) collective-permute-start(f32[576,128]{1,0:T(8,128)S(1)} %get-tuple-element.31.refs_0_), channel_id=1, source_target_pairs={{0,16},{4,20},{8,24},{12,28},{16,0},{20,4},{24,8},{28,12},{1,17},{... | collective-permute-start | bytes 884744 | tf_op jit(solution)/shard_map/ppermute | solution.py:537
  5.5 10.8 %collective-permute-start.1 = (f32[576,128]{1,0:T(8,128)S(1)}, f32[576,128]{1,0:T(8,128)S(1)}, u32[]{:S(2)}, u32[]{:S(2)}) collective-permute-start(f32[576,128]{1,0:T(8,128)S(1)} %get-tuple-element.30), channel_id=1, source_target_pairs={{0,8},{4,12},{8,0},{12,4},{16,24},{20,28},{24,16},{28,20},{1,9},{5... | collective-permute-start | bytes 884744 | tf_op jit(solution)/shard_map/ppermute | solution.py:537
  7.0 11.2 %collective-permute-start.2 = (f32[576,128]{1,0:T(8,128)S(1)}, f32[576,128]{1,0:T(8,128)S(1)}, u32[]{:S(2)}, u32[]{:S(2)}) collective-permute-start(f32[576,128]{1,0:T(8,128)S(1)} %get-tuple-element.29), channel_id=1, source_target_pairs={{0,20},{4,16},{8,28},{12,24},{16,4},{20,0},{24,12},{28,8},{1,21},{... | collective-permute-start | bytes 884744 | tf_op jit(solution)/shard_map/ppermute | solution.py:537
  7.0 13.8 %collective-permute-start.3 = (f32[576,128]{1,0:T(8,128)S(1)}, f32[576,128]{1,0:T(8,128)S(1)}, u32[]{:S(2)}, u32[]{:S(2)}) collective-permute-start(f32[576,128]{1,0:T(8,128)S(1)} %get-tuple-element.28), channel_id=1, source_target_pairs={{0,12},{4,8},{8,4},{12,0},{16,28},{20,24},{24,20},{28,16},{1,13},{... | collective-permute-start | bytes 884744 | tf_op jit(solution)/shard_map/ppermute | solution.py:537
  7.3 14.7 %collective-permute-start.4 = (f32[576,128]{1,0:T(8,128)}, f32[576,128]{1,0:T(8,128)}, u32[]{:S(2)}, u32[]{:S(2)}) collective-permute-start(f32[576,128]{1,0:T(8,128)} %get-tuple-element.27), channel_id=1, source_target_pairs={{0,4},{4,0},{8,12},{12,8},{16,20},{20,16},{24,28},{28,24},{1,5},{5... | collective-permute-start | bytes 884744 | tf_op jit(solution)/shard_map/ppermute | solution.py:537
  13.3 14.4 %collective-permute-start.5 = (f32[576,128]{1,0:T(8,128)}, f32[576,128]{1,0:T(8,128)}, u32[]{:S(2)}, u32[]{:S(2)}) collective-permute-start(f32[576,128]{1,0:T(8,128)} %get-tuple-element.26), channel_id=1, source_target_pairs={{0,24},{4,28},{8,16},{12,20},{16,8},{20,12},{24,0},{28,4},{1,25},{... | collective-permute-start | bytes 884744 | tf_op jit(solution)/shard_map/ppermute | solution.py:537
  16.3 17.2 %collective-permute-start.6 = (f32[576,128]{1,0:T(8,128)}, f32[576,128]{1,0:T(8,128)}, u32[]{:S(2)}, u32[]{:S(2)}) collective-permute-start(f32[576,128]{1,0:T(8,128)} %get-tuple-element.25), channel_id=1, source_target_pairs={{0,28},{4,24},{8,20},{12,16},{16,12},{20,8},{24,4},{28,0},{1,29},{... | collective-permute-start | bytes 884744 | tf_op jit(solution)/shard_map/ppermute | solution.py:537
  18.2 20.9 %collective-permute-start.10 = (f32[576,128]{1,0:T(8,128)}, f32[576,128]{1,0:T(8,128)}, u32[]{:S(2)}, u32[]{:S(2)}) collective-permute-start(f32[576,128]{1,0:T(8,128)} %get-tuple-element.19), channel_id=1, source_target_pairs={{0,16},{4,20},{8,24},{12,28},{16,0},{20,4},{24,8},{28,12},{1,17},{... | collective-permute-start | bytes 884744 | tf_op jit(solution)/shard_map/ppermute | solution.py:537
  20.7 20.9 %collective-permute-start.11 = (f32[576,128]{1,0:T(8,128)}, f32[576,128]{1,0:T(8,128)}, u32[]{:S(2)}, u32[]{:S(2)}) collective-permute-start(f32[576,128]{1,0:T(8,128)} %get-tuple-element.20), channel_id=1, source_target_pairs={{0,8},{4,12},{8,0},{12,4},{16,24},{20,28},{24,16},{28,20},{1,9},{5... | collective-permute-start | bytes 884744 | tf_op jit(solution)/shard_map/ppermute | solution.py:537
  22.0 25.6 %copy-start.1 = (f32[64,72,128]{2,1,0:T(8,128)S(1)}, f32[64,72,128]{2,1,0:T(8,128)}, u32[]{:S(2)}) copy-start(f32[64,72,128]{2,1,0:T(8,128)} %param.15) | copy-start | bytes 7077892
  22.1 25.4 %collective-permute-start.12 = (f32[576,128]{1,0:T(8,128)}, f32[576,128]{1,0:T(8,128)S(1)}, u32[]{:S(2)}, u32[]{:S(2)}) collective-permute-start(f32[576,128]{1,0:T(8,128)} %get-tuple-element.21), channel_id=1, source_target_pairs={{0,20},{4,16},{8,28},{12,24},{16,4},{20,0},{24,12},{28,8},{1,21},{... | collective-permute-start | bytes 884744 | tf_op jit(solution)/shard_map/ppermute | solution.py:537
  27.7 19.7 %collective-permute-start.13 = (f32[576,128]{1,0:T(8,128)}, f32[576,128]{1,0:T(8,128)S(1)}, u32[]{:S(2)}, u32[]{:S(2)}) collective-permute-start(f32[576,128]{1,0:T(8,128)} %get-tuple-element.22), channel_id=1, source_target_pairs={{0,12},{4,8},{8,4},{12,0},{16,28},{20,24},{24,20},{28,16},{1,13},{... | collective-permute-start | bytes 884744 | tf_op jit(solution)/shard_map/ppermute | solution.py:537
  33.5 13.9 %collective-permute-start.9 = (f32[576,128]{1,0:T(8,128)}, f32[576,128]{1,0:T(8,128)S(1)}, u32[]{:S(2)}, u32[]{:S(2)}) collective-permute-start(f32[576,128]{1,0:T(8,128)} %get-tuple-element.18), channel_id=1, source_target_pairs={{0,4},{4,0},{8,12},{12,8},{16,20},{20,16},{24,28},{28,24},{1,5},{5... | collective-permute-start | bytes 884744 | tf_op jit(solution)/shard_map/ppermute | solution.py:537
  39.2 13.7 %collective-permute-start.8 = (f32[576,128]{1,0:T(8,128)}, f32[576,128]{1,0:T(8,128)S(1)}, u32[]{:S(2)}, u32[]{:S(2)}) collective-permute-start(f32[576,128]{1,0:T(8,128)} %get-tuple-element.17), channel_id=1, source_target_pairs={{0,24},{4,28},{8,16},{12,20},{16,8},{20,12},{24,0},{28,4},{1,25},{... | collective-permute-start | bytes 884744 | tf_op jit(solution)/shard_map/ppermute | solution.py:537
  41.6 15.7 %collective-permute-start.7 = (f32[576,128]{1,0:T(8,128)}, f32[576,128]{1,0:T(8,128)S(1)}, u32[]{:S(2)}, u32[]{:S(2)}) collective-permute-start(f32[576,128]{1,0:T(8,128)} %get-tuple-element.16), channel_id=1, source_target_pairs={{0,28},{4,24},{8,20},{12,16},{16,12},{20,8},{24,4},{28,0},{1,29},{... | collective-permute-start | bytes 884744 | tf_op jit(solution)/shard_map/ppermute | solution.py:537
  53.3 6.5 %copy-start.2 = (bf16[2048,128]{1,0:T(8,128)(2,1)S(1)}, bf16[2048,128]{1,0:T(8,128)(2,1)}, u32[]{:S(2)}) copy-start(bf16[2048,128]{1,0:T(8,128)(2,1)} %constant.46.clone.gather_ref) | copy-start | bytes 1572868
  53.3 6.5 %copy-start.4 = (f32[72,128]{1,0:T(8,128)S(1)}, f32[72,128]{1,0:T(8,128)}, u32[]{:S(2)}) copy-start(f32[72,128]{1,0:T(8,128)} %equal_ref.5) | copy-start | bytes 110596
  53.4 6.5 %copy-start.5 = (f32[8,128]{1,0:T(8,128)S(1)}, f32[8,128]{1,0:T(8,128)}, u32[]{:S(2)}) copy-start(f32[8,128]{1,0:T(8,128)} %constant.45.clone.sign_ref) | copy-start | bytes 12292
  62.4 2.7 %collective-permute-start.14 = (f32[288,128]{1,0:T(8,128)S(1)}, f32[288,128]{1,0:T(8,128)S(1)}, u32[]{:S(2)}, u32[]{:S(2)}) collective-permute-start(f32[288,128]{1,0:T(8,128)S(1)} %contract.4), channel_id=1, source_target_pairs={{0,4},{4,0},{8,12},{12,8},{16,20},{20,16},{24,28},{28,24},{1,5},{5... | collective-permute-start | bytes 442376 | tf_op jit(solution)/shard_map/ppermute | solution.py:537
  65.2 4.9 %collective-permute-start.15 = (f32[72,128]{1,0:T(8,128)S(1)}, f32[72,128]{1,0:T(8,128)S(1)}, u32[]{:S(2)}, u32[]{:S(2)}) collective-permute-start(f32[72,128]{1,0:T(8,128)S(1)} %get-tuple-element.34), channel_id=1, source_target_pairs={{0,24},{4,28},{8,16},{12,20},{16,8},{20,12},{24,0},{28,4},{1,25},{... | collective-permute-start | bytes 110600 | tf_op jit(solution)/shard_map/ppermute | solution.py:537
  67.8 4.0 %collective-permute-start.16 = (f32[72,128]{1,0:T(8,128)S(1)}, f32[72,128]{1,0:T(8,128)S(1)}, u32[]{:S(2)}, u32[]{:S(2)}) collective-permute-start(f32[72,128]{1,0:T(8,128)S(1)} %get-tuple-element.32), channel_id=1, source_target_pairs={{0,16},{4,20},{8,24},{12,28},{16,0},{20,4},{24,8},{28,12},{1,17},{... | collective-permute-start | bytes 110600 | tf_op jit(solution)/shard_map/ppermute | solution.py:537
  68.3 4.0 %collective-permute-start.17 = (f32[72,128]{1,0:T(8,128)S(1)}, f32[72,128]{1,0:T(8,128)S(1)}, u32[]{:S(2)}, u32[]{:S(2)}) collective-permute-start(f32[72,128]{1,0:T(8,128)S(1)} %get-tuple-element.33), channel_id=1, source_target_pairs={{0,8},{4,12},{8,0},{12,4},{16,24},{20,28},{24,16},{28,20},{1,9},{5... | collective-permute-start | bytes 110600 | tf_op jit(solution)/shard_map/ppermute | solution.py:537
  72.3 8.5 %copy-start.7 = (f32[72,128]{1,0:T(8,128)S(1)}, f32[72,128]{1,0:T(8,128)}, u32[]{:S(2)}) copy-start(f32[72,128]{1,0:T(8,128)} %param.16) | copy-start | bytes 110596
  72.3 8.5 %copy-start.3 = (bf16[256,2048]{1,0:T(8,128)(2,1)S(1)}, bf16[256,2048]{1,0:T(8,128)(2,1)}, u32[]{:S(2)}) copy-start(bf16[256,2048]{1,0:T(8,128)(2,1)} %constant.47.clone.spread_ref) | copy-start | bytes 3145732
  72.4 5.9 %collective-permute-start.18 = (f32[72,128]{1,0:T(8,128)S(1)}, f32[72,128]{1,0:T(8,128)S(1)}, u32[]{:S(2)}, u32[]{:S(2)}) collective-permute-start(f32[72,128]{1,0:T(8,128)S(1)} %slice_add_fusion.1), channel_id=1, source_target_pairs={{0,3},{1,2},{2,1},{3,0},{4,7},{5,6},{6,5},{7,4},{8,11},{9,10},{10,... | collective-permute-start | bytes 110600 | tf_op jit(solution)/shard_map/ppermute | solution.py:537
  76.0 4.9 %collective-permute-start.19 = (f32[72,128]{1,0:T(8,128)S(1)}, f32[72,128]{1,0:T(8,128)S(1)}, u32[]{:S(2)}, u32[]{:S(2)}) collective-permute-start(f32[72,128]{1,0:T(8,128)S(1)} %slice_add_fusion.1), channel_id=1, source_target_pairs={{0,2},{1,3},{2,0},{3,1},{4,6},{5,7},{6,4},{7,5},{8,10},{9,11},{10,... | collective-permute-start | bytes 110600 | tf_op jit(solution)/shard_map/ppermute | solution.py:537
  76.0 4.9 %collective-permute-start.20 = (f32[72,128]{1,0:T(8,128)S(1)}, f32[72,128]{1,0:T(8,128)S(1)}, u32[]{:S(2)}, u32[]{:S(2)}) collective-permute-start(f32[72,128]{1,0:T(8,128)S(1)} %slice_add_fusion.1), channel_id=1, source_target_pairs={{0,1},{1,0},{2,3},{3,2},{4,5},{5,4},{6,7},{7,6},{8,9},{9,8},{10,11... | collective-permute-start | bytes 110600 | tf_op jit(solution)/shard_map/ppermute | solution.py:537

commit v17 on v16

--- a/solution.py
+++ b/solution.py
@@ -22,6 +22,7 @@
 quadrature = (0.375, 1.1666666, 0.9583333, 1.0)
 
 AT_ONCE = 4
+COLUMNS = 3
 LATE = 2
 AHEAD = 3
 
@@ -102,16 +103,16 @@
 
 
 def along_first(work_ref, sign, low, store):
-    def columns(pair, carry):
-        both = (2 * pair, 2 * pair + 1)
-        rows = [[work_ref[k1 * SIDE + column] for k1 in range(SIDE)] for column in both]
+    def columns(group, carry):
+        some = [COLUMNS * group + n for n in range(COLUMNS)]
+        rows = [[work_ref[k1 * SIDE + column] for k1 in range(SIDE)] for column in some]
         values = [dft24(row, sign, low) for row in rows]
-        for column, value in zip(both, values):
+        for column, value in zip(some, values):
             for r1 in range(SIDE):
                 store(r1 * SIDE + column, value[r1])
         return carry
 
-    lax.fori_loop(0, SIDE // 2, columns, 0)
+    lax.fori_loop(0, SIDE // COLUMNS, columns, 0)
 
 
 def pick_kernel(steps, parts, place_ref, whole_ref, *refs):
@@ -414,7 +415,7 @@
         in_specs=[in_smem()] + [anywhere()] * len(steps),
         out_specs=[in_vmem()] * 2,
         scratch_shapes=[pltpu.VMEM((points, TILE, WIDTH), jnp.float32)] + held_blocks(len(steps), parts),
-        compiler_params=params(8),
+        compiler_params=params(6),
         cost_estimate=cost(400, 6),
         name="forward",
     )(place, *greens)
@@ -451,7 +452,7 @@
         out_specs=[in_vmem()] * 2,
         input_output_aliases={len(inputs) - 1: 0},
         scratch_shapes=held_blocks(len(steps), parts) if steps else [],
-        compiler_params=params(4),
+        compiler_params=params(2),
         cost_estimate=cost(200, 6),
         name="sigma",
     )(*inputs)
@@ -471,7 +472,7 @@
             pltpu.VMEM((rows, STEPS * STEPS * WIDTH), jnp.float32),
             pltpu.VMEM((rows, STEPS * STEPS * WIDTH), jnp.bfloat16),
         ],
-        compiler_params=params(10),
+        compiler_params=params(6),
         cost_estimate=cost(70 * owners.shape[0], 6),
         name="contract",
     )(owners, sigma, equal_time, jnp.asarray(signs), jnp.asarray(gather), greens, *before)
@@ -518,7 +519,7 @@
             pltpu.VMEM((2, history, tile, width), jnp.float32),
             pltpu.SemaphoreType.DMA((2,)),
         ],
-        compiler_params=params(6),
+        compiler_params=params(3),
         cost_estimate=cost(32, 5),
         name="propagate",
     )(greens, pieces, effective, jnp.asarray(spread))

time: 86.4 us -> 85.8 us (level)
  Pallas kernels: 25.4 us -> 24.3 us
  transfers between devices with their start and end apart: 21 -> 21, of which waited for: 13 -> 13; matrix products, arithmetic and copies ran while one was open for 0% -> 0% of each run, Pallas kernels for 18% -> 17%
where the time goes in v17:
time: 85.8 us; the launch traced here: 85.6 us
  waiting for transfers between devices  34.6 us (40%)
  Pallas kernels  24.3 us (28%)
  starting transfers between devices  22.9 us (27%)
  local copies, waits for them, and re-layouts  2.65 us (3%)
  between operations  0.89 us (1%)
    ppermute x21, waiting for transfers between devices, exchange(): return lax.ppermute(value, axis, pairs)  34.6 us
    ppermute x21, starting transfers between devices, exchange(): return lax.ppermute(value, axis, pairs)  22.9 us
    pallas_call x1, Pallas kernels, propagate(): pl.pallas_call(propagate_kernel, out_shape=jax.ShapeDtypeStruct(greens.sh...  5.29 us
    pallas_call x3, Pallas kernels, contract(): pl.pallas_call(functools.partial(contract_kernel, share), out_shape=jax.S...  5.28 us
    pallas_call x1, Pallas kernels, forward(): pl.pallas_call(functools.partial(forward_kernel, steps, parts), out_shape...  5.06 us
    pallas_call x2, Pallas kernels, early_lines(): pl.pallas_call(functools.partial(early_kernel, steps, parts), out_shape=j...  3.19 us
    pallas_call x1, Pallas kernels, pick(): pl.pallas_call(functools.partial(pick_kernel, steps, parts), out_shape=[j...  2.83 us
    dynamic_slice x1, local copies, waits for them, and re-layouts, per_device(): lax.dynamic_slice_in_dim(wholes[0], partner_of(place, step, parts) * (TIL...  2.43 us
  transfers between devices with their start and end apart: 21, of which 13 were waited for; matrix products, arithmetic and copies ran while one was open for 0% of the time, Pallas kernels for 17%

profile of v17, /device:TPU:0, one launch (start us, length us, event | category | flops | bytes accessed | tf_op | source)
XLA Modules:
  0.0 85.6 jit_solution(9525648936164117583)
XLA Ops:
  0.0 2.4 %constant_dynamic-slice_fusion = (f32[576,128]{1,0:T(8,128)}, f32[576,128]{1,0:T(8,128)}, f32[576,128]{1,0:T(8,128)}, f32[576,128]{1,0:T(8,128)S(1)}, f32[576,12...) fusion(f32[4608,128]{1,0:T(8,128)} %bitcast.12, s32[]{:T(128)S(6)} %select_n.38, s32[]{:T(128)S(6)} %select_n.37, ...), kind=kLoop, calls=%fused_computation.6 | loop fusion | bytes 4128796 | tf_op jit(solution)/shard_map/dynamic_slice | solution.py:575
  2.5 3.0 %collective-permute-start = (f32[576,128]{1,0:T(8,128)S(1)}, f32[576,128]{1,0:T(8,128)S(1)}, u32[]{:S(2)}, u32[]{:S(2)}) collective-permute-start(f32[576,128]{1,0:T(8,128)S(1)} %get-tuple-element.31.refs_0_), channel_id=1, source_target_pairs={{0,16},{4,20},{8,24},{12,28},{16,0},{20,4},{24,8},{28,12},{1,17},{... | collective-permute-start | bytes 884744 | tf_op jit(solution)/shard_map/ppermute | solution.py:538
  5.5 1.5 %collective-permute-start.1 = (f32[576,128]{1,0:T(8,128)S(1)}, f32[576,128]{1,0:T(8,128)S(1)}, u32[]{:S(2)}, u32[]{:S(2)}) collective-permute-start(f32[576,128]{1,0:T(8,128)S(1)} %get-tuple-element.30), channel_id=1, source_target_pairs={{0,8},{4,12},{8,0},{12,4},{16,24},{20,28},{24,16},{28,20},{1,9},{5... | collective-permute-start | bytes 884744 | tf_op jit(solution)/shard_map/ppermute | solution.py:538
  7.0 0.3 collective-permute-start.3
  7.3 0.3 collective-permute-start.4
  7.6 2.8 %pick.1 = (f32[576,128]{1,0:T(8,128)}, f32[576,128]{1,0:T(8,128)}, f32[576,128]{1,0:T(8,128)}, f32[576,128]{1,0:T(8,128)}, f32[576,128]{1,0:T(8,128)}, /*index=5*/f32[576,128]{1,0:T(8,128)}, f32[576,128]{1,0:T(8,128)}) custom-call(s32[1]{0:T(128)} %bitcast.3.place_ref.owner_ref, f32[4608,128]{1,0:T(8,128)} %bitcast.14, f32[576,128]{1,0:T(8,128)} %copy-done.6), custom_call_target="tpu_custom_call" | custom-call | bytes 4718592 | tf_op jit(solution)/shard_map/pick/pallas_call | solution.py:483
  10.5 2.9 %collective-permute-done.refs_1_ = f32[576,128]{1,0:T(8,128)S(1)} collective-permute-done((f32[576,128]{1,0:T(8,128)S(1)}, f32[576,128]{1,0:T(8,128)S(1)}, u32[]{:S(2)}, u32[]{:S(2)}) %collective-permute-start) | collective-permute-done | bytes 294944 | tf_op jit(solution)/shard_map/ppermute | solution.py:538
  13.3 3.0 %collective-permute-start.5 = (f32[576,128]{1,0:T(8,128)}, f32[576,128]{1,0:T(8,128)}, u32[]{:S(2)}, u32[]{:S(2)}) collective-permute-start(f32[576,128]{1,0:T(8,128)} %get-tuple-element.26), channel_id=1, source_target_pairs={{0,24},{4,28},{8,16},{12,20},{16,8},{20,12},{24,0},{28,4},{1,25},{... | collective-permute-start | bytes 884744 | tf_op jit(solution)/shard_map/ppermute | solution.py:538
  16.3 1.9 %collective-permute-done.2.refs_3_ = f32[576,128]{1,0:T(8,128)S(1)} collective-permute-done((f32[576,128]{1,0:T(8,128)S(1)}, f32[576,128]{1,0:T(8,128)S(1)}, u32[]{:S(2)}, u32[]{:S(2)}) %collective-permute-start.2) | collective-permute-done | bytes 294944 | tf_op jit(solution)/shard_map/ppermute | solution.py:538
  18.2 1.2 %collective-permute-start.10 = (f32[576,128]{1,0:T(8,128)}, f32[576,128]{1,0:T(8,128)}, u32[]{:S(2)}, u32[]{:S(2)}) collective-permute-start(f32[576,128]{1,0:T(8,128)} %get-tuple-element.19), channel_id=1, source_target_pairs={{0,16},{4,20},{8,24},{12,28},{16,0},{20,4},{24,8},{28,12},{1,17},{... | collective-permute-start | bytes 884744 | tf_op jit(solution)/shard_map/ppermute | solution.py:538
  19.4 1.3 %collective-permute-done.3.refs_4_ = f32[576,128]{1,0:T(8,128)S(1)} collective-permute-done((f32[576,128]{1,0:T(8,128)S(1)}, f32[576,128]{1,0:T(8,128)S(1)}, u32[]{:S(2)}, u32[]{:S(2)}) %collective-permute-start.3) | collective-permute-done | bytes 294944 | tf_op jit(solution)/shard_map/ppermute | solution.py:538
  20.7 0.5 collective-permute-start.11
  22.0 0.1 select_reduce_fusion
  22.1 1.7 %collective-permute-start.12 = (f32[576,128]{1,0:T(8,128)}, f32[576,128]{1,0:T(8,128)S(1)}, u32[]{:S(2)}, u32[]{:S(2)}) collective-permute-start(f32[576,128]{1,0:T(8,128)} %get-tuple-element.21), channel_id=1, source_target_pairs={{0,20},{4,16},{8,28},{12,24},{16,4},{20,0},{24,12},{28,8},{1,21},{... | collective-permute-start | bytes 884744 | tf_op jit(solution)/shard_map/ppermute | solution.py:538
  23.7 4.0 %collective-permute-done.5.refs_6_ = f32[576,128]{1,0:T(8,128)} collective-permute-done((f32[576,128]{1,0:T(8,128)}, f32[576,128]{1,0:T(8,128)}, u32[]{:S(2)}, u32[]{:S(2)}) %collective-permute-start.5) | collective-permute-done | bytes 294944 | tf_op jit(solution)/shard_map/ppermute | solution.py:538
  27.7 5.8 %collective-permute-done.6.refs_7_ = f32[576,128]{1,0:T(8,128)} collective-permute-done((f32[576,128]{1,0:T(8,128)}, f32[576,128]{1,0:T(8,128)}, u32[]{:S(2)}, u32[]{:S(2)}) %collective-permute-start.6) | collective-permute-done | bytes 294944 | tf_op jit(solution)/shard_map/ppermute | solution.py:538
  33.5 0.3 collective-permute-start.9
  33.8 5.3 %collective-permute-done.10.refs_2_ = f32[576,128]{1,0:T(8,128)} collective-permute-done((f32[576,128]{1,0:T(8,128)}, f32[576,128]{1,0:T(8,128)}, u32[]{:S(2)}, u32[]{:S(2)}) %collective-permute-start.10) | collective-permute-done | bytes 294944 | tf_op jit(solution)/shard_map/ppermute | solution.py:538
  39.2 2.5 %collective-permute-start.8 = (f32[576,128]{1,0:T(8,128)}, f32[576,128]{1,0:T(8,128)S(1)}, u32[]{:S(2)}, u32[]{:S(2)}) collective-permute-start(f32[576,128]{1,0:T(8,128)} %get-tuple-element.17), channel_id=1, source_target_pairs={{0,24},{4,28},{8,16},{12,20},{16,8},{20,12},{24,0},{28,4},{1,25},{... | collective-permute-start | bytes 884744 | tf_op jit(solution)/shard_map/ppermute | solution.py:538
  41.6 0.1 dynamic_slice.31
  41.7 0.1 pad_add_fusion.1.owner_ref
  41.8 5.1 %forward.1 = (f32[576,8,128]{2,1,0:T(8,128)S(1)}, f32[4,4608,128]{2,1,0:T(8,128)S(1)}) custom-call(s32[1]{0:T(128)} %bitcast.3.place_ref.owner_ref, f32[4608,128]{1,0:T(8,128)S(1)} %bitcast.13, f32[576,128]{1,0:T(8,128)S(1)} %collective-permute-done.refs_1_, f32[576,128]{1,0:T(8,128)S(1)} %collective-permute-done.1.refs_2_, ...), custom_call_target="tpu_custom_call" | custom-call | flops 235929600 | bytes 14155776 | tf_op jit(solution)/shard_map/forward/pallas_call | solution.py:409
  46.9 0.1 squeeze.9.weight_ref
  47.0 2.7 %early.2.refs_1_ = f32[576,8,128]{2,1,0:T(8,128)S(1)} custom-call(s32[1]{0:T(128)} %bitcast.3.place_ref.owner_ref, f32[576,8,128]{2,1,0:T(8,128)S(1)} %get-tuple-element.15.lattice_ref, f32[8,128]{1,0:T(8,128)S(1)} %squeeze.9.weight_ref, f32[576,128]{1,0:T(8,128)S(1)} %collective-permute-done.9.refs_0_, f32[4608,128]{1,0:T(8,128)S(1)} %bitcast.15, ...), custom_call_target="tpu_custom_call" | custom-call | flops 88473600 | bytes 7077888 | tf_op jit(solution)/shard_map/early/pallas_call | solution.py:427
  49.7 3.2 %collective-permute-done.8.refs_0_ = f32[576,128]{1,0:T(8,128)S(1)} collective-permute-done((f32[576,128]{1,0:T(8,128)}, f32[576,128]{1,0:T(8,128)S(1)}, u32[]{:S(2)}, u32[]{:S(2)}) %collective-permute-start.8) | collective-permute-done | bytes 294944 | tf_op jit(solution)/shard_map/ppermute | solution.py:538
  52.9 0.5 early.3.refs_1_
  53.3 0.0 copy-start.2
  53.4 0.0 copy-start.5
  53.4 4.0 %collective-permute-done.7.refs_0_ = f32[576,128]{1,0:T(8,128)S(1)} collective-permute-done((f32[576,128]{1,0:T(8,128)}, f32[576,128]{1,0:T(8,128)S(1)}, u32[]{:S(2)}, u32[]{:S(2)}) %collective-permute-start.7) | collective-permute-done | bytes 294944 | tf_op jit(solution)/shard_map/ppermute | solution.py:538
  57.4 1.9 %sigma.1 = (f32[576,8,128]{2,1,0:T(8,128)S(1)}, f32[4608,128]{1,0:T(8,128)S(1)}) custom-call(s32[1]{0:T(128)} %bitcast.3.place_ref.owner_ref, f32[576,8,128]{2,1,0:T(8,128)S(1)} %get-tuple-element.15.lattice_ref, f32[8,128]{1,0:T(8,128)S(1)} %squeeze.9.weight_ref, f32[576,128]{1,0:T(8,128)S(1)} %collective-permute-done.7.refs_0_, ...), custom_call_target="tpu_custom_call", output_to_operand_aliasing={{0}: (4, {})} | custom-call | flops 117964800 | bytes 14155776 | tf_op jit(solution)/shard_map/sigma/pallas_call | solution.py:445
  59.3 2.5 %contract.4 = f32[288,128]{1,0:T(8,128)S(1)} custom-call(s32[4]{0:T(128)S(1)} %pad_add_fusion.1.owner_ref, f32[4608,128]{1,0:T(8,128)S(1)} %get-tuple-element.23.sigma_ref, f32[72,128]{1,0:T(8,128)S(1)} %copy-done.4, f32[8,128]{1,0:T(8,128)S(1)} %copy-done.5, bf16[2048,128]{1,0:T(8,128)(2,1)S(1)} %copy-done.2, f32[4,4608,128]{2,1,0:T(8,128)S(1)} %get-tuple-element.24.greens_ref), custom_call_target="tpu_custom_call" | custom-call | flops 165150720 | bytes 14155776 | tf_op jit(solution)/shard_map/contract/pallas_call | solution.py:466
  61.8 0.6 collective-permute-start.14
  62.4 0.1 pad_add_fusion.owner_ref
  62.5 2.1 %contract.3 = f32[216,128]{1,0:T(8,128)S(1)} custom-call(s32[3]{0:T(128)S(1)} %pad_add_fusion.owner_ref, f32[4608,128]{1,0:T(8,128)S(1)} %get-tuple-element.23.sigma_ref, f32[72,128]{1,0:T(8,128)S(1)} %copy-done.4, f32[8,128]{1,0:T(8,128)S(1)} %copy-done.5, bf16[2048,128]{1,0:T(8,128)(2,1)S(1)} %copy-done.2, f32[4,4608,128]{2,1,0:T(8,128)S(1)} %get-tuple-element.24.greens_ref), custom_call_target="tpu_custom_call" | custom-call | flops 123863040 | bytes 14155776 | tf_op jit(solution)/shard_map/contract/pallas_call | solution.py:466
  64.6 2.7 %collective-permute-start.15 = (f32[72,128]{1,0:T(8,128)S(1)}, f32[72,128]{1,0:T(8,128)S(1)}, u32[]{:S(2)}, u32[]{:S(2)}) collective-permute-start(f32[72,128]{1,0:T(8,128)S(1)} %get-tuple-element.34), channel_id=1, source_target_pairs={{0,24},{4,28},{8,16},{12,20},{16,8},{20,12},{24,0},{28,4},{1,25},{... | collective-permute-start | bytes 110600 | tf_op jit(solution)/shard_map/ppermute | solution.py:538
  67.3 0.5 collective-permute-start.16
  67.8 0.4 collective-permute-start.17
  68.2 1.4 %collective-permute-done.15.refs_0_ = f32[72,128]{1,0:T(8,128)S(1)} collective-permute-done((f32[72,128]{1,0:T(8,128)S(1)}, f32[72,128]{1,0:T(8,128)S(1)}, u32[]{:S(2)}, u32[]{:S(2)}) %collective-permute-start.15) | collective-permute-done | bytes 36896 | tf_op jit(solution)/shard_map/ppermute | solution.py:538
  69.5 0.6 contract.5
  70.2 1.1 %collective-permute-done.16 = f32[72,128]{1,0:T(8,128)S(1)} collective-permute-done((f32[72,128]{1,0:T(8,128)S(1)}, f32[72,128]{1,0:T(8,128)S(1)}, u32[]{:S(2)}, u32[]{:S(2)}) %collective-permute-start.16) | collective-permute-done | bytes 36896 | tf_op jit(solution)/shard_map/ppermute | solution.py:538
  71.2 0.5 collective-permute-done.17
  71.8 0.0 copy-start.3
  71.8 3.7 %collective-permute-start.18 = (f32[72,128]{1,0:T(8,128)S(1)}, f32[72,128]{1,0:T(8,128)S(1)}, u32[]{:S(2)}, u32[]{:S(2)}) collective-permute-start(f32[72,128]{1,0:T(8,128)S(1)} %slice_add_fusion.1), channel_id=1, source_target_pairs={{0,3},{1,2},{2,1},{3,0},{4,7},{5,6},{6,5},{7,4},{8,11},{9,10},{10,... | collective-permute-start | bytes 110600 | tf_op jit(solution)/shard_map/ppermute | solution.py:538
  75.5 0.8 collective-permute-start.20
  76.2 0.8 split_own.1.split_ref
  77.0 0.7 collective-permute-done.18
  77.7 2.6 %collective-permute-done.19 = f32[72,128]{1,0:T(8,128)S(1)} collective-permute-done((f32[72,128]{1,0:T(8,128)S(1)}, f32[72,128]{1,0:T(8,128)S(1)}, u32[]{:S(2)}, u32[]{:S(2)}) %collective-permute-start.19) | collective-permute-done | bytes 36896 | tf_op jit(solution)/shard_map/ppermute | solution.py:538
  80.3 5.3 %propagate.1 = f32[64,72,128]{2,1,0:T(8,128)} custom-call(f32[64,72,128]{2,1,0:T(8,128)S(1)} %copy-done, bf16[72,64,384]{2,1,0:T(8,128)(2,1)S(1)} %split_own.1.split_ref, f32[72,128]{1,0:T(8,128)S(1)} %add_add_fusion.effective_ref, bf16[256,2048]{1,0:T(8,128)(2,1)S(1)} %copy-done.3), custom_call_target="tpu_custom_call" | custom-call | flops 18874368 | bytes 11796480 | tf_op jit(solution)/shard_map/propagate/pallas_call | solution.py:512
  (35 shorter events, 0.1 us)
Async XLA Ops:
  2.4 5.2 %copy-start.6 = (f32[576,128]{1,0:T(8,128)}, f32[576,128]{1,0:T(8,128)S(1)}, u32[]{:S(2)}) copy-start(f32[576,128]{1,0:T(8,128)S(1)} %get-tuple-element.31.refs_0_) | copy-start | bytes 884740
  2.4 19.5 %copy-start.8 = (s32[64]{0:T(128)S(1)}, s32[64]{0:T(128)}, u32[]{:S(2)}) copy-start(s32[64]{0:T(128)} %param.18) | copy-start | bytes 772
  2.4 19.5 %copy-start.9 = (f32[4]{0:T(128)S(1)}, f32[4]{0:T(128)}, u32[]{:S(2)}) copy-start(f32[4]{0:T(128)} %constant.44.clone) | copy-start | bytes 52
  2.4 39.3 %copy-start = (f32[64,72,128]{2,1,0:T(8,128)S(1)}, f32[64,72,128]{2,1,0:T(8,128)}, u32[]{:S(2)}) copy-start(f32[64,72,128]{2,1,0:T(8,128)} %green_ref.3) | copy-start | bytes 7077892
  2.5 10.9 %collective-permute-start = (f32[576,128]{1,0:T(8,128)S(1)}, f32[576,128]{1,0:T(8,128)S(1)}, u32[]{:S(2)}, u32[]{:S(2)}) collective-permute-start(f32[576,128]{1,0:T(8,128)S(1)} %get-tuple-element.31.refs_0_), channel_id=1, source_target_pairs={{0,16},{4,20},{8,24},{12,28},{16,0},{20,4},{24,8},{28,12},{1,17},{... | collective-permute-start | bytes 884744 | tf_op jit(solution)/shard_map/ppermute | solution.py:538
  5.5 10.8 %collective-permute-start.1 = (f32[576,128]{1,0:T(8,128)S(1)}, f32[576,128]{1,0:T(8,128)S(1)}, u32[]{:S(2)}, u32[]{:S(2)}) collective-permute-start(f32[576,128]{1,0:T(8,128)S(1)} %get-tuple-element.30), channel_id=1, source_target_pairs={{0,8},{4,12},{8,0},{12,4},{16,24},{20,28},{24,16},{28,20},{1,9},{5... | collective-permute-start | bytes 884744 | tf_op jit(solution)/shard_map/ppermute | solution.py:538
  7.0 11.2 %collective-permute-start.2 = (f32[576,128]{1,0:T(8,128)S(1)}, f32[576,128]{1,0:T(8,128)S(1)}, u32[]{:S(2)}, u32[]{:S(2)}) collective-permute-start(f32[576,128]{1,0:T(8,128)S(1)} %get-tuple-element.29), channel_id=1, source_target_pairs={{0,20},{4,16},{8,28},{12,24},{16,4},{20,0},{24,12},{28,8},{1,21},{... | collective-permute-start | bytes 884744 | tf_op jit(solution)/shard_map/ppermute | solution.py:538
  7.0 13.8 %collective-permute-start.3 = (f32[576,128]{1,0:T(8,128)S(1)}, f32[576,128]{1,0:T(8,128)S(1)}, u32[]{:S(2)}, u32[]{:S(2)}) collective-permute-start(f32[576,128]{1,0:T(8,128)S(1)} %get-tuple-element.28), channel_id=1, source_target_pairs={{0,12},{4,8},{8,4},{12,0},{16,28},{20,24},{24,20},{28,16},{1,13},{... | collective-permute-start | bytes 884744 | tf_op jit(solution)/shard_map/ppermute | solution.py:538
  7.3 14.7 %collective-permute-start.4 = (f32[576,128]{1,0:T(8,128)}, f32[576,128]{1,0:T(8,128)}, u32[]{:S(2)}, u32[]{:S(2)}) collective-permute-start(f32[576,128]{1,0:T(8,128)} %get-tuple-element.27), channel_id=1, source_target_pairs={{0,4},{4,0},{8,12},{12,8},{16,20},{20,16},{24,28},{28,24},{1,5},{5... | collective-permute-start | bytes 884744 | tf_op jit(solution)/shard_map/ppermute | solution.py:538
  13.3 14.4 %collective-permute-start.5 = (f32[576,128]{1,0:T(8,128)}, f32[576,128]{1,0:T(8,128)}, u32[]{:S(2)}, u32[]{:S(2)}) collective-permute-start(f32[576,128]{1,0:T(8,128)} %get-tuple-element.26), channel_id=1, source_target_pairs={{0,24},{4,28},{8,16},{12,20},{16,8},{20,12},{24,0},{28,4},{1,25},{... | collective-permute-start | bytes 884744 | tf_op jit(solution)/shard_map/ppermute | solution.py:538
  16.3 17.2 %collective-permute-start.6 = (f32[576,128]{1,0:T(8,128)}, f32[576,128]{1,0:T(8,128)}, u32[]{:S(2)}, u32[]{:S(2)}) collective-permute-start(f32[576,128]{1,0:T(8,128)} %get-tuple-element.25), channel_id=1, source_target_pairs={{0,28},{4,24},{8,20},{12,16},{16,12},{20,8},{24,4},{28,0},{1,29},{... | collective-permute-start | bytes 884744 | tf_op jit(solution)/shard_map/ppermute | solution.py:538
  18.2 20.9 %collective-permute-start.10 = (f32[576,128]{1,0:T(8,128)}, f32[576,128]{1,0:T(8,128)}, u32[]{:S(2)}, u32[]{:S(2)}) collective-permute-start(f32[576,128]{1,0:T(8,128)} %get-tuple-element.19), channel_id=1, source_target_pairs={{0,16},{4,20},{8,24},{12,28},{16,0},{20,4},{24,8},{28,12},{1,17},{... | collective-permute-start | bytes 884744 | tf_op jit(solution)/shard_map/ppermute | solution.py:538
  20.7 20.9 %collective-permute-start.11 = (f32[576,128]{1,0:T(8,128)}, f32[576,128]{1,0:T(8,128)}, u32[]{:S(2)}, u32[]{:S(2)}) collective-permute-start(f32[576,128]{1,0:T(8,128)} %get-tuple-element.20), channel_id=1, source_target_pairs={{0,8},{4,12},{8,0},{12,4},{16,24},{20,28},{24,16},{28,20},{1,9},{5... | collective-permute-start | bytes 884744 | tf_op jit(solution)/shard_map/ppermute | solution.py:538
  22.0 25.0 %copy-start.1 = (f32[64,72,128]{2,1,0:T(8,128)S(1)}, f32[64,72,128]{2,1,0:T(8,128)}, u32[]{:S(2)}) copy-start(f32[64,72,128]{2,1,0:T(8,128)} %param.15) | copy-start | bytes 7077892
  22.1 24.8 %collective-permute-start.12 = (f32[576,128]{1,0:T(8,128)}, f32[576,128]{1,0:T(8,128)S(1)}, u32[]{:S(2)}, u32[]{:S(2)}) collective-permute-start(f32[576,128]{1,0:T(8,128)} %get-tuple-element.21), channel_id=1, source_target_pairs={{0,20},{4,16},{8,28},{12,24},{16,4},{20,0},{24,12},{28,8},{1,21},{... | collective-permute-start | bytes 884744 | tf_op jit(solution)/shard_map/ppermute | solution.py:538
  27.7 19.1 %collective-permute-start.13 = (f32[576,128]{1,0:T(8,128)}, f32[576,128]{1,0:T(8,128)S(1)}, u32[]{:S(2)}, u32[]{:S(2)}) collective-permute-start(f32[576,128]{1,0:T(8,128)} %get-tuple-element.22), channel_id=1, source_target_pairs={{0,12},{4,8},{8,4},{12,0},{16,28},{20,24},{24,20},{28,16},{1,13},{... | collective-permute-start | bytes 884744 | tf_op jit(solution)/shard_map/ppermute | solution.py:538
  33.5 13.3 %collective-permute-start.9 = (f32[576,128]{1,0:T(8,128)}, f32[576,128]{1,0:T(8,128)S(1)}, u32[]{:S(2)}, u32[]{:S(2)}) collective-permute-start(f32[576,128]{1,0:T(8,128)} %get-tuple-element.18), channel_id=1, source_target_pairs={{0,4},{4,0},{8,12},{12,8},{16,20},{20,16},{24,28},{28,24},{1,5},{5... | collective-permute-start | bytes 884744 | tf_op jit(solution)/shard_map/ppermute | solution.py:538
  39.2 13.7 %collective-permute-start.8 = (f32[576,128]{1,0:T(8,128)}, f32[576,128]{1,0:T(8,128)S(1)}, u32[]{:S(2)}, u32[]{:S(2)}) collective-permute-start(f32[576,128]{1,0:T(8,128)} %get-tuple-element.17), channel_id=1, source_target_pairs={{0,24},{4,28},{8,16},{12,20},{16,8},{20,12},{24,0},{28,4},{1,25},{... | collective-permute-start | bytes 884744 | tf_op jit(solution)/shard_map/ppermute | solution.py:538
  41.6 15.7 %collective-permute-start.7 = (f32[576,128]{1,0:T(8,128)}, f32[576,128]{1,0:T(8,128)S(1)}, u32[]{:S(2)}, u32[]{:S(2)}) collective-permute-start(f32[576,128]{1,0:T(8,128)} %get-tuple-element.16), channel_id=1, source_target_pairs={{0,28},{4,24},{8,20},{12,16},{16,12},{20,8},{24,4},{28,0},{1,29},{... | collective-permute-start | bytes 884744 | tf_op jit(solution)/shard_map/ppermute | solution.py:538
  53.3 5.9 %copy-start.2 = (bf16[2048,128]{1,0:T(8,128)(2,1)S(1)}, bf16[2048,128]{1,0:T(8,128)(2,1)}, u32[]{:S(2)}) copy-start(bf16[2048,128]{1,0:T(8,128)(2,1)} %constant.46.clone.gather_ref) | copy-start | bytes 1572868
  53.3 5.9 %copy-start.4 = (f32[72,128]{1,0:T(8,128)S(1)}, f32[72,128]{1,0:T(8,128)}, u32[]{:S(2)}) copy-start(f32[72,128]{1,0:T(8,128)} %equal_ref.5) | copy-start | bytes 110596
  53.4 5.9 %copy-start.5 = (f32[8,128]{1,0:T(8,128)S(1)}, f32[8,128]{1,0:T(8,128)}, u32[]{:S(2)}) copy-start(f32[8,128]{1,0:T(8,128)} %constant.45.clone.sign_ref) | copy-start | bytes 12292
  61.8 2.7 %collective-permute-start.14 = (f32[288,128]{1,0:T(8,128)S(1)}, f32[288,128]{1,0:T(8,128)S(1)}, u32[]{:S(2)}, u32[]{:S(2)}) collective-permute-start(f32[288,128]{1,0:T(8,128)S(1)} %contract.4), channel_id=1, source_target_pairs={{0,4},{4,0},{8,12},{12,8},{16,20},{20,16},{24,28},{28,24},{1,5},{5... | collective-permute-start | bytes 442376 | tf_op jit(solution)/shard_map/ppermute | solution.py:538
  64.6 4.9 %collective-permute-start.15 = (f32[72,128]{1,0:T(8,128)S(1)}, f32[72,128]{1,0:T(8,128)S(1)}, u32[]{:S(2)}, u32[]{:S(2)}) collective-permute-start(f32[72,128]{1,0:T(8,128)S(1)} %get-tuple-element.34), channel_id=1, source_target_pairs={{0,24},{4,28},{8,16},{12,20},{16,8},{20,12},{24,0},{28,4},{1,25},{... | collective-permute-start | bytes 110600 | tf_op jit(solution)/shard_map/ppermute | solution.py:538
  67.3 4.0 %collective-permute-start.16 = (f32[72,128]{1,0:T(8,128)S(1)}, f32[72,128]{1,0:T(8,128)S(1)}, u32[]{:S(2)}, u32[]{:S(2)}) collective-permute-start(f32[72,128]{1,0:T(8,128)S(1)} %get-tuple-element.32), channel_id=1, source_target_pairs={{0,16},{4,20},{8,24},{12,28},{16,0},{20,4},{24,8},{28,12},{1,17},{... | collective-permute-start | bytes 110600 | tf_op jit(solution)/shard_map/ppermute | solution.py:538
  67.8 4.0 %collective-permute-start.17 = (f32[72,128]{1,0:T(8,128)S(1)}, f32[72,128]{1,0:T(8,128)S(1)}, u32[]{:S(2)}, u32[]{:S(2)}) collective-permute-start(f32[72,128]{1,0:T(8,128)S(1)} %get-tuple-element.33), channel_id=1, source_target_pairs={{0,8},{4,12},{8,0},{12,4},{16,24},{20,28},{24,16},{28,20},{1,9},{5... | collective-permute-start | bytes 110600 | tf_op jit(solution)/shard_map/ppermute | solution.py:538
  71.7 8.6 %copy-start.7 = (f32[72,128]{1,0:T(8,128)S(1)}, f32[72,128]{1,0:T(8,128)}, u32[]{:S(2)}) copy-start(f32[72,128]{1,0:T(8,128)} %param.16) | copy-start | bytes 110596
  71.8 8.6 %copy-start.3 = (bf16[256,2048]{1,0:T(8,128)(2,1)S(1)}, bf16[256,2048]{1,0:T(8,128)(2,1)}, u32[]{:S(2)}) copy-start(bf16[256,2048]{1,0:T(8,128)(2,1)} %constant.47.clone.spread_ref) | copy-start | bytes 3145732
  71.8 5.9 %collective-permute-start.18 = (f32[72,128]{1,0:T(8,128)S(1)}, f32[72,128]{1,0:T(8,128)S(1)}, u32[]{:S(2)}, u32[]{:S(2)}) collective-permute-start(f32[72,128]{1,0:T(8,128)S(1)} %slice_add_fusion.1), channel_id=1, source_target_pairs={{0,3},{1,2},{2,1},{3,0},{4,7},{5,6},{6,5},{7,4},{8,11},{9,10},{10,... | collective-permute-start | bytes 110600 | tf_op jit(solution)/shard_map/ppermute | solution.py:538
  75.5 4.9 %collective-permute-start.19 = (f32[72,128]{1,0:T(8,128)S(1)}, f32[72,128]{1,0:T(8,128)S(1)}, u32[]{:S(2)}, u32[]{:S(2)}) collective-permute-start(f32[72,128]{1,0:T(8,128)S(1)} %slice_add_fusion.1), channel_id=1, source_target_pairs={{0,2},{1,3},{2,0},{3,1},{4,6},{5,7},{6,4},{7,5},{8,10},{9,11},{10,... | collective-permute-start | bytes 110600 | tf_op jit(solution)/shard_map/ppermute | solution.py:538
  75.5 4.9 %collective-permute-start.20 = (f32[72,128]{1,0:T(8,128)S(1)}, f32[72,128]{1,0:T(8,128)S(1)}, u32[]{:S(2)}, u32[]{:S(2)}) collective-permute-start(f32[72,128]{1,0:T(8,128)S(1)} %slice_add_fusion.1), channel_id=1, source_target_pairs={{0,1},{1,0},{2,3},{3,2},{4,5},{5,4},{6,7},{7,6},{8,9},{9,8},{10,11... | collective-permute-start | bytes 110600 | tf_op jit(solution)/shard_map/ppermute | solution.py:538

commit v18 on v17

--- a/solution.py
+++ b/solution.py
@@ -22,7 +22,7 @@
 quadrature = (0.375, 1.1666666, 0.9583333, 1.0)
 
 AT_ONCE = 4
-COLUMNS = 3
+COLUMNS = 4
 LATE = 2
 AHEAD = 3
 

time: 85.8 us -> 85.5 us (level)
  no operation moved by 1% of the time
where the time goes in v18:
time: 85.5 us; the launch traced here: 85.3 us
  waiting for transfers between devices  34.9 us (41%)
  Pallas kernels  23.7 us (28%)
  starting transfers between devices  22.9 us (27%)
  local copies, waits for them, and re-layouts  2.65 us (3%)
  between operations  0.89 us (1%)
    ppermute x21, waiting for transfers between devices, exchange(): return lax.ppermute(value, axis, pairs)  34.9 us
    ppermute x21, starting transfers between devices, exchange(): return lax.ppermute(value, axis, pairs)  22.9 us
    pallas_call x1, Pallas kernels, propagate(): pl.pallas_call(propagate_kernel, out_shape=jax.ShapeDtypeStruct(greens.sh...  5.28 us
    pallas_call x3, Pallas kernels, contract(): pl.pallas_call(functools.partial(contract_kernel, share), out_shape=jax.S...  5.26 us
    pallas_call x1, Pallas kernels, forward(): pl.pallas_call(functools.partial(forward_kernel, steps, parts), out_shape...  4.75 us
    pallas_call x2, Pallas kernels, early_lines(): pl.pallas_call(functools.partial(early_kernel, steps, parts), out_shape=j...  3.19 us
    pallas_call x1, Pallas kernels, pick(): pl.pallas_call(functools.partial(pick_kernel, steps, parts), out_shape=[j...  2.83 us
    dynamic_slice x1, local copies, waits for them, and re-layouts, per_device(): lax.dynamic_slice_in_dim(wholes[0], partner_of(place, step, parts) * (TIL...  2.43 us
  transfers between devices with their start and end apart: 21, of which 13 were waited for; matrix products, arithmetic and copies ran while one was open for 0% of the time, Pallas kernels for 17%

profile of v18, /device:TPU:0, one launch (start us, length us, event | category | flops | bytes accessed | tf_op | source)
XLA Modules:
  0.0 85.3 jit_solution(5818872852492145955)
XLA Ops:
  0.0 2.4 %constant_dynamic-slice_fusion = (f32[576,128]{1,0:T(8,128)}, f32[576,128]{1,0:T(8,128)}, f32[576,128]{1,0:T(8,128)}, f32[576,128]{1,0:T(8,128)S(1)}, f32[576,12...) fusion(f32[4608,128]{1,0:T(8,128)} %bitcast.12, s32[]{:T(128)S(6)} %select_n.38, s32[]{:T(128)S(6)} %select_n.37, ...), kind=kLoop, calls=%fused_computation.6 | loop fusion | bytes 4128796 | tf_op jit(solution)/shard_map/dynamic_slice | solution.py:575
  2.5 3.0 %collective-permute-start = (f32[576,128]{1,0:T(8,128)S(1)}, f32[576,128]{1,0:T(8,128)S(1)}, u32[]{:S(2)}, u32[]{:S(2)}) collective-permute-start(f32[576,128]{1,0:T(8,128)S(1)} %get-tuple-element.31.refs_0_), channel_id=1, source_target_pairs={{0,16},{4,20},{8,24},{12,28},{16,0},{20,4},{24,8},{28,12},{1,17},{... | collective-permute-start | bytes 884744 | tf_op jit(solution)/shard_map/ppermute | solution.py:538
  5.5 1.5 %collective-permute-start.1 = (f32[576,128]{1,0:T(8,128)S(1)}, f32[576,128]{1,0:T(8,128)S(1)}, u32[]{:S(2)}, u32[]{:S(2)}) collective-permute-start(f32[576,128]{1,0:T(8,128)S(1)} %get-tuple-element.30), channel_id=1, source_target_pairs={{0,8},{4,12},{8,0},{12,4},{16,24},{20,28},{24,16},{28,20},{1,9},{5... | collective-permute-start | bytes 884744 | tf_op jit(solution)/shard_map/ppermute | solution.py:538
  7.0 0.3 collective-permute-start.3
  7.3 0.3 collective-permute-start.4
  7.6 2.8 %pick.1 = (f32[576,128]{1,0:T(8,128)}, f32[576,128]{1,0:T(8,128)}, f32[576,128]{1,0:T(8,128)}, f32[576,128]{1,0:T(8,128)}, f32[576,128]{1,0:T(8,128)}, /*index=5*/f32[576,128]{1,0:T(8,128)}, f32[576,128]{1,0:T(8,128)}) custom-call(s32[1]{0:T(128)} %bitcast.3.place_ref.owner_ref, f32[4608,128]{1,0:T(8,128)} %bitcast.14, f32[576,128]{1,0:T(8,128)} %copy-done.6), custom_call_target="tpu_custom_call" | custom-call | bytes 4718592 | tf_op jit(solution)/shard_map/pick/pallas_call | solution.py:483
  10.5 2.9 %collective-permute-done.refs_1_ = f32[576,128]{1,0:T(8,128)S(1)} collective-permute-done((f32[576,128]{1,0:T(8,128)S(1)}, f32[576,128]{1,0:T(8,128)S(1)}, u32[]{:S(2)}, u32[]{:S(2)}) %collective-permute-start) | collective-permute-done | bytes 294944 | tf_op jit(solution)/shard_map/ppermute | solution.py:538
  13.3 3.0 %collective-permute-start.5 = (f32[576,128]{1,0:T(8,128)}, f32[576,128]{1,0:T(8,128)}, u32[]{:S(2)}, u32[]{:S(2)}) collective-permute-start(f32[576,128]{1,0:T(8,128)} %get-tuple-element.26), channel_id=1, source_target_pairs={{0,24},{4,28},{8,16},{12,20},{16,8},{20,12},{24,0},{28,4},{1,25},{... | collective-permute-start | bytes 884744 | tf_op jit(solution)/shard_map/ppermute | solution.py:538
  16.3 1.9 %collective-permute-done.2.refs_3_ = f32[576,128]{1,0:T(8,128)S(1)} collective-permute-done((f32[576,128]{1,0:T(8,128)S(1)}, f32[576,128]{1,0:T(8,128)S(1)}, u32[]{:S(2)}, u32[]{:S(2)}) %collective-permute-start.2) | collective-permute-done | bytes 294944 | tf_op jit(solution)/shard_map/ppermute | solution.py:538
  18.2 1.2 %collective-permute-start.10 = (f32[576,128]{1,0:T(8,128)}, f32[576,128]{1,0:T(8,128)}, u32[]{:S(2)}, u32[]{:S(2)}) collective-permute-start(f32[576,128]{1,0:T(8,128)} %get-tuple-element.19), channel_id=1, source_target_pairs={{0,16},{4,20},{8,24},{12,28},{16,0},{20,4},{24,8},{28,12},{1,17},{... | collective-permute-start | bytes 884744 | tf_op jit(solution)/shard_map/ppermute | solution.py:538
  19.4 1.3 %collective-permute-done.3.refs_4_ = f32[576,128]{1,0:T(8,128)S(1)} collective-permute-done((f32[576,128]{1,0:T(8,128)S(1)}, f32[576,128]{1,0:T(8,128)S(1)}, u32[]{:S(2)}, u32[]{:S(2)}) %collective-permute-start.3) | collective-permute-done | bytes 294944 | tf_op jit(solution)/shard_map/ppermute | solution.py:538
  20.7 0.5 collective-permute-start.11
  22.0 0.1 select_reduce_fusion
  22.1 1.7 %collective-permute-start.12 = (f32[576,128]{1,0:T(8,128)}, f32[576,128]{1,0:T(8,128)S(1)}, u32[]{:S(2)}, u32[]{:S(2)}) collective-permute-start(f32[576,128]{1,0:T(8,128)} %get-tuple-element.21), channel_id=1, source_target_pairs={{0,20},{4,16},{8,28},{12,24},{16,4},{20,0},{24,12},{28,8},{1,21},{... | collective-permute-start | bytes 884744 | tf_op jit(solution)/shard_map/ppermute | solution.py:538
  23.7 4.0 %collective-permute-done.5.refs_6_ = f32[576,128]{1,0:T(8,128)} collective-permute-done((f32[576,128]{1,0:T(8,128)}, f32[576,128]{1,0:T(8,128)}, u32[]{:S(2)}, u32[]{:S(2)}) %collective-permute-start.5) | collective-permute-done | bytes 294944 | tf_op jit(solution)/shard_map/ppermute | solution.py:538
  27.7 5.8 %collective-permute-done.6.refs_7_ = f32[576,128]{1,0:T(8,128)} collective-permute-done((f32[576,128]{1,0:T(8,128)}, f32[576,128]{1,0:T(8,128)}, u32[]{:S(2)}, u32[]{:S(2)}) %collective-permute-start.6) | collective-permute-done | bytes 294944 | tf_op jit(solution)/shard_map/ppermute | solution.py:538
  33.5 0.3 collective-permute-start.9
  33.8 5.3 %collective-permute-done.10.refs_2_ = f32[576,128]{1,0:T(8,128)} collective-permute-done((f32[576,128]{1,0:T(8,128)}, f32[576,128]{1,0:T(8,128)}, u32[]{:S(2)}, u32[]{:S(2)}) %collective-permute-start.10) | collective-permute-done | bytes 294944 | tf_op jit(solution)/shard_map/ppermute | solution.py:538
  39.2 2.5 %collective-permute-start.8 = (f32[576,128]{1,0:T(8,128)}, f32[576,128]{1,0:T(8,128)S(1)}, u32[]{:S(2)}, u32[]{:S(2)}) collective-permute-start(f32[576,128]{1,0:T(8,128)} %get-tuple-element.17), channel_id=1, source_target_pairs={{0,24},{4,28},{8,16},{12,20},{16,8},{20,12},{24,0},{28,4},{1,25},{... | collective-permute-start | bytes 884744 | tf_op jit(solution)/shard_map/ppermute | solution.py:538
  41.6 0.1 dynamic_slice.31
  41.7 0.1 pad_add_fusion.1.owner_ref
  41.8 4.8 %forward.1 = (f32[576,8,128]{2,1,0:T(8,128)S(1)}, f32[4,4608,128]{2,1,0:T(8,128)S(1)}) custom-call(s32[1]{0:T(128)} %bitcast.3.place_ref.owner_ref, f32[4608,128]{1,0:T(8,128)S(1)} %bitcast.13, f32[576,128]{1,0:T(8,128)S(1)} %collective-permute-done.refs_1_, f32[576,128]{1,0:T(8,128)S(1)} %collective-permute-done.1.refs_2_, ...), custom_call_target="tpu_custom_call" | custom-call | flops 235929600 | bytes 14155776 | tf_op jit(solution)/shard_map/forward/pallas_call | solution.py:409
  46.6 0.1 squeeze.9.weight_ref
  46.7 2.7 %early.2.refs_1_ = f32[576,8,128]{2,1,0:T(8,128)S(1)} custom-call(s32[1]{0:T(128)} %bitcast.3.place_ref.owner_ref, f32[576,8,128]{2,1,0:T(8,128)S(1)} %get-tuple-element.15.lattice_ref, f32[8,128]{1,0:T(8,128)S(1)} %squeeze.9.weight_ref, f32[576,128]{1,0:T(8,128)S(1)} %collective-permute-done.9.refs_0_, f32[4608,128]{1,0:T(8,128)S(1)} %bitcast.15, ...), custom_call_target="tpu_custom_call" | custom-call | flops 88473600 | bytes 7077888 | tf_op jit(solution)/shard_map/early/pallas_call | solution.py:427
  49.4 3.5 %collective-permute-done.8.refs_0_ = f32[576,128]{1,0:T(8,128)S(1)} collective-permute-done((f32[576,128]{1,0:T(8,128)}, f32[576,128]{1,0:T(8,128)S(1)}, u32[]{:S(2)}, u32[]{:S(2)}) %collective-permute-start.8) | collective-permute-done | bytes 294944 | tf_op jit(solution)/shard_map/ppermute | solution.py:538
  52.9 0.5 early.3.refs_1_
  53.3 0.0 copy-start.2
  53.4 0.0 copy-start.5
  53.4 4.0 %collective-permute-done.7.refs_0_ = f32[576,128]{1,0:T(8,128)S(1)} collective-permute-done((f32[576,128]{1,0:T(8,128)}, f32[576,128]{1,0:T(8,128)S(1)}, u32[]{:S(2)}, u32[]{:S(2)}) %collective-permute-start.7) | collective-permute-done | bytes 294944 | tf_op jit(solution)/shard_map/ppermute | solution.py:538
  57.4 1.6 %sigma.1 = (f32[576,8,128]{2,1,0:T(8,128)S(1)}, f32[4608,128]{1,0:T(8,128)S(1)}) custom-call(s32[1]{0:T(128)} %bitcast.3.place_ref.owner_ref, f32[576,8,128]{2,1,0:T(8,128)S(1)} %get-tuple-element.15.lattice_ref, f32[8,128]{1,0:T(8,128)S(1)} %squeeze.9.weight_ref, f32[576,128]{1,0:T(8,128)S(1)} %collective-permute-done.7.refs_0_, ...), custom_call_target="tpu_custom_call", output_to_operand_aliasing={{0}: (4, {})} | custom-call | flops 117964800 | bytes 14155776 | tf_op jit(solution)/shard_map/sigma/pallas_call | solution.py:445
  59.0 2.5 %contract.4 = f32[288,128]{1,0:T(8,128)S(1)} custom-call(s32[4]{0:T(128)S(1)} %pad_add_fusion.1.owner_ref, f32[4608,128]{1,0:T(8,128)S(1)} %get-tuple-element.23.sigma_ref, f32[72,128]{1,0:T(8,128)S(1)} %copy-done.4, f32[8,128]{1,0:T(8,128)S(1)} %copy-done.5, bf16[2048,128]{1,0:T(8,128)(2,1)S(1)} %copy-done.2, f32[4,4608,128]{2,1,0:T(8,128)S(1)} %get-tuple-element.24.greens_ref), custom_call_target="tpu_custom_call" | custom-call | flops 165150720 | bytes 14155776 | tf_op jit(solution)/shard_map/contract/pallas_call | solution.py:466
  61.5 0.6 collective-permute-start.14
  62.1 0.1 pad_add_fusion.owner_ref
  62.2 2.1 %contract.3 = f32[216,128]{1,0:T(8,128)S(1)} custom-call(s32[3]{0:T(128)S(1)} %pad_add_fusion.owner_ref, f32[4608,128]{1,0:T(8,128)S(1)} %get-tuple-element.23.sigma_ref, f32[72,128]{1,0:T(8,128)S(1)} %copy-done.4, f32[8,128]{1,0:T(8,128)S(1)} %copy-done.5, bf16[2048,128]{1,0:T(8,128)(2,1)S(1)} %copy-done.2, f32[4,4608,128]{2,1,0:T(8,128)S(1)} %get-tuple-element.24.greens_ref), custom_call_target="tpu_custom_call" | custom-call | flops 123863040 | bytes 14155776 | tf_op jit(solution)/shard_map/contract/pallas_call | solution.py:466
  64.3 2.7 %collective-permute-start.15 = (f32[72,128]{1,0:T(8,128)S(1)}, f32[72,128]{1,0:T(8,128)S(1)}, u32[]{:S(2)}, u32[]{:S(2)}) collective-permute-start(f32[72,128]{1,0:T(8,128)S(1)} %get-tuple-element.34), channel_id=1, source_target_pairs={{0,24},{4,28},{8,16},{12,20},{16,8},{20,12},{24,0},{28,4},{1,25},{... | collective-permute-start | bytes 110600 | tf_op jit(solution)/shard_map/ppermute | solution.py:538
  67.0 0.5 collective-permute-start.16
  67.5 0.4 collective-permute-start.17
  67.9 1.4 %collective-permute-done.15.refs_0_ = f32[72,128]{1,0:T(8,128)S(1)} collective-permute-done((f32[72,128]{1,0:T(8,128)S(1)}, f32[72,128]{1,0:T(8,128)S(1)}, u32[]{:S(2)}, u32[]{:S(2)}) %collective-permute-start.15) | collective-permute-done | bytes 36896 | tf_op jit(solution)/shard_map/ppermute | solution.py:538
  69.2 0.6 contract.5
  69.9 1.0 %collective-permute-done.16 = f32[72,128]{1,0:T(8,128)S(1)} collective-permute-done((f32[72,128]{1,0:T(8,128)S(1)}, f32[72,128]{1,0:T(8,128)S(1)}, u32[]{:S(2)}, u32[]{:S(2)}) %collective-permute-start.16) | collective-permute-done | bytes 36896 | tf_op jit(solution)/shard_map/ppermute | solution.py:538
  70.9 0.5 collective-permute-done.17
  71.5 0.0 copy-start.3
  71.5 3.7 %collective-permute-start.18 = (f32[72,128]{1,0:T(8,128)S(1)}, f32[72,128]{1,0:T(8,128)S(1)}, u32[]{:S(2)}, u32[]{:S(2)}) collective-permute-start(f32[72,128]{1,0:T(8,128)S(1)} %slice_add_fusion.1), channel_id=1, source_target_pairs={{0,3},{1,2},{2,1},{3,0},{4,7},{5,6},{6,5},{7,4},{8,11},{9,10},{10,... | collective-permute-start | bytes 110600 | tf_op jit(solution)/shard_map/ppermute | solution.py:538
  75.1 0.8 collective-permute-start.20
  75.9 0.8 split_own.1.split_ref
  76.7 0.7 collective-permute-done.18
  77.4 2.6 %collective-permute-done.19 = f32[72,128]{1,0:T(8,128)S(1)} collective-permute-done((f32[72,128]{1,0:T(8,128)S(1)}, f32[72,128]{1,0:T(8,128)S(1)}, u32[]{:S(2)}, u32[]{:S(2)}) %collective-permute-start.19) | collective-permute-done | bytes 36896 | tf_op jit(solution)/shard_map/ppermute | solution.py:538
  80.0 5.3 %propagate.1 = f32[64,72,128]{2,1,0:T(8,128)} custom-call(f32[64,72,128]{2,1,0:T(8,128)S(1)} %copy-done, bf16[72,64,384]{2,1,0:T(8,128)(2,1)S(1)} %split_own.1.split_ref, f32[72,128]{1,0:T(8,128)S(1)} %add_add_fusion.effective_ref, bf16[256,2048]{1,0:T(8,128)(2,1)S(1)} %copy-done.3), custom_call_target="tpu_custom_call" | custom-call | flops 18874368 | bytes 11796480 | tf_op jit(solution)/shard_map/propagate/pallas_call | solution.py:512
  (35 shorter events, 0.1 us)
Async XLA Ops:
  2.4 5.2 %copy-start.6 = (f32[576,128]{1,0:T(8,128)}, f32[576,128]{1,0:T(8,128)S(1)}, u32[]{:S(2)}) copy-start(f32[576,128]{1,0:T(8,128)S(1)} %get-tuple-element.31.refs_0_) | copy-start | bytes 884740
  2.4 19.5 %copy-start.8 = (s32[64]{0:T(128)S(1)}, s32[64]{0:T(128)}, u32[]{:S(2)}) copy-start(s32[64]{0:T(128)} %param.18) | copy-start | bytes 772
  2.4 19.5 %copy-start.9 = (f32[4]{0:T(128)S(1)}, f32[4]{0:T(128)}, u32[]{:S(2)}) copy-start(f32[4]{0:T(128)} %constant.44.clone) | copy-start | bytes 52
  2.4 39.3 %copy-start = (f32[64,72,128]{2,1,0:T(8,128)S(1)}, f32[64,72,128]{2,1,0:T(8,128)}, u32[]{:S(2)}) copy-start(f32[64,72,128]{2,1,0:T(8,128)} %green_ref.3) | copy-start | bytes 7077892
  2.5 10.9 %collective-permute-start = (f32[576,128]{1,0:T(8,128)S(1)}, f32[576,128]{1,0:T(8,128)S(1)}, u32[]{:S(2)}, u32[]{:S(2)}) collective-permute-start(f32[576,128]{1,0:T(8,128)S(1)} %get-tuple-element.31.refs_0_), channel_id=1, source_target_pairs={{0,16},{4,20},{8,24},{12,28},{16,0},{20,4},{24,8},{28,12},{1,17},{... | collective-permute-start | bytes 884744 | tf_op jit(solution)/shard_map/ppermute | solution.py:538
  5.5 10.8 %collective-permute-start.1 = (f32[576,128]{1,0:T(8,128)S(1)}, f32[576,128]{1,0:T(8,128)S(1)}, u32[]{:S(2)}, u32[]{:S(2)}) collective-permute-start(f32[576,128]{1,0:T(8,128)S(1)} %get-tuple-element.30), channel_id=1, source_target_pairs={{0,8},{4,12},{8,0},{12,4},{16,24},{20,28},{24,16},{28,20},{1,9},{5... | collective-permute-start | bytes 884744 | tf_op jit(solution)/shard_map/ppermute | solution.py:538
  7.0 11.2 %collective-permute-start.2 = (f32[576,128]{1,0:T(8,128)S(1)}, f32[576,128]{1,0:T(8,128)S(1)}, u32[]{:S(2)}, u32[]{:S(2)}) collective-permute-start(f32[576,128]{1,0:T(8,128)S(1)} %get-tuple-element.29), channel_id=1, source_target_pairs={{0,20},{4,16},{8,28},{12,24},{16,4},{20,0},{24,12},{28,8},{1,21},{... | collective-permute-start | bytes 884744 | tf_op jit(solution)/shard_map/ppermute | solution.py:538
  7.0 13.8 %collective-permute-start.3 = (f32[576,128]{1,0:T(8,128)S(1)}, f32[576,128]{1,0:T(8,128)S(1)}, u32[]{:S(2)}, u32[]{:S(2)}) collective-permute-start(f32[576,128]{1,0:T(8,128)S(1)} %get-tuple-element.28), channel_id=1, source_target_pairs={{0,12},{4,8},{8,4},{12,0},{16,28},{20,24},{24,20},{28,16},{1,13},{... | collective-permute-start | bytes 884744 | tf_op jit(solution)/shard_map/ppermute | solution.py:538
  7.3 14.7 %collective-permute-start.4 = (f32[576,128]{1,0:T(8,128)}, f32[576,128]{1,0:T(8,128)}, u32[]{:S(2)}, u32[]{:S(2)}) collective-permute-start(f32[576,128]{1,0:T(8,128)} %get-tuple-element.27), channel_id=1, source_target_pairs={{0,4},{4,0},{8,12},{12,8},{16,20},{20,16},{24,28},{28,24},{1,5},{5... | collective-permute-start | bytes 884744 | tf_op jit(solution)/shard_map/ppermute | solution.py:538
  13.3 14.4 %collective-permute-start.5 = (f32[576,128]{1,0:T(8,128)}, f32[576,128]{1,0:T(8,128)}, u32[]{:S(2)}, u32[]{:S(2)}) collective-permute-start(f32[576,128]{1,0:T(8,128)} %get-tuple-element.26), channel_id=1, source_target_pairs={{0,24},{4,28},{8,16},{12,20},{16,8},{20,12},{24,0},{28,4},{1,25},{... | collective-permute-start | bytes 884744 | tf_op jit(solution)/shard_map/ppermute | solution.py:538
  16.3 17.2 %collective-permute-start.6 = (f32[576,128]{1,0:T(8,128)}, f32[576,128]{1,0:T(8,128)}, u32[]{:S(2)}, u32[]{:S(2)}) collective-permute-start(f32[576,128]{1,0:T(8,128)} %get-tuple-element.25), channel_id=1, source_target_pairs={{0,28},{4,24},{8,20},{12,16},{16,12},{20,8},{24,4},{28,0},{1,29},{... | collective-permute-start | bytes 884744 | tf_op jit(solution)/shard_map/ppermute | solution.py:538
  18.2 20.9 %collective-permute-start.10 = (f32[576,128]{1,0:T(8,128)}, f32[576,128]{1,0:T(8,128)}, u32[]{:S(2)}, u32[]{:S(2)}) collective-permute-start(f32[576,128]{1,0:T(8,128)} %get-tuple-element.19), channel_id=1, source_target_pairs={{0,16},{4,20},{8,24},{12,28},{16,0},{20,4},{24,8},{28,12},{1,17},{... | collective-permute-start | bytes 884744 | tf_op jit(solution)/shard_map/ppermute | solution.py:538
  20.7 20.9 %collective-permute-start.11 = (f32[576,128]{1,0:T(8,128)}, f32[576,128]{1,0:T(8,128)}, u32[]{:S(2)}, u32[]{:S(2)}) collective-permute-start(f32[576,128]{1,0:T(8,128)} %get-tuple-element.20), channel_id=1, source_target_pairs={{0,8},{4,12},{8,0},{12,4},{16,24},{20,28},{24,16},{28,20},{1,9},{5... | collective-permute-start | bytes 884744 | tf_op jit(solution)/shard_map/ppermute | solution.py:538
  22.0 24.7 %copy-start.1 = (f32[64,72,128]{2,1,0:T(8,128)S(1)}, f32[64,72,128]{2,1,0:T(8,128)}, u32[]{:S(2)}) copy-start(f32[64,72,128]{2,1,0:T(8,128)} %param.15) | copy-start | bytes 7077892
  22.1 24.5 %collective-permute-start.12 = (f32[576,128]{1,0:T(8,128)}, f32[576,128]{1,0:T(8,128)S(1)}, u32[]{:S(2)}, u32[]{:S(2)}) collective-permute-start(f32[576,128]{1,0:T(8,128)} %get-tuple-element.21), channel_id=1, source_target_pairs={{0,20},{4,16},{8,28},{12,24},{16,4},{20,0},{24,12},{28,8},{1,21},{... | collective-permute-start | bytes 884744 | tf_op jit(solution)/shard_map/ppermute | solution.py:538
  27.7 18.8 %collective-permute-start.13 = (f32[576,128]{1,0:T(8,128)}, f32[576,128]{1,0:T(8,128)S(1)}, u32[]{:S(2)}, u32[]{:S(2)}) collective-permute-start(f32[576,128]{1,0:T(8,128)} %get-tuple-element.22), channel_id=1, source_target_pairs={{0,12},{4,8},{8,4},{12,0},{16,28},{20,24},{24,20},{28,16},{1,13},{... | collective-permute-start | bytes 884744 | tf_op jit(solution)/shard_map/ppermute | solution.py:538
  33.5 13.0 %collective-permute-start.9 = (f32[576,128]{1,0:T(8,128)}, f32[576,128]{1,0:T(8,128)S(1)}, u32[]{:S(2)}, u32[]{:S(2)}) collective-permute-start(f32[576,128]{1,0:T(8,128)} %get-tuple-element.18), channel_id=1, source_target_pairs={{0,4},{4,0},{8,12},{12,8},{16,20},{20,16},{24,28},{28,24},{1,5},{5... | collective-permute-start | bytes 884744 | tf_op jit(solution)/shard_map/ppermute | solution.py:538
  39.2 13.7 %collective-permute-start.8 = (f32[576,128]{1,0:T(8,128)}, f32[576,128]{1,0:T(8,128)S(1)}, u32[]{:S(2)}, u32[]{:S(2)}) collective-permute-start(f32[576,128]{1,0:T(8,128)} %get-tuple-element.17), channel_id=1, source_target_pairs={{0,24},{4,28},{8,16},{12,20},{16,8},{20,12},{24,0},{28,4},{1,25},{... | collective-permute-start | bytes 884744 | tf_op jit(solution)/shard_map/ppermute | solution.py:538
  41.6 15.7 %collective-permute-start.7 = (f32[576,128]{1,0:T(8,128)}, f32[576,128]{1,0:T(8,128)S(1)}, u32[]{:S(2)}, u32[]{:S(2)}) collective-permute-start(f32[576,128]{1,0:T(8,128)} %get-tuple-element.16), channel_id=1, source_target_pairs={{0,28},{4,24},{8,20},{12,16},{16,12},{20,8},{24,4},{28,0},{1,29},{... | collective-permute-start | bytes 884744 | tf_op jit(solution)/shard_map/ppermute | solution.py:538
  53.3 5.6 %copy-start.2 = (bf16[2048,128]{1,0:T(8,128)(2,1)S(1)}, bf16[2048,128]{1,0:T(8,128)(2,1)}, u32[]{:S(2)}) copy-start(bf16[2048,128]{1,0:T(8,128)(2,1)} %constant.46.clone.gather_ref) | copy-start | bytes 1572868
  53.3 5.6 %copy-start.4 = (f32[72,128]{1,0:T(8,128)S(1)}, f32[72,128]{1,0:T(8,128)}, u32[]{:S(2)}) copy-start(f32[72,128]{1,0:T(8,128)} %equal_ref.5) | copy-start | bytes 110596
  53.4 5.6 %copy-start.5 = (f32[8,128]{1,0:T(8,128)S(1)}, f32[8,128]{1,0:T(8,128)}, u32[]{:S(2)}) copy-start(f32[8,128]{1,0:T(8,128)} %constant.45.clone.sign_ref) | copy-start | bytes 12292
  61.5 2.7 %collective-permute-start.14 = (f32[288,128]{1,0:T(8,128)S(1)}, f32[288,128]{1,0:T(8,128)S(1)}, u32[]{:S(2)}, u32[]{:S(2)}) collective-permute-start(f32[288,128]{1,0:T(8,128)S(1)} %contract.4), channel_id=1, source_target_pairs={{0,4},{4,0},{8,12},{12,8},{16,20},{20,16},{24,28},{28,24},{1,5},{5... | collective-permute-start | bytes 442376 | tf_op jit(solution)/shard_map/ppermute | solution.py:538
  64.3 4.9 %collective-permute-start.15 = (f32[72,128]{1,0:T(8,128)S(1)}, f32[72,128]{1,0:T(8,128)S(1)}, u32[]{:S(2)}, u32[]{:S(2)}) collective-permute-start(f32[72,128]{1,0:T(8,128)S(1)} %get-tuple-element.34), channel_id=1, source_target_pairs={{0,24},{4,28},{8,16},{12,20},{16,8},{20,12},{24,0},{28,4},{1,25},{... | collective-permute-start | bytes 110600 | tf_op jit(solution)/shard_map/ppermute | solution.py:538
  67.0 4.0 %collective-permute-start.16 = (f32[72,128]{1,0:T(8,128)S(1)}, f32[72,128]{1,0:T(8,128)S(1)}, u32[]{:S(2)}, u32[]{:S(2)}) collective-permute-start(f32[72,128]{1,0:T(8,128)S(1)} %get-tuple-element.32), channel_id=1, source_target_pairs={{0,16},{4,20},{8,24},{12,28},{16,0},{20,4},{24,8},{28,12},{1,17},{... | collective-permute-start | bytes 110600 | tf_op jit(solution)/shard_map/ppermute | solution.py:538
  67.5 4.0 %collective-permute-start.17 = (f32[72,128]{1,0:T(8,128)S(1)}, f32[72,128]{1,0:T(8,128)S(1)}, u32[]{:S(2)}, u32[]{:S(2)}) collective-permute-start(f32[72,128]{1,0:T(8,128)S(1)} %get-tuple-element.33), channel_id=1, source_target_pairs={{0,8},{4,12},{8,0},{12,4},{16,24},{20,28},{24,16},{28,20},{1,9},{5... | collective-permute-start | bytes 110600 | tf_op jit(solution)/shard_map/ppermute | solution.py:538
  71.5 8.6 %copy-start.7 = (f32[72,128]{1,0:T(8,128)S(1)}, f32[72,128]{1,0:T(8,128)}, u32[]{:S(2)}) copy-start(f32[72,128]{1,0:T(8,128)} %param.16) | copy-start | bytes 110596
  71.5 8.6 %copy-start.3 = (bf16[256,2048]{1,0:T(8,128)(2,1)S(1)}, bf16[256,2048]{1,0:T(8,128)(2,1)}, u32[]{:S(2)}) copy-start(bf16[256,2048]{1,0:T(8,128)(2,1)} %constant.47.clone.spread_ref) | copy-start | bytes 3145732
  71.5 5.9 %collective-permute-start.18 = (f32[72,128]{1,0:T(8,128)S(1)}, f32[72,128]{1,0:T(8,128)S(1)}, u32[]{:S(2)}, u32[]{:S(2)}) collective-permute-start(f32[72,128]{1,0:T(8,128)S(1)} %slice_add_fusion.1), channel_id=1, source_target_pairs={{0,3},{1,2},{2,1},{3,0},{4,7},{5,6},{6,5},{7,4},{8,11},{9,10},{10,... | collective-permute-start | bytes 110600 | tf_op jit(solution)/shard_map/ppermute | solution.py:538
  75.1 4.9 %collective-permute-start.19 = (f32[72,128]{1,0:T(8,128)S(1)}, f32[72,128]{1,0:T(8,128)S(1)}, u32[]{:S(2)}, u32[]{:S(2)}) collective-permute-start(f32[72,128]{1,0:T(8,128)S(1)} %slice_add_fusion.1), channel_id=1, source_target_pairs={{0,2},{1,3},{2,0},{3,1},{4,6},{5,7},{6,4},{7,5},{8,10},{9,11},{10,... | collective-permute-start | bytes 110600 | tf_op jit(solution)/shard_map/ppermute | solution.py:538
  75.1 4.9 %collective-permute-start.20 = (f32[72,128]{1,0:T(8,128)S(1)}, f32[72,128]{1,0:T(8,128)S(1)}, u32[]{:S(2)}, u32[]{:S(2)}) collective-permute-start(f32[72,128]{1,0:T(8,128)S(1)} %slice_add_fusion.1), channel_id=1, source_target_pairs={{0,1},{1,0},{2,3},{3,2},{4,5},{5,4},{6,7},{7,6},{8,9},{9,8},{10,11... | collective-permute-start | bytes 110600 | tf_op jit(solution)/shard_map/ppermute | solution.py:538

commit v19 on v18

--- a/solution.py
+++ b/solution.py
@@ -21,8 +21,8 @@
 hubbard = 1.0
 quadrature = (0.375, 1.1666666, 0.9583333, 1.0)
 
-AT_ONCE = 4
-COLUMNS = 4
+AT_ONCE = 8
+COLUMNS = 6
 LATE = 2
 AHEAD = 3
 

time: 85.5 us -> 85.3 us (level)
  no operation moved by 1% of the time
where the time goes in v19:
time: 85.3 us; the launch traced here: 85.1 us
  waiting for transfers between devices  35.1 us (41%)
  Pallas kernels  23.4 us (27%)
  starting transfers between devices  22.9 us (27%)
  local copies, waits for them, and re-layouts  2.65 us (3%)
  between operations  0.86 us (1%)
    ppermute x21, waiting for transfers between devices, exchange(): return lax.ppermute(value, axis, pairs)  35.1 us
    ppermute x21, starting transfers between devices, exchange(): return lax.ppermute(value, axis, pairs)  22.9 us
    pallas_call x1, Pallas kernels, propagate(): pl.pallas_call(propagate_kernel, out_shape=jax.ShapeDtypeStruct(greens.sh...  5.29 us
    pallas_call x3, Pallas kernels, contract(): pl.pallas_call(functools.partial(contract_kernel, share), out_shape=jax.S...  5.27 us
    pallas_call x1, Pallas kernels, forward(): pl.pallas_call(functools.partial(forward_kernel, steps, parts), out_shape...  4.58 us
    pallas_call x2, Pallas kernels, early_lines(): pl.pallas_call(functools.partial(early_kernel, steps, parts), out_shape=j...  3.19 us
    pallas_call x1, Pallas kernels, pick(): pl.pallas_call(functools.partial(pick_kernel, steps, parts), out_shape=[j...  2.83 us
    dynamic_slice x1, local copies, waits for them, and re-layouts, per_device(): lax.dynamic_slice_in_dim(wholes[0], partner_of(place, step, parts) * (TIL...  2.43 us
  transfers between devices with their start and end apart: 21, of which 13 were waited for; matrix products, arithmetic and copies ran while one was open for 0% of the time, Pallas kernels for 17%

profile of v19, /device:TPU:0, one launch (start us, length us, event | category | flops | bytes accessed | tf_op | source)
XLA Modules:
  0.0 85.1 jit_solution(856089203178425401)
XLA Ops:
  0.0 2.4 %constant_dynamic-slice_fusion = (f32[576,128]{1,0:T(8,128)}, f32[576,128]{1,0:T(8,128)}, f32[576,128]{1,0:T(8,128)}, f32[576,128]{1,0:T(8,128)S(1)}, f32[576,12...) fusion(f32[4608,128]{1,0:T(8,128)} %bitcast.12, s32[]{:T(128)S(6)} %select_n.38, s32[]{:T(128)S(6)} %select_n.37, ...), kind=kLoop, calls=%fused_computation.6 | loop fusion | bytes 4128796 | tf_op jit(solution)/shard_map/dynamic_slice | solution.py:575
  2.5 3.0 %collective-permute-start = (f32[576,128]{1,0:T(8,128)S(1)}, f32[576,128]{1,0:T(8,128)S(1)}, u32[]{:S(2)}, u32[]{:S(2)}) collective-permute-start(f32[576,128]{1,0:T(8,128)S(1)} %get-tuple-element.31.refs_0_), channel_id=1, source_target_pairs={{0,16},{4,20},{8,24},{12,28},{16,0},{20,4},{24,8},{28,12},{1,17},{... | collective-permute-start | bytes 884744 | tf_op jit(solution)/shard_map/ppermute | solution.py:538
  5.5 1.5 %collective-permute-start.1 = (f32[576,128]{1,0:T(8,128)S(1)}, f32[576,128]{1,0:T(8,128)S(1)}, u32[]{:S(2)}, u32[]{:S(2)}) collective-permute-start(f32[576,128]{1,0:T(8,128)S(1)} %get-tuple-element.30), channel_id=1, source_target_pairs={{0,8},{4,12},{8,0},{12,4},{16,24},{20,28},{24,16},{28,20},{1,9},{5... | collective-permute-start | bytes 884744 | tf_op jit(solution)/shard_map/ppermute | solution.py:538
  7.0 0.3 collective-permute-start.3
  7.3 0.3 collective-permute-start.4
  7.6 2.8 %pick.1 = (f32[576,128]{1,0:T(8,128)}, f32[576,128]{1,0:T(8,128)}, f32[576,128]{1,0:T(8,128)}, f32[576,128]{1,0:T(8,128)}, f32[576,128]{1,0:T(8,128)}, /*index=5*/f32[576,128]{1,0:T(8,128)}, f32[576,128]{1,0:T(8,128)}) custom-call(s32[1]{0:T(128)} %bitcast.3.place_ref.owner_ref, f32[4608,128]{1,0:T(8,128)} %bitcast.14, f32[576,128]{1,0:T(8,128)} %copy-done.6), custom_call_target="tpu_custom_call" | custom-call | bytes 4718592 | tf_op jit(solution)/shard_map/pick/pallas_call | solution.py:483
  10.5 2.9 %collective-permute-done.refs_1_ = f32[576,128]{1,0:T(8,128)S(1)} collective-permute-done((f32[576,128]{1,0:T(8,128)S(1)}, f32[576,128]{1,0:T(8,128)S(1)}, u32[]{:S(2)}, u32[]{:S(2)}) %collective-permute-start) | collective-permute-done | bytes 294944 | tf_op jit(solution)/shard_map/ppermute | solution.py:538
  13.3 3.0 %collective-permute-start.5 = (f32[576,128]{1,0:T(8,128)}, f32[576,128]{1,0:T(8,128)}, u32[]{:S(2)}, u32[]{:S(2)}) collective-permute-start(f32[576,128]{1,0:T(8,128)} %get-tuple-element.26), channel_id=1, source_target_pairs={{0,24},{4,28},{8,16},{12,20},{16,8},{20,12},{24,0},{28,4},{1,25},{... | collective-permute-start | bytes 884744 | tf_op jit(solution)/shard_map/ppermute | solution.py:538
  16.3 1.9 %collective-permute-done.2.refs_3_ = f32[576,128]{1,0:T(8,128)S(1)} collective-permute-done((f32[576,128]{1,0:T(8,128)S(1)}, f32[576,128]{1,0:T(8,128)S(1)}, u32[]{:S(2)}, u32[]{:S(2)}) %collective-permute-start.2) | collective-permute-done | bytes 294944 | tf_op jit(solution)/shard_map/ppermute | solution.py:538
  18.2 1.2 %collective-permute-start.10 = (f32[576,128]{1,0:T(8,128)}, f32[576,128]{1,0:T(8,128)}, u32[]{:S(2)}, u32[]{:S(2)}) collective-permute-start(f32[576,128]{1,0:T(8,128)} %get-tuple-element.19), channel_id=1, source_target_pairs={{0,16},{4,20},{8,24},{12,28},{16,0},{20,4},{24,8},{28,12},{1,17},{... | collective-permute-start | bytes 884744 | tf_op jit(solution)/shard_map/ppermute | solution.py:538
  19.4 1.3 %collective-permute-done.3.refs_4_ = f32[576,128]{1,0:T(8,128)S(1)} collective-permute-done((f32[576,128]{1,0:T(8,128)S(1)}, f32[576,128]{1,0:T(8,128)S(1)}, u32[]{:S(2)}, u32[]{:S(2)}) %collective-permute-start.3) | collective-permute-done | bytes 294944 | tf_op jit(solution)/shard_map/ppermute | solution.py:538
  20.7 0.5 collective-permute-start.11
  22.0 0.1 select_reduce_fusion
  22.1 1.7 %collective-permute-start.12 = (f32[576,128]{1,0:T(8,128)}, f32[576,128]{1,0:T(8,128)S(1)}, u32[]{:S(2)}, u32[]{:S(2)}) collective-permute-start(f32[576,128]{1,0:T(8,128)} %get-tuple-element.21), channel_id=1, source_target_pairs={{0,20},{4,16},{8,28},{12,24},{16,4},{20,0},{24,12},{28,8},{1,21},{... | collective-permute-start | bytes 884744 | tf_op jit(solution)/shard_map/ppermute | solution.py:538
  23.7 4.0 %collective-permute-done.5.refs_6_ = f32[576,128]{1,0:T(8,128)} collective-permute-done((f32[576,128]{1,0:T(8,128)}, f32[576,128]{1,0:T(8,128)}, u32[]{:S(2)}, u32[]{:S(2)}) %collective-permute-start.5) | collective-permute-done | bytes 294944 | tf_op jit(solution)/shard_map/ppermute | solution.py:538
  27.7 5.8 %collective-permute-done.6.refs_7_ = f32[576,128]{1,0:T(8,128)} collective-permute-done((f32[576,128]{1,0:T(8,128)}, f32[576,128]{1,0:T(8,128)}, u32[]{:S(2)}, u32[]{:S(2)}) %collective-permute-start.6) | collective-permute-done | bytes 294944 | tf_op jit(solution)/shard_map/ppermute | solution.py:538
  33.5 0.3 collective-permute-start.9
  33.8 5.3 %collective-permute-done.10.refs_2_ = f32[576,128]{1,0:T(8,128)} collective-permute-done((f32[576,128]{1,0:T(8,128)}, f32[576,128]{1,0:T(8,128)}, u32[]{:S(2)}, u32[]{:S(2)}) %collective-permute-start.10) | collective-permute-done | bytes 294944 | tf_op jit(solution)/shard_map/ppermute | solution.py:538
  39.2 2.5 %collective-permute-start.8 = (f32[576,128]{1,0:T(8,128)}, f32[576,128]{1,0:T(8,128)S(1)}, u32[]{:S(2)}, u32[]{:S(2)}) collective-permute-start(f32[576,128]{1,0:T(8,128)} %get-tuple-element.17), channel_id=1, source_target_pairs={{0,24},{4,28},{8,16},{12,20},{16,8},{20,12},{24,0},{28,4},{1,25},{... | collective-permute-start | bytes 884744 | tf_op jit(solution)/shard_map/ppermute | solution.py:538
  41.6 0.1 dynamic_slice.31
  41.7 0.1 pad_add_fusion.1.owner_ref
  41.8 4.6 %forward.1 = (f32[576,8,128]{2,1,0:T(8,128)S(1)}, f32[4,4608,128]{2,1,0:T(8,128)S(1)}) custom-call(s32[1]{0:T(128)} %bitcast.3.place_ref.owner_ref, f32[4608,128]{1,0:T(8,128)S(1)} %bitcast.13, f32[576,128]{1,0:T(8,128)S(1)} %collective-permute-done.refs_1_, f32[576,128]{1,0:T(8,128)S(1)} %collective-permute-done.1.refs_2_, ...), custom_call_target="tpu_custom_call" | custom-call | flops 235929600 | bytes 14155776 | tf_op jit(solution)/shard_map/forward/pallas_call | solution.py:409
  46.4 0.0 collective-permute-done.12.refs_4_
  46.4 0.1 squeeze.9.weight_ref
  46.5 2.7 %early.2.refs_1_ = f32[576,8,128]{2,1,0:T(8,128)S(1)} custom-call(s32[1]{0:T(128)} %bitcast.3.place_ref.owner_ref, f32[576,8,128]{2,1,0:T(8,128)S(1)} %get-tuple-element.15.lattice_ref, f32[8,128]{1,0:T(8,128)S(1)} %squeeze.9.weight_ref, f32[576,128]{1,0:T(8,128)S(1)} %collective-permute-done.9.refs_0_, f32[4608,128]{1,0:T(8,128)S(1)} %bitcast.15, ...), custom_call_target="tpu_custom_call" | custom-call | flops 88473600 | bytes 7077888 | tf_op jit(solution)/shard_map/early/pallas_call | solution.py:427
  49.2 3.6 %collective-permute-done.8.refs_0_ = f32[576,128]{1,0:T(8,128)S(1)} collective-permute-done((f32[576,128]{1,0:T(8,128)}, f32[576,128]{1,0:T(8,128)S(1)}, u32[]{:S(2)}, u32[]{:S(2)}) %collective-permute-start.8) | collective-permute-done | bytes 294944 | tf_op jit(solution)/shard_map/ppermute | solution.py:538
  52.9 0.5 early.3.refs_1_
  53.3 0.0 copy-start.2
  53.4 4.0 %collective-permute-done.7.refs_0_ = f32[576,128]{1,0:T(8,128)S(1)} collective-permute-done((f32[576,128]{1,0:T(8,128)}, f32[576,128]{1,0:T(8,128)S(1)}, u32[]{:S(2)}, u32[]{:S(2)}) %collective-permute-start.7) | collective-permute-done | bytes 294944 | tf_op jit(solution)/shard_map/ppermute | solution.py:538
  57.4 1.4 %sigma.1 = (f32[576,8,128]{2,1,0:T(8,128)S(1)}, f32[4608,128]{1,0:T(8,128)S(1)}) custom-call(s32[1]{0:T(128)} %bitcast.3.place_ref.owner_ref, f32[576,8,128]{2,1,0:T(8,128)S(1)} %get-tuple-element.15.lattice_ref, f32[8,128]{1,0:T(8,128)S(1)} %squeeze.9.weight_ref, f32[576,128]{1,0:T(8,128)S(1)} %collective-permute-done.7.refs_0_, ...), custom_call_target="tpu_custom_call", output_to_operand_aliasing={{0}: (4, {})} | custom-call | flops 117964800 | bytes 14155776 | tf_op jit(solution)/shard_map/sigma/pallas_call | solution.py:445
  58.8 2.5 %contract.4 = f32[288,128]{1,0:T(8,128)S(1)} custom-call(s32[4]{0:T(128)S(1)} %pad_add_fusion.1.owner_ref, f32[4608,128]{1,0:T(8,128)S(1)} %get-tuple-element.23.sigma_ref, f32[72,128]{1,0:T(8,128)S(1)} %copy-done.4, f32[8,128]{1,0:T(8,128)S(1)} %copy-done.5, bf16[2048,128]{1,0:T(8,128)(2,1)S(1)} %copy-done.2, f32[4,4608,128]{2,1,0:T(8,128)S(1)} %get-tuple-element.24.greens_ref), custom_call_target="tpu_custom_call" | custom-call | flops 165150720 | bytes 14155776 | tf_op jit(solution)/shard_map/contract/pallas_call | solution.py:466
  61.3 0.6 collective-permute-start.14
  61.9 0.1 pad_add_fusion.owner_ref
  62.0 2.1 %contract.3 = f32[216,128]{1,0:T(8,128)S(1)} custom-call(s32[3]{0:T(128)S(1)} %pad_add_fusion.owner_ref, f32[4608,128]{1,0:T(8,128)S(1)} %get-tuple-element.23.sigma_ref, f32[72,128]{1,0:T(8,128)S(1)} %copy-done.4, f32[8,128]{1,0:T(8,128)S(1)} %copy-done.5, bf16[2048,128]{1,0:T(8,128)(2,1)S(1)} %copy-done.2, f32[4,4608,128]{2,1,0:T(8,128)S(1)} %get-tuple-element.24.greens_ref), custom_call_target="tpu_custom_call" | custom-call | flops 123863040 | bytes 14155776 | tf_op jit(solution)/shard_map/contract/pallas_call | solution.py:466
  64.1 2.7 %collective-permute-start.15 = (f32[72,128]{1,0:T(8,128)S(1)}, f32[72,128]{1,0:T(8,128)S(1)}, u32[]{:S(2)}, u32[]{:S(2)}) collective-permute-start(f32[72,128]{1,0:T(8,128)S(1)} %get-tuple-element.34), channel_id=1, source_target_pairs={{0,24},{4,28},{8,16},{12,20},{16,8},{20,12},{24,0},{28,4},{1,25},{... | collective-permute-start | bytes 110600 | tf_op jit(solution)/shard_map/ppermute | solution.py:538
  66.8 0.5 collective-permute-start.16
  67.3 0.4 collective-permute-start.17
  67.7 1.4 %collective-permute-done.15.refs_0_ = f32[72,128]{1,0:T(8,128)S(1)} collective-permute-done((f32[72,128]{1,0:T(8,128)S(1)}, f32[72,128]{1,0:T(8,128)S(1)}, u32[]{:S(2)}, u32[]{:S(2)}) %collective-permute-start.15) | collective-permute-done | bytes 36896 | tf_op jit(solution)/shard_map/ppermute | solution.py:538
  69.1 0.6 contract.5
  69.7 1.0 %collective-permute-done.16 = f32[72,128]{1,0:T(8,128)S(1)} collective-permute-done((f32[72,128]{1,0:T(8,128)S(1)}, f32[72,128]{1,0:T(8,128)S(1)}, u32[]{:S(2)}, u32[]{:S(2)}) %collective-permute-start.16) | collective-permute-done | bytes 36896 | tf_op jit(solution)/shard_map/ppermute | solution.py:538
  70.8 0.5 collective-permute-done.17
  71.3 0.0 copy-start.3
  71.3 3.7 %collective-permute-start.18 = (f32[72,128]{1,0:T(8,128)S(1)}, f32[72,128]{1,0:T(8,128)S(1)}, u32[]{:S(2)}, u32[]{:S(2)}) collective-permute-start(f32[72,128]{1,0:T(8,128)S(1)} %slice_add_fusion.1), channel_id=1, source_target_pairs={{0,3},{1,2},{2,1},{3,0},{4,7},{5,6},{6,5},{7,4},{8,11},{9,10},{10,... | collective-permute-start | bytes 110600 | tf_op jit(solution)/shard_map/ppermute | solution.py:538
  75.0 0.8 collective-permute-start.20
  75.8 0.8 split_own.1.split_ref
  76.5 0.7 collective-permute-done.18
  77.2 2.6 %collective-permute-done.19 = f32[72,128]{1,0:T(8,128)S(1)} collective-permute-done((f32[72,128]{1,0:T(8,128)S(1)}, f32[72,128]{1,0:T(8,128)S(1)}, u32[]{:S(2)}, u32[]{:S(2)}) %collective-permute-start.19) | collective-permute-done | bytes 36896 | tf_op jit(solution)/shard_map/ppermute | solution.py:538
  79.9 5.3 %propagate.1 = f32[64,72,128]{2,1,0:T(8,128)} custom-call(f32[64,72,128]{2,1,0:T(8,128)S(1)} %copy-done, bf16[72,64,384]{2,1,0:T(8,128)(2,1)S(1)} %split_own.1.split_ref, f32[72,128]{1,0:T(8,128)S(1)} %add_add_fusion.effective_ref, bf16[256,2048]{1,0:T(8,128)(2,1)S(1)} %copy-done.3), custom_call_target="tpu_custom_call" | custom-call | flops 18874368 | bytes 11796480 | tf_op jit(solution)/shard_map/propagate/pallas_call | solution.py:512
  (35 shorter events, 0.1 us)
Async XLA Ops:
  2.4 5.2 %copy-start.6 = (f32[576,128]{1,0:T(8,128)}, f32[576,128]{1,0:T(8,128)S(1)}, u32[]{:S(2)}) copy-start(f32[576,128]{1,0:T(8,128)S(1)} %get-tuple-element.31.refs_0_) | copy-start | bytes 884740
  2.4 19.5 %copy-start.8 = (s32[64]{0:T(128)S(1)}, s32[64]{0:T(128)}, u32[]{:S(2)}) copy-start(s32[64]{0:T(128)} %param.18) | copy-start | bytes 772
  2.4 19.5 %copy-start.9 = (f32[4]{0:T(128)S(1)}, f32[4]{0:T(128)}, u32[]{:S(2)}) copy-start(f32[4]{0:T(128)} %constant.44.clone) | copy-start | bytes 52
  2.4 39.3 %copy-start = (f32[64,72,128]{2,1,0:T(8,128)S(1)}, f32[64,72,128]{2,1,0:T(8,128)}, u32[]{:S(2)}) copy-start(f32[64,72,128]{2,1,0:T(8,128)} %green_ref.3) | copy-start | bytes 7077892
  2.5 10.9 %collective-permute-start = (f32[576,128]{1,0:T(8,128)S(1)}, f32[576,128]{1,0:T(8,128)S(1)}, u32[]{:S(2)}, u32[]{:S(2)}) collective-permute-start(f32[576,128]{1,0:T(8,128)S(1)} %get-tuple-element.31.refs_0_), channel_id=1, source_target_pairs={{0,16},{4,20},{8,24},{12,28},{16,0},{20,4},{24,8},{28,12},{1,17},{... | collective-permute-start | bytes 884744 | tf_op jit(solution)/shard_map/ppermute | solution.py:538
  5.5 10.8 %collective-permute-start.1 = (f32[576,128]{1,0:T(8,128)S(1)}, f32[576,128]{1,0:T(8,128)S(1)}, u32[]{:S(2)}, u32[]{:S(2)}) collective-permute-start(f32[576,128]{1,0:T(8,128)S(1)} %get-tuple-element.30), channel_id=1, source_target_pairs={{0,8},{4,12},{8,0},{12,4},{16,24},{20,28},{24,16},{28,20},{1,9},{5... | collective-permute-start | bytes 884744 | tf_op jit(solution)/shard_map/ppermute | solution.py:538
  7.0 11.2 %collective-permute-start.2 = (f32[576,128]{1,0:T(8,128)S(1)}, f32[576,128]{1,0:T(8,128)S(1)}, u32[]{:S(2)}, u32[]{:S(2)}) collective-permute-start(f32[576,128]{1,0:T(8,128)S(1)} %get-tuple-element.29), channel_id=1, source_target_pairs={{0,20},{4,16},{8,28},{12,24},{16,4},{20,0},{24,12},{28,8},{1,21},{... | collective-permute-start | bytes 884744 | tf_op jit(solution)/shard_map/ppermute | solution.py:538
  7.0 13.8 %collective-permute-start.3 = (f32[576,128]{1,0:T(8,128)S(1)}, f32[576,128]{1,0:T(8,128)S(1)}, u32[]{:S(2)}, u32[]{:S(2)}) collective-permute-start(f32[576,128]{1,0:T(8,128)S(1)} %get-tuple-element.28), channel_id=1, source_target_pairs={{0,12},{4,8},{8,4},{12,0},{16,28},{20,24},{24,20},{28,16},{1,13},{... | collective-permute-start | bytes 884744 | tf_op jit(solution)/shard_map/ppermute | solution.py:538
  7.3 14.7 %collective-permute-start.4 = (f32[576,128]{1,0:T(8,128)}, f32[576,128]{1,0:T(8,128)}, u32[]{:S(2)}, u32[]{:S(2)}) collective-permute-start(f32[576,128]{1,0:T(8,128)} %get-tuple-element.27), channel_id=1, source_target_pairs={{0,4},{4,0},{8,12},{12,8},{16,20},{20,16},{24,28},{28,24},{1,5},{5... | collective-permute-start | bytes 884744 | tf_op jit(solution)/shard_map/ppermute | solution.py:538
  13.3 14.4 %collective-permute-start.5 = (f32[576,128]{1,0:T(8,128)}, f32[576,128]{1,0:T(8,128)}, u32[]{:S(2)}, u32[]{:S(2)}) collective-permute-start(f32[576,128]{1,0:T(8,128)} %get-tuple-element.26), channel_id=1, source_target_pairs={{0,24},{4,28},{8,16},{12,20},{16,8},{20,12},{24,0},{28,4},{1,25},{... | collective-permute-start | bytes 884744 | tf_op jit(solution)/shard_map/ppermute | solution.py:538
  16.3 17.2 %collective-permute-start.6 = (f32[576,128]{1,0:T(8,128)}, f32[576,128]{1,0:T(8,128)}, u32[]{:S(2)}, u32[]{:S(2)}) collective-permute-start(f32[576,128]{1,0:T(8,128)} %get-tuple-element.25), channel_id=1, source_target_pairs={{0,28},{4,24},{8,20},{12,16},{16,12},{20,8},{24,4},{28,0},{1,29},{... | collective-permute-start | bytes 884744 | tf_op jit(solution)/shard_map/ppermute | solution.py:538
  18.2 20.9 %collective-permute-start.10 = (f32[576,128]{1,0:T(8,128)}, f32[576,128]{1,0:T(8,128)}, u32[]{:S(2)}, u32[]{:S(2)}) collective-permute-start(f32[576,128]{1,0:T(8,128)} %get-tuple-element.19), channel_id=1, source_target_pairs={{0,16},{4,20},{8,24},{12,28},{16,0},{20,4},{24,8},{28,12},{1,17},{... | collective-permute-start | bytes 884744 | tf_op jit(solution)/shard_map/ppermute | solution.py:538
  20.7 20.9 %collective-permute-start.11 = (f32[576,128]{1,0:T(8,128)}, f32[576,128]{1,0:T(8,128)}, u32[]{:S(2)}, u32[]{:S(2)}) collective-permute-start(f32[576,128]{1,0:T(8,128)} %get-tuple-element.20), channel_id=1, source_target_pairs={{0,8},{4,12},{8,0},{12,4},{16,24},{20,28},{24,16},{28,20},{1,9},{5... | collective-permute-start | bytes 884744 | tf_op jit(solution)/shard_map/ppermute | solution.py:538
  22.0 24.5 %copy-start.1 = (f32[64,72,128]{2,1,0:T(8,128)S(1)}, f32[64,72,128]{2,1,0:T(8,128)}, u32[]{:S(2)}) copy-start(f32[64,72,128]{2,1,0:T(8,128)} %param.15) | copy-start | bytes 7077892
  22.1 24.4 %collective-permute-start.12 = (f32[576,128]{1,0:T(8,128)}, f32[576,128]{1,0:T(8,128)S(1)}, u32[]{:S(2)}, u32[]{:S(2)}) collective-permute-start(f32[576,128]{1,0:T(8,128)} %get-tuple-element.21), channel_id=1, source_target_pairs={{0,20},{4,16},{8,28},{12,24},{16,4},{20,0},{24,12},{28,8},{1,21},{... | collective-permute-start | bytes 884744 | tf_op jit(solution)/shard_map/ppermute | solution.py:538
  27.7 18.7 %collective-permute-start.13 = (f32[576,128]{1,0:T(8,128)}, f32[576,128]{1,0:T(8,128)S(1)}, u32[]{:S(2)}, u32[]{:S(2)}) collective-permute-start(f32[576,128]{1,0:T(8,128)} %get-tuple-element.22), channel_id=1, source_target_pairs={{0,12},{4,8},{8,4},{12,0},{16,28},{20,24},{24,20},{28,16},{1,13},{... | collective-permute-start | bytes 884744 | tf_op jit(solution)/shard_map/ppermute | solution.py:538
  33.5 12.9 %collective-permute-start.9 = (f32[576,128]{1,0:T(8,128)}, f32[576,128]{1,0:T(8,128)S(1)}, u32[]{:S(2)}, u32[]{:S(2)}) collective-permute-start(f32[576,128]{1,0:T(8,128)} %get-tuple-element.18), channel_id=1, source_target_pairs={{0,4},{4,0},{8,12},{12,8},{16,20},{20,16},{24,28},{28,24},{1,5},{5... | collective-permute-start | bytes 884744 | tf_op jit(solution)/shard_map/ppermute | solution.py:538
  39.2 13.7 %collective-permute-start.8 = (f32[576,128]{1,0:T(8,128)}, f32[576,128]{1,0:T(8,128)S(1)}, u32[]{:S(2)}, u32[]{:S(2)}) collective-permute-start(f32[576,128]{1,0:T(8,128)} %get-tuple-element.17), channel_id=1, source_target_pairs={{0,24},{4,28},{8,16},{12,20},{16,8},{20,12},{24,0},{28,4},{1,25},{... | collective-permute-start | bytes 884744 | tf_op jit(solution)/shard_map/ppermute | solution.py:538
  41.6 15.7 %collective-permute-start.7 = (f32[576,128]{1,0:T(8,128)}, f32[576,128]{1,0:T(8,128)S(1)}, u32[]{:S(2)}, u32[]{:S(2)}) collective-permute-start(f32[576,128]{1,0:T(8,128)} %get-tuple-element.16), channel_id=1, source_target_pairs={{0,28},{4,24},{8,20},{12,16},{16,12},{20,8},{24,4},{28,0},{1,29},{... | collective-permute-start | bytes 884744 | tf_op jit(solution)/shard_map/ppermute | solution.py:538
  53.3 5.5 %copy-start.2 = (bf16[2048,128]{1,0:T(8,128)(2,1)S(1)}, bf16[2048,128]{1,0:T(8,128)(2,1)}, u32[]{:S(2)}) copy-start(bf16[2048,128]{1,0:T(8,128)(2,1)} %constant.46.clone.gather_ref) | copy-start | bytes 1572868
  53.3 5.5 %copy-start.4 = (f32[72,128]{1,0:T(8,128)S(1)}, f32[72,128]{1,0:T(8,128)}, u32[]{:S(2)}) copy-start(f32[72,128]{1,0:T(8,128)} %equal_ref.5) | copy-start | bytes 110596
  53.4 5.5 %copy-start.5 = (f32[8,128]{1,0:T(8,128)S(1)}, f32[8,128]{1,0:T(8,128)}, u32[]{:S(2)}) copy-start(f32[8,128]{1,0:T(8,128)} %constant.45.clone.sign_ref) | copy-start | bytes 12292
  61.3 2.8 %collective-permute-start.14 = (f32[288,128]{1,0:T(8,128)S(1)}, f32[288,128]{1,0:T(8,128)S(1)}, u32[]{:S(2)}, u32[]{:S(2)}) collective-permute-start(f32[288,128]{1,0:T(8,128)S(1)} %contract.4), channel_id=1, source_target_pairs={{0,4},{4,0},{8,12},{12,8},{16,20},{20,16},{24,28},{28,24},{1,5},{5... | collective-permute-start | bytes 442376 | tf_op jit(solution)/shard_map/ppermute | solution.py:538
  64.1 4.9 %collective-permute-start.15 = (f32[72,128]{1,0:T(8,128)S(1)}, f32[72,128]{1,0:T(8,128)S(1)}, u32[]{:S(2)}, u32[]{:S(2)}) collective-permute-start(f32[72,128]{1,0:T(8,128)S(1)} %get-tuple-element.34), channel_id=1, source_target_pairs={{0,24},{4,28},{8,16},{12,20},{16,8},{20,12},{24,0},{28,4},{1,25},{... | collective-permute-start | bytes 110600 | tf_op jit(solution)/shard_map/ppermute | solution.py:538
  66.8 4.0 %collective-permute-start.16 = (f32[72,128]{1,0:T(8,128)S(1)}, f32[72,128]{1,0:T(8,128)S(1)}, u32[]{:S(2)}, u32[]{:S(2)}) collective-permute-start(f32[72,128]{1,0:T(8,128)S(1)} %get-tuple-element.32), channel_id=1, source_target_pairs={{0,16},{4,20},{8,24},{12,28},{16,0},{20,4},{24,8},{28,12},{1,17},{... | collective-permute-start | bytes 110600 | tf_op jit(solution)/shard_map/ppermute | solution.py:538
  67.3 4.0 %collective-permute-start.17 = (f32[72,128]{1,0:T(8,128)S(1)}, f32[72,128]{1,0:T(8,128)S(1)}, u32[]{:S(2)}, u32[]{:S(2)}) collective-permute-start(f32[72,128]{1,0:T(8,128)S(1)} %get-tuple-element.33), channel_id=1, source_target_pairs={{0,8},{4,12},{8,0},{12,4},{16,24},{20,28},{24,16},{28,20},{1,9},{5... | collective-permute-start | bytes 110600 | tf_op jit(solution)/shard_map/ppermute | solution.py:538
  71.3 8.5 %copy-start.7 = (f32[72,128]{1,0:T(8,128)S(1)}, f32[72,128]{1,0:T(8,128)}, u32[]{:S(2)}) copy-start(f32[72,128]{1,0:T(8,128)} %param.16) | copy-start | bytes 110596
  71.3 8.6 %copy-start.3 = (bf16[256,2048]{1,0:T(8,128)(2,1)S(1)}, bf16[256,2048]{1,0:T(8,128)(2,1)}, u32[]{:S(2)}) copy-start(bf16[256,2048]{1,0:T(8,128)(2,1)} %constant.47.clone.spread_ref) | copy-start | bytes 3145732
  71.3 5.9 %collective-permute-start.18 = (f32[72,128]{1,0:T(8,128)S(1)}, f32[72,128]{1,0:T(8,128)S(1)}, u32[]{:S(2)}, u32[]{:S(2)}) collective-permute-start(f32[72,128]{1,0:T(8,128)S(1)} %slice_add_fusion.1), channel_id=1, source_target_pairs={{0,3},{1,2},{2,1},{3,0},{4,7},{5,6},{6,5},{7,4},{8,11},{9,10},{10,... | collective-permute-start | bytes 110600 | tf_op jit(solution)/shard_map/ppermute | solution.py:538
  75.0 4.9 %collective-permute-start.19 = (f32[72,128]{1,0:T(8,128)S(1)}, f32[72,128]{1,0:T(8,128)S(1)}, u32[]{:S(2)}, u32[]{:S(2)}) collective-permute-start(f32[72,128]{1,0:T(8,128)S(1)} %slice_add_fusion.1), channel_id=1, source_target_pairs={{0,2},{1,3},{2,0},{3,1},{4,6},{5,7},{6,4},{7,5},{8,10},{9,11},{10,... | collective-permute-start | bytes 110600 | tf_op jit(solution)/shard_map/ppermute | solution.py:538
  75.0 4.9 %collective-permute-start.20 = (f32[72,128]{1,0:T(8,128)S(1)}, f32[72,128]{1,0:T(8,128)S(1)}, u32[]{:S(2)}, u32[]{:S(2)}) collective-permute-start(f32[72,128]{1,0:T(8,128)S(1)} %slice_add_fusion.1), channel_id=1, source_target_pairs={{0,1},{1,0},{2,3},{3,2},{4,5},{5,4},{6,7},{7,6},{8,9},{9,8},{10,11... | collective-permute-start | bytes 110600 | tf_op jit(solution)/shard_map/ppermute | solution.py:538
